TPU v7x, 32 devices: a whole 2x2x4 slice. The times are simulated.
32 devices in a mesh: row: 2 (over x), col: 16 (over z, y, core).
Axes of the slice: x: 2, y: 2, z: 4, core: 2. Of those that a mesh axis runs over, the one named last changes fastest.
Arguments:
- sub_vectors: bfloat16 [8192, 2048], P('row', 'col'), may hold values from -6 to 6
- merge_factor: bfloat16 [128, 8192], P('row', 'col'), may hold values from -0.0625 to 0.0625
- reflectors: bfloat16 [16, 1024, 256], P('col'), may hold values from -0.1875 to 0.1875
- wy_factors: bfloat16 [16, 256, 256], P('col'), may hold values from -0.1875 to 0.1875
- owners: int32 [6], replicated, may hold values from 0 to 15, as said below
- offsets: int32 [6], replicated, may hold values from 0 to 1024, as said below
Outputs:
- eigenvectors: bfloat16 [128, 2048], P(('row', 'col'))
Inputs may be any that keep to these rules, and one draw needn't show every extreme that they name: Distinct owners; 0 and 15 each own a group. `offsets`: some group starts at 0 and some at 1024.
All inputs are finite; a program needn't handle non-finite values.
Results may differ from a plain program's by a relative error of at most 0.0011.
Values may be sent and summed in bfloat16 or wider, within the bound.
No kernel may reach another device: no remote copies, remote signals or barrier semaphores. Data moves between devices by JAX's collectives and lax.ppermute only.
A program may use at most 64 MiB of HBM per device.

v0:
```python
import jax
import jax.numpy as jnp
from jax import lax
from jax.sharding import PartitionSpec as P

GROUPS = 6


def spread(block, axis, owner):
    block = jnp.where(lax.axis_index(axis) == owner, block, jnp.zeros_like(block))
    return lax.psum(block, axis)


def local(sub_vectors, merge_factor, reflectors, wy_factors, owners, offsets):
    all_sub = lax.all_gather(sub_vectors, "row", axis=0, tiled=True)
    merged = jnp.dot(
        lax.all_gather(merge_factor, "col", axis=1, tiled=True),
        all_sub,
        preferred_element_type=jnp.float32,
    )
    vectors = lax.all_to_all(merged, "col", split_axis=0, concat_axis=1, tiled=True)
    group_rows = reflectors.shape[1]
    for group_index in range(GROUPS):
        owner_now = owners[group_index]
        offset_now = offsets[group_index]
        basis, factor = (
            spread(reflectors[0], "col", owner_now),
            spread(wy_factors[0], "col", owner_now),
        )
        basis_full = basis.astype(jnp.float32)
        factor_full = factor.astype(jnp.float32)
        block = lax.dynamic_slice_in_dim(vectors, offset_now, group_rows, 1)
        weights = jnp.dot(block, basis_full, precision=lax.Precision.HIGHEST)
        scaled = jnp.dot(weights, factor_full.T, precision=lax.Precision.HIGHEST)
        block = block - jnp.dot(scaled, basis_full.T, precision=lax.Precision.HIGHEST)
        vectors = lax.dynamic_update_slice_in_dim(vectors, block, offset_now, 1)
    return vectors.astype(jnp.bfloat16)


def solution(mesh):
    in_specs = (
        P("row", "col"),
        P("row", "col"),
        P("col", None, None),
        P("col", None, None),
        P(),
        P(),
    )
    out_specs = P(("row", "col"), None)
    return jax.shard_map(local, mesh=mesh, in_specs=in_specs, out_specs=out_specs, check_vma=False)
```

profile of v0, /device:TPU:0, one launch (start us, length us, event | category | flops | bytes accessed | tf_op | source)
XLA Modules:
  0.0 224.9 jit_solution(16737445094431974683)
XLA Ops:
  6.5 0.0 all-gather.3.cloned.1.call-start
  6.5 0.7 all-gather.3.cloned.1.call-update
  7.3 0.0 all-gather.5.cloned.1.call-start
  7.3 0.7 all-gather.5.cloned.1.call-update
  8.0 0.0 all-reduce.3.cloned.1.call-start
  8.1 1.5 fusion.19
  13.2 1.8 select_bitcast_fusion.6
  15.0 0.0 copy-done.4
  15.1 1.7 select_bitcast_fusion
  16.8 0.0 all-reduce.3.cloned.1.call-update
  16.8 0.0 copy-start.9
  16.8 32.2 %all-gather.3.cloned.1.call-done = bf16[64,8192]{1,0:T(8,128)(2,1)} async-done(((bf16[64,512]{1,0:T(8,128)(2,1)}), bf16[64,8192]{1,0:T(8,128)(2,1)}) %all-gather.3.cloned.1.call-update) | async-done | bytes 1048592 | tf_op jit(solution)/shard_map/all_gather | solution.py:17
  49.1 34.2 %all-gather.5.cloned.1.call-done = bf16[8192,128]{1,0:T(8,128)(2,1)} async-done(((bf16[4096,128]{1,0:T(8,128)(2,1)}), bf16[8192,128]{1,0:T(8,128)(2,1)}) %all-gather.5.cloned.1.call-update) | async-done | bytes 2097168 | tf_op jit(solution)/shard_map/all_gather | solution.py:15
  83.3 3.0 %fusion.20 = f32[64,128]{1,0:T(8,128)} fusion(bf16[64,8192]{1,0:T(8,128)(2,1)} %all-gather.3.cloned.1.call-done, bf16[8192,128]{1,0:T(8,128)(2,1)} %all-gather.5.cloned.1.call-done), kind=kOutput, calls=%fused_computation.38 | convolution fusion | flops 134217728 | bytes 3178496 | tf_op jit(solution)/shard_map/dot_general | solution.py:16
  86.3 5.6 %all-to-all-start = ((f32[16,4,128]{2,1,0:T(4,128)}), f32[16,4,128]{2,1,0:T(4,128)S(1)}, u32[]{:S(2)}, u32[]{:S(2)}) async-start(f32[16,4,128]{2,1,0:T(4,128)} %bitcast), calls=%async_computation | async-start | bytes 65536 | tf_op jit(solution)/shard_map/all_to_all | solution.py:21
  91.9 0.0 copy-done.9
  91.9 0.7 fusion.18
  104.3 98.2 %all-reduce.3.cloned.1.call-done = (bf16[1024,256]{1,0:T(8,128)(2,1)}, bf16[256,256]{1,0:T(8,128)(2,1)}, bf16[1024,256]{1,0:T(8,128)(2,1)}, bf16[256,256]{1,0:T(...) async-done(((bf16[1024,256]{1,0:T(8,128)(2,1)}, ...) | async-done | bytes 3932176 | tf_op jit(solution)/shard_map/psum | solution.py:11
  202.5 0.0 all-to-all-done
  202.5 0.0 copy-start.7
  202.5 1.5 fusion.10
  204.0 1.1 fusion.21
  205.1 1.7 convolution_subtract_fusion.5
  206.8 0.3 dynamic_update_slice.18
  207.1 0.0 copy-start.6
  207.1 1.4 fusion.8
  208.6 1.1 fusion.22
  209.6 1.7 convolution_subtract_fusion.4
  211.3 0.4 dynamic_update_slice.19
  211.8 0.0 copy-done.3
  211.8 0.4 fusion.6
  212.2 0.2 fusion.23
  212.3 0.6 convolution_subtract_fusion.3
  212.9 0.4 dynamic_update_slice.20
  213.4 0.0 copy-done.2
  213.4 0.4 fusion.4
  213.7 0.2 fusion.24
  213.9 0.6 convolution_subtract_fusion.2
  214.5 0.4 dynamic_update_slice.21
  214.9 0.4 fusion.2
  215.3 0.2 fusion.25
  215.4 0.6 convolution_subtract_fusion.1
  216.0 0.4 dynamic_update_slice.22
  216.4 0.4 fusion
  216.8 0.2 fusion.26
  217.0 0.6 convolution_subtract_fusion
  217.6 0.2 dynamic_update_slice.23
  217.8 0.6 convert_element_type.2
  (13 shorter events, 0.0 us)
Async XLA Ops:
  6.5 8.5 %copy-start.4 = (bf16[1,1024,256]{2,1,0:T(8,128)(2,1)S(1)}, bf16[1,1024,256]{2,1,0:T(8,128)(2,1)}, u32[]{:S(2)}) copy-start(bf16[1,1024,256]{2,1,0:T(8,128)(2,1)} %param.8) | copy-start | bytes 1572868
  6.5 42.5 %all-gather.3.cloned.1.call-start = ((), (), s32[]{:S(2)}) async-start(), calls=%async_computation.1 | async-start | bytes 1114112 | tf_op jit(solution)/shard_map/all_gather | solution.py:17
  7.3 76.0 %all-gather.5.cloned.1.call-start = ((), (), s32[]{:S(2)}) async-start(), calls=%async_computation.2 | async-start | bytes 3145728 | tf_op jit(solution)/shard_map/all_gather | solution.py:15
  8.0 194.5 %all-reduce.3.cloned.1.call-start = ((), (), s32[]{:S(2)}) async-start(), calls=%async_computation.3 | async-start | bytes 7864320 | tf_op jit(solution)/shard_map/psum | solution.py:11
  16.8 75.1 %copy-start.9 = (s32[6]{0:T(128)S(1)}, s32[6]{0:T(128)}, u32[]{:S(2)}) copy-start(s32[6]{0:T(128)} %param.11) | copy-start | bytes 76
  86.3 116.2 %all-to-all-start = ((f32[16,4,128]{2,1,0:T(4,128)}), f32[16,4,128]{2,1,0:T(4,128)S(1)}, u32[]{:S(2)}, u32[]{:S(2)}) async-start(f32[16,4,128]{2,1,0:T(4,128)} %bitcast), calls=%async_computation | async-start | bytes 65536 | tf_op jit(solution)/shard_map/all_to_all | solution.py:21
  202.5 9.3 %copy-start.3 = (bf16[1024,256]{1,0:T(8,128)(2,1)S(1)}, bf16[1024,256]{1,0:T(8,128)(2,1)}, u32[]{:S(2)}) copy-start(bf16[1024,256]{1,0:T(8,128)(2,1)} %get-tuple-element.9) | copy-start | bytes 1572868
  202.5 9.7 %copy-start.8 = (bf16[256,256]{1,0:T(8,128)(2,1)S(1)}, bf16[256,256]{1,0:T(8,128)(2,1)}, u32[]{:S(2)}) copy-start(bf16[256,256]{1,0:T(8,128)(2,1)} %get-tuple-element.10) | copy-start | bytes 393220
  202.5 10.9 %copy-start.2 = (bf16[1024,256]{1,0:T(8,128)(2,1)S(1)}, bf16[1024,256]{1,0:T(8,128)(2,1)}, u32[]{:S(2)}) copy-start(bf16[1024,256]{1,0:T(8,128)(2,1)} %get-tuple-element.11) | copy-start | bytes 1572868
  202.5 11.2 %copy-start.7 = (bf16[256,256]{1,0:T(8,128)(2,1)S(1)}, bf16[256,256]{1,0:T(8,128)(2,1)}, u32[]{:S(2)}) copy-start(bf16[256,256]{1,0:T(8,128)(2,1)} %get-tuple-element.12) | copy-start | bytes 393220
  205.1 9.8 %copy-start.1 = (bf16[1024,256]{1,0:T(8,128)(2,1)S(1)}, bf16[1024,256]{1,0:T(8,128)(2,1)}, u32[]{:S(2)}) copy-start(bf16[1024,256]{1,0:T(8,128)(2,1)} %get-tuple-element.13) | copy-start | bytes 1572868
  207.1 8.2 %copy-start.6 = (bf16[256,256]{1,0:T(8,128)(2,1)S(1)}, bf16[256,256]{1,0:T(8,128)(2,1)}, u32[]{:S(2)}) copy-start(bf16[256,256]{1,0:T(8,128)(2,1)} %get-tuple-element.14) | copy-start | bytes 393220
  209.6 6.8 %copy-start = (bf16[1024,256]{1,0:T(8,128)(2,1)S(1)}, bf16[1024,256]{1,0:T(8,128)(2,1)}, u32[]{:S(2)}) copy-start(bf16[1024,256]{1,0:T(8,128)(2,1)} %get-tuple-element.15) | copy-start | bytes 1572868
  211.8 5.0 %copy-start.5 = (bf16[256,256]{1,0:T(8,128)(2,1)S(1)}, bf16[256,256]{1,0:T(8,128)(2,1)}, u32[]{:S(2)}) copy-start(bf16[256,256]{1,0:T(8,128)(2,1)} %get-tuple-element.16) | copy-start | bytes 393220
Sparse Core Ops, SparseCore 0:
  9.5 39.5 all-gather.2
  50.6 32.5 all-gather.4
  88.4 114.0 all-reduce.2
where the time goes:
time: 226 us; the launch traced here: 225 us
  waiting for transfers between devices  166 us (73%)
  between operations  28.6 us (13%)
  matrix products  16 us (7%)
  starting transfers between devices  5.7 us (3%)
  local copies, waits for them, and re-layouts  4.43 us (2%)
  other arithmetic  4.16 us (2%)
    psum x1, waiting for transfers between devices, spread(): return lax.psum(block, axis)  98.2 us
    all_gather x1, waiting for transfers between devices, local(): all_sub = lax.all_gather(sub_vectors, 'row', axis=0, tiled=True)  34.2 us
    all_gather x1, waiting for transfers between devices, local(): lax.all_gather(merge_factor, 'col', axis=1, tiled=True)  32.2 us
    dot_general x6, matrix products, local(): jnp.dot(scaled, basis_full.T, precision=lax.Precision.HIGHEST)  5.67 us
    all_to_all x1, starting transfers between devices, local(): lax.all_to_all(merged, 'col', split_axis=0, concat_axis=1, tiled=True)  5.62 us
  transfers between devices with their start and end apart: 4, of which 3 were waited for; matrix products, arithmetic and copies ran while one was open for 4% of the time, Pallas kernels for 0%

commit v1 on v0

v1 whole, which is shorter than its diff:
```python
import jax
import jax.numpy as jnp
from jax import lax
from jax.sharding import PartitionSpec as P

GROUPS = 6


def gather_factor(merge_factor, rows, cols):
    share = cols // rows
    width = merge_factor.shape[1]
    pairs = []
    for r in range(rows):
        for c in range(cols):
            pairs.append((r * cols + c, (c // share) * cols + share * r + c % share))
    held = lax.ppermute(merge_factor, ("row", "col"), pairs)[None]
    me = lax.axis_index("col")
    bits = [1 << k for k in reversed(range(cols.bit_length() - 1))]
    for bit in bits:
        other = lax.ppermute(held, "col", [(c, c ^ bit) for c in range(cols)])
        upper = (me & bit) != 0
        first = jnp.where(upper, other, held)
        second = jnp.where(upper, held, other)
        held = jnp.concatenate([first, second], 0)
    steps = len(bits)
    shape = [2] * steps
    held = held.reshape(shape + list(merge_factor.shape))
    order = [bits[::-1].index(b) for b in sorted(bits, reverse=True)]
    held = held.transpose(order + [steps, steps + 1])
    held = held.reshape(rows, share, merge_factor.shape[0], width)
    return held.transpose(0, 2, 1, 3).reshape(rows * merge_factor.shape[0], share * width)


def local(rows, cols, sub_vectors, merge_factor, reflectors, wy_factors, owners, offsets):
    me = lax.axis_index("col")
    mine = jnp.concatenate([reflectors[0], wy_factors[0]], 0)
    low = jnp.full_like(mine, -jnp.inf)
    spread = jnp.stack([jnp.where(owners[g] == me, mine, low) for g in range(GROUPS)])
    spread = lax.pmax(spread, ("row", "col"))

    factor_part = gather_factor(merge_factor, rows, cols)
    merged = jnp.dot(factor_part, sub_vectors, preferred_element_type=jnp.float32)
    parts = rows * cols
    each = merged.shape[0] // parts
    pieces = lax.all_to_all(
        merged.reshape(parts, each, merged.shape[1]), ("row", "col"), 0, 0
    )
    pieces = pieces.reshape(rows, cols, each, merged.shape[1]).sum(0)
    vectors = pieces.transpose(1, 0, 2).reshape(each, cols * merged.shape[1])

    group_rows = reflectors.shape[1]
    for group_index in range(GROUPS):
        offset_now = offsets[group_index]
        basis_full = spread[group_index, :group_rows].astype(jnp.float32)
        factor_full = spread[group_index, group_rows:].astype(jnp.float32)
        block = lax.dynamic_slice_in_dim(vectors, offset_now, group_rows, 1)
        weights = jnp.dot(block, basis_full, precision=lax.Precision.HIGHEST)
        scaled = jnp.dot(weights, factor_full.T, precision=lax.Precision.HIGHEST)
        block = block - jnp.dot(scaled, basis_full.T, precision=lax.Precision.HIGHEST)
        vectors = lax.dynamic_update_slice_in_dim(vectors, block, offset_now, 1)
    return vectors.astype(jnp.bfloat16)


def solution(mesh):
    rows, cols = mesh.shape["row"], mesh.shape["col"]

    def body(*args):
        return local(rows, cols, *args)

    in_specs = (
        P("row", "col"),
        P("row", "col"),
        P("col", None, None),
        P("col", None, None),
        P(),
        P(),
    )
    out_specs = P(("row", "col"), None)
    return jax.shard_map(body, mesh=mesh, in_specs=in_specs, out_specs=out_specs, check_vma=False)
```

time: 226 us -> 208 us (0.920)
  waiting for transfers between devices: 166 us -> 123 us
  matrix products: 16 us -> 25.5 us
  starting transfers between devices: 5.7 us -> 15.2 us
  local copies, waits for them, and re-layouts: 4.43 us -> 8.65 us
  other arithmetic: 4.16 us -> 6.8 us
    pmax x0 -> x1, waiting for transfers between devices: none -> 106 us  [local(): spread = lax.pmax(spread, ('row', 'col'))]
    psum x1 -> x0, waiting for transfers between devices: 98.2 us -> none  [spread(): return lax.psum(block, axis)]
    all_gather x2 -> x0, waiting for transfers between devices: 66.4 us -> none  [the longest x1 34.2 us: local(): all_sub = lax.all_gather(sub_vectors, 'row', axis=0, tiled=True)]
    ppermute x0 -> x5, waiting for transfers between devices: none -> 16.7 us  [the longest x4 16.7 us: gather_factor(): other = lax.ppermute(held, 'col', [(c, c ^ bit) for c in range(cols)])]
    ppermute x0 -> x5, starting transfers between devices: none -> 9.55 us  [the longest x4 7.93 us: gather_factor(): other = lax.ppermute(held, 'col', [(c, c ^ bit) for c in range(cols)])]
    unnamed x0 -> x5, other arithmetic: none -> 4.88 us
    dot_general x6, matrix products: 5.67 us -> 9.72 us  [local(): jnp.dot(scaled, basis_full.T, precision=lax.Precision.HIGHEST)]
    dot_general x6, matrix products: 4.4 us -> 8.42 us  [local(): weights = jnp.dot(block, basis_full, precision=lax.Precision.HIGHEST)]
  transfers between devices with their start and end apart: 4 -> 7, of which waited for: 3 -> 5; matrix products, arithmetic and copies ran while one was open for 4% -> 6% of each run, Pallas kernels for 0% -> 0%
where the time goes in v1:
time: 208 us; the launch traced here: 207 us
  waiting for transfers between devices  123 us (59%)
  between operations  28.2 us (14%)
  matrix products  25.5 us (12%)
  starting transfers between devices  15.2 us (7%)
  local copies, waits for them, and re-layouts  8.65 us (4%)
  other arithmetic  6.8 us (3%)
    pmax x1, waiting for transfers between devices, local(): spread = lax.pmax(spread, ('row', 'col'))  106 us
    ppermute x4, waiting for transfers between devices, gather_factor(): other = lax.ppermute(held, 'col', [(c, c ^ bit) for c in range(cols)])  16.7 us
    dot_general x6, matrix products, local(): jnp.dot(scaled, basis_full.T, precision=lax.Precision.HIGHEST)  9.72 us
    dot_general x6, matrix products, local(): weights = jnp.dot(block, basis_full, precision=lax.Precision.HIGHEST)  8.42 us
    ppermute x4, starting transfers between devices, gather_factor(): other = lax.ppermute(held, 'col', [(c, c ^ bit) for c in range(cols)])  7.93 us
    dot_general x6, matrix products, local(): scaled = jnp.dot(weights, factor_full.T, precision=lax.Precision.HIGHEST)  6.51 us
    all_to_all x1, starting transfers between devices, local(): lax.all_to_all(merged.reshape(parts, each, merged.shape[1]), ('row', 'col...  5.67 us
    unnamed x5, other arithmetic  4.88 us
  transfers between devices with their start and end apart: 7, of which 5 were waited for; matrix products, arithmetic and copies ran while one was open for 6% of the time, Pallas kernels for 0%

profile of v1, /device:TPU:0, one launch (start us, length us, event | category | flops | bytes accessed | tf_op | source)
XLA Modules:
  0.0 207.1 jit_solution(406214727358462759)
XLA Ops:
  6.5 1.6 collective-permute-start
  8.2 1.5 fusion.28
  9.7 1.1 constant_dynamic-update-slice_fusion.1
  13.2 0.9 constant_dynamic-update-slice_fusion
  14.1 1.0 select_dynamic-update-slice_fusion.5
  15.1 1.0 select_dynamic-update-slice_fusion.4
  16.1 1.0 select_dynamic-update-slice_fusion.3
  17.1 1.0 select_dynamic-update-slice_fusion.2
  18.7 5.8 %collective-permute-start.1 = (bf16[1,64,512]{2,1,0:T(8,128)(2,1)S(1)}, bf16[1,64,512]{2,1,0:T(8,128)(2,1)S(1)}, u32[]{:S(2)}, u32[]{:S(2)}) collective-permute-start(bf16[1,64,512]{2,1,0:T(8,128)(2,1)S(1)} %bitcast.90), channel_id=1, source_target_pairs={{0,8},{1,9},{2,10},{3,11},{4,12},{5,13},{6,14},{7,15},{8,0},{9,1},... | collective-permute-start | bytes 196616 | tf_op jit(solution)/shard_map/ppermute | solution.py:20
  24.5 1.0 select_dynamic-update-slice_fusion.1
  26.1 1.9 collective-permute-done.1
  28.1 0.5 collective-permute-start.2
  28.5 1.0 select_dynamic-update-slice_fusion
  29.5 3.6 %collective-permute-done.2 = bf16[2,64,512]{2,1,0:T(8,128)(2,1)S(1)} collective-permute-done((bf16[2,64,512]{2,1,0:T(8,128)(2,1)S(1)}, bf16[2,64,512]{2,1,0:T(8,128)(2,1)S(1)}, u32[]{:S(2)}, u32[]{:S(2)}) %collective-permute-start.2) | collective-permute-done | bytes 131104 | tf_op jit(solution)/shard_map/ppermute | solution.py:20
  33.1 1.6 collective-permute-start.3
  34.7 9.3 %collective-permute-done.3 = bf16[4,64,512]{2,1,0:T(8,128)(2,1)S(1)} collective-permute-done((bf16[4,64,512]{2,1,0:T(8,128)(2,1)S(1)}, bf16[4,64,512]{2,1,0:T(8,128)(2,1)S(1)}, u32[]{:S(2)}, u32[]{:S(2)}) %collective-permute-start.3) | collective-permute-done | bytes 262176 | tf_op jit(solution)/shard_map/ppermute | solution.py:20
  44.2 1.9 collective-permute-done.4
  46.4 0.6 copy.17
  47.0 0.8 dot_general.59
  47.8 0.8 fusion
  48.6 0.7 copy.19
  49.3 5.7 %all-to-all-start = ((f32[32,4,128]{2,1,0:T(4,128)}), f32[32,4,128]{2,1,0:T(4,128)S(1)}, u32[]{:S(2)}, u32[]{:S(2)}) async-start(f32[32,4,128]{2,1,0:T(4,128)} %copy.19), calls=%async_computation | async-start | bytes 131072 | tf_op jit(solution)/shard_map/all_to_all | solution.py:45
  55.0 0.7 fusion.27
  66.6 106.0 %all-reduce.2.cloned.1.call-done = bf16[6,1280,256]{2,1,0:T(8,128)(2,1)} async-done(((bf16[6,1280,256]{2,1,0:T(8,128)(2,1)}), bf16[6,1280,256]{2,1,0:T(8,128)(2,1)}) %all-reduce.2.cloned.1.call-update) | async-done | bytes 3932176 | tf_op jit(solution)/shard_map/pmax | solution.py:39
  172.6 1.4 fusion.3
  174.0 1.1 fusion.14
  175.1 1.6 convolution_subtract_fusion.5
  177.0 1.4 fusion.4
  178.4 1.1 fusion.13
  179.5 1.6 convolution_subtract_fusion.4
  181.1 0.5 dynamic_update_slice.19
  181.5 1.4 fusion.5
  182.9 1.1 fusion.12
  184.0 1.6 convolution_subtract_fusion.3
  185.6 0.3 dynamic_update_slice.20
  186.0 1.4 fusion.6
  187.4 1.1 fusion.11
  188.5 1.6 convolution_subtract_fusion.2
  190.1 0.4 dynamic_update_slice.21
  190.5 1.4 fusion.7
  191.9 1.1 fusion.10
  193.0 1.6 convolution_subtract_fusion.1
  194.6 0.5 dynamic_update_slice.22
  195.1 1.4 fusion.8
  196.5 1.1 fusion.9
  197.6 1.6 convolution_subtract_fusion
  199.2 0.5 dynamic_update_slice.23
  199.6 0.6 convert_element_type.2
  (20 shorter events, 0.8 us)
Async XLA Ops:
  6.5 41.2 %copy-start = (bf16[4096,128]{1,0:T(8,128)(2,1)S(1)}, bf16[4096,128]{1,0:T(8,128)(2,1)}, u32[]{:S(2)}) copy-start(bf16[4096,128]{1,0:T(8,128)(2,1)} %param.6) | copy-start | bytes 3145732
  6.5 166.1 %all-reduce.2.cloned.1.call-start = ((), (), s32[]{:S(2)}) async-start(), calls=%async_computation.1 | async-start | bytes 7864320 | tf_op jit(solution)/shard_map/pmax | solution.py:39
  6.5 12.1 %collective-permute-start = (bf16[64,512]{1,0:T(8,128)(2,1)}, bf16[64,512]{1,0:T(8,128)(2,1)S(1)}, u32[]{:S(2)}, u32[]{:S(2)}) collective-permute-start(bf16[64,512]{1,0:T(8,128)(2,1)} %param.7), channel_id=1, source_target_pairs={{0,0},{1,1},{2,2},{3,3},{4,4},{5,5},{6,6},{7,7},{8,16},{9,17},{10,... | collective-permute-start | bytes 196616 | tf_op jit(solution)/shard_map/ppermute | solution.py:16
  18.7 9.3 %collective-permute-start.1 = (bf16[1,64,512]{2,1,0:T(8,128)(2,1)S(1)}, bf16[1,64,512]{2,1,0:T(8,128)(2,1)S(1)}, u32[]{:S(2)}, u32[]{:S(2)}) collective-permute-start(bf16[1,64,512]{2,1,0:T(8,128)(2,1)S(1)} %bitcast.90), channel_id=1, source_target_pairs={{0,8},{1,9},{2,10},{3,11},{4,12},{5,13},{6,14},{7,15},{8,0},{9,1},... | collective-permute-start | bytes 196616 | tf_op jit(solution)/shard_map/ppermute | solution.py:20
  28.1 5.0 %collective-permute-start.2 = (bf16[2,64,512]{2,1,0:T(8,128)(2,1)S(1)}, bf16[2,64,512]{2,1,0:T(8,128)(2,1)S(1)}, u32[]{:S(2)}, u32[]{:S(2)}) collective-permute-start(bf16[2,64,512]{2,1,0:T(8,128)(2,1)S(1)} %pad_maximum_fusion.3), channel_id=1, source_target_pairs={{0,4},{1,5},{2,6},{3,7},{4,0},{5,1},{6,2},{7,3},{8,12},{9,13},{10,... | collective-permute-start | bytes 393224 | tf_op jit(solution)/shard_map/ppermute | solution.py:20
  33.1 10.9 %collective-permute-start.3 = (bf16[4,64,512]{2,1,0:T(8,128)(2,1)S(1)}, bf16[4,64,512]{2,1,0:T(8,128)(2,1)S(1)}, u32[]{:S(2)}, u32[]{:S(2)}) collective-permute-start(bf16[4,64,512]{2,1,0:T(8,128)(2,1)S(1)} %pad_maximum_fusion.2), channel_id=1, source_target_pairs={{0,2},{1,3},{2,0},{3,1},{4,6},{5,7},{6,4},{7,5},{8,10},{9,11},{10,... | collective-permute-start | bytes 786440 | tf_op jit(solution)/shard_map/ppermute | solution.py:20
  44.1 2.0 collective-permute-start.4
  46.3 8.7 %copy-start.1 = (s32[6]{0:T(128)S(1)}, s32[6]{0:T(128)}, u32[]{:S(2)}) copy-start(s32[6]{0:T(128)} %param.11) | copy-start | bytes 76
  49.3 17.2 %all-to-all-start = ((f32[32,4,128]{2,1,0:T(4,128)}), f32[32,4,128]{2,1,0:T(4,128)S(1)}, u32[]{:S(2)}, u32[]{:S(2)}) async-start(f32[32,4,128]{2,1,0:T(4,128)} %copy.19), calls=%async_computation | async-start | bytes 131072 | tf_op jit(solution)/shard_map/all_to_all | solution.py:45
Sparse Core Ops, SparseCore 0:
  29.6 142.9 all-reduce.1

commit v2 on v0

v2 whole, which is shorter than its diff:
```python
import functools

import jax
import jax.numpy as jnp
from jax import lax
from jax.experimental import pallas as pl
from jax.experimental.pallas import tpu as pltpu
from jax.sharding import PartitionSpec as P

GROUPS = 6
PHASES = ((0, 1, 2), (3, 4, 5))
INNER = 4
VMEM = pl.BlockSpec(memory_space=pltpu.VMEM)
SMEM = pl.BlockSpec(memory_space=pltpu.SMEM)
ANY = pl.BlockSpec(memory_space=pl.ANY)
LIMIT = pltpu.CompilerParams(vmem_limit_bytes=40 * 1024 * 1024)


def pack_kernel(place, basis, factor, *outs):
    row_bit, inner = place[0], place[1]
    pv, pt = basis.shape[0] // (2 * INNER), factor.shape[0] // (2 * INNER)
    for mask, out in enumerate(outs):
        e = row_bit * INNER + jnp.bitwise_xor(inner, mask)
        out[:pv, :] = basis[pl.ds(pl.multiple_of(e * pv, pv), pv), :]
        out[pv:, :] = factor[pl.ds(pl.multiple_of(e * pt, pt), pt), :]


def pick_kernel(place, owners, *refs):
    n_phase = len(PHASES)
    held, outs, sems = refs[: -n_phase - 1], refs[-n_phase - 1 : -1], refs[-1]
    inner, outer = place[1], place[2]

    def copy(ref, near, group, phase, slot):
        return pltpu.make_async_copy(ref.at[near], outs[phase].at[slot], sems.at[group])

    for phase, groups in enumerate(PHASES):
        for slot, group in enumerate(groups):
            owner = owners[group]
            far = jnp.bitwise_xor(owner // INNER, outer)
            near = jnp.bitwise_xor(owner % INNER, inner)
            for mask, ref in enumerate(held):

                @pl.when(far == mask)
                def _():
                    copy(ref, near, group, phase, slot).start()

    for phase, groups in enumerate(PHASES):
        for slot, group in enumerate(groups):
            copy(held[0], 0, group, phase, slot).wait()


def merge_kernel(share, place, sub, *refs):
    held, out = refs[:-1], refs[-1]
    inner, outer = place[1], place[2]
    deep, tall = held[0].shape[2], held[0].shape[1]
    out[...] = jnp.zeros_like(out)
    for near, ref in enumerate(held):
        for far in range(ref.shape[0]):
            j = jnp.bitwise_xor(outer, far) * INNER + jnp.bitwise_xor(inner, near)
            high, low = j // share, j % share
            rows = pl.ds(pl.multiple_of(high * tall, tall), tall)
            part = jnp.dot(
                ref[far],
                sub[pl.ds(pl.multiple_of(low * deep, deep), deep), :],
                preferred_element_type=jnp.float32,
            )
            out[rows, :] = out[rows, :] + part


def two_terms(x):
    high = x.astype(jnp.bfloat16)
    low = (x - high.astype(jnp.float32)).astype(jnp.bfloat16)
    return jnp.concatenate([high, low], 0)


def both(products):
    half = products.shape[0] // 2
    return products[:half] + products[half:]


def chain_kernel(groups, masks, first, last, cols, place, offsets, start, *refs):
    held, out, basis_all, factor_all = refs[:-3], refs[-3], refs[-2], refs[-1]
    e = place[0] * INNER + place[1]
    slices = 2 * INNER
    pv, pt = basis_all.shape[1] // slices, factor_all.shape[1] // slices
    for mask, ref in zip(masks, held):
        at = jnp.bitwise_xor(e, mask)
        basis_all[:, pl.ds(pl.multiple_of(at * pv, pv), pv), :] = ref[:, :pv, :]
        factor_all[:, pl.ds(pl.multiple_of(at * pt, pt), pt), :] = ref[:, pv:, :]
    if first:
        pieces = start[...]
        n, each, width = pieces.shape
        pieces = pieces.reshape(n // cols, cols, each, width).sum(0)
        x = jnp.concatenate([pieces[c] for c in range(cols)], 1)
        x = jnp.concatenate([x] + [jnp.zeros_like(x)] * (8 // each - 1), 0)
    else:
        x = start[...]
    wide = x.shape[1]
    group_rows = basis_all.shape[1]
    before = jnp.int32(0)
    for slot, group in enumerate(groups):
        offset = offsets[group]
        x = pltpu.roll(x, lax.rem(before - offset + wide, wide), 1)
        before = offset
        block = x[:, :group_rows]
        weights = both(
            jnp.dot(two_terms(block), basis_all[slot], preferred_element_type=jnp.float32)
        )
        scaled = both(
            lax.dot_general(
                two_terms(weights), factor_all[slot], (((1,), (1,)), ((), ())),
                preferred_element_type=jnp.float32,
            )
        )
        change = both(
            lax.dot_general(
                two_terms(scaled), basis_all[slot], (((1,), (1,)), ((), ())),
                preferred_element_type=jnp.float32,
            )
        )
        x = jnp.concatenate([block - change, x[:, group_rows:]], 1)
    x = pltpu.roll(x, before, 1)
    if last:
        out[...] = x[: out.shape[0]].astype(out.dtype)
    else:
        out[...] = x


def local(rows, cols, sub_vectors, merge_factor, reflectors, wy_factors, owners, offsets):
    outers = cols // INNER
    share = cols // rows
    row, col = lax.axis_index("row"), lax.axis_index("col")
    row_bit, inner, outer = row % 2, col % INNER, col // INNER
    place = jnp.stack([row_bit, inner, outer]).astype(jnp.int32)

    def near(x, mask):
        return lax.ppermute(x, "col", [(c, c ^ mask) for c in range(cols)])

    def far(x, mask):
        return near(x, mask * INNER)

    def across(x):
        return lax.ppermute(x, "row", [(r, r ^ 1) for r in range(rows)])

    basis, factor = reflectors[0], wy_factors[0]
    group_rows, reflect = basis.shape
    pv, pt = group_rows // (2 * INNER), reflect // (2 * INNER)

    pairs = [
        (r * cols + c, (c // share) * cols + share * r + c % share)
        for r in range(rows)
        for c in range(cols)
    ]
    mine = lax.ppermute(merge_factor, ("row", "col"), pairs)
    packed = pl.pallas_call(
        pack_kernel,
        out_shape=[jax.ShapeDtypeStruct((pv + pt, reflect), basis.dtype)] * INNER,
        in_specs=[SMEM, VMEM, VMEM],
        out_specs=[VMEM] * INNER,
        name="pack",
    )(place, basis, factor)
    plane = jnp.stack([packed[0]] + [near(packed[m], m) for m in range(1, INNER)])

    m_outer = jnp.stack([mine] + [far(mine, m) for m in range(1, outers)])
    v_outer = [plane] + [far(plane, m) for m in range(1, outers)]

    m_held = [m_outer, None, near(m_outer, 2), None]
    m_held[1], m_held[3] = near(m_held[0], 1), near(m_held[2], 1)
    wanted = merge_factor.shape[0] * rows
    merged = pl.pallas_call(
        functools.partial(merge_kernel, share),
        out_shape=jax.ShapeDtypeStruct((wanted, sub_vectors.shape[1]), jnp.float32),
        in_specs=[SMEM, VMEM] + [VMEM] * INNER,
        out_specs=VMEM,
        compiler_params=LIMIT,
        name="merge",
    )(place, sub_vectors, *m_held)
    parts = rows * cols
    each = wanted // parts
    state = lax.all_to_all(merged.reshape(parts, each, merged.shape[1]), ("row", "col"), 0, 0)

    picked = pl.pallas_call(
        pick_kernel,
        out_shape=[
            jax.ShapeDtypeStruct((len(groups), pv + pt, reflect), basis.dtype)
            for groups in PHASES
        ],
        in_specs=[SMEM, SMEM] + [ANY] * outers,
        out_specs=[ANY] * len(PHASES),
        scratch_shapes=[pltpu.SemaphoreType.DMA((GROUPS,))],
        name="pick",
    )(place, owners, *v_outer)

    wide = cols * sub_vectors.shape[1]
    for phase, groups in enumerate(PHASES):
        last = phase == len(PHASES) - 1
        own = picked[phase]
        by_row, by_col = across(own), near(own, 2)
        corner = near(by_row, 2) if phase % 2 == 0 else across(by_col)
        held = [own, by_row, by_col, corner]
        masks = [0, INNER, 2, INNER + 2]
        held = held + [near(x, 1) for x in held]
        masks = masks + [m ^ 1 for m in masks]
        state = pl.pallas_call(
            functools.partial(chain_kernel, groups, masks, phase == 0, last, cols),
            out_shape=jax.ShapeDtypeStruct(
                (each, wide) if last else (8, wide), jnp.bfloat16 if last else jnp.float32
            ),
            in_specs=[SMEM, SMEM, VMEM] + [VMEM] * len(held),
            out_specs=VMEM,
            scratch_shapes=[
                pltpu.VMEM((len(groups), group_rows, reflect), basis.dtype),
                pltpu.VMEM((len(groups), reflect, reflect), basis.dtype),
            ],
            compiler_params=LIMIT,
            name=f"chain{phase}",
        )(place, offsets, state, *held)
    return state


def solution(mesh):
    rows, cols = mesh.shape["row"], mesh.shape["col"]
    in_specs = (
        P("row", "col"),
        P("row", "col"),
        P("col", None, None),
        P("col", None, None),
        P(),
        P(),
    )
    out_specs = P(("row", "col"), None)
    return jax.shard_map(
        functools.partial(local, rows, cols),
        mesh=mesh,
        in_specs=in_specs,
        out_specs=out_specs,
        check_vma=False,
    )
```

time: 226 us -> 111 us (0.49)
  waiting for transfers between devices: 166 us -> 38 us
  between operations: 28.6 us -> 0.19 us
  starting transfers between devices: 5.7 us -> 31.3 us
  Pallas kernels: 0 us -> 25.2 us
  matrix products: 16 us -> 0 us
  blocking collectives: 0 us -> 12.6 us
  local copies, waits for them, and re-layouts: 4.43 us -> 1.5 us
  other arithmetic: 4.16 us -> 1.54 us
    psum x1 -> x0, waiting for transfers between devices: 98.2 us -> none  [spread(): return lax.psum(block, axis)]
    all_gather x2 -> x0, waiting for transfers between devices: 66.4 us -> none  [the longest x1 34.2 us: local(): all_sub = lax.all_gather(sub_vectors, 'row', axis=0, tiled=True)]
    ppermute x0 -> x27, waiting for transfers between devices: none -> 38 us  [the longest x23 30.9 us: near(): return lax.ppermute(x, 'col', [(c, c ^ mask) for c in range(cols)])]
    ppermute x0 -> x27, starting transfers between devices: none -> 31.3 us  [the longest x23 26.8 us: near(): return lax.ppermute(x, 'col', [(c, c ^ mask) for c in range(cols)])]
    pallas_call x0 -> x5, Pallas kernels: none -> 25.2 us  [the longest x1 16.7 us: local(): pl.pallas_call(pick_kernel, out_shape=[jax.ShapeDtypeStruct((len(groups),...]
    dot_general x19 -> x0, matrix products: 16 us -> none  [the longest x6 5.67 us: local(): jnp.dot(scaled, basis_full.T, precision=lax.Precision.HIGHEST)]
    all_to_all x0 -> x1, blocking collectives: none -> 12.6 us  [local(): lax.all_to_all(merged.reshape(parts, each, merged.shape[1]), ('row', 'col...]
    all_to_all x1 -> x0, starting transfers between devices: 5.62 us -> none  [local(): lax.all_to_all(merged, 'col', split_axis=0, concat_axis=1, tiled=True)]
  transfers between devices with their start and end apart: 4 -> 27, of which waited for: 3 -> 8; matrix products, arithmetic and copies ran while one was open for 4% -> 1% of each run, Pallas kernels for 0% -> 18%
where the time goes in v2:
time: 111 us; the launch traced here: 110 us
  waiting for transfers between devices  38 us (34%)
  starting transfers between devices  31.3 us (28%)
  Pallas kernels  25.2 us (23%)
  blocking collectives  12.6 us (11%)
  other arithmetic  1.54 us (1%)
  local copies, waits for them, and re-layouts  1.5 us (1%)
    ppermute x23, waiting for transfers between devices, near(): return lax.ppermute(x, 'col', [(c, c ^ mask) for c in range(cols)])  30.9 us
    ppermute x23, starting transfers between devices, near(): return lax.ppermute(x, 'col', [(c, c ^ mask) for c in range(cols)])  26.8 us
    pallas_call x1, Pallas kernels, local(): pl.pallas_call(pick_kernel, out_shape=[jax.ShapeDtypeStruct((len(groups),...  16.7 us
    all_to_all x1, blocking collectives, local(): lax.all_to_all(merged.reshape(parts, each, merged.shape[1]), ('row', 'col...  12.6 us
    ppermute x3, waiting for transfers between devices, across(): return lax.ppermute(x, 'row', [(r, r ^ 1) for r in range(rows)])  7.08 us
    pallas_call x2, Pallas kernels, local(): pl.pallas_call(functools.partial(chain_kernel, groups, masks, phase == 0,...  5.61 us
    ppermute x3, starting transfers between devices, across(): return lax.ppermute(x, 'row', [(r, r ^ 1) for r in range(rows)])  3.84 us
  transfers between devices with their start and end apart: 27, of which 8 were waited for; matrix products, arithmetic and copies ran while one was open for 1% of the time, Pallas kernels for 18%

profile of v2, /device:TPU:0, one launch (start us, length us, event | category | flops | bytes accessed | tf_op | source)
XLA Modules:
  0.0 110.4 jit_solution(15971643158892115502)
XLA Ops:
  0.0 0.6 pad_add_fusion.place
  0.6 1.9 %pack.1 = (bf16[160,256]{1,0:T(8,128)(2,1)}, bf16[160,256]{1,0:T(8,128)(2,1)}, bf16[160,256]{1,0:T(8,128)(2,1)}, bf16[160,256]{1,0:T(8,128)(2,1)}) custom-call(s32[3]{0:T(128)} %pad_add_fusion.place, bf16[1024,256]{1,0:T(8,128)(2,1)} %bitcast.15, bf16[256,256]{1,0:T(8,128)(2,1)} %bitcast.16), custom_call_target="tpu_custom_call" | custom-call | tf_op jit(solution)/shard_map/pack/pallas_call | solution.py:155
  2.4 0.5 collective-permute-start.7
  2.9 2.5 %collective-permute-start.8 = (bf16[160,256]{1,0:T(8,128)(2,1)}, bf16[160,256]{1,0:T(8,128)(2,1)S(1)}, u32[]{:S(2)}, u32[]{:S(2)}) collective-permute-start(bf16[160,256]{1,0:T(8,128)(2,1)} %get-tuple-element.13), channel_id=1, source_target_pairs={{0,2},{1,3},{2,0},{3,1},{4,6},{5,7},{6,4},{7,5},{8,10},{9,11},{10,... | collective-permute-start | bytes 245768 | tf_op jit(solution)/shard_map/ppermute | solution.py:137
  5.4 0.1 collective-permute-start.9
  5.6 0.7 collective-permute-start
  6.2 12.4 %collective-permute-start.3 = (bf16[64,512]{1,0:T(8,128)(2,1)S(1)}, bf16[64,512]{1,0:T(8,128)(2,1)S(1)}, u32[]{:S(2)}, u32[]{:S(2)}) collective-permute-start(bf16[64,512]{1,0:T(8,128)(2,1)S(1)} %collective-permute-done), channel_id=1, source_target_pairs={{0,12},{1,13},{2,14},{3,15},{4,8},{5,9},{6,10},{7,11},{8,4},{9,5},... | collective-permute-start | bytes 196616 | tf_op jit(solution)/shard_map/ppermute | solution.py:137
  18.6 0.0 collective-permute-start.2
  18.6 0.0 collective-permute-done.7
  18.6 0.6 collective-permute-start.1
  19.2 0.0 collective-permute-done.8
  19.2 0.0 collective-permute-done.9
  19.2 0.9 pad_maximum_fusion.refs_0_
  20.1 0.0 copy-start
  20.2 3.9 %collective-permute-start.12 = (bf16[4,160,256]{2,1,0:T(8,128)(2,1)S(1)}, bf16[4,160,256]{2,1,0:T(8,128)(2,1)S(1)}, u32[]{:S(2)}, u32[]{:S(2)}) collective-permute-start(bf16[4,160,256]{2,1,0:T(8,128)(2,1)S(1)} %pad_maximum_fusion.refs_0_), channel_id=1, source_target_pairs={{0,12},{1,13},{2,14},{3,15},{4,8},{5,9},{6,10},{7,11},{8,4},{9,5},... | collective-permute-start | bytes 983048 | tf_op jit(solution)/shard_map/ppermute | solution.py:137
  24.0 0.0 collective-permute-start.11
  24.0 0.0 collective-permute-done.3
  24.0 0.6 collective-permute-start.10
  24.7 0.3 collective-permute-done.2
  25.0 1.6 %collective-permute-start.5 = (bf16[4,64,512]{2,1,0:T(8,128)(2,1)S(1)}, bf16[4,64,512]{2,1,0:T(8,128)(2,1)S(1)}, u32[]{:S(2)}, u32[]{:S(2)}) collective-permute-start(bf16[4,64,512]{2,1,0:T(8,128)(2,1)S(1)} %pad_maximum_fusion.1.refs_0_), channel_id=1, source_target_pairs={{0,2},{1,3},{2,0},{3,1},{4,6},{5,7},{6,4},{7,5},{8,10},{9,11},{10,... | collective-permute-start | bytes 786440 | tf_op jit(solution)/shard_map/ppermute | solution.py:137
  26.6 5.0 %collective-permute-done.5.refs_2_ = bf16[4,64,512]{2,1,0:T(8,128)(2,1)S(1)} collective-permute-done((bf16[4,64,512]{2,1,0:T(8,128)(2,1)S(1)}, bf16[4,64,512]{2,1,0:T(8,128)(2,1)S(1)}, u32[]{:S(2)}, u32[]{:S(2)}) %collective-permute-start.5) | collective-permute-done | bytes 262176 | tf_op jit(solution)/shard_map/ppermute | solution.py:137
  31.7 0.0 collective-permute-start.6
  31.7 1.3 %collective-permute-done.12.refs_3_ = bf16[4,160,256]{2,1,0:T(8,128)(2,1)S(1)} collective-permute-done((bf16[4,160,256]{2,1,0:T(8,128)(2,1)S(1)}, bf16[4,160,256]{2,1,0:T(8,128)(2,1)S(1)}, u32[]{:S(2)}, u32[]{:S(2)}) %collective-permute-start.12) | collective-permute-done | bytes 327712 | tf_op jit(solution)/shard_map/ppermute | solution.py:137
  32.9 18.9 %collective-permute-done.11.refs_2_ = bf16[4,160,256]{2,1,0:T(8,128)(2,1)S(1)} collective-permute-done((bf16[4,160,256]{2,1,0:T(8,128)(2,1)S(1)}, bf16[4,160,256]{2,1,0:T(8,128)(2,1)S(1)}, u32[]{:S(2)}, u32[]{:S(2)}) %collective-permute-start.11) | collective-permute-done | bytes 327712 | tf_op jit(solution)/shard_map/ppermute | solution.py:137
  51.9 0.7 copy-done.7
  52.6 0.7 copy-done.8
  53.4 16.7 %pick.1 = (bf16[3,160,256]{2,1,0:T(8,128)(2,1)}, bf16[3,160,256]{2,1,0:T(8,128)(2,1)}) custom-call(s32[3]{0:T(128)} %pad_add_fusion.place, s32[6]{0:T(128)} %owners.1, bf16[4,160,256]{2,1,0:T(8,128)(2,1)} %copy-done.5, bf16[4,160,256]{2,1,0:T(8,128)(2,1)} %copy-done.8, bf16[4,160,256]{2,1,0:T(8,128)(2,1)} %copy-done.7, bf16[4,160,256]{2,1,0:T(8,128)(2,1)} %copy-done.6), custom_call_target="tpu_custom_call" | custom-call | tf_op jit(solution)/shard_map/pick/pallas_call | solution.py:182
  70.1 0.3 collective-permute-start.13
  70.4 1.5 %collective-permute-start.14 = (bf16[3,160,256]{2,1,0:T(8,128)(2,1)}, bf16[3,160,256]{2,1,0:T(8,128)(2,1)S(1)}, u32[]{:S(2)}, u32[]{:S(2)}) collective-permute-start(bf16[3,160,256]{2,1,0:T(8,128)(2,1)} %get-tuple-element.15.refs_0_), channel_id=1, source_target_pairs={{0,2},{1,3},{2,0},{3,1},{4,6},{5,7},{6,4},{7,5},{8,10},{9,11},{10,... | collective-permute-start | bytes 737288 | tf_op jit(solution)/shard_map/ppermute | solution.py:137
  72.0 0.0 collective-permute-start.16
  72.0 0.0 collective-permute-done.4.refs_1_
  72.0 0.5 collective-permute-start.21
  72.5 0.0 collective-permute-done.6.refs_3_
  72.5 1.7 %collective-permute-start.20 = (bf16[3,160,256]{2,1,0:T(8,128)(2,1)}, bf16[3,160,256]{2,1,0:T(8,128)(2,1)S(1)}, u32[]{:S(2)}, u32[]{:S(2)}) collective-permute-start(bf16[3,160,256]{2,1,0:T(8,128)(2,1)} %get-tuple-element.16.refs_0_), channel_id=1, source_target_pairs={{0,16},{16,0},{1,17},{17,1},{2,18},{18,2},{3,19},{19,3},{4,20},{20... | collective-permute-start | bytes 737288 | tf_op jit(solution)/shard_map/ppermute | solution.py:143
  74.2 5.0 %collective-permute-done.13.refs_1_ = bf16[3,160,256]{2,1,0:T(8,128)(2,1)S(1)} collective-permute-done((bf16[3,160,256]{2,1,0:T(8,128)(2,1)}, bf16[3,160,256]{2,1,0:T(8,128)(2,1)S(1)}, u32[]{:S(2)}, u32[]{:S(2)}) %collective-permute-start.13) | collective-permute-done | bytes 245792 | tf_op jit(solution)/shard_map/ppermute | solution.py:143
  79.3 1.5 %collective-permute-start.15 = (bf16[3,160,256]{2,1,0:T(8,128)(2,1)S(1)}, bf16[3,160,256]{2,1,0:T(8,128)(2,1)S(1)}, u32[]{:S(2)}, u32[]{:S(2)}) collective-permute-start(bf16[3,160,256]{2,1,0:T(8,128)(2,1)S(1)} %collective-permute-done.13.refs_1_), channel_id=1, source_target_pairs={{0,2},{1,3},{2,0},{3,1},{4,6},{5,7},{6,4},{7,5},{8,10},{9,11},{10,... | collective-permute-start | bytes 737288 | tf_op jit(solution)/shard_map/ppermute | solution.py:137
  80.8 0.5 collective-permute-start.17
  81.3 3.5 %collective-permute-done.21.refs_2_ = bf16[3,160,256]{2,1,0:T(8,128)(2,1)S(1)} collective-permute-done((bf16[3,160,256]{2,1,0:T(8,128)(2,1)}, bf16[3,160,256]{2,1,0:T(8,128)(2,1)S(1)}, u32[]{:S(2)}, u32[]{:S(2)}) %collective-permute-start.21) | collective-permute-done | bytes 245792 | tf_op jit(solution)/shard_map/ppermute | solution.py:137
  84.8 1.7 %collective-permute-start.22 = (bf16[3,160,256]{2,1,0:T(8,128)(2,1)S(1)}, bf16[3,160,256]{2,1,0:T(8,128)(2,1)S(1)}, u32[]{:S(2)}, u32[]{:S(2)}) collective-permute-start(bf16[3,160,256]{2,1,0:T(8,128)(2,1)S(1)} %collective-permute-done.21.refs_2_), channel_id=1, source_target_pairs={{0,16},{16,0},{1,17},{17,1},{2,18},{18,2},{3,19},{19,3},{4,20},{20... | collective-permute-start | bytes 737288 | tf_op jit(solution)/shard_map/ppermute | solution.py:143
  86.6 1.8 %collective-permute-done.15.refs_3_ = bf16[3,160,256]{2,1,0:T(8,128)(2,1)S(1)} collective-permute-done((bf16[3,160,256]{2,1,0:T(8,128)(2,1)S(1)}, bf16[3,160,256]{2,1,0:T(8,128)(2,1)S(1)}, u32[]{:S(2)}, u32[]{:S(2)}) %collective-permute-start.15) | collective-permute-done | bytes 245792 | tf_op jit(solution)/shard_map/ppermute | solution.py:137
  88.4 0.5 collective-permute-start.25
  88.9 0.1 collective-permute-start.24
  89.0 2.0 %collective-permute-done.22.refs_3_ = bf16[3,160,256]{2,1,0:T(8,128)(2,1)S(1)} collective-permute-done((bf16[3,160,256]{2,1,0:T(8,128)(2,1)S(1)}, bf16[3,160,256]{2,1,0:T(8,128)(2,1)S(1)}, u32[]{:S(2)}, u32[]{:S(2)}) %collective-permute-start.22) | collective-permute-done | bytes 245792 | tf_op jit(solution)/shard_map/ppermute | solution.py:143
  91.0 1.0 merge.1
  92.1 0.0 copy-start.4
  92.1 12.6 %all_to_all.5.start = f32[32,4,128]{2,1,0:T(4,128)S(1)} all-to-all(f32[32,4,128]{2,1,0:T(4,128)S(1)} %bitcast.14), channel_id=1, replica_groups=mesh['row'=2,'col'=16] {'row','col'}, dimensions={0} | all-to-all | bytes 131072 | tf_op jit(solution)/shard_map/all_to_all | solution.py:180
  104.7 2.5 %chain0.1.start = f32[8,2048]{1,0:T(8,128)S(1)} custom-call(s32[3]{0:T(128)S(1)} %copy-done.3, s32[6]{0:T(128)S(1)} %copy-done.4, f32[32,4,128]{2,1,0:T(4,128)S(1)} %all_to_all.5.start, bf16[3,160,256]{2,1,0:T(8,128)(2,1)S(1)} %copy-done.2, bf16[3,160,256]{2,1,0:T(8,128)(2,1)S(1)} %collective-permute-done.13.refs_1_, ...), custom_call_target="tpu_custom_call" | custom-call | tf_op jit(solution)/shard_map/chain0/pallas_call | solution.py:204
  107.3 3.1 %chain1.1 = bf16[4,2048]{1,0:T(4,128)(2,1)} custom-call(s32[3]{0:T(128)S(1)} %copy-done.3, s32[6]{0:T(128)S(1)} %copy-done.4, f32[8,2048]{1,0:T(8,128)S(1)} %chain0.1.start, bf16[3,160,256]{2,1,0:T(8,128)(2,1)S(1)} %copy-done.1, bf16[3,160,256]{2,1,0:T(8,128)(2,1)S(1)} %collective-permute-done.20.refs_1_, ...), custom_call_target="tpu_custom_call" | custom-call | tf_op jit(solution)/shard_map/chain1/pallas_call | solution.py:204
  (35 shorter events, 0.1 us)
Async XLA Ops:
  0.6 5.0 %copy-start.9 = (bf16[64,512]{1,0:T(8,128)(2,1)S(1)}, bf16[64,512]{1,0:T(8,128)(2,1)}, u32[]{:S(2)}) copy-start(bf16[64,512]{1,0:T(8,128)(2,1)} %param.7) | copy-start | bytes 196612
  2.4 16.2 %collective-permute-start.7 = (bf16[160,256]{1,0:T(8,128)(2,1)}, bf16[160,256]{1,0:T(8,128)(2,1)S(1)}, u32[]{:S(2)}, u32[]{:S(2)}) collective-permute-start(bf16[160,256]{1,0:T(8,128)(2,1)} %get-tuple-element.12), channel_id=1, source_target_pairs={{0,1},{1,0},{2,3},{3,2},{4,5},{5,4},{6,7},{7,6},{8,9},{9,8},{10,11... | collective-permute-start | bytes 245768 | tf_op jit(solution)/shard_map/ppermute | solution.py:137
  2.9 16.3 %collective-permute-start.8 = (bf16[160,256]{1,0:T(8,128)(2,1)}, bf16[160,256]{1,0:T(8,128)(2,1)S(1)}, u32[]{:S(2)}, u32[]{:S(2)}) collective-permute-start(bf16[160,256]{1,0:T(8,128)(2,1)} %get-tuple-element.13), channel_id=1, source_target_pairs={{0,2},{1,3},{2,0},{3,1},{4,6},{5,7},{6,4},{7,5},{8,10},{9,11},{10,... | collective-permute-start | bytes 245768 | tf_op jit(solution)/shard_map/ppermute | solution.py:137
  5.4 13.8 %collective-permute-start.9 = (bf16[160,256]{1,0:T(8,128)(2,1)}, bf16[160,256]{1,0:T(8,128)(2,1)S(1)}, u32[]{:S(2)}, u32[]{:S(2)}) collective-permute-start(bf16[160,256]{1,0:T(8,128)(2,1)} %get-tuple-element.14), channel_id=1, source_target_pairs={{0,3},{1,2},{2,1},{3,0},{4,7},{5,6},{6,5},{7,4},{8,11},{9,10},{10,... | collective-permute-start | bytes 245768 | tf_op jit(solution)/shard_map/ppermute | solution.py:137
  5.6 0.7 collective-permute-start
  6.2 17.8 %collective-permute-start.3 = (bf16[64,512]{1,0:T(8,128)(2,1)S(1)}, bf16[64,512]{1,0:T(8,128)(2,1)S(1)}, u32[]{:S(2)}, u32[]{:S(2)}) collective-permute-start(bf16[64,512]{1,0:T(8,128)(2,1)S(1)} %collective-permute-done), channel_id=1, source_target_pairs={{0,12},{1,13},{2,14},{3,15},{4,8},{5,9},{6,10},{7,11},{8,4},{9,5},... | collective-permute-start | bytes 196616 | tf_op jit(solution)/shard_map/ppermute | solution.py:137
  18.6 6.4 %collective-permute-start.2 = (bf16[64,512]{1,0:T(8,128)(2,1)S(1)}, bf16[64,512]{1,0:T(8,128)(2,1)S(1)}, u32[]{:S(2)}, u32[]{:S(2)}) collective-permute-start(bf16[64,512]{1,0:T(8,128)(2,1)S(1)} %collective-permute-done), channel_id=1, source_target_pairs={{0,8},{1,9},{2,10},{3,11},{4,12},{5,13},{6,14},{7,15},{8,0},{9,1},... | collective-permute-start | bytes 196616 | tf_op jit(solution)/shard_map/ppermute | solution.py:137
  18.6 6.4 %collective-permute-start.1 = (bf16[64,512]{1,0:T(8,128)(2,1)S(1)}, bf16[64,512]{1,0:T(8,128)(2,1)S(1)}, u32[]{:S(2)}, u32[]{:S(2)}) collective-permute-start(bf16[64,512]{1,0:T(8,128)(2,1)S(1)} %collective-permute-done), channel_id=1, source_target_pairs={{0,4},{1,5},{2,6},{3,7},{4,0},{5,1},{6,2},{7,3},{8,12},{9,13},{10,... | collective-permute-start | bytes 196616 | tf_op jit(solution)/shard_map/ppermute | solution.py:137
  20.1 31.7 %copy-start.5 = (bf16[4,160,256]{2,1,0:T(8,128)(2,1)}, bf16[4,160,256]{2,1,0:T(8,128)(2,1)S(1)}, u32[]{:S(2)}) copy-start(bf16[4,160,256]{2,1,0:T(8,128)(2,1)S(1)} %pad_maximum_fusion.refs_0_) | copy-start | bytes 983044
  20.1 70.9 %copy-start = (bf16[4096,128]{1,0:T(8,128)(2,1)S(1)}, bf16[4096,128]{1,0:T(8,128)(2,1)}, u32[]{:S(2)}) copy-start(bf16[4096,128]{1,0:T(8,128)(2,1)} %sub.6) | copy-start | bytes 3145732
  20.2 12.8 %collective-permute-start.12 = (bf16[4,160,256]{2,1,0:T(8,128)(2,1)S(1)}, bf16[4,160,256]{2,1,0:T(8,128)(2,1)S(1)}, u32[]{:S(2)}, u32[]{:S(2)}) collective-permute-start(bf16[4,160,256]{2,1,0:T(8,128)(2,1)S(1)} %pad_maximum_fusion.refs_0_), channel_id=1, source_target_pairs={{0,12},{1,13},{2,14},{3,15},{4,8},{5,9},{6,10},{7,11},{8,4},{9,5},... | collective-permute-start | bytes 983048 | tf_op jit(solution)/shard_map/ppermute | solution.py:137
  24.0 27.8 %collective-permute-start.11 = (bf16[4,160,256]{2,1,0:T(8,128)(2,1)S(1)}, bf16[4,160,256]{2,1,0:T(8,128)(2,1)S(1)}, u32[]{:S(2)}, u32[]{:S(2)}) collective-permute-start(bf16[4,160,256]{2,1,0:T(8,128)(2,1)S(1)} %pad_maximum_fusion.refs_0_), channel_id=1, source_target_pairs={{0,8},{1,9},{2,10},{3,11},{4,12},{5,13},{6,14},{7,15},{8,0},{9,1},... | collective-permute-start | bytes 983048 | tf_op jit(solution)/shard_map/ppermute | solution.py:137
  24.0 27.8 %collective-permute-start.10 = (bf16[4,160,256]{2,1,0:T(8,128)(2,1)S(1)}, bf16[4,160,256]{2,1,0:T(8,128)(2,1)S(1)}, u32[]{:S(2)}, u32[]{:S(2)}) collective-permute-start(bf16[4,160,256]{2,1,0:T(8,128)(2,1)S(1)} %pad_maximum_fusion.refs_0_), channel_id=1, source_target_pairs={{0,4},{1,5},{2,6},{3,7},{4,0},{5,1},{6,2},{7,3},{8,12},{9,13},{10,... | collective-permute-start | bytes 983048 | tf_op jit(solution)/shard_map/ppermute | solution.py:137
  25.0 6.6 %collective-permute-start.5 = (bf16[4,64,512]{2,1,0:T(8,128)(2,1)S(1)}, bf16[4,64,512]{2,1,0:T(8,128)(2,1)S(1)}, u32[]{:S(2)}, u32[]{:S(2)}) collective-permute-start(bf16[4,64,512]{2,1,0:T(8,128)(2,1)S(1)} %pad_maximum_fusion.1.refs_0_), channel_id=1, source_target_pairs={{0,2},{1,3},{2,0},{3,1},{4,6},{5,7},{6,4},{7,5},{8,10},{9,11},{10,... | collective-permute-start | bytes 786440 | tf_op jit(solution)/shard_map/ppermute | solution.py:137
  26.6 45.4 %collective-permute-start.4 = (bf16[4,64,512]{2,1,0:T(8,128)(2,1)S(1)}, bf16[4,64,512]{2,1,0:T(8,128)(2,1)S(1)}, u32[]{:S(2)}, u32[]{:S(2)}) collective-permute-start(bf16[4,64,512]{2,1,0:T(8,128)(2,1)S(1)} %pad_maximum_fusion.1.refs_0_), channel_id=1, source_target_pairs={{0,1},{1,0},{2,3},{3,2},{4,5},{5,4},{6,7},{7,6},{8,9},{9,8},{10,11... | collective-permute-start | bytes 786440 | tf_op jit(solution)/shard_map/ppermute | solution.py:137
  31.7 40.8 %collective-permute-start.6 = (bf16[4,64,512]{2,1,0:T(8,128)(2,1)S(1)}, bf16[4,64,512]{2,1,0:T(8,128)(2,1)S(1)}, u32[]{:S(2)}, u32[]{:S(2)}) collective-permute-start(bf16[4,64,512]{2,1,0:T(8,128)(2,1)S(1)} %collective-permute-done.5.refs_2_), channel_id=1, source_target_pairs={{0,1},{1,0},{2,3},{3,2},{4,5},{5,4},{6,7},{7,6},{8,9},{9,8},{10,11... | collective-permute-start | bytes 786440 | tf_op jit(solution)/shard_map/ppermute | solution.py:137
  32.9 18.9 %copy-start.6 = (bf16[4,160,256]{2,1,0:T(8,128)(2,1)}, bf16[4,160,256]{2,1,0:T(8,128)(2,1)S(1)}, u32[]{:S(2)}) copy-start(bf16[4,160,256]{2,1,0:T(8,128)(2,1)S(1)} %collective-permute-done.12.refs_3_) | copy-start | bytes 983044
  51.9 0.7 copy-start.7
  52.6 0.7 copy-start.8
  70.1 20.9 %copy-start.3 = (s32[3]{0:T(128)S(1)}, s32[3]{0:T(128)}, u32[]{:S(2)}) copy-start(s32[3]{0:T(128)} %pad_add_fusion.place) | copy-start | bytes 40
  70.1 9.2 %collective-permute-start.13 = (bf16[3,160,256]{2,1,0:T(8,128)(2,1)}, bf16[3,160,256]{2,1,0:T(8,128)(2,1)S(1)}, u32[]{:S(2)}, u32[]{:S(2)}) collective-permute-start(bf16[3,160,256]{2,1,0:T(8,128)(2,1)} %get-tuple-element.15.refs_0_), channel_id=1, source_target_pairs={{0,16},{16,0},{1,17},{17,1},{2,18},{18,2},{3,19},{19,3},{4,20},{20... | collective-permute-start | bytes 737288 | tf_op jit(solution)/shard_map/ppermute | solution.py:143
  70.4 10.3 %collective-permute-start.14 = (bf16[3,160,256]{2,1,0:T(8,128)(2,1)}, bf16[3,160,256]{2,1,0:T(8,128)(2,1)S(1)}, u32[]{:S(2)}, u32[]{:S(2)}) collective-permute-start(bf16[3,160,256]{2,1,0:T(8,128)(2,1)} %get-tuple-element.15.refs_0_), channel_id=1, source_target_pairs={{0,2},{1,3},{2,0},{3,1},{4,6},{5,7},{6,4},{7,5},{8,10},{9,11},{10,... | collective-permute-start | bytes 737288 | tf_op jit(solution)/shard_map/ppermute | solution.py:137
  72.0 8.8 %collective-permute-start.16 = (bf16[3,160,256]{2,1,0:T(8,128)(2,1)}, bf16[3,160,256]{2,1,0:T(8,128)(2,1)S(1)}, u32[]{:S(2)}, u32[]{:S(2)}) collective-permute-start(bf16[3,160,256]{2,1,0:T(8,128)(2,1)} %get-tuple-element.15.refs_0_), channel_id=1, source_target_pairs={{0,1},{1,0},{2,3},{3,2},{4,5},{5,4},{6,7},{7,6},{8,9},{9,8},{10,11... | collective-permute-start | bytes 737288 | tf_op jit(solution)/shard_map/ppermute | solution.py:137
  72.0 12.8 %collective-permute-start.21 = (bf16[3,160,256]{2,1,0:T(8,128)(2,1)}, bf16[3,160,256]{2,1,0:T(8,128)(2,1)S(1)}, u32[]{:S(2)}, u32[]{:S(2)}) collective-permute-start(bf16[3,160,256]{2,1,0:T(8,128)(2,1)} %get-tuple-element.16.refs_0_), channel_id=1, source_target_pairs={{0,2},{1,3},{2,0},{3,1},{4,6},{5,7},{6,4},{7,5},{8,10},{9,11},{10,... | collective-permute-start | bytes 737288 | tf_op jit(solution)/shard_map/ppermute | solution.py:137
  72.5 14.1 %collective-permute-start.20 = (bf16[3,160,256]{2,1,0:T(8,128)(2,1)}, bf16[3,160,256]{2,1,0:T(8,128)(2,1)S(1)}, u32[]{:S(2)}, u32[]{:S(2)}) collective-permute-start(bf16[3,160,256]{2,1,0:T(8,128)(2,1)} %get-tuple-element.16.refs_0_), channel_id=1, source_target_pairs={{0,16},{16,0},{1,17},{17,1},{2,18},{18,2},{3,19},{19,3},{4,20},{20... | collective-permute-start | bytes 737288 | tf_op jit(solution)/shard_map/ppermute | solution.py:143
  79.3 9.1 %collective-permute-start.15 = (bf16[3,160,256]{2,1,0:T(8,128)(2,1)S(1)}, bf16[3,160,256]{2,1,0:T(8,128)(2,1)S(1)}, u32[]{:S(2)}, u32[]{:S(2)}) collective-permute-start(bf16[3,160,256]{2,1,0:T(8,128)(2,1)S(1)} %collective-permute-done.13.refs_1_), channel_id=1, source_target_pairs={{0,2},{1,3},{2,0},{3,1},{4,6},{5,7},{6,4},{7,5},{8,10},{9,11},{10,... | collective-permute-start | bytes 737288 | tf_op jit(solution)/shard_map/ppermute | solution.py:137
  80.8 7.6 %collective-permute-start.18 = (bf16[3,160,256]{2,1,0:T(8,128)(2,1)S(1)}, bf16[3,160,256]{2,1,0:T(8,128)(2,1)S(1)}, u32[]{:S(2)}, u32[]{:S(2)}) collective-permute-start(bf16[3,160,256]{2,1,0:T(8,128)(2,1)S(1)} %collective-permute-done.14.refs_2_), channel_id=1, source_target_pairs={{0,1},{1,0},{2,3},{3,2},{4,5},{5,4},{6,7},{7,6},{8,9},{9,8},{10,11... | collective-permute-start | bytes 737288 | tf_op jit(solution)/shard_map/ppermute | solution.py:137
  80.8 8.1 %collective-permute-start.17 = (bf16[3,160,256]{2,1,0:T(8,128)(2,1)S(1)}, bf16[3,160,256]{2,1,0:T(8,128)(2,1)S(1)}, u32[]{:S(2)}, u32[]{:S(2)}) collective-permute-start(bf16[3,160,256]{2,1,0:T(8,128)(2,1)S(1)} %collective-permute-done.13.refs_1_), channel_id=1, source_target_pairs={{0,1},{1,0},{2,3},{3,2},{4,5},{5,4},{6,7},{7,6},{8,9},{9,8},{10,11... | collective-permute-start | bytes 737288 | tf_op jit(solution)/shard_map/ppermute | solution.py:137
  84.8 6.2 %collective-permute-start.22 = (bf16[3,160,256]{2,1,0:T(8,128)(2,1)S(1)}, bf16[3,160,256]{2,1,0:T(8,128)(2,1)S(1)}, u32[]{:S(2)}, u32[]{:S(2)}) collective-permute-start(bf16[3,160,256]{2,1,0:T(8,128)(2,1)S(1)} %collective-permute-done.21.refs_2_), channel_id=1, source_target_pairs={{0,16},{16,0},{1,17},{17,1},{2,18},{18,2},{3,19},{19,3},{4,20},{20... | collective-permute-start | bytes 737288 | tf_op jit(solution)/shard_map/ppermute | solution.py:143
  86.6 20.7 %collective-permute-start.23 = (bf16[3,160,256]{2,1,0:T(8,128)(2,1)}, bf16[3,160,256]{2,1,0:T(8,128)(2,1)S(1)}, u32[]{:S(2)}, u32[]{:S(2)}) collective-permute-start(bf16[3,160,256]{2,1,0:T(8,128)(2,1)} %get-tuple-element.16.refs_0_), channel_id=1, source_target_pairs={{0,1},{1,0},{2,3},{3,2},{4,5},{5,4},{6,7},{7,6},{8,9},{9,8},{10,11... | collective-permute-start | bytes 737288 | tf_op jit(solution)/shard_map/ppermute | solution.py:137
  88.4 16.3 %collective-permute-start.19 = (bf16[3,160,256]{2,1,0:T(8,128)(2,1)S(1)}, bf16[3,160,256]{2,1,0:T(8,128)(2,1)S(1)}, u32[]{:S(2)}, u32[]{:S(2)}) collective-permute-start(bf16[3,160,256]{2,1,0:T(8,128)(2,1)S(1)} %collective-permute-done.15.refs_3_), channel_id=1, source_target_pairs={{0,1},{1,0},{2,3},{3,2},{4,5},{5,4},{6,7},{7,6},{8,9},{9,8},{10,11... | collective-permute-start | bytes 737288 | tf_op jit(solution)/shard_map/ppermute | solution.py:137
  88.4 18.9 %collective-permute-start.25 = (bf16[3,160,256]{2,1,0:T(8,128)(2,1)S(1)}, bf16[3,160,256]{2,1,0:T(8,128)(2,1)S(1)}, u32[]{:S(2)}, u32[]{:S(2)}) collective-permute-start(bf16[3,160,256]{2,1,0:T(8,128)(2,1)S(1)} %collective-permute-done.21.refs_2_), channel_id=1, source_target_pairs={{0,1},{1,0},{2,3},{3,2},{4,5},{5,4},{6,7},{7,6},{8,9},{9,8},{10,11... | collective-permute-start | bytes 737288 | tf_op jit(solution)/shard_map/ppermute | solution.py:137
  88.9 18.4 %collective-permute-start.24 = (bf16[3,160,256]{2,1,0:T(8,128)(2,1)S(1)}, bf16[3,160,256]{2,1,0:T(8,128)(2,1)S(1)}, u32[]{:S(2)}, u32[]{:S(2)}) collective-permute-start(bf16[3,160,256]{2,1,0:T(8,128)(2,1)S(1)} %collective-permute-done.20.refs_1_), channel_id=1, source_target_pairs={{0,1},{1,0},{2,3},{3,2},{4,5},{5,4},{6,7},{7,6},{8,9},{9,8},{10,11... | collective-permute-start | bytes 737288 | tf_op jit(solution)/shard_map/ppermute | solution.py:137
  91.0 16.2 %collective-permute-start.26 = (bf16[3,160,256]{2,1,0:T(8,128)(2,1)S(1)}, bf16[3,160,256]{2,1,0:T(8,128)(2,1)S(1)}, u32[]{:S(2)}, u32[]{:S(2)}) collective-permute-start(bf16[3,160,256]{2,1,0:T(8,128)(2,1)S(1)} %collective-permute-done.22.refs_3_), channel_id=1, source_target_pairs={{0,1},{1,0},{2,3},{3,2},{4,5},{5,4},{6,7},{7,6},{8,9},{9,8},{10,11... | collective-permute-start | bytes 737288 | tf_op jit(solution)/shard_map/ppermute | solution.py:137
  91.0 13.7 %copy-start.2 = (bf16[3,160,256]{2,1,0:T(8,128)(2,1)S(1)}, bf16[3,160,256]{2,1,0:T(8,128)(2,1)}, u32[]{:S(2)}) copy-start(bf16[3,160,256]{2,1,0:T(8,128)(2,1)} %get-tuple-element.15.refs_0_) | copy-start | bytes 737284
  92.1 12.6 %copy-start.4 = (s32[6]{0:T(128)S(1)}, s32[6]{0:T(128)}, u32[]{:S(2)}) copy-start(s32[6]{0:T(128)} %offsets.3) | copy-start | bytes 76
  104.7 2.6 %copy-start.1 = (bf16[3,160,256]{2,1,0:T(8,128)(2,1)S(1)}, bf16[3,160,256]{2,1,0:T(8,128)(2,1)}, u32[]{:S(2)}) copy-start(bf16[3,160,256]{2,1,0:T(8,128)(2,1)} %get-tuple-element.16.refs_0_) | copy-start | bytes 737284

commit v3 on v2

v3 whole, which is shorter than its diff:
```python
import functools

import jax
import jax.numpy as jnp
from jax import lax
from jax.experimental import pallas as pl
from jax.experimental.pallas import tpu as pltpu
from jax.sharding import PartitionSpec as P

GROUPS = 6
PHASES = ((0, 1, 2), (3, 4, 5))
NEAR = 4
FAR = 4
SLICES = 2 * NEAR * FAR
LANES = 128
VMEM = pl.BlockSpec(memory_space=pltpu.VMEM)
SMEM = pl.BlockSpec(memory_space=pltpu.SMEM)
ANY = pl.BlockSpec(memory_space=pl.ANY)
LIMIT = pltpu.CompilerParams(vmem_limit_bytes=40 * 1024 * 1024)


def slice_index():
    row, col = lax.axis_index("row"), lax.axis_index("col")
    return lax.rem(row, 2) * (NEAR * FAR) + lax.rem(col, NEAR * FAR)


def aligned(index, size):
    return pl.ds(pl.multiple_of(index * size, size), size)


def pack_kernel(basis_hbm, factor_hbm, *refs):
    outs, (basis, factor, sems) = refs[:-3], refs[-3:]
    half = basis.shape[0]
    row_bit = lax.rem(lax.axis_index("row"), 2)
    first = pltpu.make_async_copy(basis_hbm.at[aligned(row_bit, half)], basis, sems.at[0])
    second = pltpu.make_async_copy(factor_hbm, factor, sems.at[1])
    first.start()
    second.start()
    first.wait()
    second.wait()
    mine = slice_index()
    pv = half // (NEAR * FAR)
    lanes = basis.shape[1] // LANES
    tall = factor.shape[0] * lanes // SLICES
    for mask, out in enumerate(outs):
        e = jnp.bitwise_xor(mine, mask)
        rows = aligned(lax.rem(e, NEAR * FAR), pv)
        for k in range(lanes):
            out[k * pv : (k + 1) * pv, :] = basis[rows, k * LANES : (k + 1) * LANES]
        out[lanes * pv :, :] = factor[aligned(e // lanes, tall), aligned(lax.rem(e, lanes), LANES)]


def pick_kernel(owners, *refs):
    held, outs = refs[: -len(PHASES)], refs[-len(PHASES) :]
    col = lax.axis_index("col")
    for phase, groups in enumerate(PHASES):
        for slot, group in enumerate(groups):
            want = jnp.bitwise_xor(owners[group], col)
            piece = held[0][...]
            for mask in range(1, len(held)):
                piece = jnp.where(want == mask, held[mask][...], piece)
            outs[phase][slot] = piece


def merge_kernel(rows, cols, sub, *refs):
    held, outs, total = refs[:NEAR], refs[NEAR:-1], refs[-1]
    row, col = lax.axis_index("row"), lax.axis_index("col")
    share = cols // rows
    deep, tall = held[0].shape[2], held[0].shape[1]
    total[...] = jnp.zeros_like(total)
    for near, ref in enumerate(held):
        for far in range(ref.shape[0]):
            j = jnp.bitwise_xor(col, far * NEAR + near)
            part = jnp.dot(
                ref[far], sub[aligned(lax.rem(j, share), deep), :],
                preferred_element_type=jnp.float32,
            )
            at = aligned(j // share, tall)
            total[at, :] = total[at, :] + part
    each = outs[0].shape[1]
    for row_mask, out in enumerate(outs):
        for col_mask in range(cols):
            to = jnp.bitwise_xor(row, row_mask) * cols + jnp.bitwise_xor(col, col_mask)
            out[col_mask] = total[pl.ds(to * each, each), :]


def add_kernel(*refs):
    count = refs[0].shape[0]
    held, outs = refs[:-count], refs[-count:]
    for mask, out in enumerate(outs):
        piece = held[0][mask]
        for ref in held[1:]:
            piece = piece + ref[mask]
        out[...] = piece


def two_terms(x):
    high = x.astype(jnp.bfloat16)
    low = (x - high.astype(jnp.float32)).astype(jnp.bfloat16)
    return jnp.concatenate([high, low], 0)


def both(products):
    half = products.shape[0] // 2
    return products[:half] + products[half:]


def chain_kernel(groups, masks, first, last, offsets, *refs):
    n_state = len(refs) - len(masks) - (4 if first else 3)
    starts, held = refs[:n_state], refs[n_state : n_state + len(masks)]
    out, basis_all, factor_all = refs[n_state + len(masks) :][:3]
    mine = slice_index()
    lanes = basis_all.shape[2] // LANES
    pv = basis_all.shape[1] // SLICES
    tall = factor_all.shape[1] * lanes // SLICES
    for mask, ref in zip(masks, held):
        for far in range(FAR):
            e = jnp.bitwise_xor(mine, mask + far * NEAR)
            for k in range(lanes):
                basis_all[:, aligned(e, pv), k * LANES : (k + 1) * LANES] = ref[
                    far, :, k * pv : (k + 1) * pv, :
                ]
            factor_all[:, aligned(e // lanes, tall), aligned(lax.rem(e, lanes), LANES)] = ref[
                far, :, lanes * pv :, :
            ]
    if first:
        state = refs[-1]
        state[...] = jnp.zeros_like(state)
        col = lax.axis_index("col")
        for mask, ref in enumerate(starts):
            state[jnp.bitwise_xor(col, mask), : ref.shape[0], :] = ref[...]
        x = jnp.concatenate([state[c] for c in range(state.shape[0])], 1)
    else:
        x = starts[0][...]
    wide = x.shape[1]
    group_rows = basis_all.shape[1]
    before = jnp.int32(0)
    for slot, group in enumerate(groups):
        offset = offsets[group]
        x = pltpu.roll(x, lax.rem(before - offset + wide, wide), 1)
        before = offset
        block = x[:, :group_rows]
        weights = both(
            jnp.dot(two_terms(block), basis_all[slot], preferred_element_type=jnp.float32)
        )
        scaled = both(
            lax.dot_general(
                two_terms(weights), factor_all[slot], (((1,), (1,)), ((), ())),
                preferred_element_type=jnp.float32,
            )
        )
        change = both(
            lax.dot_general(
                two_terms(scaled), basis_all[slot], (((1,), (1,)), ((), ())),
                preferred_element_type=jnp.float32,
            )
        )
        x = jnp.concatenate([block - change, x[:, group_rows:]], 1)
    x = pltpu.roll(x, before, 1)
    if last:
        out[...] = x[: out.shape[0]].astype(out.dtype)
    else:
        out[...] = x


def local(rows, cols, sub_vectors, merge_factor, reflectors, wy_factors, owners, offsets):
    share = cols // rows

    def over_col(x, mask):
        return lax.ppermute(x, "col", [(c, c ^ mask) for c in range(cols)])

    def over_row(x, mask):
        return lax.ppermute(x, "row", [(r, r ^ mask) for r in range(rows)])

    basis, factor = reflectors[0], wy_factors[0]
    group_rows, reflect = basis.shape
    dtype = basis.dtype
    lanes = reflect // LANES
    tall = (group_rows + reflect) * lanes // SLICES

    pairs = [
        (r * cols + c, (c // share) * cols + share * r + c % share)
        for r in range(rows)
        for c in range(cols)
    ]
    mine = lax.ppermute(merge_factor, ("row", "col"), pairs)

    packed = pl.pallas_call(
        pack_kernel,
        out_shape=[jax.ShapeDtypeStruct((tall, LANES), dtype)] * (NEAR * FAR),
        in_specs=[ANY, ANY],
        out_specs=[VMEM] * (NEAR * FAR),
        scratch_shapes=[
            pltpu.VMEM((group_rows // 2, reflect), dtype),
            pltpu.VMEM(factor.shape, dtype),
            pltpu.SemaphoreType.DMA((2,)),
        ],
        name="pack",
    )(basis, factor)
    slices = [packed[0]] + [over_col(packed[m % (NEAR * FAR)], m) for m in range(1, cols)]

    m_far = jnp.stack([mine] + [over_col(mine, m) for m in range(NEAR, cols, NEAR)])
    m_two = over_col(m_far, 2)
    m_held = [m_far, over_col(m_far, 1), m_two, over_col(m_two, 1)]
    wanted, width = merge_factor.shape[0] * rows, sub_vectors.shape[1]
    each = wanted // (rows * cols)
    parts = pl.pallas_call(
        functools.partial(merge_kernel, rows, cols),
        out_shape=[jax.ShapeDtypeStruct((cols, each, width), jnp.float32)] * rows,
        in_specs=[VMEM] + [VMEM] * NEAR,
        out_specs=[VMEM] * rows,
        scratch_shapes=[pltpu.VMEM((wanted, width), jnp.float32)],
        compiler_params=LIMIT,
        name="merge",
    )(sub_vectors, *m_held)
    parts = [parts[0]] + [over_row(parts[m], m) for m in range(1, rows)]
    pieces = pl.pallas_call(
        add_kernel,
        out_shape=[jax.ShapeDtypeStruct((each, width), jnp.float32)] * cols,
        in_specs=[VMEM] * rows,
        out_specs=[VMEM] * cols,
        name="add",
    )(*parts)
    state = [pieces[0]] + [over_col(pieces[m], m) for m in range(1, cols)]

    picked = pl.pallas_call(
        pick_kernel,
        out_shape=[
            jax.ShapeDtypeStruct((len(groups), tall, LANES), dtype) for groups in PHASES
        ],
        in_specs=[SMEM] + [VMEM] * cols,
        out_specs=[VMEM] * len(PHASES),
        name="pick",
    )(owners, *slices)

    wide = cols * width
    for phase, groups in enumerate(PHASES):
        first, last = phase == 0, phase == len(PHASES) - 1
        own = picked[phase]
        own = jnp.stack([own] + [over_col(own, m * NEAR) for m in range(1, FAR)])
        by_row, by_col = over_row(own, 1), over_col(own, 2)
        corner = over_col(by_row, 2) if phase % 2 == 0 else over_row(by_col, 1)
        held = [own, by_row, by_col, corner]
        masks = [0, NEAR * FAR, 2, NEAR * FAR + 2]
        held = held + [over_col(x, 1) for x in held]
        masks = masks + [m + 1 for m in masks]
        out = pl.pallas_call(
            functools.partial(chain_kernel, groups, masks, first, last),
            out_shape=jax.ShapeDtypeStruct(
                (each, wide) if last else (8, wide), jnp.bfloat16 if last else jnp.float32
            ),
            in_specs=[SMEM] + [VMEM] * (len(state) + len(held)),
            out_specs=VMEM,
            scratch_shapes=[
                pltpu.VMEM((len(groups), group_rows, reflect), dtype),
                pltpu.VMEM((len(groups), reflect, reflect), dtype),
            ]
            + ([pltpu.VMEM((cols, 8, width), jnp.float32)] if first else []),
            compiler_params=LIMIT,
            name=f"chain{phase}",
        )(offsets, *state, *held)
        state = [out]
    return out


def solution(mesh):
    rows, cols = mesh.shape["row"], mesh.shape["col"]
    in_specs = (
        P("row", "col"),
        P("row", "col"),
        P("col", None, None),
        P("col", None, None),
        P(),
        P(),
    )
    out_specs = P(("row", "col"), None)
    return jax.shard_map(
        functools.partial(local, rows, cols),
        mesh=mesh,
        in_specs=in_specs,
        out_specs=out_specs,
        check_vma=False,
    )
```

time: 111 us -> 112 us (level)
  starting transfers between devices: 31.3 us -> 74.1 us
  waiting for transfers between devices: 38 us -> 23.4 us
  Pallas kernels: 25.2 us -> 11.8 us
  blocking collectives: 12.6 us -> 0 us
    ppermute x26 -> x57, starting transfers between devices: 30.7 us -> 72.6 us  [the longest x53 69.8 us: over_col(): return lax.ppermute(x, 'col', [(c, c ^ mask) for c in range(cols)])]
    pallas_call x1, Pallas kernels: 16.7 us -> 1.77 us  [local(): pl.pallas_call(pick_kernel, out_shape=[jax.ShapeDtypeStruct((len(groups),...]
    ppermute x26 -> x57, waiting for transfers between devices: 38 us -> 23.4 us  [the longest x53 20.5 us: over_col(): return lax.ppermute(x, 'col', [(c, c ^ mask) for c in range(cols)])]
    all_to_all x1 -> x0, blocking collectives: 12.6 us -> none  [local(): lax.all_to_all(merged.reshape(parts, each, merged.shape[1]), ('row', 'col...]
    pallas_call x4 -> x5, Pallas kernels: 8.5 us -> 10 us  [the longest x2 6.16 us: local(): pl.pallas_call(functools.partial(chain_kernel, groups, masks, first, last...]
  transfers between devices with their start and end apart: 27 -> 58, of which waited for: 8 -> 15; matrix products, arithmetic and copies ran while one was open for 1% -> 1% of each run, Pallas kernels for 18% -> 8%
where the time goes in v3:
time: 112 us
  starting transfers between devices  74.1 us (66%)
  waiting for transfers between devices  23.4 us (21%)
  Pallas kernels  11.8 us (11%)
  local copies, waits for them, and re-layouts  1.19 us (1%)
    ppermute x53, starting transfers between devices, over_col(): return lax.ppermute(x, 'col', [(c, c ^ mask) for c in range(cols)])  69.8 us
    ppermute x53, waiting for transfers between devices, over_col(): return lax.ppermute(x, 'col', [(c, c ^ mask) for c in range(cols)])  20.5 us
    pallas_call x2, Pallas kernels, local(): pl.pallas_call(functools.partial(chain_kernel, groups, masks, first, last...  6.16 us
    ppermute x4, waiting for transfers between devices, over_row(): return lax.ppermute(x, 'row', [(r, r ^ mask) for r in range(rows)])  2.85 us
    ppermute x4, starting transfers between devices, over_row(): return lax.ppermute(x, 'row', [(r, r ^ mask) for r in range(rows)])  2.75 us
  transfers between devices with their start and end apart: 58, of which 15 were waited for; matrix products, arithmetic and copies ran while one was open for 1% of the time, Pallas kernels for 8%

profile of v3, /device:TPU:0, one launch (start us, length us, event | category | flops | bytes accessed | tf_op | source)
XLA Modules:
  0.0 111.7 jit_solution(8426062562866540840)
XLA Ops:
  0.0 1.5 %collective-permute-start = (bf16[64,512]{1,0:T(8,128)(2,1)}, bf16[64,512]{1,0:T(8,128)(2,1)S(1)}, u32[]{:S(2)}, u32[]{:S(2)}) collective-permute-start(bf16[64,512]{1,0:T(8,128)(2,1)} %param.7), channel_id=1, source_target_pairs={{0,0},{1,1},{2,2},{3,3},{4,4},{5,5},{6,6},{7,7},{8,16},{9,17},{10,... | collective-permute-start | bytes 196616 | tf_op jit(solution)/shard_map/ppermute | solution.py:186
  1.5 13.3 %collective-permute-start.3 = (bf16[64,512]{1,0:T(8,128)(2,1)S(1)}, bf16[64,512]{1,0:T(8,128)(2,1)S(1)}, u32[]{:S(2)}, u32[]{:S(2)}) collective-permute-start(bf16[64,512]{1,0:T(8,128)(2,1)S(1)} %collective-permute-done), channel_id=1, source_target_pairs={{0,12},{1,13},{2,14},{3,15},{4,8},{5,9},{6,10},{7,11},{8,4},{9,5},... | collective-permute-start | bytes 196616 | tf_op jit(solution)/shard_map/ppermute | solution.py:170
  15.3 1.9 %pack.1 = (bf16[80,128]{1,0:T(8,128)(2,1)}, bf16[80,128]{1,0:T(8,128)(2,1)}, bf16[80,128]{1,0:T(8,128)(2,1)}, bf16[80,128]{1,0:T(8,128)(2,1)}, bf16[80,128]{1,0:...) custom-call(bf16[1024,256]{1,0:T(8,128)(2,1)} %bitcast.14, ...), custom_call_target="tpu_custom_call" | custom-call | tf_op jit(solution)/shard_map/pack/pallas_call | solution.py:188
  17.4 1.6 %collective-permute-start.24 = (bf16[80,128]{1,0:T(8,128)(2,1)}, bf16[80,128]{1,0:T(8,128)(2,1)S(1)}, u32[]{:S(2)}, u32[]{:S(2)}) collective-permute-start(bf16[80,128]{1,0:T(8,128)(2,1)} %get-tuple-element.61), channel_id=1, source_target_pairs={{0,2},{1,3},{2,0},{3,1},{4,6},{5,7},{6,4},{7,5},{8,10},{9,11},{10,... | collective-permute-start | bytes 61448 | tf_op jit(solution)/shard_map/ppermute | solution.py:170
  20.0 1.6 %collective-permute-start.5 = (bf16[4,64,512]{2,1,0:T(8,128)(2,1)S(1)}, bf16[4,64,512]{2,1,0:T(8,128)(2,1)S(1)}, u32[]{:S(2)}, u32[]{:S(2)}) collective-permute-start(bf16[4,64,512]{2,1,0:T(8,128)(2,1)S(1)} %pad_maximum_fusion.refs_0_), channel_id=1, source_target_pairs={{0,2},{1,3},{2,0},{3,1},{4,6},{5,7},{6,4},{7,5},{8,10},{9,11},{10,... | collective-permute-start | bytes 786440 | tf_op jit(solution)/shard_map/ppermute | solution.py:170
  21.6 0.8 collective-permute-start.26
  22.4 1.6 %collective-permute-start.28 = (bf16[80,128]{1,0:T(8,128)(2,1)}, bf16[80,128]{1,0:T(8,128)(2,1)S(1)}, u32[]{:S(2)}, u32[]{:S(2)}) collective-permute-start(bf16[80,128]{1,0:T(8,128)(2,1)} %get-tuple-element.65), channel_id=1, source_target_pairs={{0,6},{1,7},{2,4},{3,5},{4,2},{5,3},{6,0},{7,1},{8,14},{9,15},{10,... | collective-permute-start | bytes 61448 | tf_op jit(solution)/shard_map/ppermute | solution.py:170
  24.0 2.0 %collective-permute-start.29 = (bf16[80,128]{1,0:T(8,128)(2,1)}, bf16[80,128]{1,0:T(8,128)(2,1)S(1)}, u32[]{:S(2)}, u32[]{:S(2)}) collective-permute-start(bf16[80,128]{1,0:T(8,128)(2,1)} %get-tuple-element.66), channel_id=1, source_target_pairs={{0,7},{1,6},{2,5},{3,4},{4,3},{5,2},{6,1},{7,0},{8,15},{9,14},{10,... | collective-permute-start | bytes 61448 | tf_op jit(solution)/shard_map/ppermute | solution.py:170
  26.0 2.0 %collective-permute-start.30 = (bf16[80,128]{1,0:T(8,128)(2,1)}, bf16[80,128]{1,0:T(8,128)(2,1)S(1)}, u32[]{:S(2)}, u32[]{:S(2)}) collective-permute-start(bf16[80,128]{1,0:T(8,128)(2,1)} %get-tuple-element.67), channel_id=1, source_target_pairs={{0,8},{1,9},{2,10},{3,11},{4,12},{5,13},{6,14},{7,15},{8,0},{9,1},... | collective-permute-start | bytes 61448 | tf_op jit(solution)/shard_map/ppermute | solution.py:170
  28.5 2.1 %collective-permute-start.32 = (bf16[80,128]{1,0:T(8,128)(2,1)}, bf16[80,128]{1,0:T(8,128)(2,1)S(1)}, u32[]{:S(2)}, u32[]{:S(2)}) collective-permute-start(bf16[80,128]{1,0:T(8,128)(2,1)} %get-tuple-element.69), channel_id=1, source_target_pairs={{0,10},{1,11},{2,8},{3,9},{4,14},{5,15},{6,12},{7,13},{8,2},{9,3},... | collective-permute-start | bytes 61448 | tf_op jit(solution)/shard_map/ppermute | solution.py:170
  30.6 1.5 %collective-permute-start.33 = (bf16[80,128]{1,0:T(8,128)(2,1)}, bf16[80,128]{1,0:T(8,128)(2,1)S(1)}, u32[]{:S(2)}, u32[]{:S(2)}) collective-permute-start(bf16[80,128]{1,0:T(8,128)(2,1)} %get-tuple-element.70), channel_id=1, source_target_pairs={{0,11},{1,10},{2,9},{3,8},{4,15},{5,14},{6,13},{7,12},{8,3},{9,2},... | collective-permute-start | bytes 61448 | tf_op jit(solution)/shard_map/ppermute | solution.py:170
  32.2 3.1 %collective-permute-start.34 = (bf16[80,128]{1,0:T(8,128)(2,1)}, bf16[80,128]{1,0:T(8,128)(2,1)S(1)}, u32[]{:S(2)}, u32[]{:S(2)}) collective-permute-start(bf16[80,128]{1,0:T(8,128)(2,1)} %get-tuple-element.71), channel_id=1, source_target_pairs={{0,12},{1,13},{2,14},{3,15},{4,8},{5,9},{6,10},{7,11},{8,4},{9,5},... | collective-permute-start | bytes 61448 | tf_op jit(solution)/shard_map/ppermute | solution.py:170
  35.7 3.1 %collective-permute-start.36 = (bf16[80,128]{1,0:T(8,128)(2,1)}, bf16[80,128]{1,0:T(8,128)(2,1)S(1)}, u32[]{:S(2)}, u32[]{:S(2)}) collective-permute-start(bf16[80,128]{1,0:T(8,128)(2,1)} %get-tuple-element.73), channel_id=1, source_target_pairs={{0,14},{1,15},{2,12},{3,13},{4,10},{5,11},{6,8},{7,9},{8,6},{9,7},... | collective-permute-start | bytes 61448 | tf_op jit(solution)/shard_map/ppermute | solution.py:170
  38.8 1.4 %collective-permute-start.37 = (bf16[80,128]{1,0:T(8,128)(2,1)}, bf16[80,128]{1,0:T(8,128)(2,1)S(1)}, u32[]{:S(2)}, u32[]{:S(2)}) collective-permute-start(bf16[80,128]{1,0:T(8,128)(2,1)} %get-tuple-element.74), channel_id=1, source_target_pairs={{0,15},{1,14},{2,13},{3,12},{4,11},{5,10},{6,9},{7,8},{8,7},{9,6},... | collective-permute-start | bytes 61448 | tf_op jit(solution)/shard_map/ppermute | solution.py:170
  40.7 1.6 %collective-permute-done.36.refs_14_ = bf16[80,128]{1,0:T(8,128)(2,1)S(1)} collective-permute-done((bf16[80,128]{1,0:T(8,128)(2,1)}, bf16[80,128]{1,0:T(8,128)(2,1)S(1)}, u32[]{:S(2)}, u32[]{:S(2)}) %collective-permute-start.36) | collective-permute-done | bytes 20512 | tf_op jit(solution)/shard_map/ppermute | solution.py:170
  42.4 2.6 %collective-permute-done.37.refs_15_ = bf16[80,128]{1,0:T(8,128)(2,1)S(1)} collective-permute-done((bf16[80,128]{1,0:T(8,128)(2,1)}, bf16[80,128]{1,0:T(8,128)(2,1)S(1)}, u32[]{:S(2)}, u32[]{:S(2)}) %collective-permute-start.37) | collective-permute-done | bytes 20512 | tf_op jit(solution)/shard_map/ppermute | solution.py:170
  45.5 1.8 %pick.1 = (bf16[3,80,128]{2,1,0:T(8,128)(2,1)}, bf16[3,80,128]{2,1,0:T(8,128)(2,1)}) custom-call(s32[6]{0:T(128)} %owners.1, bf16[80,128]{1,0:T(8,128)(2,1)} %get-tuple-element.59.refs_0_, bf16[80,128]{1,0:T(8,128)(2,1)} %copy-done.6, bf16[80,128]{1,0:T(8,128)(2,1)} %copy-done.7, bf16[80,128]{1,0:T(8,128)(2,1)} %copy-done.8, bf16[80,128]{1,0:T(8,128)(2,1)} %copy-done.9, ...), custom_call_target="tpu_custom_call" | custom-call | tf_op jit(solution)/shard_map/pick/pallas_call | solution.py:226
  47.9 3.7 %collective-permute-start.38 = (bf16[3,80,128]{2,1,0:T(8,128)(2,1)}, bf16[3,80,128]{2,1,0:T(8,128)(2,1)S(1)}, u32[]{:S(2)}, u32[]{:S(2)}) collective-permute-start(bf16[3,80,128]{2,1,0:T(8,128)(2,1)} %get-tuple-element.75), channel_id=1, source_target_pairs={{0,4},{1,5},{2,6},{3,7},{4,0},{5,1},{6,2},{7,3},{8,12},{9,13},{10,... | collective-permute-start | bytes 184328 | tf_op jit(solution)/shard_map/ppermute | solution.py:170
  51.7 2.5 %collective-permute-done.40 = bf16[3,80,128]{2,1,0:T(8,128)(2,1)S(1)} collective-permute-done((bf16[3,80,128]{2,1,0:T(8,128)(2,1)}, bf16[3,80,128]{2,1,0:T(8,128)(2,1)S(1)}, u32[]{:S(2)}, u32[]{:S(2)}) %collective-permute-start.40) | collective-permute-done | bytes 61472 | tf_op jit(solution)/shard_map/ppermute | solution.py:170
  54.8 1.2 %collective-permute-done.39 = bf16[3,80,128]{2,1,0:T(8,128)(2,1)S(1)} collective-permute-done((bf16[3,80,128]{2,1,0:T(8,128)(2,1)}, bf16[3,80,128]{2,1,0:T(8,128)(2,1)S(1)}, u32[]{:S(2)}, u32[]{:S(2)}) %collective-permute-start.39) | collective-permute-done | bytes 61472 | tf_op jit(solution)/shard_map/ppermute | solution.py:170
  56.0 2.6 %collective-permute-start.48 = (bf16[3,80,128]{2,1,0:T(8,128)(2,1)}, bf16[3,80,128]{2,1,0:T(8,128)(2,1)S(1)}, u32[]{:S(2)}, u32[]{:S(2)}) collective-permute-start(bf16[3,80,128]{2,1,0:T(8,128)(2,1)} %get-tuple-element.76), channel_id=1, source_target_pairs={{0,4},{1,5},{2,6},{3,7},{4,0},{5,1},{6,2},{7,3},{8,12},{9,13},{10,... | collective-permute-start | bytes 184328 | tf_op jit(solution)/shard_map/ppermute | solution.py:170
  58.6 0.9 pad_maximum_fusion.1.refs_16_
  59.5 1.2 %collective-permute-done.50 = bf16[3,80,128]{2,1,0:T(8,128)(2,1)S(1)} collective-permute-done((bf16[3,80,128]{2,1,0:T(8,128)(2,1)}, bf16[3,80,128]{2,1,0:T(8,128)(2,1)S(1)}, u32[]{:S(2)}, u32[]{:S(2)}) %collective-permute-start.50) | collective-permute-done | bytes 61472 | tf_op jit(solution)/shard_map/ppermute | solution.py:170
  60.6 1.3 %collective-permute-done.49 = bf16[3,80,128]{2,1,0:T(8,128)(2,1)S(1)} collective-permute-done((bf16[3,80,128]{2,1,0:T(8,128)(2,1)}, bf16[3,80,128]{2,1,0:T(8,128)(2,1)S(1)}, u32[]{:S(2)}, u32[]{:S(2)}) %collective-permute-start.49) | collective-permute-done | bytes 61472 | tf_op jit(solution)/shard_map/ppermute | solution.py:170
  61.9 1.6 %collective-permute-start.42 = (bf16[4,3,80,128]{3,2,1,0:T(8,128)(2,1)S(1)}, bf16[4,3,80,128]{3,2,1,0:T(8,128)(2,1)S(1)}, u32[]{:S(2)}, u32[]{:S(2)}) collective-permute-start(bf16[4,3,80,128]{3,2,1,0:T(8,128)(2,1)S(1)} %pad_maximum_fusion.1.refs_16_), channel_id=1, source_target_pairs={{0,2},{1,3},{2,0},{3,1},{4,6},{5,7},{6,4},{7,5},{8,10},{9,11},{10,... | collective-permute-start | bytes 737288 | tf_op jit(solution)/shard_map/ppermute | solution.py:170
  64.6 0.8 collective-permute-done.6.refs_3_
  67.1 1.4 %collective-permute-start.51 = (bf16[4,3,80,128]{3,2,1,0:T(8,128)(2,1)S(1)}, bf16[4,3,80,128]{3,2,1,0:T(8,128)(2,1)S(1)}, u32[]{:S(2)}, u32[]{:S(2)}) collective-permute-start(bf16[4,3,80,128]{3,2,1,0:T(8,128)(2,1)S(1)} %pad_maximum_fusion.2.refs_1_), channel_id=1, source_target_pairs={{0,16},{16,0},{1,17},{17,1},{2,18},{18,2},{3,19},{19,3},{4,20},{20... | collective-permute-start | bytes 737288 | tf_op jit(solution)/shard_map/ppermute | solution.py:173
  68.5 1.1 collective-permute-done.42.refs_18_
  69.6 2.5 %collective-permute-start.43 = (bf16[4,3,80,128]{3,2,1,0:T(8,128)(2,1)S(1)}, bf16[4,3,80,128]{3,2,1,0:T(8,128)(2,1)S(1)}, u32[]{:S(2)}, u32[]{:S(2)}) collective-permute-start(bf16[4,3,80,128]{3,2,1,0:T(8,128)(2,1)S(1)} %collective-permute-done.41.refs_17_), channel_id=1, source_target_pairs={{0,2},{1,3},{2,0},{3,1},{4,6},{5,7},{6,4},{7,5},{8,10},{9,11},{10,... | collective-permute-start | bytes 737288 | tf_op jit(solution)/shard_map/ppermute | solution.py:170
  72.1 2.8 %collective-permute-done.52.refs_3_ = bf16[4,3,80,128]{3,2,1,0:T(8,128)(2,1)S(1)} collective-permute-done((bf16[4,3,80,128]{3,2,1,0:T(8,128)(2,1)S(1)}, bf16[4,3,80,128]{3,2,1,0:T(8,128)(2,1)S(1)}, u32[]{:S(2)}, u32[]{:S(2)}) %collective-permute-start.52) | collective-permute-done | bytes 245792 | tf_op jit(solution)/shard_map/ppermute | solution.py:170
  74.9 0.7 collective-permute-start.53
  75.6 1.4 %add.1 = (f32[4,128]{1,0:T(4,128)}, f32[4,128]{1,0:T(4,128)}, f32[4,128]{1,0:T(4,128)}, f32[4,128]{1,0:T(4,128)}, f32[4,128]{1,0:T(4,128)}, /*index=5*/f32[4,128...) custom-call(f32[16,4,128]{2,1,0:T(4,128)} %copy-done.1, ...), custom_call_target="tpu_custom_call" | custom-call | tf_op jit(solution)/shard_map/add/pallas_call | solution.py:217
  77.5 1.1 %collective-permute-done.43.refs_19_ = bf16[4,3,80,128]{3,2,1,0:T(8,128)(2,1)S(1)} collective-permute-done((bf16[4,3,80,128]{3,2,1,0:T(8,128)(2,1)S(1)}, bf16[4,3,80,128]{3,2,1,0:T(8,128)(2,1)S(1)}, u32[]{:S(2)}, u32[]{:S(2)}) %collective-permute-start.43) | collective-permute-done | bytes 245792 | tf_op jit(solution)/shard_map/ppermute | solution.py:170
  78.7 1.6 %collective-permute-start.9 = (f32[4,128]{1,0:T(4,128)}, f32[4,128]{1,0:T(4,128)S(1)}, u32[]{:S(2)}, u32[]{:S(2)}) collective-permute-start(f32[4,128]{1,0:T(4,128)} %get-tuple-element.45), channel_id=1, source_target_pairs={{0,2},{1,3},{2,0},{3,1},{4,6},{5,7},{6,4},{7,5},{8,10},{9,11},{10,... | collective-permute-start | bytes 6152 | tf_op jit(solution)/shard_map/ppermute | solution.py:170
  80.4 2.8 %collective-permute-done.53.refs_4_ = bf16[4,3,80,128]{3,2,1,0:T(8,128)(2,1)S(1)} collective-permute-done((bf16[4,3,80,128]{3,2,1,0:T(8,128)(2,1)S(1)}, bf16[4,3,80,128]{3,2,1,0:T(8,128)(2,1)S(1)}, u32[]{:S(2)}, u32[]{:S(2)}) %collective-permute-start.53) | collective-permute-done | bytes 245792 | tf_op jit(solution)/shard_map/ppermute | solution.py:173
  83.3 3.2 %collective-permute-start.13 = (f32[4,128]{1,0:T(4,128)S(1)}, f32[4,128]{1,0:T(4,128)S(1)}, u32[]{:S(2)}, u32[]{:S(2)}) collective-permute-start(f32[4,128]{1,0:T(4,128)S(1)} %copy-done.30), channel_id=1, source_target_pairs={{0,6},{1,7},{2,4},{3,5},{4,2},{5,3},{6,0},{7,1},{8,14},{9,15},{10,... | collective-permute-start | bytes 6152 | tf_op jit(solution)/shard_map/ppermute | solution.py:170
  87.1 0.8 collective-permute-start.15
  87.9 1.7 %collective-permute-start.16 = (f32[4,128]{1,0:T(4,128)S(1)}, f32[4,128]{1,0:T(4,128)S(1)}, u32[]{:S(2)}, u32[]{:S(2)}) collective-permute-start(f32[4,128]{1,0:T(4,128)S(1)} %copy-done.27), channel_id=1, source_target_pairs={{0,9},{1,8},{2,11},{3,10},{4,13},{5,12},{6,15},{7,14},{8,1},{9,0},... | collective-permute-start | bytes 6152 | tf_op jit(solution)/shard_map/ppermute | solution.py:170
  89.6 2.3 %collective-permute-start.17 = (f32[4,128]{1,0:T(4,128)S(1)}, f32[4,128]{1,0:T(4,128)S(1)}, u32[]{:S(2)}, u32[]{:S(2)}) collective-permute-start(f32[4,128]{1,0:T(4,128)S(1)} %copy-done.26), channel_id=1, source_target_pairs={{0,10},{1,11},{2,8},{3,9},{4,14},{5,15},{6,12},{7,13},{8,2},{9,3},... | collective-permute-start | bytes 6152 | tf_op jit(solution)/shard_map/ppermute | solution.py:170
  92.0 1.7 %collective-permute-start.18 = (f32[4,128]{1,0:T(4,128)S(1)}, f32[4,128]{1,0:T(4,128)S(1)}, u32[]{:S(2)}, u32[]{:S(2)}) collective-permute-start(f32[4,128]{1,0:T(4,128)S(1)} %copy-done.25), channel_id=1, source_target_pairs={{0,11},{1,10},{2,9},{3,8},{4,15},{5,14},{6,13},{7,12},{8,3},{9,2},... | collective-permute-start | bytes 6152 | tf_op jit(solution)/shard_map/ppermute | solution.py:170
  93.6 1.5 %collective-permute-start.19 = (f32[4,128]{1,0:T(4,128)S(1)}, f32[4,128]{1,0:T(4,128)S(1)}, u32[]{:S(2)}, u32[]{:S(2)}) collective-permute-start(f32[4,128]{1,0:T(4,128)S(1)} %copy-done.24), channel_id=1, source_target_pairs={{0,12},{1,13},{2,14},{3,15},{4,8},{5,9},{6,10},{7,11},{8,4},{9,5},... | collective-permute-start | bytes 6152 | tf_op jit(solution)/shard_map/ppermute | solution.py:170
  95.1 1.9 %collective-permute-start.20 = (f32[4,128]{1,0:T(4,128)S(1)}, f32[4,128]{1,0:T(4,128)S(1)}, u32[]{:S(2)}, u32[]{:S(2)}) collective-permute-start(f32[4,128]{1,0:T(4,128)S(1)} %copy-done.23), channel_id=1, source_target_pairs={{0,13},{1,12},{2,15},{3,14},{4,9},{5,8},{6,11},{7,10},{8,5},{9,4},... | collective-permute-start | bytes 6152 | tf_op jit(solution)/shard_map/ppermute | solution.py:170
  97.0 2.7 %collective-permute-start.21 = (f32[4,128]{1,0:T(4,128)S(1)}, f32[4,128]{1,0:T(4,128)S(1)}, u32[]{:S(2)}, u32[]{:S(2)}) collective-permute-start(f32[4,128]{1,0:T(4,128)S(1)} %copy-done.22), channel_id=1, source_target_pairs={{0,14},{1,15},{2,12},{3,13},{4,10},{5,11},{6,8},{7,9},{8,6},{9,7},... | collective-permute-start | bytes 6152 | tf_op jit(solution)/shard_map/ppermute | solution.py:170
  99.7 2.2 %collective-permute-start.22 = (f32[4,128]{1,0:T(4,128)S(1)}, f32[4,128]{1,0:T(4,128)S(1)}, u32[]{:S(2)}, u32[]{:S(2)}) collective-permute-start(f32[4,128]{1,0:T(4,128)S(1)} %copy-done.21), channel_id=1, source_target_pairs={{0,15},{1,14},{2,13},{3,12},{4,11},{5,10},{6,9},{7,8},{8,7},{9,6},... | collective-permute-start | bytes 6152 | tf_op jit(solution)/shard_map/ppermute | solution.py:170
  102.5 0.9 collective-permute-done.21.refs_14_
  103.3 2.2 %collective-permute-done.22.refs_15_ = f32[4,128]{1,0:T(4,128)S(1)} collective-permute-done((f32[4,128]{1,0:T(4,128)S(1)}, f32[4,128]{1,0:T(4,128)S(1)}, u32[]{:S(2)}, u32[]{:S(2)}) %collective-permute-start.22) | collective-permute-done | bytes 2080 | tf_op jit(solution)/shard_map/ppermute | solution.py:170
  105.5 2.8 %chain0.1.refs_0_ = f32[8,2048]{1,0:T(8,128)S(1)} custom-call(s32[6]{0:T(128)S(1)} %copy-done.3, f32[4,128]{1,0:T(4,128)S(1)} %copy-done.2, f32[4,128]{1,0:T(4,128)S(1)} %collective-permute-done.8.refs_1_, f32[4,128]{1,0:T(4,128)S(1)} %collective-permute-done.9.refs_2_, f32[4,128]{1,0:T(4,128)S(1)} %collective-permute-done.10.refs_3_, ...), custom_call_target="tpu_custom_call" | custom-call | tf_op jit(solution)/shard_map/chain0/pallas_call | solution.py:247
  108.4 3.4 %chain1.1 = bf16[4,2048]{1,0:T(4,128)(2,1)} custom-call(s32[6]{0:T(128)S(1)} %copy-done.3, f32[8,2048]{1,0:T(8,128)S(1)} %chain0.1.refs_0_, bf16[4,3,80,128]{3,2,1,0:T(8,128)(2,1)S(1)} %pad_maximum_fusion.2.refs_1_, bf16[4,3,80,128]{3,2,1,0:T(8,128)(2,1)S(1)} %collective-permute-done.51.refs_2_, bf16[4,3,80,128]{3,2,1,0:T(8,128)(2,1)S(1)} %collective-permute-done.52.refs_3_, ...), custom_call_target="tpu_custom_call" | custom-call | tf_op jit(solution)/shard_map/chain1/pallas_call | solution.py:247
  (145 shorter events, 9.5 us)
Async XLA Ops:
  1.5 17.5 %collective-permute-start.3 = (bf16[64,512]{1,0:T(8,128)(2,1)S(1)}, bf16[64,512]{1,0:T(8,128)(2,1)S(1)}, u32[]{:S(2)}, u32[]{:S(2)}) collective-permute-start(bf16[64,512]{1,0:T(8,128)(2,1)S(1)} %collective-permute-done), channel_id=1, source_target_pairs={{0,12},{1,13},{2,14},{3,15},{4,8},{5,9},{6,10},{7,11},{8,4},{9,5},... | collective-permute-start | bytes 196616 | tf_op jit(solution)/shard_map/ppermute | solution.py:170
  14.8 5.2 %collective-permute-start.1 = (bf16[64,512]{1,0:T(8,128)(2,1)S(1)}, bf16[64,512]{1,0:T(8,128)(2,1)S(1)}, u32[]{:S(2)}, u32[]{:S(2)}) collective-permute-start(bf16[64,512]{1,0:T(8,128)(2,1)S(1)} %collective-permute-done), channel_id=1, source_target_pairs={{0,4},{1,5},{2,6},{3,7},{4,0},{5,1},{6,2},{7,3},{8,12},{9,13},{10,... | collective-permute-start | bytes 196616 | tf_op jit(solution)/shard_map/ppermute | solution.py:170
  20.0 43.5 %collective-permute-start.5 = (bf16[4,64,512]{2,1,0:T(8,128)(2,1)S(1)}, bf16[4,64,512]{2,1,0:T(8,128)(2,1)S(1)}, u32[]{:S(2)}, u32[]{:S(2)}) collective-permute-start(bf16[4,64,512]{2,1,0:T(8,128)(2,1)S(1)} %pad_maximum_fusion.refs_0_), channel_id=1, source_target_pairs={{0,2},{1,3},{2,0},{3,1},{4,6},{5,7},{6,4},{7,5},{8,10},{9,11},{10,... | collective-permute-start | bytes 786440 | tf_op jit(solution)/shard_map/ppermute | solution.py:170
  22.3 5.7 %collective-permute-start.27 = (bf16[80,128]{1,0:T(8,128)(2,1)}, bf16[80,128]{1,0:T(8,128)(2,1)S(1)}, u32[]{:S(2)}, u32[]{:S(2)}) collective-permute-start(bf16[80,128]{1,0:T(8,128)(2,1)} %get-tuple-element.64), channel_id=1, source_target_pairs={{0,5},{1,4},{2,7},{3,6},{4,1},{5,0},{6,3},{7,2},{8,13},{9,12},{10,... | collective-permute-start | bytes 61448 | tf_op jit(solution)/shard_map/ppermute | solution.py:170
  22.4 6.2 %collective-permute-start.28 = (bf16[80,128]{1,0:T(8,128)(2,1)}, bf16[80,128]{1,0:T(8,128)(2,1)S(1)}, u32[]{:S(2)}, u32[]{:S(2)}) collective-permute-start(bf16[80,128]{1,0:T(8,128)(2,1)} %get-tuple-element.65), channel_id=1, source_target_pairs={{0,6},{1,7},{2,4},{3,5},{4,2},{5,3},{6,0},{7,1},{8,14},{9,15},{10,... | collective-permute-start | bytes 61448 | tf_op jit(solution)/shard_map/ppermute | solution.py:170
  24.0 6.6 %collective-permute-start.29 = (bf16[80,128]{1,0:T(8,128)(2,1)}, bf16[80,128]{1,0:T(8,128)(2,1)S(1)}, u32[]{:S(2)}, u32[]{:S(2)}) collective-permute-start(bf16[80,128]{1,0:T(8,128)(2,1)} %get-tuple-element.66), channel_id=1, source_target_pairs={{0,7},{1,6},{2,5},{3,4},{4,3},{5,2},{6,1},{7,0},{8,15},{9,14},{10,... | collective-permute-start | bytes 61448 | tf_op jit(solution)/shard_map/ppermute | solution.py:170
  26.0 6.2 %collective-permute-start.30 = (bf16[80,128]{1,0:T(8,128)(2,1)}, bf16[80,128]{1,0:T(8,128)(2,1)S(1)}, u32[]{:S(2)}, u32[]{:S(2)}) collective-permute-start(bf16[80,128]{1,0:T(8,128)(2,1)} %get-tuple-element.67), channel_id=1, source_target_pairs={{0,8},{1,9},{2,10},{3,11},{4,12},{5,13},{6,14},{7,15},{8,0},{9,1},... | collective-permute-start | bytes 61448 | tf_op jit(solution)/shard_map/ppermute | solution.py:170
  28.0 7.3 %collective-permute-start.31 = (bf16[80,128]{1,0:T(8,128)(2,1)}, bf16[80,128]{1,0:T(8,128)(2,1)S(1)}, u32[]{:S(2)}, u32[]{:S(2)}) collective-permute-start(bf16[80,128]{1,0:T(8,128)(2,1)} %get-tuple-element.68), channel_id=1, source_target_pairs={{0,9},{1,8},{2,11},{3,10},{4,13},{5,12},{6,15},{7,14},{8,1},{9,0},... | collective-permute-start | bytes 61448 | tf_op jit(solution)/shard_map/ppermute | solution.py:170
  28.5 7.1 %collective-permute-start.32 = (bf16[80,128]{1,0:T(8,128)(2,1)}, bf16[80,128]{1,0:T(8,128)(2,1)S(1)}, u32[]{:S(2)}, u32[]{:S(2)}) collective-permute-start(bf16[80,128]{1,0:T(8,128)(2,1)} %get-tuple-element.69), channel_id=1, source_target_pairs={{0,10},{1,11},{2,8},{3,9},{4,14},{5,15},{6,12},{7,13},{8,2},{9,3},... | collective-permute-start | bytes 61448 | tf_op jit(solution)/shard_map/ppermute | solution.py:170
  30.6 8.1 %collective-permute-start.33 = (bf16[80,128]{1,0:T(8,128)(2,1)}, bf16[80,128]{1,0:T(8,128)(2,1)S(1)}, u32[]{:S(2)}, u32[]{:S(2)}) collective-permute-start(bf16[80,128]{1,0:T(8,128)(2,1)} %get-tuple-element.70), channel_id=1, source_target_pairs={{0,11},{1,10},{2,9},{3,8},{4,15},{5,14},{6,13},{7,12},{8,3},{9,2},... | collective-permute-start | bytes 61448 | tf_op jit(solution)/shard_map/ppermute | solution.py:170
  32.2 8.0 %collective-permute-start.34 = (bf16[80,128]{1,0:T(8,128)(2,1)}, bf16[80,128]{1,0:T(8,128)(2,1)S(1)}, u32[]{:S(2)}, u32[]{:S(2)}) collective-permute-start(bf16[80,128]{1,0:T(8,128)(2,1)} %get-tuple-element.71), channel_id=1, source_target_pairs={{0,12},{1,13},{2,14},{3,15},{4,8},{5,9},{6,10},{7,11},{8,4},{9,5},... | collective-permute-start | bytes 61448 | tf_op jit(solution)/shard_map/ppermute | solution.py:170
  35.3 5.4 %collective-permute-start.35 = (bf16[80,128]{1,0:T(8,128)(2,1)}, bf16[80,128]{1,0:T(8,128)(2,1)S(1)}, u32[]{:S(2)}, u32[]{:S(2)}) collective-permute-start(bf16[80,128]{1,0:T(8,128)(2,1)} %get-tuple-element.72), channel_id=1, source_target_pairs={{0,13},{1,12},{2,15},{3,14},{4,9},{5,8},{6,11},{7,10},{8,5},{9,4},... | collective-permute-start | bytes 61448 | tf_op jit(solution)/shard_map/ppermute | solution.py:170
  35.7 6.7 %collective-permute-start.36 = (bf16[80,128]{1,0:T(8,128)(2,1)}, bf16[80,128]{1,0:T(8,128)(2,1)S(1)}, u32[]{:S(2)}, u32[]{:S(2)}) collective-permute-start(bf16[80,128]{1,0:T(8,128)(2,1)} %get-tuple-element.73), channel_id=1, source_target_pairs={{0,14},{1,15},{2,12},{3,13},{4,10},{5,11},{6,8},{7,9},{8,6},{9,7},... | collective-permute-start | bytes 61448 | tf_op jit(solution)/shard_map/ppermute | solution.py:170
  38.8 6.1 %collective-permute-start.37 = (bf16[80,128]{1,0:T(8,128)(2,1)}, bf16[80,128]{1,0:T(8,128)(2,1)S(1)}, u32[]{:S(2)}, u32[]{:S(2)}) collective-permute-start(bf16[80,128]{1,0:T(8,128)(2,1)} %get-tuple-element.74), channel_id=1, source_target_pairs={{0,15},{1,14},{2,13},{3,12},{4,11},{5,10},{6,9},{7,8},{8,7},{9,6},... | collective-permute-start | bytes 61448 | tf_op jit(solution)/shard_map/ppermute | solution.py:170
  47.3 6.9 %collective-permute-start.40 = (bf16[3,80,128]{2,1,0:T(8,128)(2,1)}, bf16[3,80,128]{2,1,0:T(8,128)(2,1)S(1)}, u32[]{:S(2)}, u32[]{:S(2)}) collective-permute-start(bf16[3,80,128]{2,1,0:T(8,128)(2,1)} %get-tuple-element.75), channel_id=1, source_target_pairs={{0,12},{1,13},{2,14},{3,15},{4,8},{5,9},{6,10},{7,11},{8,4},{9,5},... | collective-permute-start | bytes 184328 | tf_op jit(solution)/shard_map/ppermute | solution.py:170
  47.9 8.1 %collective-permute-start.39 = (bf16[3,80,128]{2,1,0:T(8,128)(2,1)}, bf16[3,80,128]{2,1,0:T(8,128)(2,1)S(1)}, u32[]{:S(2)}, u32[]{:S(2)}) collective-permute-start(bf16[3,80,128]{2,1,0:T(8,128)(2,1)} %get-tuple-element.75), channel_id=1, source_target_pairs={{0,8},{1,9},{2,10},{3,11},{4,12},{5,13},{6,14},{7,15},{8,0},{9,1},... | collective-permute-start | bytes 184328 | tf_op jit(solution)/shard_map/ppermute | solution.py:170
  47.9 8.1 %collective-permute-start.38 = (bf16[3,80,128]{2,1,0:T(8,128)(2,1)}, bf16[3,80,128]{2,1,0:T(8,128)(2,1)S(1)}, u32[]{:S(2)}, u32[]{:S(2)}) collective-permute-start(bf16[3,80,128]{2,1,0:T(8,128)(2,1)} %get-tuple-element.75), channel_id=1, source_target_pairs={{0,4},{1,5},{2,6},{3,7},{4,0},{5,1},{6,2},{7,3},{8,12},{9,13},{10,... | collective-permute-start | bytes 184328 | tf_op jit(solution)/shard_map/ppermute | solution.py:170
  51.7 12.4 %collective-permute-start.4 = (bf16[4,64,512]{2,1,0:T(8,128)(2,1)S(1)}, bf16[4,64,512]{2,1,0:T(8,128)(2,1)S(1)}, u32[]{:S(2)}, u32[]{:S(2)}) collective-permute-start(bf16[4,64,512]{2,1,0:T(8,128)(2,1)S(1)} %pad_maximum_fusion.refs_0_), channel_id=1, source_target_pairs={{0,1},{1,0},{2,3},{3,2},{4,5},{5,4},{6,7},{7,6},{8,9},{9,8},{10,11... | collective-permute-start | bytes 786440 | tf_op jit(solution)/shard_map/ppermute | solution.py:170
  54.2 6.4 %collective-permute-start.50 = (bf16[3,80,128]{2,1,0:T(8,128)(2,1)}, bf16[3,80,128]{2,1,0:T(8,128)(2,1)S(1)}, u32[]{:S(2)}, u32[]{:S(2)}) collective-permute-start(bf16[3,80,128]{2,1,0:T(8,128)(2,1)} %get-tuple-element.76), channel_id=1, source_target_pairs={{0,12},{1,13},{2,14},{3,15},{4,8},{5,9},{6,10},{7,11},{8,4},{9,5},... | collective-permute-start | bytes 184328 | tf_op jit(solution)/shard_map/ppermute | solution.py:170
  56.0 5.9 %collective-permute-start.49 = (bf16[3,80,128]{2,1,0:T(8,128)(2,1)}, bf16[3,80,128]{2,1,0:T(8,128)(2,1)S(1)}, u32[]{:S(2)}, u32[]{:S(2)}) collective-permute-start(bf16[3,80,128]{2,1,0:T(8,128)(2,1)} %get-tuple-element.76), channel_id=1, source_target_pairs={{0,8},{1,9},{2,10},{3,11},{4,12},{5,13},{6,14},{7,15},{8,0},{9,1},... | collective-permute-start | bytes 184328 | tf_op jit(solution)/shard_map/ppermute | solution.py:170
  56.0 7.5 %collective-permute-start.48 = (bf16[3,80,128]{2,1,0:T(8,128)(2,1)}, bf16[3,80,128]{2,1,0:T(8,128)(2,1)S(1)}, u32[]{:S(2)}, u32[]{:S(2)}) collective-permute-start(bf16[3,80,128]{2,1,0:T(8,128)(2,1)} %get-tuple-element.76), channel_id=1, source_target_pairs={{0,4},{1,5},{2,6},{3,7},{4,0},{5,1},{6,2},{7,3},{8,12},{9,13},{10,... | collective-permute-start | bytes 184328 | tf_op jit(solution)/shard_map/ppermute | solution.py:170
  60.6 6.5 %collective-permute-start.41 = (bf16[4,3,80,128]{3,2,1,0:T(8,128)(2,1)S(1)}, bf16[4,3,80,128]{3,2,1,0:T(8,128)(2,1)S(1)}, u32[]{:S(2)}, u32[]{:S(2)}) collective-permute-start(bf16[4,3,80,128]{3,2,1,0:T(8,128)(2,1)S(1)} %pad_maximum_fusion.1.refs_16_), channel_id=1, source_target_pairs={{0,16},{16,0},{1,17},{17,1},{2,18},{18,2},{3,19},{19,3},{4,20},{20... | collective-permute-start | bytes 737288 | tf_op jit(solution)/shard_map/ppermute | solution.py:173
  61.9 7.7 %collective-permute-start.42 = (bf16[4,3,80,128]{3,2,1,0:T(8,128)(2,1)S(1)}, bf16[4,3,80,128]{3,2,1,0:T(8,128)(2,1)S(1)}, u32[]{:S(2)}, u32[]{:S(2)}) collective-permute-start(bf16[4,3,80,128]{3,2,1,0:T(8,128)(2,1)S(1)} %pad_maximum_fusion.1.refs_16_), channel_id=1, source_target_pairs={{0,2},{1,3},{2,0},{3,1},{4,6},{5,7},{6,4},{7,5},{8,10},{9,11},{10,... | collective-permute-start | bytes 737288 | tf_op jit(solution)/shard_map/ppermute | solution.py:170
  63.5 8.6 %collective-permute-start.44 = (bf16[4,3,80,128]{3,2,1,0:T(8,128)(2,1)S(1)}, bf16[4,3,80,128]{3,2,1,0:T(8,128)(2,1)S(1)}, u32[]{:S(2)}, u32[]{:S(2)}) collective-permute-start(bf16[4,3,80,128]{3,2,1,0:T(8,128)(2,1)S(1)} %pad_maximum_fusion.1.refs_16_), channel_id=1, source_target_pairs={{0,1},{1,0},{2,3},{3,2},{4,5},{5,4},{6,7},{7,6},{8,9},{9,8},{10,11... | collective-permute-start | bytes 737288 | tf_op jit(solution)/shard_map/ppermute | solution.py:170
  64.1 10.8 %collective-permute-start.52 = (bf16[4,3,80,128]{3,2,1,0:T(8,128)(2,1)S(1)}, bf16[4,3,80,128]{3,2,1,0:T(8,128)(2,1)S(1)}, u32[]{:S(2)}, u32[]{:S(2)}) collective-permute-start(bf16[4,3,80,128]{3,2,1,0:T(8,128)(2,1)S(1)} %pad_maximum_fusion.2.refs_1_), channel_id=1, source_target_pairs={{0,2},{1,3},{2,0},{3,1},{4,6},{5,7},{6,4},{7,5},{8,10},{9,11},{10,... | collective-permute-start | bytes 737288 | tf_op jit(solution)/shard_map/ppermute | solution.py:170
  66.5 8.4 %collective-permute-start.7 = (f32[16,4,128]{2,1,0:T(4,128)S(1)}, f32[16,4,128]{2,1,0:T(4,128)S(1)}, u32[]{:S(2)}, u32[]{:S(2)}) collective-permute-start(f32[16,4,128]{2,1,0:T(4,128)S(1)} %get-tuple-element.42), channel_id=1, source_target_pairs={{0,16},{16,0},{1,17},{17,1},{2,18},{18,2},{3,19},{19,3},{4,20},{20... | collective-permute-start | bytes 98312 | tf_op jit(solution)/shard_map/ppermute | solution.py:173
  67.1 10.0 %collective-permute-start.51 = (bf16[4,3,80,128]{3,2,1,0:T(8,128)(2,1)S(1)}, bf16[4,3,80,128]{3,2,1,0:T(8,128)(2,1)S(1)}, u32[]{:S(2)}, u32[]{:S(2)}) collective-permute-start(bf16[4,3,80,128]{3,2,1,0:T(8,128)(2,1)S(1)} %pad_maximum_fusion.2.refs_1_), channel_id=1, source_target_pairs={{0,16},{16,0},{1,17},{17,1},{2,18},{18,2},{3,19},{19,3},{4,20},{20... | collective-permute-start | bytes 737288 | tf_op jit(solution)/shard_map/ppermute | solution.py:173
  69.6 9.0 %collective-permute-start.43 = (bf16[4,3,80,128]{3,2,1,0:T(8,128)(2,1)S(1)}, bf16[4,3,80,128]{3,2,1,0:T(8,128)(2,1)S(1)}, u32[]{:S(2)}, u32[]{:S(2)}) collective-permute-start(bf16[4,3,80,128]{3,2,1,0:T(8,128)(2,1)S(1)} %collective-permute-done.41.refs_17_), channel_id=1, source_target_pairs={{0,2},{1,3},{2,0},{3,1},{4,6},{5,7},{6,4},{7,5},{8,10},{9,11},{10,... | collective-permute-start | bytes 737288 | tf_op jit(solution)/shard_map/ppermute | solution.py:170
  72.1 8.1 %collective-permute-start.45 = (bf16[4,3,80,128]{3,2,1,0:T(8,128)(2,1)S(1)}, bf16[4,3,80,128]{3,2,1,0:T(8,128)(2,1)S(1)}, u32[]{:S(2)}, u32[]{:S(2)}) collective-permute-start(bf16[4,3,80,128]{3,2,1,0:T(8,128)(2,1)S(1)} %collective-permute-done.41.refs_17_), channel_id=1, source_target_pairs={{0,1},{1,0},{2,3},{3,2},{4,5},{5,4},{6,7},{7,6},{8,9},{9,8},{10,11... | collective-permute-start | bytes 737288 | tf_op jit(solution)/shard_map/ppermute | solution.py:170
  74.9 5.4 %collective-permute-start.46 = (bf16[4,3,80,128]{3,2,1,0:T(8,128)(2,1)S(1)}, bf16[4,3,80,128]{3,2,1,0:T(8,128)(2,1)S(1)}, u32[]{:S(2)}, u32[]{:S(2)}) collective-permute-start(bf16[4,3,80,128]{3,2,1,0:T(8,128)(2,1)S(1)} %collective-permute-done.42.refs_18_), channel_id=1, source_target_pairs={{0,1},{1,0},{2,3},{3,2},{4,5},{5,4},{6,7},{7,6},{8,9},{9,8},{10,11... | collective-permute-start | bytes 737288 | tf_op jit(solution)/shard_map/ppermute | solution.py:170
  74.9 8.4 %collective-permute-start.53 = (bf16[4,3,80,128]{3,2,1,0:T(8,128)(2,1)S(1)}, bf16[4,3,80,128]{3,2,1,0:T(8,128)(2,1)S(1)}, u32[]{:S(2)}, u32[]{:S(2)}) collective-permute-start(bf16[4,3,80,128]{3,2,1,0:T(8,128)(2,1)S(1)} %collective-permute-done.52.refs_3_), channel_id=1, source_target_pairs={{0,16},{16,0},{1,17},{17,1},{2,18},{18,2},{3,19},{19,3},{4,20},{20... | collective-permute-start | bytes 737288 | tf_op jit(solution)/shard_map/ppermute | solution.py:173
  77.1 6.2 %collective-permute-start.8 = (f32[4,128]{1,0:T(4,128)}, f32[4,128]{1,0:T(4,128)S(1)}, u32[]{:S(2)}, u32[]{:S(2)}) collective-permute-start(f32[4,128]{1,0:T(4,128)} %get-tuple-element.44), channel_id=1, source_target_pairs={{0,1},{1,0},{2,3},{3,2},{4,5},{5,4},{6,7},{7,6},{8,9},{9,8},{10,11... | collective-permute-start | bytes 6152 | tf_op jit(solution)/shard_map/ppermute | solution.py:170
  78.7 7.9 %collective-permute-start.9 = (f32[4,128]{1,0:T(4,128)}, f32[4,128]{1,0:T(4,128)S(1)}, u32[]{:S(2)}, u32[]{:S(2)}) collective-permute-start(f32[4,128]{1,0:T(4,128)} %get-tuple-element.45), channel_id=1, source_target_pairs={{0,2},{1,3},{2,0},{3,1},{4,6},{5,7},{6,4},{7,5},{8,10},{9,11},{10,... | collective-permute-start | bytes 6152 | tf_op jit(solution)/shard_map/ppermute | solution.py:170
  80.2 6.9 %collective-permute-start.10 = (f32[4,128]{1,0:T(4,128)S(1)}, f32[4,128]{1,0:T(4,128)S(1)}, u32[]{:S(2)}, u32[]{:S(2)}) collective-permute-start(f32[4,128]{1,0:T(4,128)S(1)} %copy-done.33), channel_id=1, source_target_pairs={{0,3},{1,2},{2,1},{3,0},{4,7},{5,6},{6,5},{7,4},{8,11},{9,10},{10,... | collective-permute-start | bytes 6152 | tf_op jit(solution)/shard_map/ppermute | solution.py:170
  80.3 7.6 %collective-permute-start.11 = (f32[4,128]{1,0:T(4,128)S(1)}, f32[4,128]{1,0:T(4,128)S(1)}, u32[]{:S(2)}, u32[]{:S(2)}) collective-permute-start(f32[4,128]{1,0:T(4,128)S(1)} %copy-done.32), channel_id=1, source_target_pairs={{0,4},{1,5},{2,6},{3,7},{4,0},{5,1},{6,2},{7,3},{8,12},{9,13},{10,... | collective-permute-start | bytes 6152 | tf_op jit(solution)/shard_map/ppermute | solution.py:170
  83.3 6.3 %collective-permute-start.12 = (f32[4,128]{1,0:T(4,128)S(1)}, f32[4,128]{1,0:T(4,128)S(1)}, u32[]{:S(2)}, u32[]{:S(2)}) collective-permute-start(f32[4,128]{1,0:T(4,128)S(1)} %copy-done.31), channel_id=1, source_target_pairs={{0,5},{1,4},{2,7},{3,6},{4,1},{5,0},{6,3},{7,2},{8,13},{9,12},{10,... | collective-permute-start | bytes 6152 | tf_op jit(solution)/shard_map/ppermute | solution.py:170
  83.3 8.6 %collective-permute-start.13 = (f32[4,128]{1,0:T(4,128)S(1)}, f32[4,128]{1,0:T(4,128)S(1)}, u32[]{:S(2)}, u32[]{:S(2)}) collective-permute-start(f32[4,128]{1,0:T(4,128)S(1)} %copy-done.30), channel_id=1, source_target_pairs={{0,6},{1,7},{2,4},{3,5},{4,2},{5,3},{6,0},{7,1},{8,14},{9,15},{10,... | collective-permute-start | bytes 6152 | tf_op jit(solution)/shard_map/ppermute | solution.py:170
  86.6 7.1 %collective-permute-start.14 = (f32[4,128]{1,0:T(4,128)S(1)}, f32[4,128]{1,0:T(4,128)S(1)}, u32[]{:S(2)}, u32[]{:S(2)}) collective-permute-start(f32[4,128]{1,0:T(4,128)S(1)} %copy-done.29), channel_id=1, source_target_pairs={{0,7},{1,6},{2,5},{3,4},{4,3},{5,2},{6,1},{7,0},{8,15},{9,14},{10,... | collective-permute-start | bytes 6152 | tf_op jit(solution)/shard_map/ppermute | solution.py:170
  87.1 8.0 %collective-permute-start.15 = (f32[4,128]{1,0:T(4,128)S(1)}, f32[4,128]{1,0:T(4,128)S(1)}, u32[]{:S(2)}, u32[]{:S(2)}) collective-permute-start(f32[4,128]{1,0:T(4,128)S(1)} %copy-done.28), channel_id=1, source_target_pairs={{0,8},{1,9},{2,10},{3,11},{4,12},{5,13},{6,14},{7,15},{8,0},{9,1},... | collective-permute-start | bytes 6152 | tf_op jit(solution)/shard_map/ppermute | solution.py:170
  87.9 9.1 %collective-permute-start.16 = (f32[4,128]{1,0:T(4,128)S(1)}, f32[4,128]{1,0:T(4,128)S(1)}, u32[]{:S(2)}, u32[]{:S(2)}) collective-permute-start(f32[4,128]{1,0:T(4,128)S(1)} %copy-done.27), channel_id=1, source_target_pairs={{0,9},{1,8},{2,11},{3,10},{4,13},{5,12},{6,15},{7,14},{8,1},{9,0},... | collective-permute-start | bytes 6152 | tf_op jit(solution)/shard_map/ppermute | solution.py:170
  89.6 10.1 %collective-permute-start.17 = (f32[4,128]{1,0:T(4,128)S(1)}, f32[4,128]{1,0:T(4,128)S(1)}, u32[]{:S(2)}, u32[]{:S(2)}) collective-permute-start(f32[4,128]{1,0:T(4,128)S(1)} %copy-done.26), channel_id=1, source_target_pairs={{0,10},{1,11},{2,8},{3,9},{4,14},{5,15},{6,12},{7,13},{8,2},{9,3},... | collective-permute-start | bytes 6152 | tf_op jit(solution)/shard_map/ppermute | solution.py:170
  92.0 9.9 %collective-permute-start.18 = (f32[4,128]{1,0:T(4,128)S(1)}, f32[4,128]{1,0:T(4,128)S(1)}, u32[]{:S(2)}, u32[]{:S(2)}) collective-permute-start(f32[4,128]{1,0:T(4,128)S(1)} %copy-done.25), channel_id=1, source_target_pairs={{0,11},{1,10},{2,9},{3,8},{4,15},{5,14},{6,13},{7,12},{8,3},{9,2},... | collective-permute-start | bytes 6152 | tf_op jit(solution)/shard_map/ppermute | solution.py:170
  93.6 8.3 %collective-permute-start.19 = (f32[4,128]{1,0:T(4,128)S(1)}, f32[4,128]{1,0:T(4,128)S(1)}, u32[]{:S(2)}, u32[]{:S(2)}) collective-permute-start(f32[4,128]{1,0:T(4,128)S(1)} %copy-done.24), channel_id=1, source_target_pairs={{0,12},{1,13},{2,14},{3,15},{4,8},{5,9},{6,10},{7,11},{8,4},{9,5},... | collective-permute-start | bytes 6152 | tf_op jit(solution)/shard_map/ppermute | solution.py:170
  95.1 7.3 %collective-permute-start.20 = (f32[4,128]{1,0:T(4,128)S(1)}, f32[4,128]{1,0:T(4,128)S(1)}, u32[]{:S(2)}, u32[]{:S(2)}) collective-permute-start(f32[4,128]{1,0:T(4,128)S(1)} %copy-done.23), channel_id=1, source_target_pairs={{0,13},{1,12},{2,15},{3,14},{4,9},{5,8},{6,11},{7,10},{8,5},{9,4},... | collective-permute-start | bytes 6152 | tf_op jit(solution)/shard_map/ppermute | solution.py:170
  97.0 6.3 %collective-permute-start.21 = (f32[4,128]{1,0:T(4,128)S(1)}, f32[4,128]{1,0:T(4,128)S(1)}, u32[]{:S(2)}, u32[]{:S(2)}) collective-permute-start(f32[4,128]{1,0:T(4,128)S(1)} %copy-done.22), channel_id=1, source_target_pairs={{0,14},{1,15},{2,12},{3,13},{4,10},{5,11},{6,8},{7,9},{8,6},{9,7},... | collective-permute-start | bytes 6152 | tf_op jit(solution)/shard_map/ppermute | solution.py:170
  99.7 5.8 %collective-permute-start.22 = (f32[4,128]{1,0:T(4,128)S(1)}, f32[4,128]{1,0:T(4,128)S(1)}, u32[]{:S(2)}, u32[]{:S(2)}) collective-permute-start(f32[4,128]{1,0:T(4,128)S(1)} %copy-done.21), channel_id=1, source_target_pairs={{0,15},{1,14},{2,13},{3,12},{4,11},{5,10},{6,9},{7,8},{8,7},{9,6},... | collective-permute-start | bytes 6152 | tf_op jit(solution)/shard_map/ppermute | solution.py:170
  102.0 6.4 %collective-permute-start.54 = (bf16[4,3,80,128]{3,2,1,0:T(8,128)(2,1)S(1)}, bf16[4,3,80,128]{3,2,1,0:T(8,128)(2,1)S(1)}, u32[]{:S(2)}, u32[]{:S(2)}) collective-permute-start(bf16[4,3,80,128]{3,2,1,0:T(8,128)(2,1)S(1)} %pad_maximum_fusion.2.refs_1_), channel_id=1, source_target_pairs={{0,1},{1,0},{2,3},{3,2},{4,5},{5,4},{6,7},{7,6},{8,9},{9,8},{10,11... | collective-permute-start | bytes 737288 | tf_op jit(solution)/shard_map/ppermute | solution.py:170
  102.4 5.9 %collective-permute-start.56 = (bf16[4,3,80,128]{3,2,1,0:T(8,128)(2,1)S(1)}, bf16[4,3,80,128]{3,2,1,0:T(8,128)(2,1)S(1)}, u32[]{:S(2)}, u32[]{:S(2)}) collective-permute-start(bf16[4,3,80,128]{3,2,1,0:T(8,128)(2,1)S(1)} %collective-permute-done.52.refs_3_), channel_id=1, source_target_pairs={{0,1},{1,0},{2,3},{3,2},{4,5},{5,4},{6,7},{7,6},{8,9},{9,8},{10,11... | collective-permute-start | bytes 737288 | tf_op jit(solution)/shard_map/ppermute | solution.py:170
  (44 other events, 332.6 us)

commit v4 on v3

--- a/solution.py
+++ b/solution.py
@@ -42,12 +42,34 @@
     pv = half // (NEAR * FAR)
     lanes = basis.shape[1] // LANES
     tall = factor.shape[0] * lanes // SLICES
-    for mask, out in enumerate(outs):
-        e = jnp.bitwise_xor(mine, mask)
-        rows = aligned(lax.rem(e, NEAR * FAR), pv)
-        for k in range(lanes):
-            out[k * pv : (k + 1) * pv, :] = basis[rows, k * LANES : (k + 1) * LANES]
-        out[lanes * pv :, :] = factor[aligned(e // lanes, tall), aligned(lax.rem(e, lanes), LANES)]
+    for near, out in enumerate(outs):
+        for far in range(FAR):
+            e = jnp.bitwise_xor(mine, far * NEAR + near)
+            rows = aligned(lax.rem(e, NEAR * FAR), pv)
+            for k in range(lanes):
+                out[far, k * pv : (k + 1) * pv, :] = basis[rows, k * LANES : (k + 1) * LANES]
+            out[far, lanes * pv :, :] = factor[
+                aligned(e // lanes, tall), aligned(lax.rem(e, lanes), LANES)
+            ]
+
+
+def turn_kernel(*refs):
+    count = refs[-1].shape[0]
+    held, outs = refs[:count], refs[count:]
+    for a, ref in enumerate(held):
+        for b, out in enumerate(outs):
+            out[a] = ref[b]
+
+
+def turn(arrays):
+    shape, dtype = arrays[0].shape, arrays[0].dtype
+    return pl.pallas_call(
+        turn_kernel,
+        out_shape=[jax.ShapeDtypeStruct((len(arrays),) + shape[1:], dtype)] * shape[0],
+        in_specs=[VMEM] * len(arrays),
+        out_specs=[VMEM] * shape[0],
+        name="turn",
+    )(*arrays)
 
 
 def pick_kernel(owners, *refs):
@@ -56,9 +78,10 @@
     for phase, groups in enumerate(PHASES):
         for slot, group in enumerate(groups):
             want = jnp.bitwise_xor(owners[group], col)
-            piece = held[0][...]
+            near, far = lax.rem(want, NEAR), want // NEAR
+            piece = held[0][near]
             for mask in range(1, len(held)):
-                piece = jnp.where(want == mask, held[mask][...], piece)
+                piece = jnp.where(far == mask, held[mask][near], piece)
             outs[phase][slot] = piece
 
 
@@ -69,13 +92,11 @@
     deep, tall = held[0].shape[2], held[0].shape[1]
     total[...] = jnp.zeros_like(total)
     for near, ref in enumerate(held):
-        for far in range(ref.shape[0]):
-            j = jnp.bitwise_xor(col, far * NEAR + near)
-            part = jnp.dot(
-                ref[far], sub[aligned(lax.rem(j, share), deep), :],
-                preferred_element_type=jnp.float32,
-            )
-            at = aligned(j // share, tall)
+        for index in range(ref.shape[0]):
+            far, row_mask = index // rows, index % rows
+            j = jnp.bitwise_xor(lax.rem(col, share), far * NEAR + near)
+            part = jnp.dot(ref[index], sub[aligned(j, deep), :], preferred_element_type=jnp.float32)
+            at = aligned(jnp.bitwise_xor(row, row_mask), tall)
             total[at, :] = total[at, :] + part
     each = outs[0].shape[1]
     for row_mask, out in enumerate(outs):
@@ -85,12 +106,13 @@
 
 
 def add_kernel(*refs):
-    count = refs[0].shape[0]
+    count = refs[0].shape[0] // NEAR
     held, outs = refs[:-count], refs[-count:]
-    for mask, out in enumerate(outs):
-        piece = held[0][mask]
+    for far, out in enumerate(outs):
+        at = slice(far * NEAR, (far + 1) * NEAR)
+        piece = held[0][at]
         for ref in held[1:]:
-            piece = piece + ref[mask]
+            piece = piece + ref[at]
         out[...] = piece
 
 
@@ -113,22 +135,24 @@
     lanes = basis_all.shape[2] // LANES
     pv = basis_all.shape[1] // SLICES
     tall = factor_all.shape[1] * lanes // SLICES
-    for mask, ref in zip(masks, held):
-        for far in range(FAR):
-            e = jnp.bitwise_xor(mine, mask + far * NEAR)
+    for own_masks, ref in zip(masks, held):
+        for index, mask in enumerate(own_masks):
+            e = jnp.bitwise_xor(mine, mask)
             for k in range(lanes):
                 basis_all[:, aligned(e, pv), k * LANES : (k + 1) * LANES] = ref[
-                    far, :, k * pv : (k + 1) * pv, :
+                    index, :, k * pv : (k + 1) * pv, :
                 ]
             factor_all[:, aligned(e // lanes, tall), aligned(lax.rem(e, lanes), LANES)] = ref[
-                far, :, lanes * pv :, :
+                index, :, lanes * pv :, :
             ]
     if first:
         state = refs[-1]
         state[...] = jnp.zeros_like(state)
         col = lax.axis_index("col")
-        for mask, ref in enumerate(starts):
-            state[jnp.bitwise_xor(col, mask), : ref.shape[0], :] = ref[...]
+        for near, ref in enumerate(starts):
+            for far in range(ref.shape[0]):
+                at = jnp.bitwise_xor(col, far * NEAR + near)
+                state[at, : ref.shape[1], :] = ref[far]
         x = jnp.concatenate([state[c] for c in range(state.shape[0])], 1)
     else:
         x = starts[0][...]
@@ -178,18 +202,11 @@
     lanes = reflect // LANES
     tall = (group_rows + reflect) * lanes // SLICES
 
-    pairs = [
-        (r * cols + c, (c // share) * cols + share * r + c % share)
-        for r in range(rows)
-        for c in range(cols)
-    ]
-    mine = lax.ppermute(merge_factor, ("row", "col"), pairs)
-
     packed = pl.pallas_call(
         pack_kernel,
-        out_shape=[jax.ShapeDtypeStruct((tall, LANES), dtype)] * (NEAR * FAR),
+        out_shape=[jax.ShapeDtypeStruct((FAR, tall, LANES), dtype)] * NEAR,
         in_specs=[ANY, ANY],
-        out_specs=[VMEM] * (NEAR * FAR),
+        out_specs=[VMEM] * NEAR,
         scratch_shapes=[
             pltpu.VMEM((group_rows // 2, reflect), dtype),
             pltpu.VMEM(factor.shape, dtype),
@@ -197,11 +214,35 @@
         ],
         name="pack",
     )(basis, factor)
-    slices = [packed[0]] + [over_col(packed[m % (NEAR * FAR)], m) for m in range(1, cols)]
-
-    m_far = jnp.stack([mine] + [over_col(mine, m) for m in range(NEAR, cols, NEAR)])
-    m_two = over_col(m_far, 2)
-    m_held = [m_far, over_col(m_far, 1), m_two, over_col(m_two, 1)]
+    slices = turn([packed[0]] + [over_col(packed[m], m) for m in range(1, NEAR)])
+    slices = [slices[0]] + [over_col(slices[m % FAR], m * NEAR) for m in range(1, cols // NEAR)]
+    picked = pl.pallas_call(
+        pick_kernel,
+        out_shape=[
+            jax.ShapeDtypeStruct((len(groups), tall, LANES), dtype) for groups in PHASES
+        ],
+        in_specs=[SMEM] + [VMEM] * len(slices),
+        out_specs=[VMEM] * len(PHASES),
+        name="pick",
+    )(owners, *slices)
+
+    row, top = lax.axis_index("row"), lax.axis_index("col") // share
+    across = [merge_factor] + [over_col(merge_factor, m * share) for m in range(1, rows)]
+
+    def for_row(mask):
+        index = top ^ row ^ mask
+        block = across[0]
+        for k in range(1, rows):
+            block = jnp.where(index == k, across[k], block)
+        return block
+
+    m_held = jnp.stack([for_row(0)] + [over_row(for_row(m), m) for m in range(1, rows)])
+    bit = share // 2
+    while bit >= NEAR:
+        m_held = jnp.concatenate([m_held, over_col(m_held, bit)])
+        bit //= 2
+    m_two = over_col(m_held, 2)
+    m_held = [m_held, over_col(m_held, 1), m_two, over_col(m_two, 1)]
     wanted, width = merge_factor.shape[0] * rows, sub_vectors.shape[1]
     each = wanted // (rows * cols)
     parts = pl.pallas_call(
@@ -216,34 +257,35 @@
     parts = [parts[0]] + [over_row(parts[m], m) for m in range(1, rows)]
     pieces = pl.pallas_call(
         add_kernel,
-        out_shape=[jax.ShapeDtypeStruct((each, width), jnp.float32)] * cols,
+        out_shape=[jax.ShapeDtypeStruct((NEAR, each, width), jnp.float32)] * (cols // NEAR),
         in_specs=[VMEM] * rows,
-        out_specs=[VMEM] * cols,
+        out_specs=[VMEM] * (cols // NEAR),
         name="add",
     )(*parts)
-    state = [pieces[0]] + [over_col(pieces[m], m) for m in range(1, cols)]
-
-    picked = pl.pallas_call(
-        pick_kernel,
-        out_shape=[
-            jax.ShapeDtypeStruct((len(groups), tall, LANES), dtype) for groups in PHASES
-        ],
-        in_specs=[SMEM] + [VMEM] * cols,
-        out_specs=[VMEM] * len(PHASES),
-        name="pick",
-    )(owners, *slices)
+    state = turn([pieces[0]] + [over_col(pieces[m], m * NEAR) for m in range(1, cols // NEAR)])
+    state = [state[0]] + [over_col(state[m], m) for m in range(1, NEAR)]
 
     wide = cols * width
+    x_bit, y_bit, core_bit = NEAR * FAR, 2, 1
+    own_masks = [m * NEAR for m in range(FAR)]
+    corner_masks = [m + x_bit + y_bit for m in own_masks]
     for phase, groups in enumerate(PHASES):
         first, last = phase == 0, phase == len(PHASES) - 1
         own = picked[phase]
-        own = jnp.stack([own] + [over_col(own, m * NEAR) for m in range(1, FAR)])
-        by_row, by_col = over_row(own, 1), over_col(own, 2)
-        corner = over_col(by_row, 2) if phase % 2 == 0 else over_row(by_col, 1)
-        held = [own, by_row, by_col, corner]
-        masks = [0, NEAR * FAR, 2, NEAR * FAR + 2]
-        held = held + [over_col(x, 1) for x in held]
-        masks = masks + [m + 1 for m in masks]
+        own = jnp.stack([own] + [over_col(own, m) for m in own_masks[1:]])
+        by_row, by_col = over_row(own, 1), over_col(own, y_bit)
+        corner = jnp.concatenate(
+            [over_col(by_row[: FAR // 2], y_bit), over_row(by_col[FAR // 2 :], 1)]
+        )
+        sides = jnp.concatenate([by_row, by_col])
+        held = [own, sides, corner]
+        masks = [
+            own_masks,
+            [m + x_bit for m in own_masks] + [m + y_bit for m in own_masks],
+            corner_masks,
+        ]
+        held = held + [over_col(x, core_bit) for x in held]
+        masks = masks + [[m + core_bit for m in ms] for ms in masks]
         out = pl.pallas_call(
             functools.partial(chain_kernel, groups, masks, first, last),
             out_shape=jax.ShapeDtypeStruct(

time: 112 us -> 94.6 us (0.84)
  starting transfers between devices: 74.1 us -> 37.6 us
  waiting for transfers between devices: 23.4 us -> 35.5 us
  local copies, waits for them, and re-layouts: 1.19 us -> 4.89 us
  Pallas kernels: 11.8 us -> 14.7 us
    ppermute x53 -> x33, starting transfers between devices: 69.8 us -> 33.6 us  [over_col(): return lax.ppermute(x, 'col', [(c, c ^ mask) for c in range(cols)])]
    ppermute x53 -> x33, waiting for transfers between devices: 20.5 us -> 26.7 us  [over_col(): return lax.ppermute(x, 'col', [(c, c ^ mask) for c in range(cols)])]
    ppermute x4 -> x6, waiting for transfers between devices: 2.85 us -> 8.86 us  [over_row(): return lax.ppermute(x, 'row', [(r, r ^ mask) for r in range(rows)])]
    pallas_call x2 -> x4, Pallas kernels: 3.36 us -> 6.37 us  [the longest x2 3.11 us: turn(): pl.pallas_call(turn_kernel, out_shape=[jax.ShapeDtypeStruct((len(arrays),...]
    unnamed x68 -> x44, local copies, waits for them, and re-layouts: 1.19 us -> 3.2 us
    ppermute x1 -> x0, starting transfers between devices: 1.49 us -> none  [local(): mine = lax.ppermute(merge_factor, ('row', 'col'), pairs)]
    ppermute x4 -> x6, starting transfers between devices: 2.75 us -> 4.07 us  [over_row(): return lax.ppermute(x, 'row', [(r, r ^ mask) for r in range(rows)])]
  transfers between devices with their start and end apart: 58 -> 39, of which waited for: 15 -> 14; matrix products, arithmetic and copies ran while one was open for 1% -> 2% of each run, Pallas kernels for 8% -> 12%
where the time goes in v4:
time: 94.6 us; the launch traced here: 94.1 us
  starting transfers between devices  37.6 us (40%)
  waiting for transfers between devices  35.5 us (38%)
  Pallas kernels  14.7 us (16%)
  local copies, waits for them, and re-layouts  4.89 us (5%)
  other arithmetic  0.96 us (1%)
    ppermute x33, starting transfers between devices, over_col(): return lax.ppermute(x, 'col', [(c, c ^ mask) for c in range(cols)])  33.6 us
    ppermute x33, waiting for transfers between devices, over_col(): return lax.ppermute(x, 'col', [(c, c ^ mask) for c in range(cols)])  26.7 us
    ppermute x6, waiting for transfers between devices, over_row(): return lax.ppermute(x, 'row', [(r, r ^ mask) for r in range(rows)])  8.86 us
    pallas_call x2, Pallas kernels, local(): pl.pallas_call(functools.partial(chain_kernel, groups, masks, first, last...  6.13 us
    ppermute x6, starting transfers between devices, over_row(): return lax.ppermute(x, 'row', [(r, r ^ mask) for r in range(rows)])  4.07 us
    unnamed x44, local copies, waits for them, and re-layouts  3.2 us
    pallas_call x2, Pallas kernels, turn(): pl.pallas_call(turn_kernel, out_shape=[jax.ShapeDtypeStruct((len(arrays),...  3.11 us
  transfers between devices with their start and end apart: 39, of which 14 were waited for; matrix products, arithmetic and copies ran while one was open for 2% of the time, Pallas kernels for 12%

profile of v4, /device:TPU:0, one launch (start us, length us, event | category | flops | bytes accessed | tf_op | source)
XLA Modules:
  0.0 94.1 jit_solution(14048342377748615905)
XLA Ops:
  0.0 4.0 %collective-permute-start = (bf16[64,512]{1,0:T(8,128)(2,1)}, bf16[64,512]{1,0:T(8,128)(2,1)S(1)}, u32[]{:S(2)}, u32[]{:S(2)}) collective-permute-start(bf16[64,512]{1,0:T(8,128)(2,1)} %param.7), channel_id=1, source_target_pairs={{0,8},{1,9},{2,10},{3,11},{4,12},{5,13},{6,14},{7,15},{8,0},{9,1},... | collective-permute-start | bytes 196616 | tf_op jit(solution)/shard_map/ppermute | solution.py:194
  4.0 3.9 %collective-permute-done = bf16[64,512]{1,0:T(8,128)(2,1)S(1)} collective-permute-done((bf16[64,512]{1,0:T(8,128)(2,1)}, bf16[64,512]{1,0:T(8,128)(2,1)S(1)}, u32[]{:S(2)}, u32[]{:S(2)}) %collective-permute-start) | collective-permute-done | bytes 65568 | tf_op jit(solution)/shard_map/ppermute | solution.py:194
  7.9 0.9 select_bitcast_fusion
  8.8 1.8 %collective-permute-start.1 = (bf16[64,512]{1,0:T(8,128)(2,1)S(1)}, bf16[64,512]{1,0:T(8,128)(2,1)S(1)}, u32[]{:S(2)}, u32[]{:S(2)}) collective-permute-start(bf16[64,512]{1,0:T(8,128)(2,1)S(1)} %get-tuple-element.46), channel_id=1, source_target_pairs={{0,16},{16,0},{1,17},{17,1},{2,18},{18,2},{3,19},{19,3},{4,20},{20... | collective-permute-start | bytes 196616 | tf_op jit(solution)/shard_map/ppermute | solution.py:197
  10.5 1.9 %pack.1 = (bf16[4,80,128]{2,1,0:T(8,128)(2,1)}, bf16[4,80,128]{2,1,0:T(8,128)(2,1)}, bf16[4,80,128]{2,1,0:T(8,128)(2,1)}, bf16[4,80,128]{2,1,0:T(8,128)(2,1)}) custom-call(bf16[1024,256]{1,0:T(8,128)(2,1)} %bitcast.13, bf16[256,256]{1,0:T(8,128)(2,1)} %bitcast.16), custom_call_target="tpu_custom_call" | custom-call | tf_op jit(solution)/shard_map/pack/pallas_call | solution.py:205
  12.5 1.6 %collective-permute-start.14 = (bf16[4,80,128]{2,1,0:T(8,128)(2,1)}, bf16[4,80,128]{2,1,0:T(8,128)(2,1)S(1)}, u32[]{:S(2)}, u32[]{:S(2)}) collective-permute-start(bf16[4,80,128]{2,1,0:T(8,128)(2,1)} %get-tuple-element.37), channel_id=1, source_target_pairs={{0,2},{1,3},{2,0},{3,1},{4,6},{5,7},{6,4},{7,5},{8,10},{9,11},{10,... | collective-permute-start | bytes 245768 | tf_op jit(solution)/shard_map/ppermute | solution.py:194
  14.9 2.9 %collective-permute-done.14.refs_2_ = bf16[4,80,128]{2,1,0:T(8,128)(2,1)S(1)} collective-permute-done((bf16[4,80,128]{2,1,0:T(8,128)(2,1)}, bf16[4,80,128]{2,1,0:T(8,128)(2,1)S(1)}, u32[]{:S(2)}, u32[]{:S(2)}) %collective-permute-start.14) | collective-permute-done | bytes 81952 | tf_op jit(solution)/shard_map/ppermute | solution.py:194
  17.8 1.2 %collective-permute-done.15.refs_3_ = bf16[4,80,128]{2,1,0:T(8,128)(2,1)S(1)} collective-permute-done((bf16[4,80,128]{2,1,0:T(8,128)(2,1)}, bf16[4,80,128]{2,1,0:T(8,128)(2,1)S(1)}, u32[]{:S(2)}, u32[]{:S(2)}) %collective-permute-start.15) | collective-permute-done | bytes 81952 | tf_op jit(solution)/shard_map/ppermute | solution.py:194
  19.0 0.6 copy-done.8
  19.6 1.7 %turn.3 = (bf16[4,80,128]{2,1,0:T(8,128)(2,1)}, bf16[4,80,128]{2,1,0:T(8,128)(2,1)}, bf16[4,80,128]{2,1,0:T(8,128)(2,1)}, bf16[4,80,128]{2,1,0:T(8,128)(2,1)}) custom-call(bf16[4,80,128]{2,1,0:T(8,128)(2,1)} %get-tuple-element.35.refs_0_, bf16[4,80,128]{2,1,0:T(8,128)(2,1)} %copy-done.6, bf16[4,80,128]{2,1,0:T(8,128)(2,1)} %copy-done.7, ...), custom_call_target="tpu_custom_call" | custom-call | tf_op jit(solution)/shard_map/turn/pallas_call | solution.py:66
  21.8 3.3 %collective-permute-start.17 = (bf16[4,80,128]{2,1,0:T(8,128)(2,1)}, bf16[4,80,128]{2,1,0:T(8,128)(2,1)S(1)}, u32[]{:S(2)}, u32[]{:S(2)}) collective-permute-start(bf16[4,80,128]{2,1,0:T(8,128)(2,1)} %get-tuple-element.41), channel_id=1, source_target_pairs={{0,8},{1,9},{2,10},{3,11},{4,12},{5,13},{6,14},{7,15},{8,0},{9,1},... | collective-permute-start | bytes 245768 | tf_op jit(solution)/shard_map/ppermute | solution.py:194
  25.1 0.6 collective-permute-start.18
  25.8 0.6 collective-permute-done.16.refs_1_
  26.4 5.7 %collective-permute-done.17.refs_2_ = bf16[4,80,128]{2,1,0:T(8,128)(2,1)S(1)} collective-permute-done((bf16[4,80,128]{2,1,0:T(8,128)(2,1)}, bf16[4,80,128]{2,1,0:T(8,128)(2,1)S(1)}, u32[]{:S(2)}, u32[]{:S(2)}) %collective-permute-start.17) | collective-permute-done | bytes 81952 | tf_op jit(solution)/shard_map/ppermute | solution.py:194
  32.1 0.6 copy-done.10
  32.7 1.8 %pick.1 = (bf16[3,80,128]{2,1,0:T(8,128)(2,1)}, bf16[3,80,128]{2,1,0:T(8,128)(2,1)}) custom-call(s32[6]{0:T(128)} %owners.1, bf16[4,80,128]{2,1,0:T(8,128)(2,1)} %get-tuple-element.39.refs_0_, bf16[4,80,128]{2,1,0:T(8,128)(2,1)} %copy-done.9, bf16[4,80,128]{2,1,0:T(8,128)(2,1)} %copy-done.10, bf16[4,80,128]{2,1,0:T(8,128)(2,1)} %copy-done.11), custom_call_target="tpu_custom_call" | custom-call | tf_op jit(solution)/shard_map/pick/pallas_call | solution.py:219
  34.5 2.4 %collective-permute-start.21 = (bf16[3,80,128]{2,1,0:T(8,128)(2,1)}, bf16[3,80,128]{2,1,0:T(8,128)(2,1)S(1)}, u32[]{:S(2)}, u32[]{:S(2)}) collective-permute-start(bf16[3,80,128]{2,1,0:T(8,128)(2,1)} %get-tuple-element.43), channel_id=1, source_target_pairs={{0,12},{1,13},{2,14},{3,15},{4,8},{5,9},{6,10},{7,11},{8,4},{9,5},... | collective-permute-start | bytes 184328 | tf_op jit(solution)/shard_map/ppermute | solution.py:194
  36.9 0.9 collective-permute-start.20
  37.8 1.1 %collective-permute-start.19 = (bf16[3,80,128]{2,1,0:T(8,128)(2,1)}, bf16[3,80,128]{2,1,0:T(8,128)(2,1)S(1)}, u32[]{:S(2)}, u32[]{:S(2)}) collective-permute-start(bf16[3,80,128]{2,1,0:T(8,128)(2,1)} %get-tuple-element.43), channel_id=1, source_target_pairs={{0,4},{1,5},{2,6},{3,7},{4,0},{5,1},{6,2},{7,3},{8,12},{9,13},{10,... | collective-permute-start | bytes 184328 | tf_op jit(solution)/shard_map/ppermute | solution.py:194
  38.9 2.4 %collective-permute-start.31 = (bf16[3,80,128]{2,1,0:T(8,128)(2,1)}, bf16[3,80,128]{2,1,0:T(8,128)(2,1)S(1)}, u32[]{:S(2)}, u32[]{:S(2)}) collective-permute-start(bf16[3,80,128]{2,1,0:T(8,128)(2,1)} %get-tuple-element.44), channel_id=1, source_target_pairs={{0,12},{1,13},{2,14},{3,15},{4,8},{5,9},{6,10},{7,11},{8,4},{9,5},... | collective-permute-start | bytes 184328 | tf_op jit(solution)/shard_map/ppermute | solution.py:194
  41.4 2.0 %collective-permute-start.29 = (bf16[3,80,128]{2,1,0:T(8,128)(2,1)S(1)}, bf16[3,80,128]{2,1,0:T(8,128)(2,1)S(1)}, u32[]{:S(2)}, u32[]{:S(2)}) collective-permute-start(bf16[3,80,128]{2,1,0:T(8,128)(2,1)S(1)} %copy-done.12), channel_id=1, source_target_pairs={{0,4},{1,5},{2,6},{3,7},{4,0},{5,1},{6,2},{7,3},{8,12},{9,13},{10,... | collective-permute-start | bytes 184328 | tf_op jit(solution)/shard_map/ppermute | solution.py:194
  43.4 3.4 %collective-permute-done.20 = bf16[3,80,128]{2,1,0:T(8,128)(2,1)S(1)} collective-permute-done((bf16[3,80,128]{2,1,0:T(8,128)(2,1)}, bf16[3,80,128]{2,1,0:T(8,128)(2,1)S(1)}, u32[]{:S(2)}, u32[]{:S(2)}) %collective-permute-start.20) | collective-permute-done | bytes 61472 | tf_op jit(solution)/shard_map/ppermute | solution.py:194
  46.7 1.3 %collective-permute-start.4 = (bf16[4,64,512]{2,1,0:T(8,128)(2,1)S(1)}, bf16[4,64,512]{2,1,0:T(8,128)(2,1)S(1)}, u32[]{:S(2)}, u32[]{:S(2)}) collective-permute-start(bf16[4,64,512]{2,1,0:T(8,128)(2,1)S(1)} %pad_maximum_fusion.refs_0_), channel_id=1, source_target_pairs={{0,2},{1,3},{2,0},{3,1},{4,6},{5,7},{6,4},{7,5},{8,10},{9,11},{10,... | collective-permute-start | bytes 786440 | tf_op jit(solution)/shard_map/ppermute | solution.py:194
  48.1 0.6 collective-permute-start.22
  48.8 1.6 %collective-permute-start.32 = (bf16[4,3,80,128]{3,2,1,0:T(8,128)(2,1)S(1)}, bf16[4,3,80,128]{3,2,1,0:T(8,128)(2,1)S(1)}, u32[]{:S(2)}, u32[]{:S(2)}) collective-permute-start(bf16[4,3,80,128]{3,2,1,0:T(8,128)(2,1)S(1)} %pad_maximum_fusion.2.refs_1_), channel_id=1, source_target_pairs={{0,16},{16,0},{1,17},{17,1},{2,18},{18,2},{3,19},{19,3},{4,20},{20... | collective-permute-start | bytes 737288 | tf_op jit(solution)/shard_map/ppermute | solution.py:197
  50.4 0.7 collective-permute-start.23
  51.0 1.3 %collective-permute-start.33 = (bf16[4,3,80,128]{3,2,1,0:T(8,128)(2,1)S(1)}, bf16[4,3,80,128]{3,2,1,0:T(8,128)(2,1)S(1)}, u32[]{:S(2)}, u32[]{:S(2)}) collective-permute-start(bf16[4,3,80,128]{3,2,1,0:T(8,128)(2,1)S(1)} %pad_maximum_fusion.2.refs_1_), channel_id=1, source_target_pairs={{0,2},{1,3},{2,0},{3,1},{4,6},{5,7},{6,4},{7,5},{8,10},{9,11},{10,... | collective-permute-start | bytes 737288 | tf_op jit(solution)/shard_map/ppermute | solution.py:194
  52.4 3.6 %collective-permute-done.22 = bf16[4,3,80,128]{3,2,1,0:T(8,128)(2,1)S(1)} collective-permute-done((bf16[4,3,80,128]{3,2,1,0:T(8,128)(2,1)S(1)}, bf16[4,3,80,128]{3,2,1,0:T(8,128)(2,1)S(1)}, u32[]{:S(2)}, u32[]{:S(2)}) %collective-permute-start.22) | collective-permute-done | bytes 245792 | tf_op jit(solution)/shard_map/ppermute | solution.py:197
  56.5 2.1 %collective-permute-done.32 = bf16[4,3,80,128]{3,2,1,0:T(8,128)(2,1)S(1)} collective-permute-done((bf16[4,3,80,128]{3,2,1,0:T(8,128)(2,1)S(1)}, bf16[4,3,80,128]{3,2,1,0:T(8,128)(2,1)S(1)}, u32[]{:S(2)}, u32[]{:S(2)}) %collective-permute-start.32) | collective-permute-done | bytes 245792 | tf_op jit(solution)/shard_map/ppermute | solution.py:197
  58.6 1.8 %collective-permute-start.24 = (bf16[2,3,80,128]{3,2,1,0:T(8,128)(2,1)S(1)}, bf16[2,3,80,128]{3,2,1,0:T(8,128)(2,1)S(1)}, u32[]{:S(2)}, u32[]{:S(2)}) collective-permute-start(bf16[2,3,80,128]{3,2,1,0:T(8,128)(2,1)S(1)} %slice.16), channel_id=1, source_target_pairs={{0,2},{1,3},{2,0},{3,1},{4,6},{5,7},{6,4},{7,5},{8,10},{9,11},{10,... | collective-permute-start | bytes 368648 | tf_op jit(solution)/shard_map/ppermute | solution.py:194
  60.5 0.9 collective-permute-start.34
  62.1 3.7 %collective-permute-done.33 = bf16[4,3,80,128]{3,2,1,0:T(8,128)(2,1)S(1)} collective-permute-done((bf16[4,3,80,128]{3,2,1,0:T(8,128)(2,1)S(1)}, bf16[4,3,80,128]{3,2,1,0:T(8,128)(2,1)S(1)}, u32[]{:S(2)}, u32[]{:S(2)}) %collective-permute-start.33) | collective-permute-done | bytes 245792 | tf_op jit(solution)/shard_map/ppermute | solution.py:194
  65.8 0.7 slice.19
  66.5 3.2 %collective-permute-done.6.refs_1_ = f32[16,4,128]{2,1,0:T(4,128)S(1)} collective-permute-done((f32[16,4,128]{2,1,0:T(4,128)S(1)}, f32[16,4,128]{2,1,0:T(4,128)S(1)}, u32[]{:S(2)}, u32[]{:S(2)}) %collective-permute-start.6) | collective-permute-done | bytes 32800 | tf_op jit(solution)/shard_map/ppermute | solution.py:197
  69.7 0.6 copy-done.14
  70.3 1.4 %add.2 = (f32[4,4,128]{2,1,0:T(4,128)}, f32[4,4,128]{2,1,0:T(4,128)}, f32[4,4,128]{2,1,0:T(4,128)}, f32[4,4,128]{2,1,0:T(4,128)}) custom-call(f32[16,4,128]{2,1,0:T(4,128)} %copy-done.1, f32[16,4,128]{2,1,0:T(4,128)} %copy-done.14), custom_call_target="tpu_custom_call" | custom-call | tf_op jit(solution)/shard_map/add/pallas_call | solution.py:258
  71.7 2.4 %collective-permute-start.8 = (f32[4,4,128]{2,1,0:T(4,128)}, f32[4,4,128]{2,1,0:T(4,128)S(1)}, u32[]{:S(2)}, u32[]{:S(2)}) collective-permute-start(f32[4,4,128]{2,1,0:T(4,128)} %get-tuple-element.29), channel_id=1, source_target_pairs={{0,8},{1,9},{2,10},{3,11},{4,12},{5,13},{6,14},{7,15},{8,0},{9,1},... | collective-permute-start | bytes 24584 | tf_op jit(solution)/shard_map/ppermute | solution.py:194
  74.1 0.7 copy-done.4
  74.8 1.9 %collective-permute-start.9 = (f32[4,4,128]{2,1,0:T(4,128)}, f32[4,4,128]{2,1,0:T(4,128)S(1)}, u32[]{:S(2)}, u32[]{:S(2)}) collective-permute-start(f32[4,4,128]{2,1,0:T(4,128)} %get-tuple-element.30), channel_id=1, source_target_pairs={{0,12},{1,13},{2,14},{3,15},{4,8},{5,9},{6,10},{7,11},{8,4},{9,5},... | collective-permute-start | bytes 24584 | tf_op jit(solution)/shard_map/ppermute | solution.py:194
  76.9 3.5 %collective-permute-done.9.refs_3_ = f32[4,4,128]{2,1,0:T(4,128)S(1)} collective-permute-done((f32[4,4,128]{2,1,0:T(4,128)}, f32[4,4,128]{2,1,0:T(4,128)S(1)}, u32[]{:S(2)}, u32[]{:S(2)}) %collective-permute-start.9) | collective-permute-done | bytes 8224 | tf_op jit(solution)/shard_map/ppermute | solution.py:194
  81.0 1.4 %turn.2 = (f32[4,4,128]{2,1,0:T(4,128)}, f32[4,4,128]{2,1,0:T(4,128)}, f32[4,4,128]{2,1,0:T(4,128)}, f32[4,4,128]{2,1,0:T(4,128)}) custom-call(f32[4,4,128]{2,1,0:T(4,128)} %get-tuple-element.27.refs_0_, f32[4,4,128]{2,1,0:T(4,128)} %copy-done.15, f32[4,4,128]{2,1,0:T(4,128)} %copy-done.16, f32[4,4,128]{2,1,0:T(4,128)} %copy-done.17), custom_call_target="tpu_custom_call" | custom-call | tf_op jit(solution)/shard_map/turn/pallas_call | solution.py:66
  82.5 0.6 collective-permute-start.28
  83.1 1.5 %collective-permute-start.11 = (f32[4,4,128]{2,1,0:T(4,128)S(1)}, f32[4,4,128]{2,1,0:T(4,128)S(1)}, u32[]{:S(2)}, u32[]{:S(2)}) collective-permute-start(f32[4,4,128]{2,1,0:T(4,128)S(1)} %copy-done.19), channel_id=1, source_target_pairs={{0,2},{1,3},{2,0},{3,1},{4,6},{5,7},{6,4},{7,5},{8,10},{9,11},{10,... | collective-permute-start | bytes 24584 | tf_op jit(solution)/shard_map/ppermute | solution.py:194
  85.2 0.9 constant_dynamic-update-slice_fusion.6.refs_3_
  86.1 0.6 collective-permute-done.11.refs_2_
  86.7 1.1 %collective-permute-done.12.refs_3_ = f32[4,4,128]{2,1,0:T(4,128)S(1)} collective-permute-done((f32[4,4,128]{2,1,0:T(4,128)S(1)}, f32[4,4,128]{2,1,0:T(4,128)S(1)}, u32[]{:S(2)}, u32[]{:S(2)}) %collective-permute-start.12) | collective-permute-done | bytes 8224 | tf_op jit(solution)/shard_map/ppermute | solution.py:194
  88.0 2.8 %chain0.1.refs_0_ = f32[8,2048]{1,0:T(8,128)S(1)} custom-call(s32[6]{0:T(128)S(1)} %copy-done.3, f32[4,4,128]{2,1,0:T(4,128)S(1)} %copy-done.2, f32[4,4,128]{2,1,0:T(4,128)S(1)} %collective-permute-done.10.refs_1_, f32[4,4,128]{2,1,0:T(4,128)S(1)} %collective-permute-done.11.refs_2_, f32[4,4,128]{2,1,0:T(4,128)S(1)} %collective-permute-done.12.refs_3_, ...), custom_call_target="tpu_custom_call" | custom-call | tf_op jit(solution)/shard_map/chain0/pallas_call | solution.py:289
  90.8 3.4 %chain1.1 = bf16[4,2048]{1,0:T(4,128)(2,1)} custom-call(s32[6]{0:T(128)S(1)} %copy-done.3, f32[8,2048]{1,0:T(8,128)S(1)} %chain0.1.refs_0_, bf16[4,3,80,128]{3,2,1,0:T(8,128)(2,1)S(1)} %pad_maximum_fusion.2.refs_1_, bf16[8,3,80,128]{3,2,1,0:T(8,128)(2,1)S(1)} %constant_dynamic-update-slice_fusion.4.refs_2_, ...), custom_call_target="tpu_custom_call" | custom-call | tf_op jit(solution)/shard_map/chain1/pallas_call | solution.py:289
  (95 shorter events, 4.4 us)
Async XLA Ops:
  0.0 7.9 %collective-permute-start = (bf16[64,512]{1,0:T(8,128)(2,1)}, bf16[64,512]{1,0:T(8,128)(2,1)S(1)}, u32[]{:S(2)}, u32[]{:S(2)}) collective-permute-start(bf16[64,512]{1,0:T(8,128)(2,1)} %param.7), channel_id=1, source_target_pairs={{0,8},{1,9},{2,10},{3,11},{4,12},{5,13},{6,14},{7,15},{8,0},{9,1},... | collective-permute-start | bytes 196616 | tf_op jit(solution)/shard_map/ppermute | solution.py:194
  8.8 5.6 %collective-permute-start.1 = (bf16[64,512]{1,0:T(8,128)(2,1)S(1)}, bf16[64,512]{1,0:T(8,128)(2,1)S(1)}, u32[]{:S(2)}, u32[]{:S(2)}) collective-permute-start(bf16[64,512]{1,0:T(8,128)(2,1)S(1)} %get-tuple-element.46), channel_id=1, source_target_pairs={{0,16},{16,0},{1,17},{17,1},{2,18},{18,2},{3,19},{19,3},{4,20},{20... | collective-permute-start | bytes 196616 | tf_op jit(solution)/shard_map/ppermute | solution.py:197
  12.4 2.5 %collective-permute-start.13 = (bf16[4,80,128]{2,1,0:T(8,128)(2,1)}, bf16[4,80,128]{2,1,0:T(8,128)(2,1)S(1)}, u32[]{:S(2)}, u32[]{:S(2)}) collective-permute-start(bf16[4,80,128]{2,1,0:T(8,128)(2,1)} %get-tuple-element.36), channel_id=1, source_target_pairs={{0,1},{1,0},{2,3},{3,2},{4,5},{5,4},{6,7},{7,6},{8,9},{9,8},{10,11... | collective-permute-start | bytes 245768 | tf_op jit(solution)/shard_map/ppermute | solution.py:194
  12.5 5.4 %collective-permute-start.14 = (bf16[4,80,128]{2,1,0:T(8,128)(2,1)}, bf16[4,80,128]{2,1,0:T(8,128)(2,1)S(1)}, u32[]{:S(2)}, u32[]{:S(2)}) collective-permute-start(bf16[4,80,128]{2,1,0:T(8,128)(2,1)} %get-tuple-element.37), channel_id=1, source_target_pairs={{0,2},{1,3},{2,0},{3,1},{4,6},{5,7},{6,4},{7,5},{8,10},{9,11},{10,... | collective-permute-start | bytes 245768 | tf_op jit(solution)/shard_map/ppermute | solution.py:194
  14.1 4.9 %collective-permute-start.15 = (bf16[4,80,128]{2,1,0:T(8,128)(2,1)}, bf16[4,80,128]{2,1,0:T(8,128)(2,1)S(1)}, u32[]{:S(2)}, u32[]{:S(2)}) collective-permute-start(bf16[4,80,128]{2,1,0:T(8,128)(2,1)} %get-tuple-element.38), channel_id=1, source_target_pairs={{0,3},{1,2},{2,1},{3,0},{4,7},{5,6},{6,5},{7,4},{8,11},{9,10},{10,... | collective-permute-start | bytes 245768 | tf_op jit(solution)/shard_map/ppermute | solution.py:194
  14.4 26.9 %collective-permute-start.2 = (bf16[2,64,512]{2,1,0:T(8,128)(2,1)S(1)}, bf16[2,64,512]{2,1,0:T(8,128)(2,1)S(1)}, u32[]{:S(2)}, u32[]{:S(2)}) collective-permute-start(bf16[2,64,512]{2,1,0:T(8,128)(2,1)S(1)} %pad_maximum_fusion.3), channel_id=1, source_target_pairs={{0,4},{1,5},{2,6},{3,7},{4,0},{5,1},{6,2},{7,3},{8,12},{9,13},{10,... | collective-permute-start | bytes 393224 | tf_op jit(solution)/shard_map/ppermute | solution.py:194
  14.9 4.1 %copy-start.6 = (bf16[4,80,128]{2,1,0:T(8,128)(2,1)}, bf16[4,80,128]{2,1,0:T(8,128)(2,1)S(1)}, u32[]{:S(2)}) copy-start(bf16[4,80,128]{2,1,0:T(8,128)(2,1)S(1)} %collective-permute-done.13.refs_1_) | copy-start | bytes 245764
  21.4 5.0 %collective-permute-start.16 = (bf16[4,80,128]{2,1,0:T(8,128)(2,1)}, bf16[4,80,128]{2,1,0:T(8,128)(2,1)S(1)}, u32[]{:S(2)}, u32[]{:S(2)}) collective-permute-start(bf16[4,80,128]{2,1,0:T(8,128)(2,1)} %get-tuple-element.40), channel_id=1, source_target_pairs={{0,4},{1,5},{2,6},{3,7},{4,0},{5,1},{6,2},{7,3},{8,12},{9,13},{10,... | collective-permute-start | bytes 245768 | tf_op jit(solution)/shard_map/ppermute | solution.py:194
  21.8 10.2 %collective-permute-start.17 = (bf16[4,80,128]{2,1,0:T(8,128)(2,1)}, bf16[4,80,128]{2,1,0:T(8,128)(2,1)S(1)}, u32[]{:S(2)}, u32[]{:S(2)}) collective-permute-start(bf16[4,80,128]{2,1,0:T(8,128)(2,1)} %get-tuple-element.41), channel_id=1, source_target_pairs={{0,8},{1,9},{2,10},{3,11},{4,12},{5,13},{6,14},{7,15},{8,0},{9,1},... | collective-permute-start | bytes 245768 | tf_op jit(solution)/shard_map/ppermute | solution.py:194
  25.1 7.0 %collective-permute-start.18 = (bf16[4,80,128]{2,1,0:T(8,128)(2,1)}, bf16[4,80,128]{2,1,0:T(8,128)(2,1)S(1)}, u32[]{:S(2)}, u32[]{:S(2)}) collective-permute-start(bf16[4,80,128]{2,1,0:T(8,128)(2,1)} %get-tuple-element.42), channel_id=1, source_target_pairs={{0,12},{1,13},{2,14},{3,15},{4,8},{5,9},{6,10},{7,11},{8,4},{9,5},... | collective-permute-start | bytes 245768 | tf_op jit(solution)/shard_map/ppermute | solution.py:194
  26.4 5.7 %copy-start.9 = (bf16[4,80,128]{2,1,0:T(8,128)(2,1)}, bf16[4,80,128]{2,1,0:T(8,128)(2,1)S(1)}, u32[]{:S(2)}) copy-start(bf16[4,80,128]{2,1,0:T(8,128)(2,1)S(1)} %collective-permute-done.16.refs_1_) | copy-start | bytes 245764
  34.5 6.9 %collective-permute-start.21 = (bf16[3,80,128]{2,1,0:T(8,128)(2,1)}, bf16[3,80,128]{2,1,0:T(8,128)(2,1)S(1)}, u32[]{:S(2)}, u32[]{:S(2)}) collective-permute-start(bf16[3,80,128]{2,1,0:T(8,128)(2,1)} %get-tuple-element.43), channel_id=1, source_target_pairs={{0,12},{1,13},{2,14},{3,15},{4,8},{5,9},{6,10},{7,11},{8,4},{9,5},... | collective-permute-start | bytes 184328 | tf_op jit(solution)/shard_map/ppermute | solution.py:194
  36.9 9.8 %collective-permute-start.20 = (bf16[3,80,128]{2,1,0:T(8,128)(2,1)}, bf16[3,80,128]{2,1,0:T(8,128)(2,1)S(1)}, u32[]{:S(2)}, u32[]{:S(2)}) collective-permute-start(bf16[3,80,128]{2,1,0:T(8,128)(2,1)} %get-tuple-element.43), channel_id=1, source_target_pairs={{0,8},{1,9},{2,10},{3,11},{4,12},{5,13},{6,14},{7,15},{8,0},{9,1},... | collective-permute-start | bytes 184328 | tf_op jit(solution)/shard_map/ppermute | solution.py:194
  37.8 10.3 %collective-permute-start.19 = (bf16[3,80,128]{2,1,0:T(8,128)(2,1)}, bf16[3,80,128]{2,1,0:T(8,128)(2,1)S(1)}, u32[]{:S(2)}, u32[]{:S(2)}) collective-permute-start(bf16[3,80,128]{2,1,0:T(8,128)(2,1)} %get-tuple-element.43), channel_id=1, source_target_pairs={{0,4},{1,5},{2,6},{3,7},{4,0},{5,1},{6,2},{7,3},{8,12},{9,13},{10,... | collective-permute-start | bytes 184328 | tf_op jit(solution)/shard_map/ppermute | solution.py:194
  38.9 9.2 %copy-start.13 = (bf16[3,80,128]{2,1,0:T(8,128)(2,1)S(1)}, bf16[3,80,128]{2,1,0:T(8,128)(2,1)}, u32[]{:S(2)}) copy-start(bf16[3,80,128]{2,1,0:T(8,128)(2,1)} %get-tuple-element.43) | copy-start | bytes 184324
  38.9 9.9 %collective-permute-start.31 = (bf16[3,80,128]{2,1,0:T(8,128)(2,1)}, bf16[3,80,128]{2,1,0:T(8,128)(2,1)S(1)}, u32[]{:S(2)}, u32[]{:S(2)}) collective-permute-start(bf16[3,80,128]{2,1,0:T(8,128)(2,1)} %get-tuple-element.44), channel_id=1, source_target_pairs={{0,12},{1,13},{2,14},{3,15},{4,8},{5,9},{6,10},{7,11},{8,4},{9,5},... | collective-permute-start | bytes 184328 | tf_op jit(solution)/shard_map/ppermute | solution.py:194
  41.3 7.4 %collective-permute-start.30 = (bf16[3,80,128]{2,1,0:T(8,128)(2,1)}, bf16[3,80,128]{2,1,0:T(8,128)(2,1)S(1)}, u32[]{:S(2)}, u32[]{:S(2)}) collective-permute-start(bf16[3,80,128]{2,1,0:T(8,128)(2,1)} %get-tuple-element.44), channel_id=1, source_target_pairs={{0,8},{1,9},{2,10},{3,11},{4,12},{5,13},{6,14},{7,15},{8,0},{9,1},... | collective-permute-start | bytes 184328 | tf_op jit(solution)/shard_map/ppermute | solution.py:194
  41.4 7.4 %collective-permute-start.29 = (bf16[3,80,128]{2,1,0:T(8,128)(2,1)S(1)}, bf16[3,80,128]{2,1,0:T(8,128)(2,1)S(1)}, u32[]{:S(2)}, u32[]{:S(2)}) collective-permute-start(bf16[3,80,128]{2,1,0:T(8,128)(2,1)S(1)} %copy-done.12), channel_id=1, source_target_pairs={{0,4},{1,5},{2,6},{3,7},{4,0},{5,1},{6,2},{7,3},{8,12},{9,13},{10,... | collective-permute-start | bytes 184328 | tf_op jit(solution)/shard_map/ppermute | solution.py:194
  46.7 9.2 %collective-permute-start.4 = (bf16[4,64,512]{2,1,0:T(8,128)(2,1)S(1)}, bf16[4,64,512]{2,1,0:T(8,128)(2,1)S(1)}, u32[]{:S(2)}, u32[]{:S(2)}) collective-permute-start(bf16[4,64,512]{2,1,0:T(8,128)(2,1)S(1)} %pad_maximum_fusion.refs_0_), channel_id=1, source_target_pairs={{0,2},{1,3},{2,0},{3,1},{4,6},{5,7},{6,4},{7,5},{8,10},{9,11},{10,... | collective-permute-start | bytes 786440 | tf_op jit(solution)/shard_map/ppermute | solution.py:194
  48.1 7.8 %collective-permute-start.22 = (bf16[4,3,80,128]{3,2,1,0:T(8,128)(2,1)S(1)}, bf16[4,3,80,128]{3,2,1,0:T(8,128)(2,1)S(1)}, u32[]{:S(2)}, u32[]{:S(2)}) collective-permute-start(bf16[4,3,80,128]{3,2,1,0:T(8,128)(2,1)S(1)} %pad_maximum_fusion.1.refs_4_), channel_id=1, source_target_pairs={{0,16},{16,0},{1,17},{17,1},{2,18},{18,2},{3,19},{19,3},{4,20},{20... | collective-permute-start | bytes 737288 | tf_op jit(solution)/shard_map/ppermute | solution.py:197
  48.8 12.8 %copy-start = (bf16[4096,128]{1,0:T(8,128)(2,1)S(1)}, bf16[4096,128]{1,0:T(8,128)(2,1)}, u32[]{:S(2)}) copy-start(bf16[4096,128]{1,0:T(8,128)(2,1)} %sub.6) | copy-start | bytes 3145732
  48.8 9.8 %collective-permute-start.32 = (bf16[4,3,80,128]{3,2,1,0:T(8,128)(2,1)S(1)}, bf16[4,3,80,128]{3,2,1,0:T(8,128)(2,1)S(1)}, u32[]{:S(2)}, u32[]{:S(2)}) collective-permute-start(bf16[4,3,80,128]{3,2,1,0:T(8,128)(2,1)S(1)} %pad_maximum_fusion.2.refs_1_), channel_id=1, source_target_pairs={{0,16},{16,0},{1,17},{17,1},{2,18},{18,2},{3,19},{19,3},{4,20},{20... | collective-permute-start | bytes 737288 | tf_op jit(solution)/shard_map/ppermute | solution.py:197
  50.4 10.1 %collective-permute-start.23 = (bf16[4,3,80,128]{3,2,1,0:T(8,128)(2,1)S(1)}, bf16[4,3,80,128]{3,2,1,0:T(8,128)(2,1)S(1)}, u32[]{:S(2)}, u32[]{:S(2)}) collective-permute-start(bf16[4,3,80,128]{3,2,1,0:T(8,128)(2,1)S(1)} %pad_maximum_fusion.1.refs_4_), channel_id=1, source_target_pairs={{0,2},{1,3},{2,0},{3,1},{4,6},{5,7},{6,4},{7,5},{8,10},{9,11},{10,... | collective-permute-start | bytes 737288 | tf_op jit(solution)/shard_map/ppermute | solution.py:194
  51.0 14.7 %collective-permute-start.33 = (bf16[4,3,80,128]{3,2,1,0:T(8,128)(2,1)S(1)}, bf16[4,3,80,128]{3,2,1,0:T(8,128)(2,1)S(1)}, u32[]{:S(2)}, u32[]{:S(2)}) collective-permute-start(bf16[4,3,80,128]{3,2,1,0:T(8,128)(2,1)S(1)} %pad_maximum_fusion.2.refs_1_), channel_id=1, source_target_pairs={{0,2},{1,3},{2,0},{3,1},{4,6},{5,7},{6,4},{7,5},{8,10},{9,11},{10,... | collective-permute-start | bytes 737288 | tf_op jit(solution)/shard_map/ppermute | solution.py:194
  55.9 5.5 %collective-permute-start.3 = (bf16[4,64,512]{2,1,0:T(8,128)(2,1)S(1)}, bf16[4,64,512]{2,1,0:T(8,128)(2,1)S(1)}, u32[]{:S(2)}, u32[]{:S(2)}) collective-permute-start(bf16[4,64,512]{2,1,0:T(8,128)(2,1)S(1)} %pad_maximum_fusion.refs_0_), channel_id=1, source_target_pairs={{0,1},{1,0},{2,3},{3,2},{4,5},{5,4},{6,7},{7,6},{8,9},{9,8},{10,11... | collective-permute-start | bytes 786440 | tf_op jit(solution)/shard_map/ppermute | solution.py:194
  56.0 5.6 %collective-permute-start.5 = (bf16[4,64,512]{2,1,0:T(8,128)(2,1)S(1)}, bf16[4,64,512]{2,1,0:T(8,128)(2,1)S(1)}, u32[]{:S(2)}, u32[]{:S(2)}) collective-permute-start(bf16[4,64,512]{2,1,0:T(8,128)(2,1)S(1)} %collective-permute-done.4.refs_2_), channel_id=1, source_target_pairs={{0,1},{1,0},{2,3},{3,2},{4,5},{5,4},{6,7},{7,6},{8,9},{9,8},{10,11... | collective-permute-start | bytes 786440 | tf_op jit(solution)/shard_map/ppermute | solution.py:194
  58.6 13.1 %collective-permute-start.24 = (bf16[2,3,80,128]{3,2,1,0:T(8,128)(2,1)S(1)}, bf16[2,3,80,128]{3,2,1,0:T(8,128)(2,1)S(1)}, u32[]{:S(2)}, u32[]{:S(2)}) collective-permute-start(bf16[2,3,80,128]{3,2,1,0:T(8,128)(2,1)S(1)} %slice.16), channel_id=1, source_target_pairs={{0,2},{1,3},{2,0},{3,1},{4,6},{5,7},{6,4},{7,5},{8,10},{9,11},{10,... | collective-permute-start | bytes 368648 | tf_op jit(solution)/shard_map/ppermute | solution.py:194
  60.5 13.6 %collective-permute-start.34 = (bf16[2,3,80,128]{3,2,1,0:T(8,128)(2,1)S(1)}, bf16[2,3,80,128]{3,2,1,0:T(8,128)(2,1)S(1)}, u32[]{:S(2)}, u32[]{:S(2)}) collective-permute-start(bf16[2,3,80,128]{3,2,1,0:T(8,128)(2,1)S(1)} %slice.18), channel_id=1, source_target_pairs={{0,2},{1,3},{2,0},{3,1},{4,6},{5,7},{6,4},{7,5},{8,10},{9,11},{10,... | collective-permute-start | bytes 368648 | tf_op jit(solution)/shard_map/ppermute | solution.py:194
  61.4 21.1 %collective-permute-start.26 = (bf16[4,3,80,128]{3,2,1,0:T(8,128)(2,1)S(1)}, bf16[4,3,80,128]{3,2,1,0:T(8,128)(2,1)S(1)}, u32[]{:S(2)}, u32[]{:S(2)}) collective-permute-start(bf16[4,3,80,128]{3,2,1,0:T(8,128)(2,1)S(1)} %pad_maximum_fusion.1.refs_4_), channel_id=1, source_target_pairs={{0,1},{1,0},{2,3},{3,2},{4,5},{5,4},{6,7},{7,6},{8,9},{9,8},{10,11... | collective-permute-start | bytes 737288 | tf_op jit(solution)/shard_map/ppermute | solution.py:194
  61.5 20.9 %collective-permute-start.25 = (bf16[2,3,80,128]{3,2,1,0:T(8,128)(2,1)S(1)}, bf16[2,3,80,128]{3,2,1,0:T(8,128)(2,1)S(1)}, u32[]{:S(2)}, u32[]{:S(2)}) collective-permute-start(bf16[2,3,80,128]{3,2,1,0:T(8,128)(2,1)S(1)} %slice.17), channel_id=1, source_target_pairs={{0,16},{16,0},{1,17},{17,1},{2,18},{18,2},{3,19},{19,3},{4,20},{20... | collective-permute-start | bytes 368648 | tf_op jit(solution)/shard_map/ppermute | solution.py:197
  62.1 3.7 %copy-start.1 = (f32[16,4,128]{2,1,0:T(4,128)}, f32[16,4,128]{2,1,0:T(4,128)S(1)}, u32[]{:S(2)}) copy-start(f32[16,4,128]{2,1,0:T(4,128)S(1)} %get-tuple-element.25.refs_0_) | copy-start | bytes 98308
  65.7 3.9 %collective-permute-start.6 = (f32[16,4,128]{2,1,0:T(4,128)S(1)}, f32[16,4,128]{2,1,0:T(4,128)S(1)}, u32[]{:S(2)}, u32[]{:S(2)}) collective-permute-start(f32[16,4,128]{2,1,0:T(4,128)S(1)} %get-tuple-element.26), channel_id=1, source_target_pairs={{0,16},{16,0},{1,17},{17,1},{2,18},{18,2},{3,19},{19,3},{4,20},{20... | collective-permute-start | bytes 98312 | tf_op jit(solution)/shard_map/ppermute | solution.py:197
  71.7 5.1 %collective-permute-start.7 = (f32[4,4,128]{2,1,0:T(4,128)}, f32[4,4,128]{2,1,0:T(4,128)S(1)}, u32[]{:S(2)}, u32[]{:S(2)}) collective-permute-start(f32[4,4,128]{2,1,0:T(4,128)} %get-tuple-element.28), channel_id=1, source_target_pairs={{0,4},{1,5},{2,6},{3,7},{4,0},{5,1},{6,2},{7,3},{8,12},{9,13},{10,... | collective-permute-start | bytes 24584 | tf_op jit(solution)/shard_map/ppermute | solution.py:194
  71.7 5.2 %collective-permute-start.8 = (f32[4,4,128]{2,1,0:T(4,128)}, f32[4,4,128]{2,1,0:T(4,128)S(1)}, u32[]{:S(2)}, u32[]{:S(2)}) collective-permute-start(f32[4,4,128]{2,1,0:T(4,128)} %get-tuple-element.29), channel_id=1, source_target_pairs={{0,8},{1,9},{2,10},{3,11},{4,12},{5,13},{6,14},{7,15},{8,0},{9,1},... | collective-permute-start | bytes 24584 | tf_op jit(solution)/shard_map/ppermute | solution.py:194
  74.8 5.7 %collective-permute-start.9 = (f32[4,4,128]{2,1,0:T(4,128)}, f32[4,4,128]{2,1,0:T(4,128)S(1)}, u32[]{:S(2)}, u32[]{:S(2)}) collective-permute-start(f32[4,4,128]{2,1,0:T(4,128)} %get-tuple-element.30), channel_id=1, source_target_pairs={{0,12},{1,13},{2,14},{3,15},{4,8},{5,9},{6,10},{7,11},{8,4},{9,5},... | collective-permute-start | bytes 24584 | tf_op jit(solution)/shard_map/ppermute | solution.py:194
  76.7 3.7 %copy-start.5 = (bf16[2,3,80,128]{3,2,1,0:T(8,128)(2,1)S(1)}, bf16[2,3,80,128]{3,2,1,0:T(8,128)(2,1)}, u32[]{:S(2)}) copy-start(bf16[2,3,80,128]{3,2,1,0:T(8,128)(2,1)} %copy-done.4) | copy-start | bytes 368644
  76.7 3.7 %copy-start.15 = (f32[4,4,128]{2,1,0:T(4,128)}, f32[4,4,128]{2,1,0:T(4,128)S(1)}, u32[]{:S(2)}) copy-start(f32[4,4,128]{2,1,0:T(4,128)S(1)} %collective-permute-done.7.refs_1_) | copy-start | bytes 24580
  76.7 11.2 %collective-permute-start.27 = (bf16[8,3,80,128]{3,2,1,0:T(8,128)(2,1)S(1)}, bf16[8,3,80,128]{3,2,1,0:T(8,128)(2,1)S(1)}, u32[]{:S(2)}, u32[]{:S(2)}) collective-permute-start(bf16[8,3,80,128]{3,2,1,0:T(8,128)(2,1)S(1)} %constant_dynamic-update-slice_fusion.refs_5_), channel_id=1, source_target_pairs={{0,1},{1,0},{2,3},{3,2},{4,5},{5,4},{6,7},{7,6},{8,9},{9,8},{10,11... | collective-permute-start | bytes 1474568 | tf_op jit(solution)/shard_map/ppermute | solution.py:194
  76.8 3.6 %copy-start.16 = (f32[4,4,128]{2,1,0:T(4,128)}, f32[4,4,128]{2,1,0:T(4,128)S(1)}, u32[]{:S(2)}) copy-start(f32[4,4,128]{2,1,0:T(4,128)S(1)} %collective-permute-done.8.refs_2_) | copy-start | bytes 24580
  76.8 6.2 %collective-permute-start.35 = (bf16[2,3,80,128]{3,2,1,0:T(8,128)(2,1)}, bf16[2,3,80,128]{3,2,1,0:T(8,128)(2,1)}, u32[]{:S(2)}, u32[]{:S(2)}) collective-permute-start(bf16[2,3,80,128]{3,2,1,0:T(8,128)(2,1)} %slice.19), channel_id=1, source_target_pairs={{0,16},{16,0},{1,17},{17,1},{2,18},{18,2},{3,19},{19,3},{4,20},{20... | collective-permute-start | bytes 368648 | tf_op jit(solution)/shard_map/ppermute | solution.py:197
  80.4 10.3 %collective-permute-start.37 = (bf16[8,3,80,128]{3,2,1,0:T(8,128)(2,1)S(1)}, bf16[8,3,80,128]{3,2,1,0:T(8,128)(2,1)S(1)}, u32[]{:S(2)}, u32[]{:S(2)}) collective-permute-start(bf16[8,3,80,128]{3,2,1,0:T(8,128)(2,1)S(1)} %constant_dynamic-update-slice_fusion.4.refs_2_), channel_id=1, source_target_pairs={{0,1},{1,0},{2,3},{3,2},{4,5},{5,4},{6,7},{7,6},{8,9},{9,8},{10,11... | collective-permute-start | bytes 1474568 | tf_op jit(solution)/shard_map/ppermute | solution.py:194
  82.4 2.2 %collective-permute-start.10 = (f32[4,4,128]{2,1,0:T(4,128)}, f32[4,4,128]{2,1,0:T(4,128)S(1)}, u32[]{:S(2)}, u32[]{:S(2)}) collective-permute-start(f32[4,4,128]{2,1,0:T(4,128)} %get-tuple-element.32), channel_id=1, source_target_pairs={{0,1},{1,0},{2,3},{3,2},{4,5},{5,4},{6,7},{7,6},{8,9},{9,8},{10,11... | collective-permute-start | bytes 24584 | tf_op jit(solution)/shard_map/ppermute | solution.py:194
  82.5 5.4 %collective-permute-start.28 = (bf16[4,3,80,128]{3,2,1,0:T(8,128)(2,1)S(1)}, bf16[4,3,80,128]{3,2,1,0:T(8,128)(2,1)S(1)}, u32[]{:S(2)}, u32[]{:S(2)}) collective-permute-start(bf16[4,3,80,128]{3,2,1,0:T(8,128)(2,1)S(1)} %constant_dynamic-update-slice_fusion.2.refs_6_), channel_id=1, source_target_pairs={{0,1},{1,0},{2,3},{3,2},{4,5},{5,4},{6,7},{7,6},{8,9},{9,8},{10,11... | collective-permute-start | bytes 737288 | tf_op jit(solution)/shard_map/ppermute | solution.py:194
  83.1 3.7 %collective-permute-start.11 = (f32[4,4,128]{2,1,0:T(4,128)S(1)}, f32[4,4,128]{2,1,0:T(4,128)S(1)}, u32[]{:S(2)}, u32[]{:S(2)}) collective-permute-start(f32[4,4,128]{2,1,0:T(4,128)S(1)} %copy-done.19), channel_id=1, source_target_pairs={{0,2},{1,3},{2,0},{3,1},{4,6},{5,7},{6,4},{7,5},{8,10},{9,11},{10,... | collective-permute-start | bytes 24584 | tf_op jit(solution)/shard_map/ppermute | solution.py:194
  84.6 3.3 %copy-start.2 = (f32[4,4,128]{2,1,0:T(4,128)S(1)}, f32[4,4,128]{2,1,0:T(4,128)}, u32[]{:S(2)}) copy-start(f32[4,4,128]{2,1,0:T(4,128)} %get-tuple-element.31.refs_0_) | copy-start | bytes 24580
  84.6 3.2 %collective-permute-start.12 = (f32[4,4,128]{2,1,0:T(4,128)S(1)}, f32[4,4,128]{2,1,0:T(4,128)S(1)}, u32[]{:S(2)}, u32[]{:S(2)}) collective-permute-start(f32[4,4,128]{2,1,0:T(4,128)S(1)} %copy-done.18), channel_id=1, source_target_pairs={{0,3},{1,2},{2,1},{3,0},{4,7},{5,6},{6,5},{7,4},{8,11},{9,10},{10,... | collective-permute-start | bytes 24584 | tf_op jit(solution)/shard_map/ppermute | solution.py:194
  86.7 4.0 %collective-permute-start.36 = (bf16[4,3,80,128]{3,2,1,0:T(8,128)(2,1)S(1)}, bf16[4,3,80,128]{3,2,1,0:T(8,128)(2,1)S(1)}, u32[]{:S(2)}, u32[]{:S(2)}) collective-permute-start(bf16[4,3,80,128]{3,2,1,0:T(8,128)(2,1)S(1)} %pad_maximum_fusion.2.refs_1_), channel_id=1, source_target_pairs={{0,1},{1,0},{2,3},{3,2},{4,5},{5,4},{6,7},{7,6},{8,9},{9,8},{10,11... | collective-permute-start | bytes 737288 | tf_op jit(solution)/shard_map/ppermute | solution.py:194
  87.8 2.9 %collective-permute-start.38 = (bf16[4,3,80,128]{3,2,1,0:T(8,128)(2,1)S(1)}, bf16[4,3,80,128]{3,2,1,0:T(8,128)(2,1)S(1)}, u32[]{:S(2)}, u32[]{:S(2)}) collective-permute-start(bf16[4,3,80,128]{3,2,1,0:T(8,128)(2,1)S(1)} %constant_dynamic-update-slice_fusion.6.refs_3_), channel_id=1, source_target_pairs={{0,1},{1,0},{2,3},{3,2},{4,5},{5,4},{6,7},{7,6},{8,9},{9,8},{10,11... | collective-permute-start | bytes 737288 | tf_op jit(solution)/shard_map/ppermute | solution.py:194
  (11 other events, 12.2 us)

commit v5 on v4

v5 whole, which is shorter than its diff:
```python
import functools

import jax
import jax.numpy as jnp
from jax import lax
from jax.experimental import pallas as pl
from jax.experimental.pallas import tpu as pltpu
from jax.sharding import PartitionSpec as P

GROUPS = 6
NEAR = 4
FAR = 4
SLICES = 2 * NEAR * FAR
LANES = 128
VMEM = pl.BlockSpec(memory_space=pltpu.VMEM)
SMEM = pl.BlockSpec(memory_space=pltpu.SMEM)
ANY = pl.BlockSpec(memory_space=pl.ANY)
LIMIT = pltpu.CompilerParams(vmem_limit_bytes=40 * 1024 * 1024)


def slice_index():
    row, col = lax.axis_index("row"), lax.axis_index("col")
    return lax.rem(row, 2) * (NEAR * FAR) + lax.rem(col, NEAR * FAR)


def aligned(index, size):
    return pl.ds(pl.multiple_of(index * size, size), size)


def pack_kernel(basis_hbm, factor_hbm, out, basis, factor, sems):
    half = basis.shape[0]
    row_bit = lax.rem(lax.axis_index("row"), 2)
    first = pltpu.make_async_copy(basis_hbm.at[aligned(row_bit, half)], basis, sems.at[0])
    second = pltpu.make_async_copy(factor_hbm, factor, sems.at[1])
    first.start()
    second.start()
    first.wait()
    second.wait()
    pv = half // (NEAR * FAR)
    lanes = basis.shape[1] // LANES
    tall = factor.shape[0] * lanes // SLICES
    for col in range(out.shape[0]):
        c = col % (NEAR * FAR)
        e = row_bit * (NEAR * FAR) + c
        for k in range(lanes):
            out[col, k * pv : (k + 1) * pv, :] = basis[
                c * pv : (c + 1) * pv, k * LANES : (k + 1) * LANES
            ]
        out[col, lanes * pv :, :] = factor[
            aligned(e // lanes, tall), (c % lanes) * LANES : (c % lanes + 1) * LANES
        ]


def pick_kernel(owners, held, out):
    for group in range(GROUPS):
        out[group] = held[owners[group]]


def merge_kernel(rows, cols, sub, *refs):
    held, total = refs[:NEAR], refs[NEAR]
    row, col = lax.axis_index("row"), lax.axis_index("col")
    share = cols // rows
    deep, tall = held[0].shape[2], held[0].shape[1]
    total[...] = jnp.zeros_like(total)
    for near, ref in enumerate(held):
        for index in range(ref.shape[0]):
            far, row_mask = index // rows, index % rows
            j = jnp.bitwise_xor(lax.rem(col, share), far * NEAR + near)
            part = jnp.dot(ref[index], sub[aligned(j, deep), :], preferred_element_type=jnp.float32)
            at = aligned(jnp.bitwise_xor(row, row_mask), tall)
            total[at, :] = total[at, :] + part


def two_terms(x):
    high = x.astype(jnp.bfloat16)
    low = (x - high.astype(jnp.float32)).astype(jnp.bfloat16)
    return jnp.concatenate([high, low], 0)


def both(products):
    half = products.shape[0] // 2
    return products[:half] + products[half:]


def chain_kernel(cols, masks, offsets, start, *refs):
    held, (out, basis_all, factor_all) = refs[: len(masks)], refs[len(masks) :]
    mine = slice_index()
    lanes = basis_all.shape[2] // LANES
    pv = basis_all.shape[1] // SLICES
    tall = factor_all.shape[1] * lanes // SLICES
    for own_masks, ref in zip(masks, held):
        for index, mask in enumerate(own_masks):
            e = jnp.bitwise_xor(mine, mask)
            for k in range(lanes):
                basis_all[:, aligned(e, pv), k * LANES : (k + 1) * LANES] = ref[
                    index, :, k * pv : (k + 1) * pv, :
                ]
            factor_all[:, aligned(e // lanes, tall), aligned(lax.rem(e, lanes), LANES)] = ref[
                index, :, lanes * pv :, :
            ]
    n, each, width = start.shape
    pieces = start[...].reshape(n // cols, cols, each, width).sum(0)
    x = jnp.concatenate([pieces[c] for c in range(cols)], 1)
    x = jnp.concatenate([x] + [jnp.zeros_like(x)] * (8 // each - 1), 0)
    wide = x.shape[1]
    group_rows = basis_all.shape[1]
    before = jnp.int32(0)
    for slot in range(GROUPS):
        offset = offsets[slot]
        x = pltpu.roll(x, lax.rem(before - offset + wide, wide), 1)
        before = offset
        block = x[:, :group_rows]
        weights = both(
            jnp.dot(two_terms(block), basis_all[slot], preferred_element_type=jnp.float32)
        )
        scaled = both(
            lax.dot_general(
                two_terms(weights), factor_all[slot], (((1,), (1,)), ((), ())),
                preferred_element_type=jnp.float32,
            )
        )
        change = both(
            lax.dot_general(
                two_terms(scaled), basis_all[slot], (((1,), (1,)), ((), ())),
                preferred_element_type=jnp.float32,
            )
        )
        x = jnp.concatenate([block - change, x[:, group_rows:]], 1)
    x = pltpu.roll(x, before, 1)
    out[...] = x[: out.shape[0]].astype(out.dtype)


def local(rows, cols, sub_vectors, merge_factor, reflectors, wy_factors, owners, offsets):
    share = cols // rows

    def over_col(x, mask):
        return lax.ppermute(x, "col", [(c, c ^ mask) for c in range(cols)])

    def over_row(x, mask):
        return lax.ppermute(x, "row", [(r, r ^ mask) for r in range(rows)])

    basis, factor = reflectors[0], wy_factors[0]
    group_rows, reflect = basis.shape
    dtype = basis.dtype
    lanes = reflect // LANES
    tall = (group_rows + reflect) * lanes // SLICES

    packed = pl.pallas_call(
        pack_kernel,
        out_shape=jax.ShapeDtypeStruct((cols, tall, LANES), dtype),
        in_specs=[ANY, ANY],
        out_specs=VMEM,
        scratch_shapes=[
            pltpu.VMEM((group_rows // 2, reflect), dtype),
            pltpu.VMEM(factor.shape, dtype),
            pltpu.SemaphoreType.DMA((2,)),
        ],
        name="pack",
    )(basis, factor)
    packed, merge_factor = lax.optimization_barrier((packed, merge_factor))
    slices = lax.all_to_all(packed, "col", 0, 0)
    picked = pl.pallas_call(
        pick_kernel,
        out_shape=jax.ShapeDtypeStruct((GROUPS, tall, LANES), dtype),
        in_specs=[SMEM, VMEM],
        out_specs=VMEM,
        name="pick",
    )(owners, slices)

    row, top = lax.axis_index("row"), lax.axis_index("col") // share
    across = [merge_factor] + [over_col(merge_factor, m * share) for m in range(1, rows)]

    def for_row(mask):
        index = top ^ row ^ mask
        block = across[0]
        for k in range(1, rows):
            block = jnp.where(index == k, across[k], block)
        return block

    m_held = jnp.stack([for_row(0)] + [over_row(for_row(m), m) for m in range(1, rows)])
    bit = share // 2
    while bit >= NEAR:
        m_held = jnp.concatenate([m_held, over_col(m_held, bit)])
        bit //= 2
    m_two = over_col(m_held, 2)
    m_held = [m_held, over_col(m_held, 1), m_two, over_col(m_two, 1)]
    wanted, width = merge_factor.shape[0] * rows, sub_vectors.shape[1]
    each = wanted // (rows * cols)
    merged = pl.pallas_call(
        functools.partial(merge_kernel, rows, cols),
        out_shape=jax.ShapeDtypeStruct((wanted, width), jnp.float32),
        in_specs=[VMEM] + [VMEM] * NEAR,
        out_specs=VMEM,
        compiler_params=LIMIT,
        name="merge",
    )(sub_vectors, *m_held)
    state = lax.all_to_all(merged.reshape(rows * cols, each, width), ("row", "col"), 0, 0)

    x_bit, y_bit, core_bit = NEAR * FAR, 2, 1
    own_masks = [m * NEAR for m in range(FAR)]
    own = jnp.stack([picked] + [over_col(picked, m) for m in own_masks[1:]])
    by_row, by_col = over_row(own, 1), over_col(own, y_bit)
    corner = jnp.concatenate(
        [over_col(by_row[: FAR // 2], y_bit), over_row(by_col[FAR // 2 :], 1)]
    )
    sides = jnp.concatenate([by_row, by_col])
    held = [own, sides, corner]
    masks = [
        own_masks,
        [m + x_bit for m in own_masks] + [m + y_bit for m in own_masks],
        [m + x_bit + y_bit for m in own_masks],
    ]
    held = held + [over_col(x, core_bit) for x in held]
    masks = masks + [[m + core_bit for m in ms] for ms in masks]
    return pl.pallas_call(
        functools.partial(chain_kernel, cols, masks),
        out_shape=jax.ShapeDtypeStruct((each, cols * width), jnp.bfloat16),
        in_specs=[SMEM, VMEM] + [VMEM] * len(held),
        out_specs=VMEM,
        scratch_shapes=[
            pltpu.VMEM((GROUPS, group_rows, reflect), dtype),
            pltpu.VMEM((GROUPS, reflect, reflect), dtype),
        ],
        compiler_params=LIMIT,
        name="chain",
    )(offsets, state, *held)


def solution(mesh):
    rows, cols = mesh.shape["row"], mesh.shape["col"]
    in_specs = (
        P("row", "col"),
        P("row", "col"),
        P("col", None, None),
        P("col", None, None),
        P(),
        P(),
    )
    out_specs = P(("row", "col"), None)
    return jax.shard_map(
        functools.partial(local, rows, cols),
        mesh=mesh,
        in_specs=in_specs,
        out_specs=out_specs,
        check_vma=False,
    )
```

time: 94.6 us -> 83.1 us (0.88)
  blocking collectives: 0 us -> 28.4 us
  starting transfers between devices: 37.6 us -> 10.5 us
  Pallas kernels: 14.7 us -> 9.4 us
  local copies, waits for them, and re-layouts: 4.89 us -> 0.2 us
  waiting for transfers between devices: 35.5 us -> 33.1 us
    all_to_all x0 -> x2, blocking collectives: none -> 28.4 us  [the longest x1 18.6 us: local(): slices = lax.all_to_all(packed, 'col', 0, 0)]
    ppermute x33 -> x13, starting transfers between devices: 33.6 us -> 6.81 us  [over_col(): return lax.ppermute(x, 'col', [(c, c ^ mask) for c in range(cols)])]
    pallas_call x8 -> x4, Pallas kernels: 14.7 us -> 9.4 us  [the longest x1 5.5 us: local(): pl.pallas_call(functools.partial(chain_kernel, cols, masks), out_shape=ja...]
    unnamed x44 -> x8, local copies, waits for them, and re-layouts: 3.2 us -> 0.07 us
    ppermute x6 -> x3, waiting for transfers between devices: 8.86 us -> 5.73 us  [over_row(): return lax.ppermute(x, 'row', [(r, r ^ mask) for r in range(rows)])]
    ppermute x33 -> x13, waiting for transfers between devices: 26.7 us -> 27.4 us  [over_col(): return lax.ppermute(x, 'col', [(c, c ^ mask) for c in range(cols)])]
    ppermute x6 -> x3, starting transfers between devices: 4.07 us -> 3.71 us  [over_row(): return lax.ppermute(x, 'row', [(r, r ^ mask) for r in range(rows)])]
  transfers between devices with their start and end apart: 39 -> 16, of which waited for: 14 -> 9; matrix products, arithmetic and copies ran while one was open for 2% -> 0% of each run, Pallas kernels for 12% -> 1%
where the time goes in v5:
time: 83.1 us; the launch traced here: 82.8 us
  waiting for transfers between devices  33.1 us (40%)
  blocking collectives  28.4 us (34%)
  starting transfers between devices  10.5 us (13%)
  Pallas kernels  9.4 us (11%)
  other arithmetic  1.05 us (1%)
    ppermute x13, waiting for transfers between devices, over_col(): return lax.ppermute(x, 'col', [(c, c ^ mask) for c in range(cols)])  27.4 us
    all_to_all x1, blocking collectives, local(): slices = lax.all_to_all(packed, 'col', 0, 0)  18.6 us
    all_to_all x1, blocking collectives, local(): lax.all_to_all(merged.reshape(rows * cols, each, width), ('row', 'col'),...  9.78 us
    ppermute x13, starting transfers between devices, over_col(): return lax.ppermute(x, 'col', [(c, c ^ mask) for c in range(cols)])  6.81 us
    ppermute x3, waiting for transfers between devices, over_row(): return lax.ppermute(x, 'row', [(r, r ^ mask) for r in range(rows)])  5.73 us
    pallas_call x1, Pallas kernels, local(): pl.pallas_call(functools.partial(chain_kernel, cols, masks), out_shape=ja...  5.5 us
    ppermute x3, starting transfers between devices, over_row(): return lax.ppermute(x, 'row', [(r, r ^ mask) for r in range(rows)])  3.71 us
    pallas_call x1, Pallas kernels, local(): pl.pallas_call(pack_kernel, out_shape=jax.ShapeDtypeStruct((cols, tall, L...  1.83 us
  transfers between devices with their start and end apart: 16, of which 9 were waited for; matrix products, arithmetic and copies ran while one was open for 0% of the time, Pallas kernels for 1%

profile of v5, /device:TPU:0, one launch (start us, length us, event | category | flops | bytes accessed | tf_op | source)
XLA Modules:
  0.0 82.8 jit_solution(3294687004820222411)
XLA Ops:
  0.0 1.8 %pack.1 = bf16[16,80,128]{2,1,0:T(8,128)(2,1)} custom-call(bf16[1024,256]{1,0:T(8,128)(2,1)} %bitcast.11, bf16[256,256]{1,0:T(8,128)(2,1)} %bitcast.15), custom_call_target="tpu_custom_call" | custom-call | tf_op jit(solution)/shard_map/pack/pallas_call | solution.py:148
  1.8 18.6 %all_to_all.10.held = bf16[16,80,128]{2,1,0:T(8,128)(2,1)} all-to-all(bf16[16,80,128]{2,1,0:T(8,128)(2,1)} %pack.1), channel_id=1, replica_groups=mesh['row'=2,'col'=16] {'col'}, dimensions={0} | all-to-all | bytes 655360 | tf_op jit(solution)/shard_map/all_to_all | solution.py:161
  20.4 1.6 %pick.1 = bf16[6,80,128]{2,1,0:T(8,128)(2,1)} custom-call(s32[6]{0:T(128)} %owners.1, bf16[16,80,128]{2,1,0:T(8,128)(2,1)} %all_to_all.10.held), custom_call_target="tpu_custom_call" | custom-call | tf_op jit(solution)/shard_map/pick/pallas_call | solution.py:162
  22.1 1.1 %collective-permute-start.8 = (bf16[6,80,128]{2,1,0:T(8,128)(2,1)}, bf16[6,80,128]{2,1,0:T(8,128)(2,1)S(1)}, u32[]{:S(2)}, u32[]{:S(2)}) collective-permute-start(bf16[6,80,128]{2,1,0:T(8,128)(2,1)} %pick.1), channel_id=1, source_target_pairs={{0,12},{1,13},{2,14},{3,15},{4,8},{5,9},{6,10},{7,11},{8,4},{9,5},... | collective-permute-start | bytes 368648 | tf_op jit(solution)/shard_map/ppermute | solution.py:137
  23.2 0.6 collective-permute-start.7
  23.8 2.6 %collective-permute-start.6 = (bf16[6,80,128]{2,1,0:T(8,128)(2,1)}, bf16[6,80,128]{2,1,0:T(8,128)(2,1)S(1)}, u32[]{:S(2)}, u32[]{:S(2)}) collective-permute-start(bf16[6,80,128]{2,1,0:T(8,128)(2,1)} %pick.1), channel_id=1, source_target_pairs={{0,4},{1,5},{2,6},{3,7},{4,0},{5,1},{6,2},{7,3},{8,12},{9,13},{10,... | collective-permute-start | bytes 368648 | tf_op jit(solution)/shard_map/ppermute | solution.py:137
  26.5 3.9 %collective-permute-done.8 = bf16[6,80,128]{2,1,0:T(8,128)(2,1)S(1)} collective-permute-done((bf16[6,80,128]{2,1,0:T(8,128)(2,1)}, bf16[6,80,128]{2,1,0:T(8,128)(2,1)S(1)}, u32[]{:S(2)}, u32[]{:S(2)}) %collective-permute-start.8) | collective-permute-done | bytes 122912 | tf_op jit(solution)/shard_map/ppermute | solution.py:137
  30.4 5.5 %collective-permute-done.7 = bf16[6,80,128]{2,1,0:T(8,128)(2,1)S(1)} collective-permute-done((bf16[6,80,128]{2,1,0:T(8,128)(2,1)}, bf16[6,80,128]{2,1,0:T(8,128)(2,1)S(1)}, u32[]{:S(2)}, u32[]{:S(2)}) %collective-permute-start.7) | collective-permute-done | bytes 122912 | tf_op jit(solution)/shard_map/ppermute | solution.py:137
  35.9 0.0 collective-permute-done.6
  35.9 0.0 copy-start.2
  35.9 1.0 %pad_maximum_fusion.refs_0_ = bf16[4,6,80,128]{3,2,1,0:T(8,128)(2,1)S(1)} fusion(bf16[1,6,80,128]{3,2,1,0:T(8,128)(2,1)S(1)} %bitcast.16, bf16[1,6,80,128]{3,2,1,0:T(8,128)(2,1)S(1)} %bitcast.17, bf16[1,6,80,128]{3,2,1,0:T(8,128)(2,1)S(1)} %bitcast.18, bf16[1,6,80,128]{3,2,1,0:T(8,128)(2,1)} %bitcast.12), kind=kLoop, calls=%fused_computation | loop fusion | flops 737280 | bytes 983040 | tf_op jit(solution)/shard_map/stack | solution.py:201
  36.9 1.6 %collective-permute-start.9 = (bf16[4,6,80,128]{3,2,1,0:T(8,128)(2,1)S(1)}, bf16[4,6,80,128]{3,2,1,0:T(8,128)(2,1)S(1)}, u32[]{:S(2)}, u32[]{:S(2)}) collective-permute-start(bf16[4,6,80,128]{3,2,1,0:T(8,128)(2,1)S(1)} %pad_maximum_fusion.refs_0_), channel_id=1, source_target_pairs={{0,16},{16,0},{1,17},{17,1},{2,18},{18,2},{3,19},{19,3},{4,20},{20... | collective-permute-start | bytes 1474568 | tf_op jit(solution)/shard_map/ppermute | solution.py:140
  38.4 0.8 collective-permute-start.10
  39.2 0.0 copy-done.2
  39.2 0.0 collective-permute-start
  39.2 5.2 %collective-permute-done = bf16[64,512]{1,0:T(8,128)(2,1)S(1)} collective-permute-done((bf16[64,512]{1,0:T(8,128)(2,1)S(1)}, bf16[64,512]{1,0:T(8,128)(2,1)S(1)}, u32[]{:S(2)}, u32[]{:S(2)}) %collective-permute-start) | collective-permute-done | bytes 65568 | tf_op jit(solution)/shard_map/ppermute | solution.py:137
  44.4 0.6 collective-permute-start.1
  45.0 5.6 %collective-permute-done.9 = bf16[4,6,80,128]{3,2,1,0:T(8,128)(2,1)S(1)} collective-permute-done((bf16[4,6,80,128]{3,2,1,0:T(8,128)(2,1)S(1)}, bf16[4,6,80,128]{3,2,1,0:T(8,128)(2,1)S(1)}, u32[]{:S(2)}, u32[]{:S(2)}) %collective-permute-start.9) | collective-permute-done | bytes 491552 | tf_op jit(solution)/shard_map/ppermute | solution.py:140
  50.7 0.5 collective-permute-done.10
  51.2 0.1 constant_dynamic-update-slice_fusion.refs_1_
  51.2 0.1 collective-permute-start.14
  51.3 0.0 collective-permute-done.1
  51.4 0.1 collective-permute-start.2
  51.5 0.0 copy-start
  51.5 0.5 collective-permute-start.11
  52.0 1.6 %collective-permute-start.12 = (bf16[2,6,80,128]{3,2,1,0:T(8,128)(2,1)S(1)}, bf16[2,6,80,128]{3,2,1,0:T(8,128)(2,1)S(1)}, u32[]{:S(2)}, u32[]{:S(2)}) collective-permute-start(bf16[2,6,80,128]{3,2,1,0:T(8,128)(2,1)S(1)} %slice.9), channel_id=1, source_target_pairs={{0,16},{16,0},{1,17},{17,1},{2,18},{18,2},{3,19},{19,3},{4,20},{20... | collective-permute-start | bytes 737288 | tf_op jit(solution)/shard_map/ppermute | solution.py:140
  53.5 3.8 %collective-permute-done.2 = bf16[2,64,512]{2,1,0:T(8,128)(2,1)S(1)} collective-permute-done((bf16[2,64,512]{2,1,0:T(8,128)(2,1)S(1)}, bf16[2,64,512]{2,1,0:T(8,128)(2,1)S(1)}, u32[]{:S(2)}, u32[]{:S(2)}) %collective-permute-start.2) | collective-permute-done | bytes 131104 | tf_op jit(solution)/shard_map/ppermute | solution.py:137
  57.3 0.5 collective-permute-start.4
  57.8 0.0 collective-permute-start.13
  57.8 2.2 %collective-permute-done.11 = bf16[2,6,80,128]{3,2,1,0:T(8,128)(2,1)S(1)} collective-permute-done((bf16[2,6,80,128]{3,2,1,0:T(8,128)(2,1)S(1)}, bf16[2,6,80,128]{3,2,1,0:T(8,128)(2,1)S(1)}, u32[]{:S(2)}, u32[]{:S(2)}) %collective-permute-start.11) | collective-permute-done | bytes 245792 | tf_op jit(solution)/shard_map/ppermute | solution.py:137
  60.0 0.0 collective-permute-done.12
  60.1 0.1 collective-permute-start.15
  60.2 0.5 collective-permute-start.3
  60.7 4.8 %collective-permute-done.4.refs_2_ = bf16[4,64,512]{2,1,0:T(8,128)(2,1)S(1)} collective-permute-done((bf16[4,64,512]{2,1,0:T(8,128)(2,1)S(1)}, bf16[4,64,512]{2,1,0:T(8,128)(2,1)S(1)}, u32[]{:S(2)}, u32[]{:S(2)}) %collective-permute-start.4) | collective-permute-done | bytes 262176 | tf_op jit(solution)/shard_map/ppermute | solution.py:137
  65.5 0.0 collective-permute-start.5
  65.5 0.0 collective-permute-done.3.refs_1_
  65.5 1.5 %collective-permute-done.5.refs_3_ = bf16[4,64,512]{2,1,0:T(8,128)(2,1)S(1)} collective-permute-done((bf16[4,64,512]{2,1,0:T(8,128)(2,1)S(1)}, bf16[4,64,512]{2,1,0:T(8,128)(2,1)S(1)}, u32[]{:S(2)}, u32[]{:S(2)}) %collective-permute-start.5) | collective-permute-done | bytes 262176 | tf_op jit(solution)/shard_map/ppermute | solution.py:137
  67.0 0.0 copy-done
  67.0 0.4 merge.1
  67.5 0.0 copy-start.1
  67.5 9.8 %all_to_all.11.start = f32[32,4,128]{2,1,0:T(4,128)S(1)} all-to-all(f32[32,4,128]{2,1,0:T(4,128)S(1)} %bitcast.10), channel_id=1, replica_groups=mesh['row'=2,'col'=16] {'row','col'}, dimensions={0} | all-to-all | bytes 131072 | tf_op jit(solution)/shard_map/all_to_all | solution.py:197
  77.2 0.0 collective-permute-done.13.refs_3_
  77.2 0.0 collective-permute-done.15.refs_5_
  77.3 0.0 collective-permute-done.14.refs_4_
  77.3 0.0 copy-done.1
  77.3 5.5 %chain.1 = bf16[4,2048]{1,0:T(4,128)(2,1)} custom-call(s32[6]{0:T(128)S(1)} %copy-done.1, f32[32,4,128]{2,1,0:T(4,128)S(1)} %all_to_all.11.start, bf16[4,6,80,128]{3,2,1,0:T(8,128)(2,1)S(1)} %pad_maximum_fusion.refs_0_, bf16[8,6,80,128]{3,2,1,0:T(8,128)(2,1)S(1)} %constant_dynamic-update-slice_fusion.refs_1_, ...), custom_call_target="tpu_custom_call" | custom-call | tf_op jit(solution)/shard_map/chain/pallas_call | solution.py:215
  (8 shorter events, 0.2 us)
Async XLA Ops:
  22.1 8.3 %collective-permute-start.8 = (bf16[6,80,128]{2,1,0:T(8,128)(2,1)}, bf16[6,80,128]{2,1,0:T(8,128)(2,1)S(1)}, u32[]{:S(2)}, u32[]{:S(2)}) collective-permute-start(bf16[6,80,128]{2,1,0:T(8,128)(2,1)} %pick.1), channel_id=1, source_target_pairs={{0,12},{1,13},{2,14},{3,15},{4,8},{5,9},{6,10},{7,11},{8,4},{9,5},... | collective-permute-start | bytes 368648 | tf_op jit(solution)/shard_map/ppermute | solution.py:137
  23.2 12.7 %collective-permute-start.7 = (bf16[6,80,128]{2,1,0:T(8,128)(2,1)}, bf16[6,80,128]{2,1,0:T(8,128)(2,1)S(1)}, u32[]{:S(2)}, u32[]{:S(2)}) collective-permute-start(bf16[6,80,128]{2,1,0:T(8,128)(2,1)} %pick.1), channel_id=1, source_target_pairs={{0,8},{1,9},{2,10},{3,11},{4,12},{5,13},{6,14},{7,15},{8,0},{9,1},... | collective-permute-start | bytes 368648 | tf_op jit(solution)/shard_map/ppermute | solution.py:137
  23.8 12.1 %collective-permute-start.6 = (bf16[6,80,128]{2,1,0:T(8,128)(2,1)}, bf16[6,80,128]{2,1,0:T(8,128)(2,1)S(1)}, u32[]{:S(2)}, u32[]{:S(2)}) collective-permute-start(bf16[6,80,128]{2,1,0:T(8,128)(2,1)} %pick.1), channel_id=1, source_target_pairs={{0,4},{1,5},{2,6},{3,7},{4,0},{5,1},{6,2},{7,3},{8,12},{9,13},{10,... | collective-permute-start | bytes 368648 | tf_op jit(solution)/shard_map/ppermute | solution.py:137
  35.9 3.3 %copy-start.2 = (bf16[64,512]{1,0:T(8,128)(2,1)S(1)}, bf16[64,512]{1,0:T(8,128)(2,1)}, u32[]{:S(2)}) copy-start(bf16[64,512]{1,0:T(8,128)(2,1)} %param.7) | copy-start | bytes 196612
  36.9 13.8 %collective-permute-start.9 = (bf16[4,6,80,128]{3,2,1,0:T(8,128)(2,1)S(1)}, bf16[4,6,80,128]{3,2,1,0:T(8,128)(2,1)S(1)}, u32[]{:S(2)}, u32[]{:S(2)}) collective-permute-start(bf16[4,6,80,128]{3,2,1,0:T(8,128)(2,1)S(1)} %pad_maximum_fusion.refs_0_), channel_id=1, source_target_pairs={{0,16},{16,0},{1,17},{17,1},{2,18},{18,2},{3,19},{19,3},{4,20},{20... | collective-permute-start | bytes 1474568 | tf_op jit(solution)/shard_map/ppermute | solution.py:140
  38.4 12.7 %collective-permute-start.10 = (bf16[4,6,80,128]{3,2,1,0:T(8,128)(2,1)S(1)}, bf16[4,6,80,128]{3,2,1,0:T(8,128)(2,1)S(1)}, u32[]{:S(2)}, u32[]{:S(2)}) collective-permute-start(bf16[4,6,80,128]{3,2,1,0:T(8,128)(2,1)S(1)} %pad_maximum_fusion.refs_0_), channel_id=1, source_target_pairs={{0,2},{1,3},{2,0},{3,1},{4,6},{5,7},{6,4},{7,5},{8,10},{9,11},{10,... | collective-permute-start | bytes 1474568 | tf_op jit(solution)/shard_map/ppermute | solution.py:137
  39.2 5.2 %collective-permute-start = (bf16[64,512]{1,0:T(8,128)(2,1)S(1)}, bf16[64,512]{1,0:T(8,128)(2,1)S(1)}, u32[]{:S(2)}, u32[]{:S(2)}) collective-permute-start(bf16[64,512]{1,0:T(8,128)(2,1)S(1)} %copy-done.2), channel_id=1, source_target_pairs={{0,8},{1,9},{2,10},{3,11},{4,12},{5,13},{6,14},{7,15},{8,0},{9,1},... | collective-permute-start | bytes 196616 | tf_op jit(solution)/shard_map/ppermute | solution.py:137
  44.4 6.9 %collective-permute-start.1 = (bf16[64,512]{1,0:T(8,128)(2,1)S(1)}, bf16[64,512]{1,0:T(8,128)(2,1)S(1)}, u32[]{:S(2)}, u32[]{:S(2)}) collective-permute-start(bf16[64,512]{1,0:T(8,128)(2,1)S(1)} %get-tuple-element.10), channel_id=1, source_target_pairs={{0,16},{16,0},{1,17},{17,1},{2,18},{18,2},{3,19},{19,3},{4,20},{20... | collective-permute-start | bytes 196616 | tf_op jit(solution)/shard_map/ppermute | solution.py:140
  51.2 26.0 %collective-permute-start.14 = (bf16[8,6,80,128]{3,2,1,0:T(8,128)(2,1)S(1)}, bf16[8,6,80,128]{3,2,1,0:T(8,128)(2,1)S(1)}, u32[]{:S(2)}, u32[]{:S(2)}) collective-permute-start(bf16[8,6,80,128]{3,2,1,0:T(8,128)(2,1)S(1)} %constant_dynamic-update-slice_fusion.refs_1_), channel_id=1, source_target_pairs={{0,1},{1,0},{2,3},{3,2},{4,5},{5,4},{6,7},{7,6},{8,9},{9,8},{10,11... | collective-permute-start | bytes 2949128 | tf_op jit(solution)/shard_map/ppermute | solution.py:137
  51.4 5.9 %collective-permute-start.2 = (bf16[2,64,512]{2,1,0:T(8,128)(2,1)S(1)}, bf16[2,64,512]{2,1,0:T(8,128)(2,1)S(1)}, u32[]{:S(2)}, u32[]{:S(2)}) collective-permute-start(bf16[2,64,512]{2,1,0:T(8,128)(2,1)S(1)} %pad_maximum_fusion.2), channel_id=1, source_target_pairs={{0,4},{1,5},{2,6},{3,7},{4,0},{5,1},{6,2},{7,3},{8,12},{9,13},{10,... | collective-permute-start | bytes 393224 | tf_op jit(solution)/shard_map/ppermute | solution.py:137
  51.5 15.5 %copy-start = (bf16[4096,128]{1,0:T(8,128)(2,1)S(1)}, bf16[4096,128]{1,0:T(8,128)(2,1)}, u32[]{:S(2)}) copy-start(bf16[4096,128]{1,0:T(8,128)(2,1)} %sub.6) | copy-start | bytes 3145732
  51.5 8.5 %collective-permute-start.11 = (bf16[2,6,80,128]{3,2,1,0:T(8,128)(2,1)S(1)}, bf16[2,6,80,128]{3,2,1,0:T(8,128)(2,1)S(1)}, u32[]{:S(2)}, u32[]{:S(2)}) collective-permute-start(bf16[2,6,80,128]{3,2,1,0:T(8,128)(2,1)S(1)} %slice.8), channel_id=1, source_target_pairs={{0,2},{1,3},{2,0},{3,1},{4,6},{5,7},{6,4},{7,5},{8,10},{9,11},{10,... | collective-permute-start | bytes 737288 | tf_op jit(solution)/shard_map/ppermute | solution.py:137
  52.0 8.1 %collective-permute-start.12 = (bf16[2,6,80,128]{3,2,1,0:T(8,128)(2,1)S(1)}, bf16[2,6,80,128]{3,2,1,0:T(8,128)(2,1)S(1)}, u32[]{:S(2)}, u32[]{:S(2)}) collective-permute-start(bf16[2,6,80,128]{3,2,1,0:T(8,128)(2,1)S(1)} %slice.9), channel_id=1, source_target_pairs={{0,16},{16,0},{1,17},{17,1},{2,18},{18,2},{3,19},{19,3},{4,20},{20... | collective-permute-start | bytes 737288 | tf_op jit(solution)/shard_map/ppermute | solution.py:140
  57.3 8.2 %collective-permute-start.4 = (bf16[4,64,512]{2,1,0:T(8,128)(2,1)S(1)}, bf16[4,64,512]{2,1,0:T(8,128)(2,1)S(1)}, u32[]{:S(2)}, u32[]{:S(2)}) collective-permute-start(bf16[4,64,512]{2,1,0:T(8,128)(2,1)S(1)} %pad_maximum_fusion.1.refs_0_), channel_id=1, source_target_pairs={{0,2},{1,3},{2,0},{3,1},{4,6},{5,7},{6,4},{7,5},{8,10},{9,11},{10,... | collective-permute-start | bytes 786440 | tf_op jit(solution)/shard_map/ppermute | solution.py:137
  57.8 19.5 %collective-permute-start.13 = (bf16[4,6,80,128]{3,2,1,0:T(8,128)(2,1)S(1)}, bf16[4,6,80,128]{3,2,1,0:T(8,128)(2,1)S(1)}, u32[]{:S(2)}, u32[]{:S(2)}) collective-permute-start(bf16[4,6,80,128]{3,2,1,0:T(8,128)(2,1)S(1)} %pad_maximum_fusion.refs_0_), channel_id=1, source_target_pairs={{0,1},{1,0},{2,3},{3,2},{4,5},{5,4},{6,7},{7,6},{8,9},{9,8},{10,11... | collective-permute-start | bytes 1474568 | tf_op jit(solution)/shard_map/ppermute | solution.py:137
  60.1 17.2 %collective-permute-start.15 = (bf16[4,6,80,128]{3,2,1,0:T(8,128)(2,1)S(1)}, bf16[4,6,80,128]{3,2,1,0:T(8,128)(2,1)S(1)}, u32[]{:S(2)}, u32[]{:S(2)}) collective-permute-start(bf16[4,6,80,128]{3,2,1,0:T(8,128)(2,1)S(1)} %constant_dynamic-update-slice_fusion.2.refs_2_), channel_id=1, source_target_pairs={{0,1},{1,0},{2,3},{3,2},{4,5},{5,4},{6,7},{7,6},{8,9},{9,8},{10,11... | collective-permute-start | bytes 1474568 | tf_op jit(solution)/shard_map/ppermute | solution.py:137
  60.2 5.3 %collective-permute-start.3 = (bf16[4,64,512]{2,1,0:T(8,128)(2,1)S(1)}, bf16[4,64,512]{2,1,0:T(8,128)(2,1)S(1)}, u32[]{:S(2)}, u32[]{:S(2)}) collective-permute-start(bf16[4,64,512]{2,1,0:T(8,128)(2,1)S(1)} %pad_maximum_fusion.1.refs_0_), channel_id=1, source_target_pairs={{0,1},{1,0},{2,3},{3,2},{4,5},{5,4},{6,7},{7,6},{8,9},{9,8},{10,11... | collective-permute-start | bytes 786440 | tf_op jit(solution)/shard_map/ppermute | solution.py:137
  65.5 1.5 %collective-permute-start.5 = (bf16[4,64,512]{2,1,0:T(8,128)(2,1)S(1)}, bf16[4,64,512]{2,1,0:T(8,128)(2,1)S(1)}, u32[]{:S(2)}, u32[]{:S(2)}) collective-permute-start(bf16[4,64,512]{2,1,0:T(8,128)(2,1)S(1)} %collective-permute-done.4.refs_2_), channel_id=1, source_target_pairs={{0,1},{1,0},{2,3},{3,2},{4,5},{5,4},{6,7},{7,6},{8,9},{9,8},{10,11... | collective-permute-start | bytes 786440 | tf_op jit(solution)/shard_map/ppermute | solution.py:137
  67.5 9.8 %copy-start.1 = (s32[6]{0:T(128)S(1)}, s32[6]{0:T(128)}, u32[]{:S(2)}) copy-start(s32[6]{0:T(128)} %offsets.1) | copy-start | bytes 76

commit v6 on v5

--- a/solution.py
+++ b/solution.py
@@ -8,6 +8,7 @@
 from jax.sharding import PartitionSpec as P
 
 GROUPS = 6
+COLOURS = 3
 NEAR = 4
 FAR = 4
 SLICES = 2 * NEAR * FAR
@@ -52,8 +53,9 @@
 
 
 def pick_kernel(owners, held, out):
+    each = GROUPS // COLOURS
     for group in range(GROUPS):
-        out[group] = held[owners[group]]
+        out[group // each, group % each] = held[owners[group]]
 
 
 def merge_kernel(rows, cols, sub, *refs):
@@ -82,7 +84,7 @@
     return products[:half] + products[half:]
 
 
-def chain_kernel(cols, masks, offsets, start, *refs):
+def chain_kernel(cols, groups, masks, first, last, offsets, start, *refs):
     held, (out, basis_all, factor_all) = refs[: len(masks)], refs[len(masks) :]
     mine = slice_index()
     lanes = basis_all.shape[2] // LANES
@@ -98,15 +100,18 @@
             factor_all[:, aligned(e // lanes, tall), aligned(lax.rem(e, lanes), LANES)] = ref[
                 index, :, lanes * pv :, :
             ]
-    n, each, width = start.shape
-    pieces = start[...].reshape(n // cols, cols, each, width).sum(0)
-    x = jnp.concatenate([pieces[c] for c in range(cols)], 1)
-    x = jnp.concatenate([x] + [jnp.zeros_like(x)] * (8 // each - 1), 0)
+    if first:
+        n, each, width = start.shape
+        pieces = start[...].reshape(n // cols, cols, each, width).sum(0)
+        x = jnp.concatenate([pieces[c] for c in range(cols)], 1)
+        x = jnp.concatenate([x] + [jnp.zeros_like(x)] * (8 // each - 1), 0)
+    else:
+        x = start[...]
     wide = x.shape[1]
     group_rows = basis_all.shape[1]
     before = jnp.int32(0)
-    for slot in range(GROUPS):
-        offset = offsets[slot]
+    for slot, group in enumerate(groups):
+        offset = offsets[group]
         x = pltpu.roll(x, lax.rem(before - offset + wide, wide), 1)
         before = offset
         block = x[:, :group_rows]
@@ -127,7 +132,10 @@
         )
         x = jnp.concatenate([block - change, x[:, group_rows:]], 1)
     x = pltpu.roll(x, before, 1)
-    out[...] = x[: out.shape[0]].astype(out.dtype)
+    if last:
+        out[...] = x[: out.shape[0]].astype(out.dtype)
+    else:
+        out[...] = x
 
 
 def local(rows, cols, sub_vectors, merge_factor, reflectors, wy_factors, owners, offsets):
@@ -157,18 +165,9 @@
         ],
         name="pack",
     )(basis, factor)
-    packed, merge_factor = lax.optimization_barrier((packed, merge_factor))
-    slices = lax.all_to_all(packed, "col", 0, 0)
-    picked = pl.pallas_call(
-        pick_kernel,
-        out_shape=jax.ShapeDtypeStruct((GROUPS, tall, LANES), dtype),
-        in_specs=[SMEM, VMEM],
-        out_specs=VMEM,
-        name="pick",
-    )(owners, slices)
-
     row, top = lax.axis_index("row"), lax.axis_index("col") // share
     across = [merge_factor] + [over_col(merge_factor, m * share) for m in range(1, rows)]
+    packed, across = lax.optimization_barrier((packed, across))
 
     def for_row(mask):
         index = top ^ row ^ mask
@@ -177,13 +176,48 @@
             block = jnp.where(index == k, across[k], block)
         return block
 
-    m_held = jnp.stack([for_row(0)] + [over_row(for_row(m), m) for m in range(1, rows)])
+    m_held = [for_row(0)] + [over_row(for_row(m), m) for m in range(1, rows)]
+    slices = lax.all_to_all(packed, "col", 0, 0)
+    slices, m_held = lax.optimization_barrier((slices, m_held))
+    m_held = jnp.stack(m_held)
+    picked = pl.pallas_call(
+        pick_kernel,
+        out_shape=jax.ShapeDtypeStruct((COLOURS, GROUPS // COLOURS, tall, LANES), dtype),
+        in_specs=[SMEM, VMEM],
+        out_specs=VMEM,
+        name="pick",
+    )(owners, slices)
+
+    z_two = over_col(picked, 2 * NEAR)
     bit = share // 2
     while bit >= NEAR:
         m_held = jnp.concatenate([m_held, over_col(m_held, bit)])
         bit //= 2
+    z_two, m_held = lax.optimization_barrier((z_two, m_held))
     m_two = over_col(m_held, 2)
     m_held = [m_held, over_col(m_held, 1), m_two, over_col(m_two, 1)]
+
+    links = [
+        (NEAR * FAR, lambda v: over_row(v, 1)),
+        (2, lambda v: over_col(v, 2)),
+        (NEAR, lambda v: over_col(v, NEAR)),
+    ]
+    colours = [jnp.stack([picked[k], z_two[k]]) for k in range(COLOURS)]
+    masks = [[0, 2 * NEAR] for _ in range(COLOURS)]
+    for step in range(2):
+        for k in range(COLOURS):
+            mask, send = links[(k + step) % 3]
+            colours[k] = jnp.concatenate([colours[k], send(colours[k])])
+            masks[k] = masks[k] + [m ^ mask for m in masks[k]]
+    held, held_masks = [], []
+    for k in range(COLOURS):
+        mask, send = links[(k + 2) % 3]
+        held.append([colours[k], send(colours[k])])
+        held_masks.append([masks[k], [m ^ mask for m in masks[k]]])
+    for k in range(COLOURS):
+        held[k] += [over_col(v, 1) for v in held[k]]
+        held_masks[k] += [[m ^ 1 for m in ms] for ms in held_masks[k]]
+
     wanted, width = merge_factor.shape[0] * rows, sub_vectors.shape[1]
     each = wanted // (rows * cols)
     merged = pl.pallas_call(
@@ -196,34 +230,26 @@
     )(sub_vectors, *m_held)
     state = lax.all_to_all(merged.reshape(rows * cols, each, width), ("row", "col"), 0, 0)
 
-    x_bit, y_bit, core_bit = NEAR * FAR, 2, 1
-    own_masks = [m * NEAR for m in range(FAR)]
-    own = jnp.stack([picked] + [over_col(picked, m) for m in own_masks[1:]])
-    by_row, by_col = over_row(own, 1), over_col(own, y_bit)
-    corner = jnp.concatenate(
-        [over_col(by_row[: FAR // 2], y_bit), over_row(by_col[FAR // 2 :], 1)]
-    )
-    sides = jnp.concatenate([by_row, by_col])
-    held = [own, sides, corner]
-    masks = [
-        own_masks,
-        [m + x_bit for m in own_masks] + [m + y_bit for m in own_masks],
-        [m + x_bit + y_bit for m in own_masks],
-    ]
-    held = held + [over_col(x, core_bit) for x in held]
-    masks = masks + [[m + core_bit for m in ms] for ms in masks]
-    return pl.pallas_call(
-        functools.partial(chain_kernel, cols, masks),
-        out_shape=jax.ShapeDtypeStruct((each, cols * width), jnp.bfloat16),
-        in_specs=[SMEM, VMEM] + [VMEM] * len(held),
-        out_specs=VMEM,
-        scratch_shapes=[
-            pltpu.VMEM((GROUPS, group_rows, reflect), dtype),
-            pltpu.VMEM((GROUPS, reflect, reflect), dtype),
-        ],
-        compiler_params=LIMIT,
-        name="chain",
-    )(offsets, state, *held)
+    wide = cols * width
+    for k in range(COLOURS):
+        first, last = k == 0, k == COLOURS - 1
+        per = GROUPS // COLOURS
+        groups = range(k * per, (k + 1) * per)
+        state = pl.pallas_call(
+            functools.partial(chain_kernel, cols, groups, held_masks[k], first, last),
+            out_shape=jax.ShapeDtypeStruct(
+                (each, wide) if last else (8, wide), jnp.bfloat16 if last else jnp.float32
+            ),
+            in_specs=[SMEM, VMEM] + [VMEM] * len(held[k]),
+            out_specs=VMEM,
+            scratch_shapes=[
+                pltpu.VMEM((per, group_rows, reflect), dtype),
+                pltpu.VMEM((per, reflect, reflect), dtype),
+            ],
+            compiler_params=LIMIT,
+            name=f"chain{k}",
+        )(offsets, state, *held[k])
+    return state
 
 
 def solution(mesh):

time: 83.1 us -> 82.1 us (0.988)
  blocking collectives: 28.4 us -> 10.2 us
  starting transfers between devices: 10.5 us -> 24.3 us
  waiting for transfers between devices: 33.1 us -> 34.8 us
  Pallas kernels: 9.4 us -> 10.7 us
  local copies, waits for them, and re-layouts: 0.2 us -> 1.34 us
    all_to_all x1 -> x0, blocking collectives: 18.6 us -> none  [local(): slices = lax.all_to_all(packed, 'col', 0, 0)]
    all_to_all x0 -> x1, waiting for transfers between devices: none -> 6.6 us  [local(): slices = lax.all_to_all(packed, 'col', 0, 0)]
    ppermute x13 -> x18, waiting for transfers between devices: 27.4 us -> 21.1 us  [over_col(): return lax.ppermute(x, 'col', [(c, c ^ mask) for c in range(cols)])]
    all_to_all x0 -> x1, starting transfers between devices: none -> 5.86 us  [local(): slices = lax.all_to_all(packed, 'col', 0, 0)]
    ppermute x13 -> x18, starting transfers between devices: 6.81 us -> 12.3 us  [over_col(): return lax.ppermute(x, 'col', [(c, c ^ mask) for c in range(cols)])]
    ppermute x3 -> x4, starting transfers between devices: 3.71 us -> 6.18 us  [over_row(): return lax.ppermute(x, 'row', [(r, r ^ mask) for r in range(rows)])]
    ppermute x3 -> x4, waiting for transfers between devices: 5.73 us -> 7.08 us  [over_row(): return lax.ppermute(x, 'row', [(r, r ^ mask) for r in range(rows)])]
    pallas_call x2 -> x4, Pallas kernels: 7.14 us -> 8.44 us  [the longest x3 6.8 us: local(): pl.pallas_call(functools.partial(chain_kernel, cols, groups, held_masks[k...]
  transfers between devices with their start and end apart: 16 -> 23, of which waited for: 9 -> 13; matrix products, arithmetic and copies ran while one was open for 0% -> 0% of each run, Pallas kernels for 1% -> 8%
where the time goes in v6:
time: 82.1 us; the launch traced here: 81.8 us
  waiting for transfers between devices  34.8 us (42%)
  starting transfers between devices  24.3 us (30%)
  Pallas kernels  10.7 us (13%)
  blocking collectives  10.2 us (12%)
  local copies, waits for them, and re-layouts  1.34 us (2%)
    ppermute x18, waiting for transfers between devices, over_col(): return lax.ppermute(x, 'col', [(c, c ^ mask) for c in range(cols)])  21.1 us
    ppermute x18, starting transfers between devices, over_col(): return lax.ppermute(x, 'col', [(c, c ^ mask) for c in range(cols)])  12.3 us
    all_to_all x1, blocking collectives, local(): lax.all_to_all(merged.reshape(rows * cols, each, width), ('row', 'col'),...  10.2 us
    ppermute x4, waiting for transfers between devices, over_row(): return lax.ppermute(x, 'row', [(r, r ^ mask) for r in range(rows)])  7.08 us
    pallas_call x3, Pallas kernels, local(): pl.pallas_call(functools.partial(chain_kernel, cols, groups, held_masks[k...  6.8 us
    all_to_all x1, waiting for transfers between devices, local(): slices = lax.all_to_all(packed, 'col', 0, 0)  6.6 us
    ppermute x4, starting transfers between devices, over_row(): return lax.ppermute(x, 'row', [(r, r ^ mask) for r in range(rows)])  6.18 us
    all_to_all x1, starting transfers between devices, local(): slices = lax.all_to_all(packed, 'col', 0, 0)  5.86 us
  transfers between devices with their start and end apart: 23, of which 13 were waited for; matrix products, arithmetic and copies ran while one was open for 0% of the time, Pallas kernels for 8%

profile of v6, /device:TPU:0, one launch (start us, length us, event | category | flops | bytes accessed | tf_op | source)
XLA Modules:
  0.0 81.8 jit_solution(11203797216366906490)
XLA Ops:
  0.0 4.0 %collective-permute-start = (bf16[64,512]{1,0:T(8,128)(2,1)}, bf16[64,512]{1,0:T(8,128)(2,1)S(1)}, u32[]{:S(2)}, u32[]{:S(2)}) collective-permute-start(bf16[64,512]{1,0:T(8,128)(2,1)} %param.7), channel_id=1, source_target_pairs={{0,8},{1,9},{2,10},{3,11},{4,12},{5,13},{6,14},{7,15},{8,0},{9,1},... | collective-permute-start | bytes 196616 | tf_op jit(solution)/shard_map/ppermute | solution.py:145
  4.0 1.8 %pack.1 = bf16[16,80,128]{2,1,0:T(8,128)(2,1)} custom-call(bf16[1024,256]{1,0:T(8,128)(2,1)} %bitcast.8, bf16[256,256]{1,0:T(8,128)(2,1)} %bitcast.11), custom_call_target="tpu_custom_call" | custom-call | tf_op jit(solution)/shard_map/pack/pallas_call | solution.py:156
  5.9 2.0 %collective-permute-done = bf16[64,512]{1,0:T(8,128)(2,1)S(1)} collective-permute-done((bf16[64,512]{1,0:T(8,128)(2,1)}, bf16[64,512]{1,0:T(8,128)(2,1)S(1)}, u32[]{:S(2)}, u32[]{:S(2)}) %collective-permute-start) | collective-permute-done | bytes 65568 | tf_op jit(solution)/shard_map/ppermute | solution.py:145
  7.9 5.9 %all-to-all-start = ((bf16[16,80,128]{2,1,0:T(8,128)(2,1)}), bf16[16,80,128]{2,1,0:T(8,128)(2,1)S(1)}, u32[]{:S(2)}, u32[]{:S(2)}) async-start(bf16[16,80,128]{2,1,0:T(8,128)(2,1)} %pack.1), calls=%async_computation | async-start | bytes 655360 | tf_op jit(solution)/shard_map/all_to_all | solution.py:180
  13.8 1.6 %collective-permute-start.1 = (bf16[64,512]{1,0:T(8,128)(2,1)S(1)}, bf16[64,512]{1,0:T(8,128)(2,1)S(1)}, u32[]{:S(2)}, u32[]{:S(2)}) collective-permute-start(bf16[64,512]{1,0:T(8,128)(2,1)S(1)} %get-tuple-element.21), channel_id=1, source_target_pairs={{0,16},{16,0},{1,17},{17,1},{2,18},{18,2},{3,19},{19,3},{4,20},{20... | collective-permute-start | bytes 196616 | tf_op jit(solution)/shard_map/ppermute | solution.py:148
  15.4 2.9 %collective-permute-done.1 = bf16[64,512]{1,0:T(8,128)(2,1)S(1)} collective-permute-done((bf16[64,512]{1,0:T(8,128)(2,1)S(1)}, bf16[64,512]{1,0:T(8,128)(2,1)S(1)}, u32[]{:S(2)}, u32[]{:S(2)}) %collective-permute-start.1) | collective-permute-done | bytes 65568 | tf_op jit(solution)/shard_map/ppermute | solution.py:148
  18.3 6.6 %all-to-all-done.held = bf16[16,80,128]{2,1,0:T(8,128)(2,1)S(1)} async-done(((bf16[16,80,128]{2,1,0:T(8,128)(2,1)}), bf16[16,80,128]{2,1,0:T(8,128)(2,1)S(1)}, u32[]{:S(2)}, u32[]{:S(2)}) %all-to-all-start) | async-done | bytes 327712 | tf_op jit(solution)/shard_map/all_to_all | solution.py:180
  24.9 0.7 copy-done.2
  25.6 1.6 %pick.1 = bf16[3,2,80,128]{3,2,1,0:T(8,128)(2,1)} custom-call(s32[6]{0:T(128)} %owners.1, bf16[16,80,128]{2,1,0:T(8,128)(2,1)} %copy-done.2), custom_call_target="tpu_custom_call" | custom-call | tf_op jit(solution)/shard_map/pick/pallas_call | solution.py:183
  27.2 1.4 %collective-permute-start.2 = (bf16[3,2,80,128]{3,2,1,0:T(8,128)(2,1)}, bf16[3,2,80,128]{3,2,1,0:T(8,128)(2,1)S(1)}, u32[]{:S(2)}, u32[]{:S(2)}) collective-permute-start(bf16[3,2,80,128]{3,2,1,0:T(8,128)(2,1)} %pick.1), channel_id=1, source_target_pairs={{0,8},{1,9},{2,10},{3,11},{4,12},{5,13},{6,14},{7,15},{8,0},{9,1},... | collective-permute-start | bytes 368648 | tf_op jit(solution)/shard_map/ppermute | solution.py:145
  28.7 0.3 collective-permute-start.3
  29.0 0.6 copy-done.3
  29.6 4.4 %collective-permute-done.3 = bf16[2,64,512]{2,1,0:T(8,128)(2,1)S(1)} collective-permute-done((bf16[2,64,512]{2,1,0:T(8,128)(2,1)S(1)}, bf16[2,64,512]{2,1,0:T(8,128)(2,1)S(1)}, u32[]{:S(2)}, u32[]{:S(2)}) %collective-permute-start.3) | collective-permute-done | bytes 131104 | tf_op jit(solution)/shard_map/ppermute | solution.py:145
  34.0 2.3 %collective-permute-done.2 = bf16[3,2,80,128]{3,2,1,0:T(8,128)(2,1)S(1)} collective-permute-done((bf16[3,2,80,128]{3,2,1,0:T(8,128)(2,1)}, bf16[3,2,80,128]{3,2,1,0:T(8,128)(2,1)S(1)}, u32[]{:S(2)}, u32[]{:S(2)}) %collective-permute-start.2) | collective-permute-done | bytes 122912 | tf_op jit(solution)/shard_map/ppermute | solution.py:145
  36.3 0.7 collective-permute-start.5
  37.0 1.6 %collective-permute-start.7 = (bf16[2,2,80,128]{3,2,1,0:T(8,128)(2,1)S(1)}, bf16[2,2,80,128]{3,2,1,0:T(8,128)(2,1)S(1)}, u32[]{:S(2)}, u32[]{:S(2)}) collective-permute-start(bf16[2,2,80,128]{3,2,1,0:T(8,128)(2,1)S(1)} %pad_maximum_fusion.8), channel_id=1, source_target_pairs={{0,16},{16,0},{1,17},{17,1},{2,18},{18,2},{3,19},{19,3},{4,20},{20... | collective-permute-start | bytes 245768 | tf_op jit(solution)/shard_map/ppermute | solution.py:148
  38.6 1.4 %collective-permute-start.12 = (bf16[2,2,80,128]{3,2,1,0:T(8,128)(2,1)S(1)}, bf16[2,2,80,128]{3,2,1,0:T(8,128)(2,1)S(1)}, u32[]{:S(2)}, u32[]{:S(2)}) collective-permute-start(bf16[2,2,80,128]{3,2,1,0:T(8,128)(2,1)S(1)} %pad_maximum_fusion.9), channel_id=1, source_target_pairs={{0,2},{1,3},{2,0},{3,1},{4,6},{5,7},{6,4},{7,5},{8,10},{9,11},{10,... | collective-permute-start | bytes 245768 | tf_op jit(solution)/shard_map/ppermute | solution.py:145
  40.0 0.4 collective-permute-start.17
  40.4 1.3 %collective-permute-done.7 = bf16[2,2,80,128]{3,2,1,0:T(8,128)(2,1)S(1)} collective-permute-done((bf16[2,2,80,128]{3,2,1,0:T(8,128)(2,1)S(1)}, bf16[2,2,80,128]{3,2,1,0:T(8,128)(2,1)S(1)}, u32[]{:S(2)}, u32[]{:S(2)}) %collective-permute-start.7) | collective-permute-done | bytes 81952 | tf_op jit(solution)/shard_map/ppermute | solution.py:148
  41.7 1.4 %collective-permute-start.8 = (bf16[4,2,80,128]{3,2,1,0:T(8,128)(2,1)S(1)}, bf16[4,2,80,128]{3,2,1,0:T(8,128)(2,1)S(1)}, u32[]{:S(2)}, u32[]{:S(2)}) collective-permute-start(bf16[4,2,80,128]{3,2,1,0:T(8,128)(2,1)S(1)} %pad_maximum_fusion.4), channel_id=1, source_target_pairs={{0,2},{1,3},{2,0},{3,1},{4,6},{5,7},{6,4},{7,5},{8,10},{9,11},{10,... | collective-permute-start | bytes 491528 | tf_op jit(solution)/shard_map/ppermute | solution.py:145
  43.1 4.1 %collective-permute-done.12 = bf16[2,2,80,128]{3,2,1,0:T(8,128)(2,1)S(1)} collective-permute-done((bf16[2,2,80,128]{3,2,1,0:T(8,128)(2,1)S(1)}, bf16[2,2,80,128]{3,2,1,0:T(8,128)(2,1)S(1)}, u32[]{:S(2)}, u32[]{:S(2)}) %collective-permute-start.12) | collective-permute-done | bytes 81952 | tf_op jit(solution)/shard_map/ppermute | solution.py:145
  47.2 0.4 collective-permute-start.13
  47.6 0.0 collective-permute-done.17
  47.6 0.0 copy-start
  47.6 1.6 %collective-permute-start.18 = (bf16[4,2,80,128]{3,2,1,0:T(8,128)(2,1)S(1)}, bf16[4,2,80,128]{3,2,1,0:T(8,128)(2,1)S(1)}, u32[]{:S(2)}, u32[]{:S(2)}) collective-permute-start(bf16[4,2,80,128]{3,2,1,0:T(8,128)(2,1)S(1)} %pad_maximum_fusion.6), channel_id=1, source_target_pairs={{0,16},{16,0},{1,17},{17,1},{2,18},{18,2},{3,19},{19,3},{4,20},{20... | collective-permute-start | bytes 491528 | tf_op jit(solution)/shard_map/ppermute | solution.py:148
  49.2 1.1 %collective-permute-done.8 = bf16[4,2,80,128]{3,2,1,0:T(8,128)(2,1)S(1)} collective-permute-done((bf16[4,2,80,128]{3,2,1,0:T(8,128)(2,1)S(1)}, bf16[4,2,80,128]{3,2,1,0:T(8,128)(2,1)S(1)}, u32[]{:S(2)}, u32[]{:S(2)}) %collective-permute-start.8) | collective-permute-done | bytes 163872 | tf_op jit(solution)/shard_map/ppermute | solution.py:145
  50.3 0.7 collective-permute-start.9
  51.0 1.7 %collective-permute-done.13 = bf16[4,2,80,128]{3,2,1,0:T(8,128)(2,1)S(1)} collective-permute-done((bf16[4,2,80,128]{3,2,1,0:T(8,128)(2,1)S(1)}, bf16[4,2,80,128]{3,2,1,0:T(8,128)(2,1)S(1)}, u32[]{:S(2)}, u32[]{:S(2)}) %collective-permute-start.13) | collective-permute-done | bytes 163872 | tf_op jit(solution)/shard_map/ppermute | solution.py:145
  52.7 0.0 collective-permute-start.10
  52.7 0.2 collective-permute-done.18
  53.0 1.5 %collective-permute-start.14 = (bf16[8,2,80,128]{3,2,1,0:T(8,128)(2,1)S(1)}, bf16[8,2,80,128]{3,2,1,0:T(8,128)(2,1)S(1)}, u32[]{:S(2)}, u32[]{:S(2)}) collective-permute-start(bf16[8,2,80,128]{3,2,1,0:T(8,128)(2,1)S(1)} %pad_maximum_fusion.1.refs_0_), channel_id=1, source_target_pairs={{0,16},{16,0},{1,17},{17,1},{2,18},{18,2},{3,19},{19,3},{4,20},{20... | collective-permute-start | bytes 983048 | tf_op jit(solution)/shard_map/ppermute | solution.py:148
  54.5 0.0 collective-permute-done.4.refs_1_
  54.5 0.6 collective-permute-start.19
  55.1 0.0 collective-permute-done.5.refs_2_
  55.1 0.0 collective-permute-start.6
  55.1 4.6 %collective-permute-done.9.refs_1_ = bf16[8,2,80,128]{3,2,1,0:T(8,128)(2,1)S(1)} collective-permute-done((bf16[8,2,80,128]{3,2,1,0:T(8,128)(2,1)S(1)}, bf16[8,2,80,128]{3,2,1,0:T(8,128)(2,1)S(1)}, u32[]{:S(2)}, u32[]{:S(2)}) %collective-permute-start.9) | collective-permute-done | bytes 327712 | tf_op jit(solution)/shard_map/ppermute | solution.py:145
  59.7 0.5 collective-permute-start.15
  60.3 2.7 %collective-permute-done.14.refs_1_ = bf16[8,2,80,128]{3,2,1,0:T(8,128)(2,1)S(1)} collective-permute-done((bf16[8,2,80,128]{3,2,1,0:T(8,128)(2,1)S(1)}, bf16[8,2,80,128]{3,2,1,0:T(8,128)(2,1)S(1)}, u32[]{:S(2)}, u32[]{:S(2)}) %collective-permute-start.14) | collective-permute-done | bytes 327712 | tf_op jit(solution)/shard_map/ppermute | solution.py:148
  62.9 0.5 collective-permute-start.20
  63.5 0.8 collective-permute-done.19.refs_1_
  64.3 0.0 collective-permute-start.21
  64.3 0.4 merge.1
  64.7 0.0 copy-start.1
  64.7 10.2 %all_to_all.10.start = f32[32,4,128]{2,1,0:T(4,128)S(1)} all-to-all(f32[32,4,128]{2,1,0:T(4,128)S(1)} %bitcast.5), channel_id=1, replica_groups=mesh['row'=2,'col'=16] {'row','col'}, dimensions={0} | all-to-all | bytes 131072 | tf_op jit(solution)/shard_map/all_to_all | solution.py:231
  75.0 2.1 %chain0.1.start = f32[8,2048]{1,0:T(8,128)S(1)} custom-call(s32[6]{0:T(128)S(1)} %copy-done.1, f32[32,4,128]{2,1,0:T(4,128)S(1)} %all_to_all.10.start, bf16[8,2,80,128]{3,2,1,0:T(8,128)(2,1)S(1)} %pad_maximum_fusion.refs_0_, bf16[8,2,80,128]{3,2,1,0:T(8,128)(2,1)S(1)} %collective-permute-done.9.refs_1_, ...), custom_call_target="tpu_custom_call" | custom-call | tf_op jit(solution)/shard_map/chain0/pallas_call | solution.py:238
  77.0 0.0 collective-permute-done.15.refs_2_
  77.0 2.1 %chain1.1.start = f32[8,2048]{1,0:T(8,128)S(1)} custom-call(s32[6]{0:T(128)S(1)} %copy-done.1, f32[8,2048]{1,0:T(8,128)S(1)} %chain0.1.start, bf16[8,2,80,128]{3,2,1,0:T(8,128)(2,1)S(1)} %pad_maximum_fusion.1.refs_0_, bf16[8,2,80,128]{3,2,1,0:T(8,128)(2,1)S(1)} %collective-permute-done.14.refs_1_, ...), custom_call_target="tpu_custom_call" | custom-call | tf_op jit(solution)/shard_map/chain1/pallas_call | solution.py:238
  79.1 2.7 %chain2.1 = bf16[4,2048]{1,0:T(4,128)(2,1)} custom-call(s32[6]{0:T(128)S(1)} %copy-done.1, f32[8,2048]{1,0:T(8,128)S(1)} %chain1.1.start, bf16[8,2,80,128]{3,2,1,0:T(8,128)(2,1)S(1)} %pad_maximum_fusion.2.refs_0_, bf16[8,2,80,128]{3,2,1,0:T(8,128)(2,1)S(1)} %collective-permute-done.19.refs_1_, bf16[8,2,80,128]{3,2,1,0:T(8,128)(2,1)S(1)} %collective-permute-done.20.refs_2_, ...), custom_call_target="tpu_custom_call" | custom-call | tf_op jit(solution)/shard_map/chain2/pallas_call | solution.py:238
  (29 shorter events, 0.3 us)
Async XLA Ops:
  0.0 7.9 %collective-permute-start = (bf16[64,512]{1,0:T(8,128)(2,1)}, bf16[64,512]{1,0:T(8,128)(2,1)S(1)}, u32[]{:S(2)}, u32[]{:S(2)}) collective-permute-start(bf16[64,512]{1,0:T(8,128)(2,1)} %param.7), channel_id=1, source_target_pairs={{0,8},{1,9},{2,10},{3,11},{4,12},{5,13},{6,14},{7,15},{8,0},{9,1},... | collective-permute-start | bytes 196616 | tf_op jit(solution)/shard_map/ppermute | solution.py:145
  7.9 5.9 %copy-start.4 = (bf16[64,512]{1,0:T(8,128)(2,1)S(1)}, bf16[64,512]{1,0:T(8,128)(2,1)}, u32[]{:S(2)}) copy-start(bf16[64,512]{1,0:T(8,128)(2,1)} %param.7) | copy-start | bytes 196612
  7.9 17.0 %all-to-all-start = ((bf16[16,80,128]{2,1,0:T(8,128)(2,1)}), bf16[16,80,128]{2,1,0:T(8,128)(2,1)S(1)}, u32[]{:S(2)}, u32[]{:S(2)}) async-start(bf16[16,80,128]{2,1,0:T(8,128)(2,1)} %pack.1), calls=%async_computation | async-start | bytes 655360 | tf_op jit(solution)/shard_map/all_to_all | solution.py:180
  13.8 4.4 %collective-permute-start.1 = (bf16[64,512]{1,0:T(8,128)(2,1)S(1)}, bf16[64,512]{1,0:T(8,128)(2,1)S(1)}, u32[]{:S(2)}, u32[]{:S(2)}) collective-permute-start(bf16[64,512]{1,0:T(8,128)(2,1)S(1)} %get-tuple-element.21), channel_id=1, source_target_pairs={{0,16},{16,0},{1,17},{17,1},{2,18},{18,2},{3,19},{19,3},{4,20},{20... | collective-permute-start | bytes 196616 | tf_op jit(solution)/shard_map/ppermute | solution.py:148
  24.9 0.7 copy-start.2
  27.2 9.1 %collective-permute-start.2 = (bf16[3,2,80,128]{3,2,1,0:T(8,128)(2,1)}, bf16[3,2,80,128]{3,2,1,0:T(8,128)(2,1)S(1)}, u32[]{:S(2)}, u32[]{:S(2)}) collective-permute-start(bf16[3,2,80,128]{3,2,1,0:T(8,128)(2,1)} %pick.1), channel_id=1, source_target_pairs={{0,8},{1,9},{2,10},{3,11},{4,12},{5,13},{6,14},{7,15},{8,0},{9,1},... | collective-permute-start | bytes 368648 | tf_op jit(solution)/shard_map/ppermute | solution.py:145
  28.6 0.9 %copy-start.3 = (bf16[3,2,80,128]{3,2,1,0:T(8,128)(2,1)S(1)}, bf16[3,2,80,128]{3,2,1,0:T(8,128)(2,1)}, u32[]{:S(2)}) copy-start(bf16[3,2,80,128]{3,2,1,0:T(8,128)(2,1)} %pick.1) | copy-start | bytes 368644
  28.7 5.3 %collective-permute-start.3 = (bf16[2,64,512]{2,1,0:T(8,128)(2,1)S(1)}, bf16[2,64,512]{2,1,0:T(8,128)(2,1)S(1)}, u32[]{:S(2)}, u32[]{:S(2)}) collective-permute-start(bf16[2,64,512]{2,1,0:T(8,128)(2,1)S(1)} %pad_maximum_fusion.7), channel_id=1, source_target_pairs={{0,4},{1,5},{2,6},{3,7},{4,0},{5,1},{6,2},{7,3},{8,12},{9,13},{10,... | collective-permute-start | bytes 393224 | tf_op jit(solution)/shard_map/ppermute | solution.py:145
  36.3 18.2 %collective-permute-start.4 = (bf16[4,64,512]{2,1,0:T(8,128)(2,1)S(1)}, bf16[4,64,512]{2,1,0:T(8,128)(2,1)S(1)}, u32[]{:S(2)}, u32[]{:S(2)}) collective-permute-start(bf16[4,64,512]{2,1,0:T(8,128)(2,1)S(1)} %pad_maximum_fusion.3.refs_0_), channel_id=1, source_target_pairs={{0,1},{1,0},{2,3},{3,2},{4,5},{5,4},{6,7},{7,6},{8,9},{9,8},{10,11... | collective-permute-start | bytes 786440 | tf_op jit(solution)/shard_map/ppermute | solution.py:145
  36.3 18.8 %collective-permute-start.5 = (bf16[4,64,512]{2,1,0:T(8,128)(2,1)S(1)}, bf16[4,64,512]{2,1,0:T(8,128)(2,1)S(1)}, u32[]{:S(2)}, u32[]{:S(2)}) collective-permute-start(bf16[4,64,512]{2,1,0:T(8,128)(2,1)S(1)} %pad_maximum_fusion.3.refs_0_), channel_id=1, source_target_pairs={{0,2},{1,3},{2,0},{3,1},{4,6},{5,7},{6,4},{7,5},{8,10},{9,11},{10,... | collective-permute-start | bytes 786440 | tf_op jit(solution)/shard_map/ppermute | solution.py:145
  37.0 4.6 %collective-permute-start.7 = (bf16[2,2,80,128]{3,2,1,0:T(8,128)(2,1)S(1)}, bf16[2,2,80,128]{3,2,1,0:T(8,128)(2,1)S(1)}, u32[]{:S(2)}, u32[]{:S(2)}) collective-permute-start(bf16[2,2,80,128]{3,2,1,0:T(8,128)(2,1)S(1)} %pad_maximum_fusion.8), channel_id=1, source_target_pairs={{0,16},{16,0},{1,17},{17,1},{2,18},{18,2},{3,19},{19,3},{4,20},{20... | collective-permute-start | bytes 245768 | tf_op jit(solution)/shard_map/ppermute | solution.py:148
  38.6 8.5 %collective-permute-start.12 = (bf16[2,2,80,128]{3,2,1,0:T(8,128)(2,1)S(1)}, bf16[2,2,80,128]{3,2,1,0:T(8,128)(2,1)S(1)}, u32[]{:S(2)}, u32[]{:S(2)}) collective-permute-start(bf16[2,2,80,128]{3,2,1,0:T(8,128)(2,1)S(1)} %pad_maximum_fusion.9), channel_id=1, source_target_pairs={{0,2},{1,3},{2,0},{3,1},{4,6},{5,7},{6,4},{7,5},{8,10},{9,11},{10,... | collective-permute-start | bytes 245768 | tf_op jit(solution)/shard_map/ppermute | solution.py:145
  40.0 7.6 %collective-permute-start.17 = (bf16[2,2,80,128]{3,2,1,0:T(8,128)(2,1)S(1)}, bf16[2,2,80,128]{3,2,1,0:T(8,128)(2,1)S(1)}, u32[]{:S(2)}, u32[]{:S(2)}) collective-permute-start(bf16[2,2,80,128]{3,2,1,0:T(8,128)(2,1)S(1)} %pad_maximum_fusion.10), channel_id=1, source_target_pairs={{0,4},{1,5},{2,6},{3,7},{4,0},{5,1},{6,2},{7,3},{8,12},{9,13},{10,... | collective-permute-start | bytes 245768 | tf_op jit(solution)/shard_map/ppermute | solution.py:145
  41.7 8.6 %collective-permute-start.8 = (bf16[4,2,80,128]{3,2,1,0:T(8,128)(2,1)S(1)}, bf16[4,2,80,128]{3,2,1,0:T(8,128)(2,1)S(1)}, u32[]{:S(2)}, u32[]{:S(2)}) collective-permute-start(bf16[4,2,80,128]{3,2,1,0:T(8,128)(2,1)S(1)} %pad_maximum_fusion.4), channel_id=1, source_target_pairs={{0,2},{1,3},{2,0},{3,1},{4,6},{5,7},{6,4},{7,5},{8,10},{9,11},{10,... | collective-permute-start | bytes 491528 | tf_op jit(solution)/shard_map/ppermute | solution.py:145
  47.2 5.5 %collective-permute-start.13 = (bf16[4,2,80,128]{3,2,1,0:T(8,128)(2,1)S(1)}, bf16[4,2,80,128]{3,2,1,0:T(8,128)(2,1)S(1)}, u32[]{:S(2)}, u32[]{:S(2)}) collective-permute-start(bf16[4,2,80,128]{3,2,1,0:T(8,128)(2,1)S(1)} %pad_maximum_fusion.5), channel_id=1, source_target_pairs={{0,4},{1,5},{2,6},{3,7},{4,0},{5,1},{6,2},{7,3},{8,12},{9,13},{10,... | collective-permute-start | bytes 491528 | tf_op jit(solution)/shard_map/ppermute | solution.py:145
  47.6 16.7 %copy-start = (bf16[4096,128]{1,0:T(8,128)(2,1)S(1)}, bf16[4096,128]{1,0:T(8,128)(2,1)}, u32[]{:S(2)}) copy-start(bf16[4096,128]{1,0:T(8,128)(2,1)} %sub.6) | copy-start | bytes 3145732
  47.6 5.4 %collective-permute-start.18 = (bf16[4,2,80,128]{3,2,1,0:T(8,128)(2,1)S(1)}, bf16[4,2,80,128]{3,2,1,0:T(8,128)(2,1)S(1)}, u32[]{:S(2)}, u32[]{:S(2)}) collective-permute-start(bf16[4,2,80,128]{3,2,1,0:T(8,128)(2,1)S(1)} %pad_maximum_fusion.6), channel_id=1, source_target_pairs={{0,16},{16,0},{1,17},{17,1},{2,18},{18,2},{3,19},{19,3},{4,20},{20... | collective-permute-start | bytes 491528 | tf_op jit(solution)/shard_map/ppermute | solution.py:148
  50.3 9.4 %collective-permute-start.9 = (bf16[8,2,80,128]{3,2,1,0:T(8,128)(2,1)S(1)}, bf16[8,2,80,128]{3,2,1,0:T(8,128)(2,1)S(1)}, u32[]{:S(2)}, u32[]{:S(2)}) collective-permute-start(bf16[8,2,80,128]{3,2,1,0:T(8,128)(2,1)S(1)} %pad_maximum_fusion.refs_0_), channel_id=1, source_target_pairs={{0,4},{1,5},{2,6},{3,7},{4,0},{5,1},{6,2},{7,3},{8,12},{9,13},{10,... | collective-permute-start | bytes 983048 | tf_op jit(solution)/shard_map/ppermute | solution.py:145
  52.7 10.2 %collective-permute-start.10 = (bf16[8,2,80,128]{3,2,1,0:T(8,128)(2,1)S(1)}, bf16[8,2,80,128]{3,2,1,0:T(8,128)(2,1)S(1)}, u32[]{:S(2)}, u32[]{:S(2)}) collective-permute-start(bf16[8,2,80,128]{3,2,1,0:T(8,128)(2,1)S(1)} %pad_maximum_fusion.refs_0_), channel_id=1, source_target_pairs={{0,1},{1,0},{2,3},{3,2},{4,5},{5,4},{6,7},{7,6},{8,9},{9,8},{10,11... | collective-permute-start | bytes 983048 | tf_op jit(solution)/shard_map/ppermute | solution.py:145
  53.0 10.0 %collective-permute-start.14 = (bf16[8,2,80,128]{3,2,1,0:T(8,128)(2,1)S(1)}, bf16[8,2,80,128]{3,2,1,0:T(8,128)(2,1)S(1)}, u32[]{:S(2)}, u32[]{:S(2)}) collective-permute-start(bf16[8,2,80,128]{3,2,1,0:T(8,128)(2,1)S(1)} %pad_maximum_fusion.1.refs_0_), channel_id=1, source_target_pairs={{0,16},{16,0},{1,17},{17,1},{2,18},{18,2},{3,19},{19,3},{4,20},{20... | collective-permute-start | bytes 983048 | tf_op jit(solution)/shard_map/ppermute | solution.py:148
  54.5 9.7 %collective-permute-start.19 = (bf16[8,2,80,128]{3,2,1,0:T(8,128)(2,1)S(1)}, bf16[8,2,80,128]{3,2,1,0:T(8,128)(2,1)S(1)}, u32[]{:S(2)}, u32[]{:S(2)}) collective-permute-start(bf16[8,2,80,128]{3,2,1,0:T(8,128)(2,1)S(1)} %pad_maximum_fusion.2.refs_0_), channel_id=1, source_target_pairs={{0,2},{1,3},{2,0},{3,1},{4,6},{5,7},{6,4},{7,5},{8,10},{9,11},{10,... | collective-permute-start | bytes 983048 | tf_op jit(solution)/shard_map/ppermute | solution.py:145
  55.1 4.6 %collective-permute-start.6 = (bf16[4,64,512]{2,1,0:T(8,128)(2,1)S(1)}, bf16[4,64,512]{2,1,0:T(8,128)(2,1)S(1)}, u32[]{:S(2)}, u32[]{:S(2)}) collective-permute-start(bf16[4,64,512]{2,1,0:T(8,128)(2,1)S(1)} %collective-permute-done.5.refs_2_), channel_id=1, source_target_pairs={{0,1},{1,0},{2,3},{3,2},{4,5},{5,4},{6,7},{7,6},{8,9},{9,8},{10,11... | collective-permute-start | bytes 786440 | tf_op jit(solution)/shard_map/ppermute | solution.py:145
  59.7 15.2 %collective-permute-start.11 = (bf16[8,2,80,128]{3,2,1,0:T(8,128)(2,1)S(1)}, bf16[8,2,80,128]{3,2,1,0:T(8,128)(2,1)S(1)}, u32[]{:S(2)}, u32[]{:S(2)}) collective-permute-start(bf16[8,2,80,128]{3,2,1,0:T(8,128)(2,1)S(1)} %collective-permute-done.9.refs_1_), channel_id=1, source_target_pairs={{0,1},{1,0},{2,3},{3,2},{4,5},{5,4},{6,7},{7,6},{8,9},{9,8},{10,11... | collective-permute-start | bytes 983048 | tf_op jit(solution)/shard_map/ppermute | solution.py:145
  59.7 17.3 %collective-permute-start.15 = (bf16[8,2,80,128]{3,2,1,0:T(8,128)(2,1)S(1)}, bf16[8,2,80,128]{3,2,1,0:T(8,128)(2,1)S(1)}, u32[]{:S(2)}, u32[]{:S(2)}) collective-permute-start(bf16[8,2,80,128]{3,2,1,0:T(8,128)(2,1)S(1)} %pad_maximum_fusion.1.refs_0_), channel_id=1, source_target_pairs={{0,1},{1,0},{2,3},{3,2},{4,5},{5,4},{6,7},{7,6},{8,9},{9,8},{10,11... | collective-permute-start | bytes 983048 | tf_op jit(solution)/shard_map/ppermute | solution.py:145
  62.9 14.1 %collective-permute-start.16 = (bf16[8,2,80,128]{3,2,1,0:T(8,128)(2,1)S(1)}, bf16[8,2,80,128]{3,2,1,0:T(8,128)(2,1)S(1)}, u32[]{:S(2)}, u32[]{:S(2)}) collective-permute-start(bf16[8,2,80,128]{3,2,1,0:T(8,128)(2,1)S(1)} %collective-permute-done.14.refs_1_), channel_id=1, source_target_pairs={{0,1},{1,0},{2,3},{3,2},{4,5},{5,4},{6,7},{7,6},{8,9},{9,8},{10,11... | collective-permute-start | bytes 983048 | tf_op jit(solution)/shard_map/ppermute | solution.py:145
  62.9 16.2 %collective-permute-start.20 = (bf16[8,2,80,128]{3,2,1,0:T(8,128)(2,1)S(1)}, bf16[8,2,80,128]{3,2,1,0:T(8,128)(2,1)S(1)}, u32[]{:S(2)}, u32[]{:S(2)}) collective-permute-start(bf16[8,2,80,128]{3,2,1,0:T(8,128)(2,1)S(1)} %pad_maximum_fusion.2.refs_0_), channel_id=1, source_target_pairs={{0,1},{1,0},{2,3},{3,2},{4,5},{5,4},{6,7},{7,6},{8,9},{9,8},{10,11... | collective-permute-start | bytes 983048 | tf_op jit(solution)/shard_map/ppermute | solution.py:145
  64.3 14.9 %collective-permute-start.21 = (bf16[8,2,80,128]{3,2,1,0:T(8,128)(2,1)S(1)}, bf16[8,2,80,128]{3,2,1,0:T(8,128)(2,1)S(1)}, u32[]{:S(2)}, u32[]{:S(2)}) collective-permute-start(bf16[8,2,80,128]{3,2,1,0:T(8,128)(2,1)S(1)} %collective-permute-done.19.refs_1_), channel_id=1, source_target_pairs={{0,1},{1,0},{2,3},{3,2},{4,5},{5,4},{6,7},{7,6},{8,9},{9,8},{10,11... | collective-permute-start | bytes 983048 | tf_op jit(solution)/shard_map/ppermute | solution.py:145
  64.7 10.2 %copy-start.1 = (s32[6]{0:T(128)S(1)}, s32[6]{0:T(128)}, u32[]{:S(2)}) copy-start(s32[6]{0:T(128)} %offsets.5) | copy-start | bytes 76

commit v7 on v6

v7 whole, which is shorter than its diff:
```python
import functools

import jax
import jax.numpy as jnp
from jax import lax
from jax.experimental import pallas as pl
from jax.experimental.pallas import tpu as pltpu
from jax.sharding import PartitionSpec as P

GROUPS = 6
COLOURS = 3
HALF = 8
SLICES = 2 * HALF
LANES = 128
VMEM = pl.BlockSpec(memory_space=pltpu.VMEM)
SMEM = pl.BlockSpec(memory_space=pltpu.SMEM)
ANY = pl.BlockSpec(memory_space=pl.ANY)


def limit(mib):
    return pltpu.CompilerParams(vmem_limit_bytes=mib * 1024 * 1024)


def slice_index():
    row, col = lax.axis_index("row"), lax.axis_index("col")
    return lax.rem(row, 2) * HALF + lax.rem(col, HALF)


def aligned(index, size):
    return pl.ds(pl.multiple_of(index * size, size), size)


def pack_kernel(basis_hbm, factor_hbm, out, basis, factor, sems):
    row_bit = lax.rem(lax.axis_index("row"), 2)
    first = pltpu.make_async_copy(
        basis_hbm.at[aligned(row_bit, basis.shape[0])], basis, sems.at[0]
    )
    second = pltpu.make_async_copy(
        factor_hbm.at[aligned(row_bit, factor.shape[0])], factor, sems.at[1]
    )
    first.start()
    second.start()
    first.wait()
    second.wait()
    pv, pt = basis.shape[0] // HALF, factor.shape[0] // HALF
    lanes = basis.shape[1] // LANES
    for c in range(HALF):
        for k in range(lanes):
            at = slice(k * LANES, (k + 1) * LANES)
            out[c, k * pv : (k + 1) * pv, :] = basis[c * pv : (c + 1) * pv, at]
            low = lanes * pv + k * pt
            out[c, low : low + pt, :] = factor[c * pt : (c + 1) * pt, at]


def places(owners, group):
    half = owners[group] // HALF
    rank = jnp.int32(0)
    for before in range(group):
        rank = rank + (owners[before] // HALF == half).astype(jnp.int32)
    return half, rank


def pick_kernel(owners, held, out):
    mine = lax.axis_index("col") // HALF
    for group in range(GROUPS):
        half, rank = places(owners, group)
        rank = jnp.minimum(rank, out.shape[0] - 1)

        @pl.when(half == mine)
        def _():
            out[rank] = held[lax.rem(owners[group], HALF)]


def order_kernel(owners, held, *refs):
    others, outs = refs[:-COLOURS], refs[-COLOURS:]
    mine = lax.axis_index("col") // HALF
    each = GROUPS // COLOURS
    for group in range(GROUPS):
        half, rank = places(owners, group)
        piece = held[lax.rem(owners[group], HALF)]
        for mask, ref in enumerate(others, 1):
            other = ref[jnp.minimum(rank, ref.shape[0] - 1)]
            piece = jnp.where(jnp.bitwise_xor(half, mine) == mask, other, piece)
        outs[group // each][0, group % each] = piece


def merge_kernel(rows, cols, sub, *refs):
    held, total = refs[:-1], refs[-1]
    row, col = lax.axis_index("row"), lax.axis_index("col")
    share = cols // rows
    deep, tall = held[0].shape[2], held[0].shape[1]
    total[...] = jnp.zeros_like(total)
    for near, ref in enumerate(held):
        for index in range(ref.shape[0]):
            far, row_mask = index // rows, index % rows
            j = jnp.bitwise_xor(lax.rem(col, share), far * len(held) + near)
            part = jnp.dot(ref[index], sub[aligned(j, deep), :], preferred_element_type=jnp.float32)
            at = aligned(jnp.bitwise_xor(row, row_mask), tall)
            total[at, :] = total[at, :] + part


def two_terms(x):
    high = x.astype(jnp.bfloat16)
    low = (x - high.astype(jnp.float32)).astype(jnp.bfloat16)
    return jnp.concatenate([high, low], 0)


def both(products):
    half = products.shape[0] // 2
    return products[:half] + products[half:]


def chain_kernel(cols, groups, masks, first, last, offsets, start, *refs):
    held, (out, basis_all, factor_all) = refs[: len(masks)], refs[len(masks) :]
    mine = slice_index()
    lanes = basis_all.shape[2] // LANES
    pv = basis_all.shape[1] // SLICES
    pt = factor_all.shape[1] // SLICES
    for own_masks, ref in zip(masks, held):
        for index, mask in enumerate(own_masks):
            e = jnp.bitwise_xor(mine, mask)
            for k in range(lanes):
                at = slice(k * LANES, (k + 1) * LANES)
                basis_all[:, aligned(e, pv), at] = ref[index, :, k * pv : (k + 1) * pv, :]
                low = lanes * pv + k * pt
                factor_all[:, aligned(e, pt), at] = ref[index, :, low : low + pt, :]
    if first:
        n, each, width = start.shape
        pieces = start[...].reshape(n // cols, cols, each, width).sum(0)
        x = jnp.concatenate([pieces[c] for c in range(cols)], 1)
        x = jnp.concatenate([x] + [jnp.zeros_like(x)] * (8 // each - 1), 0)
    else:
        x = start[...]
    wide = x.shape[1]
    group_rows = basis_all.shape[1]
    before = jnp.int32(0)
    for slot, group in enumerate(groups):
        offset = offsets[group]
        x = pltpu.roll(x, lax.rem(before - offset + wide, wide), 1)
        before = offset
        block = x[:, :group_rows]
        weights = both(
            jnp.dot(two_terms(block), basis_all[slot], preferred_element_type=jnp.float32)
        )
        scaled = both(
            lax.dot_general(
                two_terms(weights), factor_all[slot], (((1,), (1,)), ((), ())),
                preferred_element_type=jnp.float32,
            )
        )
        change = both(
            lax.dot_general(
                two_terms(scaled), basis_all[slot], (((1,), (1,)), ((), ())),
                preferred_element_type=jnp.float32,
            )
        )
        x = jnp.concatenate([block - change, x[:, group_rows:]], 1)
    x = pltpu.roll(x, before, 1)
    if last:
        out[...] = x[: out.shape[0]].astype(out.dtype)
    else:
        out[...] = x


def local(rows, cols, sub_vectors, merge_factor, reflectors, wy_factors, owners, offsets):
    share = cols // rows
    halves = cols // HALF

    def over_col(x, mask):
        return lax.ppermute(x, "col", [(c, c ^ mask) for c in range(cols)])

    def over_row(x, mask):
        return lax.ppermute(x, "row", [(r, r ^ mask) for r in range(rows)])

    basis, factor = reflectors[0], wy_factors[0]
    group_rows, reflect = basis.shape
    dtype = basis.dtype
    tall = (group_rows + reflect) * (reflect // LANES) // SLICES

    across = [merge_factor] + [over_col(merge_factor, m * share) for m in range(1, rows)]

    packed = pl.pallas_call(
        pack_kernel,
        out_shape=jax.ShapeDtypeStruct((HALF, tall, LANES), dtype),
        in_specs=[ANY, ANY],
        out_specs=VMEM,
        scratch_shapes=[
            pltpu.VMEM((group_rows // 2, reflect), dtype),
            pltpu.VMEM((factor.shape[0] // 2, reflect), dtype),
            pltpu.SemaphoreType.DMA((2,)),
        ],
        compiler_params=limit(4),
        name="pack",
    )(basis, factor)
    members = [[h * HALF + c for c in range(HALF)] for h in range(halves)]
    slices = lax.all_to_all(packed, "col", 0, 0, axis_index_groups=members)
    slices, across = lax.optimization_barrier((slices, across))

    picked = pl.pallas_call(
        pick_kernel,
        out_shape=jax.ShapeDtypeStruct((GROUPS - 1, tall, LANES), dtype),
        in_specs=[SMEM, VMEM],
        out_specs=VMEM,
        compiler_params=limit(4),
        name="pick",
    )(owners, slices)
    others = [over_col(picked, m * HALF) for m in range(1, halves)]

    row, top = lax.axis_index("row"), lax.axis_index("col") // share

    def for_row(mask):
        index = top ^ row ^ mask
        block = across[0]
        for k in range(1, rows):
            block = jnp.where(index == k, across[k], block)
        return block

    m_held = jnp.stack([for_row(0)] + [over_row(for_row(m), m) for m in range(1, rows)])
    bit = share // 2
    while bit >= 4:
        m_held = jnp.concatenate([m_held, over_col(m_held, bit)])
        bit //= 2
    others, m_held = lax.optimization_barrier((others, m_held))
    m_two = over_col(m_held, 2)

    per = GROUPS // COLOURS
    colours = pl.pallas_call(
        order_kernel,
        out_shape=[jax.ShapeDtypeStruct((1, per, tall, LANES), dtype)] * COLOURS,
        in_specs=[SMEM, VMEM] + [VMEM] * len(others),
        out_specs=[VMEM] * COLOURS,
        compiler_params=limit(4),
        name="order",
    )(owners, slices, *others)
    colours = list(colours)
    links = [
        (HALF, lambda v: over_row(v, 1)),
        (2, lambda v: over_col(v, 2)),
        (4, lambda v: over_col(v, 4)),
    ]
    masks = [[0] for _ in range(COLOURS)]
    for step in range(2):
        for k in range(COLOURS):
            mask, send = links[(k + step) % 3]
            colours[k] = jnp.concatenate([colours[k], send(colours[k])])
            masks[k] = masks[k] + [m ^ mask for m in masks[k]]
        if step == 0:
            colours, m_two = lax.optimization_barrier((list(colours), m_two))
    m_held = [m_held, over_col(m_held, 1), m_two, over_col(m_two, 1)]

    wanted, width = merge_factor.shape[0] * rows, sub_vectors.shape[1]
    each = wanted // (rows * cols)
    merged = pl.pallas_call(
        functools.partial(merge_kernel, rows, cols),
        out_shape=jax.ShapeDtypeStruct((wanted, width), jnp.float32),
        in_specs=[VMEM] + [VMEM] * len(m_held),
        out_specs=VMEM,
        compiler_params=limit(8),
        name="merge",
    )(sub_vectors, *m_held)
    state = lax.all_to_all(merged.reshape(rows * cols, each, width), ("row", "col"), 0, 0)

    last_round = []
    for k in range(COLOURS):
        mask, send = links[(k + 2) % 3]
        last_round.append(send(colours[k]))
        masks[k] = [masks[k], [m ^ mask for m in masks[k]]]
        masks[k] += [[m ^ 1 for m in ms] for ms in masks[k]]
    last_round, state = lax.optimization_barrier((last_round, state))
    held = []
    for k in range(COLOURS):
        held.append([colours[k], last_round[k], over_col(colours[k], 1), over_col(last_round[k], 1)])

    wide = cols * width
    for k in range(COLOURS):
        first, last = k == 0, k == COLOURS - 1
        groups = range(k * per, (k + 1) * per)
        state = pl.pallas_call(
            functools.partial(chain_kernel, cols, groups, masks[k], first, last),
            out_shape=jax.ShapeDtypeStruct(
                (each, wide) if last else (8, wide), jnp.bfloat16 if last else jnp.float32
            ),
            in_specs=[SMEM, VMEM] + [VMEM] * len(held[k]),
            out_specs=VMEM,
            scratch_shapes=[
                pltpu.VMEM((per, group_rows, reflect), dtype),
                pltpu.VMEM((per, reflect, reflect), dtype),
            ],
            compiler_params=limit(12),
            name=f"chain{k}",
        )(offsets, state, *held[k])
    return state


def solution(mesh):
    rows, cols = mesh.shape["row"], mesh.shape["col"]
    in_specs = (
        P("row", "col"),
        P("row", "col"),
        P("col", None, None),
        P("col", None, None),
        P(),
        P(),
    )
    out_specs = P(("row", "col"), None)
    return jax.shard_map(
        functools.partial(local, rows, cols),
        mesh=mesh,
        in_specs=in_specs,
        out_specs=out_specs,
        check_vma=False,
    )
```

time: 82.1 us -> 74.8 us (0.911)
  waiting for transfers between devices: 34.8 us -> 25.7 us
  starting transfers between devices: 24.3 us -> 26.5 us
  Pallas kernels: 10.7 us -> 9.3 us
    all_to_all x1, waiting for transfers between devices: 6.6 us -> 2.03 us  [local(): slices = lax.all_to_all(packed, 'col', 0, 0, axis_index_groups=members)]
    ppermute x4, waiting for transfers between devices: 7.08 us -> 3.31 us  [over_row(): return lax.ppermute(x, 'row', [(r, r ^ mask) for r in range(rows)])]
    ppermute x18, starting transfers between devices: 12.3 us -> 14.9 us  [over_col(): return lax.ppermute(x, 'col', [(c, c ^ mask) for c in range(cols)])]
    pallas_call x5 -> x6, Pallas kernels: 10.3 us -> 8.86 us  [the longest x3 6.59 us: local(): pl.pallas_call(functools.partial(chain_kernel, cols, groups, masks[k], fi...]
    unnamed x10 -> x15, local copies, waits for them, and re-layouts: 1.33 us -> 2 us
  transfers between devices with their start and end apart: 23 -> 23, of which waited for: 13 -> 10; matrix products, arithmetic and copies ran while one was open for 0% -> 0% of each run, Pallas kernels for 8% -> 7%
where the time goes in v7:
time: 74.8 us; the launch traced here: 74.5 us
  starting transfers between devices  26.5 us (35%)
  waiting for transfers between devices  25.7 us (34%)
  blocking collectives  10.7 us (14%)
  Pallas kernels  9.3 us (12%)
  local copies, waits for them, and re-layouts  2.07 us (3%)
    ppermute x18, waiting for transfers between devices, over_col(): return lax.ppermute(x, 'col', [(c, c ^ mask) for c in range(cols)])  20.3 us
    ppermute x18, starting transfers between devices, over_col(): return lax.ppermute(x, 'col', [(c, c ^ mask) for c in range(cols)])  14.9 us
    all_to_all x1, blocking collectives, local(): lax.all_to_all(merged.reshape(rows * cols, each, width), ('row', 'col'),...  10.7 us
    pallas_call x3, Pallas kernels, local(): pl.pallas_call(functools.partial(chain_kernel, cols, groups, masks[k], fi...  6.59 us
    ppermute x4, starting transfers between devices, over_row(): return lax.ppermute(x, 'row', [(r, r ^ mask) for r in range(rows)])  6.15 us
    all_to_all x1, starting transfers between devices, local(): slices = lax.all_to_all(packed, 'col', 0, 0, axis_index_groups=members)  5.4 us
    ppermute x4, waiting for transfers between devices, over_row(): return lax.ppermute(x, 'row', [(r, r ^ mask) for r in range(rows)])  3.31 us
    all_to_all x1, waiting for transfers between devices, local(): slices = lax.all_to_all(packed, 'col', 0, 0, axis_index_groups=members)  2.03 us
  transfers between devices with their start and end apart: 23, of which 10 were waited for; matrix products, arithmetic and copies ran while one was open for 0% of the time, Pallas kernels for 7%

profile of v7, /device:TPU:0, one launch (start us, length us, event | category | flops | bytes accessed | tf_op | source)
XLA Modules:
  0.0 74.5 jit_solution(8980620709999625822)
XLA Ops:
  0.0 1.0 %copy-done.1 = bf16[1,1024,256]{2,1,0:T(8,128)(2,1)S(1)} copy-done((bf16[1,1024,256]{2,1,0:T(8,128)(2,1)S(1)}, bf16[1,1024,256]{2,1,0:T(8,128)(2,1)}, u32[]{:S(2)}) %copy-start.1) | copy-done | bytes 524312
  1.0 0.9 %copy-done.2 = bf16[1,256,256]{2,1,0:T(8,128)(2,1)S(1)} copy-done((bf16[1,256,256]{2,1,0:T(8,128)(2,1)S(1)}, bf16[1,256,256]{2,1,0:T(8,128)(2,1)}, u32[]{:S(2)}) %copy-start.2) | copy-done | bytes 131096
  1.9 0.9 %pack.1 = bf16[8,160,128]{2,1,0:T(8,128)(2,1)} custom-call(bf16[1024,256]{1,0:T(8,128)(2,1)S(1)} %bitcast.6, bf16[256,256]{1,0:T(8,128)(2,1)S(1)} %bitcast.8), custom_call_target="tpu_custom_call" | custom-call | tf_op jit(solution)/shard_map/pack/pallas_call | solution.py:182
  2.9 0.0 copy-start.5
  2.9 5.4 %all-to-all-start = ((bf16[8,160,128]{2,1,0:T(8,128)(2,1)}), bf16[8,160,128]{2,1,0:T(8,128)(2,1)S(1)}, u32[]{:S(2)}, u32[]{:S(2)}) async-start(bf16[8,160,128]{2,1,0:T(8,128)(2,1)} %pack.1), calls=%async_computation | async-start | bytes 655360 | tf_op jit(solution)/shard_map/all_to_all | solution.py:196
  8.3 2.7 %collective-permute-start = (bf16[64,512]{1,0:T(8,128)(2,1)S(1)}, bf16[64,512]{1,0:T(8,128)(2,1)S(1)}, u32[]{:S(2)}, u32[]{:S(2)}) collective-permute-start(bf16[64,512]{1,0:T(8,128)(2,1)S(1)} %copy-done.5), channel_id=1, source_target_pairs={{0,8},{1,9},{2,10},{3,11},{4,12},{5,13},{6,14},{7,15},{8,0},{9,1},... | collective-permute-start | bytes 196616 | tf_op jit(solution)/shard_map/ppermute | solution.py:170
  10.9 3.4 %collective-permute-done = bf16[64,512]{1,0:T(8,128)(2,1)S(1)} collective-permute-done((bf16[64,512]{1,0:T(8,128)(2,1)S(1)}, bf16[64,512]{1,0:T(8,128)(2,1)S(1)}, u32[]{:S(2)}, u32[]{:S(2)}) %collective-permute-start) | collective-permute-done | bytes 65568 | tf_op jit(solution)/shard_map/ppermute | solution.py:170
  14.4 2.0 %all-to-all-done.held = bf16[8,160,128]{2,1,0:T(8,128)(2,1)S(1)} async-done(((bf16[8,160,128]{2,1,0:T(8,128)(2,1)}), bf16[8,160,128]{2,1,0:T(8,128)(2,1)S(1)}, u32[]{:S(2)}, u32[]{:S(2)}) %all-to-all-start) | async-done | bytes 327712 | tf_op jit(solution)/shard_map/all_to_all | solution.py:196
  16.4 1.6 %collective-permute-start.2 = (bf16[64,512]{1,0:T(8,128)(2,1)S(1)}, bf16[64,512]{1,0:T(8,128)(2,1)S(1)}, u32[]{:S(2)}, u32[]{:S(2)}) collective-permute-start(bf16[64,512]{1,0:T(8,128)(2,1)S(1)} %get-tuple-element.38), channel_id=1, source_target_pairs={{0,16},{16,0},{1,17},{17,1},{2,18},{18,2},{3,19},{19,3},{4,20},{20... | collective-permute-start | bytes 196616 | tf_op jit(solution)/shard_map/ppermute | solution.py:173
  18.0 2.8 %collective-permute-done.2 = bf16[64,512]{1,0:T(8,128)(2,1)S(1)} collective-permute-done((bf16[64,512]{1,0:T(8,128)(2,1)S(1)}, bf16[64,512]{1,0:T(8,128)(2,1)S(1)}, u32[]{:S(2)}, u32[]{:S(2)}) %collective-permute-start.2) | collective-permute-done | bytes 65568 | tf_op jit(solution)/shard_map/ppermute | solution.py:173
  20.8 2.7 %collective-permute-start.3 = (bf16[2,64,512]{2,1,0:T(8,128)(2,1)S(1)}, bf16[2,64,512]{2,1,0:T(8,128)(2,1)S(1)}, u32[]{:S(2)}, u32[]{:S(2)}) collective-permute-start(bf16[2,64,512]{2,1,0:T(8,128)(2,1)S(1)} %pad_maximum_fusion.4), channel_id=1, source_target_pairs={{0,4},{1,5},{2,6},{3,7},{4,0},{5,1},{6,2},{7,3},{8,12},{9,13},{10,... | collective-permute-start | bytes 393224 | tf_op jit(solution)/shard_map/ppermute | solution.py:170
  23.5 0.7 pick.1
  24.2 0.5 collective-permute-start.1
  24.7 2.5 %collective-permute-done.3 = bf16[2,64,512]{2,1,0:T(8,128)(2,1)S(1)} collective-permute-done((bf16[2,64,512]{2,1,0:T(8,128)(2,1)S(1)}, bf16[2,64,512]{2,1,0:T(8,128)(2,1)S(1)}, u32[]{:S(2)}, u32[]{:S(2)}) %collective-permute-start.3) | collective-permute-done | bytes 131104 | tf_op jit(solution)/shard_map/ppermute | solution.py:170
  27.2 7.6 %collective-permute-done.1.refs_0_ = bf16[5,160,128]{2,1,0:T(8,128)(2,1)S(1)} collective-permute-done((bf16[5,160,128]{2,1,0:T(8,128)(2,1)S(1)}, bf16[5,160,128]{2,1,0:T(8,128)(2,1)S(1)}, u32[]{:S(2)}, u32[]{:S(2)}) %collective-permute-start.1) | collective-permute-done | bytes 204832 | tf_op jit(solution)/shard_map/ppermute | solution.py:170
  34.8 0.7 order.1
  35.4 0.1 collective-permute-start.6
  35.5 1.5 %collective-permute-start.7 = (bf16[4,64,512]{2,1,0:T(8,128)(2,1)S(1)}, bf16[4,64,512]{2,1,0:T(8,128)(2,1)S(1)}, u32[]{:S(2)}, u32[]{:S(2)}) collective-permute-start(bf16[4,64,512]{2,1,0:T(8,128)(2,1)S(1)} %pad_maximum_fusion.refs_0_), channel_id=1, source_target_pairs={{0,2},{1,3},{2,0},{3,1},{4,6},{5,7},{6,4},{7,5},{8,10},{9,11},{10,... | collective-permute-start | bytes 786440 | tf_op jit(solution)/shard_map/ppermute | solution.py:170
  37.0 0.0 collective-permute-start.14
  37.0 0.6 collective-permute-start.5
  37.6 1.5 %collective-permute-start.4 = (bf16[1,2,160,128]{3,2,1,0:T(8,128)(2,1)S(1)}, bf16[1,2,160,128]{3,2,1,0:T(8,128)(2,1)S(1)}, u32[]{:S(2)}, u32[]{:S(2)}) collective-permute-start(bf16[1,2,160,128]{3,2,1,0:T(8,128)(2,1)S(1)} %get-tuple-element.25), channel_id=1, source_target_pairs={{0,16},{16,0},{1,17},{17,1},{2,18},{18,2},{3,19},{19,3},{4,20},{20... | collective-permute-start | bytes 245768 | tf_op jit(solution)/shard_map/ppermute | solution.py:173
  39.1 0.8 %collective-permute-done.6 = bf16[1,2,160,128]{3,2,1,0:T(8,128)(2,1)S(1)} collective-permute-done((bf16[1,2,160,128]{3,2,1,0:T(8,128)(2,1)S(1)}, bf16[1,2,160,128]{3,2,1,0:T(8,128)(2,1)S(1)}, u32[]{:S(2)}, u32[]{:S(2)}) %collective-permute-start.6) | collective-permute-done | bytes 81952 | tf_op jit(solution)/shard_map/ppermute | solution.py:170
  39.9 4.7 %collective-permute-done.5 = bf16[1,2,160,128]{3,2,1,0:T(8,128)(2,1)S(1)} collective-permute-done((bf16[1,2,160,128]{3,2,1,0:T(8,128)(2,1)S(1)}, bf16[1,2,160,128]{3,2,1,0:T(8,128)(2,1)S(1)}, u32[]{:S(2)}, u32[]{:S(2)}) %collective-permute-start.5) | collective-permute-done | bytes 81952 | tf_op jit(solution)/shard_map/ppermute | solution.py:170
  44.6 0.0 collective-permute-done.4
  44.7 0.0 copy-start
  44.7 0.0 collective-permute-done.7.refs_2_
  44.7 1.6 %collective-permute-start.12 = (bf16[2,2,160,128]{3,2,1,0:T(8,128)(2,1)S(1)}, bf16[2,2,160,128]{3,2,1,0:T(8,128)(2,1)S(1)}, u32[]{:S(2)}, u32[]{:S(2)}) collective-permute-start(bf16[2,2,160,128]{3,2,1,0:T(8,128)(2,1)S(1)} %pad_maximum_fusion.3), channel_id=1, source_target_pairs={{0,16},{16,0},{1,17},{17,1},{2,18},{18,2},{3,19},{19,3},{4,20},{20... | collective-permute-start | bytes 491528 | tf_op jit(solution)/shard_map/ppermute | solution.py:173
  46.3 1.7 %collective-permute-start.10 = (bf16[2,2,160,128]{3,2,1,0:T(8,128)(2,1)S(1)}, bf16[2,2,160,128]{3,2,1,0:T(8,128)(2,1)S(1)}, u32[]{:S(2)}, u32[]{:S(2)}) collective-permute-start(bf16[2,2,160,128]{3,2,1,0:T(8,128)(2,1)S(1)} %pad_maximum_fusion.2), channel_id=1, source_target_pairs={{0,4},{1,5},{2,6},{3,7},{4,0},{5,1},{6,2},{7,3},{8,12},{9,13},{10,... | collective-permute-start | bytes 491528 | tf_op jit(solution)/shard_map/ppermute | solution.py:170
  48.0 1.5 %collective-permute-start.8 = (bf16[2,2,160,128]{3,2,1,0:T(8,128)(2,1)S(1)}, bf16[2,2,160,128]{3,2,1,0:T(8,128)(2,1)S(1)}, u32[]{:S(2)}, u32[]{:S(2)}) collective-permute-start(bf16[2,2,160,128]{3,2,1,0:T(8,128)(2,1)S(1)} %pad_maximum_fusion.1), channel_id=1, source_target_pairs={{0,2},{1,3},{2,0},{3,1},{4,6},{5,7},{6,4},{7,5},{8,10},{9,11},{10,... | collective-permute-start | bytes 491528 | tf_op jit(solution)/shard_map/ppermute | solution.py:170
  49.6 0.5 collective-permute-done.12
  50.1 1.5 %collective-permute-start.13 = (bf16[4,2,160,128]{3,2,1,0:T(8,128)(2,1)S(1)}, bf16[4,2,160,128]{3,2,1,0:T(8,128)(2,1)S(1)}, u32[]{:S(2)}, u32[]{:S(2)}) collective-permute-start(bf16[4,2,160,128]{3,2,1,0:T(8,128)(2,1)S(1)} %constant_dynamic-update-slice_fusion.4.refs_0_), channel_id=1, source_target_pairs={{0,2},{1,3},{2,0},{3,1},{4,6},{5,7},{6,4},{7,5},{8,10},{9,11},{10,... | collective-permute-start | bytes 983048 | tf_op jit(solution)/shard_map/ppermute | solution.py:170
  51.6 0.0 collective-permute-done.10
  51.7 1.5 %collective-permute-start.11 = (bf16[4,2,160,128]{3,2,1,0:T(8,128)(2,1)S(1)}, bf16[4,2,160,128]{3,2,1,0:T(8,128)(2,1)S(1)}, u32[]{:S(2)}, u32[]{:S(2)}) collective-permute-start(bf16[4,2,160,128]{3,2,1,0:T(8,128)(2,1)S(1)} %constant_dynamic-update-slice_fusion.2.refs_0_), channel_id=1, source_target_pairs={{0,16},{16,0},{1,17},{17,1},{2,18},{18,2},{3,19},{19,3},{4,20},{20... | collective-permute-start | bytes 983048 | tf_op jit(solution)/shard_map/ppermute | solution.py:173
  53.2 0.8 %collective-permute-done.8 = bf16[2,2,160,128]{3,2,1,0:T(8,128)(2,1)S(1)} collective-permute-done((bf16[2,2,160,128]{3,2,1,0:T(8,128)(2,1)S(1)}, bf16[2,2,160,128]{3,2,1,0:T(8,128)(2,1)S(1)}, u32[]{:S(2)}, u32[]{:S(2)}) %collective-permute-start.8) | collective-permute-done | bytes 163872 | tf_op jit(solution)/shard_map/ppermute | solution.py:170
  54.1 0.9 %collective-permute-start.9 = (bf16[4,2,160,128]{3,2,1,0:T(8,128)(2,1)S(1)}, bf16[4,2,160,128]{3,2,1,0:T(8,128)(2,1)S(1)}, u32[]{:S(2)}, u32[]{:S(2)}) collective-permute-start(bf16[4,2,160,128]{3,2,1,0:T(8,128)(2,1)S(1)} %constant_dynamic-update-slice_fusion.refs_0_), channel_id=1, source_target_pairs={{0,4},{1,5},{2,6},{3,7},{4,0},{5,1},{6,2},{7,3},{8,12},{9,13},{10,... | collective-permute-start | bytes 983048 | tf_op jit(solution)/shard_map/ppermute | solution.py:170
  55.0 0.0 collective-permute-done.14.refs_1_
  55.0 0.4 merge.1
  55.5 0.0 copy-start.3
  55.5 10.7 %all_to_all.10.start = f32[32,4,128]{2,1,0:T(4,128)S(1)} all-to-all(f32[32,4,128]{2,1,0:T(4,128)S(1)} %bitcast.7), channel_id=1, replica_groups=mesh['row'=2,'col'=16] {'row','col'}, dimensions={0} | all-to-all | bytes 131072 | tf_op jit(solution)/shard_map/all_to_all | solution.py:261
  66.2 0.2 collective-permute-start.17
  66.3 0.4 collective-permute-start.18
  66.7 0.1 collective-permute-start.20
  66.8 0.4 collective-permute-start.19
  67.2 0.1 collective-permute-start.21
  67.4 0.5 collective-permute-done.17.refs_3_
  67.9 2.0 %chain0.1.start = f32[8,2048]{1,0:T(8,128)S(1)} custom-call(s32[6]{0:T(128)S(1)} %copy-done.3, f32[32,4,128]{2,1,0:T(4,128)S(1)} %all_to_all.10.start, bf16[4,2,160,128]{3,2,1,0:T(8,128)(2,1)S(1)} %constant_dynamic-update-slice_fusion.refs_0_, bf16[4,2,160,128]{3,2,1,0:T(8,128)(2,1)S(1)} %collective-permute-done.9.refs_1_, ...), custom_call_target="tpu_custom_call" | custom-call | tf_op jit(solution)/shard_map/chain0/pallas_call | solution.py:278
  69.9 2.0 %chain1.1.start = f32[8,2048]{1,0:T(8,128)S(1)} custom-call(s32[6]{0:T(128)S(1)} %copy-done.3, f32[8,2048]{1,0:T(8,128)S(1)} %chain0.1.start, bf16[4,2,160,128]{3,2,1,0:T(8,128)(2,1)S(1)} %constant_dynamic-update-slice_fusion.2.refs_0_, bf16[4,2,160,128]{3,2,1,0:T(8,128)(2,1)S(1)} %collective-permute-done.11.refs_1_, ...), custom_call_target="tpu_custom_call" | custom-call | tf_op jit(solution)/shard_map/chain1/pallas_call | solution.py:278
  71.9 2.6 %chain2.1 = bf16[4,2048]{1,0:T(4,128)(2,1)} custom-call(s32[6]{0:T(128)S(1)} %copy-done.3, f32[8,2048]{1,0:T(8,128)S(1)} %chain1.1.start, bf16[4,2,160,128]{3,2,1,0:T(8,128)(2,1)S(1)} %constant_dynamic-update-slice_fusion.4.refs_0_, bf16[4,2,160,128]{3,2,1,0:T(8,128)(2,1)S(1)} %collective-permute-done.13.refs_1_, ...), custom_call_target="tpu_custom_call" | custom-call | tf_op jit(solution)/shard_map/chain2/pallas_call | solution.py:278
  (30 shorter events, 0.3 us)
Async XLA Ops:
  0.0 1.0 %copy-start.1 = (bf16[1,1024,256]{2,1,0:T(8,128)(2,1)S(1)}, bf16[1,1024,256]{2,1,0:T(8,128)(2,1)}, u32[]{:S(2)}) copy-start(bf16[1,1024,256]{2,1,0:T(8,128)(2,1)} %param.8) | copy-start | bytes 1572868
  1.0 0.9 %copy-start.2 = (bf16[1,256,256]{2,1,0:T(8,128)(2,1)S(1)}, bf16[1,256,256]{2,1,0:T(8,128)(2,1)}, u32[]{:S(2)}) copy-start(bf16[1,256,256]{2,1,0:T(8,128)(2,1)} %param.9) | copy-start | bytes 393220
  2.9 5.4 %copy-start.5 = (bf16[64,512]{1,0:T(8,128)(2,1)S(1)}, bf16[64,512]{1,0:T(8,128)(2,1)}, u32[]{:S(2)}) copy-start(bf16[64,512]{1,0:T(8,128)(2,1)} %param.7) | copy-start | bytes 196612
  2.9 13.5 %all-to-all-start = ((bf16[8,160,128]{2,1,0:T(8,128)(2,1)}), bf16[8,160,128]{2,1,0:T(8,128)(2,1)S(1)}, u32[]{:S(2)}, u32[]{:S(2)}) async-start(bf16[8,160,128]{2,1,0:T(8,128)(2,1)} %pack.1), calls=%async_computation | async-start | bytes 655360 | tf_op jit(solution)/shard_map/all_to_all | solution.py:196
  8.3 6.1 %collective-permute-start = (bf16[64,512]{1,0:T(8,128)(2,1)S(1)}, bf16[64,512]{1,0:T(8,128)(2,1)S(1)}, u32[]{:S(2)}, u32[]{:S(2)}) collective-permute-start(bf16[64,512]{1,0:T(8,128)(2,1)S(1)} %copy-done.5), channel_id=1, source_target_pairs={{0,8},{1,9},{2,10},{3,11},{4,12},{5,13},{6,14},{7,15},{8,0},{9,1},... | collective-permute-start | bytes 196616 | tf_op jit(solution)/shard_map/ppermute | solution.py:170
  16.4 4.3 %collective-permute-start.2 = (bf16[64,512]{1,0:T(8,128)(2,1)S(1)}, bf16[64,512]{1,0:T(8,128)(2,1)S(1)}, u32[]{:S(2)}, u32[]{:S(2)}) collective-permute-start(bf16[64,512]{1,0:T(8,128)(2,1)S(1)} %get-tuple-element.38), channel_id=1, source_target_pairs={{0,16},{16,0},{1,17},{17,1},{2,18},{18,2},{3,19},{19,3},{4,20},{20... | collective-permute-start | bytes 196616 | tf_op jit(solution)/shard_map/ppermute | solution.py:173
  20.8 2.7 %copy-start.4 = (s32[6]{0:T(128)S(1)}, s32[6]{0:T(128)}, u32[]{:S(2)}) copy-start(s32[6]{0:T(128)} %owners.3) | copy-start | bytes 76
  20.8 6.4 %collective-permute-start.3 = (bf16[2,64,512]{2,1,0:T(8,128)(2,1)S(1)}, bf16[2,64,512]{2,1,0:T(8,128)(2,1)S(1)}, u32[]{:S(2)}, u32[]{:S(2)}) collective-permute-start(bf16[2,64,512]{2,1,0:T(8,128)(2,1)S(1)} %pad_maximum_fusion.4), channel_id=1, source_target_pairs={{0,4},{1,5},{2,6},{3,7},{4,0},{5,1},{6,2},{7,3},{8,12},{9,13},{10,... | collective-permute-start | bytes 393224 | tf_op jit(solution)/shard_map/ppermute | solution.py:170
  24.2 10.5 %collective-permute-start.1 = (bf16[5,160,128]{2,1,0:T(8,128)(2,1)S(1)}, bf16[5,160,128]{2,1,0:T(8,128)(2,1)S(1)}, u32[]{:S(2)}, u32[]{:S(2)}) collective-permute-start(bf16[5,160,128]{2,1,0:T(8,128)(2,1)S(1)} %pick.1), channel_id=1, source_target_pairs={{0,8},{1,9},{2,10},{3,11},{4,12},{5,13},{6,14},{7,15},{8,0},{9,1},... | collective-permute-start | bytes 614408 | tf_op jit(solution)/shard_map/ppermute | solution.py:170
  35.4 4.5 %collective-permute-start.6 = (bf16[1,2,160,128]{3,2,1,0:T(8,128)(2,1)S(1)}, bf16[1,2,160,128]{3,2,1,0:T(8,128)(2,1)S(1)}, u32[]{:S(2)}, u32[]{:S(2)}) collective-permute-start(bf16[1,2,160,128]{3,2,1,0:T(8,128)(2,1)S(1)} %get-tuple-element.27), channel_id=1, source_target_pairs={{0,4},{1,5},{2,6},{3,7},{4,0},{5,1},{6,2},{7,3},{8,12},{9,13},{10,... | collective-permute-start | bytes 245768 | tf_op jit(solution)/shard_map/ppermute | solution.py:170
  35.5 9.2 %collective-permute-start.7 = (bf16[4,64,512]{2,1,0:T(8,128)(2,1)S(1)}, bf16[4,64,512]{2,1,0:T(8,128)(2,1)S(1)}, u32[]{:S(2)}, u32[]{:S(2)}) collective-permute-start(bf16[4,64,512]{2,1,0:T(8,128)(2,1)S(1)} %pad_maximum_fusion.refs_0_), channel_id=1, source_target_pairs={{0,2},{1,3},{2,0},{3,1},{4,6},{5,7},{6,4},{7,5},{8,10},{9,11},{10,... | collective-permute-start | bytes 786440 | tf_op jit(solution)/shard_map/ppermute | solution.py:170
  37.0 18.0 %collective-permute-start.14 = (bf16[4,64,512]{2,1,0:T(8,128)(2,1)S(1)}, bf16[4,64,512]{2,1,0:T(8,128)(2,1)S(1)}, u32[]{:S(2)}, u32[]{:S(2)}) collective-permute-start(bf16[4,64,512]{2,1,0:T(8,128)(2,1)S(1)} %pad_maximum_fusion.refs_0_), channel_id=1, source_target_pairs={{0,1},{1,0},{2,3},{3,2},{4,5},{5,4},{6,7},{7,6},{8,9},{9,8},{10,11... | collective-permute-start | bytes 786440 | tf_op jit(solution)/shard_map/ppermute | solution.py:170
  37.0 7.6 %collective-permute-start.5 = (bf16[1,2,160,128]{3,2,1,0:T(8,128)(2,1)S(1)}, bf16[1,2,160,128]{3,2,1,0:T(8,128)(2,1)S(1)}, u32[]{:S(2)}, u32[]{:S(2)}) collective-permute-start(bf16[1,2,160,128]{3,2,1,0:T(8,128)(2,1)S(1)} %get-tuple-element.26), channel_id=1, source_target_pairs={{0,2},{1,3},{2,0},{3,1},{4,6},{5,7},{6,4},{7,5},{8,10},{9,11},{10,... | collective-permute-start | bytes 245768 | tf_op jit(solution)/shard_map/ppermute | solution.py:170
  37.6 7.0 %collective-permute-start.4 = (bf16[1,2,160,128]{3,2,1,0:T(8,128)(2,1)S(1)}, bf16[1,2,160,128]{3,2,1,0:T(8,128)(2,1)S(1)}, u32[]{:S(2)}, u32[]{:S(2)}) collective-permute-start(bf16[1,2,160,128]{3,2,1,0:T(8,128)(2,1)S(1)} %get-tuple-element.25), channel_id=1, source_target_pairs={{0,16},{16,0},{1,17},{17,1},{2,18},{18,2},{3,19},{19,3},{4,20},{20... | collective-permute-start | bytes 245768 | tf_op jit(solution)/shard_map/ppermute | solution.py:173
  44.7 10.4 %copy-start = (bf16[4096,128]{1,0:T(8,128)(2,1)S(1)}, bf16[4096,128]{1,0:T(8,128)(2,1)}, u32[]{:S(2)}) copy-start(bf16[4096,128]{1,0:T(8,128)(2,1)} %sub.6) | copy-start | bytes 3145732
  44.7 5.4 %collective-permute-start.12 = (bf16[2,2,160,128]{3,2,1,0:T(8,128)(2,1)S(1)}, bf16[2,2,160,128]{3,2,1,0:T(8,128)(2,1)S(1)}, u32[]{:S(2)}, u32[]{:S(2)}) collective-permute-start(bf16[2,2,160,128]{3,2,1,0:T(8,128)(2,1)S(1)} %pad_maximum_fusion.3), channel_id=1, source_target_pairs={{0,16},{16,0},{1,17},{17,1},{2,18},{18,2},{3,19},{19,3},{4,20},{20... | collective-permute-start | bytes 491528 | tf_op jit(solution)/shard_map/ppermute | solution.py:173
  46.3 5.4 %collective-permute-start.10 = (bf16[2,2,160,128]{3,2,1,0:T(8,128)(2,1)S(1)}, bf16[2,2,160,128]{3,2,1,0:T(8,128)(2,1)S(1)}, u32[]{:S(2)}, u32[]{:S(2)}) collective-permute-start(bf16[2,2,160,128]{3,2,1,0:T(8,128)(2,1)S(1)} %pad_maximum_fusion.2), channel_id=1, source_target_pairs={{0,4},{1,5},{2,6},{3,7},{4,0},{5,1},{6,2},{7,3},{8,12},{9,13},{10,... | collective-permute-start | bytes 491528 | tf_op jit(solution)/shard_map/ppermute | solution.py:170
  48.0 6.0 %collective-permute-start.8 = (bf16[2,2,160,128]{3,2,1,0:T(8,128)(2,1)S(1)}, bf16[2,2,160,128]{3,2,1,0:T(8,128)(2,1)S(1)}, u32[]{:S(2)}, u32[]{:S(2)}) collective-permute-start(bf16[2,2,160,128]{3,2,1,0:T(8,128)(2,1)S(1)} %pad_maximum_fusion.1), channel_id=1, source_target_pairs={{0,2},{1,3},{2,0},{3,1},{4,6},{5,7},{6,4},{7,5},{8,10},{9,11},{10,... | collective-permute-start | bytes 491528 | tf_op jit(solution)/shard_map/ppermute | solution.py:170
  49.6 5.5 %collective-permute-start.15 = (bf16[4,64,512]{2,1,0:T(8,128)(2,1)S(1)}, bf16[4,64,512]{2,1,0:T(8,128)(2,1)S(1)}, u32[]{:S(2)}, u32[]{:S(2)}) collective-permute-start(bf16[4,64,512]{2,1,0:T(8,128)(2,1)S(1)} %collective-permute-done.7.refs_2_), channel_id=1, source_target_pairs={{0,1},{1,0},{2,3},{3,2},{4,5},{5,4},{6,7},{7,6},{8,9},{9,8},{10,11... | collective-permute-start | bytes 786440 | tf_op jit(solution)/shard_map/ppermute | solution.py:170
  50.1 16.0 %collective-permute-start.13 = (bf16[4,2,160,128]{3,2,1,0:T(8,128)(2,1)S(1)}, bf16[4,2,160,128]{3,2,1,0:T(8,128)(2,1)S(1)}, u32[]{:S(2)}, u32[]{:S(2)}) collective-permute-start(bf16[4,2,160,128]{3,2,1,0:T(8,128)(2,1)S(1)} %constant_dynamic-update-slice_fusion.4.refs_0_), channel_id=1, source_target_pairs={{0,2},{1,3},{2,0},{3,1},{4,6},{5,7},{6,4},{7,5},{8,10},{9,11},{10,... | collective-permute-start | bytes 983048 | tf_op jit(solution)/shard_map/ppermute | solution.py:170
  51.7 14.5 %collective-permute-start.11 = (bf16[4,2,160,128]{3,2,1,0:T(8,128)(2,1)S(1)}, bf16[4,2,160,128]{3,2,1,0:T(8,128)(2,1)S(1)}, u32[]{:S(2)}, u32[]{:S(2)}) collective-permute-start(bf16[4,2,160,128]{3,2,1,0:T(8,128)(2,1)S(1)} %constant_dynamic-update-slice_fusion.2.refs_0_), channel_id=1, source_target_pairs={{0,16},{16,0},{1,17},{17,1},{2,18},{18,2},{3,19},{19,3},{4,20},{20... | collective-permute-start | bytes 983048 | tf_op jit(solution)/shard_map/ppermute | solution.py:173
  54.1 12.1 %collective-permute-start.9 = (bf16[4,2,160,128]{3,2,1,0:T(8,128)(2,1)S(1)}, bf16[4,2,160,128]{3,2,1,0:T(8,128)(2,1)S(1)}, u32[]{:S(2)}, u32[]{:S(2)}) collective-permute-start(bf16[4,2,160,128]{3,2,1,0:T(8,128)(2,1)S(1)} %constant_dynamic-update-slice_fusion.refs_0_), channel_id=1, source_target_pairs={{0,4},{1,5},{2,6},{3,7},{4,0},{5,1},{6,2},{7,3},{8,12},{9,13},{10,... | collective-permute-start | bytes 983048 | tf_op jit(solution)/shard_map/ppermute | solution.py:170
  55.0 12.2 %collective-permute-start.16 = (bf16[4,2,160,128]{3,2,1,0:T(8,128)(2,1)S(1)}, bf16[4,2,160,128]{3,2,1,0:T(8,128)(2,1)S(1)}, u32[]{:S(2)}, u32[]{:S(2)}) collective-permute-start(bf16[4,2,160,128]{3,2,1,0:T(8,128)(2,1)S(1)} %constant_dynamic-update-slice_fusion.refs_0_), channel_id=1, source_target_pairs={{0,1},{1,0},{2,3},{3,2},{4,5},{5,4},{6,7},{7,6},{8,9},{9,8},{10,11... | collective-permute-start | bytes 983048 | tf_op jit(solution)/shard_map/ppermute | solution.py:170
  55.5 12.4 %copy-start.3 = (s32[6]{0:T(128)S(1)}, s32[6]{0:T(128)}, u32[]{:S(2)}) copy-start(s32[6]{0:T(128)} %offsets.5) | copy-start | bytes 76
  66.2 1.7 %collective-permute-start.17 = (bf16[4,2,160,128]{3,2,1,0:T(8,128)(2,1)S(1)}, bf16[4,2,160,128]{3,2,1,0:T(8,128)(2,1)S(1)}, u32[]{:S(2)}, u32[]{:S(2)}) collective-permute-start(bf16[4,2,160,128]{3,2,1,0:T(8,128)(2,1)S(1)} %collective-permute-done.9.refs_1_), channel_id=1, source_target_pairs={{0,1},{1,0},{2,3},{3,2},{4,5},{5,4},{6,7},{7,6},{8,9},{9,8},{10,11... | collective-permute-start | bytes 983048 | tf_op jit(solution)/shard_map/ppermute | solution.py:170
  66.3 3.5 %collective-permute-start.18 = (bf16[4,2,160,128]{3,2,1,0:T(8,128)(2,1)S(1)}, bf16[4,2,160,128]{3,2,1,0:T(8,128)(2,1)S(1)}, u32[]{:S(2)}, u32[]{:S(2)}) collective-permute-start(bf16[4,2,160,128]{3,2,1,0:T(8,128)(2,1)S(1)} %constant_dynamic-update-slice_fusion.2.refs_0_), channel_id=1, source_target_pairs={{0,1},{1,0},{2,3},{3,2},{4,5},{5,4},{6,7},{7,6},{8,9},{9,8},{10,11... | collective-permute-start | bytes 983048 | tf_op jit(solution)/shard_map/ppermute | solution.py:170
  66.7 5.1 %collective-permute-start.20 = (bf16[4,2,160,128]{3,2,1,0:T(8,128)(2,1)S(1)}, bf16[4,2,160,128]{3,2,1,0:T(8,128)(2,1)S(1)}, u32[]{:S(2)}, u32[]{:S(2)}) collective-permute-start(bf16[4,2,160,128]{3,2,1,0:T(8,128)(2,1)S(1)} %constant_dynamic-update-slice_fusion.4.refs_0_), channel_id=1, source_target_pairs={{0,1},{1,0},{2,3},{3,2},{4,5},{5,4},{6,7},{7,6},{8,9},{9,8},{10,11... | collective-permute-start | bytes 983048 | tf_op jit(solution)/shard_map/ppermute | solution.py:170
  66.8 3.0 %collective-permute-start.19 = (bf16[4,2,160,128]{3,2,1,0:T(8,128)(2,1)S(1)}, bf16[4,2,160,128]{3,2,1,0:T(8,128)(2,1)S(1)}, u32[]{:S(2)}, u32[]{:S(2)}) collective-permute-start(bf16[4,2,160,128]{3,2,1,0:T(8,128)(2,1)S(1)} %collective-permute-done.11.refs_1_), channel_id=1, source_target_pairs={{0,1},{1,0},{2,3},{3,2},{4,5},{5,4},{6,7},{7,6},{8,9},{9,8},{10,11... | collective-permute-start | bytes 983048 | tf_op jit(solution)/shard_map/ppermute | solution.py:170
  67.2 4.6 %collective-permute-start.21 = (bf16[4,2,160,128]{3,2,1,0:T(8,128)(2,1)S(1)}, bf16[4,2,160,128]{3,2,1,0:T(8,128)(2,1)S(1)}, u32[]{:S(2)}, u32[]{:S(2)}) collective-permute-start(bf16[4,2,160,128]{3,2,1,0:T(8,128)(2,1)S(1)} %collective-permute-done.13.refs_1_), channel_id=1, source_target_pairs={{0,1},{1,0},{2,3},{3,2},{4,5},{5,4},{6,7},{7,6},{8,9},{9,8},{10,11... | collective-permute-start | bytes 983048 | tf_op jit(solution)/shard_map/ppermute | solution.py:170

commit v8 on v7

--- a/solution.py
+++ b/solution.py
@@ -11,10 +11,9 @@
 COLOURS = 3
 HALF = 8
 SLICES = 2 * HALF
-LANES = 128
 VMEM = pl.BlockSpec(memory_space=pltpu.VMEM)
 SMEM = pl.BlockSpec(memory_space=pltpu.SMEM)
-ANY = pl.BlockSpec(memory_space=pl.ANY)
+HBM = pl.BlockSpec(memory_space=pltpu.HBM)
 
 
 def limit(mib):
@@ -30,26 +29,17 @@
     return pl.ds(pl.multiple_of(index * size, size), size)
 
 
-def pack_kernel(basis_hbm, factor_hbm, out, basis, factor, sems):
-    row_bit = lax.rem(lax.axis_index("row"), 2)
-    first = pltpu.make_async_copy(
-        basis_hbm.at[aligned(row_bit, basis.shape[0])], basis, sems.at[0]
-    )
-    second = pltpu.make_async_copy(
-        factor_hbm.at[aligned(row_bit, factor.shape[0])], factor, sems.at[1]
-    )
-    first.start()
-    second.start()
-    first.wait()
-    second.wait()
-    pv, pt = basis.shape[0] // HALF, factor.shape[0] // HALF
-    lanes = basis.shape[1] // LANES
-    for c in range(HALF):
-        for k in range(lanes):
-            at = slice(k * LANES, (k + 1) * LANES)
-            out[c, k * pv : (k + 1) * pv, :] = basis[c * pv : (c + 1) * pv, at]
-            low = lanes * pv + k * pt
-            out[c, low : low + pt, :] = factor[c * pt : (c + 1) * pt, at]
+def pack_kernel(basis, factor, out, sems):
+    at = aligned(lax.rem(lax.axis_index("row"), 2), HALF)
+    pv = basis.shape[1]
+    copies = [
+        pltpu.make_async_copy(basis.at[at], out.at[:, :pv, :], sems.at[0]),
+        pltpu.make_async_copy(factor.at[at], out.at[:, pv:, :], sems.at[1]),
+    ]
+    for copy in copies:
+        copy.start()
+    for copy in copies:
+        copy.wait()
 
 
 def places(owners, group):
@@ -113,17 +103,12 @@
 def chain_kernel(cols, groups, masks, first, last, offsets, start, *refs):
     held, (out, basis_all, factor_all) = refs[: len(masks)], refs[len(masks) :]
     mine = slice_index()
-    lanes = basis_all.shape[2] // LANES
-    pv = basis_all.shape[1] // SLICES
-    pt = factor_all.shape[1] // SLICES
+    pv, pt = basis_all.shape[1] // SLICES, factor_all.shape[1] // SLICES
     for own_masks, ref in zip(masks, held):
         for index, mask in enumerate(own_masks):
             e = jnp.bitwise_xor(mine, mask)
-            for k in range(lanes):
-                at = slice(k * LANES, (k + 1) * LANES)
-                basis_all[:, aligned(e, pv), at] = ref[index, :, k * pv : (k + 1) * pv, :]
-                low = lanes * pv + k * pt
-                factor_all[:, aligned(e, pt), at] = ref[index, :, low : low + pt, :]
+            basis_all[:, aligned(e, pv), :] = ref[index, :, :pv, :]
+            factor_all[:, aligned(e, pt), :] = ref[index, :, pv:, :]
     if first:
         n, each, width = start.shape
         pieces = start[...].reshape(n // cols, cols, each, width).sum(0)
@@ -175,35 +160,32 @@
     basis, factor = reflectors[0], wy_factors[0]
     group_rows, reflect = basis.shape
     dtype = basis.dtype
-    tall = (group_rows + reflect) * (reflect // LANES) // SLICES
+    pv, pt = group_rows // SLICES, reflect // SLICES
+    piece = (pv + pt, reflect)
 
     across = [merge_factor] + [over_col(merge_factor, m * share) for m in range(1, rows)]
 
     packed = pl.pallas_call(
         pack_kernel,
-        out_shape=jax.ShapeDtypeStruct((HALF, tall, LANES), dtype),
-        in_specs=[ANY, ANY],
+        out_shape=jax.ShapeDtypeStruct((HALF,) + piece, dtype),
+        in_specs=[HBM, HBM],
         out_specs=VMEM,
-        scratch_shapes=[
-            pltpu.VMEM((group_rows // 2, reflect), dtype),
-            pltpu.VMEM((factor.shape[0] // 2, reflect), dtype),
-            pltpu.SemaphoreType.DMA((2,)),
-        ],
-        compiler_params=limit(4),
+        scratch_shapes=[pltpu.SemaphoreType.DMA((2,))],
+        compiler_params=limit(2),
         name="pack",
-    )(basis, factor)
+    )(basis.reshape(SLICES, pv, reflect), factor.reshape(SLICES, pt, reflect))
     members = [[h * HALF + c for c in range(HALF)] for h in range(halves)]
     slices = lax.all_to_all(packed, "col", 0, 0, axis_index_groups=members)
-    slices, across = lax.optimization_barrier((slices, across))
 
     picked = pl.pallas_call(
         pick_kernel,
-        out_shape=jax.ShapeDtypeStruct((GROUPS - 1, tall, LANES), dtype),
+        out_shape=jax.ShapeDtypeStruct((GROUPS - 1,) + piece, dtype),
         in_specs=[SMEM, VMEM],
         out_specs=VMEM,
         compiler_params=limit(4),
         name="pick",
     )(owners, slices)
+    picked, across = lax.optimization_barrier((picked, across))
     others = [over_col(picked, m * HALF) for m in range(1, halves)]
 
     row, top = lax.axis_index("row"), lax.axis_index("col") // share
@@ -226,7 +208,7 @@
     per = GROUPS // COLOURS
     colours = pl.pallas_call(
         order_kernel,
-        out_shape=[jax.ShapeDtypeStruct((1, per, tall, LANES), dtype)] * COLOURS,
+        out_shape=[jax.ShapeDtypeStruct((1, per) + piece, dtype)] * COLOURS,
         in_specs=[SMEM, VMEM] + [VMEM] * len(others),
         out_specs=[VMEM] * COLOURS,
         compiler_params=limit(4),
@@ -244,8 +226,6 @@
             mask, send = links[(k + step) % 3]
             colours[k] = jnp.concatenate([colours[k], send(colours[k])])
             masks[k] = masks[k] + [m ^ mask for m in masks[k]]
-        if step == 0:
-            colours, m_two = lax.optimization_barrier((list(colours), m_two))
     m_held = [m_held, over_col(m_held, 1), m_two, over_col(m_two, 1)]
 
     wanted, width = merge_factor.shape[0] * rows, sub_vectors.shape[1]

time: 74.8 us -> 72.5 us (0.969)
  blocking collectives: 10.7 us -> 0 us
  waiting for transfers between devices: 25.7 us -> 32.9 us
  starting transfers between devices: 26.5 us -> 27.5 us
    all_to_all x1 -> x0, blocking collectives: 10.7 us -> none  [local(): lax.all_to_all(merged.reshape(rows * cols, each, width), ('row', 'col'),...]
    all_to_all x0 -> x1, waiting for transfers between devices: none -> 3.85 us  [local(): lax.all_to_all(merged.reshape(rows * cols, each, width), ('row', 'col'),...]
    all_to_all x0 -> x1, starting transfers between devices: none -> 3.78 us  [local(): lax.all_to_all(merged.reshape(rows * cols, each, width), ('row', 'col'),...]
    all_to_all x1, waiting for transfers between devices: 2.03 us -> 5.48 us  [local(): slices = lax.all_to_all(packed, 'col', 0, 0, axis_index_groups=members)]
    ppermute x18, waiting for transfers between devices: 20.3 us -> 17.8 us  [over_col(): return lax.ppermute(x, 'col', [(c, c ^ mask) for c in range(cols)])]
    ppermute x4, waiting for transfers between devices: 3.31 us -> 5.75 us  [over_row(): return lax.ppermute(x, 'row', [(r, r ^ mask) for r in range(rows)])]
    ppermute x4, starting transfers between devices: 6.15 us -> 4.34 us  [over_row(): return lax.ppermute(x, 'row', [(r, r ^ mask) for r in range(rows)])]
    ppermute x18, starting transfers between devices: 14.9 us -> 13.9 us  [over_col(): return lax.ppermute(x, 'col', [(c, c ^ mask) for c in range(cols)])]
  transfers between devices with their start and end apart: 23 -> 24, of which waited for: 10 -> 9; matrix products, arithmetic and copies ran while one was open for 0% -> 0% of each run, Pallas kernels for 7% -> 9%
where the time goes in v8:
time: 72.5 us; the launch traced here: 72.2 us
  waiting for transfers between devices  32.9 us (45%)
  starting transfers between devices  27.5 us (38%)
  Pallas kernels  9.45 us (13%)
  local copies, waits for them, and re-layouts  2.04 us (3%)
    ppermute x18, waiting for transfers between devices, over_col(): return lax.ppermute(x, 'col', [(c, c ^ mask) for c in range(cols)])  17.8 us
    ppermute x18, starting transfers between devices, over_col(): return lax.ppermute(x, 'col', [(c, c ^ mask) for c in range(cols)])  13.9 us
    pallas_call x3, Pallas kernels, local(): pl.pallas_call(functools.partial(chain_kernel, cols, groups, masks[k], fi...  6.27 us
    ppermute x4, waiting for transfers between devices, over_row(): return lax.ppermute(x, 'row', [(r, r ^ mask) for r in range(rows)])  5.75 us
    all_to_all x1, waiting for transfers between devices, local(): slices = lax.all_to_all(packed, 'col', 0, 0, axis_index_groups=members)  5.48 us
    all_to_all x1, starting transfers between devices, local(): slices = lax.all_to_all(packed, 'col', 0, 0, axis_index_groups=members)  5.4 us
    ppermute x4, starting transfers between devices, over_row(): return lax.ppermute(x, 'row', [(r, r ^ mask) for r in range(rows)])  4.34 us
    all_to_all x1, waiting for transfers between devices, local(): lax.all_to_all(merged.reshape(rows * cols, each, width), ('row', 'col'),...  3.85 us
  transfers between devices with their start and end apart: 24, of which 9 were waited for; matrix products, arithmetic and copies ran while one was open for 0% of the time, Pallas kernels for 9%

profile of v8, /device:TPU:0, one launch (start us, length us, event | category | flops | bytes accessed | tf_op | source)
XLA Modules:
  0.0 72.2 jit_solution(1429087334696483152)
XLA Ops:
  0.0 1.0 %copy-done.1 = bf16[1,1024,256]{2,1,0:T(8,128)(2,1)S(1)} copy-done((bf16[1,1024,256]{2,1,0:T(8,128)(2,1)S(1)}, bf16[1,1024,256]{2,1,0:T(8,128)(2,1)}, u32[]{:S(2)}) %copy-start.1) | copy-done | bytes 524312
  1.0 0.9 %copy-done.2 = bf16[1,256,256]{2,1,0:T(8,128)(2,1)S(1)} copy-done((bf16[1,256,256]{2,1,0:T(8,128)(2,1)S(1)}, bf16[1,256,256]{2,1,0:T(8,128)(2,1)}, u32[]{:S(2)}) %copy-start.2) | copy-done | bytes 131096
  1.9 0.8 %pack.1 = bf16[8,80,256]{2,1,0:T(8,128)(2,1)} custom-call(bf16[16,64,256]{2,1,0:T(8,128)(2,1)S(1)} %bitcast.6, bf16[16,16,256]{2,1,0:T(8,128)(2,1)S(1)} %bitcast.7), custom_call_target="tpu_custom_call" | custom-call | tf_op jit(solution)/shard_map/pack/pallas_call | solution.py:168
  2.7 0.0 copy-start.5
  2.7 5.4 %all-to-all-start = ((bf16[8,80,256]{2,1,0:T(8,128)(2,1)}), bf16[8,80,256]{2,1,0:T(8,128)(2,1)S(1)}, u32[]{:S(2)}, u32[]{:S(2)}) async-start(bf16[8,80,256]{2,1,0:T(8,128)(2,1)} %pack.1), calls=%async_computation | async-start | bytes 655360 | tf_op jit(solution)/shard_map/all_to_all | solution.py:178
  8.2 2.7 %collective-permute-start = (bf16[64,512]{1,0:T(8,128)(2,1)S(1)}, bf16[64,512]{1,0:T(8,128)(2,1)S(1)}, u32[]{:S(2)}, u32[]{:S(2)}) collective-permute-start(bf16[64,512]{1,0:T(8,128)(2,1)S(1)} %copy-done.5), channel_id=1, source_target_pairs={{0,8},{1,9},{2,10},{3,11},{4,12},{5,13},{6,14},{7,15},{8,0},{9,1},... | collective-permute-start | bytes 196616 | tf_op jit(solution)/shard_map/ppermute | solution.py:155
  10.8 5.5 %all-to-all-done.held = bf16[8,80,256]{2,1,0:T(8,128)(2,1)S(1)} async-done(((bf16[8,80,256]{2,1,0:T(8,128)(2,1)}), bf16[8,80,256]{2,1,0:T(8,128)(2,1)S(1)}, u32[]{:S(2)}, u32[]{:S(2)}) %all-to-all-start) | async-done | bytes 327712 | tf_op jit(solution)/shard_map/all_to_all | solution.py:178
  16.3 0.7 pick.1
  17.0 1.6 %collective-permute-start.2 = (bf16[64,512]{1,0:T(8,128)(2,1)S(1)}, bf16[64,512]{1,0:T(8,128)(2,1)S(1)}, u32[]{:S(2)}, u32[]{:S(2)}) collective-permute-start(bf16[64,512]{1,0:T(8,128)(2,1)S(1)} %get-tuple-element.30), channel_id=1, source_target_pairs={{0,16},{16,0},{1,17},{17,1},{2,18},{18,2},{3,19},{19,3},{4,20},{20... | collective-permute-start | bytes 196616 | tf_op jit(solution)/shard_map/ppermute | solution.py:158
  18.6 2.8 %collective-permute-done.2 = bf16[64,512]{1,0:T(8,128)(2,1)S(1)} collective-permute-done((bf16[64,512]{1,0:T(8,128)(2,1)S(1)}, bf16[64,512]{1,0:T(8,128)(2,1)S(1)}, u32[]{:S(2)}, u32[]{:S(2)}) %collective-permute-start.2) | collective-permute-done | bytes 65568 | tf_op jit(solution)/shard_map/ppermute | solution.py:158
  21.4 2.0 %collective-permute-start.3 = (bf16[2,64,512]{2,1,0:T(8,128)(2,1)S(1)}, bf16[2,64,512]{2,1,0:T(8,128)(2,1)S(1)}, u32[]{:S(2)}, u32[]{:S(2)}) collective-permute-start(bf16[2,64,512]{2,1,0:T(8,128)(2,1)S(1)} %pad_maximum_fusion.4), channel_id=1, source_target_pairs={{0,4},{1,5},{2,6},{3,7},{4,0},{5,1},{6,2},{7,3},{8,12},{9,13},{10,... | collective-permute-start | bytes 393224 | tf_op jit(solution)/shard_map/ppermute | solution.py:155
  23.4 0.9 %collective-permute-start.1 = (bf16[5,80,256]{2,1,0:T(8,128)(2,1)S(1)}, bf16[5,80,256]{2,1,0:T(8,128)(2,1)S(1)}, u32[]{:S(2)}, u32[]{:S(2)}) collective-permute-start(bf16[5,80,256]{2,1,0:T(8,128)(2,1)S(1)} %pick.1), channel_id=1, source_target_pairs={{0,8},{1,9},{2,10},{3,11},{4,12},{5,13},{6,14},{7,15},{8,0},{9,1},... | collective-permute-start | bytes 614408 | tf_op jit(solution)/shard_map/ppermute | solution.py:155
  24.3 2.7 %collective-permute-done.3 = bf16[2,64,512]{2,1,0:T(8,128)(2,1)S(1)} collective-permute-done((bf16[2,64,512]{2,1,0:T(8,128)(2,1)S(1)}, bf16[2,64,512]{2,1,0:T(8,128)(2,1)S(1)}, u32[]{:S(2)}, u32[]{:S(2)}) %collective-permute-start.3) | collective-permute-done | bytes 131104 | tf_op jit(solution)/shard_map/ppermute | solution.py:155
  27.0 6.6 %collective-permute-done.1.refs_0_ = bf16[5,80,256]{2,1,0:T(8,128)(2,1)S(1)} collective-permute-done((bf16[5,80,256]{2,1,0:T(8,128)(2,1)S(1)}, bf16[5,80,256]{2,1,0:T(8,128)(2,1)S(1)}, u32[]{:S(2)}, u32[]{:S(2)}) %collective-permute-start.1) | collective-permute-done | bytes 204832 | tf_op jit(solution)/shard_map/ppermute | solution.py:155
  33.6 1.5 %collective-permute-start.14 = (bf16[4,64,512]{2,1,0:T(8,128)(2,1)S(1)}, bf16[4,64,512]{2,1,0:T(8,128)(2,1)S(1)}, u32[]{:S(2)}, u32[]{:S(2)}) collective-permute-start(bf16[4,64,512]{2,1,0:T(8,128)(2,1)S(1)} %pad_maximum_fusion.refs_0_), channel_id=1, source_target_pairs={{0,2},{1,3},{2,0},{3,1},{4,6},{5,7},{6,4},{7,5},{8,10},{9,11},{10,... | collective-permute-start | bytes 786440 | tf_op jit(solution)/shard_map/ppermute | solution.py:155
  35.1 0.6 order.1
  35.7 0.6 collective-permute-start.7
  36.4 1.6 %collective-permute-start.4 = (bf16[1,2,80,256]{3,2,1,0:T(8,128)(2,1)S(1)}, bf16[1,2,80,256]{3,2,1,0:T(8,128)(2,1)S(1)}, u32[]{:S(2)}, u32[]{:S(2)}) collective-permute-start(bf16[1,2,80,256]{3,2,1,0:T(8,128)(2,1)S(1)} %get-tuple-element.21), channel_id=1, source_target_pairs={{0,16},{16,0},{1,17},{17,1},{2,18},{18,2},{3,19},{19,3},{4,20},{20... | collective-permute-start | bytes 245768 | tf_op jit(solution)/shard_map/ppermute | solution.py:158
  37.9 4.4 %collective-permute-done.10 = bf16[1,2,80,256]{3,2,1,0:T(8,128)(2,1)S(1)} collective-permute-done((bf16[1,2,80,256]{3,2,1,0:T(8,128)(2,1)S(1)}, bf16[1,2,80,256]{3,2,1,0:T(8,128)(2,1)S(1)}, u32[]{:S(2)}, u32[]{:S(2)}) %collective-permute-start.10) | collective-permute-done | bytes 81952 | tf_op jit(solution)/shard_map/ppermute | solution.py:155
  42.4 0.0 copy-start
  42.4 0.6 collective-permute-start.11
  43.0 0.2 collective-permute-start.8
  43.2 0.0 collective-permute-done.4
  43.2 1.5 %collective-permute-start.5 = (bf16[2,2,80,256]{3,2,1,0:T(8,128)(2,1)S(1)}, bf16[2,2,80,256]{3,2,1,0:T(8,128)(2,1)S(1)}, u32[]{:S(2)}, u32[]{:S(2)}) collective-permute-start(bf16[2,2,80,256]{3,2,1,0:T(8,128)(2,1)S(1)} %pad_maximum_fusion.1), channel_id=1, source_target_pairs={{0,2},{1,3},{2,0},{3,1},{4,6},{5,7},{6,4},{7,5},{8,10},{9,11},{10,... | collective-permute-start | bytes 491528 | tf_op jit(solution)/shard_map/ppermute | solution.py:155
  44.8 3.0 %collective-permute-done.11 = bf16[2,2,80,256]{3,2,1,0:T(8,128)(2,1)S(1)} collective-permute-done((bf16[2,2,80,256]{3,2,1,0:T(8,128)(2,1)S(1)}, bf16[2,2,80,256]{3,2,1,0:T(8,128)(2,1)S(1)}, u32[]{:S(2)}, u32[]{:S(2)}) %collective-permute-start.11) | collective-permute-done | bytes 163872 | tf_op jit(solution)/shard_map/ppermute | solution.py:158
  47.8 1.5 %collective-permute-start.12 = (bf16[4,2,80,256]{3,2,1,0:T(8,128)(2,1)S(1)}, bf16[4,2,80,256]{3,2,1,0:T(8,128)(2,1)S(1)}, u32[]{:S(2)}, u32[]{:S(2)}) collective-permute-start(bf16[4,2,80,256]{3,2,1,0:T(8,128)(2,1)S(1)} %constant_dynamic-update-slice_fusion.6.refs_0_), channel_id=1, source_target_pairs={{0,2},{1,3},{2,0},{3,1},{4,6},{5,7},{6,4},{7,5},{8,10},{9,11},{10,... | collective-permute-start | bytes 983048 | tf_op jit(solution)/shard_map/ppermute | solution.py:155
  49.3 0.0 collective-permute-done.8
  49.3 0.6 collective-permute-start.9
  50.0 0.0 collective-permute-done.14.refs_2_
  50.0 0.0 collective-permute-start.15
  50.0 0.0 collective-permute-done.5
  50.0 1.9 %collective-permute-start.6 = (bf16[4,2,80,256]{3,2,1,0:T(8,128)(2,1)S(1)}, bf16[4,2,80,256]{3,2,1,0:T(8,128)(2,1)S(1)}, u32[]{:S(2)}, u32[]{:S(2)}) collective-permute-start(bf16[4,2,80,256]{3,2,1,0:T(8,128)(2,1)S(1)} %constant_dynamic-update-slice_fusion.refs_0_), channel_id=1, source_target_pairs={{0,4},{1,5},{2,6},{3,7},{4,0},{5,1},{6,2},{7,3},{8,12},{9,13},{10,... | collective-permute-start | bytes 983048 | tf_op jit(solution)/shard_map/ppermute | solution.py:155
  51.9 0.0 collective-permute-done.13.refs_1_
  51.9 0.0 collective-permute-start.16
  51.9 0.0 collective-permute-done.15.refs_3_
  51.9 1.1 %merge.1 = f32[128,128]{1,0:T(8,128)} custom-call(bf16[4096,128]{1,0:T(8,128)(2,1)S(1)} %copy-done, bf16[4,64,512]{2,1,0:T(8,128)(2,1)S(1)} %pad_maximum_fusion.refs_0_, bf16[4,64,512]{2,1,0:T(8,128)(2,1)S(1)} %collective-permute-done.13.refs_1_, bf16[4,64,512]{2,1,0:T(8,128)(2,1)S(1)} %collective-permute-done.14.refs_2_, ...), custom_call_target="tpu_custom_call" | custom-call | tf_op jit(solution)/shard_map/merge/pallas_call | solution.py:233
  53.0 3.8 %all-to-all-start.1 = ((f32[32,4,128]{2,1,0:T(4,128)}), f32[32,4,128]{2,1,0:T(4,128)S(1)}, u32[]{:S(2)}, u32[]{:S(2)}) async-start(f32[32,4,128]{2,1,0:T(4,128)} %bitcast.4), calls=%async_computation.1 | async-start | bytes 131072 | tf_op jit(solution)/shard_map/all_to_all | solution.py:241
  56.8 3.5 %collective-permute-done.6.refs_1_ = bf16[4,2,80,256]{3,2,1,0:T(8,128)(2,1)S(1)} collective-permute-done((bf16[4,2,80,256]{3,2,1,0:T(8,128)(2,1)S(1)}, bf16[4,2,80,256]{3,2,1,0:T(8,128)(2,1)S(1)}, u32[]{:S(2)}, u32[]{:S(2)}) %collective-permute-start.6) | collective-permute-done | bytes 327712 | tf_op jit(solution)/shard_map/ppermute | solution.py:155
  60.4 3.9 %all-to-all-done.1.start = f32[32,4,128]{2,1,0:T(4,128)S(1)} async-done(((f32[32,4,128]{2,1,0:T(4,128)}), f32[32,4,128]{2,1,0:T(4,128)S(1)}, u32[]{:S(2)}, u32[]{:S(2)}) %all-to-all-start.1) | async-done | bytes 65568 | tf_op jit(solution)/shard_map/all_to_all | solution.py:241
  64.2 0.1 collective-permute-start.17
  64.3 0.4 collective-permute-start.18
  64.7 0.1 collective-permute-start.20
  64.8 0.4 collective-permute-start.19
  65.2 0.1 collective-permute-start.21
  65.4 0.5 collective-permute-done.17.refs_3_
  65.8 1.9 %chain0.1.start = f32[8,2048]{1,0:T(8,128)S(1)} custom-call(s32[6]{0:T(128)S(1)} %copy-done.3, f32[32,4,128]{2,1,0:T(4,128)S(1)} %all-to-all-done.1.start, bf16[4,2,80,256]{3,2,1,0:T(8,128)(2,1)S(1)} %constant_dynamic-update-slice_fusion.refs_0_, bf16[4,2,80,256]{3,2,1,0:T(8,128)(2,1)S(1)} %collective-permute-done.6.refs_1_, ...), custom_call_target="tpu_custom_call" | custom-call | tf_op jit(solution)/shard_map/chain0/pallas_call | solution.py:258
  67.8 1.9 %chain1.1.start = f32[8,2048]{1,0:T(8,128)S(1)} custom-call(s32[6]{0:T(128)S(1)} %copy-done.3, f32[8,2048]{1,0:T(8,128)S(1)} %chain0.1.start, bf16[4,2,80,256]{3,2,1,0:T(8,128)(2,1)S(1)} %constant_dynamic-update-slice_fusion.3.refs_0_, bf16[4,2,80,256]{3,2,1,0:T(8,128)(2,1)S(1)} %collective-permute-done.9.refs_1_, ...), custom_call_target="tpu_custom_call" | custom-call | tf_op jit(solution)/shard_map/chain1/pallas_call | solution.py:258
  69.7 2.5 %chain2.1 = bf16[4,2048]{1,0:T(4,128)(2,1)} custom-call(s32[6]{0:T(128)S(1)} %copy-done.3, f32[8,2048]{1,0:T(8,128)S(1)} %chain1.1.start, bf16[4,2,80,256]{3,2,1,0:T(8,128)(2,1)S(1)} %constant_dynamic-update-slice_fusion.6.refs_0_, bf16[4,2,80,256]{3,2,1,0:T(8,128)(2,1)S(1)} %collective-permute-done.12.refs_1_, ...), custom_call_target="tpu_custom_call" | custom-call | tf_op jit(solution)/shard_map/chain2/pallas_call | solution.py:258
  (33 shorter events, 0.2 us)
Async XLA Ops:
  0.0 1.0 %copy-start.1 = (bf16[1,1024,256]{2,1,0:T(8,128)(2,1)S(1)}, bf16[1,1024,256]{2,1,0:T(8,128)(2,1)}, u32[]{:S(2)}) copy-start(bf16[1,1024,256]{2,1,0:T(8,128)(2,1)} %param.8) | copy-start | bytes 1572868
  1.0 0.9 %copy-start.2 = (bf16[1,256,256]{2,1,0:T(8,128)(2,1)S(1)}, bf16[1,256,256]{2,1,0:T(8,128)(2,1)}, u32[]{:S(2)}) copy-start(bf16[1,256,256]{2,1,0:T(8,128)(2,1)} %param.9) | copy-start | bytes 393220
  2.7 5.4 %copy-start.5 = (bf16[64,512]{1,0:T(8,128)(2,1)S(1)}, bf16[64,512]{1,0:T(8,128)(2,1)}, u32[]{:S(2)}) copy-start(bf16[64,512]{1,0:T(8,128)(2,1)} %param.7) | copy-start | bytes 196612
  2.7 13.5 %all-to-all-start = ((bf16[8,80,256]{2,1,0:T(8,128)(2,1)}), bf16[8,80,256]{2,1,0:T(8,128)(2,1)S(1)}, u32[]{:S(2)}, u32[]{:S(2)}) async-start(bf16[8,80,256]{2,1,0:T(8,128)(2,1)} %pack.1), calls=%async_computation | async-start | bytes 655360 | tf_op jit(solution)/shard_map/all_to_all | solution.py:178
  8.2 8.9 %collective-permute-start = (bf16[64,512]{1,0:T(8,128)(2,1)S(1)}, bf16[64,512]{1,0:T(8,128)(2,1)S(1)}, u32[]{:S(2)}, u32[]{:S(2)}) collective-permute-start(bf16[64,512]{1,0:T(8,128)(2,1)S(1)} %copy-done.5), channel_id=1, source_target_pairs={{0,8},{1,9},{2,10},{3,11},{4,12},{5,13},{6,14},{7,15},{8,0},{9,1},... | collective-permute-start | bytes 196616 | tf_op jit(solution)/shard_map/ppermute | solution.py:155
  10.8 5.5 %copy-start.4 = (s32[6]{0:T(128)S(1)}, s32[6]{0:T(128)}, u32[]{:S(2)}) copy-start(s32[6]{0:T(128)} %owners.3) | copy-start | bytes 76
  17.0 4.3 %collective-permute-start.2 = (bf16[64,512]{1,0:T(8,128)(2,1)S(1)}, bf16[64,512]{1,0:T(8,128)(2,1)S(1)}, u32[]{:S(2)}, u32[]{:S(2)}) collective-permute-start(bf16[64,512]{1,0:T(8,128)(2,1)S(1)} %get-tuple-element.30), channel_id=1, source_target_pairs={{0,16},{16,0},{1,17},{17,1},{2,18},{18,2},{3,19},{19,3},{4,20},{20... | collective-permute-start | bytes 196616 | tf_op jit(solution)/shard_map/ppermute | solution.py:158
  21.4 5.6 %collective-permute-start.3 = (bf16[2,64,512]{2,1,0:T(8,128)(2,1)S(1)}, bf16[2,64,512]{2,1,0:T(8,128)(2,1)S(1)}, u32[]{:S(2)}, u32[]{:S(2)}) collective-permute-start(bf16[2,64,512]{2,1,0:T(8,128)(2,1)S(1)} %pad_maximum_fusion.4), channel_id=1, source_target_pairs={{0,4},{1,5},{2,6},{3,7},{4,0},{5,1},{6,2},{7,3},{8,12},{9,13},{10,... | collective-permute-start | bytes 393224 | tf_op jit(solution)/shard_map/ppermute | solution.py:155
  23.4 10.3 %collective-permute-start.1 = (bf16[5,80,256]{2,1,0:T(8,128)(2,1)S(1)}, bf16[5,80,256]{2,1,0:T(8,128)(2,1)S(1)}, u32[]{:S(2)}, u32[]{:S(2)}) collective-permute-start(bf16[5,80,256]{2,1,0:T(8,128)(2,1)S(1)} %pick.1), channel_id=1, source_target_pairs={{0,8},{1,9},{2,10},{3,11},{4,12},{5,13},{6,14},{7,15},{8,0},{9,1},... | collective-permute-start | bytes 614408 | tf_op jit(solution)/shard_map/ppermute | solution.py:155
  33.6 16.3 %collective-permute-start.14 = (bf16[4,64,512]{2,1,0:T(8,128)(2,1)S(1)}, bf16[4,64,512]{2,1,0:T(8,128)(2,1)S(1)}, u32[]{:S(2)}, u32[]{:S(2)}) collective-permute-start(bf16[4,64,512]{2,1,0:T(8,128)(2,1)S(1)} %pad_maximum_fusion.refs_0_), channel_id=1, source_target_pairs={{0,2},{1,3},{2,0},{3,1},{4,6},{5,7},{6,4},{7,5},{8,10},{9,11},{10,... | collective-permute-start | bytes 786440 | tf_op jit(solution)/shard_map/ppermute | solution.py:155
  35.1 16.8 %collective-permute-start.13 = (bf16[4,64,512]{2,1,0:T(8,128)(2,1)S(1)}, bf16[4,64,512]{2,1,0:T(8,128)(2,1)S(1)}, u32[]{:S(2)}, u32[]{:S(2)}) collective-permute-start(bf16[4,64,512]{2,1,0:T(8,128)(2,1)S(1)} %pad_maximum_fusion.refs_0_), channel_id=1, source_target_pairs={{0,1},{1,0},{2,3},{3,2},{4,5},{5,4},{6,7},{7,6},{8,9},{9,8},{10,11... | collective-permute-start | bytes 786440 | tf_op jit(solution)/shard_map/ppermute | solution.py:155
  35.7 7.3 %collective-permute-start.7 = (bf16[1,2,80,256]{3,2,1,0:T(8,128)(2,1)S(1)}, bf16[1,2,80,256]{3,2,1,0:T(8,128)(2,1)S(1)}, u32[]{:S(2)}, u32[]{:S(2)}) collective-permute-start(bf16[1,2,80,256]{3,2,1,0:T(8,128)(2,1)S(1)} %get-tuple-element.22), channel_id=1, source_target_pairs={{0,2},{1,3},{2,0},{3,1},{4,6},{5,7},{6,4},{7,5},{8,10},{9,11},{10,... | collective-permute-start | bytes 245768 | tf_op jit(solution)/shard_map/ppermute | solution.py:155
  36.4 6.9 %collective-permute-start.4 = (bf16[1,2,80,256]{3,2,1,0:T(8,128)(2,1)S(1)}, bf16[1,2,80,256]{3,2,1,0:T(8,128)(2,1)S(1)}, u32[]{:S(2)}, u32[]{:S(2)}) collective-permute-start(bf16[1,2,80,256]{3,2,1,0:T(8,128)(2,1)S(1)} %get-tuple-element.21), channel_id=1, source_target_pairs={{0,16},{16,0},{1,17},{17,1},{2,18},{18,2},{3,19},{19,3},{4,20},{20... | collective-permute-start | bytes 245768 | tf_op jit(solution)/shard_map/ppermute | solution.py:158
  37.9 4.4 %collective-permute-start.10 = (bf16[1,2,80,256]{3,2,1,0:T(8,128)(2,1)S(1)}, bf16[1,2,80,256]{3,2,1,0:T(8,128)(2,1)S(1)}, u32[]{:S(2)}, u32[]{:S(2)}) collective-permute-start(bf16[1,2,80,256]{3,2,1,0:T(8,128)(2,1)S(1)} %get-tuple-element.23), channel_id=1, source_target_pairs={{0,4},{1,5},{2,6},{3,7},{4,0},{5,1},{6,2},{7,3},{8,12},{9,13},{10,... | collective-permute-start | bytes 245768 | tf_op jit(solution)/shard_map/ppermute | solution.py:155
  42.4 9.5 %copy-start = (bf16[4096,128]{1,0:T(8,128)(2,1)S(1)}, bf16[4096,128]{1,0:T(8,128)(2,1)}, u32[]{:S(2)}) copy-start(bf16[4096,128]{1,0:T(8,128)(2,1)} %sub.6) | copy-start | bytes 3145732
  42.4 5.4 %collective-permute-start.11 = (bf16[2,2,80,256]{3,2,1,0:T(8,128)(2,1)S(1)}, bf16[2,2,80,256]{3,2,1,0:T(8,128)(2,1)S(1)}, u32[]{:S(2)}, u32[]{:S(2)}) collective-permute-start(bf16[2,2,80,256]{3,2,1,0:T(8,128)(2,1)S(1)} %pad_maximum_fusion.3), channel_id=1, source_target_pairs={{0,16},{16,0},{1,17},{17,1},{2,18},{18,2},{3,19},{19,3},{4,20},{20... | collective-permute-start | bytes 491528 | tf_op jit(solution)/shard_map/ppermute | solution.py:158
  43.0 6.3 %collective-permute-start.8 = (bf16[2,2,80,256]{3,2,1,0:T(8,128)(2,1)S(1)}, bf16[2,2,80,256]{3,2,1,0:T(8,128)(2,1)S(1)}, u32[]{:S(2)}, u32[]{:S(2)}) collective-permute-start(bf16[2,2,80,256]{3,2,1,0:T(8,128)(2,1)S(1)} %pad_maximum_fusion.2), channel_id=1, source_target_pairs={{0,4},{1,5},{2,6},{3,7},{4,0},{5,1},{6,2},{7,3},{8,12},{9,13},{10,... | collective-permute-start | bytes 491528 | tf_op jit(solution)/shard_map/ppermute | solution.py:155
  43.2 6.7 %collective-permute-start.5 = (bf16[2,2,80,256]{3,2,1,0:T(8,128)(2,1)S(1)}, bf16[2,2,80,256]{3,2,1,0:T(8,128)(2,1)S(1)}, u32[]{:S(2)}, u32[]{:S(2)}) collective-permute-start(bf16[2,2,80,256]{3,2,1,0:T(8,128)(2,1)S(1)} %pad_maximum_fusion.1), channel_id=1, source_target_pairs={{0,2},{1,3},{2,0},{3,1},{4,6},{5,7},{6,4},{7,5},{8,10},{9,11},{10,... | collective-permute-start | bytes 491528 | tf_op jit(solution)/shard_map/ppermute | solution.py:155
  47.8 9.0 %collective-permute-start.12 = (bf16[4,2,80,256]{3,2,1,0:T(8,128)(2,1)S(1)}, bf16[4,2,80,256]{3,2,1,0:T(8,128)(2,1)S(1)}, u32[]{:S(2)}, u32[]{:S(2)}) collective-permute-start(bf16[4,2,80,256]{3,2,1,0:T(8,128)(2,1)S(1)} %constant_dynamic-update-slice_fusion.6.refs_0_), channel_id=1, source_target_pairs={{0,2},{1,3},{2,0},{3,1},{4,6},{5,7},{6,4},{7,5},{8,10},{9,11},{10,... | collective-permute-start | bytes 983048 | tf_op jit(solution)/shard_map/ppermute | solution.py:155
  49.3 7.5 %collective-permute-start.9 = (bf16[4,2,80,256]{3,2,1,0:T(8,128)(2,1)S(1)}, bf16[4,2,80,256]{3,2,1,0:T(8,128)(2,1)S(1)}, u32[]{:S(2)}, u32[]{:S(2)}) collective-permute-start(bf16[4,2,80,256]{3,2,1,0:T(8,128)(2,1)S(1)} %constant_dynamic-update-slice_fusion.3.refs_0_), channel_id=1, source_target_pairs={{0,16},{16,0},{1,17},{17,1},{2,18},{18,2},{3,19},{19,3},{4,20},{20... | collective-permute-start | bytes 983048 | tf_op jit(solution)/shard_map/ppermute | solution.py:158
  50.0 1.9 %collective-permute-start.15 = (bf16[4,64,512]{2,1,0:T(8,128)(2,1)S(1)}, bf16[4,64,512]{2,1,0:T(8,128)(2,1)S(1)}, u32[]{:S(2)}, u32[]{:S(2)}) collective-permute-start(bf16[4,64,512]{2,1,0:T(8,128)(2,1)S(1)} %collective-permute-done.14.refs_2_), channel_id=1, source_target_pairs={{0,1},{1,0},{2,3},{3,2},{4,5},{5,4},{6,7},{7,6},{8,9},{9,8},{10,11... | collective-permute-start | bytes 786440 | tf_op jit(solution)/shard_map/ppermute | solution.py:155
  50.0 10.4 %collective-permute-start.6 = (bf16[4,2,80,256]{3,2,1,0:T(8,128)(2,1)S(1)}, bf16[4,2,80,256]{3,2,1,0:T(8,128)(2,1)S(1)}, u32[]{:S(2)}, u32[]{:S(2)}) collective-permute-start(bf16[4,2,80,256]{3,2,1,0:T(8,128)(2,1)S(1)} %constant_dynamic-update-slice_fusion.refs_0_), channel_id=1, source_target_pairs={{0,4},{1,5},{2,6},{3,7},{4,0},{5,1},{6,2},{7,3},{8,12},{9,13},{10,... | collective-permute-start | bytes 983048 | tf_op jit(solution)/shard_map/ppermute | solution.py:155
  51.9 13.3 %collective-permute-start.16 = (bf16[4,2,80,256]{3,2,1,0:T(8,128)(2,1)S(1)}, bf16[4,2,80,256]{3,2,1,0:T(8,128)(2,1)S(1)}, u32[]{:S(2)}, u32[]{:S(2)}) collective-permute-start(bf16[4,2,80,256]{3,2,1,0:T(8,128)(2,1)S(1)} %constant_dynamic-update-slice_fusion.refs_0_), channel_id=1, source_target_pairs={{0,1},{1,0},{2,3},{3,2},{4,5},{5,4},{6,7},{7,6},{8,9},{9,8},{10,11... | collective-permute-start | bytes 983048 | tf_op jit(solution)/shard_map/ppermute | solution.py:155
  53.0 12.8 %copy-start.3 = (s32[6]{0:T(128)S(1)}, s32[6]{0:T(128)}, u32[]{:S(2)}) copy-start(s32[6]{0:T(128)} %offsets.5) | copy-start | bytes 76
  53.0 11.2 %all-to-all-start.1 = ((f32[32,4,128]{2,1,0:T(4,128)}), f32[32,4,128]{2,1,0:T(4,128)S(1)}, u32[]{:S(2)}, u32[]{:S(2)}) async-start(f32[32,4,128]{2,1,0:T(4,128)} %bitcast.4), calls=%async_computation.1 | async-start | bytes 131072 | tf_op jit(solution)/shard_map/all_to_all | solution.py:241
  64.2 1.6 %collective-permute-start.17 = (bf16[4,2,80,256]{3,2,1,0:T(8,128)(2,1)S(1)}, bf16[4,2,80,256]{3,2,1,0:T(8,128)(2,1)S(1)}, u32[]{:S(2)}, u32[]{:S(2)}) collective-permute-start(bf16[4,2,80,256]{3,2,1,0:T(8,128)(2,1)S(1)} %collective-permute-done.6.refs_1_), channel_id=1, source_target_pairs={{0,1},{1,0},{2,3},{3,2},{4,5},{5,4},{6,7},{7,6},{8,9},{9,8},{10,11... | collective-permute-start | bytes 983048 | tf_op jit(solution)/shard_map/ppermute | solution.py:155
  64.3 3.4 %collective-permute-start.18 = (bf16[4,2,80,256]{3,2,1,0:T(8,128)(2,1)S(1)}, bf16[4,2,80,256]{3,2,1,0:T(8,128)(2,1)S(1)}, u32[]{:S(2)}, u32[]{:S(2)}) collective-permute-start(bf16[4,2,80,256]{3,2,1,0:T(8,128)(2,1)S(1)} %constant_dynamic-update-slice_fusion.3.refs_0_), channel_id=1, source_target_pairs={{0,1},{1,0},{2,3},{3,2},{4,5},{5,4},{6,7},{7,6},{8,9},{9,8},{10,11... | collective-permute-start | bytes 983048 | tf_op jit(solution)/shard_map/ppermute | solution.py:155
  64.7 4.9 %collective-permute-start.20 = (bf16[4,2,80,256]{3,2,1,0:T(8,128)(2,1)S(1)}, bf16[4,2,80,256]{3,2,1,0:T(8,128)(2,1)S(1)}, u32[]{:S(2)}, u32[]{:S(2)}) collective-permute-start(bf16[4,2,80,256]{3,2,1,0:T(8,128)(2,1)S(1)} %constant_dynamic-update-slice_fusion.6.refs_0_), channel_id=1, source_target_pairs={{0,1},{1,0},{2,3},{3,2},{4,5},{5,4},{6,7},{7,6},{8,9},{9,8},{10,11... | collective-permute-start | bytes 983048 | tf_op jit(solution)/shard_map/ppermute | solution.py:155
  64.8 2.9 %collective-permute-start.19 = (bf16[4,2,80,256]{3,2,1,0:T(8,128)(2,1)S(1)}, bf16[4,2,80,256]{3,2,1,0:T(8,128)(2,1)S(1)}, u32[]{:S(2)}, u32[]{:S(2)}) collective-permute-start(bf16[4,2,80,256]{3,2,1,0:T(8,128)(2,1)S(1)} %collective-permute-done.9.refs_1_), channel_id=1, source_target_pairs={{0,1},{1,0},{2,3},{3,2},{4,5},{5,4},{6,7},{7,6},{8,9},{9,8},{10,11... | collective-permute-start | bytes 983048 | tf_op jit(solution)/shard_map/ppermute | solution.py:155
  65.2 4.4 %collective-permute-start.21 = (bf16[4,2,80,256]{3,2,1,0:T(8,128)(2,1)S(1)}, bf16[4,2,80,256]{3,2,1,0:T(8,128)(2,1)S(1)}, u32[]{:S(2)}, u32[]{:S(2)}) collective-permute-start(bf16[4,2,80,256]{3,2,1,0:T(8,128)(2,1)S(1)} %collective-permute-done.12.refs_1_), channel_id=1, source_target_pairs={{0,1},{1,0},{2,3},{3,2},{4,5},{5,4},{6,7},{7,6},{8,9},{9,8},{10,11... | collective-permute-start | bytes 983048 | tf_op jit(solution)/shard_map/ppermute | solution.py:155

commit v9 on v8

--- a/solution.py
+++ b/solution.py
@@ -174,6 +174,7 @@
         compiler_params=limit(2),
         name="pack",
     )(basis.reshape(SLICES, pv, reflect), factor.reshape(SLICES, pt, reflect))
+    packed, across = lax.optimization_barrier((packed, across))
     members = [[h * HALF + c for c in range(HALF)] for h in range(halves)]
     slices = lax.all_to_all(packed, "col", 0, 0, axis_index_groups=members)
 
@@ -185,8 +186,6 @@
         compiler_params=limit(4),
         name="pick",
     )(owners, slices)
-    picked, across = lax.optimization_barrier((picked, across))
-    others = [over_col(picked, m * HALF) for m in range(1, halves)]
 
     row, top = lax.axis_index("row"), lax.axis_index("col") // share
 
@@ -202,7 +201,8 @@
     while bit >= 4:
         m_held = jnp.concatenate([m_held, over_col(m_held, bit)])
         bit //= 2
-    others, m_held = lax.optimization_barrier((others, m_held))
+    picked, m_held = lax.optimization_barrier((picked, m_held))
+    others = [over_col(picked, m * HALF) for m in range(1, halves)]
     m_two = over_col(m_held, 2)
 
     per = GROUPS // COLOURS

time: 72.5 us -> 69.5 us (0.959)
  waiting for transfers between devices: 32.9 us -> 18.4 us
  blocking collectives: 0 us -> 13.1 us
  starting transfers between devices: 27.5 us -> 26.5 us
    all_to_all x0 -> x1, blocking collectives: none -> 13.1 us  [local(): lax.all_to_all(merged.reshape(rows * cols, each, width), ('row', 'col'),...]
    all_to_all x1, waiting for transfers between devices: 5.48 us -> 0.01 us  [local(): slices = lax.all_to_all(packed, 'col', 0, 0, axis_index_groups=members)]
    ppermute x18, waiting for transfers between devices: 17.8 us -> 13.6 us  [over_col(): return lax.ppermute(x, 'col', [(c, c ^ mask) for c in range(cols)])]
    all_to_all x1 -> x0, waiting for transfers between devices: 3.85 us -> none  [local(): lax.all_to_all(merged.reshape(rows * cols, each, width), ('row', 'col'),...]
    all_to_all x1 -> x0, starting transfers between devices: 3.78 us -> none  [local(): lax.all_to_all(merged.reshape(rows * cols, each, width), ('row', 'col'),...]
    ppermute x18, starting transfers between devices: 13.9 us -> 17.2 us  [over_col(): return lax.ppermute(x, 'col', [(c, c ^ mask) for c in range(cols)])]
    all_to_all x1, starting transfers between devices: 5.4 us -> 3.43 us  [local(): slices = lax.all_to_all(packed, 'col', 0, 0, axis_index_groups=members)]
    ppermute x4, starting transfers between devices: 4.34 us -> 5.86 us  [over_row(): return lax.ppermute(x, 'row', [(r, r ^ mask) for r in range(rows)])]
  transfers between devices with their start and end apart: 24 -> 23, of which waited for: 9 -> 9; matrix products, arithmetic and copies ran while one was open for 0% -> 0% of each run, Pallas kernels for 9% -> 8%
where the time goes in v9:
time: 69.5 us; the launch traced here: 69.2 us
  starting transfers between devices  26.5 us (38%)
  waiting for transfers between devices  18.4 us (26%)
  blocking collectives  13.1 us (19%)
  Pallas kernels  8.8 us (13%)
  local copies, waits for them, and re-layouts  2.04 us (3%)
    ppermute x18, starting transfers between devices, over_col(): return lax.ppermute(x, 'col', [(c, c ^ mask) for c in range(cols)])  17.2 us
    ppermute x18, waiting for transfers between devices, over_col(): return lax.ppermute(x, 'col', [(c, c ^ mask) for c in range(cols)])  13.6 us
    all_to_all x1, blocking collectives, local(): lax.all_to_all(merged.reshape(rows * cols, each, width), ('row', 'col'),...  13.1 us
    pallas_call x3, Pallas kernels, local(): pl.pallas_call(functools.partial(chain_kernel, cols, groups, masks[k], fi...  6.28 us
    ppermute x4, starting transfers between devices, over_row(): return lax.ppermute(x, 'row', [(r, r ^ mask) for r in range(rows)])  5.86 us
    ppermute x4, waiting for transfers between devices, over_row(): return lax.ppermute(x, 'row', [(r, r ^ mask) for r in range(rows)])  4.73 us
    all_to_all x1, starting transfers between devices, local(): slices = lax.all_to_all(packed, 'col', 0, 0, axis_index_groups=members)  3.43 us
    unnamed x17, local copies, waits for them, and re-layouts  2.01 us
  transfers between devices with their start and end apart: 23, of which 9 were waited for; matrix products, arithmetic and copies ran while one was open for 0% of the time, Pallas kernels for 8%

profile of v9, /device:TPU:0, one launch (start us, length us, event | category | flops | bytes accessed | tf_op | source)
XLA Modules:
  0.0 69.2 jit_solution(12149287728905615267)
XLA Ops:
  0.0 4.0 %collective-permute-start = (bf16[64,512]{1,0:T(8,128)(2,1)}, bf16[64,512]{1,0:T(8,128)(2,1)S(1)}, u32[]{:S(2)}, u32[]{:S(2)}) collective-permute-start(bf16[64,512]{1,0:T(8,128)(2,1)} %param.7), channel_id=1, source_target_pairs={{0,8},{1,9},{2,10},{3,11},{4,12},{5,13},{6,14},{7,15},{8,0},{9,1},... | collective-permute-start | bytes 196616 | tf_op jit(solution)/shard_map/ppermute | solution.py:155
  4.0 1.0 %copy-done.1 = bf16[1,1024,256]{2,1,0:T(8,128)(2,1)S(1)} copy-done((bf16[1,1024,256]{2,1,0:T(8,128)(2,1)S(1)}, bf16[1,1024,256]{2,1,0:T(8,128)(2,1)}, u32[]{:S(2)}) %copy-start.1) | copy-done | bytes 524312
  5.1 0.9 %copy-done.2 = bf16[1,256,256]{2,1,0:T(8,128)(2,1)S(1)} copy-done((bf16[1,256,256]{2,1,0:T(8,128)(2,1)S(1)}, bf16[1,256,256]{2,1,0:T(8,128)(2,1)}, u32[]{:S(2)}) %copy-start.2) | copy-done | bytes 131096
  6.0 0.8 %pack.1 = bf16[8,80,256]{2,1,0:T(8,128)(2,1)} custom-call(bf16[16,64,256]{2,1,0:T(8,128)(2,1)S(1)} %bitcast.6, bf16[16,16,256]{2,1,0:T(8,128)(2,1)S(1)} %bitcast.8), custom_call_target="tpu_custom_call" | custom-call | tf_op jit(solution)/shard_map/pack/pallas_call | solution.py:168
  6.8 0.0 copy-start.5
  6.8 1.1 %collective-permute-done = bf16[64,512]{1,0:T(8,128)(2,1)S(1)} collective-permute-done((bf16[64,512]{1,0:T(8,128)(2,1)}, bf16[64,512]{1,0:T(8,128)(2,1)S(1)}, u32[]{:S(2)}, u32[]{:S(2)}) %collective-permute-start) | collective-permute-done | bytes 65568 | tf_op jit(solution)/shard_map/ppermute | solution.py:155
  7.9 3.4 %all-to-all-start = ((bf16[8,80,256]{2,1,0:T(8,128)(2,1)}), bf16[8,80,256]{2,1,0:T(8,128)(2,1)S(1)}, u32[]{:S(2)}, u32[]{:S(2)}) async-start(bf16[8,80,256]{2,1,0:T(8,128)(2,1)} %pack.1), calls=%async_computation | async-start | bytes 655360 | tf_op jit(solution)/shard_map/all_to_all | solution.py:179
  11.4 1.8 %collective-permute-start.1 = (bf16[64,512]{1,0:T(8,128)(2,1)S(1)}, bf16[64,512]{1,0:T(8,128)(2,1)S(1)}, u32[]{:S(2)}, u32[]{:S(2)}) collective-permute-start(bf16[64,512]{1,0:T(8,128)(2,1)S(1)} %get-tuple-element.30), channel_id=1, source_target_pairs={{0,16},{16,0},{1,17},{17,1},{2,18},{18,2},{3,19},{19,3},{4,20},{20... | collective-permute-start | bytes 196616 | tf_op jit(solution)/shard_map/ppermute | solution.py:158
  13.2 2.7 %collective-permute-done.1 = bf16[64,512]{1,0:T(8,128)(2,1)S(1)} collective-permute-done((bf16[64,512]{1,0:T(8,128)(2,1)S(1)}, bf16[64,512]{1,0:T(8,128)(2,1)S(1)}, u32[]{:S(2)}, u32[]{:S(2)}) %collective-permute-start.1) | collective-permute-done | bytes 65568 | tf_op jit(solution)/shard_map/ppermute | solution.py:158
  15.8 0.0 copy-start.4
  15.9 1.9 %collective-permute-start.2 = (bf16[2,64,512]{2,1,0:T(8,128)(2,1)S(1)}, bf16[2,64,512]{2,1,0:T(8,128)(2,1)S(1)}, u32[]{:S(2)}, u32[]{:S(2)}) collective-permute-start(bf16[2,64,512]{2,1,0:T(8,128)(2,1)S(1)} %pad_maximum_fusion.4), channel_id=1, source_target_pairs={{0,4},{1,5},{2,6},{3,7},{4,0},{5,1},{6,2},{7,3},{8,12},{9,13},{10,... | collective-permute-start | bytes 393224 | tf_op jit(solution)/shard_map/ppermute | solution.py:155
  17.7 3.2 %collective-permute-done.2 = bf16[2,64,512]{2,1,0:T(8,128)(2,1)S(1)} collective-permute-done((bf16[2,64,512]{2,1,0:T(8,128)(2,1)S(1)}, bf16[2,64,512]{2,1,0:T(8,128)(2,1)S(1)}, u32[]{:S(2)}, u32[]{:S(2)}) %collective-permute-start.2) | collective-permute-done | bytes 131104 | tf_op jit(solution)/shard_map/ppermute | solution.py:155
  20.9 0.0 all-to-all-done.held
  20.9 0.7 %pick.1 = bf16[5,80,256]{2,1,0:T(8,128)(2,1)S(1)} custom-call(s32[6]{0:T(128)S(1)} %copy-done.4, bf16[8,80,256]{2,1,0:T(8,128)(2,1)S(1)} %all-to-all-done.held), custom_call_target="tpu_custom_call" | custom-call | tf_op jit(solution)/shard_map/pick/pallas_call | solution.py:181
  21.7 3.1 %collective-permute-start.3 = (bf16[5,80,256]{2,1,0:T(8,128)(2,1)S(1)}, bf16[5,80,256]{2,1,0:T(8,128)(2,1)S(1)}, u32[]{:S(2)}, u32[]{:S(2)}) collective-permute-start(bf16[5,80,256]{2,1,0:T(8,128)(2,1)S(1)} %pick.1), channel_id=1, source_target_pairs={{0,8},{1,9},{2,10},{3,11},{4,12},{5,13},{6,14},{7,15},{8,0},{9,1},... | collective-permute-start | bytes 614408 | tf_op jit(solution)/shard_map/ppermute | solution.py:155
  24.7 1.6 %collective-permute-start.14 = (bf16[4,64,512]{2,1,0:T(8,128)(2,1)S(1)}, bf16[4,64,512]{2,1,0:T(8,128)(2,1)S(1)}, u32[]{:S(2)}, u32[]{:S(2)}) collective-permute-start(bf16[4,64,512]{2,1,0:T(8,128)(2,1)S(1)} %pad_maximum_fusion.refs_0_), channel_id=1, source_target_pairs={{0,2},{1,3},{2,0},{3,1},{4,6},{5,7},{6,4},{7,5},{8,10},{9,11},{10,... | collective-permute-start | bytes 786440 | tf_op jit(solution)/shard_map/ppermute | solution.py:155
  26.4 0.0 collective-permute-start.13
  26.4 6.8 %collective-permute-done.3.refs_0_ = bf16[5,80,256]{2,1,0:T(8,128)(2,1)S(1)} collective-permute-done((bf16[5,80,256]{2,1,0:T(8,128)(2,1)S(1)}, bf16[5,80,256]{2,1,0:T(8,128)(2,1)S(1)}, u32[]{:S(2)}, u32[]{:S(2)}) %collective-permute-start.3) | collective-permute-done | bytes 204832 | tf_op jit(solution)/shard_map/ppermute | solution.py:155
  33.2 0.6 order.1
  33.8 0.3 collective-permute-start.10
  34.1 1.5 %collective-permute-start.7 = (bf16[1,2,80,256]{3,2,1,0:T(8,128)(2,1)S(1)}, bf16[1,2,80,256]{3,2,1,0:T(8,128)(2,1)S(1)}, u32[]{:S(2)}, u32[]{:S(2)}) collective-permute-start(bf16[1,2,80,256]{3,2,1,0:T(8,128)(2,1)S(1)} %get-tuple-element.22), channel_id=1, source_target_pairs={{0,2},{1,3},{2,0},{3,1},{4,6},{5,7},{6,4},{7,5},{8,10},{9,11},{10,... | collective-permute-start | bytes 245768 | tf_op jit(solution)/shard_map/ppermute | solution.py:155
  35.5 1.5 %collective-permute-start.4 = (bf16[1,2,80,256]{3,2,1,0:T(8,128)(2,1)S(1)}, bf16[1,2,80,256]{3,2,1,0:T(8,128)(2,1)S(1)}, u32[]{:S(2)}, u32[]{:S(2)}) collective-permute-start(bf16[1,2,80,256]{3,2,1,0:T(8,128)(2,1)S(1)} %get-tuple-element.21), channel_id=1, source_target_pairs={{0,16},{16,0},{1,17},{17,1},{2,18},{18,2},{3,19},{19,3},{4,20},{20... | collective-permute-start | bytes 245768 | tf_op jit(solution)/shard_map/ppermute | solution.py:158
  37.1 0.0 collective-permute-done.14.refs_2_
  37.1 0.1 collective-permute-start.15
  37.2 1.1 %collective-permute-done.10 = bf16[1,2,80,256]{3,2,1,0:T(8,128)(2,1)S(1)} collective-permute-done((bf16[1,2,80,256]{3,2,1,0:T(8,128)(2,1)S(1)}, bf16[1,2,80,256]{3,2,1,0:T(8,128)(2,1)S(1)}, u32[]{:S(2)}, u32[]{:S(2)}) %collective-permute-start.10) | collective-permute-done | bytes 81952 | tf_op jit(solution)/shard_map/ppermute | solution.py:155
  38.3 0.0 copy-start
  38.3 1.6 %collective-permute-start.11 = (bf16[2,2,80,256]{3,2,1,0:T(8,128)(2,1)S(1)}, bf16[2,2,80,256]{3,2,1,0:T(8,128)(2,1)S(1)}, u32[]{:S(2)}, u32[]{:S(2)}) collective-permute-start(bf16[2,2,80,256]{3,2,1,0:T(8,128)(2,1)S(1)} %pad_maximum_fusion.3), channel_id=1, source_target_pairs={{0,16},{16,0},{1,17},{17,1},{2,18},{18,2},{3,19},{19,3},{4,20},{20... | collective-permute-start | bytes 491528 | tf_op jit(solution)/shard_map/ppermute | solution.py:158
  39.9 0.5 collective-permute-start.8
  40.4 1.3 %collective-permute-start.5 = (bf16[2,2,80,256]{3,2,1,0:T(8,128)(2,1)S(1)}, bf16[2,2,80,256]{3,2,1,0:T(8,128)(2,1)S(1)}, u32[]{:S(2)}, u32[]{:S(2)}) collective-permute-start(bf16[2,2,80,256]{3,2,1,0:T(8,128)(2,1)S(1)} %pad_maximum_fusion.1), channel_id=1, source_target_pairs={{0,2},{1,3},{2,0},{3,1},{4,6},{5,7},{6,4},{7,5},{8,10},{9,11},{10,... | collective-permute-start | bytes 491528 | tf_op jit(solution)/shard_map/ppermute | solution.py:155
  41.8 2.1 %collective-permute-done.11 = bf16[2,2,80,256]{3,2,1,0:T(8,128)(2,1)S(1)} collective-permute-done((bf16[2,2,80,256]{3,2,1,0:T(8,128)(2,1)S(1)}, bf16[2,2,80,256]{3,2,1,0:T(8,128)(2,1)S(1)}, u32[]{:S(2)}, u32[]{:S(2)}) %collective-permute-start.11) | collective-permute-done | bytes 163872 | tf_op jit(solution)/shard_map/ppermute | solution.py:158
  43.9 0.9 %collective-permute-start.12 = (bf16[4,2,80,256]{3,2,1,0:T(8,128)(2,1)S(1)}, bf16[4,2,80,256]{3,2,1,0:T(8,128)(2,1)S(1)}, u32[]{:S(2)}, u32[]{:S(2)}) collective-permute-start(bf16[4,2,80,256]{3,2,1,0:T(8,128)(2,1)S(1)} %constant_dynamic-update-slice_fusion.6.refs_0_), channel_id=1, source_target_pairs={{0,2},{1,3},{2,0},{3,1},{4,6},{5,7},{6,4},{7,5},{8,10},{9,11},{10,... | collective-permute-start | bytes 983048 | tf_op jit(solution)/shard_map/ppermute | solution.py:155
  44.8 0.5 collective-permute-done.8
  45.3 1.0 %collective-permute-start.9 = (bf16[4,2,80,256]{3,2,1,0:T(8,128)(2,1)S(1)}, bf16[4,2,80,256]{3,2,1,0:T(8,128)(2,1)S(1)}, u32[]{:S(2)}, u32[]{:S(2)}) collective-permute-start(bf16[4,2,80,256]{3,2,1,0:T(8,128)(2,1)S(1)} %constant_dynamic-update-slice_fusion.3.refs_0_), channel_id=1, source_target_pairs={{0,16},{16,0},{1,17},{17,1},{2,18},{18,2},{3,19},{19,3},{4,20},{20... | collective-permute-start | bytes 983048 | tf_op jit(solution)/shard_map/ppermute | solution.py:158
  46.3 0.4 collective-permute-done.5
  46.7 0.9 %collective-permute-start.6 = (bf16[4,2,80,256]{3,2,1,0:T(8,128)(2,1)S(1)}, bf16[4,2,80,256]{3,2,1,0:T(8,128)(2,1)S(1)}, u32[]{:S(2)}, u32[]{:S(2)}) collective-permute-start(bf16[4,2,80,256]{3,2,1,0:T(8,128)(2,1)S(1)} %constant_dynamic-update-slice_fusion.refs_0_), channel_id=1, source_target_pairs={{0,4},{1,5},{2,6},{3,7},{4,0},{5,1},{6,2},{7,3},{8,12},{9,13},{10,... | collective-permute-start | bytes 983048 | tf_op jit(solution)/shard_map/ppermute | solution.py:155
  47.6 0.0 collective-permute-done.13.refs_1_
  47.6 0.4 merge.1
  48.1 0.0 copy-start.3
  48.1 13.1 %all_to_all.10.start = f32[32,4,128]{2,1,0:T(4,128)S(1)} all-to-all(f32[32,4,128]{2,1,0:T(4,128)S(1)} %bitcast.7), channel_id=1, replica_groups=mesh['row'=2,'col'=16] {'row','col'}, dimensions={0} | all-to-all | bytes 131072 | tf_op jit(solution)/shard_map/all_to_all | solution.py:241
  61.2 0.2 collective-permute-start.17
  61.4 0.4 collective-permute-start.18
  61.8 0.1 collective-permute-start.20
  61.9 0.4 collective-permute-start.19
  62.3 0.1 collective-permute-start.21
  62.4 0.5 collective-permute-done.17.refs_3_
  62.9 1.9 %chain0.1.start = f32[8,2048]{1,0:T(8,128)S(1)} custom-call(s32[6]{0:T(128)S(1)} %copy-done.3, f32[32,4,128]{2,1,0:T(4,128)S(1)} %all_to_all.10.start, bf16[4,2,80,256]{3,2,1,0:T(8,128)(2,1)S(1)} %constant_dynamic-update-slice_fusion.refs_0_, bf16[4,2,80,256]{3,2,1,0:T(8,128)(2,1)S(1)} %collective-permute-done.6.refs_1_, ...), custom_call_target="tpu_custom_call" | custom-call | tf_op jit(solution)/shard_map/chain0/pallas_call | solution.py:258
  64.8 1.9 %chain1.1.start = f32[8,2048]{1,0:T(8,128)S(1)} custom-call(s32[6]{0:T(128)S(1)} %copy-done.3, f32[8,2048]{1,0:T(8,128)S(1)} %chain0.1.start, bf16[4,2,80,256]{3,2,1,0:T(8,128)(2,1)S(1)} %constant_dynamic-update-slice_fusion.3.refs_0_, bf16[4,2,80,256]{3,2,1,0:T(8,128)(2,1)S(1)} %collective-permute-done.9.refs_1_, ...), custom_call_target="tpu_custom_call" | custom-call | tf_op jit(solution)/shard_map/chain1/pallas_call | solution.py:258
  66.7 2.5 %chain2.1 = bf16[4,2048]{1,0:T(4,128)(2,1)} custom-call(s32[6]{0:T(128)S(1)} %copy-done.3, f32[8,2048]{1,0:T(8,128)S(1)} %chain1.1.start, bf16[4,2,80,256]{3,2,1,0:T(8,128)(2,1)S(1)} %constant_dynamic-update-slice_fusion.6.refs_0_, bf16[4,2,80,256]{3,2,1,0:T(8,128)(2,1)S(1)} %collective-permute-done.12.refs_1_, ...), custom_call_target="tpu_custom_call" | custom-call | tf_op jit(solution)/shard_map/chain2/pallas_call | solution.py:258
  (32 shorter events, 0.2 us)
Async XLA Ops:
  0.0 7.9 %collective-permute-start = (bf16[64,512]{1,0:T(8,128)(2,1)}, bf16[64,512]{1,0:T(8,128)(2,1)S(1)}, u32[]{:S(2)}, u32[]{:S(2)}) collective-permute-start(bf16[64,512]{1,0:T(8,128)(2,1)} %param.7), channel_id=1, source_target_pairs={{0,8},{1,9},{2,10},{3,11},{4,12},{5,13},{6,14},{7,15},{8,0},{9,1},... | collective-permute-start | bytes 196616 | tf_op jit(solution)/shard_map/ppermute | solution.py:155
  4.0 1.0 %copy-start.1 = (bf16[1,1024,256]{2,1,0:T(8,128)(2,1)S(1)}, bf16[1,1024,256]{2,1,0:T(8,128)(2,1)}, u32[]{:S(2)}) copy-start(bf16[1,1024,256]{2,1,0:T(8,128)(2,1)} %param.8) | copy-start | bytes 1572868
  5.1 0.9 %copy-start.2 = (bf16[1,256,256]{2,1,0:T(8,128)(2,1)S(1)}, bf16[1,256,256]{2,1,0:T(8,128)(2,1)}, u32[]{:S(2)}) copy-start(bf16[1,256,256]{2,1,0:T(8,128)(2,1)} %param.9) | copy-start | bytes 393220
  6.8 4.6 %copy-start.5 = (bf16[64,512]{1,0:T(8,128)(2,1)S(1)}, bf16[64,512]{1,0:T(8,128)(2,1)}, u32[]{:S(2)}) copy-start(bf16[64,512]{1,0:T(8,128)(2,1)} %param.7) | copy-start | bytes 196612
  7.9 13.0 %all-to-all-start = ((bf16[8,80,256]{2,1,0:T(8,128)(2,1)}), bf16[8,80,256]{2,1,0:T(8,128)(2,1)S(1)}, u32[]{:S(2)}, u32[]{:S(2)}) async-start(bf16[8,80,256]{2,1,0:T(8,128)(2,1)} %pack.1), calls=%async_computation | async-start | bytes 655360 | tf_op jit(solution)/shard_map/all_to_all | solution.py:179
  11.4 4.4 %collective-permute-start.1 = (bf16[64,512]{1,0:T(8,128)(2,1)S(1)}, bf16[64,512]{1,0:T(8,128)(2,1)S(1)}, u32[]{:S(2)}, u32[]{:S(2)}) collective-permute-start(bf16[64,512]{1,0:T(8,128)(2,1)S(1)} %get-tuple-element.30), channel_id=1, source_target_pairs={{0,16},{16,0},{1,17},{17,1},{2,18},{18,2},{3,19},{19,3},{4,20},{20... | collective-permute-start | bytes 196616 | tf_op jit(solution)/shard_map/ppermute | solution.py:158
  15.8 5.1 %copy-start.4 = (s32[6]{0:T(128)S(1)}, s32[6]{0:T(128)}, u32[]{:S(2)}) copy-start(s32[6]{0:T(128)} %owners.3) | copy-start | bytes 76
  15.9 5.0 %collective-permute-start.2 = (bf16[2,64,512]{2,1,0:T(8,128)(2,1)S(1)}, bf16[2,64,512]{2,1,0:T(8,128)(2,1)S(1)}, u32[]{:S(2)}, u32[]{:S(2)}) collective-permute-start(bf16[2,64,512]{2,1,0:T(8,128)(2,1)S(1)} %pad_maximum_fusion.4), channel_id=1, source_target_pairs={{0,4},{1,5},{2,6},{3,7},{4,0},{5,1},{6,2},{7,3},{8,12},{9,13},{10,... | collective-permute-start | bytes 393224 | tf_op jit(solution)/shard_map/ppermute | solution.py:155
  21.7 11.5 %collective-permute-start.3 = (bf16[5,80,256]{2,1,0:T(8,128)(2,1)S(1)}, bf16[5,80,256]{2,1,0:T(8,128)(2,1)S(1)}, u32[]{:S(2)}, u32[]{:S(2)}) collective-permute-start(bf16[5,80,256]{2,1,0:T(8,128)(2,1)S(1)} %pick.1), channel_id=1, source_target_pairs={{0,8},{1,9},{2,10},{3,11},{4,12},{5,13},{6,14},{7,15},{8,0},{9,1},... | collective-permute-start | bytes 614408 | tf_op jit(solution)/shard_map/ppermute | solution.py:155
  24.7 12.3 %collective-permute-start.14 = (bf16[4,64,512]{2,1,0:T(8,128)(2,1)S(1)}, bf16[4,64,512]{2,1,0:T(8,128)(2,1)S(1)}, u32[]{:S(2)}, u32[]{:S(2)}) collective-permute-start(bf16[4,64,512]{2,1,0:T(8,128)(2,1)S(1)} %pad_maximum_fusion.refs_0_), channel_id=1, source_target_pairs={{0,2},{1,3},{2,0},{3,1},{4,6},{5,7},{6,4},{7,5},{8,10},{9,11},{10,... | collective-permute-start | bytes 786440 | tf_op jit(solution)/shard_map/ppermute | solution.py:155
  26.4 21.2 %collective-permute-start.13 = (bf16[4,64,512]{2,1,0:T(8,128)(2,1)S(1)}, bf16[4,64,512]{2,1,0:T(8,128)(2,1)S(1)}, u32[]{:S(2)}, u32[]{:S(2)}) collective-permute-start(bf16[4,64,512]{2,1,0:T(8,128)(2,1)S(1)} %pad_maximum_fusion.refs_0_), channel_id=1, source_target_pairs={{0,1},{1,0},{2,3},{3,2},{4,5},{5,4},{6,7},{7,6},{8,9},{9,8},{10,11... | collective-permute-start | bytes 786440 | tf_op jit(solution)/shard_map/ppermute | solution.py:155
  33.8 4.5 %collective-permute-start.10 = (bf16[1,2,80,256]{3,2,1,0:T(8,128)(2,1)S(1)}, bf16[1,2,80,256]{3,2,1,0:T(8,128)(2,1)S(1)}, u32[]{:S(2)}, u32[]{:S(2)}) collective-permute-start(bf16[1,2,80,256]{3,2,1,0:T(8,128)(2,1)S(1)} %get-tuple-element.23), channel_id=1, source_target_pairs={{0,4},{1,5},{2,6},{3,7},{4,0},{5,1},{6,2},{7,3},{8,12},{9,13},{10,... | collective-permute-start | bytes 245768 | tf_op jit(solution)/shard_map/ppermute | solution.py:155
  34.1 5.8 %collective-permute-start.7 = (bf16[1,2,80,256]{3,2,1,0:T(8,128)(2,1)S(1)}, bf16[1,2,80,256]{3,2,1,0:T(8,128)(2,1)S(1)}, u32[]{:S(2)}, u32[]{:S(2)}) collective-permute-start(bf16[1,2,80,256]{3,2,1,0:T(8,128)(2,1)S(1)} %get-tuple-element.22), channel_id=1, source_target_pairs={{0,2},{1,3},{2,0},{3,1},{4,6},{5,7},{6,4},{7,5},{8,10},{9,11},{10,... | collective-permute-start | bytes 245768 | tf_op jit(solution)/shard_map/ppermute | solution.py:155
  35.5 4.9 %collective-permute-start.4 = (bf16[1,2,80,256]{3,2,1,0:T(8,128)(2,1)S(1)}, bf16[1,2,80,256]{3,2,1,0:T(8,128)(2,1)S(1)}, u32[]{:S(2)}, u32[]{:S(2)}) collective-permute-start(bf16[1,2,80,256]{3,2,1,0:T(8,128)(2,1)S(1)} %get-tuple-element.21), channel_id=1, source_target_pairs={{0,16},{16,0},{1,17},{17,1},{2,18},{18,2},{3,19},{19,3},{4,20},{20... | collective-permute-start | bytes 245768 | tf_op jit(solution)/shard_map/ppermute | solution.py:158
  37.1 10.5 %collective-permute-start.15 = (bf16[4,64,512]{2,1,0:T(8,128)(2,1)S(1)}, bf16[4,64,512]{2,1,0:T(8,128)(2,1)S(1)}, u32[]{:S(2)}, u32[]{:S(2)}) collective-permute-start(bf16[4,64,512]{2,1,0:T(8,128)(2,1)S(1)} %collective-permute-done.14.refs_2_), channel_id=1, source_target_pairs={{0,1},{1,0},{2,3},{3,2},{4,5},{5,4},{6,7},{7,6},{8,9},{9,8},{10,11... | collective-permute-start | bytes 786440 | tf_op jit(solution)/shard_map/ppermute | solution.py:155
  38.3 9.3 %copy-start = (bf16[4096,128]{1,0:T(8,128)(2,1)S(1)}, bf16[4096,128]{1,0:T(8,128)(2,1)}, u32[]{:S(2)}) copy-start(bf16[4096,128]{1,0:T(8,128)(2,1)} %sub.6) | copy-start | bytes 3145732
  38.3 5.5 %collective-permute-start.11 = (bf16[2,2,80,256]{3,2,1,0:T(8,128)(2,1)S(1)}, bf16[2,2,80,256]{3,2,1,0:T(8,128)(2,1)S(1)}, u32[]{:S(2)}, u32[]{:S(2)}) collective-permute-start(bf16[2,2,80,256]{3,2,1,0:T(8,128)(2,1)S(1)} %pad_maximum_fusion.3), channel_id=1, source_target_pairs={{0,16},{16,0},{1,17},{17,1},{2,18},{18,2},{3,19},{19,3},{4,20},{20... | collective-permute-start | bytes 491528 | tf_op jit(solution)/shard_map/ppermute | solution.py:158
  39.9 5.4 %collective-permute-start.8 = (bf16[2,2,80,256]{3,2,1,0:T(8,128)(2,1)S(1)}, bf16[2,2,80,256]{3,2,1,0:T(8,128)(2,1)S(1)}, u32[]{:S(2)}, u32[]{:S(2)}) collective-permute-start(bf16[2,2,80,256]{3,2,1,0:T(8,128)(2,1)S(1)} %pad_maximum_fusion.2), channel_id=1, source_target_pairs={{0,4},{1,5},{2,6},{3,7},{4,0},{5,1},{6,2},{7,3},{8,12},{9,13},{10,... | collective-permute-start | bytes 491528 | tf_op jit(solution)/shard_map/ppermute | solution.py:155
  40.4 6.3 %collective-permute-start.5 = (bf16[2,2,80,256]{3,2,1,0:T(8,128)(2,1)S(1)}, bf16[2,2,80,256]{3,2,1,0:T(8,128)(2,1)S(1)}, u32[]{:S(2)}, u32[]{:S(2)}) collective-permute-start(bf16[2,2,80,256]{3,2,1,0:T(8,128)(2,1)S(1)} %pad_maximum_fusion.1), channel_id=1, source_target_pairs={{0,2},{1,3},{2,0},{3,1},{4,6},{5,7},{6,4},{7,5},{8,10},{9,11},{10,... | collective-permute-start | bytes 491528 | tf_op jit(solution)/shard_map/ppermute | solution.py:155
  43.9 17.3 %collective-permute-start.12 = (bf16[4,2,80,256]{3,2,1,0:T(8,128)(2,1)S(1)}, bf16[4,2,80,256]{3,2,1,0:T(8,128)(2,1)S(1)}, u32[]{:S(2)}, u32[]{:S(2)}) collective-permute-start(bf16[4,2,80,256]{3,2,1,0:T(8,128)(2,1)S(1)} %constant_dynamic-update-slice_fusion.6.refs_0_), channel_id=1, source_target_pairs={{0,2},{1,3},{2,0},{3,1},{4,6},{5,7},{6,4},{7,5},{8,10},{9,11},{10,... | collective-permute-start | bytes 983048 | tf_op jit(solution)/shard_map/ppermute | solution.py:155
  45.3 15.9 %collective-permute-start.9 = (bf16[4,2,80,256]{3,2,1,0:T(8,128)(2,1)S(1)}, bf16[4,2,80,256]{3,2,1,0:T(8,128)(2,1)S(1)}, u32[]{:S(2)}, u32[]{:S(2)}) collective-permute-start(bf16[4,2,80,256]{3,2,1,0:T(8,128)(2,1)S(1)} %constant_dynamic-update-slice_fusion.3.refs_0_), channel_id=1, source_target_pairs={{0,16},{16,0},{1,17},{17,1},{2,18},{18,2},{3,19},{19,3},{4,20},{20... | collective-permute-start | bytes 983048 | tf_op jit(solution)/shard_map/ppermute | solution.py:158
  46.7 14.5 %collective-permute-start.6 = (bf16[4,2,80,256]{3,2,1,0:T(8,128)(2,1)S(1)}, bf16[4,2,80,256]{3,2,1,0:T(8,128)(2,1)S(1)}, u32[]{:S(2)}, u32[]{:S(2)}) collective-permute-start(bf16[4,2,80,256]{3,2,1,0:T(8,128)(2,1)S(1)} %constant_dynamic-update-slice_fusion.refs_0_), channel_id=1, source_target_pairs={{0,4},{1,5},{2,6},{3,7},{4,0},{5,1},{6,2},{7,3},{8,12},{9,13},{10,... | collective-permute-start | bytes 983048 | tf_op jit(solution)/shard_map/ppermute | solution.py:155
  47.6 14.7 %collective-permute-start.16 = (bf16[4,2,80,256]{3,2,1,0:T(8,128)(2,1)S(1)}, bf16[4,2,80,256]{3,2,1,0:T(8,128)(2,1)S(1)}, u32[]{:S(2)}, u32[]{:S(2)}) collective-permute-start(bf16[4,2,80,256]{3,2,1,0:T(8,128)(2,1)S(1)} %constant_dynamic-update-slice_fusion.refs_0_), channel_id=1, source_target_pairs={{0,1},{1,0},{2,3},{3,2},{4,5},{5,4},{6,7},{7,6},{8,9},{9,8},{10,11... | collective-permute-start | bytes 983048 | tf_op jit(solution)/shard_map/ppermute | solution.py:155
  48.1 14.8 %copy-start.3 = (s32[6]{0:T(128)S(1)}, s32[6]{0:T(128)}, u32[]{:S(2)}) copy-start(s32[6]{0:T(128)} %offsets.5) | copy-start | bytes 76
  61.2 1.7 %collective-permute-start.17 = (bf16[4,2,80,256]{3,2,1,0:T(8,128)(2,1)S(1)}, bf16[4,2,80,256]{3,2,1,0:T(8,128)(2,1)S(1)}, u32[]{:S(2)}, u32[]{:S(2)}) collective-permute-start(bf16[4,2,80,256]{3,2,1,0:T(8,128)(2,1)S(1)} %collective-permute-done.6.refs_1_), channel_id=1, source_target_pairs={{0,1},{1,0},{2,3},{3,2},{4,5},{5,4},{6,7},{7,6},{8,9},{9,8},{10,11... | collective-permute-start | bytes 983048 | tf_op jit(solution)/shard_map/ppermute | solution.py:155
  61.4 3.4 %collective-permute-start.18 = (bf16[4,2,80,256]{3,2,1,0:T(8,128)(2,1)S(1)}, bf16[4,2,80,256]{3,2,1,0:T(8,128)(2,1)S(1)}, u32[]{:S(2)}, u32[]{:S(2)}) collective-permute-start(bf16[4,2,80,256]{3,2,1,0:T(8,128)(2,1)S(1)} %constant_dynamic-update-slice_fusion.3.refs_0_), channel_id=1, source_target_pairs={{0,1},{1,0},{2,3},{3,2},{4,5},{5,4},{6,7},{7,6},{8,9},{9,8},{10,11... | collective-permute-start | bytes 983048 | tf_op jit(solution)/shard_map/ppermute | solution.py:155
  61.8 4.9 %collective-permute-start.20 = (bf16[4,2,80,256]{3,2,1,0:T(8,128)(2,1)S(1)}, bf16[4,2,80,256]{3,2,1,0:T(8,128)(2,1)S(1)}, u32[]{:S(2)}, u32[]{:S(2)}) collective-permute-start(bf16[4,2,80,256]{3,2,1,0:T(8,128)(2,1)S(1)} %constant_dynamic-update-slice_fusion.6.refs_0_), channel_id=1, source_target_pairs={{0,1},{1,0},{2,3},{3,2},{4,5},{5,4},{6,7},{7,6},{8,9},{9,8},{10,11... | collective-permute-start | bytes 983048 | tf_op jit(solution)/shard_map/ppermute | solution.py:155
  61.9 2.9 %collective-permute-start.19 = (bf16[4,2,80,256]{3,2,1,0:T(8,128)(2,1)S(1)}, bf16[4,2,80,256]{3,2,1,0:T(8,128)(2,1)S(1)}, u32[]{:S(2)}, u32[]{:S(2)}) collective-permute-start(bf16[4,2,80,256]{3,2,1,0:T(8,128)(2,1)S(1)} %collective-permute-done.9.refs_1_), channel_id=1, source_target_pairs={{0,1},{1,0},{2,3},{3,2},{4,5},{5,4},{6,7},{7,6},{8,9},{9,8},{10,11... | collective-permute-start | bytes 983048 | tf_op jit(solution)/shard_map/ppermute | solution.py:155
  62.3 4.4 %collective-permute-start.21 = (bf16[4,2,80,256]{3,2,1,0:T(8,128)(2,1)S(1)}, bf16[4,2,80,256]{3,2,1,0:T(8,128)(2,1)S(1)}, u32[]{:S(2)}, u32[]{:S(2)}) collective-permute-start(bf16[4,2,80,256]{3,2,1,0:T(8,128)(2,1)S(1)} %collective-permute-done.12.refs_1_), channel_id=1, source_target_pairs={{0,1},{1,0},{2,3},{3,2},{4,5},{5,4},{6,7},{7,6},{8,9},{9,8},{10,11... | collective-permute-start | bytes 983048 | tf_op jit(solution)/shard_map/ppermute | solution.py:155

commit v10 on v9

--- a/solution.py
+++ b/solution.py
@@ -74,16 +74,14 @@
         outs[group // each][0, group % each] = piece
 
 
-def merge_kernel(rows, cols, sub, *refs):
+def merge_kernel(rows, cols, tags, sub, *refs):
     held, total = refs[:-1], refs[-1]
     row, col = lax.axis_index("row"), lax.axis_index("col")
-    share = cols // rows
     deep, tall = held[0].shape[2], held[0].shape[1]
     total[...] = jnp.zeros_like(total)
-    for near, ref in enumerate(held):
-        for index in range(ref.shape[0]):
-            far, row_mask = index // rows, index % rows
-            j = jnp.bitwise_xor(lax.rem(col, share), far * len(held) + near)
+    for own_tags, ref in zip(tags, held):
+        for index, (row_mask, col_mask) in enumerate(own_tags):
+            j = jnp.bitwise_xor(lax.rem(col, cols // rows), col_mask)
             part = jnp.dot(ref[index], sub[aligned(j, deep), :], preferred_element_type=jnp.float32)
             at = aligned(jnp.bitwise_xor(row, row_mask), tall)
             total[at, :] = total[at, :] + part
@@ -196,14 +194,42 @@
             block = jnp.where(index == k, across[k], block)
         return block
 
-    m_held = jnp.stack([for_row(0)] + [over_row(for_row(m), m) for m in range(1, rows)])
+    blocks = [for_row(0)] + [over_row(for_row(m), m) for m in range(1, rows)]
+    groups = [range(rows // 2), range(rows // 2, rows)]
+    sides = [jnp.stack([blocks[m] for m in group]) for group in groups]
+    tags = [[(m, 0) for m in group] for group in groups]
+
+    def double(side, bit):
+        sides[side] = jnp.concatenate([sides[side], over_col(sides[side], bit)])
+        tags[side] = tags[side] + [(m, c ^ bit) for m, c in tags[side]]
+
     bit = share // 2
-    while bit >= 4:
-        m_held = jnp.concatenate([m_held, over_col(m_held, bit)])
+    while bit > 4:
+        double(0, bit)
+        double(1, bit)
         bit //= 2
-    picked, m_held = lax.optimization_barrier((picked, m_held))
+    double(0, 2)
+    double(1, 4)
+    picked, sides = lax.optimization_barrier((picked, sides))
     others = [over_col(picked, m * HALF) for m in range(1, halves)]
-    m_two = over_col(m_held, 2)
+    late = jnp.concatenate([over_col(sides[0], 4), over_col(sides[1], 2)])
+    late_tags = [(m, c ^ 4) for m, c in tags[0]] + [(m, c ^ 2) for m, c in tags[1]]
+    m_held = [jnp.concatenate(sides), late]
+    tags = [tags[0] + tags[1], late_tags]
+    m_held += [over_col(x, 1) for x in m_held]
+    tags += [[(m, c ^ 1) for m, c in ts] for ts in tags]
+    wanted, width = merge_factor.shape[0] * rows, sub_vectors.shape[1]
+    each = wanted // (rows * cols)
+    merged = pl.pallas_call(
+        functools.partial(merge_kernel, rows, cols, tags),
+        out_shape=jax.ShapeDtypeStruct((wanted, width), jnp.float32),
+        in_specs=[VMEM] + [VMEM] * len(m_held),
+        out_specs=VMEM,
+        compiler_params=limit(8),
+        name="merge",
+    )(sub_vectors, *m_held)
+    others, merged = lax.optimization_barrier((others, merged))
+    state = lax.all_to_all(merged.reshape(rows * cols, each, width), ("row", "col"), 0, 0)
 
     per = GROUPS // COLOURS
     colours = pl.pallas_call(
@@ -226,27 +252,14 @@
             mask, send = links[(k + step) % 3]
             colours[k] = jnp.concatenate([colours[k], send(colours[k])])
             masks[k] = masks[k] + [m ^ mask for m in masks[k]]
-    m_held = [m_held, over_col(m_held, 1), m_two, over_col(m_two, 1)]
-
-    wanted, width = merge_factor.shape[0] * rows, sub_vectors.shape[1]
-    each = wanted // (rows * cols)
-    merged = pl.pallas_call(
-        functools.partial(merge_kernel, rows, cols),
-        out_shape=jax.ShapeDtypeStruct((wanted, width), jnp.float32),
-        in_specs=[VMEM] + [VMEM] * len(m_held),
-        out_specs=VMEM,
-        compiler_params=limit(8),
-        name="merge",
-    )(sub_vectors, *m_held)
-    state = lax.all_to_all(merged.reshape(rows * cols, each, width), ("row", "col"), 0, 0)
-
+        if step == 0:
+            colours, state = lax.optimization_barrier((colours, state))
     last_round = []
     for k in range(COLOURS):
         mask, send = links[(k + 2) % 3]
         last_round.append(send(colours[k]))
         masks[k] = [masks[k], [m ^ mask for m in masks[k]]]
         masks[k] += [[m ^ 1 for m in ms] for ms in masks[k]]
-    last_round, state = lax.optimization_barrier((last_round, state))
     held = []
     for k in range(COLOURS):
         held.append([colours[k], last_round[k], over_col(colours[k], 1), over_col(last_round[k], 1)])

time: 69.5 us -> 79.8 us (1.15)
  waiting for transfers between devices: 18.4 us -> 35.5 us
  blocking collectives: 13.1 us -> 0 us
  starting transfers between devices: 26.5 us -> 32 us
    ppermute x18 -> x20, waiting for transfers between devices: 13.6 us -> 27.1 us  [over_col(): return lax.ppermute(x, 'col', [(c, c ^ mask) for c in range(cols)])]
    all_to_all x1 -> x0, blocking collectives: 13.1 us -> none  [local(): lax.all_to_all(merged.reshape(rows * cols, each, width), ('row', 'col'),...]
    all_to_all x0 -> x1, waiting for transfers between devices: none -> 6.49 us  [local(): lax.all_to_all(merged.reshape(rows * cols, each, width), ('row', 'col'),...]
    all_to_all x0 -> x1, starting transfers between devices: none -> 3.53 us  [local(): lax.all_to_all(merged.reshape(rows * cols, each, width), ('row', 'col'),...]
    ppermute x18 -> x20, starting transfers between devices: 17.2 us -> 20.2 us  [over_col(): return lax.ppermute(x, 'col', [(c, c ^ mask) for c in range(cols)])]
    ppermute x4, waiting for transfers between devices: 4.73 us -> 1.94 us  [over_row(): return lax.ppermute(x, 'row', [(r, r ^ mask) for r in range(rows)])]
    ppermute x4, starting transfers between devices: 5.86 us -> 4.71 us  [over_row(): return lax.ppermute(x, 'row', [(r, r ^ mask) for r in range(rows)])]
  transfers between devices with their start and end apart: 23 -> 26, of which waited for: 9 -> 12; matrix products, arithmetic and copies ran while one was open for 0% -> 0% of each run, Pallas kernels for 8% -> 7%
where the time goes in v10:
time: 79.8 us; the launch traced here: 79.5 us
  waiting for transfers between devices  35.5 us (44%)
  starting transfers between devices  32 us (40%)
  Pallas kernels  9.48 us (12%)
  local copies, waits for them, and re-layouts  2.07 us (3%)
    ppermute x20, waiting for transfers between devices, over_col(): return lax.ppermute(x, 'col', [(c, c ^ mask) for c in range(cols)])  27.1 us
    ppermute x20, starting transfers between devices, over_col(): return lax.ppermute(x, 'col', [(c, c ^ mask) for c in range(cols)])  20.2 us
    all_to_all x1, waiting for transfers between devices, local(): lax.all_to_all(merged.reshape(rows * cols, each, width), ('row', 'col'),...  6.49 us
    pallas_call x3, Pallas kernels, local(): pl.pallas_call(functools.partial(chain_kernel, cols, groups, masks[k], fi...  6.28 us
    ppermute x4, starting transfers between devices, over_row(): return lax.ppermute(x, 'row', [(r, r ^ mask) for r in range(rows)])  4.71 us
    all_to_all x1, starting transfers between devices, local(): slices = lax.all_to_all(packed, 'col', 0, 0, axis_index_groups=members)  3.56 us
    all_to_all x1, starting transfers between devices, local(): lax.all_to_all(merged.reshape(rows * cols, each, width), ('row', 'col'),...  3.53 us
    unnamed x17, local copies, waits for them, and re-layouts  2.02 us
  transfers between devices with their start and end apart: 26, of which 12 were waited for; matrix products, arithmetic and copies ran while one was open for 0% of the time, Pallas kernels for 7%

profile of v10, /device:TPU:0, one launch (start us, length us, event | category | flops | bytes accessed | tf_op | source)
XLA Modules:
  0.0 79.5 jit_solution(16336856902260336815)
XLA Ops:
  0.0 4.0 %collective-permute-start = (bf16[64,512]{1,0:T(8,128)(2,1)}, bf16[64,512]{1,0:T(8,128)(2,1)S(1)}, u32[]{:S(2)}, u32[]{:S(2)}) collective-permute-start(bf16[64,512]{1,0:T(8,128)(2,1)} %param.7), channel_id=1, source_target_pairs={{0,8},{1,9},{2,10},{3,11},{4,12},{5,13},{6,14},{7,15},{8,0},{9,1},... | collective-permute-start | bytes 196616 | tf_op jit(solution)/shard_map/ppermute | solution.py:153
  4.0 1.0 %copy-done.1 = bf16[1,1024,256]{2,1,0:T(8,128)(2,1)S(1)} copy-done((bf16[1,1024,256]{2,1,0:T(8,128)(2,1)S(1)}, bf16[1,1024,256]{2,1,0:T(8,128)(2,1)}, u32[]{:S(2)}) %copy-start.1) | copy-done | bytes 524312
  5.1 0.9 %copy-done.2 = bf16[1,256,256]{2,1,0:T(8,128)(2,1)S(1)} copy-done((bf16[1,256,256]{2,1,0:T(8,128)(2,1)S(1)}, bf16[1,256,256]{2,1,0:T(8,128)(2,1)}, u32[]{:S(2)}) %copy-start.2) | copy-done | bytes 131096
  6.0 0.8 pack.1
  6.8 1.1 %collective-permute-done = bf16[64,512]{1,0:T(8,128)(2,1)S(1)} collective-permute-done((bf16[64,512]{1,0:T(8,128)(2,1)}, bf16[64,512]{1,0:T(8,128)(2,1)S(1)}, u32[]{:S(2)}, u32[]{:S(2)}) %collective-permute-start) | collective-permute-done | bytes 65568 | tf_op jit(solution)/shard_map/ppermute | solution.py:153
  7.9 3.6 %all-to-all-start = ((bf16[8,80,256]{2,1,0:T(8,128)(2,1)}), bf16[8,80,256]{2,1,0:T(8,128)(2,1)S(1)}, u32[]{:S(2)}, u32[]{:S(2)}) async-start(bf16[8,80,256]{2,1,0:T(8,128)(2,1)} %pack.1), calls=%async_computation | async-start | bytes 655360 | tf_op jit(solution)/shard_map/all_to_all | solution.py:177
  11.5 0.0 copy-start.4
  11.5 1.8 %collective-permute-start.2 = (bf16[64,512]{1,0:T(8,128)(2,1)S(1)}, bf16[64,512]{1,0:T(8,128)(2,1)S(1)}, u32[]{:S(2)}, u32[]{:S(2)}) collective-permute-start(bf16[64,512]{1,0:T(8,128)(2,1)S(1)} %get-tuple-element.35), channel_id=1, source_target_pairs={{0,16},{16,0},{1,17},{17,1},{2,18},{18,2},{3,19},{19,3},{4,20},{20... | collective-permute-start | bytes 196616 | tf_op jit(solution)/shard_map/ppermute | solution.py:156
  13.3 1.9 %collective-permute-start.1 = (bf16[1,64,512]{2,1,0:T(8,128)(2,1)S(1)}, bf16[1,64,512]{2,1,0:T(8,128)(2,1)S(1)}, u32[]{:S(2)}, u32[]{:S(2)}) collective-permute-start(bf16[1,64,512]{2,1,0:T(8,128)(2,1)S(1)} %get-tuple-element.36), channel_id=1, source_target_pairs={{0,2},{1,3},{2,0},{3,1},{4,6},{5,7},{6,4},{7,5},{8,10},{9,11},{10,... | collective-permute-start | bytes 196616 | tf_op jit(solution)/shard_map/ppermute | solution.py:153
  15.2 0.8 collective-permute-done.2
  16.0 1.8 %collective-permute-start.3 = (bf16[1,64,512]{2,1,0:T(8,128)(2,1)S(1)}, bf16[1,64,512]{2,1,0:T(8,128)(2,1)S(1)}, u32[]{:S(2)}, u32[]{:S(2)}) collective-permute-start(bf16[1,64,512]{2,1,0:T(8,128)(2,1)S(1)} %bitcast.8), channel_id=1, source_target_pairs={{0,4},{1,5},{2,6},{3,7},{4,0},{5,1},{6,2},{7,3},{8,12},{9,13},{10,... | collective-permute-start | bytes 196616 | tf_op jit(solution)/shard_map/ppermute | solution.py:153
  17.8 1.7 %collective-permute-done.1 = bf16[1,64,512]{2,1,0:T(8,128)(2,1)S(1)} collective-permute-done((bf16[1,64,512]{2,1,0:T(8,128)(2,1)S(1)}, bf16[1,64,512]{2,1,0:T(8,128)(2,1)S(1)}, u32[]{:S(2)}, u32[]{:S(2)}) %collective-permute-start.1) | collective-permute-done | bytes 65568 | tf_op jit(solution)/shard_map/ppermute | solution.py:153
  19.5 0.7 collective-permute-done.3
  20.2 0.0 all-to-all-done.held
  20.3 0.7 pick.1
  21.0 1.9 %collective-permute-start.5 = (bf16[2,64,512]{2,1,0:T(8,128)(2,1)S(1)}, bf16[2,64,512]{2,1,0:T(8,128)(2,1)S(1)}, u32[]{:S(2)}, u32[]{:S(2)}) collective-permute-start(bf16[2,64,512]{2,1,0:T(8,128)(2,1)S(1)} %pad_maximum_fusion.3), channel_id=1, source_target_pairs={{0,4},{1,5},{2,6},{3,7},{4,0},{5,1},{6,2},{7,3},{8,12},{9,13},{10,... | collective-permute-start | bytes 393224 | tf_op jit(solution)/shard_map/ppermute | solution.py:153
  22.9 1.5 %collective-permute-start.6 = (bf16[2,64,512]{2,1,0:T(8,128)(2,1)S(1)}, bf16[2,64,512]{2,1,0:T(8,128)(2,1)S(1)}, u32[]{:S(2)}, u32[]{:S(2)}) collective-permute-start(bf16[2,64,512]{2,1,0:T(8,128)(2,1)S(1)} %pad_maximum_fusion.4), channel_id=1, source_target_pairs={{0,2},{1,3},{2,0},{3,1},{4,6},{5,7},{6,4},{7,5},{8,10},{9,11},{10,... | collective-permute-start | bytes 393224 | tf_op jit(solution)/shard_map/ppermute | solution.py:153
  24.4 0.1 collective-permute-start.7
  24.5 1.5 %collective-permute-done.5 = bf16[2,64,512]{2,1,0:T(8,128)(2,1)S(1)} collective-permute-done((bf16[2,64,512]{2,1,0:T(8,128)(2,1)S(1)}, bf16[2,64,512]{2,1,0:T(8,128)(2,1)S(1)}, u32[]{:S(2)}, u32[]{:S(2)}) %collective-permute-start.5) | collective-permute-done | bytes 131104 | tf_op jit(solution)/shard_map/ppermute | solution.py:153
  26.0 1.9 %collective-permute-done.6 = bf16[2,64,512]{2,1,0:T(8,128)(2,1)S(1)} collective-permute-done((bf16[2,64,512]{2,1,0:T(8,128)(2,1)S(1)}, bf16[2,64,512]{2,1,0:T(8,128)(2,1)S(1)}, u32[]{:S(2)}, u32[]{:S(2)}) %collective-permute-start.6) | collective-permute-done | bytes 131104 | tf_op jit(solution)/shard_map/ppermute | solution.py:153
  27.9 0.1 collective-permute-start.8
  28.0 2.9 %collective-permute-start.4 = (bf16[5,80,256]{2,1,0:T(8,128)(2,1)S(1)}, bf16[5,80,256]{2,1,0:T(8,128)(2,1)S(1)}, u32[]{:S(2)}, u32[]{:S(2)}) collective-permute-start(bf16[5,80,256]{2,1,0:T(8,128)(2,1)S(1)} %pick.1), channel_id=1, source_target_pairs={{0,8},{1,9},{2,10},{3,11},{4,12},{5,13},{6,14},{7,15},{8,0},{9,1},... | collective-permute-start | bytes 614408 | tf_op jit(solution)/shard_map/ppermute | solution.py:153
  30.9 0.0 collective-permute-done.7.refs_2_
  30.9 0.0 collective-permute-done.8.refs_3_
  30.9 1.1 %merge.1 = f32[128,128]{1,0:T(8,128)} custom-call(bf16[4096,128]{1,0:T(8,128)(2,1)S(1)} %copy-done, bf16[4,64,512]{2,1,0:T(8,128)(2,1)S(1)} %constant_dynamic-update-slice_fusion.refs_0_, bf16[4,64,512]{2,1,0:T(8,128)(2,1)S(1)} %constant_dynamic-update-slice_fusion.2.refs_1_, bf16[4,64,512]{2,1,0:T(8,128)(2,1)S(1)} %collective-permute-done.7.refs_2_, ...), custom_call_target="tpu_custom_call" | custom-call | tf_op jit(solution)/shard_map/merge/pallas_call | solution.py:223
  32.0 8.6 %collective-permute-done.4.refs_0_ = bf16[5,80,256]{2,1,0:T(8,128)(2,1)S(1)} collective-permute-done((bf16[5,80,256]{2,1,0:T(8,128)(2,1)S(1)}, bf16[5,80,256]{2,1,0:T(8,128)(2,1)S(1)}, u32[]{:S(2)}, u32[]{:S(2)}) %collective-permute-start.4) | collective-permute-done | bytes 204832 | tf_op jit(solution)/shard_map/ppermute | solution.py:153
  40.6 0.6 order.1
  41.2 1.6 %collective-permute-start.9 = (bf16[1,2,80,256]{3,2,1,0:T(8,128)(2,1)S(1)}, bf16[1,2,80,256]{3,2,1,0:T(8,128)(2,1)S(1)}, u32[]{:S(2)}, u32[]{:S(2)}) collective-permute-start(bf16[1,2,80,256]{3,2,1,0:T(8,128)(2,1)S(1)} %get-tuple-element.27), channel_id=1, source_target_pairs={{0,16},{16,0},{1,17},{17,1},{2,18},{18,2},{3,19},{19,3},{4,20},{20... | collective-permute-start | bytes 245768 | tf_op jit(solution)/shard_map/ppermute | solution.py:156
  42.8 1.8 %collective-permute-start.10 = (bf16[1,2,80,256]{3,2,1,0:T(8,128)(2,1)S(1)}, bf16[1,2,80,256]{3,2,1,0:T(8,128)(2,1)S(1)}, u32[]{:S(2)}, u32[]{:S(2)}) collective-permute-start(bf16[1,2,80,256]{3,2,1,0:T(8,128)(2,1)S(1)} %get-tuple-element.28), channel_id=1, source_target_pairs={{0,2},{1,3},{2,0},{3,1},{4,6},{5,7},{6,4},{7,5},{8,10},{9,11},{10,... | collective-permute-start | bytes 245768 | tf_op jit(solution)/shard_map/ppermute | solution.py:153
  44.6 3.5 %all-to-all-start.1 = ((f32[32,4,128]{2,1,0:T(4,128)}), f32[32,4,128]{2,1,0:T(4,128)S(1)}, u32[]{:S(2)}, u32[]{:S(2)}) async-start(f32[32,4,128]{2,1,0:T(4,128)} %bitcast.4), calls=%async_computation.1 | async-start | bytes 131072 | tf_op jit(solution)/shard_map/all_to_all | solution.py:232
  48.2 0.8 %collective-permute-done.11 = bf16[1,2,80,256]{3,2,1,0:T(8,128)(2,1)S(1)} collective-permute-done((bf16[1,2,80,256]{3,2,1,0:T(8,128)(2,1)S(1)}, bf16[1,2,80,256]{3,2,1,0:T(8,128)(2,1)S(1)}, u32[]{:S(2)}, u32[]{:S(2)}) %collective-permute-start.11) | collective-permute-done | bytes 81952 | tf_op jit(solution)/shard_map/ppermute | solution.py:153
  49.1 6.5 %all-to-all-done.1.start = f32[32,4,128]{2,1,0:T(4,128)S(1)} async-done(((f32[32,4,128]{2,1,0:T(4,128)}), f32[32,4,128]{2,1,0:T(4,128)S(1)}, u32[]{:S(2)}, u32[]{:S(2)}) %all-to-all-start.1) | async-done | bytes 65568 | tf_op jit(solution)/shard_map/all_to_all | solution.py:232
  55.6 0.5 collective-permute-start.12
  56.1 0.9 %collective-permute-start.16 = (bf16[2,2,80,256]{3,2,1,0:T(8,128)(2,1)S(1)}, bf16[2,2,80,256]{3,2,1,0:T(8,128)(2,1)S(1)}, u32[]{:S(2)}, u32[]{:S(2)}) collective-permute-start(bf16[2,2,80,256]{3,2,1,0:T(8,128)(2,1)S(1)} %pad_maximum_fusion.1), channel_id=1, source_target_pairs={{0,4},{1,5},{2,6},{3,7},{4,0},{5,1},{6,2},{7,3},{8,12},{9,13},{10,... | collective-permute-start | bytes 491528 | tf_op jit(solution)/shard_map/ppermute | solution.py:153
  57.1 0.6 collective-permute-start.20
  57.7 4.2 %collective-permute-done.12 = bf16[2,2,80,256]{3,2,1,0:T(8,128)(2,1)S(1)} collective-permute-done((bf16[2,2,80,256]{3,2,1,0:T(8,128)(2,1)S(1)}, bf16[2,2,80,256]{3,2,1,0:T(8,128)(2,1)S(1)}, u32[]{:S(2)}, u32[]{:S(2)}) %collective-permute-start.12) | collective-permute-done | bytes 163872 | tf_op jit(solution)/shard_map/ppermute | solution.py:153
  61.9 0.4 collective-permute-start.13
  62.3 0.0 copy-start.3
  62.3 0.7 collective-permute-start.17
  63.1 1.4 %collective-permute-start.21 = (bf16[4,2,80,256]{3,2,1,0:T(8,128)(2,1)S(1)}, bf16[4,2,80,256]{3,2,1,0:T(8,128)(2,1)S(1)}, u32[]{:S(2)}, u32[]{:S(2)}) collective-permute-start(bf16[4,2,80,256]{3,2,1,0:T(8,128)(2,1)S(1)} %constant_dynamic-update-slice_fusion.8.refs_0_), channel_id=1, source_target_pairs={{0,2},{1,3},{2,0},{3,1},{4,6},{5,7},{6,4},{7,5},{8,10},{9,11},{10,... | collective-permute-start | bytes 983048 | tf_op jit(solution)/shard_map/ppermute | solution.py:153
  64.4 6.4 %collective-permute-done.13.refs_1_ = bf16[4,2,80,256]{3,2,1,0:T(8,128)(2,1)S(1)} collective-permute-done((bf16[4,2,80,256]{3,2,1,0:T(8,128)(2,1)S(1)}, bf16[4,2,80,256]{3,2,1,0:T(8,128)(2,1)S(1)}, u32[]{:S(2)}, u32[]{:S(2)}) %collective-permute-start.13) | collective-permute-done | bytes 327712 | tf_op jit(solution)/shard_map/ppermute | solution.py:153
  70.9 0.5 collective-permute-start.18
  71.4 1.2 %collective-permute-done.17.refs_1_ = bf16[4,2,80,256]{3,2,1,0:T(8,128)(2,1)S(1)} collective-permute-done((bf16[4,2,80,256]{3,2,1,0:T(8,128)(2,1)S(1)}, bf16[4,2,80,256]{3,2,1,0:T(8,128)(2,1)S(1)}, u32[]{:S(2)}, u32[]{:S(2)}) %collective-permute-start.17) | collective-permute-done | bytes 327712 | tf_op jit(solution)/shard_map/ppermute | solution.py:156
  72.5 0.5 collective-permute-start.22
  73.0 0.1 collective-permute-start.23
  73.1 1.9 %chain0.1.start = f32[8,2048]{1,0:T(8,128)S(1)} custom-call(s32[6]{0:T(128)S(1)} %copy-done.3, f32[32,4,128]{2,1,0:T(4,128)S(1)} %all-to-all-done.1.start, bf16[4,2,80,256]{3,2,1,0:T(8,128)(2,1)S(1)} %constant_dynamic-update-slice_fusion.4.refs_0_, bf16[4,2,80,256]{3,2,1,0:T(8,128)(2,1)S(1)} %collective-permute-done.13.refs_1_, ...), custom_call_target="tpu_custom_call" | custom-call | tf_op jit(solution)/shard_map/chain0/pallas_call | solution.py:271
  75.0 1.9 %chain1.1.start = f32[8,2048]{1,0:T(8,128)S(1)} custom-call(s32[6]{0:T(128)S(1)} %copy-done.3, f32[8,2048]{1,0:T(8,128)S(1)} %chain0.1.start, bf16[4,2,80,256]{3,2,1,0:T(8,128)(2,1)S(1)} %constant_dynamic-update-slice_fusion.6.refs_0_, bf16[4,2,80,256]{3,2,1,0:T(8,128)(2,1)S(1)} %collective-permute-done.17.refs_1_, ...), custom_call_target="tpu_custom_call" | custom-call | tf_op jit(solution)/shard_map/chain1/pallas_call | solution.py:271
  77.0 2.5 %chain2.1 = bf16[4,2048]{1,0:T(4,128)(2,1)} custom-call(s32[6]{0:T(128)S(1)} %copy-done.3, f32[8,2048]{1,0:T(8,128)S(1)} %chain1.1.start, bf16[4,2,80,256]{3,2,1,0:T(8,128)(2,1)S(1)} %constant_dynamic-update-slice_fusion.8.refs_0_, bf16[4,2,80,256]{3,2,1,0:T(8,128)(2,1)S(1)} %collective-permute-done.21.refs_1_, ...), custom_call_target="tpu_custom_call" | custom-call | tf_op jit(solution)/shard_map/chain2/pallas_call | solution.py:271
  (39 shorter events, 0.3 us)
Async XLA Ops:
  0.0 7.9 %collective-permute-start = (bf16[64,512]{1,0:T(8,128)(2,1)}, bf16[64,512]{1,0:T(8,128)(2,1)S(1)}, u32[]{:S(2)}, u32[]{:S(2)}) collective-permute-start(bf16[64,512]{1,0:T(8,128)(2,1)} %param.7), channel_id=1, source_target_pairs={{0,8},{1,9},{2,10},{3,11},{4,12},{5,13},{6,14},{7,15},{8,0},{9,1},... | collective-permute-start | bytes 196616 | tf_op jit(solution)/shard_map/ppermute | solution.py:153
  4.0 1.0 %copy-start.1 = (bf16[1,1024,256]{2,1,0:T(8,128)(2,1)S(1)}, bf16[1,1024,256]{2,1,0:T(8,128)(2,1)}, u32[]{:S(2)}) copy-start(bf16[1,1024,256]{2,1,0:T(8,128)(2,1)} %param.8) | copy-start | bytes 1572868
  5.1 0.9 %copy-start.2 = (bf16[1,256,256]{2,1,0:T(8,128)(2,1)S(1)}, bf16[1,256,256]{2,1,0:T(8,128)(2,1)}, u32[]{:S(2)}) copy-start(bf16[1,256,256]{2,1,0:T(8,128)(2,1)} %param.9) | copy-start | bytes 393220
  7.9 3.6 %copy-start.5 = (bf16[64,512]{1,0:T(8,128)(2,1)S(1)}, bf16[64,512]{1,0:T(8,128)(2,1)}, u32[]{:S(2)}) copy-start(bf16[64,512]{1,0:T(8,128)(2,1)} %param.7) | copy-start | bytes 196612
  7.9 12.4 %all-to-all-start = ((bf16[8,80,256]{2,1,0:T(8,128)(2,1)}), bf16[8,80,256]{2,1,0:T(8,128)(2,1)S(1)}, u32[]{:S(2)}, u32[]{:S(2)}) async-start(bf16[8,80,256]{2,1,0:T(8,128)(2,1)} %pack.1), calls=%async_computation | async-start | bytes 655360 | tf_op jit(solution)/shard_map/all_to_all | solution.py:177
  11.5 8.8 %copy-start.4 = (s32[6]{0:T(128)S(1)}, s32[6]{0:T(128)}, u32[]{:S(2)}) copy-start(s32[6]{0:T(128)} %owners.3) | copy-start | bytes 76
  11.5 4.4 %collective-permute-start.2 = (bf16[64,512]{1,0:T(8,128)(2,1)S(1)}, bf16[64,512]{1,0:T(8,128)(2,1)S(1)}, u32[]{:S(2)}, u32[]{:S(2)}) collective-permute-start(bf16[64,512]{1,0:T(8,128)(2,1)S(1)} %get-tuple-element.35), channel_id=1, source_target_pairs={{0,16},{16,0},{1,17},{17,1},{2,18},{18,2},{3,19},{19,3},{4,20},{20... | collective-permute-start | bytes 196616 | tf_op jit(solution)/shard_map/ppermute | solution.py:156
  13.3 6.2 %collective-permute-start.1 = (bf16[1,64,512]{2,1,0:T(8,128)(2,1)S(1)}, bf16[1,64,512]{2,1,0:T(8,128)(2,1)S(1)}, u32[]{:S(2)}, u32[]{:S(2)}) collective-permute-start(bf16[1,64,512]{2,1,0:T(8,128)(2,1)S(1)} %get-tuple-element.36), channel_id=1, source_target_pairs={{0,2},{1,3},{2,0},{3,1},{4,6},{5,7},{6,4},{7,5},{8,10},{9,11},{10,... | collective-permute-start | bytes 196616 | tf_op jit(solution)/shard_map/ppermute | solution.py:153
  16.0 14.9 %copy-start = (bf16[4096,128]{1,0:T(8,128)(2,1)S(1)}, bf16[4096,128]{1,0:T(8,128)(2,1)}, u32[]{:S(2)}) copy-start(bf16[4096,128]{1,0:T(8,128)(2,1)} %sub.6) | copy-start | bytes 3145732
  16.0 4.3 %collective-permute-start.3 = (bf16[1,64,512]{2,1,0:T(8,128)(2,1)S(1)}, bf16[1,64,512]{2,1,0:T(8,128)(2,1)S(1)}, u32[]{:S(2)}, u32[]{:S(2)}) collective-permute-start(bf16[1,64,512]{2,1,0:T(8,128)(2,1)S(1)} %bitcast.8), channel_id=1, source_target_pairs={{0,4},{1,5},{2,6},{3,7},{4,0},{5,1},{6,2},{7,3},{8,12},{9,13},{10,... | collective-permute-start | bytes 196616 | tf_op jit(solution)/shard_map/ppermute | solution.py:153
  21.0 5.0 %collective-permute-start.5 = (bf16[2,64,512]{2,1,0:T(8,128)(2,1)S(1)}, bf16[2,64,512]{2,1,0:T(8,128)(2,1)S(1)}, u32[]{:S(2)}, u32[]{:S(2)}) collective-permute-start(bf16[2,64,512]{2,1,0:T(8,128)(2,1)S(1)} %pad_maximum_fusion.3), channel_id=1, source_target_pairs={{0,4},{1,5},{2,6},{3,7},{4,0},{5,1},{6,2},{7,3},{8,12},{9,13},{10,... | collective-permute-start | bytes 393224 | tf_op jit(solution)/shard_map/ppermute | solution.py:153
  22.9 5.0 %collective-permute-start.6 = (bf16[2,64,512]{2,1,0:T(8,128)(2,1)S(1)}, bf16[2,64,512]{2,1,0:T(8,128)(2,1)S(1)}, u32[]{:S(2)}, u32[]{:S(2)}) collective-permute-start(bf16[2,64,512]{2,1,0:T(8,128)(2,1)S(1)} %pad_maximum_fusion.4), channel_id=1, source_target_pairs={{0,2},{1,3},{2,0},{3,1},{4,6},{5,7},{6,4},{7,5},{8,10},{9,11},{10,... | collective-permute-start | bytes 393224 | tf_op jit(solution)/shard_map/ppermute | solution.py:153
  24.4 6.4 %collective-permute-start.7 = (bf16[4,64,512]{2,1,0:T(8,128)(2,1)S(1)}, bf16[4,64,512]{2,1,0:T(8,128)(2,1)S(1)}, u32[]{:S(2)}, u32[]{:S(2)}) collective-permute-start(bf16[4,64,512]{2,1,0:T(8,128)(2,1)S(1)} %constant_dynamic-update-slice_fusion.refs_0_), channel_id=1, source_target_pairs={{0,1},{1,0},{2,3},{3,2},{4,5},{5,4},{6,7},{7,6},{8,9},{9,8},{10,11... | collective-permute-start | bytes 786440 | tf_op jit(solution)/shard_map/ppermute | solution.py:153
  27.9 3.0 %collective-permute-start.8 = (bf16[4,64,512]{2,1,0:T(8,128)(2,1)S(1)}, bf16[4,64,512]{2,1,0:T(8,128)(2,1)S(1)}, u32[]{:S(2)}, u32[]{:S(2)}) collective-permute-start(bf16[4,64,512]{2,1,0:T(8,128)(2,1)S(1)} %constant_dynamic-update-slice_fusion.2.refs_1_), channel_id=1, source_target_pairs={{0,1},{1,0},{2,3},{3,2},{4,5},{5,4},{6,7},{7,6},{8,9},{9,8},{10,11... | collective-permute-start | bytes 786440 | tf_op jit(solution)/shard_map/ppermute | solution.py:153
  28.0 12.6 %collective-permute-start.4 = (bf16[5,80,256]{2,1,0:T(8,128)(2,1)S(1)}, bf16[5,80,256]{2,1,0:T(8,128)(2,1)S(1)}, u32[]{:S(2)}, u32[]{:S(2)}) collective-permute-start(bf16[5,80,256]{2,1,0:T(8,128)(2,1)S(1)} %pick.1), channel_id=1, source_target_pairs={{0,8},{1,9},{2,10},{3,11},{4,12},{5,13},{6,14},{7,15},{8,0},{9,1},... | collective-permute-start | bytes 614408 | tf_op jit(solution)/shard_map/ppermute | solution.py:153
  41.2 6.9 %collective-permute-start.9 = (bf16[1,2,80,256]{3,2,1,0:T(8,128)(2,1)S(1)}, bf16[1,2,80,256]{3,2,1,0:T(8,128)(2,1)S(1)}, u32[]{:S(2)}, u32[]{:S(2)}) collective-permute-start(bf16[1,2,80,256]{3,2,1,0:T(8,128)(2,1)S(1)} %get-tuple-element.27), channel_id=1, source_target_pairs={{0,16},{16,0},{1,17},{17,1},{2,18},{18,2},{3,19},{19,3},{4,20},{20... | collective-permute-start | bytes 245768 | tf_op jit(solution)/shard_map/ppermute | solution.py:156
  42.8 5.4 %collective-permute-start.10 = (bf16[1,2,80,256]{3,2,1,0:T(8,128)(2,1)S(1)}, bf16[1,2,80,256]{3,2,1,0:T(8,128)(2,1)S(1)}, u32[]{:S(2)}, u32[]{:S(2)}) collective-permute-start(bf16[1,2,80,256]{3,2,1,0:T(8,128)(2,1)S(1)} %get-tuple-element.28), channel_id=1, source_target_pairs={{0,2},{1,3},{2,0},{3,1},{4,6},{5,7},{6,4},{7,5},{8,10},{9,11},{10,... | collective-permute-start | bytes 245768 | tf_op jit(solution)/shard_map/ppermute | solution.py:153
  44.6 4.4 %collective-permute-start.11 = (bf16[1,2,80,256]{3,2,1,0:T(8,128)(2,1)S(1)}, bf16[1,2,80,256]{3,2,1,0:T(8,128)(2,1)S(1)}, u32[]{:S(2)}, u32[]{:S(2)}) collective-permute-start(bf16[1,2,80,256]{3,2,1,0:T(8,128)(2,1)S(1)} %get-tuple-element.29), channel_id=1, source_target_pairs={{0,4},{1,5},{2,6},{3,7},{4,0},{5,1},{6,2},{7,3},{8,12},{9,13},{10,... | collective-permute-start | bytes 245768 | tf_op jit(solution)/shard_map/ppermute | solution.py:153
  44.6 10.9 %all-to-all-start.1 = ((f32[32,4,128]{2,1,0:T(4,128)}), f32[32,4,128]{2,1,0:T(4,128)S(1)}, u32[]{:S(2)}, u32[]{:S(2)}) async-start(f32[32,4,128]{2,1,0:T(4,128)} %bitcast.4), calls=%async_computation.1 | async-start | bytes 131072 | tf_op jit(solution)/shard_map/all_to_all | solution.py:232
  55.6 6.3 %collective-permute-start.12 = (bf16[2,2,80,256]{3,2,1,0:T(8,128)(2,1)S(1)}, bf16[2,2,80,256]{3,2,1,0:T(8,128)(2,1)S(1)}, u32[]{:S(2)}, u32[]{:S(2)}) collective-permute-start(bf16[2,2,80,256]{3,2,1,0:T(8,128)(2,1)S(1)} %pad_maximum_fusion), channel_id=1, source_target_pairs={{0,2},{1,3},{2,0},{3,1},{4,6},{5,7},{6,4},{7,5},{8,10},{9,11},{10,... | collective-permute-start | bytes 491528 | tf_op jit(solution)/shard_map/ppermute | solution.py:153
  56.1 6.2 %collective-permute-start.16 = (bf16[2,2,80,256]{3,2,1,0:T(8,128)(2,1)S(1)}, bf16[2,2,80,256]{3,2,1,0:T(8,128)(2,1)S(1)}, u32[]{:S(2)}, u32[]{:S(2)}) collective-permute-start(bf16[2,2,80,256]{3,2,1,0:T(8,128)(2,1)S(1)} %pad_maximum_fusion.1), channel_id=1, source_target_pairs={{0,4},{1,5},{2,6},{3,7},{4,0},{5,1},{6,2},{7,3},{8,12},{9,13},{10,... | collective-permute-start | bytes 491528 | tf_op jit(solution)/shard_map/ppermute | solution.py:153
  57.1 6.0 %collective-permute-start.20 = (bf16[2,2,80,256]{3,2,1,0:T(8,128)(2,1)S(1)}, bf16[2,2,80,256]{3,2,1,0:T(8,128)(2,1)S(1)}, u32[]{:S(2)}, u32[]{:S(2)}) collective-permute-start(bf16[2,2,80,256]{3,2,1,0:T(8,128)(2,1)S(1)} %pad_maximum_fusion.2), channel_id=1, source_target_pairs={{0,16},{16,0},{1,17},{17,1},{2,18},{18,2},{3,19},{19,3},{4,20},{20... | collective-permute-start | bytes 491528 | tf_op jit(solution)/shard_map/ppermute | solution.py:156
  61.9 9.0 %collective-permute-start.13 = (bf16[4,2,80,256]{3,2,1,0:T(8,128)(2,1)S(1)}, bf16[4,2,80,256]{3,2,1,0:T(8,128)(2,1)S(1)}, u32[]{:S(2)}, u32[]{:S(2)}) collective-permute-start(bf16[4,2,80,256]{3,2,1,0:T(8,128)(2,1)S(1)} %constant_dynamic-update-slice_fusion.4.refs_0_), channel_id=1, source_target_pairs={{0,4},{1,5},{2,6},{3,7},{4,0},{5,1},{6,2},{7,3},{8,12},{9,13},{10,... | collective-permute-start | bytes 983048 | tf_op jit(solution)/shard_map/ppermute | solution.py:153
  62.3 10.2 %collective-permute-start.14 = (bf16[4,2,80,256]{3,2,1,0:T(8,128)(2,1)S(1)}, bf16[4,2,80,256]{3,2,1,0:T(8,128)(2,1)S(1)}, u32[]{:S(2)}, u32[]{:S(2)}) collective-permute-start(bf16[4,2,80,256]{3,2,1,0:T(8,128)(2,1)S(1)} %constant_dynamic-update-slice_fusion.4.refs_0_), channel_id=1, source_target_pairs={{0,1},{1,0},{2,3},{3,2},{4,5},{5,4},{6,7},{7,6},{8,9},{9,8},{10,11... | collective-permute-start | bytes 983048 | tf_op jit(solution)/shard_map/ppermute | solution.py:153
  62.3 10.8 %copy-start.3 = (s32[6]{0:T(128)S(1)}, s32[6]{0:T(128)}, u32[]{:S(2)}) copy-start(s32[6]{0:T(128)} %offsets.5) | copy-start | bytes 76
  62.3 10.2 %collective-permute-start.17 = (bf16[4,2,80,256]{3,2,1,0:T(8,128)(2,1)S(1)}, bf16[4,2,80,256]{3,2,1,0:T(8,128)(2,1)S(1)}, u32[]{:S(2)}, u32[]{:S(2)}) collective-permute-start(bf16[4,2,80,256]{3,2,1,0:T(8,128)(2,1)S(1)} %constant_dynamic-update-slice_fusion.6.refs_0_), channel_id=1, source_target_pairs={{0,16},{16,0},{1,17},{17,1},{2,18},{18,2},{3,19},{19,3},{4,20},{20... | collective-permute-start | bytes 983048 | tf_op jit(solution)/shard_map/ppermute | solution.py:156
  63.1 10.0 %collective-permute-start.21 = (bf16[4,2,80,256]{3,2,1,0:T(8,128)(2,1)S(1)}, bf16[4,2,80,256]{3,2,1,0:T(8,128)(2,1)S(1)}, u32[]{:S(2)}, u32[]{:S(2)}) collective-permute-start(bf16[4,2,80,256]{3,2,1,0:T(8,128)(2,1)S(1)} %constant_dynamic-update-slice_fusion.8.refs_0_), channel_id=1, source_target_pairs={{0,2},{1,3},{2,0},{3,1},{4,6},{5,7},{6,4},{7,5},{8,10},{9,11},{10,... | collective-permute-start | bytes 983048 | tf_op jit(solution)/shard_map/ppermute | solution.py:153
  70.9 2.3 %collective-permute-start.15 = (bf16[4,2,80,256]{3,2,1,0:T(8,128)(2,1)S(1)}, bf16[4,2,80,256]{3,2,1,0:T(8,128)(2,1)S(1)}, u32[]{:S(2)}, u32[]{:S(2)}) collective-permute-start(bf16[4,2,80,256]{3,2,1,0:T(8,128)(2,1)S(1)} %collective-permute-done.13.refs_1_), channel_id=1, source_target_pairs={{0,1},{1,0},{2,3},{3,2},{4,5},{5,4},{6,7},{7,6},{8,9},{9,8},{10,11... | collective-permute-start | bytes 983048 | tf_op jit(solution)/shard_map/ppermute | solution.py:153
  70.9 4.2 %collective-permute-start.18 = (bf16[4,2,80,256]{3,2,1,0:T(8,128)(2,1)S(1)}, bf16[4,2,80,256]{3,2,1,0:T(8,128)(2,1)S(1)}, u32[]{:S(2)}, u32[]{:S(2)}) collective-permute-start(bf16[4,2,80,256]{3,2,1,0:T(8,128)(2,1)S(1)} %constant_dynamic-update-slice_fusion.6.refs_0_), channel_id=1, source_target_pairs={{0,1},{1,0},{2,3},{3,2},{4,5},{5,4},{6,7},{7,6},{8,9},{9,8},{10,11... | collective-permute-start | bytes 983048 | tf_op jit(solution)/shard_map/ppermute | solution.py:153
  72.5 2.5 %collective-permute-start.19 = (bf16[4,2,80,256]{3,2,1,0:T(8,128)(2,1)S(1)}, bf16[4,2,80,256]{3,2,1,0:T(8,128)(2,1)S(1)}, u32[]{:S(2)}, u32[]{:S(2)}) collective-permute-start(bf16[4,2,80,256]{3,2,1,0:T(8,128)(2,1)S(1)} %collective-permute-done.17.refs_1_), channel_id=1, source_target_pairs={{0,1},{1,0},{2,3},{3,2},{4,5},{5,4},{6,7},{7,6},{8,9},{9,8},{10,11... | collective-permute-start | bytes 983048 | tf_op jit(solution)/shard_map/ppermute | solution.py:153
  72.5 4.4 %collective-permute-start.22 = (bf16[4,2,80,256]{3,2,1,0:T(8,128)(2,1)S(1)}, bf16[4,2,80,256]{3,2,1,0:T(8,128)(2,1)S(1)}, u32[]{:S(2)}, u32[]{:S(2)}) collective-permute-start(bf16[4,2,80,256]{3,2,1,0:T(8,128)(2,1)S(1)} %constant_dynamic-update-slice_fusion.8.refs_0_), channel_id=1, source_target_pairs={{0,1},{1,0},{2,3},{3,2},{4,5},{5,4},{6,7},{7,6},{8,9},{9,8},{10,11... | collective-permute-start | bytes 983048 | tf_op jit(solution)/shard_map/ppermute | solution.py:153
  73.0 3.9 %collective-permute-start.23 = (bf16[4,2,80,256]{3,2,1,0:T(8,128)(2,1)S(1)}, bf16[4,2,80,256]{3,2,1,0:T(8,128)(2,1)S(1)}, u32[]{:S(2)}, u32[]{:S(2)}) collective-permute-start(bf16[4,2,80,256]{3,2,1,0:T(8,128)(2,1)S(1)} %collective-permute-done.21.refs_1_), channel_id=1, source_target_pairs={{0,1},{1,0},{2,3},{3,2},{4,5},{5,4},{6,7},{7,6},{8,9},{9,8},{10,11... | collective-permute-start | bytes 983048 | tf_op jit(solution)/shard_map/ppermute | solution.py:153

commit v11 on v10

--- a/solution.py
+++ b/solution.py
@@ -68,8 +68,10 @@
     for group in range(GROUPS):
         half, rank = places(owners, group)
         piece = held[lax.rem(owners[group], HALF)]
-        for mask, ref in enumerate(others, 1):
-            other = ref[jnp.minimum(rank, ref.shape[0] - 1)]
+        for mask in range(1, len(others) // 2 + 1):
+            head, tail = others[2 * mask - 2 : 2 * mask]
+            other = tail[jnp.clip(rank - 1, 0, tail.shape[0] - 1)]
+            other = jnp.where(rank == 0, head[0], other)
             piece = jnp.where(jnp.bitwise_xor(half, mine) == mask, other, piece)
         outs[group // each][0, group % each] = piece
 
@@ -211,7 +213,10 @@
     double(0, 2)
     double(1, 4)
     picked, sides = lax.optimization_barrier((picked, sides))
-    others = [over_col(picked, m * HALF) for m in range(1, halves)]
+    heads = [over_col(picked[:1], m * HALF) for m in range(1, halves)]
+    tails = [over_col(picked[1:], m * HALF) for m in range(1, halves)]
+    heads, sides = lax.optimization_barrier((heads, sides))
+    others = [x for pair in zip(heads, tails) for x in pair]
     late = jnp.concatenate([over_col(sides[0], 4), over_col(sides[1], 2)])
     late_tags = [(m, c ^ 4) for m, c in tags[0]] + [(m, c ^ 2) for m, c in tags[1]]
     m_held = [jnp.concatenate(sides), late]
@@ -252,8 +257,7 @@
             mask, send = links[(k + step) % 3]
             colours[k] = jnp.concatenate([colours[k], send(colours[k])])
             masks[k] = masks[k] + [m ^ mask for m in masks[k]]
-        if step == 0:
-            colours, state = lax.optimization_barrier((colours, state))
+    colours, state = lax.optimization_barrier((colours, state))
     last_round = []
     for k in range(COLOURS):
         mask, send = links[(k + 2) % 3]

time: 79.8 us -> 82.2 us (1.030)
  starting transfers between devices: 32 us -> 40.8 us
  waiting for transfers between devices: 35.5 us -> 29.1 us
    all_to_all x1, waiting for transfers between devices: 6.49 us -> 0.01 us  [local(): lax.all_to_all(merged.reshape(rows * cols, each, width), ('row', 'col'),...]
    ppermute x20 -> x21, starting transfers between devices: 20.2 us -> 26.4 us  [over_col(): return lax.ppermute(x, 'col', [(c, c ^ mask) for c in range(cols)])]
    ppermute x4, starting transfers between devices: 4.71 us -> 6.34 us  [over_row(): return lax.ppermute(x, 'row', [(r, r ^ mask) for r in range(rows)])]
    all_to_all x1, starting transfers between devices: 3.53 us -> 4.45 us  [local(): lax.all_to_all(merged.reshape(rows * cols, each, width), ('row', 'col'),...]
    ppermute x4, waiting for transfers between devices: 1.94 us -> 2.85 us  [over_row(): return lax.ppermute(x, 'row', [(r, r ^ mask) for r in range(rows)])]
    ppermute x20 -> x21, waiting for transfers between devices: 27.1 us -> 26.2 us  [over_col(): return lax.ppermute(x, 'col', [(c, c ^ mask) for c in range(cols)])]
    unnamed x17 -> x14, local copies, waits for them, and re-layouts: 2.02 us -> 1.99 us
  transfers between devices with their start and end apart: 26 -> 27, of which waited for: 12 -> 14; matrix products, arithmetic and copies ran while one was open for 0% -> 0% of each run, Pallas kernels for 7% -> 7%
where the time goes in v11:
time: 82.2 us; the launch traced here: 81.8 us
  starting transfers between devices  40.8 us (50%)
  waiting for transfers between devices  29.1 us (35%)
  Pallas kernels  9.51 us (12%)
  local copies, waits for them, and re-layouts  2.02 us (2%)
    ppermute x21, starting transfers between devices, over_col(): return lax.ppermute(x, 'col', [(c, c ^ mask) for c in range(cols)])  26.4 us
    ppermute x21, waiting for transfers between devices, over_col(): return lax.ppermute(x, 'col', [(c, c ^ mask) for c in range(cols)])  26.2 us
    ppermute x4, starting transfers between devices, over_row(): return lax.ppermute(x, 'row', [(r, r ^ mask) for r in range(rows)])  6.34 us
    pallas_call x3, Pallas kernels, local(): pl.pallas_call(functools.partial(chain_kernel, cols, groups, masks[k], fi...  6.28 us
    all_to_all x1, starting transfers between devices, local(): lax.all_to_all(merged.reshape(rows * cols, each, width), ('row', 'col'),...  4.45 us
    all_to_all x1, starting transfers between devices, local(): slices = lax.all_to_all(packed, 'col', 0, 0, axis_index_groups=members)  3.56 us
    ppermute x4, waiting for transfers between devices, over_row(): return lax.ppermute(x, 'row', [(r, r ^ mask) for r in range(rows)])  2.85 us
    unnamed x14, local copies, waits for them, and re-layouts  1.99 us
  transfers between devices with their start and end apart: 27, of which 14 were waited for; matrix products, arithmetic and copies ran while one was open for 0% of the time, Pallas kernels for 7%

profile of v11, /device:TPU:0, one launch (start us, length us, event | category | flops | bytes accessed | tf_op | source)
XLA Modules:
  0.0 81.8 jit_solution(1080295956604467577)
XLA Ops:
  0.0 4.0 %collective-permute-start = (bf16[64,512]{1,0:T(8,128)(2,1)}, bf16[64,512]{1,0:T(8,128)(2,1)S(1)}, u32[]{:S(2)}, u32[]{:S(2)}) collective-permute-start(bf16[64,512]{1,0:T(8,128)(2,1)} %param.7), channel_id=1, source_target_pairs={{0,8},{1,9},{2,10},{3,11},{4,12},{5,13},{6,14},{7,15},{8,0},{9,1},... | collective-permute-start | bytes 196616 | tf_op jit(solution)/shard_map/ppermute | solution.py:155
  4.0 1.0 %copy-done.1 = bf16[1,1024,256]{2,1,0:T(8,128)(2,1)S(1)} copy-done((bf16[1,1024,256]{2,1,0:T(8,128)(2,1)S(1)}, bf16[1,1024,256]{2,1,0:T(8,128)(2,1)}, u32[]{:S(2)}) %copy-start.1) | copy-done | bytes 524312
  5.1 0.9 %copy-done.2 = bf16[1,256,256]{2,1,0:T(8,128)(2,1)S(1)} copy-done((bf16[1,256,256]{2,1,0:T(8,128)(2,1)S(1)}, bf16[1,256,256]{2,1,0:T(8,128)(2,1)}, u32[]{:S(2)}) %copy-start.2) | copy-done | bytes 131096
  6.0 0.8 pack.1
  6.8 1.1 %collective-permute-done = bf16[64,512]{1,0:T(8,128)(2,1)S(1)} collective-permute-done((bf16[64,512]{1,0:T(8,128)(2,1)}, bf16[64,512]{1,0:T(8,128)(2,1)S(1)}, u32[]{:S(2)}, u32[]{:S(2)}) %collective-permute-start) | collective-permute-done | bytes 65568 | tf_op jit(solution)/shard_map/ppermute | solution.py:155
  7.9 3.6 %all-to-all-start = ((bf16[8,80,256]{2,1,0:T(8,128)(2,1)}), bf16[8,80,256]{2,1,0:T(8,128)(2,1)S(1)}, u32[]{:S(2)}, u32[]{:S(2)}) async-start(bf16[8,80,256]{2,1,0:T(8,128)(2,1)} %pack.1), calls=%async_computation | async-start | bytes 655360 | tf_op jit(solution)/shard_map/all_to_all | solution.py:179
  11.5 1.8 %collective-permute-start.2 = (bf16[64,512]{1,0:T(8,128)(2,1)S(1)}, bf16[64,512]{1,0:T(8,128)(2,1)S(1)}, u32[]{:S(2)}, u32[]{:S(2)}) collective-permute-start(bf16[64,512]{1,0:T(8,128)(2,1)S(1)} %get-tuple-element.43), channel_id=1, source_target_pairs={{0,16},{16,0},{1,17},{17,1},{2,18},{18,2},{3,19},{19,3},{4,20},{20... | collective-permute-start | bytes 196616 | tf_op jit(solution)/shard_map/ppermute | solution.py:158
  13.3 1.9 %collective-permute-start.1 = (bf16[1,64,512]{2,1,0:T(8,128)(2,1)S(1)}, bf16[1,64,512]{2,1,0:T(8,128)(2,1)S(1)}, u32[]{:S(2)}, u32[]{:S(2)}) collective-permute-start(bf16[1,64,512]{2,1,0:T(8,128)(2,1)S(1)} %get-tuple-element.44), channel_id=1, source_target_pairs={{0,2},{1,3},{2,0},{3,1},{4,6},{5,7},{6,4},{7,5},{8,10},{9,11},{10,... | collective-permute-start | bytes 196616 | tf_op jit(solution)/shard_map/ppermute | solution.py:155
  15.2 0.8 collective-permute-done.2
  16.0 1.8 %collective-permute-start.3 = (bf16[1,64,512]{2,1,0:T(8,128)(2,1)S(1)}, bf16[1,64,512]{2,1,0:T(8,128)(2,1)S(1)}, u32[]{:S(2)}, u32[]{:S(2)}) collective-permute-start(bf16[1,64,512]{2,1,0:T(8,128)(2,1)S(1)} %bitcast.8), channel_id=1, source_target_pairs={{0,4},{1,5},{2,6},{3,7},{4,0},{5,1},{6,2},{7,3},{8,12},{9,13},{10,... | collective-permute-start | bytes 196616 | tf_op jit(solution)/shard_map/ppermute | solution.py:155
  17.8 1.8 %collective-permute-done.1 = bf16[1,64,512]{2,1,0:T(8,128)(2,1)S(1)} collective-permute-done((bf16[1,64,512]{2,1,0:T(8,128)(2,1)S(1)}, bf16[1,64,512]{2,1,0:T(8,128)(2,1)S(1)}, u32[]{:S(2)}, u32[]{:S(2)}) %collective-permute-start.1) | collective-permute-done | bytes 65568 | tf_op jit(solution)/shard_map/ppermute | solution.py:155
  19.5 0.0 copy-start.4
  19.5 0.7 collective-permute-done.3
  20.3 0.7 pick.1
  21.0 2.9 %collective-permute-start.4 = (bf16[1,80,256]{2,1,0:T(8,128)(2,1)S(1)}, bf16[1,80,256]{2,1,0:T(8,128)(2,1)S(1)}, u32[]{:S(2)}, u32[]{:S(2)}) collective-permute-start(bf16[1,80,256]{2,1,0:T(8,128)(2,1)S(1)} %slice.6), channel_id=1, source_target_pairs={{0,8},{1,9},{2,10},{3,11},{4,12},{5,13},{6,14},{7,15},{8,0},{9,1},... | collective-permute-start | bytes 122888 | tf_op jit(solution)/shard_map/ppermute | solution.py:155
  23.9 2.2 %collective-permute-done.4.refs_0_ = bf16[1,80,256]{2,1,0:T(8,128)(2,1)S(1)} collective-permute-done((bf16[1,80,256]{2,1,0:T(8,128)(2,1)S(1)}, bf16[1,80,256]{2,1,0:T(8,128)(2,1)S(1)}, u32[]{:S(2)}, u32[]{:S(2)}) %collective-permute-start.4) | collective-permute-done | bytes 40992 | tf_op jit(solution)/shard_map/ppermute | solution.py:155
  26.1 1.7 %collective-permute-start.6 = (bf16[2,64,512]{2,1,0:T(8,128)(2,1)S(1)}, bf16[2,64,512]{2,1,0:T(8,128)(2,1)S(1)}, u32[]{:S(2)}, u32[]{:S(2)}) collective-permute-start(bf16[2,64,512]{2,1,0:T(8,128)(2,1)S(1)} %pad_maximum_fusion.6), channel_id=1, source_target_pairs={{0,4},{1,5},{2,6},{3,7},{4,0},{5,1},{6,2},{7,3},{8,12},{9,13},{10,... | collective-permute-start | bytes 393224 | tf_op jit(solution)/shard_map/ppermute | solution.py:155
  27.8 1.5 %collective-permute-start.7 = (bf16[2,64,512]{2,1,0:T(8,128)(2,1)S(1)}, bf16[2,64,512]{2,1,0:T(8,128)(2,1)S(1)}, u32[]{:S(2)}, u32[]{:S(2)}) collective-permute-start(bf16[2,64,512]{2,1,0:T(8,128)(2,1)S(1)} %pad_maximum_fusion.7), channel_id=1, source_target_pairs={{0,2},{1,3},{2,0},{3,1},{4,6},{5,7},{6,4},{7,5},{8,10},{9,11},{10,... | collective-permute-start | bytes 393224 | tf_op jit(solution)/shard_map/ppermute | solution.py:155
  29.3 0.1 collective-permute-start.8
  29.4 1.7 %collective-permute-done.6 = bf16[2,64,512]{2,1,0:T(8,128)(2,1)S(1)} collective-permute-done((bf16[2,64,512]{2,1,0:T(8,128)(2,1)S(1)}, bf16[2,64,512]{2,1,0:T(8,128)(2,1)S(1)}, u32[]{:S(2)}, u32[]{:S(2)}) %collective-permute-start.6) | collective-permute-done | bytes 131104 | tf_op jit(solution)/shard_map/ppermute | solution.py:155
  31.1 1.7 %collective-permute-done.7 = bf16[2,64,512]{2,1,0:T(8,128)(2,1)S(1)} collective-permute-done((bf16[2,64,512]{2,1,0:T(8,128)(2,1)S(1)}, bf16[2,64,512]{2,1,0:T(8,128)(2,1)S(1)}, u32[]{:S(2)}, u32[]{:S(2)}) %collective-permute-start.7) | collective-permute-done | bytes 131104 | tf_op jit(solution)/shard_map/ppermute | solution.py:155
  32.8 0.1 collective-permute-start.9
  32.9 3.0 %collective-permute-start.5 = (bf16[4,80,256]{2,1,0:T(8,128)(2,1)S(1)}, bf16[4,80,256]{2,1,0:T(8,128)(2,1)S(1)}, u32[]{:S(2)}, u32[]{:S(2)}) collective-permute-start(bf16[4,80,256]{2,1,0:T(8,128)(2,1)S(1)} %slice.7), channel_id=1, source_target_pairs={{0,8},{1,9},{2,10},{3,11},{4,12},{5,13},{6,14},{7,15},{8,0},{9,1},... | collective-permute-start | bytes 491528 | tf_op jit(solution)/shard_map/ppermute | solution.py:155
  36.0 1.1 %merge.1 = f32[128,128]{1,0:T(8,128)} custom-call(bf16[4096,128]{1,0:T(8,128)(2,1)S(1)} %copy-done, bf16[4,64,512]{2,1,0:T(8,128)(2,1)S(1)} %constant_dynamic-update-slice_fusion.refs_0_, bf16[4,64,512]{2,1,0:T(8,128)(2,1)S(1)} %constant_dynamic-update-slice_fusion.2.refs_1_, bf16[4,64,512]{2,1,0:T(8,128)(2,1)S(1)} %collective-permute-done.8.refs_2_, ...), custom_call_target="tpu_custom_call" | custom-call | tf_op jit(solution)/shard_map/merge/pallas_call | solution.py:228
  37.1 6.9 %collective-permute-done.5.refs_1_ = bf16[4,80,256]{2,1,0:T(8,128)(2,1)S(1)} collective-permute-done((bf16[4,80,256]{2,1,0:T(8,128)(2,1)S(1)}, bf16[4,80,256]{2,1,0:T(8,128)(2,1)S(1)}, u32[]{:S(2)}, u32[]{:S(2)}) %collective-permute-start.5) | collective-permute-done | bytes 163872 | tf_op jit(solution)/shard_map/ppermute | solution.py:155
  44.0 0.6 order.1
  44.6 1.6 %collective-permute-start.10 = (bf16[1,2,80,256]{3,2,1,0:T(8,128)(2,1)S(1)}, bf16[1,2,80,256]{3,2,1,0:T(8,128)(2,1)S(1)}, u32[]{:S(2)}, u32[]{:S(2)}) collective-permute-start(bf16[1,2,80,256]{3,2,1,0:T(8,128)(2,1)S(1)} %get-tuple-element.35), channel_id=1, source_target_pairs={{0,16},{16,0},{1,17},{17,1},{2,18},{18,2},{3,19},{19,3},{4,20},{20... | collective-permute-start | bytes 245768 | tf_op jit(solution)/shard_map/ppermute | solution.py:158
  46.2 4.4 %all-to-all-start.1 = ((f32[32,4,128]{2,1,0:T(4,128)}), f32[32,4,128]{2,1,0:T(4,128)S(1)}, u32[]{:S(2)}, u32[]{:S(2)}) async-start(f32[32,4,128]{2,1,0:T(4,128)} %bitcast.4), calls=%async_computation.1 | async-start | bytes 131072 | tf_op jit(solution)/shard_map/all_to_all | solution.py:237
  50.6 1.8 %collective-permute-start.12 = (bf16[1,2,80,256]{3,2,1,0:T(8,128)(2,1)S(1)}, bf16[1,2,80,256]{3,2,1,0:T(8,128)(2,1)S(1)}, u32[]{:S(2)}, u32[]{:S(2)}) collective-permute-start(bf16[1,2,80,256]{3,2,1,0:T(8,128)(2,1)S(1)} %get-tuple-element.36), channel_id=1, source_target_pairs={{0,2},{1,3},{2,0},{3,1},{4,6},{5,7},{6,4},{7,5},{8,10},{9,11},{10,... | collective-permute-start | bytes 245768 | tf_op jit(solution)/shard_map/ppermute | solution.py:155
  52.5 1.5 %collective-permute-start.14 = (bf16[1,2,80,256]{3,2,1,0:T(8,128)(2,1)S(1)}, bf16[1,2,80,256]{3,2,1,0:T(8,128)(2,1)S(1)}, u32[]{:S(2)}, u32[]{:S(2)}) collective-permute-start(bf16[1,2,80,256]{3,2,1,0:T(8,128)(2,1)S(1)} %get-tuple-element.37), channel_id=1, source_target_pairs={{0,4},{1,5},{2,6},{3,7},{4,0},{5,1},{6,2},{7,3},{8,12},{9,13},{10,... | collective-permute-start | bytes 245768 | tf_op jit(solution)/shard_map/ppermute | solution.py:155
  53.9 0.6 collective-permute-start.11
  54.6 1.0 %collective-permute-done.12 = bf16[1,2,80,256]{3,2,1,0:T(8,128)(2,1)S(1)} collective-permute-done((bf16[1,2,80,256]{3,2,1,0:T(8,128)(2,1)S(1)}, bf16[1,2,80,256]{3,2,1,0:T(8,128)(2,1)S(1)}, u32[]{:S(2)}, u32[]{:S(2)}) %collective-permute-start.12) | collective-permute-done | bytes 81952 | tf_op jit(solution)/shard_map/ppermute | solution.py:155
  55.6 2.6 %collective-permute-start.13 = (bf16[2,2,80,256]{3,2,1,0:T(8,128)(2,1)S(1)}, bf16[2,2,80,256]{3,2,1,0:T(8,128)(2,1)S(1)}, u32[]{:S(2)}, u32[]{:S(2)}) collective-permute-start(bf16[2,2,80,256]{3,2,1,0:T(8,128)(2,1)S(1)} %pad_maximum_fusion.4), channel_id=1, source_target_pairs={{0,4},{1,5},{2,6},{3,7},{4,0},{5,1},{6,2},{7,3},{8,12},{9,13},{10,... | collective-permute-start | bytes 491528 | tf_op jit(solution)/shard_map/ppermute | solution.py:155
  58.2 1.5 %collective-permute-start.15 = (bf16[2,2,80,256]{3,2,1,0:T(8,128)(2,1)S(1)}, bf16[2,2,80,256]{3,2,1,0:T(8,128)(2,1)S(1)}, u32[]{:S(2)}, u32[]{:S(2)}) collective-permute-start(bf16[2,2,80,256]{3,2,1,0:T(8,128)(2,1)S(1)} %pad_maximum_fusion.5), channel_id=1, source_target_pairs={{0,16},{16,0},{1,17},{17,1},{2,18},{18,2},{3,19},{19,3},{4,20},{20... | collective-permute-start | bytes 491528 | tf_op jit(solution)/shard_map/ppermute | solution.py:158
  59.7 0.3 collective-permute-done.11
  60.0 1.5 %collective-permute-done.13 = bf16[2,2,80,256]{3,2,1,0:T(8,128)(2,1)S(1)} collective-permute-done((bf16[2,2,80,256]{3,2,1,0:T(8,128)(2,1)S(1)}, bf16[2,2,80,256]{3,2,1,0:T(8,128)(2,1)S(1)}, u32[]{:S(2)}, u32[]{:S(2)}) %collective-permute-start.13) | collective-permute-done | bytes 163872 | tf_op jit(solution)/shard_map/ppermute | solution.py:155
  61.5 2.1 %collective-permute-done.15 = bf16[2,2,80,256]{3,2,1,0:T(8,128)(2,1)S(1)} collective-permute-done((bf16[2,2,80,256]{3,2,1,0:T(8,128)(2,1)S(1)}, bf16[2,2,80,256]{3,2,1,0:T(8,128)(2,1)S(1)}, u32[]{:S(2)}, u32[]{:S(2)}) %collective-permute-start.15) | collective-permute-done | bytes 163872 | tf_op jit(solution)/shard_map/ppermute | solution.py:158
  63.6 0.3 collective-permute-start.16
  63.9 1.5 %collective-permute-start.19 = (bf16[4,2,80,256]{3,2,1,0:T(8,128)(2,1)S(1)}, bf16[4,2,80,256]{3,2,1,0:T(8,128)(2,1)S(1)}, u32[]{:S(2)}, u32[]{:S(2)}) collective-permute-start(bf16[4,2,80,256]{3,2,1,0:T(8,128)(2,1)S(1)} %pad_maximum_fusion.1.refs_0_), channel_id=1, source_target_pairs={{0,16},{16,0},{1,17},{17,1},{2,18},{18,2},{3,19},{19,3},{4,20},{20... | collective-permute-start | bytes 983048 | tf_op jit(solution)/shard_map/ppermute | solution.py:158
  65.3 1.6 %collective-permute-start.22 = (bf16[4,2,80,256]{3,2,1,0:T(8,128)(2,1)S(1)}, bf16[4,2,80,256]{3,2,1,0:T(8,128)(2,1)S(1)}, u32[]{:S(2)}, u32[]{:S(2)}) collective-permute-start(bf16[4,2,80,256]{3,2,1,0:T(8,128)(2,1)S(1)} %pad_maximum_fusion.2.refs_0_), channel_id=1, source_target_pairs={{0,2},{1,3},{2,0},{3,1},{4,6},{5,7},{6,4},{7,5},{8,10},{9,11},{10,... | collective-permute-start | bytes 983048 | tf_op jit(solution)/shard_map/ppermute | solution.py:155
  67.0 3.9 %collective-permute-done.16.refs_1_ = bf16[4,2,80,256]{3,2,1,0:T(8,128)(2,1)S(1)} collective-permute-done((bf16[4,2,80,256]{3,2,1,0:T(8,128)(2,1)S(1)}, bf16[4,2,80,256]{3,2,1,0:T(8,128)(2,1)S(1)}, u32[]{:S(2)}, u32[]{:S(2)}) %collective-permute-start.16) | collective-permute-done | bytes 327712 | tf_op jit(solution)/shard_map/ppermute | solution.py:155
  70.9 0.5 collective-permute-start.20
  71.4 0.0 collective-permute-done.19.refs_1_
  71.4 0.5 collective-permute-start.23
  71.9 3.6 %collective-permute-done.22.refs_1_ = bf16[4,2,80,256]{3,2,1,0:T(8,128)(2,1)S(1)} collective-permute-done((bf16[4,2,80,256]{3,2,1,0:T(8,128)(2,1)S(1)}, bf16[4,2,80,256]{3,2,1,0:T(8,128)(2,1)S(1)}, u32[]{:S(2)}, u32[]{:S(2)}) %collective-permute-start.22) | collective-permute-done | bytes 327712 | tf_op jit(solution)/shard_map/ppermute | solution.py:155
  75.5 1.9 %chain0.1.start = f32[8,2048]{1,0:T(8,128)S(1)} custom-call(s32[6]{0:T(128)S(1)} %copy-done.3, f32[32,4,128]{2,1,0:T(4,128)S(1)} %all-to-all-done.1.start, bf16[4,2,80,256]{3,2,1,0:T(8,128)(2,1)S(1)} %pad_maximum_fusion.refs_0_, bf16[4,2,80,256]{3,2,1,0:T(8,128)(2,1)S(1)} %collective-permute-done.16.refs_1_, ...), custom_call_target="tpu_custom_call" | custom-call | tf_op jit(solution)/shard_map/chain0/pallas_call | solution.py:275
  77.4 1.9 %chain1.1.start = f32[8,2048]{1,0:T(8,128)S(1)} custom-call(s32[6]{0:T(128)S(1)} %copy-done.3, f32[8,2048]{1,0:T(8,128)S(1)} %chain0.1.start, bf16[4,2,80,256]{3,2,1,0:T(8,128)(2,1)S(1)} %pad_maximum_fusion.1.refs_0_, bf16[4,2,80,256]{3,2,1,0:T(8,128)(2,1)S(1)} %collective-permute-done.19.refs_1_, ...), custom_call_target="tpu_custom_call" | custom-call | tf_op jit(solution)/shard_map/chain1/pallas_call | solution.py:275
  79.3 2.5 %chain2.1 = bf16[4,2048]{1,0:T(4,128)(2,1)} custom-call(s32[6]{0:T(128)S(1)} %copy-done.3, f32[8,2048]{1,0:T(8,128)S(1)} %chain1.1.start, bf16[4,2,80,256]{3,2,1,0:T(8,128)(2,1)S(1)} %pad_maximum_fusion.2.refs_0_, bf16[4,2,80,256]{3,2,1,0:T(8,128)(2,1)S(1)} %collective-permute-done.22.refs_1_, bf16[4,2,80,256]{3,2,1,0:T(8,128)(2,1)S(1)} %collective-permute-done.23.refs_2_, ...), custom_call_target="tpu_custom_call" | custom-call | tf_op jit(solution)/shard_map/chain2/pallas_call | solution.py:275
  (40 shorter events, 0.3 us)
Async XLA Ops:
  0.0 7.9 %collective-permute-start = (bf16[64,512]{1,0:T(8,128)(2,1)}, bf16[64,512]{1,0:T(8,128)(2,1)S(1)}, u32[]{:S(2)}, u32[]{:S(2)}) collective-permute-start(bf16[64,512]{1,0:T(8,128)(2,1)} %param.7), channel_id=1, source_target_pairs={{0,8},{1,9},{2,10},{3,11},{4,12},{5,13},{6,14},{7,15},{8,0},{9,1},... | collective-permute-start | bytes 196616 | tf_op jit(solution)/shard_map/ppermute | solution.py:155
  4.0 1.0 %copy-start.1 = (bf16[1,1024,256]{2,1,0:T(8,128)(2,1)S(1)}, bf16[1,1024,256]{2,1,0:T(8,128)(2,1)}, u32[]{:S(2)}) copy-start(bf16[1,1024,256]{2,1,0:T(8,128)(2,1)} %param.8) | copy-start | bytes 1572868
  5.1 0.9 %copy-start.2 = (bf16[1,256,256]{2,1,0:T(8,128)(2,1)S(1)}, bf16[1,256,256]{2,1,0:T(8,128)(2,1)}, u32[]{:S(2)}) copy-start(bf16[1,256,256]{2,1,0:T(8,128)(2,1)} %param.9) | copy-start | bytes 393220
  7.9 3.6 %copy-start.5 = (bf16[64,512]{1,0:T(8,128)(2,1)S(1)}, bf16[64,512]{1,0:T(8,128)(2,1)}, u32[]{:S(2)}) copy-start(bf16[64,512]{1,0:T(8,128)(2,1)} %param.7) | copy-start | bytes 196612
  7.9 12.4 %all-to-all-start = ((bf16[8,80,256]{2,1,0:T(8,128)(2,1)}), bf16[8,80,256]{2,1,0:T(8,128)(2,1)S(1)}, u32[]{:S(2)}, u32[]{:S(2)}) async-start(bf16[8,80,256]{2,1,0:T(8,128)(2,1)} %pack.1), calls=%async_computation | async-start | bytes 655360 | tf_op jit(solution)/shard_map/all_to_all | solution.py:179
  11.5 4.4 %collective-permute-start.2 = (bf16[64,512]{1,0:T(8,128)(2,1)S(1)}, bf16[64,512]{1,0:T(8,128)(2,1)S(1)}, u32[]{:S(2)}, u32[]{:S(2)}) collective-permute-start(bf16[64,512]{1,0:T(8,128)(2,1)S(1)} %get-tuple-element.43), channel_id=1, source_target_pairs={{0,16},{16,0},{1,17},{17,1},{2,18},{18,2},{3,19},{19,3},{4,20},{20... | collective-permute-start | bytes 196616 | tf_op jit(solution)/shard_map/ppermute | solution.py:158
  13.3 6.2 %collective-permute-start.1 = (bf16[1,64,512]{2,1,0:T(8,128)(2,1)S(1)}, bf16[1,64,512]{2,1,0:T(8,128)(2,1)S(1)}, u32[]{:S(2)}, u32[]{:S(2)}) collective-permute-start(bf16[1,64,512]{2,1,0:T(8,128)(2,1)S(1)} %get-tuple-element.44), channel_id=1, source_target_pairs={{0,2},{1,3},{2,0},{3,1},{4,6},{5,7},{6,4},{7,5},{8,10},{9,11},{10,... | collective-permute-start | bytes 196616 | tf_op jit(solution)/shard_map/ppermute | solution.py:155
  16.0 4.3 %collective-permute-start.3 = (bf16[1,64,512]{2,1,0:T(8,128)(2,1)S(1)}, bf16[1,64,512]{2,1,0:T(8,128)(2,1)S(1)}, u32[]{:S(2)}, u32[]{:S(2)}) collective-permute-start(bf16[1,64,512]{2,1,0:T(8,128)(2,1)S(1)} %bitcast.8), channel_id=1, source_target_pairs={{0,4},{1,5},{2,6},{3,7},{4,0},{5,1},{6,2},{7,3},{8,12},{9,13},{10,... | collective-permute-start | bytes 196616 | tf_op jit(solution)/shard_map/ppermute | solution.py:155
  19.5 0.7 copy-start.4
  20.2 15.7 %copy-start = (bf16[4096,128]{1,0:T(8,128)(2,1)S(1)}, bf16[4096,128]{1,0:T(8,128)(2,1)}, u32[]{:S(2)}) copy-start(bf16[4096,128]{1,0:T(8,128)(2,1)} %sub.6) | copy-start | bytes 3145732
  21.0 5.1 %collective-permute-start.4 = (bf16[1,80,256]{2,1,0:T(8,128)(2,1)S(1)}, bf16[1,80,256]{2,1,0:T(8,128)(2,1)S(1)}, u32[]{:S(2)}, u32[]{:S(2)}) collective-permute-start(bf16[1,80,256]{2,1,0:T(8,128)(2,1)S(1)} %slice.6), channel_id=1, source_target_pairs={{0,8},{1,9},{2,10},{3,11},{4,12},{5,13},{6,14},{7,15},{8,0},{9,1},... | collective-permute-start | bytes 122888 | tf_op jit(solution)/shard_map/ppermute | solution.py:155
  26.1 5.0 %collective-permute-start.6 = (bf16[2,64,512]{2,1,0:T(8,128)(2,1)S(1)}, bf16[2,64,512]{2,1,0:T(8,128)(2,1)S(1)}, u32[]{:S(2)}, u32[]{:S(2)}) collective-permute-start(bf16[2,64,512]{2,1,0:T(8,128)(2,1)S(1)} %pad_maximum_fusion.6), channel_id=1, source_target_pairs={{0,4},{1,5},{2,6},{3,7},{4,0},{5,1},{6,2},{7,3},{8,12},{9,13},{10,... | collective-permute-start | bytes 393224 | tf_op jit(solution)/shard_map/ppermute | solution.py:155
  27.8 5.0 %collective-permute-start.7 = (bf16[2,64,512]{2,1,0:T(8,128)(2,1)S(1)}, bf16[2,64,512]{2,1,0:T(8,128)(2,1)S(1)}, u32[]{:S(2)}, u32[]{:S(2)}) collective-permute-start(bf16[2,64,512]{2,1,0:T(8,128)(2,1)S(1)} %pad_maximum_fusion.7), channel_id=1, source_target_pairs={{0,2},{1,3},{2,0},{3,1},{4,6},{5,7},{6,4},{7,5},{8,10},{9,11},{10,... | collective-permute-start | bytes 393224 | tf_op jit(solution)/shard_map/ppermute | solution.py:155
  29.3 6.6 %collective-permute-start.8 = (bf16[4,64,512]{2,1,0:T(8,128)(2,1)S(1)}, bf16[4,64,512]{2,1,0:T(8,128)(2,1)S(1)}, u32[]{:S(2)}, u32[]{:S(2)}) collective-permute-start(bf16[4,64,512]{2,1,0:T(8,128)(2,1)S(1)} %constant_dynamic-update-slice_fusion.refs_0_), channel_id=1, source_target_pairs={{0,1},{1,0},{2,3},{3,2},{4,5},{5,4},{6,7},{7,6},{8,9},{9,8},{10,11... | collective-permute-start | bytes 786440 | tf_op jit(solution)/shard_map/ppermute | solution.py:155
  32.8 3.1 %collective-permute-start.9 = (bf16[4,64,512]{2,1,0:T(8,128)(2,1)S(1)}, bf16[4,64,512]{2,1,0:T(8,128)(2,1)S(1)}, u32[]{:S(2)}, u32[]{:S(2)}) collective-permute-start(bf16[4,64,512]{2,1,0:T(8,128)(2,1)S(1)} %constant_dynamic-update-slice_fusion.2.refs_1_), channel_id=1, source_target_pairs={{0,1},{1,0},{2,3},{3,2},{4,5},{5,4},{6,7},{7,6},{8,9},{9,8},{10,11... | collective-permute-start | bytes 786440 | tf_op jit(solution)/shard_map/ppermute | solution.py:155
  32.9 11.0 %collective-permute-start.5 = (bf16[4,80,256]{2,1,0:T(8,128)(2,1)S(1)}, bf16[4,80,256]{2,1,0:T(8,128)(2,1)S(1)}, u32[]{:S(2)}, u32[]{:S(2)}) collective-permute-start(bf16[4,80,256]{2,1,0:T(8,128)(2,1)S(1)} %slice.7), channel_id=1, source_target_pairs={{0,8},{1,9},{2,10},{3,11},{4,12},{5,13},{6,14},{7,15},{8,0},{9,1},... | collective-permute-start | bytes 491528 | tf_op jit(solution)/shard_map/ppermute | solution.py:155
  44.6 9.3 %collective-permute-start.10 = (bf16[1,2,80,256]{3,2,1,0:T(8,128)(2,1)S(1)}, bf16[1,2,80,256]{3,2,1,0:T(8,128)(2,1)S(1)}, u32[]{:S(2)}, u32[]{:S(2)}) collective-permute-start(bf16[1,2,80,256]{3,2,1,0:T(8,128)(2,1)S(1)} %get-tuple-element.35), channel_id=1, source_target_pairs={{0,16},{16,0},{1,17},{17,1},{2,18},{18,2},{3,19},{19,3},{4,20},{20... | collective-permute-start | bytes 245768 | tf_op jit(solution)/shard_map/ppermute | solution.py:158
  46.2 17.4 %all-to-all-start.1 = ((f32[32,4,128]{2,1,0:T(4,128)}), f32[32,4,128]{2,1,0:T(4,128)S(1)}, u32[]{:S(2)}, u32[]{:S(2)}) async-start(f32[32,4,128]{2,1,0:T(4,128)} %bitcast.4), calls=%async_computation.1 | async-start | bytes 131072 | tf_op jit(solution)/shard_map/all_to_all | solution.py:237
  50.6 5.0 %collective-permute-start.12 = (bf16[1,2,80,256]{3,2,1,0:T(8,128)(2,1)S(1)}, bf16[1,2,80,256]{3,2,1,0:T(8,128)(2,1)S(1)}, u32[]{:S(2)}, u32[]{:S(2)}) collective-permute-start(bf16[1,2,80,256]{3,2,1,0:T(8,128)(2,1)S(1)} %get-tuple-element.36), channel_id=1, source_target_pairs={{0,2},{1,3},{2,0},{3,1},{4,6},{5,7},{6,4},{7,5},{8,10},{9,11},{10,... | collective-permute-start | bytes 245768 | tf_op jit(solution)/shard_map/ppermute | solution.py:155
  52.5 5.7 %collective-permute-start.14 = (bf16[1,2,80,256]{3,2,1,0:T(8,128)(2,1)S(1)}, bf16[1,2,80,256]{3,2,1,0:T(8,128)(2,1)S(1)}, u32[]{:S(2)}, u32[]{:S(2)}) collective-permute-start(bf16[1,2,80,256]{3,2,1,0:T(8,128)(2,1)S(1)} %get-tuple-element.37), channel_id=1, source_target_pairs={{0,4},{1,5},{2,6},{3,7},{4,0},{5,1},{6,2},{7,3},{8,12},{9,13},{10,... | collective-permute-start | bytes 245768 | tf_op jit(solution)/shard_map/ppermute | solution.py:155
  53.9 6.0 %collective-permute-start.11 = (bf16[2,2,80,256]{3,2,1,0:T(8,128)(2,1)S(1)}, bf16[2,2,80,256]{3,2,1,0:T(8,128)(2,1)S(1)}, u32[]{:S(2)}, u32[]{:S(2)}) collective-permute-start(bf16[2,2,80,256]{3,2,1,0:T(8,128)(2,1)S(1)} %pad_maximum_fusion.3), channel_id=1, source_target_pairs={{0,2},{1,3},{2,0},{3,1},{4,6},{5,7},{6,4},{7,5},{8,10},{9,11},{10,... | collective-permute-start | bytes 491528 | tf_op jit(solution)/shard_map/ppermute | solution.py:155
  55.6 5.9 %collective-permute-start.13 = (bf16[2,2,80,256]{3,2,1,0:T(8,128)(2,1)S(1)}, bf16[2,2,80,256]{3,2,1,0:T(8,128)(2,1)S(1)}, u32[]{:S(2)}, u32[]{:S(2)}) collective-permute-start(bf16[2,2,80,256]{3,2,1,0:T(8,128)(2,1)S(1)} %pad_maximum_fusion.4), channel_id=1, source_target_pairs={{0,4},{1,5},{2,6},{3,7},{4,0},{5,1},{6,2},{7,3},{8,12},{9,13},{10,... | collective-permute-start | bytes 491528 | tf_op jit(solution)/shard_map/ppermute | solution.py:155
  58.2 5.4 %collective-permute-start.15 = (bf16[2,2,80,256]{3,2,1,0:T(8,128)(2,1)S(1)}, bf16[2,2,80,256]{3,2,1,0:T(8,128)(2,1)S(1)}, u32[]{:S(2)}, u32[]{:S(2)}) collective-permute-start(bf16[2,2,80,256]{3,2,1,0:T(8,128)(2,1)S(1)} %pad_maximum_fusion.5), channel_id=1, source_target_pairs={{0,16},{16,0},{1,17},{17,1},{2,18},{18,2},{3,19},{19,3},{4,20},{20... | collective-permute-start | bytes 491528 | tf_op jit(solution)/shard_map/ppermute | solution.py:158
  61.5 14.0 %copy-start.3 = (s32[6]{0:T(128)S(1)}, s32[6]{0:T(128)}, u32[]{:S(2)}) copy-start(s32[6]{0:T(128)} %offsets.5) | copy-start | bytes 76
  63.6 7.2 %collective-permute-start.16 = (bf16[4,2,80,256]{3,2,1,0:T(8,128)(2,1)S(1)}, bf16[4,2,80,256]{3,2,1,0:T(8,128)(2,1)S(1)}, u32[]{:S(2)}, u32[]{:S(2)}) collective-permute-start(bf16[4,2,80,256]{3,2,1,0:T(8,128)(2,1)S(1)} %pad_maximum_fusion.refs_0_), channel_id=1, source_target_pairs={{0,4},{1,5},{2,6},{3,7},{4,0},{5,1},{6,2},{7,3},{8,12},{9,13},{10,... | collective-permute-start | bytes 983048 | tf_op jit(solution)/shard_map/ppermute | solution.py:155
  63.9 7.5 %collective-permute-start.19 = (bf16[4,2,80,256]{3,2,1,0:T(8,128)(2,1)S(1)}, bf16[4,2,80,256]{3,2,1,0:T(8,128)(2,1)S(1)}, u32[]{:S(2)}, u32[]{:S(2)}) collective-permute-start(bf16[4,2,80,256]{3,2,1,0:T(8,128)(2,1)S(1)} %pad_maximum_fusion.1.refs_0_), channel_id=1, source_target_pairs={{0,16},{16,0},{1,17},{17,1},{2,18},{18,2},{3,19},{19,3},{4,20},{20... | collective-permute-start | bytes 983048 | tf_op jit(solution)/shard_map/ppermute | solution.py:158
  65.3 6.0 %collective-permute-start.17 = (bf16[4,2,80,256]{3,2,1,0:T(8,128)(2,1)S(1)}, bf16[4,2,80,256]{3,2,1,0:T(8,128)(2,1)S(1)}, u32[]{:S(2)}, u32[]{:S(2)}) collective-permute-start(bf16[4,2,80,256]{3,2,1,0:T(8,128)(2,1)S(1)} %pad_maximum_fusion.refs_0_), channel_id=1, source_target_pairs={{0,1},{1,0},{2,3},{3,2},{4,5},{5,4},{6,7},{7,6},{8,9},{9,8},{10,11... | collective-permute-start | bytes 983048 | tf_op jit(solution)/shard_map/ppermute | solution.py:155
  65.3 10.1 %collective-permute-start.22 = (bf16[4,2,80,256]{3,2,1,0:T(8,128)(2,1)S(1)}, bf16[4,2,80,256]{3,2,1,0:T(8,128)(2,1)S(1)}, u32[]{:S(2)}, u32[]{:S(2)}) collective-permute-start(bf16[4,2,80,256]{3,2,1,0:T(8,128)(2,1)S(1)} %pad_maximum_fusion.2.refs_0_), channel_id=1, source_target_pairs={{0,2},{1,3},{2,0},{3,1},{4,6},{5,7},{6,4},{7,5},{8,10},{9,11},{10,... | collective-permute-start | bytes 983048 | tf_op jit(solution)/shard_map/ppermute | solution.py:155
  70.9 4.6 %collective-permute-start.18 = (bf16[4,2,80,256]{3,2,1,0:T(8,128)(2,1)S(1)}, bf16[4,2,80,256]{3,2,1,0:T(8,128)(2,1)S(1)}, u32[]{:S(2)}, u32[]{:S(2)}) collective-permute-start(bf16[4,2,80,256]{3,2,1,0:T(8,128)(2,1)S(1)} %collective-permute-done.16.refs_1_), channel_id=1, source_target_pairs={{0,1},{1,0},{2,3},{3,2},{4,5},{5,4},{6,7},{7,6},{8,9},{9,8},{10,11... | collective-permute-start | bytes 983048 | tf_op jit(solution)/shard_map/ppermute | solution.py:155
  70.9 6.5 %collective-permute-start.20 = (bf16[4,2,80,256]{3,2,1,0:T(8,128)(2,1)S(1)}, bf16[4,2,80,256]{3,2,1,0:T(8,128)(2,1)S(1)}, u32[]{:S(2)}, u32[]{:S(2)}) collective-permute-start(bf16[4,2,80,256]{3,2,1,0:T(8,128)(2,1)S(1)} %pad_maximum_fusion.1.refs_0_), channel_id=1, source_target_pairs={{0,1},{1,0},{2,3},{3,2},{4,5},{5,4},{6,7},{7,6},{8,9},{9,8},{10,11... | collective-permute-start | bytes 983048 | tf_op jit(solution)/shard_map/ppermute | solution.py:155
  71.4 6.0 %collective-permute-start.21 = (bf16[4,2,80,256]{3,2,1,0:T(8,128)(2,1)S(1)}, bf16[4,2,80,256]{3,2,1,0:T(8,128)(2,1)S(1)}, u32[]{:S(2)}, u32[]{:S(2)}) collective-permute-start(bf16[4,2,80,256]{3,2,1,0:T(8,128)(2,1)S(1)} %collective-permute-done.19.refs_1_), channel_id=1, source_target_pairs={{0,1},{1,0},{2,3},{3,2},{4,5},{5,4},{6,7},{7,6},{8,9},{9,8},{10,11... | collective-permute-start | bytes 983048 | tf_op jit(solution)/shard_map/ppermute | solution.py:155
  71.4 7.9 %collective-permute-start.23 = (bf16[4,2,80,256]{3,2,1,0:T(8,128)(2,1)S(1)}, bf16[4,2,80,256]{3,2,1,0:T(8,128)(2,1)S(1)}, u32[]{:S(2)}, u32[]{:S(2)}) collective-permute-start(bf16[4,2,80,256]{3,2,1,0:T(8,128)(2,1)S(1)} %pad_maximum_fusion.2.refs_0_), channel_id=1, source_target_pairs={{0,1},{1,0},{2,3},{3,2},{4,5},{5,4},{6,7},{7,6},{8,9},{9,8},{10,11... | collective-permute-start | bytes 983048 | tf_op jit(solution)/shard_map/ppermute | solution.py:155
  75.5 3.8 %collective-permute-start.24 = (bf16[4,2,80,256]{3,2,1,0:T(8,128)(2,1)S(1)}, bf16[4,2,80,256]{3,2,1,0:T(8,128)(2,1)S(1)}, u32[]{:S(2)}, u32[]{:S(2)}) collective-permute-start(bf16[4,2,80,256]{3,2,1,0:T(8,128)(2,1)S(1)} %collective-permute-done.22.refs_1_), channel_id=1, source_target_pairs={{0,1},{1,0},{2,3},{3,2},{4,5},{5,4},{6,7},{7,6},{8,9},{9,8},{10,11... | collective-permute-start | bytes 983048 | tf_op jit(solution)/shard_map/ppermute | solution.py:155

commit v12 on v10

--- a/solution.py
+++ b/solution.py
@@ -18,6 +18,11 @@
 
 def limit(mib):
     return pltpu.CompilerParams(vmem_limit_bytes=mib * 1024 * 1024)
+
+
+def cost(arrays, flops=0):
+    size = sum(a.size * a.dtype.itemsize for a in arrays)
+    return pl.CostEstimate(flops=flops, bytes_accessed=size, transcendentals=0)
 
 
 def slice_index():
@@ -170,20 +175,11 @@
         out_specs=VMEM,
         scratch_shapes=[pltpu.SemaphoreType.DMA((2,))],
         compiler_params=limit(2),
+        cost_estimate=cost([basis, factor]),
         name="pack",
     )(basis.reshape(SLICES, pv, reflect), factor.reshape(SLICES, pt, reflect))
-    packed, across = lax.optimization_barrier((packed, across))
     members = [[h * HALF + c for c in range(HALF)] for h in range(halves)]
     slices = lax.all_to_all(packed, "col", 0, 0, axis_index_groups=members)
-
-    picked = pl.pallas_call(
-        pick_kernel,
-        out_shape=jax.ShapeDtypeStruct((GROUPS - 1,) + piece, dtype),
-        in_specs=[SMEM, VMEM],
-        out_specs=VMEM,
-        compiler_params=limit(4),
-        name="pick",
-    )(owners, slices)
 
     row, top = lax.axis_index("row"), lax.axis_index("col") // share
 
@@ -210,7 +206,17 @@
         bit //= 2
     double(0, 2)
     double(1, 4)
-    picked, sides = lax.optimization_barrier((picked, sides))
+    slices, sides = lax.optimization_barrier((slices, sides))
+
+    picked = pl.pallas_call(
+        pick_kernel,
+        out_shape=jax.ShapeDtypeStruct((GROUPS - 1,) + piece, dtype),
+        in_specs=[SMEM, VMEM],
+        out_specs=VMEM,
+        compiler_params=limit(4),
+        cost_estimate=cost([slices]),
+        name="pick",
+    )(owners, slices)
     others = [over_col(picked, m * HALF) for m in range(1, halves)]
     late = jnp.concatenate([over_col(sides[0], 4), over_col(sides[1], 2)])
     late_tags = [(m, c ^ 4) for m, c in tags[0]] + [(m, c ^ 2) for m, c in tags[1]]
@@ -226,11 +232,9 @@
         in_specs=[VMEM] + [VMEM] * len(m_held),
         out_specs=VMEM,
         compiler_params=limit(8),
+        cost_estimate=cost([sub_vectors], 2 * wanted * sub_vectors.size),
         name="merge",
     )(sub_vectors, *m_held)
-    others, merged = lax.optimization_barrier((others, merged))
-    state = lax.all_to_all(merged.reshape(rows * cols, each, width), ("row", "col"), 0, 0)
-
     per = GROUPS // COLOURS
     colours = pl.pallas_call(
         order_kernel,
@@ -238,6 +242,7 @@
         in_specs=[SMEM, VMEM] + [VMEM] * len(others),
         out_specs=[VMEM] * COLOURS,
         compiler_params=limit(4),
+        cost_estimate=cost([slices]),
         name="order",
     )(owners, slices, *others)
     colours = list(colours)
@@ -253,13 +258,15 @@
             colours[k] = jnp.concatenate([colours[k], send(colours[k])])
             masks[k] = masks[k] + [m ^ mask for m in masks[k]]
         if step == 0:
-            colours, state = lax.optimization_barrier((colours, state))
+            colours, merged = lax.optimization_barrier((colours, merged))
+    state = lax.all_to_all(merged.reshape(rows * cols, each, width), ("row", "col"), 0, 0)
     last_round = []
     for k in range(COLOURS):
         mask, send = links[(k + 2) % 3]
         last_round.append(send(colours[k]))
         masks[k] = [masks[k], [m ^ mask for m in masks[k]]]
         masks[k] += [[m ^ 1 for m in ms] for ms in masks[k]]
+    last_round, state = lax.optimization_barrier((last_round, state))
     held = []
     for k in range(COLOURS):
         held.append([colours[k], last_round[k], over_col(colours[k], 1), over_col(last_round[k], 1)])
@@ -280,6 +287,7 @@
                 pltpu.VMEM((per, reflect, reflect), dtype),
             ],
             compiler_params=limit(12),
+            cost_estimate=cost(held[k], 2 * per * 64 * group_rows * reflect),
             name=f"chain{k}",
         )(offsets, state, *held[k])
     return state

time: 79.8 us -> 70.1 us (0.88)
  waiting for transfers between devices: 35.5 us -> 20.4 us
  blocking collectives: 0 us -> 10 us
  starting transfers between devices: 32 us -> 28.1 us
    all_to_all x0 -> x1, blocking collectives: none -> 10 us  [local(): lax.all_to_all(merged.reshape(rows * cols, each, width), ('row', 'col'),...]
    ppermute x20, waiting for transfers between devices: 27.1 us -> 17.8 us  [over_col(): return lax.ppermute(x, 'col', [(c, c ^ mask) for c in range(cols)])]
    all_to_all x1 -> x0, waiting for transfers between devices: 6.49 us -> none  [local(): lax.all_to_all(merged.reshape(rows * cols, each, width), ('row', 'col'),...]
    all_to_all x1 -> x0, starting transfers between devices: 3.53 us -> none  [local(): lax.all_to_all(merged.reshape(rows * cols, each, width), ('row', 'col'),...]
    ppermute x20, starting transfers between devices: 20.2 us -> 18.4 us  [over_col(): return lax.ppermute(x, 'col', [(c, c ^ mask) for c in range(cols)])]
    ppermute x4, starting transfers between devices: 4.71 us -> 5.66 us  [over_row(): return lax.ppermute(x, 'row', [(r, r ^ mask) for r in range(rows)])]
  transfers between devices with their start and end apart: 26 -> 25, of which waited for: 12 -> 12; matrix products, arithmetic and copies ran while one was open for 0% -> 0% of each run, Pallas kernels for 7% -> 8%
where the time goes in v12:
time: 70.1 us; the launch traced here: 69.7 us
  starting transfers between devices  28.1 us (40%)
  waiting for transfers between devices  20.4 us (29%)
  blocking collectives  10 us (14%)
  Pallas kernels  8.81 us (13%)
  local copies, waits for them, and re-layouts  2.08 us (3%)
    ppermute x20, starting transfers between devices, over_col(): return lax.ppermute(x, 'col', [(c, c ^ mask) for c in range(cols)])  18.4 us
    ppermute x20, waiting for transfers between devices, over_col(): return lax.ppermute(x, 'col', [(c, c ^ mask) for c in range(cols)])  17.8 us
    all_to_all x1, blocking collectives, local(): lax.all_to_all(merged.reshape(rows * cols, each, width), ('row', 'col'),...  10 us
    pallas_call x3, Pallas kernels, local(): pl.pallas_call(functools.partial(chain_kernel, cols, groups, masks[k], fi...  6.28 us
    ppermute x4, starting transfers between devices, over_row(): return lax.ppermute(x, 'row', [(r, r ^ mask) for r in range(rows)])  5.66 us
    all_to_all x1, starting transfers between devices, local(): slices = lax.all_to_all(packed, 'col', 0, 0, axis_index_groups=members)  3.95 us
    ppermute x4, waiting for transfers between devices, over_row(): return lax.ppermute(x, 'row', [(r, r ^ mask) for r in range(rows)])  2.56 us
    unnamed x17, local copies, waits for them, and re-layouts  2.02 us
  transfers between devices with their start and end apart: 25, of which 12 were waited for; matrix products, arithmetic and copies ran while one was open for 0% of the time, Pallas kernels for 8%

profile of v12, /device:TPU:0, one launch (start us, length us, event | category | flops | bytes accessed | tf_op | source)
XLA Modules:
  0.0 69.7 jit_solution(13734530667432517868)
XLA Ops:
  0.0 4.0 %collective-permute-start = (bf16[64,512]{1,0:T(8,128)(2,1)}, bf16[64,512]{1,0:T(8,128)(2,1)S(1)}, u32[]{:S(2)}, u32[]{:S(2)}) collective-permute-start(bf16[64,512]{1,0:T(8,128)(2,1)} %param.7), channel_id=1, source_target_pairs={{0,8},{1,9},{2,10},{3,11},{4,12},{5,13},{6,14},{7,15},{8,0},{9,1},... | collective-permute-start | bytes 196616 | tf_op jit(solution)/shard_map/ppermute | solution.py:158
  4.0 1.0 %copy-done.1 = bf16[1,1024,256]{2,1,0:T(8,128)(2,1)S(1)} copy-done((bf16[1,1024,256]{2,1,0:T(8,128)(2,1)S(1)}, bf16[1,1024,256]{2,1,0:T(8,128)(2,1)}, u32[]{:S(2)}) %copy-start.1) | copy-done | bytes 524312
  5.1 0.9 %copy-done.2 = bf16[1,256,256]{2,1,0:T(8,128)(2,1)S(1)} copy-done((bf16[1,256,256]{2,1,0:T(8,128)(2,1)S(1)}, bf16[1,256,256]{2,1,0:T(8,128)(2,1)}, u32[]{:S(2)}) %copy-start.2) | copy-done | bytes 131096
  6.0 0.8 %pack.1 = bf16[8,80,256]{2,1,0:T(8,128)(2,1)} custom-call(bf16[16,64,256]{2,1,0:T(8,128)(2,1)S(1)} %bitcast.6, bf16[16,16,256]{2,1,0:T(8,128)(2,1)S(1)} %bitcast.8), custom_call_target="tpu_custom_call" | custom-call | bytes 655360 | tf_op jit(solution)/shard_map/pack/pallas_call | solution.py:171
  6.8 4.0 %all-to-all-start = ((bf16[8,80,256]{2,1,0:T(8,128)(2,1)}), bf16[8,80,256]{2,1,0:T(8,128)(2,1)S(1)}, u32[]{:S(2)}, u32[]{:S(2)}) async-start(bf16[8,80,256]{2,1,0:T(8,128)(2,1)} %pack.1), calls=%async_computation | async-start | bytes 655360 | tf_op jit(solution)/shard_map/all_to_all | solution.py:182
  10.8 1.6 %collective-permute-start.2 = (bf16[64,512]{1,0:T(8,128)(2,1)S(1)}, bf16[64,512]{1,0:T(8,128)(2,1)S(1)}, u32[]{:S(2)}, u32[]{:S(2)}) collective-permute-start(bf16[64,512]{1,0:T(8,128)(2,1)S(1)} %get-tuple-element.33), channel_id=1, source_target_pairs={{0,16},{16,0},{1,17},{17,1},{2,18},{18,2},{3,19},{19,3},{4,20},{20... | collective-permute-start | bytes 196616 | tf_op jit(solution)/shard_map/ppermute | solution.py:161
  12.3 2.0 %collective-permute-start.1 = (bf16[1,64,512]{2,1,0:T(8,128)(2,1)S(1)}, bf16[1,64,512]{2,1,0:T(8,128)(2,1)S(1)}, u32[]{:S(2)}, u32[]{:S(2)}) collective-permute-start(bf16[1,64,512]{2,1,0:T(8,128)(2,1)S(1)} %get-tuple-element.34), channel_id=1, source_target_pairs={{0,2},{1,3},{2,0},{3,1},{4,6},{5,7},{6,4},{7,5},{8,10},{9,11},{10,... | collective-permute-start | bytes 196616 | tf_op jit(solution)/shard_map/ppermute | solution.py:158
  14.3 1.0 %collective-permute-done.2 = bf16[64,512]{1,0:T(8,128)(2,1)S(1)} collective-permute-done((bf16[64,512]{1,0:T(8,128)(2,1)S(1)}, bf16[64,512]{1,0:T(8,128)(2,1)S(1)}, u32[]{:S(2)}, u32[]{:S(2)}) %collective-permute-start.2) | collective-permute-done | bytes 65568 | tf_op jit(solution)/shard_map/ppermute | solution.py:161
  15.3 1.8 %collective-permute-start.3 = (bf16[1,64,512]{2,1,0:T(8,128)(2,1)S(1)}, bf16[1,64,512]{2,1,0:T(8,128)(2,1)S(1)}, u32[]{:S(2)}, u32[]{:S(2)}) collective-permute-start(bf16[1,64,512]{2,1,0:T(8,128)(2,1)S(1)} %bitcast.9), channel_id=1, source_target_pairs={{0,4},{1,5},{2,6},{3,7},{4,0},{5,1},{6,2},{7,3},{8,12},{9,13},{10,... | collective-permute-start | bytes 196616 | tf_op jit(solution)/shard_map/ppermute | solution.py:158
  17.1 1.8 %collective-permute-done.1 = bf16[1,64,512]{2,1,0:T(8,128)(2,1)S(1)} collective-permute-done((bf16[1,64,512]{2,1,0:T(8,128)(2,1)S(1)}, bf16[1,64,512]{2,1,0:T(8,128)(2,1)S(1)}, u32[]{:S(2)}, u32[]{:S(2)}) %collective-permute-start.1) | collective-permute-done | bytes 65568 | tf_op jit(solution)/shard_map/ppermute | solution.py:158
  18.9 0.7 %collective-permute-done.3 = bf16[1,64,512]{2,1,0:T(8,128)(2,1)S(1)} collective-permute-done((bf16[1,64,512]{2,1,0:T(8,128)(2,1)S(1)}, bf16[1,64,512]{2,1,0:T(8,128)(2,1)S(1)}, u32[]{:S(2)}, u32[]{:S(2)}) %collective-permute-start.3) | collective-permute-done | bytes 65568 | tf_op jit(solution)/shard_map/ppermute | solution.py:158
  19.6 0.0 copy-start.4
  19.6 1.9 %collective-permute-start.8 = (bf16[2,64,512]{2,1,0:T(8,128)(2,1)S(1)}, bf16[2,64,512]{2,1,0:T(8,128)(2,1)S(1)}, u32[]{:S(2)}, u32[]{:S(2)}) collective-permute-start(bf16[2,64,512]{2,1,0:T(8,128)(2,1)S(1)} %pad_maximum_fusion.3), channel_id=1, source_target_pairs={{0,4},{1,5},{2,6},{3,7},{4,0},{5,1},{6,2},{7,3},{8,12},{9,13},{10,... | collective-permute-start | bytes 393224 | tf_op jit(solution)/shard_map/ppermute | solution.py:158
  21.5 1.5 %collective-permute-start.9 = (bf16[2,64,512]{2,1,0:T(8,128)(2,1)S(1)}, bf16[2,64,512]{2,1,0:T(8,128)(2,1)S(1)}, u32[]{:S(2)}, u32[]{:S(2)}) collective-permute-start(bf16[2,64,512]{2,1,0:T(8,128)(2,1)S(1)} %pad_maximum_fusion.4), channel_id=1, source_target_pairs={{0,2},{1,3},{2,0},{3,1},{4,6},{5,7},{6,4},{7,5},{8,10},{9,11},{10,... | collective-permute-start | bytes 393224 | tf_op jit(solution)/shard_map/ppermute | solution.py:158
  23.0 0.7 %pick.1 = bf16[5,80,256]{2,1,0:T(8,128)(2,1)S(1)} custom-call(s32[6]{0:T(128)S(1)} %copy-done.4, bf16[8,80,256]{2,1,0:T(8,128)(2,1)S(1)} %all-to-all-done.held), custom_call_target="tpu_custom_call" | custom-call | bytes 327680 | tf_op jit(solution)/shard_map/pick/pallas_call | solution.py:211
  23.7 0.4 collective-permute-start.4
  24.2 0.1 collective-permute-start.10
  24.3 1.1 %collective-permute-done.8 = bf16[2,64,512]{2,1,0:T(8,128)(2,1)S(1)} collective-permute-done((bf16[2,64,512]{2,1,0:T(8,128)(2,1)S(1)}, bf16[2,64,512]{2,1,0:T(8,128)(2,1)S(1)}, u32[]{:S(2)}, u32[]{:S(2)}) %collective-permute-start.8) | collective-permute-done | bytes 131104 | tf_op jit(solution)/shard_map/ppermute | solution.py:158
  25.3 8.3 %collective-permute-done.4.refs_0_ = bf16[5,80,256]{2,1,0:T(8,128)(2,1)S(1)} collective-permute-done((bf16[5,80,256]{2,1,0:T(8,128)(2,1)S(1)}, bf16[5,80,256]{2,1,0:T(8,128)(2,1)S(1)}, u32[]{:S(2)}, u32[]{:S(2)}) %collective-permute-start.4) | collective-permute-done | bytes 204832 | tf_op jit(solution)/shard_map/ppermute | solution.py:158
  33.7 0.6 order.1
  34.3 0.1 collective-permute-start.7
  34.4 0.1 collective-permute-start.11
  34.5 1.1 %collective-permute-start.6 = (bf16[1,2,80,256]{3,2,1,0:T(8,128)(2,1)S(1)}, bf16[1,2,80,256]{3,2,1,0:T(8,128)(2,1)S(1)}, u32[]{:S(2)}, u32[]{:S(2)}) collective-permute-start(bf16[1,2,80,256]{3,2,1,0:T(8,128)(2,1)S(1)} %get-tuple-element.21), channel_id=1, source_target_pairs={{0,2},{1,3},{2,0},{3,1},{4,6},{5,7},{6,4},{7,5},{8,10},{9,11},{10,... | collective-permute-start | bytes 245768 | tf_op jit(solution)/shard_map/ppermute | solution.py:158
  35.6 1.5 %collective-permute-start.5 = (bf16[1,2,80,256]{3,2,1,0:T(8,128)(2,1)S(1)}, bf16[1,2,80,256]{3,2,1,0:T(8,128)(2,1)S(1)}, u32[]{:S(2)}, u32[]{:S(2)}) collective-permute-start(bf16[1,2,80,256]{3,2,1,0:T(8,128)(2,1)S(1)} %get-tuple-element.20), channel_id=1, source_target_pairs={{0,16},{16,0},{1,17},{17,1},{2,18},{18,2},{3,19},{19,3},{4,20},{20... | collective-permute-start | bytes 245768 | tf_op jit(solution)/shard_map/ppermute | solution.py:161
  37.1 1.7 %collective-permute-done.7 = bf16[1,2,80,256]{3,2,1,0:T(8,128)(2,1)S(1)} collective-permute-done((bf16[1,2,80,256]{3,2,1,0:T(8,128)(2,1)S(1)}, bf16[1,2,80,256]{3,2,1,0:T(8,128)(2,1)S(1)}, u32[]{:S(2)}, u32[]{:S(2)}) %collective-permute-start.7) | collective-permute-done | bytes 81952 | tf_op jit(solution)/shard_map/ppermute | solution.py:158
  38.8 0.5 collective-permute-done.6
  39.3 0.8 %collective-permute-done.5 = bf16[1,2,80,256]{3,2,1,0:T(8,128)(2,1)S(1)} collective-permute-done((bf16[1,2,80,256]{3,2,1,0:T(8,128)(2,1)S(1)}, bf16[1,2,80,256]{3,2,1,0:T(8,128)(2,1)S(1)}, u32[]{:S(2)}, u32[]{:S(2)}) %collective-permute-start.5) | collective-permute-done | bytes 81952 | tf_op jit(solution)/shard_map/ppermute | solution.py:161
  40.2 0.4 merge.1
  40.6 1.6 %collective-permute-start.16 = (bf16[2,2,80,256]{3,2,1,0:T(8,128)(2,1)S(1)}, bf16[2,2,80,256]{3,2,1,0:T(8,128)(2,1)S(1)}, u32[]{:S(2)}, u32[]{:S(2)}) collective-permute-start(bf16[2,2,80,256]{3,2,1,0:T(8,128)(2,1)S(1)} %pad_maximum_fusion.2), channel_id=1, source_target_pairs={{0,16},{16,0},{1,17},{17,1},{2,18},{18,2},{3,19},{19,3},{4,20},{20... | collective-permute-start | bytes 491528 | tf_op jit(solution)/shard_map/ppermute | solution.py:161
  42.2 2.1 %collective-permute-start.14 = (bf16[2,2,80,256]{3,2,1,0:T(8,128)(2,1)S(1)}, bf16[2,2,80,256]{3,2,1,0:T(8,128)(2,1)S(1)}, u32[]{:S(2)}, u32[]{:S(2)}) collective-permute-start(bf16[2,2,80,256]{3,2,1,0:T(8,128)(2,1)S(1)} %pad_maximum_fusion.1), channel_id=1, source_target_pairs={{0,4},{1,5},{2,6},{3,7},{4,0},{5,1},{6,2},{7,3},{8,12},{9,13},{10,... | collective-permute-start | bytes 491528 | tf_op jit(solution)/shard_map/ppermute | solution.py:158
  44.3 1.0 %collective-permute-start.12 = (bf16[2,2,80,256]{3,2,1,0:T(8,128)(2,1)S(1)}, bf16[2,2,80,256]{3,2,1,0:T(8,128)(2,1)S(1)}, u32[]{:S(2)}, u32[]{:S(2)}) collective-permute-start(bf16[2,2,80,256]{3,2,1,0:T(8,128)(2,1)S(1)} %pad_maximum_fusion), channel_id=1, source_target_pairs={{0,2},{1,3},{2,0},{3,1},{4,6},{5,7},{6,4},{7,5},{8,10},{9,11},{10,... | collective-permute-start | bytes 491528 | tf_op jit(solution)/shard_map/ppermute | solution.py:158
  45.3 0.8 %collective-permute-done.16 = bf16[2,2,80,256]{3,2,1,0:T(8,128)(2,1)S(1)} collective-permute-done((bf16[2,2,80,256]{3,2,1,0:T(8,128)(2,1)S(1)}, bf16[2,2,80,256]{3,2,1,0:T(8,128)(2,1)S(1)}, u32[]{:S(2)}, u32[]{:S(2)}) %collective-permute-start.16) | collective-permute-done | bytes 163872 | tf_op jit(solution)/shard_map/ppermute | solution.py:161
  46.1 1.0 %collective-permute-start.17 = (bf16[4,2,80,256]{3,2,1,0:T(8,128)(2,1)S(1)}, bf16[4,2,80,256]{3,2,1,0:T(8,128)(2,1)S(1)}, u32[]{:S(2)}, u32[]{:S(2)}) collective-permute-start(bf16[4,2,80,256]{3,2,1,0:T(8,128)(2,1)S(1)} %constant_dynamic-update-slice_fusion.8.refs_0_), channel_id=1, source_target_pairs={{0,2},{1,3},{2,0},{3,1},{4,6},{5,7},{6,4},{7,5},{8,10},{9,11},{10,... | collective-permute-start | bytes 983048 | tf_op jit(solution)/shard_map/ppermute | solution.py:158
  47.2 0.5 collective-permute-done.14
  47.7 1.1 %collective-permute-start.15 = (bf16[4,2,80,256]{3,2,1,0:T(8,128)(2,1)S(1)}, bf16[4,2,80,256]{3,2,1,0:T(8,128)(2,1)S(1)}, u32[]{:S(2)}, u32[]{:S(2)}) collective-permute-start(bf16[4,2,80,256]{3,2,1,0:T(8,128)(2,1)S(1)} %constant_dynamic-update-slice_fusion.6.refs_0_), channel_id=1, source_target_pairs={{0,16},{16,0},{1,17},{17,1},{2,18},{18,2},{3,19},{19,3},{4,20},{20... | collective-permute-start | bytes 983048 | tf_op jit(solution)/shard_map/ppermute | solution.py:161
  48.8 2.7 %collective-permute-done.12 = bf16[2,2,80,256]{3,2,1,0:T(8,128)(2,1)S(1)} collective-permute-done((bf16[2,2,80,256]{3,2,1,0:T(8,128)(2,1)S(1)}, bf16[2,2,80,256]{3,2,1,0:T(8,128)(2,1)S(1)}, u32[]{:S(2)}, u32[]{:S(2)}) %collective-permute-start.12) | collective-permute-done | bytes 163872 | tf_op jit(solution)/shard_map/ppermute | solution.py:158
  51.5 0.1 collective-permute-start.13
  51.6 0.1 collective-permute-start.18
  51.7 10.0 %all_to_all.10.start = f32[32,4,128]{2,1,0:T(4,128)S(1)} all-to-all(f32[32,4,128]{2,1,0:T(4,128)S(1)} %bitcast.7), channel_id=1, replica_groups=mesh['row'=2,'col'=16] {'row','col'}, dimensions={0} | all-to-all | bytes 131072 | tf_op jit(solution)/shard_map/all_to_all | solution.py:262
  61.7 0.2 collective-permute-start.19
  61.9 0.4 collective-permute-start.20
  62.3 0.1 collective-permute-start.21
  62.4 0.4 collective-permute-start.22
  62.8 0.1 collective-permute-start.23
  62.9 0.5 collective-permute-done.19.refs_3_
  63.4 1.9 %chain0.1.start = f32[8,2048]{1,0:T(8,128)S(1)} custom-call(s32[6]{0:T(128)S(1)} %copy-done.3, f32[32,4,128]{2,1,0:T(4,128)S(1)} %all_to_all.10.start, bf16[4,2,80,256]{3,2,1,0:T(8,128)(2,1)S(1)} %constant_dynamic-update-slice_fusion.4.refs_0_, bf16[4,2,80,256]{3,2,1,0:T(8,128)(2,1)S(1)} %collective-permute-done.13.refs_1_, ...), custom_call_target="tpu_custom_call" | custom-call | flops 67108864 | bytes 1310720 | tf_op jit(solution)/shard_map/chain0/pallas_call | solution.py:278
  65.3 1.9 %chain1.1.start = f32[8,2048]{1,0:T(8,128)S(1)} custom-call(s32[6]{0:T(128)S(1)} %copy-done.3, f32[8,2048]{1,0:T(8,128)S(1)} %chain0.1.start, bf16[4,2,80,256]{3,2,1,0:T(8,128)(2,1)S(1)} %constant_dynamic-update-slice_fusion.6.refs_0_, bf16[4,2,80,256]{3,2,1,0:T(8,128)(2,1)S(1)} %collective-permute-done.15.refs_1_, ...), custom_call_target="tpu_custom_call" | custom-call | flops 67108864 | bytes 1310720 | tf_op jit(solution)/shard_map/chain1/pallas_call | solution.py:278
  67.2 2.5 %chain2.1 = bf16[4,2048]{1,0:T(4,128)(2,1)} custom-call(s32[6]{0:T(128)S(1)} %copy-done.3, f32[8,2048]{1,0:T(8,128)S(1)} %chain1.1.start, bf16[4,2,80,256]{3,2,1,0:T(8,128)(2,1)S(1)} %constant_dynamic-update-slice_fusion.8.refs_0_, bf16[4,2,80,256]{3,2,1,0:T(8,128)(2,1)S(1)} %collective-permute-done.17.refs_1_, ...), custom_call_target="tpu_custom_call" | custom-call | flops 67108864 | bytes 1310720 | tf_op jit(solution)/shard_map/chain2/pallas_call | solution.py:278
  (38 shorter events, 0.3 us)
Async XLA Ops:
  0.0 10.7 %collective-permute-start = (bf16[64,512]{1,0:T(8,128)(2,1)}, bf16[64,512]{1,0:T(8,128)(2,1)S(1)}, u32[]{:S(2)}, u32[]{:S(2)}) collective-permute-start(bf16[64,512]{1,0:T(8,128)(2,1)} %param.7), channel_id=1, source_target_pairs={{0,8},{1,9},{2,10},{3,11},{4,12},{5,13},{6,14},{7,15},{8,0},{9,1},... | collective-permute-start | bytes 196616 | tf_op jit(solution)/shard_map/ppermute | solution.py:158
  4.0 1.0 %copy-start.1 = (bf16[1,1024,256]{2,1,0:T(8,128)(2,1)S(1)}, bf16[1,1024,256]{2,1,0:T(8,128)(2,1)}, u32[]{:S(2)}) copy-start(bf16[1,1024,256]{2,1,0:T(8,128)(2,1)} %param.8) | copy-start | bytes 1572868
  5.1 0.9 %copy-start.2 = (bf16[1,256,256]{2,1,0:T(8,128)(2,1)S(1)}, bf16[1,256,256]{2,1,0:T(8,128)(2,1)}, u32[]{:S(2)}) copy-start(bf16[1,256,256]{2,1,0:T(8,128)(2,1)} %param.9) | copy-start | bytes 393220
  6.8 4.0 %copy-start.5 = (bf16[64,512]{1,0:T(8,128)(2,1)S(1)}, bf16[64,512]{1,0:T(8,128)(2,1)}, u32[]{:S(2)}) copy-start(bf16[64,512]{1,0:T(8,128)(2,1)} %param.7) | copy-start | bytes 196612
  6.8 12.9 %all-to-all-start = ((bf16[8,80,256]{2,1,0:T(8,128)(2,1)}), bf16[8,80,256]{2,1,0:T(8,128)(2,1)S(1)}, u32[]{:S(2)}, u32[]{:S(2)}) async-start(bf16[8,80,256]{2,1,0:T(8,128)(2,1)} %pack.1), calls=%async_computation | async-start | bytes 655360 | tf_op jit(solution)/shard_map/all_to_all | solution.py:182
  10.8 4.6 %collective-permute-start.2 = (bf16[64,512]{1,0:T(8,128)(2,1)S(1)}, bf16[64,512]{1,0:T(8,128)(2,1)S(1)}, u32[]{:S(2)}, u32[]{:S(2)}) collective-permute-start(bf16[64,512]{1,0:T(8,128)(2,1)S(1)} %get-tuple-element.33), channel_id=1, source_target_pairs={{0,16},{16,0},{1,17},{17,1},{2,18},{18,2},{3,19},{19,3},{4,20},{20... | collective-permute-start | bytes 196616 | tf_op jit(solution)/shard_map/ppermute | solution.py:161
  12.3 6.5 %collective-permute-start.1 = (bf16[1,64,512]{2,1,0:T(8,128)(2,1)S(1)}, bf16[1,64,512]{2,1,0:T(8,128)(2,1)S(1)}, u32[]{:S(2)}, u32[]{:S(2)}) collective-permute-start(bf16[1,64,512]{2,1,0:T(8,128)(2,1)S(1)} %get-tuple-element.34), channel_id=1, source_target_pairs={{0,2},{1,3},{2,0},{3,1},{4,6},{5,7},{6,4},{7,5},{8,10},{9,11},{10,... | collective-permute-start | bytes 196616 | tf_op jit(solution)/shard_map/ppermute | solution.py:158
  15.3 4.3 %collective-permute-start.3 = (bf16[1,64,512]{2,1,0:T(8,128)(2,1)S(1)}, bf16[1,64,512]{2,1,0:T(8,128)(2,1)S(1)}, u32[]{:S(2)}, u32[]{:S(2)}) collective-permute-start(bf16[1,64,512]{2,1,0:T(8,128)(2,1)S(1)} %bitcast.9), channel_id=1, source_target_pairs={{0,4},{1,5},{2,6},{3,7},{4,0},{5,1},{6,2},{7,3},{8,12},{9,13},{10,... | collective-permute-start | bytes 196616 | tf_op jit(solution)/shard_map/ppermute | solution.py:158
  19.6 3.4 %copy-start.4 = (s32[6]{0:T(128)S(1)}, s32[6]{0:T(128)}, u32[]{:S(2)}) copy-start(s32[6]{0:T(128)} %owners.3) | copy-start | bytes 76
  19.6 5.7 %collective-permute-start.8 = (bf16[2,64,512]{2,1,0:T(8,128)(2,1)S(1)}, bf16[2,64,512]{2,1,0:T(8,128)(2,1)S(1)}, u32[]{:S(2)}, u32[]{:S(2)}) collective-permute-start(bf16[2,64,512]{2,1,0:T(8,128)(2,1)S(1)} %pad_maximum_fusion.3), channel_id=1, source_target_pairs={{0,4},{1,5},{2,6},{3,7},{4,0},{5,1},{6,2},{7,3},{8,12},{9,13},{10,... | collective-permute-start | bytes 393224 | tf_op jit(solution)/shard_map/ppermute | solution.py:158
  21.5 12.9 %collective-permute-start.9 = (bf16[2,64,512]{2,1,0:T(8,128)(2,1)S(1)}, bf16[2,64,512]{2,1,0:T(8,128)(2,1)S(1)}, u32[]{:S(2)}, u32[]{:S(2)}) collective-permute-start(bf16[2,64,512]{2,1,0:T(8,128)(2,1)S(1)} %pad_maximum_fusion.4), channel_id=1, source_target_pairs={{0,2},{1,3},{2,0},{3,1},{4,6},{5,7},{6,4},{7,5},{8,10},{9,11},{10,... | collective-permute-start | bytes 393224 | tf_op jit(solution)/shard_map/ppermute | solution.py:158
  23.7 9.9 %collective-permute-start.4 = (bf16[5,80,256]{2,1,0:T(8,128)(2,1)S(1)}, bf16[5,80,256]{2,1,0:T(8,128)(2,1)S(1)}, u32[]{:S(2)}, u32[]{:S(2)}) collective-permute-start(bf16[5,80,256]{2,1,0:T(8,128)(2,1)S(1)} %pick.1), channel_id=1, source_target_pairs={{0,8},{1,9},{2,10},{3,11},{4,12},{5,13},{6,14},{7,15},{8,0},{9,1},... | collective-permute-start | bytes 614408 | tf_op jit(solution)/shard_map/ppermute | solution.py:158
  24.2 16.0 %copy-start = (bf16[4096,128]{1,0:T(8,128)(2,1)S(1)}, bf16[4096,128]{1,0:T(8,128)(2,1)}, u32[]{:S(2)}) copy-start(bf16[4096,128]{1,0:T(8,128)(2,1)} %sub.6) | copy-start | bytes 3145732
  24.2 15.9 %collective-permute-start.10 = (bf16[4,64,512]{2,1,0:T(8,128)(2,1)S(1)}, bf16[4,64,512]{2,1,0:T(8,128)(2,1)S(1)}, u32[]{:S(2)}, u32[]{:S(2)}) collective-permute-start(bf16[4,64,512]{2,1,0:T(8,128)(2,1)S(1)} %constant_dynamic-update-slice_fusion.refs_0_), channel_id=1, source_target_pairs={{0,1},{1,0},{2,3},{3,2},{4,5},{5,4},{6,7},{7,6},{8,9},{9,8},{10,11... | collective-permute-start | bytes 786440 | tf_op jit(solution)/shard_map/ppermute | solution.py:158
  34.3 4.5 %collective-permute-start.7 = (bf16[1,2,80,256]{3,2,1,0:T(8,128)(2,1)S(1)}, bf16[1,2,80,256]{3,2,1,0:T(8,128)(2,1)S(1)}, u32[]{:S(2)}, u32[]{:S(2)}) collective-permute-start(bf16[1,2,80,256]{3,2,1,0:T(8,128)(2,1)S(1)} %get-tuple-element.22), channel_id=1, source_target_pairs={{0,4},{1,5},{2,6},{3,7},{4,0},{5,1},{6,2},{7,3},{8,12},{9,13},{10,... | collective-permute-start | bytes 245768 | tf_op jit(solution)/shard_map/ppermute | solution.py:158
  34.4 5.7 %collective-permute-start.11 = (bf16[4,64,512]{2,1,0:T(8,128)(2,1)S(1)}, bf16[4,64,512]{2,1,0:T(8,128)(2,1)S(1)}, u32[]{:S(2)}, u32[]{:S(2)}) collective-permute-start(bf16[4,64,512]{2,1,0:T(8,128)(2,1)S(1)} %constant_dynamic-update-slice_fusion.2.refs_1_), channel_id=1, source_target_pairs={{0,1},{1,0},{2,3},{3,2},{4,5},{5,4},{6,7},{7,6},{8,9},{9,8},{10,11... | collective-permute-start | bytes 786440 | tf_op jit(solution)/shard_map/ppermute | solution.py:158
  34.5 4.9 %collective-permute-start.6 = (bf16[1,2,80,256]{3,2,1,0:T(8,128)(2,1)S(1)}, bf16[1,2,80,256]{3,2,1,0:T(8,128)(2,1)S(1)}, u32[]{:S(2)}, u32[]{:S(2)}) collective-permute-start(bf16[1,2,80,256]{3,2,1,0:T(8,128)(2,1)S(1)} %get-tuple-element.21), channel_id=1, source_target_pairs={{0,2},{1,3},{2,0},{3,1},{4,6},{5,7},{6,4},{7,5},{8,10},{9,11},{10,... | collective-permute-start | bytes 245768 | tf_op jit(solution)/shard_map/ppermute | solution.py:158
  35.6 4.5 %collective-permute-start.5 = (bf16[1,2,80,256]{3,2,1,0:T(8,128)(2,1)S(1)}, bf16[1,2,80,256]{3,2,1,0:T(8,128)(2,1)S(1)}, u32[]{:S(2)}, u32[]{:S(2)}) collective-permute-start(bf16[1,2,80,256]{3,2,1,0:T(8,128)(2,1)S(1)} %get-tuple-element.20), channel_id=1, source_target_pairs={{0,16},{16,0},{1,17},{17,1},{2,18},{18,2},{3,19},{19,3},{4,20},{20... | collective-permute-start | bytes 245768 | tf_op jit(solution)/shard_map/ppermute | solution.py:161
  40.6 5.5 %collective-permute-start.16 = (bf16[2,2,80,256]{3,2,1,0:T(8,128)(2,1)S(1)}, bf16[2,2,80,256]{3,2,1,0:T(8,128)(2,1)S(1)}, u32[]{:S(2)}, u32[]{:S(2)}) collective-permute-start(bf16[2,2,80,256]{3,2,1,0:T(8,128)(2,1)S(1)} %pad_maximum_fusion.2), channel_id=1, source_target_pairs={{0,16},{16,0},{1,17},{17,1},{2,18},{18,2},{3,19},{19,3},{4,20},{20... | collective-permute-start | bytes 491528 | tf_op jit(solution)/shard_map/ppermute | solution.py:161
  42.2 5.5 %collective-permute-start.14 = (bf16[2,2,80,256]{3,2,1,0:T(8,128)(2,1)S(1)}, bf16[2,2,80,256]{3,2,1,0:T(8,128)(2,1)S(1)}, u32[]{:S(2)}, u32[]{:S(2)}) collective-permute-start(bf16[2,2,80,256]{3,2,1,0:T(8,128)(2,1)S(1)} %pad_maximum_fusion.1), channel_id=1, source_target_pairs={{0,4},{1,5},{2,6},{3,7},{4,0},{5,1},{6,2},{7,3},{8,12},{9,13},{10,... | collective-permute-start | bytes 491528 | tf_op jit(solution)/shard_map/ppermute | solution.py:158
  44.3 7.2 %collective-permute-start.12 = (bf16[2,2,80,256]{3,2,1,0:T(8,128)(2,1)S(1)}, bf16[2,2,80,256]{3,2,1,0:T(8,128)(2,1)S(1)}, u32[]{:S(2)}, u32[]{:S(2)}) collective-permute-start(bf16[2,2,80,256]{3,2,1,0:T(8,128)(2,1)S(1)} %pad_maximum_fusion), channel_id=1, source_target_pairs={{0,2},{1,3},{2,0},{3,1},{4,6},{5,7},{6,4},{7,5},{8,10},{9,11},{10,... | collective-permute-start | bytes 491528 | tf_op jit(solution)/shard_map/ppermute | solution.py:158
  46.1 15.5 %collective-permute-start.17 = (bf16[4,2,80,256]{3,2,1,0:T(8,128)(2,1)S(1)}, bf16[4,2,80,256]{3,2,1,0:T(8,128)(2,1)S(1)}, u32[]{:S(2)}, u32[]{:S(2)}) collective-permute-start(bf16[4,2,80,256]{3,2,1,0:T(8,128)(2,1)S(1)} %constant_dynamic-update-slice_fusion.8.refs_0_), channel_id=1, source_target_pairs={{0,2},{1,3},{2,0},{3,1},{4,6},{5,7},{6,4},{7,5},{8,10},{9,11},{10,... | collective-permute-start | bytes 983048 | tf_op jit(solution)/shard_map/ppermute | solution.py:158
  47.7 14.0 %collective-permute-start.15 = (bf16[4,2,80,256]{3,2,1,0:T(8,128)(2,1)S(1)}, bf16[4,2,80,256]{3,2,1,0:T(8,128)(2,1)S(1)}, u32[]{:S(2)}, u32[]{:S(2)}) collective-permute-start(bf16[4,2,80,256]{3,2,1,0:T(8,128)(2,1)S(1)} %constant_dynamic-update-slice_fusion.6.refs_0_), channel_id=1, source_target_pairs={{0,16},{16,0},{1,17},{17,1},{2,18},{18,2},{3,19},{19,3},{4,20},{20... | collective-permute-start | bytes 983048 | tf_op jit(solution)/shard_map/ppermute | solution.py:161
  51.5 10.2 %collective-permute-start.13 = (bf16[4,2,80,256]{3,2,1,0:T(8,128)(2,1)S(1)}, bf16[4,2,80,256]{3,2,1,0:T(8,128)(2,1)S(1)}, u32[]{:S(2)}, u32[]{:S(2)}) collective-permute-start(bf16[4,2,80,256]{3,2,1,0:T(8,128)(2,1)S(1)} %constant_dynamic-update-slice_fusion.4.refs_0_), channel_id=1, source_target_pairs={{0,4},{1,5},{2,6},{3,7},{4,0},{5,1},{6,2},{7,3},{8,12},{9,13},{10,... | collective-permute-start | bytes 983048 | tf_op jit(solution)/shard_map/ppermute | solution.py:158
  51.6 11.2 %collective-permute-start.18 = (bf16[4,2,80,256]{3,2,1,0:T(8,128)(2,1)S(1)}, bf16[4,2,80,256]{3,2,1,0:T(8,128)(2,1)S(1)}, u32[]{:S(2)}, u32[]{:S(2)}) collective-permute-start(bf16[4,2,80,256]{3,2,1,0:T(8,128)(2,1)S(1)} %constant_dynamic-update-slice_fusion.4.refs_0_), channel_id=1, source_target_pairs={{0,1},{1,0},{2,3},{3,2},{4,5},{5,4},{6,7},{7,6},{8,9},{9,8},{10,11... | collective-permute-start | bytes 983048 | tf_op jit(solution)/shard_map/ppermute | solution.py:158
  51.7 11.7 %copy-start.3 = (s32[6]{0:T(128)S(1)}, s32[6]{0:T(128)}, u32[]{:S(2)}) copy-start(s32[6]{0:T(128)} %offsets.5) | copy-start | bytes 76
  61.7 1.7 %collective-permute-start.19 = (bf16[4,2,80,256]{3,2,1,0:T(8,128)(2,1)S(1)}, bf16[4,2,80,256]{3,2,1,0:T(8,128)(2,1)S(1)}, u32[]{:S(2)}, u32[]{:S(2)}) collective-permute-start(bf16[4,2,80,256]{3,2,1,0:T(8,128)(2,1)S(1)} %collective-permute-done.13.refs_1_), channel_id=1, source_target_pairs={{0,1},{1,0},{2,3},{3,2},{4,5},{5,4},{6,7},{7,6},{8,9},{9,8},{10,11... | collective-permute-start | bytes 983048 | tf_op jit(solution)/shard_map/ppermute | solution.py:158
  61.9 3.4 %collective-permute-start.20 = (bf16[4,2,80,256]{3,2,1,0:T(8,128)(2,1)S(1)}, bf16[4,2,80,256]{3,2,1,0:T(8,128)(2,1)S(1)}, u32[]{:S(2)}, u32[]{:S(2)}) collective-permute-start(bf16[4,2,80,256]{3,2,1,0:T(8,128)(2,1)S(1)} %constant_dynamic-update-slice_fusion.6.refs_0_), channel_id=1, source_target_pairs={{0,1},{1,0},{2,3},{3,2},{4,5},{5,4},{6,7},{7,6},{8,9},{9,8},{10,11... | collective-permute-start | bytes 983048 | tf_op jit(solution)/shard_map/ppermute | solution.py:158
  62.3 3.0 %collective-permute-start.21 = (bf16[4,2,80,256]{3,2,1,0:T(8,128)(2,1)S(1)}, bf16[4,2,80,256]{3,2,1,0:T(8,128)(2,1)S(1)}, u32[]{:S(2)}, u32[]{:S(2)}) collective-permute-start(bf16[4,2,80,256]{3,2,1,0:T(8,128)(2,1)S(1)} %collective-permute-done.15.refs_1_), channel_id=1, source_target_pairs={{0,1},{1,0},{2,3},{3,2},{4,5},{5,4},{6,7},{7,6},{8,9},{9,8},{10,11... | collective-permute-start | bytes 983048 | tf_op jit(solution)/shard_map/ppermute | solution.py:158
  62.4 4.8 %collective-permute-start.22 = (bf16[4,2,80,256]{3,2,1,0:T(8,128)(2,1)S(1)}, bf16[4,2,80,256]{3,2,1,0:T(8,128)(2,1)S(1)}, u32[]{:S(2)}, u32[]{:S(2)}) collective-permute-start(bf16[4,2,80,256]{3,2,1,0:T(8,128)(2,1)S(1)} %constant_dynamic-update-slice_fusion.8.refs_0_), channel_id=1, source_target_pairs={{0,1},{1,0},{2,3},{3,2},{4,5},{5,4},{6,7},{7,6},{8,9},{9,8},{10,11... | collective-permute-start | bytes 983048 | tf_op jit(solution)/shard_map/ppermute | solution.py:158
  62.8 4.4 %collective-permute-start.23 = (bf16[4,2,80,256]{3,2,1,0:T(8,128)(2,1)S(1)}, bf16[4,2,80,256]{3,2,1,0:T(8,128)(2,1)S(1)}, u32[]{:S(2)}, u32[]{:S(2)}) collective-permute-start(bf16[4,2,80,256]{3,2,1,0:T(8,128)(2,1)S(1)} %collective-permute-done.17.refs_1_), channel_id=1, source_target_pairs={{0,1},{1,0},{2,3},{3,2},{4,5},{5,4},{6,7},{7,6},{8,9},{9,8},{10,11... | collective-permute-start | bytes 983048 | tf_op jit(solution)/shard_map/ppermute | solution.py:158

commit v13 on v12

--- a/solution.py
+++ b/solution.py
@@ -73,8 +73,10 @@
     for group in range(GROUPS):
         half, rank = places(owners, group)
         piece = held[lax.rem(owners[group], HALF)]
-        for mask, ref in enumerate(others, 1):
-            other = ref[jnp.minimum(rank, ref.shape[0] - 1)]
+        for mask in range(1, len(others) // 2 + 1):
+            head, tail = others[2 * mask - 2 : 2 * mask]
+            other = tail[jnp.clip(rank - 1, 0, tail.shape[0] - 1)]
+            other = jnp.where(rank == 0, head[0], other)
             piece = jnp.where(jnp.bitwise_xor(half, mine) == mask, other, piece)
         outs[group // each][0, group % each] = piece
 
@@ -174,7 +176,7 @@
         in_specs=[HBM, HBM],
         out_specs=VMEM,
         scratch_shapes=[pltpu.SemaphoreType.DMA((2,))],
-        compiler_params=limit(2),
+        compiler_params=limit(56),
         cost_estimate=cost([basis, factor]),
         name="pack",
     )(basis.reshape(SLICES, pv, reflect), factor.reshape(SLICES, pt, reflect))
@@ -217,7 +219,10 @@
         cost_estimate=cost([slices]),
         name="pick",
     )(owners, slices)
-    others = [over_col(picked, m * HALF) for m in range(1, halves)]
+    heads = [over_col(picked[:1], m * HALF) for m in range(1, halves)]
+    tails = [over_col(picked[1:], m * HALF) for m in range(1, halves)]
+    heads, sides = lax.optimization_barrier((heads, sides))
+    others = [x for pair in zip(heads, tails) for x in pair]
     late = jnp.concatenate([over_col(sides[0], 4), over_col(sides[1], 2)])
     late_tags = [(m, c ^ 4) for m, c in tags[0]] + [(m, c ^ 2) for m, c in tags[1]]
     m_held = [jnp.concatenate(sides), late]

time: 70.1 us -> 67.9 us (0.969)
  local copies, waits for them, and re-layouts: 2.08 us -> 0.15 us
  waiting for transfers between devices: 20.4 us -> 18.8 us
  Pallas kernels: 8.81 us -> 9.75 us
  blocking collectives: 10 us -> 10.8 us
    unnamed x17 -> x13, local copies, waits for them, and re-layouts: 2.02 us -> 0.08 us
    ppermute x20 -> x21, waiting for transfers between devices: 17.8 us -> 16.2 us  [over_col(): return lax.ppermute(x, 'col', [(c, c ^ mask) for c in range(cols)])]
    pallas_call x1, Pallas kernels: 0.77 us -> 1.69 us  [local(): pl.pallas_call(pack_kernel, out_shape=jax.ShapeDtypeStruct((HALF,) + piec...]
    all_to_all x1, blocking collectives: 10 us -> 10.8 us  [local(): lax.all_to_all(merged.reshape(rows * cols, each, width), ('row', 'col'),...]
    ppermute x20 -> x21, starting transfers between devices: 18.4 us -> 18.1 us  [over_col(): return lax.ppermute(x, 'col', [(c, c ^ mask) for c in range(cols)])]
  transfers between devices with their start and end apart: 25 -> 26, of which waited for: 12 -> 12; matrix products, arithmetic and copies ran while one was open for 0% -> 0% of each run, Pallas kernels for 8% -> 9%
where the time goes in v13:
time: 67.9 us; the launch traced here: 67.7 us
  starting transfers between devices  27.8 us (41%)
  waiting for transfers between devices  18.8 us (28%)
  blocking collectives  10.8 us (16%)
  Pallas kernels  9.75 us (14%)
    ppermute x21, starting transfers between devices, over_col(): return lax.ppermute(x, 'col', [(c, c ^ mask) for c in range(cols)])  18.1 us
    ppermute x21, waiting for transfers between devices, over_col(): return lax.ppermute(x, 'col', [(c, c ^ mask) for c in range(cols)])  16.2 us
    all_to_all x1, blocking collectives, local(): lax.all_to_all(merged.reshape(rows * cols, each, width), ('row', 'col'),...  10.8 us
    pallas_call x3, Pallas kernels, local(): pl.pallas_call(functools.partial(chain_kernel, cols, groups, masks[k], fi...  6.28 us
    ppermute x4, starting transfers between devices, over_row(): return lax.ppermute(x, 'row', [(r, r ^ mask) for r in range(rows)])  5.73 us
    all_to_all x1, starting transfers between devices, local(): slices = lax.all_to_all(packed, 'col', 0, 0, axis_index_groups=members)  3.95 us
    ppermute x4, waiting for transfers between devices, over_row(): return lax.ppermute(x, 'row', [(r, r ^ mask) for r in range(rows)])  2.6 us
    pallas_call x1, Pallas kernels, local(): pl.pallas_call(pack_kernel, out_shape=jax.ShapeDtypeStruct((HALF,) + piec...  1.69 us
  transfers between devices with their start and end apart: 26, of which 12 were waited for; matrix products, arithmetic and copies ran while one was open for 0% of the time, Pallas kernels for 9%

profile of v13, /device:TPU:0, one launch (start us, length us, event | category | flops | bytes accessed | tf_op | source)
XLA Modules:
  0.0 67.7 jit_solution(5331592952524773135)
XLA Ops:
  0.0 4.0 %collective-permute-start = (bf16[64,512]{1,0:T(8,128)(2,1)}, bf16[64,512]{1,0:T(8,128)(2,1)S(1)}, u32[]{:S(2)}, u32[]{:S(2)}) collective-permute-start(bf16[64,512]{1,0:T(8,128)(2,1)} %param.7), channel_id=1, source_target_pairs={{0,8},{1,9},{2,10},{3,11},{4,12},{5,13},{6,14},{7,15},{8,0},{9,1},... | collective-permute-start | bytes 196616 | tf_op jit(solution)/shard_map/ppermute | solution.py:160
  4.0 1.7 %pack.1 = bf16[8,80,256]{2,1,0:T(8,128)(2,1)} custom-call(bf16[16,64,256]{2,1,0:T(8,128)(2,1)} %bitcast.7, bf16[16,16,256]{2,1,0:T(8,128)(2,1)} %bitcast.8), custom_call_target="tpu_custom_call" | custom-call | bytes 655360 | tf_op jit(solution)/shard_map/pack/pallas_call | solution.py:173
  5.7 0.0 copy-start.3
  5.7 4.0 %all-to-all-start = ((bf16[8,80,256]{2,1,0:T(8,128)(2,1)}), bf16[8,80,256]{2,1,0:T(8,128)(2,1)S(1)}, u32[]{:S(2)}, u32[]{:S(2)}) async-start(bf16[8,80,256]{2,1,0:T(8,128)(2,1)} %pack.1), calls=%async_computation | async-start | bytes 655360 | tf_op jit(solution)/shard_map/all_to_all | solution.py:184
  9.7 1.6 %collective-permute-start.2 = (bf16[64,512]{1,0:T(8,128)(2,1)S(1)}, bf16[64,512]{1,0:T(8,128)(2,1)S(1)}, u32[]{:S(2)}, u32[]{:S(2)}) collective-permute-start(bf16[64,512]{1,0:T(8,128)(2,1)S(1)} %get-tuple-element.39), channel_id=1, source_target_pairs={{0,16},{16,0},{1,17},{17,1},{2,18},{18,2},{3,19},{19,3},{4,20},{20... | collective-permute-start | bytes 196616 | tf_op jit(solution)/shard_map/ppermute | solution.py:163
  11.3 2.0 %collective-permute-start.1 = (bf16[1,64,512]{2,1,0:T(8,128)(2,1)S(1)}, bf16[1,64,512]{2,1,0:T(8,128)(2,1)S(1)}, u32[]{:S(2)}, u32[]{:S(2)}) collective-permute-start(bf16[1,64,512]{2,1,0:T(8,128)(2,1)S(1)} %get-tuple-element.40), channel_id=1, source_target_pairs={{0,2},{1,3},{2,0},{3,1},{4,6},{5,7},{6,4},{7,5},{8,10},{9,11},{10,... | collective-permute-start | bytes 196616 | tf_op jit(solution)/shard_map/ppermute | solution.py:160
  13.3 1.0 %collective-permute-done.2 = bf16[64,512]{1,0:T(8,128)(2,1)S(1)} collective-permute-done((bf16[64,512]{1,0:T(8,128)(2,1)S(1)}, bf16[64,512]{1,0:T(8,128)(2,1)S(1)}, u32[]{:S(2)}, u32[]{:S(2)}) %collective-permute-start.2) | collective-permute-done | bytes 65568 | tf_op jit(solution)/shard_map/ppermute | solution.py:163
  14.3 1.8 %collective-permute-start.3 = (bf16[1,64,512]{2,1,0:T(8,128)(2,1)S(1)}, bf16[1,64,512]{2,1,0:T(8,128)(2,1)S(1)}, u32[]{:S(2)}, u32[]{:S(2)}) collective-permute-start(bf16[1,64,512]{2,1,0:T(8,128)(2,1)S(1)} %bitcast.9), channel_id=1, source_target_pairs={{0,4},{1,5},{2,6},{3,7},{4,0},{5,1},{6,2},{7,3},{8,12},{9,13},{10,... | collective-permute-start | bytes 196616 | tf_op jit(solution)/shard_map/ppermute | solution.py:160
  16.1 1.8 %collective-permute-done.1 = bf16[1,64,512]{2,1,0:T(8,128)(2,1)S(1)} collective-permute-done((bf16[1,64,512]{2,1,0:T(8,128)(2,1)S(1)}, bf16[1,64,512]{2,1,0:T(8,128)(2,1)S(1)}, u32[]{:S(2)}, u32[]{:S(2)}) %collective-permute-start.1) | collective-permute-done | bytes 65568 | tf_op jit(solution)/shard_map/ppermute | solution.py:160
  17.9 0.0 copy-start.2
  17.9 0.7 %collective-permute-done.3 = bf16[1,64,512]{2,1,0:T(8,128)(2,1)S(1)} collective-permute-done((bf16[1,64,512]{2,1,0:T(8,128)(2,1)S(1)}, bf16[1,64,512]{2,1,0:T(8,128)(2,1)S(1)}, u32[]{:S(2)}, u32[]{:S(2)}) %collective-permute-start.3) | collective-permute-done | bytes 65568 | tf_op jit(solution)/shard_map/ppermute | solution.py:160
  18.6 0.7 %pick.1 = bf16[5,80,256]{2,1,0:T(8,128)(2,1)S(1)} custom-call(s32[6]{0:T(128)S(1)} %copy-done.2, bf16[8,80,256]{2,1,0:T(8,128)(2,1)S(1)} %all-to-all-done.held), custom_call_target="tpu_custom_call" | custom-call | bytes 327680 | tf_op jit(solution)/shard_map/pick/pallas_call | solution.py:213
  19.3 0.4 collective-permute-start.4
  19.8 2.7 %collective-permute-start.5 = (bf16[4,80,256]{2,1,0:T(8,128)(2,1)S(1)}, bf16[4,80,256]{2,1,0:T(8,128)(2,1)S(1)}, u32[]{:S(2)}, u32[]{:S(2)}) collective-permute-start(bf16[4,80,256]{2,1,0:T(8,128)(2,1)S(1)} %slice.9), channel_id=1, source_target_pairs={{0,8},{1,9},{2,10},{3,11},{4,12},{5,13},{6,14},{7,15},{8,0},{9,1},... | collective-permute-start | bytes 491528 | tf_op jit(solution)/shard_map/ppermute | solution.py:160
  22.4 5.6 %collective-permute-done.4.refs_0_ = bf16[1,80,256]{2,1,0:T(8,128)(2,1)S(1)} collective-permute-done((bf16[1,80,256]{2,1,0:T(8,128)(2,1)S(1)}, bf16[1,80,256]{2,1,0:T(8,128)(2,1)S(1)}, u32[]{:S(2)}, u32[]{:S(2)}) %collective-permute-start.4) | collective-permute-done | bytes 40992 | tf_op jit(solution)/shard_map/ppermute | solution.py:160
  28.0 0.1 collective-permute-start.10
  28.1 0.0 copy-start
  28.2 0.1 collective-permute-start.11
  28.2 3.0 %collective-permute-done.5.refs_1_ = bf16[4,80,256]{2,1,0:T(8,128)(2,1)S(1)} collective-permute-done((bf16[4,80,256]{2,1,0:T(8,128)(2,1)S(1)}, bf16[4,80,256]{2,1,0:T(8,128)(2,1)S(1)}, u32[]{:S(2)}, u32[]{:S(2)}) %collective-permute-start.5) | collective-permute-done | bytes 163872 | tf_op jit(solution)/shard_map/ppermute | solution.py:160
  31.2 0.6 order.1
  31.9 0.1 collective-permute-start.8
  31.9 1.0 %collective-permute-start.7 = (bf16[1,2,80,256]{3,2,1,0:T(8,128)(2,1)S(1)}, bf16[1,2,80,256]{3,2,1,0:T(8,128)(2,1)S(1)}, u32[]{:S(2)}, u32[]{:S(2)}) collective-permute-start(bf16[1,2,80,256]{3,2,1,0:T(8,128)(2,1)S(1)} %get-tuple-element.27), channel_id=1, source_target_pairs={{0,2},{1,3},{2,0},{3,1},{4,6},{5,7},{6,4},{7,5},{8,10},{9,11},{10,... | collective-permute-start | bytes 245768 | tf_op jit(solution)/shard_map/ppermute | solution.py:160
  33.0 0.0 collective-permute-done.9
  33.0 1.5 %collective-permute-start.6 = (bf16[1,2,80,256]{3,2,1,0:T(8,128)(2,1)S(1)}, bf16[1,2,80,256]{3,2,1,0:T(8,128)(2,1)S(1)}, u32[]{:S(2)}, u32[]{:S(2)}) collective-permute-start(bf16[1,2,80,256]{3,2,1,0:T(8,128)(2,1)S(1)} %get-tuple-element.26), channel_id=1, source_target_pairs={{0,16},{16,0},{1,17},{17,1},{2,18},{18,2},{3,19},{19,3},{4,20},{20... | collective-permute-start | bytes 245768 | tf_op jit(solution)/shard_map/ppermute | solution.py:163
  34.5 0.1 collective-permute-start.12
  34.6 1.8 %collective-permute-done.8 = bf16[1,2,80,256]{3,2,1,0:T(8,128)(2,1)S(1)} collective-permute-done((bf16[1,2,80,256]{3,2,1,0:T(8,128)(2,1)S(1)}, bf16[1,2,80,256]{3,2,1,0:T(8,128)(2,1)S(1)}, u32[]{:S(2)}, u32[]{:S(2)}) %collective-permute-start.8) | collective-permute-done | bytes 81952 | tf_op jit(solution)/shard_map/ppermute | solution.py:160
  36.4 0.1 collective-permute-done.7
  36.5 1.0 %collective-permute-done.6 = bf16[1,2,80,256]{3,2,1,0:T(8,128)(2,1)S(1)} collective-permute-done((bf16[1,2,80,256]{3,2,1,0:T(8,128)(2,1)S(1)}, bf16[1,2,80,256]{3,2,1,0:T(8,128)(2,1)S(1)}, u32[]{:S(2)}, u32[]{:S(2)}) %collective-permute-start.6) | collective-permute-done | bytes 81952 | tf_op jit(solution)/shard_map/ppermute | solution.py:163
  37.5 0.4 merge.1
  37.9 1.6 %collective-permute-start.17 = (bf16[2,2,80,256]{3,2,1,0:T(8,128)(2,1)S(1)}, bf16[2,2,80,256]{3,2,1,0:T(8,128)(2,1)S(1)}, u32[]{:S(2)}, u32[]{:S(2)}) collective-permute-start(bf16[2,2,80,256]{3,2,1,0:T(8,128)(2,1)S(1)} %pad_maximum_fusion.2), channel_id=1, source_target_pairs={{0,16},{16,0},{1,17},{17,1},{2,18},{18,2},{3,19},{19,3},{4,20},{20... | collective-permute-start | bytes 491528 | tf_op jit(solution)/shard_map/ppermute | solution.py:163
  39.5 1.7 %collective-permute-start.15 = (bf16[2,2,80,256]{3,2,1,0:T(8,128)(2,1)S(1)}, bf16[2,2,80,256]{3,2,1,0:T(8,128)(2,1)S(1)}, u32[]{:S(2)}, u32[]{:S(2)}) collective-permute-start(bf16[2,2,80,256]{3,2,1,0:T(8,128)(2,1)S(1)} %pad_maximum_fusion.1), channel_id=1, source_target_pairs={{0,4},{1,5},{2,6},{3,7},{4,0},{5,1},{6,2},{7,3},{8,12},{9,13},{10,... | collective-permute-start | bytes 491528 | tf_op jit(solution)/shard_map/ppermute | solution.py:160
  41.3 1.4 %collective-permute-start.13 = (bf16[2,2,80,256]{3,2,1,0:T(8,128)(2,1)S(1)}, bf16[2,2,80,256]{3,2,1,0:T(8,128)(2,1)S(1)}, u32[]{:S(2)}, u32[]{:S(2)}) collective-permute-start(bf16[2,2,80,256]{3,2,1,0:T(8,128)(2,1)S(1)} %pad_maximum_fusion), channel_id=1, source_target_pairs={{0,2},{1,3},{2,0},{3,1},{4,6},{5,7},{6,4},{7,5},{8,10},{9,11},{10,... | collective-permute-start | bytes 491528 | tf_op jit(solution)/shard_map/ppermute | solution.py:160
  42.7 0.7 collective-permute-done.17
  43.3 1.1 %collective-permute-start.18 = (bf16[4,2,80,256]{3,2,1,0:T(8,128)(2,1)S(1)}, bf16[4,2,80,256]{3,2,1,0:T(8,128)(2,1)S(1)}, u32[]{:S(2)}, u32[]{:S(2)}) collective-permute-start(bf16[4,2,80,256]{3,2,1,0:T(8,128)(2,1)S(1)} %constant_dynamic-update-slice_fusion.8.refs_0_), channel_id=1, source_target_pairs={{0,2},{1,3},{2,0},{3,1},{4,6},{5,7},{6,4},{7,5},{8,10},{9,11},{10,... | collective-permute-start | bytes 983048 | tf_op jit(solution)/shard_map/ppermute | solution.py:160
  44.5 0.4 collective-permute-done.15
  44.9 1.1 %collective-permute-start.16 = (bf16[4,2,80,256]{3,2,1,0:T(8,128)(2,1)S(1)}, bf16[4,2,80,256]{3,2,1,0:T(8,128)(2,1)S(1)}, u32[]{:S(2)}, u32[]{:S(2)}) collective-permute-start(bf16[4,2,80,256]{3,2,1,0:T(8,128)(2,1)S(1)} %constant_dynamic-update-slice_fusion.6.refs_0_), channel_id=1, source_target_pairs={{0,16},{16,0},{1,17},{17,1},{2,18},{18,2},{3,19},{19,3},{4,20},{20... | collective-permute-start | bytes 983048 | tf_op jit(solution)/shard_map/ppermute | solution.py:163
  46.0 2.3 %collective-permute-done.13 = bf16[2,2,80,256]{3,2,1,0:T(8,128)(2,1)S(1)} collective-permute-done((bf16[2,2,80,256]{3,2,1,0:T(8,128)(2,1)S(1)}, bf16[2,2,80,256]{3,2,1,0:T(8,128)(2,1)S(1)}, u32[]{:S(2)}, u32[]{:S(2)}) %collective-permute-start.13) | collective-permute-done | bytes 163872 | tf_op jit(solution)/shard_map/ppermute | solution.py:160
  48.4 0.4 collective-permute-start.14
  48.8 10.8 %all_to_all.10.start = f32[32,4,128]{2,1,0:T(4,128)S(1)} all-to-all(f32[32,4,128]{2,1,0:T(4,128)S(1)} %bitcast.6), channel_id=1, replica_groups=mesh['row'=2,'col'=16] {'row','col'}, dimensions={0} | all-to-all | bytes 131072 | tf_op jit(solution)/shard_map/all_to_all | solution.py:267
  59.6 0.2 collective-permute-start.20
  59.8 0.4 collective-permute-start.21
  60.2 0.1 collective-permute-start.22
  60.3 0.4 collective-permute-start.23
  60.7 0.1 collective-permute-start.24
  60.8 0.5 collective-permute-done.20.refs_3_
  61.3 1.9 %chain0.1.start = f32[8,2048]{1,0:T(8,128)S(1)} custom-call(s32[6]{0:T(128)S(1)} %copy-done.1, f32[32,4,128]{2,1,0:T(4,128)S(1)} %all_to_all.10.start, bf16[4,2,80,256]{3,2,1,0:T(8,128)(2,1)S(1)} %constant_dynamic-update-slice_fusion.4.refs_0_, bf16[4,2,80,256]{3,2,1,0:T(8,128)(2,1)S(1)} %collective-permute-done.14.refs_1_, ...), custom_call_target="tpu_custom_call" | custom-call | flops 67108864 | bytes 1310720 | tf_op jit(solution)/shard_map/chain0/pallas_call | solution.py:283
  63.2 1.9 %chain1.1.start = f32[8,2048]{1,0:T(8,128)S(1)} custom-call(s32[6]{0:T(128)S(1)} %copy-done.1, f32[8,2048]{1,0:T(8,128)S(1)} %chain0.1.start, bf16[4,2,80,256]{3,2,1,0:T(8,128)(2,1)S(1)} %constant_dynamic-update-slice_fusion.6.refs_0_, bf16[4,2,80,256]{3,2,1,0:T(8,128)(2,1)S(1)} %collective-permute-done.16.refs_1_, ...), custom_call_target="tpu_custom_call" | custom-call | flops 67108864 | bytes 1310720 | tf_op jit(solution)/shard_map/chain1/pallas_call | solution.py:283
  65.2 2.5 %chain2.1 = bf16[4,2048]{1,0:T(4,128)(2,1)} custom-call(s32[6]{0:T(128)S(1)} %copy-done.1, f32[8,2048]{1,0:T(8,128)S(1)} %chain1.1.start, bf16[4,2,80,256]{3,2,1,0:T(8,128)(2,1)S(1)} %constant_dynamic-update-slice_fusion.8.refs_0_, bf16[4,2,80,256]{3,2,1,0:T(8,128)(2,1)S(1)} %collective-permute-done.18.refs_1_, ...), custom_call_target="tpu_custom_call" | custom-call | flops 67108864 | bytes 1310720 | tf_op jit(solution)/shard_map/chain2/pallas_call | solution.py:283
  (38 shorter events, 0.3 us)
Async XLA Ops:
  0.0 9.7 %collective-permute-start = (bf16[64,512]{1,0:T(8,128)(2,1)}, bf16[64,512]{1,0:T(8,128)(2,1)S(1)}, u32[]{:S(2)}, u32[]{:S(2)}) collective-permute-start(bf16[64,512]{1,0:T(8,128)(2,1)} %param.7), channel_id=1, source_target_pairs={{0,8},{1,9},{2,10},{3,11},{4,12},{5,13},{6,14},{7,15},{8,0},{9,1},... | collective-permute-start | bytes 196616 | tf_op jit(solution)/shard_map/ppermute | solution.py:160
  5.7 4.0 %copy-start.3 = (bf16[64,512]{1,0:T(8,128)(2,1)S(1)}, bf16[64,512]{1,0:T(8,128)(2,1)}, u32[]{:S(2)}) copy-start(bf16[64,512]{1,0:T(8,128)(2,1)} %param.7) | copy-start | bytes 196612
  5.7 12.8 %all-to-all-start = ((bf16[8,80,256]{2,1,0:T(8,128)(2,1)}), bf16[8,80,256]{2,1,0:T(8,128)(2,1)S(1)}, u32[]{:S(2)}, u32[]{:S(2)}) async-start(bf16[8,80,256]{2,1,0:T(8,128)(2,1)} %pack.1), calls=%async_computation | async-start | bytes 655360 | tf_op jit(solution)/shard_map/all_to_all | solution.py:184
  9.7 4.6 %collective-permute-start.2 = (bf16[64,512]{1,0:T(8,128)(2,1)S(1)}, bf16[64,512]{1,0:T(8,128)(2,1)S(1)}, u32[]{:S(2)}, u32[]{:S(2)}) collective-permute-start(bf16[64,512]{1,0:T(8,128)(2,1)S(1)} %get-tuple-element.39), channel_id=1, source_target_pairs={{0,16},{16,0},{1,17},{17,1},{2,18},{18,2},{3,19},{19,3},{4,20},{20... | collective-permute-start | bytes 196616 | tf_op jit(solution)/shard_map/ppermute | solution.py:163
  11.3 6.5 %collective-permute-start.1 = (bf16[1,64,512]{2,1,0:T(8,128)(2,1)S(1)}, bf16[1,64,512]{2,1,0:T(8,128)(2,1)S(1)}, u32[]{:S(2)}, u32[]{:S(2)}) collective-permute-start(bf16[1,64,512]{2,1,0:T(8,128)(2,1)S(1)} %get-tuple-element.40), channel_id=1, source_target_pairs={{0,2},{1,3},{2,0},{3,1},{4,6},{5,7},{6,4},{7,5},{8,10},{9,11},{10,... | collective-permute-start | bytes 196616 | tf_op jit(solution)/shard_map/ppermute | solution.py:160
  14.3 4.3 %collective-permute-start.3 = (bf16[1,64,512]{2,1,0:T(8,128)(2,1)S(1)}, bf16[1,64,512]{2,1,0:T(8,128)(2,1)S(1)}, u32[]{:S(2)}, u32[]{:S(2)}) collective-permute-start(bf16[1,64,512]{2,1,0:T(8,128)(2,1)S(1)} %bitcast.9), channel_id=1, source_target_pairs={{0,4},{1,5},{2,6},{3,7},{4,0},{5,1},{6,2},{7,3},{8,12},{9,13},{10,... | collective-permute-start | bytes 196616 | tf_op jit(solution)/shard_map/ppermute | solution.py:160
  17.9 0.7 %copy-start.2 = (s32[6]{0:T(128)S(1)}, s32[6]{0:T(128)}, u32[]{:S(2)}) copy-start(s32[6]{0:T(128)} %owners.3) | copy-start | bytes 76
  19.3 8.7 %collective-permute-start.4 = (bf16[1,80,256]{2,1,0:T(8,128)(2,1)S(1)}, bf16[1,80,256]{2,1,0:T(8,128)(2,1)S(1)}, u32[]{:S(2)}, u32[]{:S(2)}) collective-permute-start(bf16[1,80,256]{2,1,0:T(8,128)(2,1)S(1)} %slice.8), channel_id=1, source_target_pairs={{0,8},{1,9},{2,10},{3,11},{4,12},{5,13},{6,14},{7,15},{8,0},{9,1},... | collective-permute-start | bytes 122888 | tf_op jit(solution)/shard_map/ppermute | solution.py:160
  19.8 11.5 %collective-permute-start.5 = (bf16[4,80,256]{2,1,0:T(8,128)(2,1)S(1)}, bf16[4,80,256]{2,1,0:T(8,128)(2,1)S(1)}, u32[]{:S(2)}, u32[]{:S(2)}) collective-permute-start(bf16[4,80,256]{2,1,0:T(8,128)(2,1)S(1)} %slice.9), channel_id=1, source_target_pairs={{0,8},{1,9},{2,10},{3,11},{4,12},{5,13},{6,14},{7,15},{8,0},{9,1},... | collective-permute-start | bytes 491528 | tf_op jit(solution)/shard_map/ppermute | solution.py:160
  28.0 5.0 %collective-permute-start.9 = (bf16[2,64,512]{2,1,0:T(8,128)(2,1)S(1)}, bf16[2,64,512]{2,1,0:T(8,128)(2,1)S(1)}, u32[]{:S(2)}, u32[]{:S(2)}) collective-permute-start(bf16[2,64,512]{2,1,0:T(8,128)(2,1)S(1)} %pad_maximum_fusion.3), channel_id=1, source_target_pairs={{0,4},{1,5},{2,6},{3,7},{4,0},{5,1},{6,2},{7,3},{8,12},{9,13},{10,... | collective-permute-start | bytes 393224 | tf_op jit(solution)/shard_map/ppermute | solution.py:160
  28.0 6.5 %collective-permute-start.10 = (bf16[2,64,512]{2,1,0:T(8,128)(2,1)S(1)}, bf16[2,64,512]{2,1,0:T(8,128)(2,1)S(1)}, u32[]{:S(2)}, u32[]{:S(2)}) collective-permute-start(bf16[2,64,512]{2,1,0:T(8,128)(2,1)S(1)} %pad_maximum_fusion.4), channel_id=1, source_target_pairs={{0,2},{1,3},{2,0},{3,1},{4,6},{5,7},{6,4},{7,5},{8,10},{9,11},{10,... | collective-permute-start | bytes 393224 | tf_op jit(solution)/shard_map/ppermute | solution.py:160
  28.1 9.3 %copy-start = (bf16[4096,128]{1,0:T(8,128)(2,1)S(1)}, bf16[4096,128]{1,0:T(8,128)(2,1)}, u32[]{:S(2)}) copy-start(bf16[4096,128]{1,0:T(8,128)(2,1)} %sub.6) | copy-start | bytes 3145732
  28.2 9.3 %collective-permute-start.11 = (bf16[4,64,512]{2,1,0:T(8,128)(2,1)S(1)}, bf16[4,64,512]{2,1,0:T(8,128)(2,1)S(1)}, u32[]{:S(2)}, u32[]{:S(2)}) collective-permute-start(bf16[4,64,512]{2,1,0:T(8,128)(2,1)S(1)} %constant_dynamic-update-slice_fusion.refs_0_), channel_id=1, source_target_pairs={{0,1},{1,0},{2,3},{3,2},{4,5},{5,4},{6,7},{7,6},{8,9},{9,8},{10,11... | collective-permute-start | bytes 786440 | tf_op jit(solution)/shard_map/ppermute | solution.py:160
  31.9 4.5 %collective-permute-start.8 = (bf16[1,2,80,256]{3,2,1,0:T(8,128)(2,1)S(1)}, bf16[1,2,80,256]{3,2,1,0:T(8,128)(2,1)S(1)}, u32[]{:S(2)}, u32[]{:S(2)}) collective-permute-start(bf16[1,2,80,256]{3,2,1,0:T(8,128)(2,1)S(1)} %get-tuple-element.28), channel_id=1, source_target_pairs={{0,4},{1,5},{2,6},{3,7},{4,0},{5,1},{6,2},{7,3},{8,12},{9,13},{10,... | collective-permute-start | bytes 245768 | tf_op jit(solution)/shard_map/ppermute | solution.py:160
  31.9 4.5 %collective-permute-start.7 = (bf16[1,2,80,256]{3,2,1,0:T(8,128)(2,1)S(1)}, bf16[1,2,80,256]{3,2,1,0:T(8,128)(2,1)S(1)}, u32[]{:S(2)}, u32[]{:S(2)}) collective-permute-start(bf16[1,2,80,256]{3,2,1,0:T(8,128)(2,1)S(1)} %get-tuple-element.27), channel_id=1, source_target_pairs={{0,2},{1,3},{2,0},{3,1},{4,6},{5,7},{6,4},{7,5},{8,10},{9,11},{10,... | collective-permute-start | bytes 245768 | tf_op jit(solution)/shard_map/ppermute | solution.py:160
  33.0 4.4 %collective-permute-start.6 = (bf16[1,2,80,256]{3,2,1,0:T(8,128)(2,1)S(1)}, bf16[1,2,80,256]{3,2,1,0:T(8,128)(2,1)S(1)}, u32[]{:S(2)}, u32[]{:S(2)}) collective-permute-start(bf16[1,2,80,256]{3,2,1,0:T(8,128)(2,1)S(1)} %get-tuple-element.26), channel_id=1, source_target_pairs={{0,16},{16,0},{1,17},{17,1},{2,18},{18,2},{3,19},{19,3},{4,20},{20... | collective-permute-start | bytes 245768 | tf_op jit(solution)/shard_map/ppermute | solution.py:163
  34.5 2.9 %collective-permute-start.12 = (bf16[4,64,512]{2,1,0:T(8,128)(2,1)S(1)}, bf16[4,64,512]{2,1,0:T(8,128)(2,1)S(1)}, u32[]{:S(2)}, u32[]{:S(2)}) collective-permute-start(bf16[4,64,512]{2,1,0:T(8,128)(2,1)S(1)} %constant_dynamic-update-slice_fusion.2.refs_1_), channel_id=1, source_target_pairs={{0,1},{1,0},{2,3},{3,2},{4,5},{5,4},{6,7},{7,6},{8,9},{9,8},{10,11... | collective-permute-start | bytes 786440 | tf_op jit(solution)/shard_map/ppermute | solution.py:160
  37.9 5.4 %collective-permute-start.17 = (bf16[2,2,80,256]{3,2,1,0:T(8,128)(2,1)S(1)}, bf16[2,2,80,256]{3,2,1,0:T(8,128)(2,1)S(1)}, u32[]{:S(2)}, u32[]{:S(2)}) collective-permute-start(bf16[2,2,80,256]{3,2,1,0:T(8,128)(2,1)S(1)} %pad_maximum_fusion.2), channel_id=1, source_target_pairs={{0,16},{16,0},{1,17},{17,1},{2,18},{18,2},{3,19},{19,3},{4,20},{20... | collective-permute-start | bytes 491528 | tf_op jit(solution)/shard_map/ppermute | solution.py:163
  39.5 5.4 %collective-permute-start.15 = (bf16[2,2,80,256]{3,2,1,0:T(8,128)(2,1)S(1)}, bf16[2,2,80,256]{3,2,1,0:T(8,128)(2,1)S(1)}, u32[]{:S(2)}, u32[]{:S(2)}) collective-permute-start(bf16[2,2,80,256]{3,2,1,0:T(8,128)(2,1)S(1)} %pad_maximum_fusion.1), channel_id=1, source_target_pairs={{0,4},{1,5},{2,6},{3,7},{4,0},{5,1},{6,2},{7,3},{8,12},{9,13},{10,... | collective-permute-start | bytes 491528 | tf_op jit(solution)/shard_map/ppermute | solution.py:160
  41.3 7.1 %collective-permute-start.13 = (bf16[2,2,80,256]{3,2,1,0:T(8,128)(2,1)S(1)}, bf16[2,2,80,256]{3,2,1,0:T(8,128)(2,1)S(1)}, u32[]{:S(2)}, u32[]{:S(2)}) collective-permute-start(bf16[2,2,80,256]{3,2,1,0:T(8,128)(2,1)S(1)} %pad_maximum_fusion), channel_id=1, source_target_pairs={{0,2},{1,3},{2,0},{3,1},{4,6},{5,7},{6,4},{7,5},{8,10},{9,11},{10,... | collective-permute-start | bytes 491528 | tf_op jit(solution)/shard_map/ppermute | solution.py:160
  43.3 16.3 %collective-permute-start.18 = (bf16[4,2,80,256]{3,2,1,0:T(8,128)(2,1)S(1)}, bf16[4,2,80,256]{3,2,1,0:T(8,128)(2,1)S(1)}, u32[]{:S(2)}, u32[]{:S(2)}) collective-permute-start(bf16[4,2,80,256]{3,2,1,0:T(8,128)(2,1)S(1)} %constant_dynamic-update-slice_fusion.8.refs_0_), channel_id=1, source_target_pairs={{0,2},{1,3},{2,0},{3,1},{4,6},{5,7},{6,4},{7,5},{8,10},{9,11},{10,... | collective-permute-start | bytes 983048 | tf_op jit(solution)/shard_map/ppermute | solution.py:160
  44.9 14.7 %collective-permute-start.16 = (bf16[4,2,80,256]{3,2,1,0:T(8,128)(2,1)S(1)}, bf16[4,2,80,256]{3,2,1,0:T(8,128)(2,1)S(1)}, u32[]{:S(2)}, u32[]{:S(2)}) collective-permute-start(bf16[4,2,80,256]{3,2,1,0:T(8,128)(2,1)S(1)} %constant_dynamic-update-slice_fusion.6.refs_0_), channel_id=1, source_target_pairs={{0,16},{16,0},{1,17},{17,1},{2,18},{18,2},{3,19},{19,3},{4,20},{20... | collective-permute-start | bytes 983048 | tf_op jit(solution)/shard_map/ppermute | solution.py:163
  48.4 11.2 %collective-permute-start.14 = (bf16[4,2,80,256]{3,2,1,0:T(8,128)(2,1)S(1)}, bf16[4,2,80,256]{3,2,1,0:T(8,128)(2,1)S(1)}, u32[]{:S(2)}, u32[]{:S(2)}) collective-permute-start(bf16[4,2,80,256]{3,2,1,0:T(8,128)(2,1)S(1)} %constant_dynamic-update-slice_fusion.4.refs_0_), channel_id=1, source_target_pairs={{0,4},{1,5},{2,6},{3,7},{4,0},{5,1},{6,2},{7,3},{8,12},{9,13},{10,... | collective-permute-start | bytes 983048 | tf_op jit(solution)/shard_map/ppermute | solution.py:160
  48.8 11.9 %collective-permute-start.19 = (bf16[4,2,80,256]{3,2,1,0:T(8,128)(2,1)S(1)}, bf16[4,2,80,256]{3,2,1,0:T(8,128)(2,1)S(1)}, u32[]{:S(2)}, u32[]{:S(2)}) collective-permute-start(bf16[4,2,80,256]{3,2,1,0:T(8,128)(2,1)S(1)} %constant_dynamic-update-slice_fusion.4.refs_0_), channel_id=1, source_target_pairs={{0,1},{1,0},{2,3},{3,2},{4,5},{5,4},{6,7},{7,6},{8,9},{9,8},{10,11... | collective-permute-start | bytes 983048 | tf_op jit(solution)/shard_map/ppermute | solution.py:160
  48.8 12.5 %copy-start.1 = (s32[6]{0:T(128)S(1)}, s32[6]{0:T(128)}, u32[]{:S(2)}) copy-start(s32[6]{0:T(128)} %offsets.5) | copy-start | bytes 76
  59.6 1.7 %collective-permute-start.20 = (bf16[4,2,80,256]{3,2,1,0:T(8,128)(2,1)S(1)}, bf16[4,2,80,256]{3,2,1,0:T(8,128)(2,1)S(1)}, u32[]{:S(2)}, u32[]{:S(2)}) collective-permute-start(bf16[4,2,80,256]{3,2,1,0:T(8,128)(2,1)S(1)} %collective-permute-done.14.refs_1_), channel_id=1, source_target_pairs={{0,1},{1,0},{2,3},{3,2},{4,5},{5,4},{6,7},{7,6},{8,9},{9,8},{10,11... | collective-permute-start | bytes 983048 | tf_op jit(solution)/shard_map/ppermute | solution.py:160
  59.8 3.4 %collective-permute-start.21 = (bf16[4,2,80,256]{3,2,1,0:T(8,128)(2,1)S(1)}, bf16[4,2,80,256]{3,2,1,0:T(8,128)(2,1)S(1)}, u32[]{:S(2)}, u32[]{:S(2)}) collective-permute-start(bf16[4,2,80,256]{3,2,1,0:T(8,128)(2,1)S(1)} %constant_dynamic-update-slice_fusion.6.refs_0_), channel_id=1, source_target_pairs={{0,1},{1,0},{2,3},{3,2},{4,5},{5,4},{6,7},{7,6},{8,9},{9,8},{10,11... | collective-permute-start | bytes 983048 | tf_op jit(solution)/shard_map/ppermute | solution.py:160
  60.2 3.0 %collective-permute-start.22 = (bf16[4,2,80,256]{3,2,1,0:T(8,128)(2,1)S(1)}, bf16[4,2,80,256]{3,2,1,0:T(8,128)(2,1)S(1)}, u32[]{:S(2)}, u32[]{:S(2)}) collective-permute-start(bf16[4,2,80,256]{3,2,1,0:T(8,128)(2,1)S(1)} %collective-permute-done.16.refs_1_), channel_id=1, source_target_pairs={{0,1},{1,0},{2,3},{3,2},{4,5},{5,4},{6,7},{7,6},{8,9},{9,8},{10,11... | collective-permute-start | bytes 983048 | tf_op jit(solution)/shard_map/ppermute | solution.py:160
  60.3 4.8 %collective-permute-start.23 = (bf16[4,2,80,256]{3,2,1,0:T(8,128)(2,1)S(1)}, bf16[4,2,80,256]{3,2,1,0:T(8,128)(2,1)S(1)}, u32[]{:S(2)}, u32[]{:S(2)}) collective-permute-start(bf16[4,2,80,256]{3,2,1,0:T(8,128)(2,1)S(1)} %constant_dynamic-update-slice_fusion.8.refs_0_), channel_id=1, source_target_pairs={{0,1},{1,0},{2,3},{3,2},{4,5},{5,4},{6,7},{7,6},{8,9},{9,8},{10,11... | collective-permute-start | bytes 983048 | tf_op jit(solution)/shard_map/ppermute | solution.py:160
  60.7 4.4 %collective-permute-start.24 = (bf16[4,2,80,256]{3,2,1,0:T(8,128)(2,1)S(1)}, bf16[4,2,80,256]{3,2,1,0:T(8,128)(2,1)S(1)}, u32[]{:S(2)}, u32[]{:S(2)}) collective-permute-start(bf16[4,2,80,256]{3,2,1,0:T(8,128)(2,1)S(1)} %collective-permute-done.18.refs_1_), channel_id=1, source_target_pairs={{0,1},{1,0},{2,3},{3,2},{4,5},{5,4},{6,7},{7,6},{8,9},{9,8},{10,11... | collective-permute-start | bytes 983048 | tf_op jit(solution)/shard_map/ppermute | solution.py:160

commit v14 on v12

--- a/solution.py
+++ b/solution.py
@@ -8,7 +8,7 @@
 from jax.sharding import PartitionSpec as P
 
 GROUPS = 6
-COLOURS = 3
+SETS = ((0, 1, 2, 3), (4, 5))
 HALF = 8
 SLICES = 2 * HALF
 VMEM = pl.BlockSpec(memory_space=pltpu.VMEM)
@@ -67,26 +67,36 @@
 
 
 def order_kernel(owners, held, *refs):
-    others, outs = refs[:-COLOURS], refs[-COLOURS:]
+    others, outs = refs[: -len(SETS)], refs[-len(SETS) :]
     mine = lax.axis_index("col") // HALF
-    each = GROUPS // COLOURS
-    for group in range(GROUPS):
-        half, rank = places(owners, group)
-        piece = held[lax.rem(owners[group], HALF)]
-        for mask, ref in enumerate(others, 1):
-            other = ref[jnp.minimum(rank, ref.shape[0] - 1)]
-            piece = jnp.where(jnp.bitwise_xor(half, mine) == mask, other, piece)
-        outs[group // each][0, group % each] = piece
-
-
-def merge_kernel(rows, cols, tags, sub, *refs):
+    for groups, out in zip(SETS, outs):
+        for slot, group in enumerate(groups):
+            half, rank = places(owners, group)
+            piece = held[lax.rem(owners[group], HALF)]
+            for mask, ref in enumerate(others, 1):
+                other = ref[jnp.minimum(rank, ref.shape[0] - 1)]
+                piece = jnp.where(jnp.bitwise_xor(half, mine) == mask, other, piece)
+            out[0, slot] = piece
+
+
+def by_core(pair):
+    if pair[0] == pair[1]:
+        return pair[0]
+    return jnp.where(lax.rem(lax.axis_index("col"), 2) == 0, pair[0], pair[1])
+
+
+def swap(pair):
+    return (pair[1] ^ 1, pair[0] ^ 1)
+
+
+def merge_kernel(rows, cols, tags, ready, sub, *refs):
     held, total = refs[:-1], refs[-1]
     row, col = lax.axis_index("row"), lax.axis_index("col")
     deep, tall = held[0].shape[2], held[0].shape[1]
     total[...] = jnp.zeros_like(total)
     for own_tags, ref in zip(tags, held):
         for index, (row_mask, col_mask) in enumerate(own_tags):
-            j = jnp.bitwise_xor(lax.rem(col, cols // rows), col_mask)
+            j = jnp.bitwise_xor(lax.rem(col, cols // rows), by_core(col_mask))
             part = jnp.dot(ref[index], sub[aligned(j, deep), :], preferred_element_type=jnp.float32)
             at = aligned(jnp.bitwise_xor(row, row_mask), tall)
             total[at, :] = total[at, :] + part
@@ -109,7 +119,7 @@
     pv, pt = basis_all.shape[1] // SLICES, factor_all.shape[1] // SLICES
     for own_masks, ref in zip(masks, held):
         for index, mask in enumerate(own_masks):
-            e = jnp.bitwise_xor(mine, mask)
+            e = jnp.bitwise_xor(mine, by_core(mask))
             basis_all[:, aligned(e, pv), :] = ref[index, :, :pv, :]
             factor_all[:, aligned(e, pt), :] = ref[index, :, pv:, :]
     if first:
@@ -160,6 +170,15 @@
     def over_row(x, mask):
         return lax.ppermute(x, "row", [(r, r ^ mask) for r in range(rows)])
 
+    def over_links(x, *bits):
+        pairs = []
+        for r in range(rows):
+            for c in range(cols):
+                bit = bits[c % 2]
+                to = (r ^ 1) * cols + c if bit == HALF else r * cols + (c ^ bit)
+                pairs.append((r * cols + c, to))
+        return lax.ppermute(x, ("row", "col"), pairs)
+
     basis, factor = reflectors[0], wy_factors[0]
     group_rows, reflect = basis.shape
     dtype = basis.dtype
@@ -174,7 +193,7 @@
         in_specs=[HBM, HBM],
         out_specs=VMEM,
         scratch_shapes=[pltpu.SemaphoreType.DMA((2,))],
-        compiler_params=limit(2),
+        compiler_params=limit(56),
         cost_estimate=cost([basis, factor]),
         name="pack",
     )(basis.reshape(SLICES, pv, reflect), factor.reshape(SLICES, pt, reflect))
@@ -190,23 +209,19 @@
             block = jnp.where(index == k, across[k], block)
         return block
 
-    blocks = [for_row(0)] + [over_row(for_row(m), m) for m in range(1, rows)]
-    groups = [range(rows // 2), range(rows // 2, rows)]
-    sides = [jnp.stack([blocks[m] for m in group]) for group in groups]
-    tags = [[(m, 0) for m in group] for group in groups]
-
-    def double(side, bit):
-        sides[side] = jnp.concatenate([sides[side], over_col(sides[side], bit)])
-        tags[side] = tags[side] + [(m, c ^ bit) for m, c in tags[side]]
+    m_held = jnp.stack([for_row(0)] + [over_row(for_row(m), m) for m in range(1, rows)])
+    tags = [(m, (0, 0)) for m in range(rows)]
+
+    def double(held, tags, *bits):
+        held = jnp.concatenate([held, over_links(held, *bits)])
+        return held, tags + [(m, (c[0] ^ bits[0], c[1] ^ bits[1])) for m, c in tags]
 
     bit = share // 2
     while bit > 4:
-        double(0, bit)
-        double(1, bit)
+        m_held, tags = double(m_held, tags, bit, bit)
         bit //= 2
-    double(0, 2)
-    double(1, 4)
-    slices, sides = lax.optimization_barrier((slices, sides))
+    m_held, tags = double(m_held, tags, 2, 4)
+    slices, m_held = lax.optimization_barrier((slices, m_held))
 
     picked = pl.pallas_call(
         pick_kernel,
@@ -218,63 +233,63 @@
         name="pick",
     )(owners, slices)
     others = [over_col(picked, m * HALF) for m in range(1, halves)]
-    late = jnp.concatenate([over_col(sides[0], 4), over_col(sides[1], 2)])
-    late_tags = [(m, c ^ 4) for m, c in tags[0]] + [(m, c ^ 2) for m, c in tags[1]]
-    m_held = [jnp.concatenate(sides), late]
-    tags = [tags[0] + tags[1], late_tags]
+    ready = over_col(picked[0, :16], 1)
+    ready, m_held = lax.optimization_barrier((ready, m_held))
+    late = over_links(m_held, 4, 2)
+    late_tags = [(m, (c[0] ^ 4, c[1] ^ 2)) for m, c in tags]
+    m_held, tags = [m_held, late], [tags, late_tags]
     m_held += [over_col(x, 1) for x in m_held]
-    tags += [[(m, c ^ 1) for m, c in ts] for ts in tags]
+    tags += [[(m, swap(c)) for m, c in ts] for ts in tags]
     wanted, width = merge_factor.shape[0] * rows, sub_vectors.shape[1]
     each = wanted // (rows * cols)
     merged = pl.pallas_call(
         functools.partial(merge_kernel, rows, cols, tags),
         out_shape=jax.ShapeDtypeStruct((wanted, width), jnp.float32),
-        in_specs=[VMEM] + [VMEM] * len(m_held),
+        in_specs=[HBM, VMEM] + [VMEM] * len(m_held),
         out_specs=VMEM,
         compiler_params=limit(8),
         cost_estimate=cost([sub_vectors], 2 * wanted * sub_vectors.size),
         name="merge",
-    )(sub_vectors, *m_held)
-    per = GROUPS // COLOURS
-    colours = pl.pallas_call(
+    )(ready, sub_vectors, *m_held)
+    parts = pl.pallas_call(
         order_kernel,
-        out_shape=[jax.ShapeDtypeStruct((1, per) + piece, dtype)] * COLOURS,
+        out_shape=[jax.ShapeDtypeStruct((1, len(groups)) + piece, dtype) for groups in SETS],
         in_specs=[SMEM, VMEM] + [VMEM] * len(others),
-        out_specs=[VMEM] * COLOURS,
+        out_specs=[VMEM] * len(SETS),
         compiler_params=limit(4),
         cost_estimate=cost([slices]),
         name="order",
     )(owners, slices, *others)
-    colours = list(colours)
-    links = [
-        (HALF, lambda v: over_row(v, 1)),
-        (2, lambda v: over_col(v, 2)),
-        (4, lambda v: over_col(v, 4)),
-    ]
-    masks = [[0] for _ in range(COLOURS)]
+    parts = list(parts)
+    x, y, z = HALF, 2, 4
+    links = [[(x, y), (y, z), (z, x)], [(z, z), (x, x), (y, y)]]
+    masks = [[(0, 0)] for _ in SETS]
+
+    def other_masks(k, step):
+        bits = links[k][step]
+        return [(m[0] ^ bits[0], m[1] ^ bits[1]) for m in masks[k]]
+
     for step in range(2):
-        for k in range(COLOURS):
-            mask, send = links[(k + step) % 3]
-            colours[k] = jnp.concatenate([colours[k], send(colours[k])])
-            masks[k] = masks[k] + [m ^ mask for m in masks[k]]
+        for k in range(len(SETS)):
+            parts[k] = jnp.concatenate([parts[k], over_links(parts[k], *links[k][step])])
+            masks[k] = masks[k] + other_masks(k, step)
         if step == 0:
-            colours, merged = lax.optimization_barrier((colours, merged))
+            parts, merged = lax.optimization_barrier((parts, merged))
+
     state = lax.all_to_all(merged.reshape(rows * cols, each, width), ("row", "col"), 0, 0)
     last_round = []
-    for k in range(COLOURS):
-        mask, send = links[(k + 2) % 3]
-        last_round.append(send(colours[k]))
-        masks[k] = [masks[k], [m ^ mask for m in masks[k]]]
-        masks[k] += [[m ^ 1 for m in ms] for ms in masks[k]]
+    for k in range(len(SETS)):
+        last_round.append(over_links(parts[k], *links[k][2]))
+        masks[k] = [masks[k], other_masks(k, 2)]
+        masks[k] += [[swap(m) for m in ms] for ms in masks[k]]
     last_round, state = lax.optimization_barrier((last_round, state))
     held = []
-    for k in range(COLOURS):
-        held.append([colours[k], last_round[k], over_col(colours[k], 1), over_col(last_round[k], 1)])
+    for k in range(len(SETS)):
+        held.append([parts[k], last_round[k], over_col(parts[k], 1), over_col(last_round[k], 1)])
 
     wide = cols * width
-    for k in range(COLOURS):
-        first, last = k == 0, k == COLOURS - 1
-        groups = range(k * per, (k + 1) * per)
+    for k, groups in enumerate(SETS):
+        first, last = k == 0, k == len(SETS) - 1
         state = pl.pallas_call(
             functools.partial(chain_kernel, cols, groups, masks[k], first, last),
             out_shape=jax.ShapeDtypeStruct(
@@ -283,11 +298,11 @@
             in_specs=[SMEM, VMEM] + [VMEM] * len(held[k]),
             out_specs=VMEM,
             scratch_shapes=[
-                pltpu.VMEM((per, group_rows, reflect), dtype),
-                pltpu.VMEM((per, reflect, reflect), dtype),
+                pltpu.VMEM((len(groups), group_rows, reflect), dtype),
+                pltpu.VMEM((len(groups), reflect, reflect), dtype),
             ],
             compiler_params=limit(12),
-            cost_estimate=cost(held[k], 2 * per * 64 * group_rows * reflect),
+            cost_estimate=cost(held[k], 2 * len(groups) * 64 * group_rows * reflect),
             name=f"chain{k}",
         )(offsets, state, *held[k])
     return state

time: 70.1 us -> 80.2 us (1.14)
  waiting for transfers between devices: 20.4 us -> 43.4 us
  blocking collectives: 10 us -> 0 us
  local copies, waits for them, and re-layouts: 2.08 us -> 0.09 us
  starting transfers between devices: 28.1 us -> 26.3 us
  Pallas kernels: 8.81 us -> 9.78 us
    ppermute x0 -> x8, waiting for transfers between devices: none -> 18.9 us  [over_links(): return lax.ppermute(x, ('row', 'col'), pairs)]
    ppermute x20 -> x9, starting transfers between devices: 18.4 us -> 5.9 us  [over_col(): return lax.ppermute(x, 'col', [(c, c ^ mask) for c in range(cols)])]
    all_to_all x1 -> x0, blocking collectives: 10 us -> none  [local(): lax.all_to_all(merged.reshape(rows * cols, each, width), ('row', 'col'),...]
    ppermute x0 -> x8, starting transfers between devices: none -> 9.45 us  [over_links(): return lax.ppermute(x, ('row', 'col'), pairs)]
    all_to_all x0 -> x1, waiting for transfers between devices: none -> 7.09 us  [local(): lax.all_to_all(merged.reshape(rows * cols, each, width), ('row', 'col'),...]
    all_to_all x0 -> x1, starting transfers between devices: none -> 5.47 us  [local(): lax.all_to_all(merged.reshape(rows * cols, each, width), ('row', 'col'),...]
    ppermute x4 -> x1, starting transfers between devices: 5.66 us -> 1.56 us  [over_row(): return lax.ppermute(x, 'row', [(r, r ^ mask) for r in range(rows)])]
    ppermute x20 -> x9, waiting for transfers between devices: 17.8 us -> 14.5 us  [over_col(): return lax.ppermute(x, 'col', [(c, c ^ mask) for c in range(cols)])]
  transfers between devices with their start and end apart: 25 -> 20, of which waited for: 12 -> 10; matrix products, arithmetic and copies ran while one was open for 0% -> 0% of each run, Pallas kernels for 8% -> 7%
where the time goes in v14:
time: 80.2 us; the launch traced here: 79.9 us
  waiting for transfers between devices  43.4 us (54%)
  starting transfers between devices  26.3 us (33%)
  Pallas kernels  9.78 us (12%)
    ppermute x8, waiting for transfers between devices, over_links(): return lax.ppermute(x, ('row', 'col'), pairs)  18.9 us
    ppermute x9, waiting for transfers between devices, over_col(): return lax.ppermute(x, 'col', [(c, c ^ mask) for c in range(cols)])  14.5 us
    ppermute x8, starting transfers between devices, over_links(): return lax.ppermute(x, ('row', 'col'), pairs)  9.45 us
    all_to_all x1, waiting for transfers between devices, local(): lax.all_to_all(merged.reshape(rows * cols, each, width), ('row', 'col'),...  7.09 us
    ppermute x9, starting transfers between devices, over_col(): return lax.ppermute(x, 'col', [(c, c ^ mask) for c in range(cols)])  5.9 us
    pallas_call x2, Pallas kernels, local(): pl.pallas_call(functools.partial(chain_kernel, cols, groups, masks[k], fi...  5.68 us
    all_to_all x1, starting transfers between devices, local(): lax.all_to_all(merged.reshape(rows * cols, each, width), ('row', 'col'),...  5.47 us
    all_to_all x1, starting transfers between devices, local(): slices = lax.all_to_all(packed, 'col', 0, 0, axis_index_groups=members)  3.95 us
  transfers between devices with their start and end apart: 20, of which 10 were waited for; matrix products, arithmetic and copies ran while one was open for 0% of the time, Pallas kernels for 7%

profile of v14, /device:TPU:0, one launch (start us, length us, event | category | flops | bytes accessed | tf_op | source)
XLA Modules:
  0.0 79.9 jit_solution(12038603593393114327)
XLA Ops:
  0.0 4.0 %collective-permute-start = (bf16[64,512]{1,0:T(8,128)(2,1)}, bf16[64,512]{1,0:T(8,128)(2,1)S(1)}, u32[]{:S(2)}, u32[]{:S(2)}) collective-permute-start(bf16[64,512]{1,0:T(8,128)(2,1)} %param.7), channel_id=1, source_target_pairs={{0,8},{1,9},{2,10},{3,11},{4,12},{5,13},{6,14},{7,15},{8,0},{9,1},... | collective-permute-start | bytes 196616 | tf_op jit(solution)/shard_map/ppermute | solution.py:168
  4.0 1.7 %pack.1 = bf16[8,80,256]{2,1,0:T(8,128)(2,1)} custom-call(bf16[16,64,256]{2,1,0:T(8,128)(2,1)} %bitcast.8, bf16[16,16,256]{2,1,0:T(8,128)(2,1)} %bitcast.11), custom_call_target="tpu_custom_call" | custom-call | bytes 655360 | tf_op jit(solution)/shard_map/pack/pallas_call | solution.py:190
  5.7 0.0 copy-start.3
  5.8 4.0 %all-to-all-start = ((bf16[8,80,256]{2,1,0:T(8,128)(2,1)}), bf16[8,80,256]{2,1,0:T(8,128)(2,1)S(1)}, u32[]{:S(2)}, u32[]{:S(2)}) async-start(bf16[8,80,256]{2,1,0:T(8,128)(2,1)} %pack.1), calls=%async_computation | async-start | bytes 655360 | tf_op jit(solution)/shard_map/all_to_all | solution.py:201
  9.7 0.0 collective-permute-done
  9.7 1.6 %collective-permute-start.1 = (bf16[64,512]{1,0:T(8,128)(2,1)S(1)}, bf16[64,512]{1,0:T(8,128)(2,1)S(1)}, u32[]{:S(2)}, u32[]{:S(2)}) collective-permute-start(bf16[64,512]{1,0:T(8,128)(2,1)S(1)} %get-tuple-element.30), channel_id=1, source_target_pairs={{0,16},{16,0},{1,17},{17,1},{2,18},{18,2},{3,19},{19,3},{4,20},{20... | collective-permute-start | bytes 196616 | tf_op jit(solution)/shard_map/ppermute | solution.py:171
  11.3 3.0 %collective-permute-done.1 = bf16[64,512]{1,0:T(8,128)(2,1)S(1)} collective-permute-done((bf16[64,512]{1,0:T(8,128)(2,1)S(1)}, bf16[64,512]{1,0:T(8,128)(2,1)S(1)}, u32[]{:S(2)}, u32[]{:S(2)}) %collective-permute-start.1) | collective-permute-done | bytes 65568 | tf_op jit(solution)/shard_map/ppermute | solution.py:171
  14.3 0.0 copy-start.2
  14.3 1.8 %collective-permute-start.2 = (bf16[2,64,512]{2,1,0:T(8,128)(2,1)S(1)}, bf16[2,64,512]{2,1,0:T(8,128)(2,1)S(1)}, u32[]{:S(2)}, u32[]{:S(2)}) collective-permute-start(bf16[2,64,512]{2,1,0:T(8,128)(2,1)S(1)} %pad_maximum_fusion.3), channel_id=1, source_target_pairs={{0,2},{1,5},{2,0},{3,7},{4,6},{5,1},{6,4},{7,3},{8,10},{9,13},{10,... | collective-permute-start | bytes 393224 | tf_op jit(solution)/shard_map/ppermute | solution.py:180
  16.2 3.2 %collective-permute-done.2 = bf16[2,64,512]{2,1,0:T(8,128)(2,1)S(1)} collective-permute-done((bf16[2,64,512]{2,1,0:T(8,128)(2,1)S(1)}, bf16[2,64,512]{2,1,0:T(8,128)(2,1)S(1)}, u32[]{:S(2)}, u32[]{:S(2)}) %collective-permute-start.2) | collective-permute-done | bytes 131104 | tf_op jit(solution)/shard_map/ppermute | solution.py:180
  19.4 0.0 copy-start
  19.4 0.0 all-to-all-done.held
  19.4 0.7 pick.1
  20.2 0.1 collective-permute-start.6
  20.2 1.2 %collective-permute-done.6.ready = bf16[16,256]{1,0:T(8,128)(2,1)S(1)} collective-permute-done((bf16[16,256]{1,0:T(8,128)(2,1)S(1)}, bf16[16,256]{1,0:T(8,128)(2,1)S(1)}, u32[]{:S(2)}, u32[]{:S(2)}) %collective-permute-start.6) | collective-permute-done | bytes 8224 | tf_op jit(solution)/shard_map/ppermute | solution.py:168
  21.4 1.8 %collective-permute-start.7 = (bf16[4,64,512]{2,1,0:T(8,128)(2,1)S(1)}, bf16[4,64,512]{2,1,0:T(8,128)(2,1)S(1)}, u32[]{:S(2)}, u32[]{:S(2)}) collective-permute-start(bf16[4,64,512]{2,1,0:T(8,128)(2,1)S(1)} %pad_maximum_fusion.1.refs_0_), channel_id=1, source_target_pairs={{0,4},{1,3},{2,6},{3,1},{4,0},{5,7},{6,2},{7,5},{8,12},{9,11},{10,... | collective-permute-start | bytes 786440 | tf_op jit(solution)/shard_map/ppermute | solution.py:180
  23.2 0.3 collective-permute-start.3
  23.5 11.8 %collective-permute-done.3.refs_0_ = bf16[5,80,256]{2,1,0:T(8,128)(2,1)S(1)} collective-permute-done((bf16[5,80,256]{2,1,0:T(8,128)(2,1)S(1)}, bf16[5,80,256]{2,1,0:T(8,128)(2,1)S(1)}, u32[]{:S(2)}, u32[]{:S(2)}) %collective-permute-start.3) | collective-permute-done | bytes 204832 | tf_op jit(solution)/shard_map/ppermute | solution.py:168
  35.4 0.6 order.1
  36.0 0.1 collective-permute-start.5
  36.1 1.6 %collective-permute-start.4 = (bf16[1,4,80,256]{3,2,1,0:T(8,128)(2,1)S(1)}, bf16[1,4,80,256]{3,2,1,0:T(8,128)(2,1)S(1)}, u32[]{:S(2)}, u32[]{:S(2)}) collective-permute-start(bf16[1,4,80,256]{3,2,1,0:T(8,128)(2,1)S(1)} %get-tuple-element.18), channel_id=1, source_target_pairs={{0,16},{1,3},{2,18},{3,1},{4,20},{5,7},{6,22},{7,5},{8,24},{9,11},... | collective-permute-start | bytes 491528 | tf_op jit(solution)/shard_map/ppermute | solution.py:180
  37.6 0.0 collective-permute-start.8
  37.6 0.0 collective-permute-done.7.refs_1_
  37.6 0.5 collective-permute-start.9
  38.1 2.4 %collective-permute-done.5 = bf16[1,2,80,256]{3,2,1,0:T(8,128)(2,1)S(1)} collective-permute-done((bf16[1,2,80,256]{3,2,1,0:T(8,128)(2,1)S(1)}, bf16[1,2,80,256]{3,2,1,0:T(8,128)(2,1)S(1)}, u32[]{:S(2)}, u32[]{:S(2)}) %collective-permute-start.5) | collective-permute-done | bytes 81952 | tf_op jit(solution)/shard_map/ppermute | solution.py:180
  40.5 0.9 %collective-permute-done.4 = bf16[1,4,80,256]{3,2,1,0:T(8,128)(2,1)S(1)} collective-permute-done((bf16[1,4,80,256]{3,2,1,0:T(8,128)(2,1)S(1)}, bf16[1,4,80,256]{3,2,1,0:T(8,128)(2,1)S(1)}, u32[]{:S(2)}, u32[]{:S(2)}) %collective-permute-start.4) | collective-permute-done | bytes 163872 | tf_op jit(solution)/shard_map/ppermute | solution.py:180
  41.5 0.0 collective-permute-done.8.refs_2_
  41.5 0.0 collective-permute-done.9.refs_3_
  41.5 1.1 %merge.1 = f32[128,128]{1,0:T(8,128)} custom-call(bf16[16,256]{1,0:T(8,128)(2,1)S(1)} %collective-permute-done.6.ready, bf16[4096,128]{1,0:T(8,128)(2,1)S(1)} %copy-done, bf16[4,64,512]{2,1,0:T(8,128)(2,1)S(1)} %pad_maximum_fusion.1.refs_0_, bf16[4,64,512]{2,1,0:T(8,128)(2,1)S(1)} %collective-permute-done.7.refs_1_, ...), custom_call_target="tpu_custom_call" | custom-call | flops 134217728 | bytes 1048576 | tf_op jit(solution)/shard_map/merge/pallas_call | solution.py:245
  42.6 0.3 collective-permute-start.10
  42.9 6.7 %collective-permute-done.10 = bf16[2,4,80,256]{3,2,1,0:T(8,128)(2,1)S(1)} collective-permute-done((bf16[2,4,80,256]{3,2,1,0:T(8,128)(2,1)S(1)}, bf16[2,4,80,256]{3,2,1,0:T(8,128)(2,1)S(1)}, u32[]{:S(2)}, u32[]{:S(2)}) %collective-permute-start.10) | collective-permute-done | bytes 327712 | tf_op jit(solution)/shard_map/ppermute | solution.py:180
  49.7 2.0 %collective-permute-start.11 = (bf16[4,4,80,256]{3,2,1,0:T(8,128)(2,1)S(1)}, bf16[4,4,80,256]{3,2,1,0:T(8,128)(2,1)S(1)}, u32[]{:S(2)}, u32[]{:S(2)}) collective-permute-start(bf16[4,4,80,256]{3,2,1,0:T(8,128)(2,1)S(1)} %constant_dynamic-update-slice_fusion.refs_0_), channel_id=1, source_target_pairs={{0,4},{1,17},{2,6},{3,19},{4,0},{5,21},{6,2},{7,23},{8,12},{9,25},... | collective-permute-start | bytes 1966088 | tf_op jit(solution)/shard_map/ppermute | solution.py:180
  51.7 1.5 %collective-permute-start.12 = (bf16[2,2,80,256]{3,2,1,0:T(8,128)(2,1)S(1)}, bf16[2,2,80,256]{3,2,1,0:T(8,128)(2,1)S(1)}, u32[]{:S(2)}, u32[]{:S(2)}) collective-permute-start(bf16[2,2,80,256]{3,2,1,0:T(8,128)(2,1)S(1)} %pad_maximum_fusion.2), channel_id=1, source_target_pairs={{0,16},{1,17},{2,18},{3,19},{4,20},{5,21},{6,22},{7,23},{8,24},{9,... | collective-permute-start | bytes 491528 | tf_op jit(solution)/shard_map/ppermute | solution.py:180
  53.2 5.6 %collective-permute-done.12 = bf16[2,2,80,256]{3,2,1,0:T(8,128)(2,1)S(1)} collective-permute-done((bf16[2,2,80,256]{3,2,1,0:T(8,128)(2,1)S(1)}, bf16[2,2,80,256]{3,2,1,0:T(8,128)(2,1)S(1)}, u32[]{:S(2)}, u32[]{:S(2)}) %collective-permute-start.12) | collective-permute-done | bytes 163872 | tf_op jit(solution)/shard_map/ppermute | solution.py:180
  58.9 0.4 collective-permute-start.13
  59.2 5.5 %all-to-all-start.1 = ((f32[32,4,128]{2,1,0:T(4,128)}), f32[32,4,128]{2,1,0:T(4,128)S(1)}, u32[]{:S(2)}, u32[]{:S(2)}) async-start(f32[32,4,128]{2,1,0:T(4,128)} %bitcast.5), calls=%async_computation.1 | async-start | bytes 131072 | tf_op jit(solution)/shard_map/all_to_all | solution.py:279
  64.7 0.3 collective-permute-start.14
  65.0 7.1 %all-to-all-done.1.start = f32[32,4,128]{2,1,0:T(4,128)S(1)} async-done(((f32[32,4,128]{2,1,0:T(4,128)}), f32[32,4,128]{2,1,0:T(4,128)S(1)}, u32[]{:S(2)}, u32[]{:S(2)}) %all-to-all-start.1) | async-done | bytes 65568 | tf_op jit(solution)/shard_map/all_to_all | solution.py:279
  72.1 0.0 collective-permute-done.13.refs_1_
  72.1 0.0 collective-permute-done.11.refs_1_
  72.1 0.1 collective-permute-start.15
  72.3 0.4 collective-permute-start.16
  72.7 0.1 collective-permute-start.17
  72.8 1.5 %collective-permute-done.15.refs_3_ = bf16[4,4,80,256]{3,2,1,0:T(8,128)(2,1)S(1)} collective-permute-done((bf16[4,4,80,256]{3,2,1,0:T(8,128)(2,1)S(1)}, bf16[4,4,80,256]{3,2,1,0:T(8,128)(2,1)S(1)}, u32[]{:S(2)}, u32[]{:S(2)}) %collective-permute-start.15) | collective-permute-done | bytes 655392 | tf_op jit(solution)/shard_map/ppermute | solution.py:168
  74.2 3.2 %chain0.1.start = f32[8,2048]{1,0:T(8,128)S(1)} custom-call(s32[6]{0:T(128)S(1)} %copy-done.1, f32[32,4,128]{2,1,0:T(4,128)S(1)} %all-to-all-done.1.start, bf16[4,4,80,256]{3,2,1,0:T(8,128)(2,1)S(1)} %constant_dynamic-update-slice_fusion.refs_0_, bf16[4,4,80,256]{3,2,1,0:T(8,128)(2,1)S(1)} %collective-permute-done.11.refs_1_, ...), custom_call_target="tpu_custom_call" | custom-call | flops 134217728 | bytes 2621440 | tf_op jit(solution)/shard_map/chain0/pallas_call | solution.py:293
  77.4 0.0 collective-permute-done.16.refs_2_
  77.4 0.0 collective-permute-done.17.refs_3_
  77.4 2.5 %chain1.1 = bf16[4,2048]{1,0:T(4,128)(2,1)} custom-call(s32[6]{0:T(128)S(1)} %copy-done.1, f32[8,2048]{1,0:T(8,128)S(1)} %chain0.1.start, bf16[4,2,80,256]{3,2,1,0:T(8,128)(2,1)S(1)} %constant_dynamic-update-slice_fusion.2.refs_0_, bf16[4,2,80,256]{3,2,1,0:T(8,128)(2,1)S(1)} %collective-permute-done.13.refs_1_, ...), custom_call_target="tpu_custom_call" | custom-call | flops 67108864 | bytes 1310720 | tf_op jit(solution)/shard_map/chain1/pallas_call | solution.py:293
  (16 shorter events, 0.2 us)
Async XLA Ops:
  0.0 9.7 %collective-permute-start = (bf16[64,512]{1,0:T(8,128)(2,1)}, bf16[64,512]{1,0:T(8,128)(2,1)S(1)}, u32[]{:S(2)}, u32[]{:S(2)}) collective-permute-start(bf16[64,512]{1,0:T(8,128)(2,1)} %param.7), channel_id=1, source_target_pairs={{0,8},{1,9},{2,10},{3,11},{4,12},{5,13},{6,14},{7,15},{8,0},{9,1},... | collective-permute-start | bytes 196616 | tf_op jit(solution)/shard_map/ppermute | solution.py:168
  5.7 4.0 %copy-start.3 = (bf16[64,512]{1,0:T(8,128)(2,1)S(1)}, bf16[64,512]{1,0:T(8,128)(2,1)}, u32[]{:S(2)}) copy-start(bf16[64,512]{1,0:T(8,128)(2,1)} %param.7) | copy-start | bytes 196612
  5.8 13.7 %all-to-all-start = ((bf16[8,80,256]{2,1,0:T(8,128)(2,1)}), bf16[8,80,256]{2,1,0:T(8,128)(2,1)S(1)}, u32[]{:S(2)}, u32[]{:S(2)}) async-start(bf16[8,80,256]{2,1,0:T(8,128)(2,1)} %pack.1), calls=%async_computation | async-start | bytes 655360 | tf_op jit(solution)/shard_map/all_to_all | solution.py:201
  9.7 4.6 %collective-permute-start.1 = (bf16[64,512]{1,0:T(8,128)(2,1)S(1)}, bf16[64,512]{1,0:T(8,128)(2,1)S(1)}, u32[]{:S(2)}, u32[]{:S(2)}) collective-permute-start(bf16[64,512]{1,0:T(8,128)(2,1)S(1)} %get-tuple-element.30), channel_id=1, source_target_pairs={{0,16},{16,0},{1,17},{17,1},{2,18},{18,2},{3,19},{19,3},{4,20},{20... | collective-permute-start | bytes 196616 | tf_op jit(solution)/shard_map/ppermute | solution.py:171
  14.3 5.1 %copy-start.2 = (s32[6]{0:T(128)S(1)}, s32[6]{0:T(128)}, u32[]{:S(2)}) copy-start(s32[6]{0:T(128)} %owners.3) | copy-start | bytes 76
  14.3 5.0 %collective-permute-start.2 = (bf16[2,64,512]{2,1,0:T(8,128)(2,1)S(1)}, bf16[2,64,512]{2,1,0:T(8,128)(2,1)S(1)}, u32[]{:S(2)}, u32[]{:S(2)}) collective-permute-start(bf16[2,64,512]{2,1,0:T(8,128)(2,1)S(1)} %pad_maximum_fusion.3), channel_id=1, source_target_pairs={{0,2},{1,5},{2,0},{3,7},{4,6},{5,1},{6,4},{7,3},{8,10},{9,13},{10,... | collective-permute-start | bytes 393224 | tf_op jit(solution)/shard_map/ppermute | solution.py:180
  19.4 22.1 %copy-start = (bf16[4096,128]{1,0:T(8,128)(2,1)S(1)}, bf16[4096,128]{1,0:T(8,128)(2,1)}, u32[]{:S(2)}) copy-start(bf16[4096,128]{1,0:T(8,128)(2,1)} %sub.6) | copy-start | bytes 3145732
  20.2 1.2 %collective-permute-start.6 = (bf16[16,256]{1,0:T(8,128)(2,1)S(1)}, bf16[16,256]{1,0:T(8,128)(2,1)S(1)}, u32[]{:S(2)}, u32[]{:S(2)}) collective-permute-start(bf16[16,256]{1,0:T(8,128)(2,1)S(1)} %slice_bitcast_fusion), channel_id=1, source_target_pairs={{0,1},{1,0},{2,3},{3,2},{4,5},{5,4},{6,7},{7,6},{8,9},{9,8},{10,11... | collective-permute-start | bytes 24584 | tf_op jit(solution)/shard_map/ppermute | solution.py:168
  21.4 16.2 %collective-permute-start.7 = (bf16[4,64,512]{2,1,0:T(8,128)(2,1)S(1)}, bf16[4,64,512]{2,1,0:T(8,128)(2,1)S(1)}, u32[]{:S(2)}, u32[]{:S(2)}) collective-permute-start(bf16[4,64,512]{2,1,0:T(8,128)(2,1)S(1)} %pad_maximum_fusion.1.refs_0_), channel_id=1, source_target_pairs={{0,4},{1,3},{2,6},{3,1},{4,0},{5,7},{6,2},{7,5},{8,12},{9,11},{10,... | collective-permute-start | bytes 786440 | tf_op jit(solution)/shard_map/ppermute | solution.py:180
  23.2 12.2 %collective-permute-start.3 = (bf16[5,80,256]{2,1,0:T(8,128)(2,1)S(1)}, bf16[5,80,256]{2,1,0:T(8,128)(2,1)S(1)}, u32[]{:S(2)}, u32[]{:S(2)}) collective-permute-start(bf16[5,80,256]{2,1,0:T(8,128)(2,1)S(1)} %pick.1), channel_id=1, source_target_pairs={{0,8},{1,9},{2,10},{3,11},{4,12},{5,13},{6,14},{7,15},{8,0},{9,1},... | collective-permute-start | bytes 614408 | tf_op jit(solution)/shard_map/ppermute | solution.py:168
  36.0 4.5 %collective-permute-start.5 = (bf16[1,2,80,256]{3,2,1,0:T(8,128)(2,1)S(1)}, bf16[1,2,80,256]{3,2,1,0:T(8,128)(2,1)S(1)}, u32[]{:S(2)}, u32[]{:S(2)}) collective-permute-start(bf16[1,2,80,256]{3,2,1,0:T(8,128)(2,1)S(1)} %get-tuple-element.19), channel_id=1, source_target_pairs={{0,4},{1,5},{2,6},{3,7},{4,0},{5,1},{6,2},{7,3},{8,12},{9,13},{10,... | collective-permute-start | bytes 245768 | tf_op jit(solution)/shard_map/ppermute | solution.py:180
  36.1 5.4 %collective-permute-start.4 = (bf16[1,4,80,256]{3,2,1,0:T(8,128)(2,1)S(1)}, bf16[1,4,80,256]{3,2,1,0:T(8,128)(2,1)S(1)}, u32[]{:S(2)}, u32[]{:S(2)}) collective-permute-start(bf16[1,4,80,256]{3,2,1,0:T(8,128)(2,1)S(1)} %get-tuple-element.18), channel_id=1, source_target_pairs={{0,16},{1,3},{2,18},{3,1},{4,20},{5,7},{6,22},{7,5},{8,24},{9,11},... | collective-permute-start | bytes 491528 | tf_op jit(solution)/shard_map/ppermute | solution.py:180
  37.6 3.9 %collective-permute-start.8 = (bf16[4,64,512]{2,1,0:T(8,128)(2,1)S(1)}, bf16[4,64,512]{2,1,0:T(8,128)(2,1)S(1)}, u32[]{:S(2)}, u32[]{:S(2)}) collective-permute-start(bf16[4,64,512]{2,1,0:T(8,128)(2,1)S(1)} %pad_maximum_fusion.1.refs_0_), channel_id=1, source_target_pairs={{0,1},{1,0},{2,3},{3,2},{4,5},{5,4},{6,7},{7,6},{8,9},{9,8},{10,11... | collective-permute-start | bytes 786440 | tf_op jit(solution)/shard_map/ppermute | solution.py:168
  37.6 3.9 %collective-permute-start.9 = (bf16[4,64,512]{2,1,0:T(8,128)(2,1)S(1)}, bf16[4,64,512]{2,1,0:T(8,128)(2,1)S(1)}, u32[]{:S(2)}, u32[]{:S(2)}) collective-permute-start(bf16[4,64,512]{2,1,0:T(8,128)(2,1)S(1)} %collective-permute-done.7.refs_1_), channel_id=1, source_target_pairs={{0,1},{1,0},{2,3},{3,2},{4,5},{5,4},{6,7},{7,6},{8,9},{9,8},{10,11... | collective-permute-start | bytes 786440 | tf_op jit(solution)/shard_map/ppermute | solution.py:168
  42.6 7.1 %collective-permute-start.10 = (bf16[2,4,80,256]{3,2,1,0:T(8,128)(2,1)S(1)}, bf16[2,4,80,256]{3,2,1,0:T(8,128)(2,1)S(1)}, u32[]{:S(2)}, u32[]{:S(2)}) collective-permute-start(bf16[2,4,80,256]{3,2,1,0:T(8,128)(2,1)S(1)} %pad_maximum_fusion), channel_id=1, source_target_pairs={{0,2},{1,5},{2,0},{3,7},{4,6},{5,1},{6,4},{7,3},{8,10},{9,13},{10,... | collective-permute-start | bytes 983048 | tf_op jit(solution)/shard_map/ppermute | solution.py:180
  49.7 22.4 %collective-permute-start.11 = (bf16[4,4,80,256]{3,2,1,0:T(8,128)(2,1)S(1)}, bf16[4,4,80,256]{3,2,1,0:T(8,128)(2,1)S(1)}, u32[]{:S(2)}, u32[]{:S(2)}) collective-permute-start(bf16[4,4,80,256]{3,2,1,0:T(8,128)(2,1)S(1)} %constant_dynamic-update-slice_fusion.refs_0_), channel_id=1, source_target_pairs={{0,4},{1,17},{2,6},{3,19},{4,0},{5,21},{6,2},{7,23},{8,12},{9,25},... | collective-permute-start | bytes 1966088 | tf_op jit(solution)/shard_map/ppermute | solution.py:180
  51.7 7.1 %collective-permute-start.12 = (bf16[2,2,80,256]{3,2,1,0:T(8,128)(2,1)S(1)}, bf16[2,2,80,256]{3,2,1,0:T(8,128)(2,1)S(1)}, u32[]{:S(2)}, u32[]{:S(2)}) collective-permute-start(bf16[2,2,80,256]{3,2,1,0:T(8,128)(2,1)S(1)} %pad_maximum_fusion.2), channel_id=1, source_target_pairs={{0,16},{1,17},{2,18},{3,19},{4,20},{5,21},{6,22},{7,23},{8,24},{9,... | collective-permute-start | bytes 491528 | tf_op jit(solution)/shard_map/ppermute | solution.py:180
  58.9 13.3 %collective-permute-start.13 = (bf16[4,2,80,256]{3,2,1,0:T(8,128)(2,1)S(1)}, bf16[4,2,80,256]{3,2,1,0:T(8,128)(2,1)S(1)}, u32[]{:S(2)}, u32[]{:S(2)}) collective-permute-start(bf16[4,2,80,256]{3,2,1,0:T(8,128)(2,1)S(1)} %constant_dynamic-update-slice_fusion.2.refs_0_), channel_id=1, source_target_pairs={{0,2},{1,3},{2,0},{3,1},{4,6},{5,7},{6,4},{7,5},{8,10},{9,11},{10,... | collective-permute-start | bytes 983048 | tf_op jit(solution)/shard_map/ppermute | solution.py:180
  59.2 15.0 %copy-start.1 = (s32[6]{0:T(128)S(1)}, s32[6]{0:T(128)}, u32[]{:S(2)}) copy-start(s32[6]{0:T(128)} %offsets.3) | copy-start | bytes 76
  59.2 12.9 %all-to-all-start.1 = ((f32[32,4,128]{2,1,0:T(4,128)}), f32[32,4,128]{2,1,0:T(4,128)S(1)}, u32[]{:S(2)}, u32[]{:S(2)}) async-start(f32[32,4,128]{2,1,0:T(4,128)} %bitcast.5), calls=%async_computation.1 | async-start | bytes 131072 | tf_op jit(solution)/shard_map/all_to_all | solution.py:279
  64.7 8.0 %collective-permute-start.14 = (bf16[4,4,80,256]{3,2,1,0:T(8,128)(2,1)S(1)}, bf16[4,4,80,256]{3,2,1,0:T(8,128)(2,1)S(1)}, u32[]{:S(2)}, u32[]{:S(2)}) collective-permute-start(bf16[4,4,80,256]{3,2,1,0:T(8,128)(2,1)S(1)} %constant_dynamic-update-slice_fusion.refs_0_), channel_id=1, source_target_pairs={{0,1},{1,0},{2,3},{3,2},{4,5},{5,4},{6,7},{7,6},{8,9},{9,8},{10,11... | collective-permute-start | bytes 1966088 | tf_op jit(solution)/shard_map/ppermute | solution.py:168
  72.1 2.1 %collective-permute-start.15 = (bf16[4,4,80,256]{3,2,1,0:T(8,128)(2,1)S(1)}, bf16[4,4,80,256]{3,2,1,0:T(8,128)(2,1)S(1)}, u32[]{:S(2)}, u32[]{:S(2)}) collective-permute-start(bf16[4,4,80,256]{3,2,1,0:T(8,128)(2,1)S(1)} %collective-permute-done.11.refs_1_), channel_id=1, source_target_pairs={{0,1},{1,0},{2,3},{3,2},{4,5},{5,4},{6,7},{7,6},{8,9},{9,8},{10,11... | collective-permute-start | bytes 1966088 | tf_op jit(solution)/shard_map/ppermute | solution.py:168
  72.3 5.2 %collective-permute-start.16 = (bf16[4,2,80,256]{3,2,1,0:T(8,128)(2,1)S(1)}, bf16[4,2,80,256]{3,2,1,0:T(8,128)(2,1)S(1)}, u32[]{:S(2)}, u32[]{:S(2)}) collective-permute-start(bf16[4,2,80,256]{3,2,1,0:T(8,128)(2,1)S(1)} %constant_dynamic-update-slice_fusion.2.refs_0_), channel_id=1, source_target_pairs={{0,1},{1,0},{2,3},{3,2},{4,5},{5,4},{6,7},{7,6},{8,9},{9,8},{10,11... | collective-permute-start | bytes 983048 | tf_op jit(solution)/shard_map/ppermute | solution.py:168
  72.7 4.8 %collective-permute-start.17 = (bf16[4,2,80,256]{3,2,1,0:T(8,128)(2,1)S(1)}, bf16[4,2,80,256]{3,2,1,0:T(8,128)(2,1)S(1)}, u32[]{:S(2)}, u32[]{:S(2)}) collective-permute-start(bf16[4,2,80,256]{3,2,1,0:T(8,128)(2,1)S(1)} %collective-permute-done.13.refs_1_), channel_id=1, source_target_pairs={{0,1},{1,0},{2,3},{3,2},{4,5},{5,4},{6,7},{7,6},{8,9},{9,8},{10,11... | collective-permute-start | bytes 983048 | tf_op jit(solution)/shard_map/ppermute | solution.py:168

commit v15 on v10

--- a/solution.py
+++ b/solution.py
@@ -9,6 +9,7 @@
 
 GROUPS = 6
 COLOURS = 3
+CHAINS = ((0,), (1, 2))
 HALF = 8
 SLICES = 2 * HALF
 VMEM = pl.BlockSpec(memory_space=pltpu.VMEM)
@@ -18,6 +19,11 @@
 
 def limit(mib):
     return pltpu.CompilerParams(vmem_limit_bytes=mib * 1024 * 1024)
+
+
+def cost(arrays, flops=0):
+    size = sum(a.size * a.dtype.itemsize for a in arrays)
+    return pl.CostEstimate(flops=flops, bytes_accessed=size, transcendentals=0)
 
 
 def slice_index():
@@ -74,7 +80,7 @@
         outs[group // each][0, group % each] = piece
 
 
-def merge_kernel(rows, cols, tags, sub, *refs):
+def merge_kernel(rows, cols, tags, ready, sub, *refs):
     held, total = refs[:-1], refs[-1]
     row, col = lax.axis_index("row"), lax.axis_index("col")
     deep, tall = held[0].shape[2], held[0].shape[1]
@@ -98,15 +104,16 @@
     return products[:half] + products[half:]
 
 
-def chain_kernel(cols, groups, masks, first, last, offsets, start, *refs):
+def chain_kernel(cols, groups, slots, masks, first, last, offsets, start, *refs):
     held, (out, basis_all, factor_all) = refs[: len(masks)], refs[len(masks) :]
     mine = slice_index()
     pv, pt = basis_all.shape[1] // SLICES, factor_all.shape[1] // SLICES
-    for own_masks, ref in zip(masks, held):
+    for slot, own_masks, ref in zip(slots, masks, held):
+        to = slice(slot, slot + ref.shape[1])
         for index, mask in enumerate(own_masks):
             e = jnp.bitwise_xor(mine, mask)
-            basis_all[:, aligned(e, pv), :] = ref[index, :, :pv, :]
-            factor_all[:, aligned(e, pt), :] = ref[index, :, pv:, :]
+            basis_all[to, aligned(e, pv), :] = ref[index, :, :pv, :]
+            factor_all[to, aligned(e, pt), :] = ref[index, :, pv:, :]
     if first:
         n, each, width = start.shape
         pieces = start[...].reshape(n // cols, cols, each, width).sum(0)
@@ -161,18 +168,17 @@
     pv, pt = group_rows // SLICES, reflect // SLICES
     piece = (pv + pt, reflect)
 
-    across = [merge_factor] + [over_col(merge_factor, m * share) for m in range(1, rows)]
-
     packed = pl.pallas_call(
         pack_kernel,
         out_shape=jax.ShapeDtypeStruct((HALF,) + piece, dtype),
         in_specs=[HBM, HBM],
         out_specs=VMEM,
         scratch_shapes=[pltpu.SemaphoreType.DMA((2,))],
-        compiler_params=limit(2),
+        compiler_params=limit(56),
+        cost_estimate=cost([basis, factor]),
         name="pack",
     )(basis.reshape(SLICES, pv, reflect), factor.reshape(SLICES, pt, reflect))
-    packed, across = lax.optimization_barrier((packed, across))
+    packed, merge_factor = lax.optimization_barrier((packed, merge_factor))
     members = [[h * HALF + c for c in range(HALF)] for h in range(halves)]
     slices = lax.all_to_all(packed, "col", 0, 0, axis_index_groups=members)
 
@@ -182,8 +188,13 @@
         in_specs=[SMEM, VMEM],
         out_specs=VMEM,
         compiler_params=limit(4),
+        cost_estimate=cost([slices]),
         name="pick",
     )(owners, slices)
+    ready = over_col(picked[0, :16], HALF)
+    others = [over_col(picked, m * HALF) for m in range(1, halves)]
+
+    across = [merge_factor] + [over_col(merge_factor, m * share) for m in range(1, rows)]
 
     row, top = lax.axis_index("row"), lax.axis_index("col") // share
 
@@ -194,28 +205,17 @@
             block = jnp.where(index == k, across[k], block)
         return block
 
-    blocks = [for_row(0)] + [over_row(for_row(m), m) for m in range(1, rows)]
-    groups = [range(rows // 2), range(rows // 2, rows)]
-    sides = [jnp.stack([blocks[m] for m in group]) for group in groups]
-    tags = [[(m, 0) for m in group] for group in groups]
-
-    def double(side, bit):
-        sides[side] = jnp.concatenate([sides[side], over_col(sides[side], bit)])
-        tags[side] = tags[side] + [(m, c ^ bit) for m, c in tags[side]]
-
+    m_held = jnp.stack([for_row(0)] + [over_row(for_row(m), m) for m in range(1, rows)])
+    ready, m_held = lax.optimization_barrier((ready, m_held))
+    tags = [(m, 0) for m in range(rows)]
     bit = share // 2
     while bit > 4:
-        double(0, bit)
-        double(1, bit)
+        m_held = jnp.concatenate([m_held, over_col(m_held, bit)])
+        tags = tags + [(m, c ^ bit) for m, c in tags]
         bit //= 2
-    double(0, 2)
-    double(1, 4)
-    picked, sides = lax.optimization_barrier((picked, sides))
-    others = [over_col(picked, m * HALF) for m in range(1, halves)]
-    late = jnp.concatenate([over_col(sides[0], 4), over_col(sides[1], 2)])
-    late_tags = [(m, c ^ 4) for m, c in tags[0]] + [(m, c ^ 2) for m, c in tags[1]]
-    m_held = [jnp.concatenate(sides), late]
-    tags = [tags[0] + tags[1], late_tags]
+    late = jnp.concatenate([over_col(m_held, mask) for mask in (2, 4, 6)])
+    late_tags = [(m, c ^ mask) for mask in (2, 4, 6) for m, c in tags]
+    m_held, tags = [m_held, late], [tags, late_tags]
     m_held += [over_col(x, 1) for x in m_held]
     tags += [[(m, c ^ 1) for m, c in ts] for ts in tags]
     wanted, width = merge_factor.shape[0] * rows, sub_vectors.shape[1]
@@ -223,14 +223,12 @@
     merged = pl.pallas_call(
         functools.partial(merge_kernel, rows, cols, tags),
         out_shape=jax.ShapeDtypeStruct((wanted, width), jnp.float32),
-        in_specs=[VMEM] + [VMEM] * len(m_held),
+        in_specs=[HBM, VMEM] + [VMEM] * len(m_held),
         out_specs=VMEM,
         compiler_params=limit(8),
+        cost_estimate=cost([sub_vectors], 2 * wanted * sub_vectors.size),
         name="merge",
-    )(sub_vectors, *m_held)
-    others, merged = lax.optimization_barrier((others, merged))
-    state = lax.all_to_all(merged.reshape(rows * cols, each, width), ("row", "col"), 0, 0)
-
+    )(ready, sub_vectors, *m_held)
     per = GROUPS // COLOURS
     colours = pl.pallas_call(
         order_kernel,
@@ -238,6 +236,7 @@
         in_specs=[SMEM, VMEM] + [VMEM] * len(others),
         out_specs=[VMEM] * COLOURS,
         compiler_params=limit(4),
+        cost_estimate=cost([slices]),
         name="order",
     )(owners, slices, *others)
     colours = list(colours)
@@ -253,35 +252,42 @@
             colours[k] = jnp.concatenate([colours[k], send(colours[k])])
             masks[k] = masks[k] + [m ^ mask for m in masks[k]]
         if step == 0:
-            colours, state = lax.optimization_barrier((colours, state))
+            colours, merged = lax.optimization_barrier((colours, merged))
+    state = lax.all_to_all(merged.reshape(rows * cols, each, width), ("row", "col"), 0, 0)
     last_round = []
     for k in range(COLOURS):
         mask, send = links[(k + 2) % 3]
         last_round.append(send(colours[k]))
         masks[k] = [masks[k], [m ^ mask for m in masks[k]]]
         masks[k] += [[m ^ 1 for m in ms] for ms in masks[k]]
+    last_round, state = lax.optimization_barrier((last_round, state))
     held = []
     for k in range(COLOURS):
         held.append([colours[k], last_round[k], over_col(colours[k], 1), over_col(last_round[k], 1)])
 
     wide = cols * width
-    for k in range(COLOURS):
-        first, last = k == 0, k == COLOURS - 1
-        groups = range(k * per, (k + 1) * per)
+    for members in CHAINS:
+        first, last = members[0] == 0, members[-1] == COLOURS - 1
+        groups = range(members[0] * per, (members[-1] + 1) * per)
+        arrays = [x for k in members for x in held[k]]
+        slots = [per * i for i, k in enumerate(members) for _ in held[k]]
         state = pl.pallas_call(
-            functools.partial(chain_kernel, cols, groups, masks[k], first, last),
+            functools.partial(
+                chain_kernel, cols, groups, slots, sum((masks[k] for k in members), []), first, last
+            ),
             out_shape=jax.ShapeDtypeStruct(
                 (each, wide) if last else (8, wide), jnp.bfloat16 if last else jnp.float32
             ),
-            in_specs=[SMEM, VMEM] + [VMEM] * len(held[k]),
+            in_specs=[SMEM, VMEM] + [VMEM] * len(arrays),
             out_specs=VMEM,
             scratch_shapes=[
-                pltpu.VMEM((per, group_rows, reflect), dtype),
-                pltpu.VMEM((per, reflect, reflect), dtype),
+                pltpu.VMEM((len(groups), group_rows, reflect), dtype),
+                pltpu.VMEM((len(groups), reflect, reflect), dtype),
             ],
             compiler_params=limit(12),
-            name=f"chain{k}",
-        )(offsets, state, *held[k])
+            cost_estimate=cost(arrays, 2 * len(groups) * 64 * group_rows * reflect),
+            name=f"chain{members[0]}",
+        )(offsets, state, *arrays)
     return state
 
 

time: 79.8 us -> 72 us (0.902)
  waiting for transfers between devices: 35.5 us -> 21.6 us
  blocking collectives: 0 us -> 11.1 us
  starting transfers between devices: 32 us -> 29.4 us
  local copies, waits for them, and re-layouts: 2.07 us -> 0.13 us
    all_to_all x0 -> x1, blocking collectives: none -> 11.1 us  [local(): lax.all_to_all(merged.reshape(rows * cols, each, width), ('row', 'col'),...]
    ppermute x20, waiting for transfers between devices: 27.1 us -> 19.6 us  [over_col(): return lax.ppermute(x, 'col', [(c, c ^ mask) for c in range(cols)])]
    all_to_all x1 -> x0, waiting for transfers between devices: 6.49 us -> none  [local(): lax.all_to_all(merged.reshape(rows * cols, each, width), ('row', 'col'),...]
    all_to_all x1 -> x0, starting transfers between devices: 3.53 us -> none  [local(): lax.all_to_all(merged.reshape(rows * cols, each, width), ('row', 'col'),...]
    unnamed x17 -> x13, local copies, waits for them, and re-layouts: 2.02 us -> 0.08 us
    all_to_all x1, starting transfers between devices: 3.56 us -> 5.4 us  [local(): slices = lax.all_to_all(packed, 'col', 0, 0, axis_index_groups=members)]
    pallas_call x1, Pallas kernels: 0.77 us -> 1.69 us  [local(): pl.pallas_call(pack_kernel, out_shape=jax.ShapeDtypeStruct((HALF,) + piec...]
    pallas_call x3 -> x2, Pallas kernels: 6.28 us -> 5.68 us  [local(): pl.pallas_call(functools.partial(chain_kernel, cols, groups, slots, sum((...]
  transfers between devices with their start and end apart: 26 -> 25, of which waited for: 12 -> 11; matrix products, arithmetic and copies ran while one was open for 0% -> 0% of each run, Pallas kernels for 7% -> 4%
where the time goes in v15:
time: 72 us; the launch traced here: 71.7 us
  starting transfers between devices  29.4 us (41%)
  waiting for transfers between devices  21.6 us (30%)
  blocking collectives  11.1 us (15%)
  Pallas kernels  9.14 us (13%)
    ppermute x20, starting transfers between devices, over_col(): return lax.ppermute(x, 'col', [(c, c ^ mask) for c in range(cols)])  19.7 us
    ppermute x20, waiting for transfers between devices, over_col(): return lax.ppermute(x, 'col', [(c, c ^ mask) for c in range(cols)])  19.6 us
    all_to_all x1, blocking collectives, local(): lax.all_to_all(merged.reshape(rows * cols, each, width), ('row', 'col'),...  11.1 us
    pallas_call x2, Pallas kernels, local(): pl.pallas_call(functools.partial(chain_kernel, cols, groups, slots, sum((...  5.68 us
    all_to_all x1, starting transfers between devices, local(): slices = lax.all_to_all(packed, 'col', 0, 0, axis_index_groups=members)  5.4 us
    ppermute x4, starting transfers between devices, over_row(): return lax.ppermute(x, 'row', [(r, r ^ mask) for r in range(rows)])  4.25 us
    pallas_call x1, Pallas kernels, local(): pl.pallas_call(pack_kernel, out_shape=jax.ShapeDtypeStruct((HALF,) + piec...  1.69 us
    ppermute x4, waiting for transfers between devices, over_row(): return lax.ppermute(x, 'row', [(r, r ^ mask) for r in range(rows)])  1.58 us
  transfers between devices with their start and end apart: 25, of which 11 were waited for; matrix products, arithmetic and copies ran while one was open for 0% of the time, Pallas kernels for 4%

profile of v15, /device:TPU:0, one launch (start us, length us, event | category | flops | bytes accessed | tf_op | source)
XLA Modules:
  0.0 71.7 jit_solution(4814051007961211185)
XLA Ops:
  0.0 1.7 %pack.1 = bf16[8,80,256]{2,1,0:T(8,128)(2,1)} custom-call(bf16[16,64,256]{2,1,0:T(8,128)(2,1)} %bitcast.9, bf16[16,16,256]{2,1,0:T(8,128)(2,1)} %bitcast.10), custom_call_target="tpu_custom_call" | custom-call | bytes 655360 | tf_op jit(solution)/shard_map/pack/pallas_call | solution.py:171
  1.7 0.0 copy-start.3
  1.7 5.4 %all-to-all-start = ((bf16[8,80,256]{2,1,0:T(8,128)(2,1)}), bf16[8,80,256]{2,1,0:T(8,128)(2,1)S(1)}, u32[]{:S(2)}, u32[]{:S(2)}) async-start(bf16[8,80,256]{2,1,0:T(8,128)(2,1)} %pack.1), calls=%async_computation | async-start | bytes 655360 | tf_op jit(solution)/shard_map/all_to_all | solution.py:183
  7.1 2.7 %collective-permute-start.5 = (bf16[64,512]{1,0:T(8,128)(2,1)S(1)}, bf16[64,512]{1,0:T(8,128)(2,1)S(1)}, u32[]{:S(2)}, u32[]{:S(2)}) collective-permute-start(bf16[64,512]{1,0:T(8,128)(2,1)S(1)} %copy-done.3), channel_id=1, source_target_pairs={{0,8},{1,9},{2,10},{3,11},{4,12},{5,13},{6,14},{7,15},{8,0},{9,1},... | collective-permute-start | bytes 196616 | tf_op jit(solution)/shard_map/ppermute | solution.py:160
  9.8 3.4 %collective-permute-done.5 = bf16[64,512]{1,0:T(8,128)(2,1)S(1)} collective-permute-done((bf16[64,512]{1,0:T(8,128)(2,1)S(1)}, bf16[64,512]{1,0:T(8,128)(2,1)S(1)}, u32[]{:S(2)}, u32[]{:S(2)}) %collective-permute-start.5) | collective-permute-done | bytes 65568 | tf_op jit(solution)/shard_map/ppermute | solution.py:160
  13.2 0.0 copy-start.1
  13.3 1.6 %collective-permute-start.6 = (bf16[64,512]{1,0:T(8,128)(2,1)S(1)}, bf16[64,512]{1,0:T(8,128)(2,1)S(1)}, u32[]{:S(2)}, u32[]{:S(2)}) collective-permute-start(bf16[64,512]{1,0:T(8,128)(2,1)S(1)} %get-tuple-element.36), channel_id=1, source_target_pairs={{0,16},{16,0},{1,17},{17,1},{2,18},{18,2},{3,19},{19,3},{4,20},{20... | collective-permute-start | bytes 196616 | tf_op jit(solution)/shard_map/ppermute | solution.py:163
  14.8 0.4 all-to-all-done.held
  15.3 0.7 pick.1
  16.0 3.1 %collective-permute-start.4 = (bf16[16,256]{1,0:T(8,128)(2,1)S(1)}, bf16[16,256]{1,0:T(8,128)(2,1)S(1)}, u32[]{:S(2)}, u32[]{:S(2)}) collective-permute-start(bf16[16,256]{1,0:T(8,128)(2,1)S(1)} %slice_bitcast_fusion), channel_id=1, source_target_pairs={{0,8},{1,9},{2,10},{3,11},{4,12},{5,13},{6,14},{7,15},{8,0},{9,1},... | collective-permute-start | bytes 24584 | tf_op jit(solution)/shard_map/ppermute | solution.py:160
  19.1 1.6 %collective-permute-done.4.ready = bf16[16,256]{1,0:T(8,128)(2,1)S(1)} collective-permute-done((bf16[16,256]{1,0:T(8,128)(2,1)S(1)}, bf16[16,256]{1,0:T(8,128)(2,1)S(1)}, u32[]{:S(2)}, u32[]{:S(2)}) %collective-permute-start.4) | collective-permute-done | bytes 8224 | tf_op jit(solution)/shard_map/ppermute | solution.py:160
  20.7 1.6 %collective-permute-start.7 = (bf16[2,64,512]{2,1,0:T(8,128)(2,1)S(1)}, bf16[2,64,512]{2,1,0:T(8,128)(2,1)S(1)}, u32[]{:S(2)}, u32[]{:S(2)}) collective-permute-start(bf16[2,64,512]{2,1,0:T(8,128)(2,1)S(1)} %pad_maximum_fusion.3.refs_0_), channel_id=1, source_target_pairs={{0,2},{1,3},{2,0},{3,1},{4,6},{5,7},{6,4},{7,5},{8,10},{9,11},{10,... | collective-permute-start | bytes 393224 | tf_op jit(solution)/shard_map/ppermute | solution.py:160
  22.3 4.0 %collective-permute-start.8 = (bf16[2,64,512]{2,1,0:T(8,128)(2,1)S(1)}, bf16[2,64,512]{2,1,0:T(8,128)(2,1)S(1)}, u32[]{:S(2)}, u32[]{:S(2)}) collective-permute-start(bf16[2,64,512]{2,1,0:T(8,128)(2,1)S(1)} %pad_maximum_fusion.3.refs_0_), channel_id=1, source_target_pairs={{0,4},{1,5},{2,6},{3,7},{4,0},{5,1},{6,2},{7,3},{8,12},{9,13},{10,... | collective-permute-start | bytes 393224 | tf_op jit(solution)/shard_map/ppermute | solution.py:160
  26.3 0.0 collective-permute-start
  26.3 0.8 %collective-permute-start.9 = (bf16[2,64,512]{2,1,0:T(8,128)(2,1)S(1)}, bf16[2,64,512]{2,1,0:T(8,128)(2,1)S(1)}, u32[]{:S(2)}, u32[]{:S(2)}) collective-permute-start(bf16[2,64,512]{2,1,0:T(8,128)(2,1)S(1)} %pad_maximum_fusion.3.refs_0_), channel_id=1, source_target_pairs={{0,6},{1,7},{2,4},{3,5},{4,2},{5,3},{6,0},{7,1},{8,14},{9,15},{10,... | collective-permute-start | bytes 393224 | tf_op jit(solution)/shard_map/ppermute | solution.py:160
  27.1 0.0 copy-start
  27.1 3.3 %collective-permute-done.8 = bf16[2,64,512]{2,1,0:T(8,128)(2,1)S(1)} collective-permute-done((bf16[2,64,512]{2,1,0:T(8,128)(2,1)S(1)}, bf16[2,64,512]{2,1,0:T(8,128)(2,1)S(1)}, u32[]{:S(2)}, u32[]{:S(2)}) %collective-permute-start.8) | collective-permute-done | bytes 131104 | tf_op jit(solution)/shard_map/ppermute | solution.py:160
  30.4 5.5 %collective-permute-done.refs_0_ = bf16[5,80,256]{2,1,0:T(8,128)(2,1)S(1)} collective-permute-done((bf16[5,80,256]{2,1,0:T(8,128)(2,1)S(1)}, bf16[5,80,256]{2,1,0:T(8,128)(2,1)S(1)}, u32[]{:S(2)}, u32[]{:S(2)}) %collective-permute-start) | collective-permute-done | bytes 204832 | tf_op jit(solution)/shard_map/ppermute | solution.py:160
  35.9 0.6 order.1
  36.5 0.1 collective-permute-start.3
  36.7 0.1 collective-permute-start.11
  36.7 0.5 collective-permute-start.10
  37.2 0.7 collective-permute-start.2
  37.9 0.9 %collective-permute-start.1 = (bf16[1,2,80,256]{3,2,1,0:T(8,128)(2,1)S(1)}, bf16[1,2,80,256]{3,2,1,0:T(8,128)(2,1)S(1)}, u32[]{:S(2)}, u32[]{:S(2)}) collective-permute-start(bf16[1,2,80,256]{3,2,1,0:T(8,128)(2,1)S(1)} %get-tuple-element.21), channel_id=1, source_target_pairs={{0,16},{16,0},{1,17},{17,1},{2,18},{18,2},{3,19},{19,3},{4,20},{20... | collective-permute-start | bytes 245768 | tf_op jit(solution)/shard_map/ppermute | solution.py:163
  38.7 2.3 %collective-permute-done.3 = bf16[1,2,80,256]{3,2,1,0:T(8,128)(2,1)S(1)} collective-permute-done((bf16[1,2,80,256]{3,2,1,0:T(8,128)(2,1)S(1)}, bf16[1,2,80,256]{3,2,1,0:T(8,128)(2,1)S(1)}, u32[]{:S(2)}, u32[]{:S(2)}) %collective-permute-start.3) | collective-permute-done | bytes 81952 | tf_op jit(solution)/shard_map/ppermute | solution.py:160
  41.1 0.6 collective-permute-done.2
  41.7 0.6 collective-permute-done.1
  42.4 0.0 collective-permute-done.10.refs_2_
  42.4 0.4 merge.1
  42.9 0.9 %collective-permute-start.16 = (bf16[2,2,80,256]{3,2,1,0:T(8,128)(2,1)S(1)}, bf16[2,2,80,256]{3,2,1,0:T(8,128)(2,1)S(1)}, u32[]{:S(2)}, u32[]{:S(2)}) collective-permute-start(bf16[2,2,80,256]{3,2,1,0:T(8,128)(2,1)S(1)} %pad_maximum_fusion.2), channel_id=1, source_target_pairs={{0,16},{16,0},{1,17},{17,1},{2,18},{18,2},{3,19},{19,3},{4,20},{20... | collective-permute-start | bytes 491528 | tf_op jit(solution)/shard_map/ppermute | solution.py:163
  43.8 2.1 %collective-permute-start.14 = (bf16[2,2,80,256]{3,2,1,0:T(8,128)(2,1)S(1)}, bf16[2,2,80,256]{3,2,1,0:T(8,128)(2,1)S(1)}, u32[]{:S(2)}, u32[]{:S(2)}) collective-permute-start(bf16[2,2,80,256]{3,2,1,0:T(8,128)(2,1)S(1)} %pad_maximum_fusion.1), channel_id=1, source_target_pairs={{0,4},{1,5},{2,6},{3,7},{4,0},{5,1},{6,2},{7,3},{8,12},{9,13},{10,... | collective-permute-start | bytes 491528 | tf_op jit(solution)/shard_map/ppermute | solution.py:160
  45.9 1.4 %collective-permute-start.12 = (bf16[2,2,80,256]{3,2,1,0:T(8,128)(2,1)S(1)}, bf16[2,2,80,256]{3,2,1,0:T(8,128)(2,1)S(1)}, u32[]{:S(2)}, u32[]{:S(2)}) collective-permute-start(bf16[2,2,80,256]{3,2,1,0:T(8,128)(2,1)S(1)} %pad_maximum_fusion), channel_id=1, source_target_pairs={{0,2},{1,3},{2,0},{3,1},{4,6},{5,7},{6,4},{7,5},{8,10},{9,11},{10,... | collective-permute-start | bytes 491528 | tf_op jit(solution)/shard_map/ppermute | solution.py:160
  47.3 0.9 %collective-permute-done.16 = bf16[2,2,80,256]{3,2,1,0:T(8,128)(2,1)S(1)} collective-permute-done((bf16[2,2,80,256]{3,2,1,0:T(8,128)(2,1)S(1)}, bf16[2,2,80,256]{3,2,1,0:T(8,128)(2,1)S(1)}, u32[]{:S(2)}, u32[]{:S(2)}) %collective-permute-start.16) | collective-permute-done | bytes 163872 | tf_op jit(solution)/shard_map/ppermute | solution.py:163
  48.3 1.4 %collective-permute-start.17 = (bf16[4,2,80,256]{3,2,1,0:T(8,128)(2,1)S(1)}, bf16[4,2,80,256]{3,2,1,0:T(8,128)(2,1)S(1)}, u32[]{:S(2)}, u32[]{:S(2)}) collective-permute-start(bf16[4,2,80,256]{3,2,1,0:T(8,128)(2,1)S(1)} %constant_dynamic-update-slice_fusion.7.refs_4_), channel_id=1, source_target_pairs={{0,2},{1,3},{2,0},{3,1},{4,6},{5,7},{6,4},{7,5},{8,10},{9,11},{10,... | collective-permute-start | bytes 983048 | tf_op jit(solution)/shard_map/ppermute | solution.py:160
  49.7 0.9 %collective-permute-start.15 = (bf16[4,2,80,256]{3,2,1,0:T(8,128)(2,1)S(1)}, bf16[4,2,80,256]{3,2,1,0:T(8,128)(2,1)S(1)}, u32[]{:S(2)}, u32[]{:S(2)}) collective-permute-start(bf16[4,2,80,256]{3,2,1,0:T(8,128)(2,1)S(1)} %constant_dynamic-update-slice_fusion.5.refs_0_), channel_id=1, source_target_pairs={{0,16},{16,0},{1,17},{17,1},{2,18},{18,2},{3,19},{19,3},{4,20},{20... | collective-permute-start | bytes 983048 | tf_op jit(solution)/shard_map/ppermute | solution.py:163
  50.6 2.3 %collective-permute-done.12 = bf16[2,2,80,256]{3,2,1,0:T(8,128)(2,1)S(1)} collective-permute-done((bf16[2,2,80,256]{3,2,1,0:T(8,128)(2,1)S(1)}, bf16[2,2,80,256]{3,2,1,0:T(8,128)(2,1)S(1)}, u32[]{:S(2)}, u32[]{:S(2)}) %collective-permute-start.12) | collective-permute-done | bytes 163872 | tf_op jit(solution)/shard_map/ppermute | solution.py:160
  53.0 0.1 collective-permute-start.13
  53.1 0.1 collective-permute-start.18
  53.1 0.0 copy-start.2
  53.2 11.1 %all_to_all.10.start = f32[32,4,128]{2,1,0:T(4,128)S(1)} all-to-all(f32[32,4,128]{2,1,0:T(4,128)S(1)} %bitcast.8), channel_id=1, replica_groups=mesh['row'=2,'col'=16] {'row','col'}, dimensions={0} | all-to-all | bytes 131072 | tf_op jit(solution)/shard_map/all_to_all | solution.py:256
  64.3 0.2 collective-permute-start.19
  64.5 0.4 collective-permute-start.22
  64.9 0.1 collective-permute-start.20
  65.0 0.4 collective-permute-start.21
  65.4 0.1 collective-permute-start.23
  65.5 0.5 collective-permute-done.19.refs_3_
  66.0 1.9 %chain0.1.start = f32[8,2048]{1,0:T(8,128)S(1)} custom-call(s32[6]{0:T(128)S(1)} %copy-done.2, f32[32,4,128]{2,1,0:T(4,128)S(1)} %all_to_all.10.start, bf16[4,2,80,256]{3,2,1,0:T(8,128)(2,1)S(1)} %constant_dynamic-update-slice_fusion.3.refs_0_, bf16[4,2,80,256]{3,2,1,0:T(8,128)(2,1)S(1)} %collective-permute-done.13.refs_1_, ...), custom_call_target="tpu_custom_call" | custom-call | flops 67108864 | bytes 1310720 | tf_op jit(solution)/shard_map/chain0/pallas_call | solution.py:274
  67.9 3.8 %chain1.1 = bf16[4,2048]{1,0:T(4,128)(2,1)} custom-call(s32[6]{0:T(128)S(1)} %copy-done.2, f32[8,2048]{1,0:T(8,128)S(1)} %chain0.1.start, bf16[4,2,80,256]{3,2,1,0:T(8,128)(2,1)S(1)} %constant_dynamic-update-slice_fusion.5.refs_0_, bf16[4,2,80,256]{3,2,1,0:T(8,128)(2,1)S(1)} %collective-permute-done.15.refs_1_, ...), custom_call_target="tpu_custom_call" | custom-call | flops 134217728 | bytes 2621440 | tf_op jit(solution)/shard_map/chain1/pallas_call | solution.py:274
  (32 shorter events, 0.2 us)
Async XLA Ops:
  1.7 5.4 %copy-start.3 = (bf16[64,512]{1,0:T(8,128)(2,1)S(1)}, bf16[64,512]{1,0:T(8,128)(2,1)}, u32[]{:S(2)}) copy-start(bf16[64,512]{1,0:T(8,128)(2,1)} %param.7) | copy-start | bytes 196612
  1.7 13.5 %all-to-all-start = ((bf16[8,80,256]{2,1,0:T(8,128)(2,1)}), bf16[8,80,256]{2,1,0:T(8,128)(2,1)S(1)}, u32[]{:S(2)}, u32[]{:S(2)}) async-start(bf16[8,80,256]{2,1,0:T(8,128)(2,1)} %pack.1), calls=%async_computation | async-start | bytes 655360 | tf_op jit(solution)/shard_map/all_to_all | solution.py:183
  7.1 6.1 %collective-permute-start.5 = (bf16[64,512]{1,0:T(8,128)(2,1)S(1)}, bf16[64,512]{1,0:T(8,128)(2,1)S(1)}, u32[]{:S(2)}, u32[]{:S(2)}) collective-permute-start(bf16[64,512]{1,0:T(8,128)(2,1)S(1)} %copy-done.3), channel_id=1, source_target_pairs={{0,8},{1,9},{2,10},{3,11},{4,12},{5,13},{6,14},{7,15},{8,0},{9,1},... | collective-permute-start | bytes 196616 | tf_op jit(solution)/shard_map/ppermute | solution.py:160
  13.2 2.0 %copy-start.1 = (s32[6]{0:T(128)S(1)}, s32[6]{0:T(128)}, u32[]{:S(2)}) copy-start(s32[6]{0:T(128)} %owners.3) | copy-start | bytes 76
  13.3 5.8 %collective-permute-start.6 = (bf16[64,512]{1,0:T(8,128)(2,1)S(1)}, bf16[64,512]{1,0:T(8,128)(2,1)S(1)}, u32[]{:S(2)}, u32[]{:S(2)}) collective-permute-start(bf16[64,512]{1,0:T(8,128)(2,1)S(1)} %get-tuple-element.36), channel_id=1, source_target_pairs={{0,16},{16,0},{1,17},{17,1},{2,18},{18,2},{3,19},{19,3},{4,20},{20... | collective-permute-start | bytes 196616 | tf_op jit(solution)/shard_map/ppermute | solution.py:163
  16.0 4.7 %collective-permute-start.4 = (bf16[16,256]{1,0:T(8,128)(2,1)S(1)}, bf16[16,256]{1,0:T(8,128)(2,1)S(1)}, u32[]{:S(2)}, u32[]{:S(2)}) collective-permute-start(bf16[16,256]{1,0:T(8,128)(2,1)S(1)} %slice_bitcast_fusion), channel_id=1, source_target_pairs={{0,8},{1,9},{2,10},{3,11},{4,12},{5,13},{6,14},{7,15},{8,0},{9,1},... | collective-permute-start | bytes 24584 | tf_op jit(solution)/shard_map/ppermute | solution.py:160
  20.7 6.4 %collective-permute-start.7 = (bf16[2,64,512]{2,1,0:T(8,128)(2,1)S(1)}, bf16[2,64,512]{2,1,0:T(8,128)(2,1)S(1)}, u32[]{:S(2)}, u32[]{:S(2)}) collective-permute-start(bf16[2,64,512]{2,1,0:T(8,128)(2,1)S(1)} %pad_maximum_fusion.3.refs_0_), channel_id=1, source_target_pairs={{0,2},{1,3},{2,0},{3,1},{4,6},{5,7},{6,4},{7,5},{8,10},{9,11},{10,... | collective-permute-start | bytes 393224 | tf_op jit(solution)/shard_map/ppermute | solution.py:160
  22.3 8.1 %collective-permute-start.8 = (bf16[2,64,512]{2,1,0:T(8,128)(2,1)S(1)}, bf16[2,64,512]{2,1,0:T(8,128)(2,1)S(1)}, u32[]{:S(2)}, u32[]{:S(2)}) collective-permute-start(bf16[2,64,512]{2,1,0:T(8,128)(2,1)S(1)} %pad_maximum_fusion.3.refs_0_), channel_id=1, source_target_pairs={{0,4},{1,5},{2,6},{3,7},{4,0},{5,1},{6,2},{7,3},{8,12},{9,13},{10,... | collective-permute-start | bytes 393224 | tf_op jit(solution)/shard_map/ppermute | solution.py:160
  26.3 9.6 %collective-permute-start = (bf16[5,80,256]{2,1,0:T(8,128)(2,1)S(1)}, bf16[5,80,256]{2,1,0:T(8,128)(2,1)S(1)}, u32[]{:S(2)}, u32[]{:S(2)}) collective-permute-start(bf16[5,80,256]{2,1,0:T(8,128)(2,1)S(1)} %pick.1), channel_id=1, source_target_pairs={{0,8},{1,9},{2,10},{3,11},{4,12},{5,13},{6,14},{7,15},{8,0},{9,1},... | collective-permute-start | bytes 614408 | tf_op jit(solution)/shard_map/ppermute | solution.py:160
  26.3 10.3 %collective-permute-start.9 = (bf16[2,64,512]{2,1,0:T(8,128)(2,1)S(1)}, bf16[2,64,512]{2,1,0:T(8,128)(2,1)S(1)}, u32[]{:S(2)}, u32[]{:S(2)}) collective-permute-start(bf16[2,64,512]{2,1,0:T(8,128)(2,1)S(1)} %pad_maximum_fusion.3.refs_0_), channel_id=1, source_target_pairs={{0,6},{1,7},{2,4},{3,5},{4,2},{5,3},{6,0},{7,1},{8,14},{9,15},{10,... | collective-permute-start | bytes 393224 | tf_op jit(solution)/shard_map/ppermute | solution.py:160
  27.1 15.3 %copy-start = (bf16[4096,128]{1,0:T(8,128)(2,1)S(1)}, bf16[4096,128]{1,0:T(8,128)(2,1)}, u32[]{:S(2)}) copy-start(bf16[4096,128]{1,0:T(8,128)(2,1)} %sub.6) | copy-start | bytes 3145732
  36.5 4.5 %collective-permute-start.3 = (bf16[1,2,80,256]{3,2,1,0:T(8,128)(2,1)S(1)}, bf16[1,2,80,256]{3,2,1,0:T(8,128)(2,1)S(1)}, u32[]{:S(2)}, u32[]{:S(2)}) collective-permute-start(bf16[1,2,80,256]{3,2,1,0:T(8,128)(2,1)S(1)} %get-tuple-element.23), channel_id=1, source_target_pairs={{0,4},{1,5},{2,6},{3,7},{4,0},{5,1},{6,2},{7,3},{8,12},{9,13},{10,... | collective-permute-start | bytes 245768 | tf_op jit(solution)/shard_map/ppermute | solution.py:160
  36.7 5.7 %collective-permute-start.11 = (bf16[6,64,512]{2,1,0:T(8,128)(2,1)S(1)}, bf16[6,64,512]{2,1,0:T(8,128)(2,1)S(1)}, u32[]{:S(2)}, u32[]{:S(2)}) collective-permute-start(bf16[6,64,512]{2,1,0:T(8,128)(2,1)S(1)} %constant_dynamic-update-slice_fusion.refs_1_), channel_id=1, source_target_pairs={{0,1},{1,0},{2,3},{3,2},{4,5},{5,4},{6,7},{7,6},{8,9},{9,8},{10,11... | collective-permute-start | bytes 1179656 | tf_op jit(solution)/shard_map/ppermute | solution.py:160
  36.7 5.6 %collective-permute-start.10 = (bf16[2,64,512]{2,1,0:T(8,128)(2,1)S(1)}, bf16[2,64,512]{2,1,0:T(8,128)(2,1)S(1)}, u32[]{:S(2)}, u32[]{:S(2)}) collective-permute-start(bf16[2,64,512]{2,1,0:T(8,128)(2,1)S(1)} %pad_maximum_fusion.3.refs_0_), channel_id=1, source_target_pairs={{0,1},{1,0},{2,3},{3,2},{4,5},{5,4},{6,7},{7,6},{8,9},{9,8},{10,11... | collective-permute-start | bytes 393224 | tf_op jit(solution)/shard_map/ppermute | solution.py:160
  37.2 4.4 %collective-permute-start.2 = (bf16[1,2,80,256]{3,2,1,0:T(8,128)(2,1)S(1)}, bf16[1,2,80,256]{3,2,1,0:T(8,128)(2,1)S(1)}, u32[]{:S(2)}, u32[]{:S(2)}) collective-permute-start(bf16[1,2,80,256]{3,2,1,0:T(8,128)(2,1)S(1)} %get-tuple-element.22), channel_id=1, source_target_pairs={{0,2},{1,3},{2,0},{3,1},{4,6},{5,7},{6,4},{7,5},{8,10},{9,11},{10,... | collective-permute-start | bytes 245768 | tf_op jit(solution)/shard_map/ppermute | solution.py:160
  37.9 4.4 %collective-permute-start.1 = (bf16[1,2,80,256]{3,2,1,0:T(8,128)(2,1)S(1)}, bf16[1,2,80,256]{3,2,1,0:T(8,128)(2,1)S(1)}, u32[]{:S(2)}, u32[]{:S(2)}) collective-permute-start(bf16[1,2,80,256]{3,2,1,0:T(8,128)(2,1)S(1)} %get-tuple-element.21), channel_id=1, source_target_pairs={{0,16},{16,0},{1,17},{17,1},{2,18},{18,2},{3,19},{19,3},{4,20},{20... | collective-permute-start | bytes 245768 | tf_op jit(solution)/shard_map/ppermute | solution.py:163
  42.9 5.4 %collective-permute-start.16 = (bf16[2,2,80,256]{3,2,1,0:T(8,128)(2,1)S(1)}, bf16[2,2,80,256]{3,2,1,0:T(8,128)(2,1)S(1)}, u32[]{:S(2)}, u32[]{:S(2)}) collective-permute-start(bf16[2,2,80,256]{3,2,1,0:T(8,128)(2,1)S(1)} %pad_maximum_fusion.2), channel_id=1, source_target_pairs={{0,16},{16,0},{1,17},{17,1},{2,18},{18,2},{3,19},{19,3},{4,20},{20... | collective-permute-start | bytes 491528 | tf_op jit(solution)/shard_map/ppermute | solution.py:163
  43.8 5.9 %collective-permute-start.14 = (bf16[2,2,80,256]{3,2,1,0:T(8,128)(2,1)S(1)}, bf16[2,2,80,256]{3,2,1,0:T(8,128)(2,1)S(1)}, u32[]{:S(2)}, u32[]{:S(2)}) collective-permute-start(bf16[2,2,80,256]{3,2,1,0:T(8,128)(2,1)S(1)} %pad_maximum_fusion.1), channel_id=1, source_target_pairs={{0,4},{1,5},{2,6},{3,7},{4,0},{5,1},{6,2},{7,3},{8,12},{9,13},{10,... | collective-permute-start | bytes 491528 | tf_op jit(solution)/shard_map/ppermute | solution.py:160
  45.9 7.1 %collective-permute-start.12 = (bf16[2,2,80,256]{3,2,1,0:T(8,128)(2,1)S(1)}, bf16[2,2,80,256]{3,2,1,0:T(8,128)(2,1)S(1)}, u32[]{:S(2)}, u32[]{:S(2)}) collective-permute-start(bf16[2,2,80,256]{3,2,1,0:T(8,128)(2,1)S(1)} %pad_maximum_fusion), channel_id=1, source_target_pairs={{0,2},{1,3},{2,0},{3,1},{4,6},{5,7},{6,4},{7,5},{8,10},{9,11},{10,... | collective-permute-start | bytes 491528 | tf_op jit(solution)/shard_map/ppermute | solution.py:160
  48.3 16.0 %collective-permute-start.17 = (bf16[4,2,80,256]{3,2,1,0:T(8,128)(2,1)S(1)}, bf16[4,2,80,256]{3,2,1,0:T(8,128)(2,1)S(1)}, u32[]{:S(2)}, u32[]{:S(2)}) collective-permute-start(bf16[4,2,80,256]{3,2,1,0:T(8,128)(2,1)S(1)} %constant_dynamic-update-slice_fusion.7.refs_4_), channel_id=1, source_target_pairs={{0,2},{1,3},{2,0},{3,1},{4,6},{5,7},{6,4},{7,5},{8,10},{9,11},{10,... | collective-permute-start | bytes 983048 | tf_op jit(solution)/shard_map/ppermute | solution.py:160
  49.7 14.6 %collective-permute-start.15 = (bf16[4,2,80,256]{3,2,1,0:T(8,128)(2,1)S(1)}, bf16[4,2,80,256]{3,2,1,0:T(8,128)(2,1)S(1)}, u32[]{:S(2)}, u32[]{:S(2)}) collective-permute-start(bf16[4,2,80,256]{3,2,1,0:T(8,128)(2,1)S(1)} %constant_dynamic-update-slice_fusion.5.refs_0_), channel_id=1, source_target_pairs={{0,16},{16,0},{1,17},{17,1},{2,18},{18,2},{3,19},{19,3},{4,20},{20... | collective-permute-start | bytes 983048 | tf_op jit(solution)/shard_map/ppermute | solution.py:163
  53.0 11.3 %collective-permute-start.13 = (bf16[4,2,80,256]{3,2,1,0:T(8,128)(2,1)S(1)}, bf16[4,2,80,256]{3,2,1,0:T(8,128)(2,1)S(1)}, u32[]{:S(2)}, u32[]{:S(2)}) collective-permute-start(bf16[4,2,80,256]{3,2,1,0:T(8,128)(2,1)S(1)} %constant_dynamic-update-slice_fusion.3.refs_0_), channel_id=1, source_target_pairs={{0,4},{1,5},{2,6},{3,7},{4,0},{5,1},{6,2},{7,3},{8,12},{9,13},{10,... | collective-permute-start | bytes 983048 | tf_op jit(solution)/shard_map/ppermute | solution.py:160
  53.1 12.3 %collective-permute-start.18 = (bf16[4,2,80,256]{3,2,1,0:T(8,128)(2,1)S(1)}, bf16[4,2,80,256]{3,2,1,0:T(8,128)(2,1)S(1)}, u32[]{:S(2)}, u32[]{:S(2)}) collective-permute-start(bf16[4,2,80,256]{3,2,1,0:T(8,128)(2,1)S(1)} %constant_dynamic-update-slice_fusion.3.refs_0_), channel_id=1, source_target_pairs={{0,1},{1,0},{2,3},{3,2},{4,5},{5,4},{6,7},{7,6},{8,9},{9,8},{10,11... | collective-permute-start | bytes 983048 | tf_op jit(solution)/shard_map/ppermute | solution.py:160
  53.1 12.8 %copy-start.2 = (s32[6]{0:T(128)S(1)}, s32[6]{0:T(128)}, u32[]{:S(2)}) copy-start(s32[6]{0:T(128)} %offsets.3) | copy-start | bytes 76
  64.3 1.7 %collective-permute-start.19 = (bf16[4,2,80,256]{3,2,1,0:T(8,128)(2,1)S(1)}, bf16[4,2,80,256]{3,2,1,0:T(8,128)(2,1)S(1)}, u32[]{:S(2)}, u32[]{:S(2)}) collective-permute-start(bf16[4,2,80,256]{3,2,1,0:T(8,128)(2,1)S(1)} %collective-permute-done.13.refs_1_), channel_id=1, source_target_pairs={{0,1},{1,0},{2,3},{3,2},{4,5},{5,4},{6,7},{7,6},{8,9},{9,8},{10,11... | collective-permute-start | bytes 983048 | tf_op jit(solution)/shard_map/ppermute | solution.py:160
  64.5 3.4 %collective-permute-start.22 = (bf16[4,2,80,256]{3,2,1,0:T(8,128)(2,1)S(1)}, bf16[4,2,80,256]{3,2,1,0:T(8,128)(2,1)S(1)}, u32[]{:S(2)}, u32[]{:S(2)}) collective-permute-start(bf16[4,2,80,256]{3,2,1,0:T(8,128)(2,1)S(1)} %constant_dynamic-update-slice_fusion.7.refs_4_), channel_id=1, source_target_pairs={{0,1},{1,0},{2,3},{3,2},{4,5},{5,4},{6,7},{7,6},{8,9},{9,8},{10,11... | collective-permute-start | bytes 983048 | tf_op jit(solution)/shard_map/ppermute | solution.py:160
  64.9 3.0 %collective-permute-start.20 = (bf16[4,2,80,256]{3,2,1,0:T(8,128)(2,1)S(1)}, bf16[4,2,80,256]{3,2,1,0:T(8,128)(2,1)S(1)}, u32[]{:S(2)}, u32[]{:S(2)}) collective-permute-start(bf16[4,2,80,256]{3,2,1,0:T(8,128)(2,1)S(1)} %constant_dynamic-update-slice_fusion.5.refs_0_), channel_id=1, source_target_pairs={{0,1},{1,0},{2,3},{3,2},{4,5},{5,4},{6,7},{7,6},{8,9},{9,8},{10,11... | collective-permute-start | bytes 983048 | tf_op jit(solution)/shard_map/ppermute | solution.py:160
  65.0 2.9 %collective-permute-start.21 = (bf16[4,2,80,256]{3,2,1,0:T(8,128)(2,1)S(1)}, bf16[4,2,80,256]{3,2,1,0:T(8,128)(2,1)S(1)}, u32[]{:S(2)}, u32[]{:S(2)}) collective-permute-start(bf16[4,2,80,256]{3,2,1,0:T(8,128)(2,1)S(1)} %collective-permute-done.15.refs_1_), channel_id=1, source_target_pairs={{0,1},{1,0},{2,3},{3,2},{4,5},{5,4},{6,7},{7,6},{8,9},{9,8},{10,11... | collective-permute-start | bytes 983048 | tf_op jit(solution)/shard_map/ppermute | solution.py:160
  65.4 2.5 %collective-permute-start.23 = (bf16[4,2,80,256]{3,2,1,0:T(8,128)(2,1)S(1)}, bf16[4,2,80,256]{3,2,1,0:T(8,128)(2,1)S(1)}, u32[]{:S(2)}, u32[]{:S(2)}) collective-permute-start(bf16[4,2,80,256]{3,2,1,0:T(8,128)(2,1)S(1)} %collective-permute-done.17.refs_5_), channel_id=1, source_target_pairs={{0,1},{1,0},{2,3},{3,2},{4,5},{5,4},{6,7},{7,6},{8,9},{9,8},{10,11... | collective-permute-start | bytes 983048 | tf_op jit(solution)/shard_map/ppermute | solution.py:160

commit v16 on v15

--- a/solution.py
+++ b/solution.py
@@ -80,7 +80,7 @@
         outs[group // each][0, group % each] = piece
 
 
-def merge_kernel(rows, cols, tags, ready, sub, *refs):
+def merge_kernel(rows, cols, tags, sub, *refs):
     held, total = refs[:-1], refs[-1]
     row, col = lax.axis_index("row"), lax.axis_index("col")
     deep, tall = held[0].shape[2], held[0].shape[1]
@@ -168,6 +168,8 @@
     pv, pt = group_rows // SLICES, reflect // SLICES
     piece = (pv + pt, reflect)
 
+    across = [merge_factor] + [over_col(merge_factor, m * share) for m in range(1, rows)]
+
     packed = pl.pallas_call(
         pack_kernel,
         out_shape=jax.ShapeDtypeStruct((HALF,) + piece, dtype),
@@ -178,9 +180,20 @@
         cost_estimate=cost([basis, factor]),
         name="pack",
     )(basis.reshape(SLICES, pv, reflect), factor.reshape(SLICES, pt, reflect))
-    packed, merge_factor = lax.optimization_barrier((packed, merge_factor))
     members = [[h * HALF + c for c in range(HALF)] for h in range(halves)]
     slices = lax.all_to_all(packed, "col", 0, 0, axis_index_groups=members)
+
+    row, top = lax.axis_index("row"), lax.axis_index("col") // share
+
+    def for_row(mask):
+        index = top ^ row ^ mask
+        block = across[0]
+        for k in range(1, rows):
+            block = jnp.where(index == k, across[k], block)
+        return block
+
+    m_held = jnp.stack([for_row(0)] + [over_row(for_row(m), m) for m in range(1, rows)])
+    slices, m_held = lax.optimization_barrier((slices, m_held))
 
     picked = pl.pallas_call(
         pick_kernel,
@@ -191,22 +204,8 @@
         cost_estimate=cost([slices]),
         name="pick",
     )(owners, slices)
-    ready = over_col(picked[0, :16], HALF)
     others = [over_col(picked, m * HALF) for m in range(1, halves)]
 
-    across = [merge_factor] + [over_col(merge_factor, m * share) for m in range(1, rows)]
-
-    row, top = lax.axis_index("row"), lax.axis_index("col") // share
-
-    def for_row(mask):
-        index = top ^ row ^ mask
-        block = across[0]
-        for k in range(1, rows):
-            block = jnp.where(index == k, across[k], block)
-        return block
-
-    m_held = jnp.stack([for_row(0)] + [over_row(for_row(m), m) for m in range(1, rows)])
-    ready, m_held = lax.optimization_barrier((ready, m_held))
     tags = [(m, 0) for m in range(rows)]
     bit = share // 2
     while bit > 4:
@@ -223,12 +222,12 @@
     merged = pl.pallas_call(
         functools.partial(merge_kernel, rows, cols, tags),
         out_shape=jax.ShapeDtypeStruct((wanted, width), jnp.float32),
-        in_specs=[HBM, VMEM] + [VMEM] * len(m_held),
+        in_specs=[VMEM] + [VMEM] * len(m_held),
         out_specs=VMEM,
         compiler_params=limit(8),
         cost_estimate=cost([sub_vectors], 2 * wanted * sub_vectors.size),
         name="merge",
-    )(ready, sub_vectors, *m_held)
+    )(sub_vectors, *m_held)
     per = GROUPS // COLOURS
     colours = pl.pallas_call(
         order_kernel,

time: 72 us -> 71.3 us (level)
  waiting for transfers between devices: 21.6 us -> 24.1 us
  starting transfers between devices: 29.4 us -> 27.3 us
  blocking collectives: 11.1 us -> 10 us
    ppermute x4, waiting for transfers between devices: 1.58 us -> 5.11 us  [over_row(): return lax.ppermute(x, 'row', [(r, r ^ mask) for r in range(rows)])]
    ppermute x20 -> x19, starting transfers between devices: 19.7 us -> 16.6 us  [over_col(): return lax.ppermute(x, 'col', [(c, c ^ mask) for c in range(cols)])]
    all_to_all x1, blocking collectives: 11.1 us -> 10 us  [local(): lax.all_to_all(merged.reshape(rows * cols, each, width), ('row', 'col'),...]
    ppermute x4, starting transfers between devices: 4.25 us -> 5.34 us  [over_row(): return lax.ppermute(x, 'row', [(r, r ^ mask) for r in range(rows)])]
    ppermute x20 -> x19, waiting for transfers between devices: 19.6 us -> 19 us  [over_col(): return lax.ppermute(x, 'col', [(c, c ^ mask) for c in range(cols)])]
  transfers between devices with their start and end apart: 25 -> 24, of which waited for: 11 -> 11; matrix products, arithmetic and copies ran while one was open for 0% -> 0% of each run, Pallas kernels for 4% -> 5%
where the time goes in v16:
time: 71.3 us; the launch traced here: 71.1 us
  starting transfers between devices  27.3 us (38%)
  waiting for transfers between devices  24.1 us (34%)
  blocking collectives  10 us (14%)
  Pallas kernels  9.14 us (13%)
    ppermute x19, waiting for transfers between devices, over_col(): return lax.ppermute(x, 'col', [(c, c ^ mask) for c in range(cols)])  19 us
    ppermute x19, starting transfers between devices, over_col(): return lax.ppermute(x, 'col', [(c, c ^ mask) for c in range(cols)])  16.6 us
    all_to_all x1, blocking collectives, local(): lax.all_to_all(merged.reshape(rows * cols, each, width), ('row', 'col'),...  10 us
    pallas_call x2, Pallas kernels, local(): pl.pallas_call(functools.partial(chain_kernel, cols, groups, slots, sum((...  5.68 us
    all_to_all x1, starting transfers between devices, local(): slices = lax.all_to_all(packed, 'col', 0, 0, axis_index_groups=members)  5.4 us
    ppermute x4, starting transfers between devices, over_row(): return lax.ppermute(x, 'row', [(r, r ^ mask) for r in range(rows)])  5.34 us
    ppermute x4, waiting for transfers between devices, over_row(): return lax.ppermute(x, 'row', [(r, r ^ mask) for r in range(rows)])  5.11 us
    pallas_call x1, Pallas kernels, local(): pl.pallas_call(pack_kernel, out_shape=jax.ShapeDtypeStruct((HALF,) + piec...  1.69 us
  transfers between devices with their start and end apart: 24, of which 11 were waited for; matrix products, arithmetic and copies ran while one was open for 0% of the time, Pallas kernels for 5%

profile of v16, /device:TPU:0, one launch (start us, length us, event | category | flops | bytes accessed | tf_op | source)
XLA Modules:
  0.0 71.1 jit_solution(7351349782278061931)
XLA Ops:
  0.0 1.7 %pack.1 = bf16[8,80,256]{2,1,0:T(8,128)(2,1)} custom-call(bf16[16,64,256]{2,1,0:T(8,128)(2,1)} %bitcast.7, bf16[16,16,256]{2,1,0:T(8,128)(2,1)} %bitcast.8), custom_call_target="tpu_custom_call" | custom-call | bytes 655360 | tf_op jit(solution)/shard_map/pack/pallas_call | solution.py:173
  1.7 0.0 copy-start.3
  1.7 5.4 %all-to-all-start = ((bf16[8,80,256]{2,1,0:T(8,128)(2,1)}), bf16[8,80,256]{2,1,0:T(8,128)(2,1)S(1)}, u32[]{:S(2)}, u32[]{:S(2)}) async-start(bf16[8,80,256]{2,1,0:T(8,128)(2,1)} %pack.1), calls=%async_computation | async-start | bytes 655360 | tf_op jit(solution)/shard_map/all_to_all | solution.py:184
  7.1 2.7 %collective-permute-start = (bf16[64,512]{1,0:T(8,128)(2,1)S(1)}, bf16[64,512]{1,0:T(8,128)(2,1)S(1)}, u32[]{:S(2)}, u32[]{:S(2)}) collective-permute-start(bf16[64,512]{1,0:T(8,128)(2,1)S(1)} %copy-done.3), channel_id=1, source_target_pairs={{0,8},{1,9},{2,10},{3,11},{4,12},{5,13},{6,14},{7,15},{8,0},{9,1},... | collective-permute-start | bytes 196616 | tf_op jit(solution)/shard_map/ppermute | solution.py:160
  9.8 3.4 %collective-permute-done = bf16[64,512]{1,0:T(8,128)(2,1)S(1)} collective-permute-done((bf16[64,512]{1,0:T(8,128)(2,1)S(1)}, bf16[64,512]{1,0:T(8,128)(2,1)S(1)}, u32[]{:S(2)}, u32[]{:S(2)}) %collective-permute-start) | collective-permute-done | bytes 65568 | tf_op jit(solution)/shard_map/ppermute | solution.py:160
  13.2 1.6 %collective-permute-start.1 = (bf16[64,512]{1,0:T(8,128)(2,1)S(1)}, bf16[64,512]{1,0:T(8,128)(2,1)S(1)}, u32[]{:S(2)}, u32[]{:S(2)}) collective-permute-start(bf16[64,512]{1,0:T(8,128)(2,1)S(1)} %get-tuple-element.32), channel_id=1, source_target_pairs={{0,16},{16,0},{1,17},{17,1},{2,18},{18,2},{3,19},{19,3},{4,20},{20... | collective-permute-start | bytes 196616 | tf_op jit(solution)/shard_map/ppermute | solution.py:163
  14.8 2.8 %collective-permute-done.1 = bf16[64,512]{1,0:T(8,128)(2,1)S(1)} collective-permute-done((bf16[64,512]{1,0:T(8,128)(2,1)S(1)}, bf16[64,512]{1,0:T(8,128)(2,1)S(1)}, u32[]{:S(2)}, u32[]{:S(2)}) %collective-permute-start.1) | collective-permute-done | bytes 65568 | tf_op jit(solution)/shard_map/ppermute | solution.py:163
  17.6 1.7 %collective-permute-start.6 = (bf16[2,64,512]{2,1,0:T(8,128)(2,1)S(1)}, bf16[2,64,512]{2,1,0:T(8,128)(2,1)S(1)}, u32[]{:S(2)}, u32[]{:S(2)}) collective-permute-start(bf16[2,64,512]{2,1,0:T(8,128)(2,1)S(1)} %pad_maximum_fusion.3.refs_0_), channel_id=1, source_target_pairs={{0,2},{1,3},{2,0},{3,1},{4,6},{5,7},{6,4},{7,5},{8,10},{9,11},{10,... | collective-permute-start | bytes 393224 | tf_op jit(solution)/shard_map/ppermute | solution.py:160
  19.3 4.5 %collective-permute-start.7 = (bf16[2,64,512]{2,1,0:T(8,128)(2,1)S(1)}, bf16[2,64,512]{2,1,0:T(8,128)(2,1)S(1)}, u32[]{:S(2)}, u32[]{:S(2)}) collective-permute-start(bf16[2,64,512]{2,1,0:T(8,128)(2,1)S(1)} %pad_maximum_fusion.3.refs_0_), channel_id=1, source_target_pairs={{0,4},{1,5},{2,6},{3,7},{4,0},{5,1},{6,2},{7,3},{8,12},{9,13},{10,... | collective-permute-start | bytes 393224 | tf_op jit(solution)/shard_map/ppermute | solution.py:160
  23.8 0.0 collective-permute-start.8
  23.8 0.7 pick.1
  24.5 0.9 %collective-permute-start.2 = (bf16[5,80,256]{2,1,0:T(8,128)(2,1)S(1)}, bf16[5,80,256]{2,1,0:T(8,128)(2,1)S(1)}, u32[]{:S(2)}, u32[]{:S(2)}) collective-permute-start(bf16[5,80,256]{2,1,0:T(8,128)(2,1)S(1)} %pick.1), channel_id=1, source_target_pairs={{0,8},{1,9},{2,10},{3,11},{4,12},{5,13},{6,14},{7,15},{8,0},{9,1},... | collective-permute-start | bytes 614408 | tf_op jit(solution)/shard_map/ppermute | solution.py:160
  25.4 0.0 collective-permute-done.6
  25.4 0.0 copy-start
  25.4 3.9 %collective-permute-done.7 = bf16[2,64,512]{2,1,0:T(8,128)(2,1)S(1)} collective-permute-done((bf16[2,64,512]{2,1,0:T(8,128)(2,1)S(1)}, bf16[2,64,512]{2,1,0:T(8,128)(2,1)S(1)}, u32[]{:S(2)}, u32[]{:S(2)}) %collective-permute-start.7) | collective-permute-done | bytes 131104 | tf_op jit(solution)/shard_map/ppermute | solution.py:160
  29.3 5.6 %collective-permute-done.2.refs_0_ = bf16[5,80,256]{2,1,0:T(8,128)(2,1)S(1)} collective-permute-done((bf16[5,80,256]{2,1,0:T(8,128)(2,1)S(1)}, bf16[5,80,256]{2,1,0:T(8,128)(2,1)S(1)}, u32[]{:S(2)}, u32[]{:S(2)}) %collective-permute-start.2) | collective-permute-done | bytes 204832 | tf_op jit(solution)/shard_map/ppermute | solution.py:160
  34.9 0.6 order.1
  35.6 0.1 collective-permute-start.5
  35.6 0.0 collective-permute-done.8
  35.7 0.1 collective-permute-start.10
  35.7 0.5 collective-permute-start.9
  36.2 1.4 %collective-permute-start.4 = (bf16[1,2,80,256]{3,2,1,0:T(8,128)(2,1)S(1)}, bf16[1,2,80,256]{3,2,1,0:T(8,128)(2,1)S(1)}, u32[]{:S(2)}, u32[]{:S(2)}) collective-permute-start(bf16[1,2,80,256]{3,2,1,0:T(8,128)(2,1)S(1)} %get-tuple-element.20), channel_id=1, source_target_pairs={{0,2},{1,3},{2,0},{3,1},{4,6},{5,7},{6,4},{7,5},{8,10},{9,11},{10,... | collective-permute-start | bytes 245768 | tf_op jit(solution)/shard_map/ppermute | solution.py:160
  37.6 1.5 %collective-permute-start.3 = (bf16[1,2,80,256]{3,2,1,0:T(8,128)(2,1)S(1)}, bf16[1,2,80,256]{3,2,1,0:T(8,128)(2,1)S(1)}, u32[]{:S(2)}, u32[]{:S(2)}) collective-permute-start(bf16[1,2,80,256]{3,2,1,0:T(8,128)(2,1)S(1)} %get-tuple-element.19), channel_id=1, source_target_pairs={{0,16},{16,0},{1,17},{17,1},{2,18},{18,2},{3,19},{19,3},{4,20},{20... | collective-permute-start | bytes 245768 | tf_op jit(solution)/shard_map/ppermute | solution.py:163
  39.1 1.0 %collective-permute-done.5 = bf16[1,2,80,256]{3,2,1,0:T(8,128)(2,1)S(1)} collective-permute-done((bf16[1,2,80,256]{3,2,1,0:T(8,128)(2,1)S(1)}, bf16[1,2,80,256]{3,2,1,0:T(8,128)(2,1)S(1)}, u32[]{:S(2)}, u32[]{:S(2)}) %collective-permute-start.5) | collective-permute-done | bytes 81952 | tf_op jit(solution)/shard_map/ppermute | solution.py:160
  40.1 0.6 collective-permute-done.4
  40.7 1.3 %collective-permute-done.3 = bf16[1,2,80,256]{3,2,1,0:T(8,128)(2,1)S(1)} collective-permute-done((bf16[1,2,80,256]{3,2,1,0:T(8,128)(2,1)S(1)}, bf16[1,2,80,256]{3,2,1,0:T(8,128)(2,1)S(1)}, u32[]{:S(2)}, u32[]{:S(2)}) %collective-permute-start.3) | collective-permute-done | bytes 81952 | tf_op jit(solution)/shard_map/ppermute | solution.py:163
  42.1 0.0 collective-permute-done.9.refs_2_
  42.1 0.5 merge.1
  42.6 1.6 %collective-permute-start.15 = (bf16[2,2,80,256]{3,2,1,0:T(8,128)(2,1)S(1)}, bf16[2,2,80,256]{3,2,1,0:T(8,128)(2,1)S(1)}, u32[]{:S(2)}, u32[]{:S(2)}) collective-permute-start(bf16[2,2,80,256]{3,2,1,0:T(8,128)(2,1)S(1)} %pad_maximum_fusion.2), channel_id=1, source_target_pairs={{0,16},{16,0},{1,17},{17,1},{2,18},{18,2},{3,19},{19,3},{4,20},{20... | collective-permute-start | bytes 491528 | tf_op jit(solution)/shard_map/ppermute | solution.py:163
  44.1 2.1 %collective-permute-start.13 = (bf16[2,2,80,256]{3,2,1,0:T(8,128)(2,1)S(1)}, bf16[2,2,80,256]{3,2,1,0:T(8,128)(2,1)S(1)}, u32[]{:S(2)}, u32[]{:S(2)}) collective-permute-start(bf16[2,2,80,256]{3,2,1,0:T(8,128)(2,1)S(1)} %pad_maximum_fusion.1), channel_id=1, source_target_pairs={{0,4},{1,5},{2,6},{3,7},{4,0},{5,1},{6,2},{7,3},{8,12},{9,13},{10,... | collective-permute-start | bytes 491528 | tf_op jit(solution)/shard_map/ppermute | solution.py:160
  46.2 0.7 %collective-permute-start.11 = (bf16[2,2,80,256]{3,2,1,0:T(8,128)(2,1)S(1)}, bf16[2,2,80,256]{3,2,1,0:T(8,128)(2,1)S(1)}, u32[]{:S(2)}, u32[]{:S(2)}) collective-permute-start(bf16[2,2,80,256]{3,2,1,0:T(8,128)(2,1)S(1)} %pad_maximum_fusion), channel_id=1, source_target_pairs={{0,2},{1,3},{2,0},{3,1},{4,6},{5,7},{6,4},{7,5},{8,10},{9,11},{10,... | collective-permute-start | bytes 491528 | tf_op jit(solution)/shard_map/ppermute | solution.py:160
  47.0 1.0 %collective-permute-done.15 = bf16[2,2,80,256]{3,2,1,0:T(8,128)(2,1)S(1)} collective-permute-done((bf16[2,2,80,256]{3,2,1,0:T(8,128)(2,1)S(1)}, bf16[2,2,80,256]{3,2,1,0:T(8,128)(2,1)S(1)}, u32[]{:S(2)}, u32[]{:S(2)}) %collective-permute-start.15) | collective-permute-done | bytes 163872 | tf_op jit(solution)/shard_map/ppermute | solution.py:163
  48.0 0.7 %collective-permute-start.16 = (bf16[4,2,80,256]{3,2,1,0:T(8,128)(2,1)S(1)}, bf16[4,2,80,256]{3,2,1,0:T(8,128)(2,1)S(1)}, u32[]{:S(2)}, u32[]{:S(2)}) collective-permute-start(bf16[4,2,80,256]{3,2,1,0:T(8,128)(2,1)S(1)} %constant_dynamic-update-slice_fusion.7.refs_4_), channel_id=1, source_target_pairs={{0,2},{1,3},{2,0},{3,1},{4,6},{5,7},{6,4},{7,5},{8,10},{9,11},{10,... | collective-permute-start | bytes 983048 | tf_op jit(solution)/shard_map/ppermute | solution.py:160
  48.7 0.8 %collective-permute-done.13 = bf16[2,2,80,256]{3,2,1,0:T(8,128)(2,1)S(1)} collective-permute-done((bf16[2,2,80,256]{3,2,1,0:T(8,128)(2,1)S(1)}, bf16[2,2,80,256]{3,2,1,0:T(8,128)(2,1)S(1)}, u32[]{:S(2)}, u32[]{:S(2)}) %collective-permute-start.13) | collective-permute-done | bytes 163872 | tf_op jit(solution)/shard_map/ppermute | solution.py:160
  49.5 0.7 %collective-permute-start.14 = (bf16[4,2,80,256]{3,2,1,0:T(8,128)(2,1)S(1)}, bf16[4,2,80,256]{3,2,1,0:T(8,128)(2,1)S(1)}, u32[]{:S(2)}, u32[]{:S(2)}) collective-permute-start(bf16[4,2,80,256]{3,2,1,0:T(8,128)(2,1)S(1)} %constant_dynamic-update-slice_fusion.5.refs_0_), channel_id=1, source_target_pairs={{0,16},{16,0},{1,17},{17,1},{2,18},{18,2},{3,19},{19,3},{4,20},{20... | collective-permute-start | bytes 983048 | tf_op jit(solution)/shard_map/ppermute | solution.py:163
  50.3 3.1 %collective-permute-done.11 = bf16[2,2,80,256]{3,2,1,0:T(8,128)(2,1)S(1)} collective-permute-done((bf16[2,2,80,256]{3,2,1,0:T(8,128)(2,1)S(1)}, bf16[2,2,80,256]{3,2,1,0:T(8,128)(2,1)S(1)}, u32[]{:S(2)}, u32[]{:S(2)}) %collective-permute-start.11) | collective-permute-done | bytes 163872 | tf_op jit(solution)/shard_map/ppermute | solution.py:160
  53.4 0.1 collective-permute-start.12
  53.5 0.1 collective-permute-start.17
  53.6 0.0 copy-start.2
  53.6 10.0 %all_to_all.10.start = f32[32,4,128]{2,1,0:T(4,128)S(1)} all-to-all(f32[32,4,128]{2,1,0:T(4,128)S(1)} %bitcast.6), channel_id=1, replica_groups=mesh['row'=2,'col'=16] {'row','col'}, dimensions={0} | all-to-all | bytes 131072 | tf_op jit(solution)/shard_map/all_to_all | solution.py:255
  63.6 0.2 collective-permute-start.18
  63.8 0.4 collective-permute-start.21
  64.2 0.1 collective-permute-start.19
  64.3 0.4 collective-permute-start.20
  64.7 0.1 collective-permute-start.22
  64.8 0.5 collective-permute-done.18.refs_3_
  65.3 1.9 %chain0.1.start = f32[8,2048]{1,0:T(8,128)S(1)} custom-call(s32[6]{0:T(128)S(1)} %copy-done.2, f32[32,4,128]{2,1,0:T(4,128)S(1)} %all_to_all.10.start, bf16[4,2,80,256]{3,2,1,0:T(8,128)(2,1)S(1)} %constant_dynamic-update-slice_fusion.3.refs_0_, bf16[4,2,80,256]{3,2,1,0:T(8,128)(2,1)S(1)} %collective-permute-done.12.refs_1_, ...), custom_call_target="tpu_custom_call" | custom-call | flops 67108864 | bytes 1310720 | tf_op jit(solution)/shard_map/chain0/pallas_call | solution.py:273
  67.3 3.8 %chain1.1 = bf16[4,2048]{1,0:T(4,128)(2,1)} custom-call(s32[6]{0:T(128)S(1)} %copy-done.2, f32[8,2048]{1,0:T(8,128)S(1)} %chain0.1.start, bf16[4,2,80,256]{3,2,1,0:T(8,128)(2,1)S(1)} %constant_dynamic-update-slice_fusion.5.refs_0_, bf16[4,2,80,256]{3,2,1,0:T(8,128)(2,1)S(1)} %collective-permute-done.14.refs_1_, ...), custom_call_target="tpu_custom_call" | custom-call | flops 134217728 | bytes 2621440 | tf_op jit(solution)/shard_map/chain1/pallas_call | solution.py:273
  (29 shorter events, 0.2 us)
Async XLA Ops:
  1.7 5.4 %copy-start.3 = (bf16[64,512]{1,0:T(8,128)(2,1)S(1)}, bf16[64,512]{1,0:T(8,128)(2,1)}, u32[]{:S(2)}) copy-start(bf16[64,512]{1,0:T(8,128)(2,1)} %param.7) | copy-start | bytes 196612
  1.7 15.9 %all-to-all-start = ((bf16[8,80,256]{2,1,0:T(8,128)(2,1)}), bf16[8,80,256]{2,1,0:T(8,128)(2,1)S(1)}, u32[]{:S(2)}, u32[]{:S(2)}) async-start(bf16[8,80,256]{2,1,0:T(8,128)(2,1)} %pack.1), calls=%async_computation | async-start | bytes 655360 | tf_op jit(solution)/shard_map/all_to_all | solution.py:184
  7.1 6.1 %collective-permute-start = (bf16[64,512]{1,0:T(8,128)(2,1)S(1)}, bf16[64,512]{1,0:T(8,128)(2,1)S(1)}, u32[]{:S(2)}, u32[]{:S(2)}) collective-permute-start(bf16[64,512]{1,0:T(8,128)(2,1)S(1)} %copy-done.3), channel_id=1, source_target_pairs={{0,8},{1,9},{2,10},{3,11},{4,12},{5,13},{6,14},{7,15},{8,0},{9,1},... | collective-permute-start | bytes 196616 | tf_op jit(solution)/shard_map/ppermute | solution.py:160
  13.2 4.3 %collective-permute-start.1 = (bf16[64,512]{1,0:T(8,128)(2,1)S(1)}, bf16[64,512]{1,0:T(8,128)(2,1)S(1)}, u32[]{:S(2)}, u32[]{:S(2)}) collective-permute-start(bf16[64,512]{1,0:T(8,128)(2,1)S(1)} %get-tuple-element.32), channel_id=1, source_target_pairs={{0,16},{16,0},{1,17},{17,1},{2,18},{18,2},{3,19},{19,3},{4,20},{20... | collective-permute-start | bytes 196616 | tf_op jit(solution)/shard_map/ppermute | solution.py:163
  17.6 6.2 %copy-start.1 = (s32[6]{0:T(128)S(1)}, s32[6]{0:T(128)}, u32[]{:S(2)}) copy-start(s32[6]{0:T(128)} %owners.3) | copy-start | bytes 76
  17.6 7.8 %collective-permute-start.6 = (bf16[2,64,512]{2,1,0:T(8,128)(2,1)S(1)}, bf16[2,64,512]{2,1,0:T(8,128)(2,1)S(1)}, u32[]{:S(2)}, u32[]{:S(2)}) collective-permute-start(bf16[2,64,512]{2,1,0:T(8,128)(2,1)S(1)} %pad_maximum_fusion.3.refs_0_), channel_id=1, source_target_pairs={{0,2},{1,3},{2,0},{3,1},{4,6},{5,7},{6,4},{7,5},{8,10},{9,11},{10,... | collective-permute-start | bytes 393224 | tf_op jit(solution)/shard_map/ppermute | solution.py:160
  19.3 10.0 %collective-permute-start.7 = (bf16[2,64,512]{2,1,0:T(8,128)(2,1)S(1)}, bf16[2,64,512]{2,1,0:T(8,128)(2,1)S(1)}, u32[]{:S(2)}, u32[]{:S(2)}) collective-permute-start(bf16[2,64,512]{2,1,0:T(8,128)(2,1)S(1)} %pad_maximum_fusion.3.refs_0_), channel_id=1, source_target_pairs={{0,4},{1,5},{2,6},{3,7},{4,0},{5,1},{6,2},{7,3},{8,12},{9,13},{10,... | collective-permute-start | bytes 393224 | tf_op jit(solution)/shard_map/ppermute | solution.py:160
  23.8 11.8 %collective-permute-start.8 = (bf16[2,64,512]{2,1,0:T(8,128)(2,1)S(1)}, bf16[2,64,512]{2,1,0:T(8,128)(2,1)S(1)}, u32[]{:S(2)}, u32[]{:S(2)}) collective-permute-start(bf16[2,64,512]{2,1,0:T(8,128)(2,1)S(1)} %pad_maximum_fusion.3.refs_0_), channel_id=1, source_target_pairs={{0,6},{1,7},{2,4},{3,5},{4,2},{5,3},{6,0},{7,1},{8,14},{9,15},{10,... | collective-permute-start | bytes 393224 | tf_op jit(solution)/shard_map/ppermute | solution.py:160
  24.5 10.4 %collective-permute-start.2 = (bf16[5,80,256]{2,1,0:T(8,128)(2,1)S(1)}, bf16[5,80,256]{2,1,0:T(8,128)(2,1)S(1)}, u32[]{:S(2)}, u32[]{:S(2)}) collective-permute-start(bf16[5,80,256]{2,1,0:T(8,128)(2,1)S(1)} %pick.1), channel_id=1, source_target_pairs={{0,8},{1,9},{2,10},{3,11},{4,12},{5,13},{6,14},{7,15},{8,0},{9,1},... | collective-permute-start | bytes 614408 | tf_op jit(solution)/shard_map/ppermute | solution.py:160
  25.4 16.7 %copy-start = (bf16[4096,128]{1,0:T(8,128)(2,1)S(1)}, bf16[4096,128]{1,0:T(8,128)(2,1)}, u32[]{:S(2)}) copy-start(bf16[4096,128]{1,0:T(8,128)(2,1)} %sub.6) | copy-start | bytes 3145732
  35.6 4.5 %collective-permute-start.5 = (bf16[1,2,80,256]{3,2,1,0:T(8,128)(2,1)S(1)}, bf16[1,2,80,256]{3,2,1,0:T(8,128)(2,1)S(1)}, u32[]{:S(2)}, u32[]{:S(2)}) collective-permute-start(bf16[1,2,80,256]{3,2,1,0:T(8,128)(2,1)S(1)} %get-tuple-element.21), channel_id=1, source_target_pairs={{0,4},{1,5},{2,6},{3,7},{4,0},{5,1},{6,2},{7,3},{8,12},{9,13},{10,... | collective-permute-start | bytes 245768 | tf_op jit(solution)/shard_map/ppermute | solution.py:160
  35.7 6.4 %collective-permute-start.10 = (bf16[6,64,512]{2,1,0:T(8,128)(2,1)S(1)}, bf16[6,64,512]{2,1,0:T(8,128)(2,1)S(1)}, u32[]{:S(2)}, u32[]{:S(2)}) collective-permute-start(bf16[6,64,512]{2,1,0:T(8,128)(2,1)S(1)} %constant_dynamic-update-slice_fusion.refs_1_), channel_id=1, source_target_pairs={{0,1},{1,0},{2,3},{3,2},{4,5},{5,4},{6,7},{7,6},{8,9},{9,8},{10,11... | collective-permute-start | bytes 1179656 | tf_op jit(solution)/shard_map/ppermute | solution.py:160
  35.7 6.3 %collective-permute-start.9 = (bf16[2,64,512]{2,1,0:T(8,128)(2,1)S(1)}, bf16[2,64,512]{2,1,0:T(8,128)(2,1)S(1)}, u32[]{:S(2)}, u32[]{:S(2)}) collective-permute-start(bf16[2,64,512]{2,1,0:T(8,128)(2,1)S(1)} %pad_maximum_fusion.3.refs_0_), channel_id=1, source_target_pairs={{0,1},{1,0},{2,3},{3,2},{4,5},{5,4},{6,7},{7,6},{8,9},{9,8},{10,11... | collective-permute-start | bytes 393224 | tf_op jit(solution)/shard_map/ppermute | solution.py:160
  36.2 4.4 %collective-permute-start.4 = (bf16[1,2,80,256]{3,2,1,0:T(8,128)(2,1)S(1)}, bf16[1,2,80,256]{3,2,1,0:T(8,128)(2,1)S(1)}, u32[]{:S(2)}, u32[]{:S(2)}) collective-permute-start(bf16[1,2,80,256]{3,2,1,0:T(8,128)(2,1)S(1)} %get-tuple-element.20), channel_id=1, source_target_pairs={{0,2},{1,3},{2,0},{3,1},{4,6},{5,7},{6,4},{7,5},{8,10},{9,11},{10,... | collective-permute-start | bytes 245768 | tf_op jit(solution)/shard_map/ppermute | solution.py:160
  37.6 4.4 %collective-permute-start.3 = (bf16[1,2,80,256]{3,2,1,0:T(8,128)(2,1)S(1)}, bf16[1,2,80,256]{3,2,1,0:T(8,128)(2,1)S(1)}, u32[]{:S(2)}, u32[]{:S(2)}) collective-permute-start(bf16[1,2,80,256]{3,2,1,0:T(8,128)(2,1)S(1)} %get-tuple-element.19), channel_id=1, source_target_pairs={{0,16},{16,0},{1,17},{17,1},{2,18},{18,2},{3,19},{19,3},{4,20},{20... | collective-permute-start | bytes 245768 | tf_op jit(solution)/shard_map/ppermute | solution.py:163
  42.6 5.4 %collective-permute-start.15 = (bf16[2,2,80,256]{3,2,1,0:T(8,128)(2,1)S(1)}, bf16[2,2,80,256]{3,2,1,0:T(8,128)(2,1)S(1)}, u32[]{:S(2)}, u32[]{:S(2)}) collective-permute-start(bf16[2,2,80,256]{3,2,1,0:T(8,128)(2,1)S(1)} %pad_maximum_fusion.2), channel_id=1, source_target_pairs={{0,16},{16,0},{1,17},{17,1},{2,18},{18,2},{3,19},{19,3},{4,20},{20... | collective-permute-start | bytes 491528 | tf_op jit(solution)/shard_map/ppermute | solution.py:163
  44.1 5.4 %collective-permute-start.13 = (bf16[2,2,80,256]{3,2,1,0:T(8,128)(2,1)S(1)}, bf16[2,2,80,256]{3,2,1,0:T(8,128)(2,1)S(1)}, u32[]{:S(2)}, u32[]{:S(2)}) collective-permute-start(bf16[2,2,80,256]{3,2,1,0:T(8,128)(2,1)S(1)} %pad_maximum_fusion.1), channel_id=1, source_target_pairs={{0,4},{1,5},{2,6},{3,7},{4,0},{5,1},{6,2},{7,3},{8,12},{9,13},{10,... | collective-permute-start | bytes 491528 | tf_op jit(solution)/shard_map/ppermute | solution.py:160
  46.2 7.2 %collective-permute-start.11 = (bf16[2,2,80,256]{3,2,1,0:T(8,128)(2,1)S(1)}, bf16[2,2,80,256]{3,2,1,0:T(8,128)(2,1)S(1)}, u32[]{:S(2)}, u32[]{:S(2)}) collective-permute-start(bf16[2,2,80,256]{3,2,1,0:T(8,128)(2,1)S(1)} %pad_maximum_fusion), channel_id=1, source_target_pairs={{0,2},{1,3},{2,0},{3,1},{4,6},{5,7},{6,4},{7,5},{8,10},{9,11},{10,... | collective-permute-start | bytes 491528 | tf_op jit(solution)/shard_map/ppermute | solution.py:160
  48.0 15.7 %collective-permute-start.16 = (bf16[4,2,80,256]{3,2,1,0:T(8,128)(2,1)S(1)}, bf16[4,2,80,256]{3,2,1,0:T(8,128)(2,1)S(1)}, u32[]{:S(2)}, u32[]{:S(2)}) collective-permute-start(bf16[4,2,80,256]{3,2,1,0:T(8,128)(2,1)S(1)} %constant_dynamic-update-slice_fusion.7.refs_4_), channel_id=1, source_target_pairs={{0,2},{1,3},{2,0},{3,1},{4,6},{5,7},{6,4},{7,5},{8,10},{9,11},{10,... | collective-permute-start | bytes 983048 | tf_op jit(solution)/shard_map/ppermute | solution.py:160
  49.5 14.1 %collective-permute-start.14 = (bf16[4,2,80,256]{3,2,1,0:T(8,128)(2,1)S(1)}, bf16[4,2,80,256]{3,2,1,0:T(8,128)(2,1)S(1)}, u32[]{:S(2)}, u32[]{:S(2)}) collective-permute-start(bf16[4,2,80,256]{3,2,1,0:T(8,128)(2,1)S(1)} %constant_dynamic-update-slice_fusion.5.refs_0_), channel_id=1, source_target_pairs={{0,16},{16,0},{1,17},{17,1},{2,18},{18,2},{3,19},{19,3},{4,20},{20... | collective-permute-start | bytes 983048 | tf_op jit(solution)/shard_map/ppermute | solution.py:163
  53.4 10.2 %collective-permute-start.12 = (bf16[4,2,80,256]{3,2,1,0:T(8,128)(2,1)S(1)}, bf16[4,2,80,256]{3,2,1,0:T(8,128)(2,1)S(1)}, u32[]{:S(2)}, u32[]{:S(2)}) collective-permute-start(bf16[4,2,80,256]{3,2,1,0:T(8,128)(2,1)S(1)} %constant_dynamic-update-slice_fusion.3.refs_0_), channel_id=1, source_target_pairs={{0,4},{1,5},{2,6},{3,7},{4,0},{5,1},{6,2},{7,3},{8,12},{9,13},{10,... | collective-permute-start | bytes 983048 | tf_op jit(solution)/shard_map/ppermute | solution.py:160
  53.5 11.2 %collective-permute-start.17 = (bf16[4,2,80,256]{3,2,1,0:T(8,128)(2,1)S(1)}, bf16[4,2,80,256]{3,2,1,0:T(8,128)(2,1)S(1)}, u32[]{:S(2)}, u32[]{:S(2)}) collective-permute-start(bf16[4,2,80,256]{3,2,1,0:T(8,128)(2,1)S(1)} %constant_dynamic-update-slice_fusion.3.refs_0_), channel_id=1, source_target_pairs={{0,1},{1,0},{2,3},{3,2},{4,5},{5,4},{6,7},{7,6},{8,9},{9,8},{10,11... | collective-permute-start | bytes 983048 | tf_op jit(solution)/shard_map/ppermute | solution.py:160
  53.6 11.7 %copy-start.2 = (s32[6]{0:T(128)S(1)}, s32[6]{0:T(128)}, u32[]{:S(2)}) copy-start(s32[6]{0:T(128)} %offsets.3) | copy-start | bytes 76
  63.6 1.7 %collective-permute-start.18 = (bf16[4,2,80,256]{3,2,1,0:T(8,128)(2,1)S(1)}, bf16[4,2,80,256]{3,2,1,0:T(8,128)(2,1)S(1)}, u32[]{:S(2)}, u32[]{:S(2)}) collective-permute-start(bf16[4,2,80,256]{3,2,1,0:T(8,128)(2,1)S(1)} %collective-permute-done.12.refs_1_), channel_id=1, source_target_pairs={{0,1},{1,0},{2,3},{3,2},{4,5},{5,4},{6,7},{7,6},{8,9},{9,8},{10,11... | collective-permute-start | bytes 983048 | tf_op jit(solution)/shard_map/ppermute | solution.py:160
  63.8 3.4 %collective-permute-start.21 = (bf16[4,2,80,256]{3,2,1,0:T(8,128)(2,1)S(1)}, bf16[4,2,80,256]{3,2,1,0:T(8,128)(2,1)S(1)}, u32[]{:S(2)}, u32[]{:S(2)}) collective-permute-start(bf16[4,2,80,256]{3,2,1,0:T(8,128)(2,1)S(1)} %constant_dynamic-update-slice_fusion.7.refs_4_), channel_id=1, source_target_pairs={{0,1},{1,0},{2,3},{3,2},{4,5},{5,4},{6,7},{7,6},{8,9},{9,8},{10,11... | collective-permute-start | bytes 983048 | tf_op jit(solution)/shard_map/ppermute | solution.py:160
  64.2 3.0 %collective-permute-start.19 = (bf16[4,2,80,256]{3,2,1,0:T(8,128)(2,1)S(1)}, bf16[4,2,80,256]{3,2,1,0:T(8,128)(2,1)S(1)}, u32[]{:S(2)}, u32[]{:S(2)}) collective-permute-start(bf16[4,2,80,256]{3,2,1,0:T(8,128)(2,1)S(1)} %constant_dynamic-update-slice_fusion.5.refs_0_), channel_id=1, source_target_pairs={{0,1},{1,0},{2,3},{3,2},{4,5},{5,4},{6,7},{7,6},{8,9},{9,8},{10,11... | collective-permute-start | bytes 983048 | tf_op jit(solution)/shard_map/ppermute | solution.py:160
  64.3 2.9 %collective-permute-start.20 = (bf16[4,2,80,256]{3,2,1,0:T(8,128)(2,1)S(1)}, bf16[4,2,80,256]{3,2,1,0:T(8,128)(2,1)S(1)}, u32[]{:S(2)}, u32[]{:S(2)}) collective-permute-start(bf16[4,2,80,256]{3,2,1,0:T(8,128)(2,1)S(1)} %collective-permute-done.14.refs_1_), channel_id=1, source_target_pairs={{0,1},{1,0},{2,3},{3,2},{4,5},{5,4},{6,7},{7,6},{8,9},{9,8},{10,11... | collective-permute-start | bytes 983048 | tf_op jit(solution)/shard_map/ppermute | solution.py:160
  64.7 2.5 %collective-permute-start.22 = (bf16[4,2,80,256]{3,2,1,0:T(8,128)(2,1)S(1)}, bf16[4,2,80,256]{3,2,1,0:T(8,128)(2,1)S(1)}, u32[]{:S(2)}, u32[]{:S(2)}) collective-permute-start(bf16[4,2,80,256]{3,2,1,0:T(8,128)(2,1)S(1)} %collective-permute-done.16.refs_5_), channel_id=1, source_target_pairs={{0,1},{1,0},{2,3},{3,2},{4,5},{5,4},{6,7},{7,6},{8,9},{9,8},{10,11... | collective-permute-start | bytes 983048 | tf_op jit(solution)/shard_map/ppermute | solution.py:160

commit v17 on v15

--- a/solution.py
+++ b/solution.py
@@ -80,7 +80,7 @@
         outs[group // each][0, group % each] = piece
 
 
-def merge_kernel(rows, cols, tags, ready, sub, *refs):
+def merge_kernel(rows, cols, tags, sub, *refs):
     held, total = refs[:-1], refs[-1]
     row, col = lax.axis_index("row"), lax.axis_index("col")
     deep, tall = held[0].shape[2], held[0].shape[1]
@@ -191,7 +191,6 @@
         cost_estimate=cost([slices]),
         name="pick",
     )(owners, slices)
-    ready = over_col(picked[0, :16], HALF)
     others = [over_col(picked, m * HALF) for m in range(1, halves)]
 
     across = [merge_factor] + [over_col(merge_factor, m * share) for m in range(1, rows)]
@@ -205,17 +204,27 @@
             block = jnp.where(index == k, across[k], block)
         return block
 
-    m_held = jnp.stack([for_row(0)] + [over_row(for_row(m), m) for m in range(1, rows)])
-    ready, m_held = lax.optimization_barrier((ready, m_held))
-    tags = [(m, 0) for m in range(rows)]
+    blocks = [for_row(0)] + [over_row(for_row(m), m) for m in range(1, rows)]
+    others, blocks = lax.optimization_barrier((others, blocks))
+    groups = [range(rows // 2), range(rows // 2, rows)]
+    sides = [jnp.stack([blocks[m] for m in group]) for group in groups]
+    tags = [[(m, 0) for m in group] for group in groups]
+
+    def double(side, bit):
+        sides[side] = jnp.concatenate([sides[side], over_col(sides[side], bit)])
+        tags[side] = tags[side] + [(m, c ^ bit) for m, c in tags[side]]
+
     bit = share // 2
     while bit > 4:
-        m_held = jnp.concatenate([m_held, over_col(m_held, bit)])
-        tags = tags + [(m, c ^ bit) for m, c in tags]
+        double(0, bit)
+        double(1, bit)
         bit //= 2
-    late = jnp.concatenate([over_col(m_held, mask) for mask in (2, 4, 6)])
-    late_tags = [(m, c ^ mask) for mask in (2, 4, 6) for m, c in tags]
-    m_held, tags = [m_held, late], [tags, late_tags]
+    double(0, 2)
+    double(1, 4)
+    late = jnp.concatenate([over_col(sides[0], 4), over_col(sides[1], 2)])
+    late_tags = [(m, c ^ 4) for m, c in tags[0]] + [(m, c ^ 2) for m, c in tags[1]]
+    m_held = [jnp.concatenate(sides), late]
+    tags = [tags[0] + tags[1], late_tags]
     m_held += [over_col(x, 1) for x in m_held]
     tags += [[(m, c ^ 1) for m, c in ts] for ts in tags]
     wanted, width = merge_factor.shape[0] * rows, sub_vectors.shape[1]
@@ -223,12 +232,12 @@
     merged = pl.pallas_call(
         functools.partial(merge_kernel, rows, cols, tags),
         out_shape=jax.ShapeDtypeStruct((wanted, width), jnp.float32),
-        in_specs=[HBM, VMEM] + [VMEM] * len(m_held),
+        in_specs=[VMEM] + [VMEM] * len(m_held),
         out_specs=VMEM,
         compiler_params=limit(8),
         cost_estimate=cost([sub_vectors], 2 * wanted * sub_vectors.size),
         name="merge",
-    )(ready, sub_vectors, *m_held)
+    )(sub_vectors, *m_held)
     per = GROUPS // COLOURS
     colours = pl.pallas_call(
         order_kernel,
@@ -251,8 +260,6 @@
             mask, send = links[(k + step) % 3]
             colours[k] = jnp.concatenate([colours[k], send(colours[k])])
             masks[k] = masks[k] + [m ^ mask for m in masks[k]]
-        if step == 0:
-            colours, merged = lax.optimization_barrier((colours, merged))
     state = lax.all_to_all(merged.reshape(rows * cols, each, width), ("row", "col"), 0, 0)
     last_round = []
     for k in range(COLOURS):

time: 72 us -> 68.3 us (0.949)
  blocking collectives: 11.1 us -> 0 us
  waiting for transfers between devices: 21.6 us -> 27.3 us
  starting transfers between devices: 29.4 us -> 30.4 us
    all_to_all x1 -> x0, blocking collectives: 11.1 us -> none  [local(): lax.all_to_all(merged.reshape(rows * cols, each, width), ('row', 'col'),...]
    ppermute x20, waiting for transfers between devices: 19.6 us -> 9.88 us  [over_col(): return lax.ppermute(x, 'col', [(c, c ^ mask) for c in range(cols)])]
    ppermute x4, waiting for transfers between devices: 1.58 us -> 6.94 us  [over_row(): return lax.ppermute(x, 'row', [(r, r ^ mask) for r in range(rows)])]
    all_to_all x1, waiting for transfers between devices: 0.45 us -> 5.48 us  [local(): slices = lax.all_to_all(packed, 'col', 0, 0, axis_index_groups=members)]
    all_to_all x0 -> x1, waiting for transfers between devices: none -> 5.03 us  [local(): lax.all_to_all(merged.reshape(rows * cols, each, width), ('row', 'col'),...]
    all_to_all x0 -> x1, starting transfers between devices: none -> 3.89 us  [local(): lax.all_to_all(merged.reshape(rows * cols, each, width), ('row', 'col'),...]
    ppermute x20, starting transfers between devices: 19.7 us -> 17.1 us  [over_col(): return lax.ppermute(x, 'col', [(c, c ^ mask) for c in range(cols)])]
  transfers between devices with their start and end apart: 25 -> 26, of which waited for: 11 -> 12; matrix products, arithmetic and copies ran while one was open for 0% -> 0% of each run, Pallas kernels for 4% -> 5%
where the time goes in v17:
time: 68.3 us; the launch traced here: 68 us
  starting transfers between devices  30.4 us (45%)
  waiting for transfers between devices  27.3 us (40%)
  Pallas kernels  9.78 us (14%)
    ppermute x20, starting transfers between devices, over_col(): return lax.ppermute(x, 'col', [(c, c ^ mask) for c in range(cols)])  17.1 us
    ppermute x20, waiting for transfers between devices, over_col(): return lax.ppermute(x, 'col', [(c, c ^ mask) for c in range(cols)])  9.88 us
    ppermute x4, waiting for transfers between devices, over_row(): return lax.ppermute(x, 'row', [(r, r ^ mask) for r in range(rows)])  6.94 us
    pallas_call x2, Pallas kernels, local(): pl.pallas_call(functools.partial(chain_kernel, cols, groups, slots, sum((...  5.68 us
    all_to_all x1, waiting for transfers between devices, local(): slices = lax.all_to_all(packed, 'col', 0, 0, axis_index_groups=members)  5.48 us
    all_to_all x1, starting transfers between devices, local(): slices = lax.all_to_all(packed, 'col', 0, 0, axis_index_groups=members)  5.4 us
    all_to_all x1, waiting for transfers between devices, local(): lax.all_to_all(merged.reshape(rows * cols, each, width), ('row', 'col'),...  5.03 us
    ppermute x4, starting transfers between devices, over_row(): return lax.ppermute(x, 'row', [(r, r ^ mask) for r in range(rows)])  4.06 us
  transfers between devices with their start and end apart: 26, of which 12 were waited for; matrix products, arithmetic and copies ran while one was open for 0% of the time, Pallas kernels for 5%

profile of v17, /device:TPU:0, one launch (start us, length us, event | category | flops | bytes accessed | tf_op | source)
XLA Modules:
  0.0 68.0 jit_solution(14234988285535905650)
XLA Ops:
  0.0 1.7 %pack.1 = bf16[8,80,256]{2,1,0:T(8,128)(2,1)} custom-call(bf16[16,64,256]{2,1,0:T(8,128)(2,1)} %bitcast.8, bf16[16,16,256]{2,1,0:T(8,128)(2,1)} %bitcast.12), custom_call_target="tpu_custom_call" | custom-call | bytes 655360 | tf_op jit(solution)/shard_map/pack/pallas_call | solution.py:171
  1.7 0.0 copy-start.3
  1.7 5.4 %all-to-all-start = ((bf16[8,80,256]{2,1,0:T(8,128)(2,1)}), bf16[8,80,256]{2,1,0:T(8,128)(2,1)S(1)}, u32[]{:S(2)}, u32[]{:S(2)}) async-start(bf16[8,80,256]{2,1,0:T(8,128)(2,1)} %pack.1), calls=%async_computation | async-start | bytes 655360 | tf_op jit(solution)/shard_map/all_to_all | solution.py:183
  7.1 2.7 %collective-permute-start.1 = (bf16[64,512]{1,0:T(8,128)(2,1)S(1)}, bf16[64,512]{1,0:T(8,128)(2,1)S(1)}, u32[]{:S(2)}, u32[]{:S(2)}) collective-permute-start(bf16[64,512]{1,0:T(8,128)(2,1)S(1)} %copy-done.3), channel_id=1, source_target_pairs={{0,8},{1,9},{2,10},{3,11},{4,12},{5,13},{6,14},{7,15},{8,0},{9,1},... | collective-permute-start | bytes 196616 | tf_op jit(solution)/shard_map/ppermute | solution.py:160
  9.8 5.5 %all-to-all-done.held = bf16[8,80,256]{2,1,0:T(8,128)(2,1)S(1)} async-done(((bf16[8,80,256]{2,1,0:T(8,128)(2,1)}), bf16[8,80,256]{2,1,0:T(8,128)(2,1)S(1)}, u32[]{:S(2)}, u32[]{:S(2)}) %all-to-all-start) | async-done | bytes 327712 | tf_op jit(solution)/shard_map/all_to_all | solution.py:183
  15.3 0.7 %pick.1 = bf16[5,80,256]{2,1,0:T(8,128)(2,1)S(1)} custom-call(s32[6]{0:T(128)S(1)} %copy-done.1, bf16[8,80,256]{2,1,0:T(8,128)(2,1)S(1)} %all-to-all-done.held), custom_call_target="tpu_custom_call" | custom-call | bytes 327680 | tf_op jit(solution)/shard_map/pick/pallas_call | solution.py:185
  16.0 1.8 %collective-permute-start = (bf16[5,80,256]{2,1,0:T(8,128)(2,1)S(1)}, bf16[5,80,256]{2,1,0:T(8,128)(2,1)S(1)}, u32[]{:S(2)}, u32[]{:S(2)}) collective-permute-start(bf16[5,80,256]{2,1,0:T(8,128)(2,1)S(1)} %pick.1), channel_id=1, source_target_pairs={{0,8},{1,9},{2,10},{3,11},{4,12},{5,13},{6,14},{7,15},{8,0},{9,1},... | collective-permute-start | bytes 614408 | tf_op jit(solution)/shard_map/ppermute | solution.py:160
  17.7 0.0 collective-permute-done.1
  17.8 1.6 %collective-permute-start.2 = (bf16[64,512]{1,0:T(8,128)(2,1)S(1)}, bf16[64,512]{1,0:T(8,128)(2,1)S(1)}, u32[]{:S(2)}, u32[]{:S(2)}) collective-permute-start(bf16[64,512]{1,0:T(8,128)(2,1)S(1)} %get-tuple-element.29), channel_id=1, source_target_pairs={{0,16},{16,0},{1,17},{17,1},{2,18},{18,2},{3,19},{19,3},{4,20},{20... | collective-permute-start | bytes 196616 | tf_op jit(solution)/shard_map/ppermute | solution.py:163
  19.3 2.8 %collective-permute-done.2 = bf16[64,512]{1,0:T(8,128)(2,1)S(1)} collective-permute-done((bf16[64,512]{1,0:T(8,128)(2,1)S(1)}, bf16[64,512]{1,0:T(8,128)(2,1)S(1)}, u32[]{:S(2)}, u32[]{:S(2)}) %collective-permute-start.2) | collective-permute-done | bytes 65568 | tf_op jit(solution)/shard_map/ppermute | solution.py:163
  22.1 5.8 %collective-permute-done.refs_0_ = bf16[5,80,256]{2,1,0:T(8,128)(2,1)S(1)} collective-permute-done((bf16[5,80,256]{2,1,0:T(8,128)(2,1)S(1)}, bf16[5,80,256]{2,1,0:T(8,128)(2,1)S(1)}, u32[]{:S(2)}, u32[]{:S(2)}) %collective-permute-start) | collective-permute-done | bytes 204832 | tf_op jit(solution)/shard_map/ppermute | solution.py:160
  27.9 0.6 order.1
  28.5 1.4 %collective-permute-start.6 = (bf16[1,2,80,256]{3,2,1,0:T(8,128)(2,1)S(1)}, bf16[1,2,80,256]{3,2,1,0:T(8,128)(2,1)S(1)}, u32[]{:S(2)}, u32[]{:S(2)}) collective-permute-start(bf16[1,2,80,256]{3,2,1,0:T(8,128)(2,1)S(1)} %get-tuple-element.21), channel_id=1, source_target_pairs={{0,2},{1,3},{2,0},{3,1},{4,6},{5,7},{6,4},{7,5},{8,10},{9,11},{10,... | collective-permute-start | bytes 245768 | tf_op jit(solution)/shard_map/ppermute | solution.py:160
  29.9 1.6 %collective-permute-start.3 = (bf16[1,2,80,256]{3,2,1,0:T(8,128)(2,1)S(1)}, bf16[1,2,80,256]{3,2,1,0:T(8,128)(2,1)S(1)}, u32[]{:S(2)}, u32[]{:S(2)}) collective-permute-start(bf16[1,2,80,256]{3,2,1,0:T(8,128)(2,1)S(1)} %get-tuple-element.20), channel_id=1, source_target_pairs={{0,16},{16,0},{1,17},{17,1},{2,18},{18,2},{3,19},{19,3},{4,20},{20... | collective-permute-start | bytes 245768 | tf_op jit(solution)/shard_map/ppermute | solution.py:163
  31.4 0.7 %collective-permute-start.12 = (bf16[1,64,512]{2,1,0:T(8,128)(2,1)S(1)}, bf16[1,64,512]{2,1,0:T(8,128)(2,1)S(1)}, u32[]{:S(2)}, u32[]{:S(2)}) collective-permute-start(bf16[1,64,512]{2,1,0:T(8,128)(2,1)S(1)} %bitcast.5), channel_id=1, source_target_pairs={{0,2},{1,3},{2,0},{3,1},{4,6},{5,7},{6,4},{7,5},{8,10},{9,11},{10,... | collective-permute-start | bytes 196616 | tf_op jit(solution)/shard_map/ppermute | solution.py:160
  32.1 2.0 %collective-permute-start.9 = (bf16[1,2,80,256]{3,2,1,0:T(8,128)(2,1)S(1)}, bf16[1,2,80,256]{3,2,1,0:T(8,128)(2,1)S(1)}, u32[]{:S(2)}, u32[]{:S(2)}) collective-permute-start(bf16[1,2,80,256]{3,2,1,0:T(8,128)(2,1)S(1)} %get-tuple-element.22), channel_id=1, source_target_pairs={{0,4},{1,5},{2,6},{3,7},{4,0},{5,1},{6,2},{7,3},{8,12},{9,13},{10,... | collective-permute-start | bytes 245768 | tf_op jit(solution)/shard_map/ppermute | solution.py:160
  34.2 1.5 %collective-permute-done.12 = bf16[1,64,512]{2,1,0:T(8,128)(2,1)S(1)} collective-permute-done((bf16[1,64,512]{2,1,0:T(8,128)(2,1)S(1)}, bf16[1,64,512]{2,1,0:T(8,128)(2,1)S(1)}, u32[]{:S(2)}, u32[]{:S(2)}) %collective-permute-start.12) | collective-permute-done | bytes 65568 | tf_op jit(solution)/shard_map/ppermute | solution.py:160
  35.7 0.1 collective-permute-start.14
  35.8 0.6 collective-permute-done.13
  36.4 1.4 %collective-permute-start.15 = (bf16[2,64,512]{2,1,0:T(8,128)(2,1)S(1)}, bf16[2,64,512]{2,1,0:T(8,128)(2,1)S(1)}, u32[]{:S(2)}, u32[]{:S(2)}) collective-permute-start(bf16[2,64,512]{2,1,0:T(8,128)(2,1)S(1)} %pad_maximum_fusion.5), channel_id=1, source_target_pairs={{0,2},{1,3},{2,0},{3,1},{4,6},{5,7},{6,4},{7,5},{8,10},{9,11},{10,... | collective-permute-start | bytes 393224 | tf_op jit(solution)/shard_map/ppermute | solution.py:160
  37.8 0.0 collective-permute-done.9
  37.8 0.1 collective-permute-start.16
  38.0 0.6 collective-permute-start.10
  38.6 0.0 copy-start
  38.6 0.0 collective-permute-done.3
  38.6 1.6 %collective-permute-start.7 = (bf16[2,2,80,256]{3,2,1,0:T(8,128)(2,1)S(1)}, bf16[2,2,80,256]{3,2,1,0:T(8,128)(2,1)S(1)}, u32[]{:S(2)}, u32[]{:S(2)}) collective-permute-start(bf16[2,2,80,256]{3,2,1,0:T(8,128)(2,1)S(1)} %pad_maximum_fusion.2), channel_id=1, source_target_pairs={{0,4},{1,5},{2,6},{3,7},{4,0},{5,1},{6,2},{7,3},{8,12},{9,13},{10,... | collective-permute-start | bytes 491528 | tf_op jit(solution)/shard_map/ppermute | solution.py:160
  40.3 0.4 collective-permute-done.14
  40.7 0.9 %collective-permute-start.4 = (bf16[2,2,80,256]{3,2,1,0:T(8,128)(2,1)S(1)}, bf16[2,2,80,256]{3,2,1,0:T(8,128)(2,1)S(1)}, u32[]{:S(2)}, u32[]{:S(2)}) collective-permute-start(bf16[2,2,80,256]{3,2,1,0:T(8,128)(2,1)S(1)} %pad_maximum_fusion.1), channel_id=1, source_target_pairs={{0,2},{1,3},{2,0},{3,1},{4,6},{5,7},{6,4},{7,5},{8,10},{9,11},{10,... | collective-permute-start | bytes 491528 | tf_op jit(solution)/shard_map/ppermute | solution.py:160
  41.7 0.1 collective-permute-start.17
  41.8 2.8 %collective-permute-done.10 = bf16[2,2,80,256]{3,2,1,0:T(8,128)(2,1)S(1)} collective-permute-done((bf16[2,2,80,256]{3,2,1,0:T(8,128)(2,1)S(1)}, bf16[2,2,80,256]{3,2,1,0:T(8,128)(2,1)S(1)}, u32[]{:S(2)}, u32[]{:S(2)}) %collective-permute-start.10) | collective-permute-done | bytes 163872 | tf_op jit(solution)/shard_map/ppermute | solution.py:163
  44.6 1.6 %collective-permute-start.11 = (bf16[4,2,80,256]{3,2,1,0:T(8,128)(2,1)S(1)}, bf16[4,2,80,256]{3,2,1,0:T(8,128)(2,1)S(1)}, u32[]{:S(2)}, u32[]{:S(2)}) collective-permute-start(bf16[4,2,80,256]{3,2,1,0:T(8,128)(2,1)S(1)} %constant_dynamic-update-slice_fusion.6.refs_4_), channel_id=1, source_target_pairs={{0,2},{1,3},{2,0},{3,1},{4,6},{5,7},{6,4},{7,5},{8,10},{9,11},{10,... | collective-permute-start | bytes 983048 | tf_op jit(solution)/shard_map/ppermute | solution.py:160
  46.2 0.0 collective-permute-done.7
  46.2 0.4 collective-permute-start.8
  46.6 1.7 %collective-permute-start.5 = (bf16[4,2,80,256]{3,2,1,0:T(8,128)(2,1)S(1)}, bf16[4,2,80,256]{3,2,1,0:T(8,128)(2,1)S(1)}, u32[]{:S(2)}, u32[]{:S(2)}) collective-permute-start(bf16[4,2,80,256]{3,2,1,0:T(8,128)(2,1)S(1)} %constant_dynamic-update-slice_fusion.refs_0_), channel_id=1, source_target_pairs={{0,4},{1,5},{2,6},{3,7},{4,0},{5,1},{6,2},{7,3},{8,12},{9,13},{10,... | collective-permute-start | bytes 983048 | tf_op jit(solution)/shard_map/ppermute | solution.py:160
  48.3 1.1 %merge.1 = f32[128,128]{1,0:T(8,128)} custom-call(bf16[4096,128]{1,0:T(8,128)(2,1)S(1)} %copy-done, bf16[4,64,512]{2,1,0:T(8,128)(2,1)S(1)} %pad_maximum_fusion.refs_0_, bf16[4,64,512]{2,1,0:T(8,128)(2,1)S(1)} %constant_dynamic-update-slice_fusion.9.refs_1_, bf16[4,64,512]{2,1,0:T(8,128)(2,1)S(1)} %collective-permute-done.16.refs_2_, ...), custom_call_target="tpu_custom_call" | custom-call | flops 134217728 | bytes 1048576 | tf_op jit(solution)/shard_map/merge/pallas_call | solution.py:232
  49.4 3.9 %all-to-all-start.1 = ((f32[32,4,128]{2,1,0:T(4,128)}), f32[32,4,128]{2,1,0:T(4,128)S(1)}, u32[]{:S(2)}, u32[]{:S(2)}) async-start(f32[32,4,128]{2,1,0:T(4,128)} %bitcast.4), calls=%async_computation.1 | async-start | bytes 131072 | tf_op jit(solution)/shard_map/all_to_all | solution.py:263
  53.3 0.7 %collective-permute-done.11.refs_5_ = bf16[4,2,80,256]{3,2,1,0:T(8,128)(2,1)S(1)} collective-permute-done((bf16[4,2,80,256]{3,2,1,0:T(8,128)(2,1)S(1)}, bf16[4,2,80,256]{3,2,1,0:T(8,128)(2,1)S(1)}, u32[]{:S(2)}, u32[]{:S(2)}) %collective-permute-start.11) | collective-permute-done | bytes 327712 | tf_op jit(solution)/shard_map/ppermute | solution.py:160
  54.0 1.3 %collective-permute-done.8.refs_1_ = bf16[4,2,80,256]{3,2,1,0:T(8,128)(2,1)S(1)} collective-permute-done((bf16[4,2,80,256]{3,2,1,0:T(8,128)(2,1)S(1)}, bf16[4,2,80,256]{3,2,1,0:T(8,128)(2,1)S(1)}, u32[]{:S(2)}, u32[]{:S(2)}) %collective-permute-start.8) | collective-permute-done | bytes 327712 | tf_op jit(solution)/shard_map/ppermute | solution.py:163
  55.4 0.3 collective-permute-done.5.refs_1_
  55.7 5.0 %all-to-all-done.1.start = f32[32,4,128]{2,1,0:T(4,128)S(1)} async-done(((f32[32,4,128]{2,1,0:T(4,128)}), f32[32,4,128]{2,1,0:T(4,128)S(1)}, u32[]{:S(2)}, u32[]{:S(2)}) %all-to-all-start.1) | async-done | bytes 65568 | tf_op jit(solution)/shard_map/all_to_all | solution.py:263
  60.7 0.1 collective-permute-start.19
  60.8 0.4 collective-permute-start.22
  61.2 0.1 collective-permute-start.20
  61.3 0.4 collective-permute-start.21
  61.7 0.1 collective-permute-start.23
  61.8 0.5 collective-permute-done.19.refs_3_
  62.3 1.9 %chain0.1.start = f32[8,2048]{1,0:T(8,128)S(1)} custom-call(s32[6]{0:T(128)S(1)} %copy-done.2, f32[32,4,128]{2,1,0:T(4,128)S(1)} %all-to-all-done.1.start, bf16[4,2,80,256]{3,2,1,0:T(8,128)(2,1)S(1)} %constant_dynamic-update-slice_fusion.refs_0_, bf16[4,2,80,256]{3,2,1,0:T(8,128)(2,1)S(1)} %collective-permute-done.5.refs_1_, ...), custom_call_target="tpu_custom_call" | custom-call | flops 67108864 | bytes 1310720 | tf_op jit(solution)/shard_map/chain0/pallas_call | solution.py:281
  64.3 3.8 %chain1.1 = bf16[4,2048]{1,0:T(4,128)(2,1)} custom-call(s32[6]{0:T(128)S(1)} %copy-done.2, f32[8,2048]{1,0:T(8,128)S(1)} %chain0.1.start, bf16[4,2,80,256]{3,2,1,0:T(8,128)(2,1)S(1)} %constant_dynamic-update-slice_fusion.3.refs_0_, bf16[4,2,80,256]{3,2,1,0:T(8,128)(2,1)S(1)} %collective-permute-done.8.refs_1_, ...), custom_call_target="tpu_custom_call" | custom-call | flops 134217728 | bytes 2621440 | tf_op jit(solution)/shard_map/chain1/pallas_call | solution.py:281
  (35 shorter events, 0.3 us)
Async XLA Ops:
  1.7 5.4 %copy-start.3 = (bf16[64,512]{1,0:T(8,128)(2,1)S(1)}, bf16[64,512]{1,0:T(8,128)(2,1)}, u32[]{:S(2)}) copy-start(bf16[64,512]{1,0:T(8,128)(2,1)} %param.7) | copy-start | bytes 196612
  1.7 13.5 %all-to-all-start = ((bf16[8,80,256]{2,1,0:T(8,128)(2,1)}), bf16[8,80,256]{2,1,0:T(8,128)(2,1)S(1)}, u32[]{:S(2)}, u32[]{:S(2)}) async-start(bf16[8,80,256]{2,1,0:T(8,128)(2,1)} %pack.1), calls=%async_computation | async-start | bytes 655360 | tf_op jit(solution)/shard_map/all_to_all | solution.py:183
  7.1 10.6 %collective-permute-start.1 = (bf16[64,512]{1,0:T(8,128)(2,1)S(1)}, bf16[64,512]{1,0:T(8,128)(2,1)S(1)}, u32[]{:S(2)}, u32[]{:S(2)}) collective-permute-start(bf16[64,512]{1,0:T(8,128)(2,1)S(1)} %copy-done.3), channel_id=1, source_target_pairs={{0,8},{1,9},{2,10},{3,11},{4,12},{5,13},{6,14},{7,15},{8,0},{9,1},... | collective-permute-start | bytes 196616 | tf_op jit(solution)/shard_map/ppermute | solution.py:160
  9.8 5.5 %copy-start.1 = (s32[6]{0:T(128)S(1)}, s32[6]{0:T(128)}, u32[]{:S(2)}) copy-start(s32[6]{0:T(128)} %owners.3) | copy-start | bytes 76
  16.0 11.9 %collective-permute-start = (bf16[5,80,256]{2,1,0:T(8,128)(2,1)S(1)}, bf16[5,80,256]{2,1,0:T(8,128)(2,1)S(1)}, u32[]{:S(2)}, u32[]{:S(2)}) collective-permute-start(bf16[5,80,256]{2,1,0:T(8,128)(2,1)S(1)} %pick.1), channel_id=1, source_target_pairs={{0,8},{1,9},{2,10},{3,11},{4,12},{5,13},{6,14},{7,15},{8,0},{9,1},... | collective-permute-start | bytes 614408 | tf_op jit(solution)/shard_map/ppermute | solution.py:160
  17.8 4.3 %collective-permute-start.2 = (bf16[64,512]{1,0:T(8,128)(2,1)S(1)}, bf16[64,512]{1,0:T(8,128)(2,1)S(1)}, u32[]{:S(2)}, u32[]{:S(2)}) collective-permute-start(bf16[64,512]{1,0:T(8,128)(2,1)S(1)} %get-tuple-element.29), channel_id=1, source_target_pairs={{0,16},{16,0},{1,17},{17,1},{2,18},{18,2},{3,19},{19,3},{4,20},{20... | collective-permute-start | bytes 196616 | tf_op jit(solution)/shard_map/ppermute | solution.py:163
  28.5 9.5 %collective-permute-start.6 = (bf16[1,2,80,256]{3,2,1,0:T(8,128)(2,1)S(1)}, bf16[1,2,80,256]{3,2,1,0:T(8,128)(2,1)S(1)}, u32[]{:S(2)}, u32[]{:S(2)}) collective-permute-start(bf16[1,2,80,256]{3,2,1,0:T(8,128)(2,1)S(1)} %get-tuple-element.21), channel_id=1, source_target_pairs={{0,2},{1,3},{2,0},{3,1},{4,6},{5,7},{6,4},{7,5},{8,10},{9,11},{10,... | collective-permute-start | bytes 245768 | tf_op jit(solution)/shard_map/ppermute | solution.py:160
  29.9 8.7 %collective-permute-start.3 = (bf16[1,2,80,256]{3,2,1,0:T(8,128)(2,1)S(1)}, bf16[1,2,80,256]{3,2,1,0:T(8,128)(2,1)S(1)}, u32[]{:S(2)}, u32[]{:S(2)}) collective-permute-start(bf16[1,2,80,256]{3,2,1,0:T(8,128)(2,1)S(1)} %get-tuple-element.20), channel_id=1, source_target_pairs={{0,16},{16,0},{1,17},{17,1},{2,18},{18,2},{3,19},{19,3},{4,20},{20... | collective-permute-start | bytes 245768 | tf_op jit(solution)/shard_map/ppermute | solution.py:163
  31.4 4.3 %collective-permute-start.12 = (bf16[1,64,512]{2,1,0:T(8,128)(2,1)S(1)}, bf16[1,64,512]{2,1,0:T(8,128)(2,1)S(1)}, u32[]{:S(2)}, u32[]{:S(2)}) collective-permute-start(bf16[1,64,512]{2,1,0:T(8,128)(2,1)S(1)} %bitcast.5), channel_id=1, source_target_pairs={{0,2},{1,3},{2,0},{3,1},{4,6},{5,7},{6,4},{7,5},{8,10},{9,11},{10,... | collective-permute-start | bytes 196616 | tf_op jit(solution)/shard_map/ppermute | solution.py:160
  32.1 4.3 %collective-permute-start.13 = (bf16[1,64,512]{2,1,0:T(8,128)(2,1)S(1)}, bf16[1,64,512]{2,1,0:T(8,128)(2,1)S(1)}, u32[]{:S(2)}, u32[]{:S(2)}) collective-permute-start(bf16[1,64,512]{2,1,0:T(8,128)(2,1)S(1)} %bitcast.9), channel_id=1, source_target_pairs={{0,4},{1,5},{2,6},{3,7},{4,0},{5,1},{6,2},{7,3},{8,12},{9,13},{10,... | collective-permute-start | bytes 196616 | tf_op jit(solution)/shard_map/ppermute | solution.py:160
  32.1 5.7 %collective-permute-start.9 = (bf16[1,2,80,256]{3,2,1,0:T(8,128)(2,1)S(1)}, bf16[1,2,80,256]{3,2,1,0:T(8,128)(2,1)S(1)}, u32[]{:S(2)}, u32[]{:S(2)}) collective-permute-start(bf16[1,2,80,256]{3,2,1,0:T(8,128)(2,1)S(1)} %get-tuple-element.22), channel_id=1, source_target_pairs={{0,4},{1,5},{2,6},{3,7},{4,0},{5,1},{6,2},{7,3},{8,12},{9,13},{10,... | collective-permute-start | bytes 245768 | tf_op jit(solution)/shard_map/ppermute | solution.py:160
  35.7 5.0 %collective-permute-start.14 = (bf16[2,64,512]{2,1,0:T(8,128)(2,1)S(1)}, bf16[2,64,512]{2,1,0:T(8,128)(2,1)S(1)}, u32[]{:S(2)}, u32[]{:S(2)}) collective-permute-start(bf16[2,64,512]{2,1,0:T(8,128)(2,1)S(1)} %pad_maximum_fusion.4), channel_id=1, source_target_pairs={{0,4},{1,5},{2,6},{3,7},{4,0},{5,1},{6,2},{7,3},{8,12},{9,13},{10,... | collective-permute-start | bytes 393224 | tf_op jit(solution)/shard_map/ppermute | solution.py:160
  36.4 5.3 %collective-permute-start.15 = (bf16[2,64,512]{2,1,0:T(8,128)(2,1)S(1)}, bf16[2,64,512]{2,1,0:T(8,128)(2,1)S(1)}, u32[]{:S(2)}, u32[]{:S(2)}) collective-permute-start(bf16[2,64,512]{2,1,0:T(8,128)(2,1)S(1)} %pad_maximum_fusion.5), channel_id=1, source_target_pairs={{0,2},{1,3},{2,0},{3,1},{4,6},{5,7},{6,4},{7,5},{8,10},{9,11},{10,... | collective-permute-start | bytes 393224 | tf_op jit(solution)/shard_map/ppermute | solution.py:160
  37.8 10.4 %collective-permute-start.16 = (bf16[4,64,512]{2,1,0:T(8,128)(2,1)S(1)}, bf16[4,64,512]{2,1,0:T(8,128)(2,1)S(1)}, u32[]{:S(2)}, u32[]{:S(2)}) collective-permute-start(bf16[4,64,512]{2,1,0:T(8,128)(2,1)S(1)} %pad_maximum_fusion.refs_0_), channel_id=1, source_target_pairs={{0,1},{1,0},{2,3},{3,2},{4,5},{5,4},{6,7},{7,6},{8,9},{9,8},{10,11... | collective-permute-start | bytes 786440 | tf_op jit(solution)/shard_map/ppermute | solution.py:160
  38.0 6.7 %collective-permute-start.10 = (bf16[2,2,80,256]{3,2,1,0:T(8,128)(2,1)S(1)}, bf16[2,2,80,256]{3,2,1,0:T(8,128)(2,1)S(1)}, u32[]{:S(2)}, u32[]{:S(2)}) collective-permute-start(bf16[2,2,80,256]{3,2,1,0:T(8,128)(2,1)S(1)} %pad_maximum_fusion.3), channel_id=1, source_target_pairs={{0,16},{16,0},{1,17},{17,1},{2,18},{18,2},{3,19},{19,3},{4,20},{20... | collective-permute-start | bytes 491528 | tf_op jit(solution)/shard_map/ppermute | solution.py:163
  38.6 9.7 %copy-start = (bf16[4096,128]{1,0:T(8,128)(2,1)S(1)}, bf16[4096,128]{1,0:T(8,128)(2,1)}, u32[]{:S(2)}) copy-start(bf16[4096,128]{1,0:T(8,128)(2,1)} %sub.6) | copy-start | bytes 3145732
  38.6 7.6 %collective-permute-start.7 = (bf16[2,2,80,256]{3,2,1,0:T(8,128)(2,1)S(1)}, bf16[2,2,80,256]{3,2,1,0:T(8,128)(2,1)S(1)}, u32[]{:S(2)}, u32[]{:S(2)}) collective-permute-start(bf16[2,2,80,256]{3,2,1,0:T(8,128)(2,1)S(1)} %pad_maximum_fusion.2), channel_id=1, source_target_pairs={{0,4},{1,5},{2,6},{3,7},{4,0},{5,1},{6,2},{7,3},{8,12},{9,13},{10,... | collective-permute-start | bytes 491528 | tf_op jit(solution)/shard_map/ppermute | solution.py:160
  40.7 5.9 %collective-permute-start.4 = (bf16[2,2,80,256]{3,2,1,0:T(8,128)(2,1)S(1)}, bf16[2,2,80,256]{3,2,1,0:T(8,128)(2,1)S(1)}, u32[]{:S(2)}, u32[]{:S(2)}) collective-permute-start(bf16[2,2,80,256]{3,2,1,0:T(8,128)(2,1)S(1)} %pad_maximum_fusion.1), channel_id=1, source_target_pairs={{0,2},{1,3},{2,0},{3,1},{4,6},{5,7},{6,4},{7,5},{8,10},{9,11},{10,... | collective-permute-start | bytes 491528 | tf_op jit(solution)/shard_map/ppermute | solution.py:160
  41.7 6.6 %collective-permute-start.17 = (bf16[4,64,512]{2,1,0:T(8,128)(2,1)S(1)}, bf16[4,64,512]{2,1,0:T(8,128)(2,1)S(1)}, u32[]{:S(2)}, u32[]{:S(2)}) collective-permute-start(bf16[4,64,512]{2,1,0:T(8,128)(2,1)S(1)} %constant_dynamic-update-slice_fusion.9.refs_1_), channel_id=1, source_target_pairs={{0,1},{1,0},{2,3},{3,2},{4,5},{5,4},{6,7},{7,6},{8,9},{9,8},{10,11... | collective-permute-start | bytes 786440 | tf_op jit(solution)/shard_map/ppermute | solution.py:160
  44.6 9.4 %collective-permute-start.11 = (bf16[4,2,80,256]{3,2,1,0:T(8,128)(2,1)S(1)}, bf16[4,2,80,256]{3,2,1,0:T(8,128)(2,1)S(1)}, u32[]{:S(2)}, u32[]{:S(2)}) collective-permute-start(bf16[4,2,80,256]{3,2,1,0:T(8,128)(2,1)S(1)} %constant_dynamic-update-slice_fusion.6.refs_4_), channel_id=1, source_target_pairs={{0,2},{1,3},{2,0},{3,1},{4,6},{5,7},{6,4},{7,5},{8,10},{9,11},{10,... | collective-permute-start | bytes 983048 | tf_op jit(solution)/shard_map/ppermute | solution.py:160
  46.2 9.1 %collective-permute-start.8 = (bf16[4,2,80,256]{3,2,1,0:T(8,128)(2,1)S(1)}, bf16[4,2,80,256]{3,2,1,0:T(8,128)(2,1)S(1)}, u32[]{:S(2)}, u32[]{:S(2)}) collective-permute-start(bf16[4,2,80,256]{3,2,1,0:T(8,128)(2,1)S(1)} %constant_dynamic-update-slice_fusion.3.refs_0_), channel_id=1, source_target_pairs={{0,16},{16,0},{1,17},{17,1},{2,18},{18,2},{3,19},{19,3},{4,20},{20... | collective-permute-start | bytes 983048 | tf_op jit(solution)/shard_map/ppermute | solution.py:163
  46.6 9.0 %collective-permute-start.5 = (bf16[4,2,80,256]{3,2,1,0:T(8,128)(2,1)S(1)}, bf16[4,2,80,256]{3,2,1,0:T(8,128)(2,1)S(1)}, u32[]{:S(2)}, u32[]{:S(2)}) collective-permute-start(bf16[4,2,80,256]{3,2,1,0:T(8,128)(2,1)S(1)} %constant_dynamic-update-slice_fusion.refs_0_), channel_id=1, source_target_pairs={{0,4},{1,5},{2,6},{3,7},{4,0},{5,1},{6,2},{7,3},{8,12},{9,13},{10,... | collective-permute-start | bytes 983048 | tf_op jit(solution)/shard_map/ppermute | solution.py:160
  48.3 13.4 %collective-permute-start.18 = (bf16[4,2,80,256]{3,2,1,0:T(8,128)(2,1)S(1)}, bf16[4,2,80,256]{3,2,1,0:T(8,128)(2,1)S(1)}, u32[]{:S(2)}, u32[]{:S(2)}) collective-permute-start(bf16[4,2,80,256]{3,2,1,0:T(8,128)(2,1)S(1)} %constant_dynamic-update-slice_fusion.refs_0_), channel_id=1, source_target_pairs={{0,1},{1,0},{2,3},{3,2},{4,5},{5,4},{6,7},{7,6},{8,9},{9,8},{10,11... | collective-permute-start | bytes 983048 | tf_op jit(solution)/shard_map/ppermute | solution.py:160
  49.4 12.9 %copy-start.2 = (s32[6]{0:T(128)S(1)}, s32[6]{0:T(128)}, u32[]{:S(2)}) copy-start(s32[6]{0:T(128)} %offsets.3) | copy-start | bytes 76
  49.4 11.3 %all-to-all-start.1 = ((f32[32,4,128]{2,1,0:T(4,128)}), f32[32,4,128]{2,1,0:T(4,128)S(1)}, u32[]{:S(2)}, u32[]{:S(2)}) async-start(f32[32,4,128]{2,1,0:T(4,128)} %bitcast.4), calls=%async_computation.1 | async-start | bytes 131072 | tf_op jit(solution)/shard_map/all_to_all | solution.py:263
  60.7 1.6 %collective-permute-start.19 = (bf16[4,2,80,256]{3,2,1,0:T(8,128)(2,1)S(1)}, bf16[4,2,80,256]{3,2,1,0:T(8,128)(2,1)S(1)}, u32[]{:S(2)}, u32[]{:S(2)}) collective-permute-start(bf16[4,2,80,256]{3,2,1,0:T(8,128)(2,1)S(1)} %collective-permute-done.5.refs_1_), channel_id=1, source_target_pairs={{0,1},{1,0},{2,3},{3,2},{4,5},{5,4},{6,7},{7,6},{8,9},{9,8},{10,11... | collective-permute-start | bytes 983048 | tf_op jit(solution)/shard_map/ppermute | solution.py:160
  60.8 3.4 %collective-permute-start.22 = (bf16[4,2,80,256]{3,2,1,0:T(8,128)(2,1)S(1)}, bf16[4,2,80,256]{3,2,1,0:T(8,128)(2,1)S(1)}, u32[]{:S(2)}, u32[]{:S(2)}) collective-permute-start(bf16[4,2,80,256]{3,2,1,0:T(8,128)(2,1)S(1)} %constant_dynamic-update-slice_fusion.6.refs_4_), channel_id=1, source_target_pairs={{0,1},{1,0},{2,3},{3,2},{4,5},{5,4},{6,7},{7,6},{8,9},{9,8},{10,11... | collective-permute-start | bytes 983048 | tf_op jit(solution)/shard_map/ppermute | solution.py:160
  61.2 3.0 %collective-permute-start.20 = (bf16[4,2,80,256]{3,2,1,0:T(8,128)(2,1)S(1)}, bf16[4,2,80,256]{3,2,1,0:T(8,128)(2,1)S(1)}, u32[]{:S(2)}, u32[]{:S(2)}) collective-permute-start(bf16[4,2,80,256]{3,2,1,0:T(8,128)(2,1)S(1)} %constant_dynamic-update-slice_fusion.3.refs_0_), channel_id=1, source_target_pairs={{0,1},{1,0},{2,3},{3,2},{4,5},{5,4},{6,7},{7,6},{8,9},{9,8},{10,11... | collective-permute-start | bytes 983048 | tf_op jit(solution)/shard_map/ppermute | solution.py:160
  61.3 2.9 %collective-permute-start.21 = (bf16[4,2,80,256]{3,2,1,0:T(8,128)(2,1)S(1)}, bf16[4,2,80,256]{3,2,1,0:T(8,128)(2,1)S(1)}, u32[]{:S(2)}, u32[]{:S(2)}) collective-permute-start(bf16[4,2,80,256]{3,2,1,0:T(8,128)(2,1)S(1)} %collective-permute-done.8.refs_1_), channel_id=1, source_target_pairs={{0,1},{1,0},{2,3},{3,2},{4,5},{5,4},{6,7},{7,6},{8,9},{9,8},{10,11... | collective-permute-start | bytes 983048 | tf_op jit(solution)/shard_map/ppermute | solution.py:160
  61.7 2.5 %collective-permute-start.23 = (bf16[4,2,80,256]{3,2,1,0:T(8,128)(2,1)S(1)}, bf16[4,2,80,256]{3,2,1,0:T(8,128)(2,1)S(1)}, u32[]{:S(2)}, u32[]{:S(2)}) collective-permute-start(bf16[4,2,80,256]{3,2,1,0:T(8,128)(2,1)S(1)} %collective-permute-done.11.refs_5_), channel_id=1, source_target_pairs={{0,1},{1,0},{2,3},{3,2},{4,5},{5,4},{6,7},{7,6},{8,9},{9,8},{10,11... | collective-permute-start | bytes 983048 | tf_op jit(solution)/shard_map/ppermute | solution.py:160

commit v18 on v17

--- a/solution.py
+++ b/solution.py
@@ -81,7 +81,7 @@
 
 
 def merge_kernel(rows, cols, tags, sub, *refs):
-    held, total = refs[:-1], refs[-1]
+    held, outs, total = refs[: -rows - 1], refs[-rows - 1 : -1], refs[-1]
     row, col = lax.axis_index("row"), lax.axis_index("col")
     deep, tall = held[0].shape[2], held[0].shape[1]
     total[...] = jnp.zeros_like(total)
@@ -91,6 +91,8 @@
             part = jnp.dot(ref[index], sub[aligned(j, deep), :], preferred_element_type=jnp.float32)
             at = aligned(jnp.bitwise_xor(row, row_mask), tall)
             total[at, :] = total[at, :] + part
+    for row_mask, out in enumerate(outs):
+        out[...] = total[aligned(jnp.bitwise_xor(row, row_mask), tall), :]
 
 
 def two_terms(x):
@@ -115,8 +117,8 @@
             basis_all[to, aligned(e, pv), :] = ref[index, :, :pv, :]
             factor_all[to, aligned(e, pt), :] = ref[index, :, pv:, :]
     if first:
-        n, each, width = start.shape
-        pieces = start[...].reshape(n // cols, cols, each, width).sum(0)
+        pieces = start[...]
+        each = pieces.shape[1]
         x = jnp.concatenate([pieces[c] for c in range(cols)], 1)
         x = jnp.concatenate([x] + [jnp.zeros_like(x)] * (8 // each - 1), 0)
     else:
@@ -231,9 +233,10 @@
     each = wanted // (rows * cols)
     merged = pl.pallas_call(
         functools.partial(merge_kernel, rows, cols, tags),
-        out_shape=jax.ShapeDtypeStruct((wanted, width), jnp.float32),
+        out_shape=[jax.ShapeDtypeStruct((wanted // rows, width), jnp.float32)] * rows,
         in_specs=[VMEM] + [VMEM] * len(m_held),
-        out_specs=VMEM,
+        out_specs=[VMEM] * rows,
+        scratch_shapes=[pltpu.VMEM((wanted, width), jnp.float32)],
         compiler_params=limit(8),
         cost_estimate=cost([sub_vectors], 2 * wanted * sub_vectors.size),
         name="merge",
@@ -260,7 +263,9 @@
             mask, send = links[(k + step) % 3]
             colours[k] = jnp.concatenate([colours[k], send(colours[k])])
             masks[k] = masks[k] + [m ^ mask for m in masks[k]]
-    state = lax.all_to_all(merged.reshape(rows * cols, each, width), ("row", "col"), 0, 0)
+    colours[-1], merged = lax.optimization_barrier((colours[-1], list(merged)))
+    merged = merged[0] + sum(over_row(merged[m], m) for m in range(1, rows))
+    state = lax.all_to_all(merged.reshape(cols, each, width), "col", 0, 0)
     last_round = []
     for k in range(COLOURS):
         mask, send = links[(k + 2) % 3]

time: 68.3 us -> 71.5 us (1.047)
  blocking collectives: 0 us -> 11.3 us
  starting transfers between devices: 30.4 us -> 26.6 us
  waiting for transfers between devices: 27.3 us -> 23.6 us
    all_to_all x0 -> x1, blocking collectives: none -> 11.3 us  [local(): state = lax.all_to_all(merged.reshape(cols, each, width), 'col', 0, 0)]
    all_to_all x1 -> x0, waiting for transfers between devices: 5.03 us -> none  [local(): lax.all_to_all(merged.reshape(rows * cols, each, width), ('row', 'col'),...]
    all_to_all x1 -> x0, starting transfers between devices: 3.89 us -> none  [local(): lax.all_to_all(merged.reshape(rows * cols, each, width), ('row', 'col'),...]
    ppermute x4 -> x5, starting transfers between devices: 4.06 us -> 6.17 us  [over_row(): return lax.ppermute(x, 'row', [(r, r ^ mask) for r in range(rows)])]
    ppermute x20, starting transfers between devices: 17.1 us -> 15 us  [over_col(): return lax.ppermute(x, 'col', [(c, c ^ mask) for c in range(cols)])]
    ppermute x20, waiting for transfers between devices: 9.88 us -> 11.6 us  [over_col(): return lax.ppermute(x, 'col', [(c, c ^ mask) for c in range(cols)])]
    ppermute x4 -> x5, waiting for transfers between devices: 6.94 us -> 6.5 us  [over_row(): return lax.ppermute(x, 'row', [(r, r ^ mask) for r in range(rows)])]
  transfers between devices with their start and end apart: 26 -> 26, of which waited for: 12 -> 9; matrix products, arithmetic and copies ran while one was open for 0% -> 0% of each run, Pallas kernels for 5% -> 5%
where the time goes in v18:
time: 71.5 us; the launch traced here: 71.2 us
  starting transfers between devices  26.6 us (37%)
  waiting for transfers between devices  23.6 us (33%)
  blocking collectives  11.3 us (16%)
  Pallas kernels  9.15 us (13%)
    ppermute x20, starting transfers between devices, over_col(): return lax.ppermute(x, 'col', [(c, c ^ mask) for c in range(cols)])  15 us
    ppermute x20, waiting for transfers between devices, over_col(): return lax.ppermute(x, 'col', [(c, c ^ mask) for c in range(cols)])  11.6 us
    all_to_all x1, blocking collectives, local(): state = lax.all_to_all(merged.reshape(cols, each, width), 'col', 0, 0)  11.3 us
    ppermute x5, waiting for transfers between devices, over_row(): return lax.ppermute(x, 'row', [(r, r ^ mask) for r in range(rows)])  6.5 us
    ppermute x5, starting transfers between devices, over_row(): return lax.ppermute(x, 'row', [(r, r ^ mask) for r in range(rows)])  6.17 us
    pallas_call x2, Pallas kernels, local(): pl.pallas_call(functools.partial(chain_kernel, cols, groups, slots, sum((...  5.68 us
    all_to_all x1, waiting for transfers between devices, local(): slices = lax.all_to_all(packed, 'col', 0, 0, axis_index_groups=members)  5.48 us
    all_to_all x1, starting transfers between devices, local(): slices = lax.all_to_all(packed, 'col', 0, 0, axis_index_groups=members)  5.4 us
  transfers between devices with their start and end apart: 26, of which 9 were waited for; matrix products, arithmetic and copies ran while one was open for 0% of the time, Pallas kernels for 5%

profile of v18, /device:TPU:0, one launch (start us, length us, event | category | flops | bytes accessed | tf_op | source)
XLA Modules:
  0.0 71.2 jit_solution(14159092401326479316)
XLA Ops:
  0.0 1.7 %pack.1 = bf16[8,80,256]{2,1,0:T(8,128)(2,1)} custom-call(bf16[16,64,256]{2,1,0:T(8,128)(2,1)} %bitcast.8, bf16[16,16,256]{2,1,0:T(8,128)(2,1)} %bitcast.12), custom_call_target="tpu_custom_call" | custom-call | bytes 655360 | tf_op jit(solution)/shard_map/pack/pallas_call | solution.py:173
  1.7 0.0 copy-start.3
  1.7 5.4 %all-to-all-start = ((bf16[8,80,256]{2,1,0:T(8,128)(2,1)}), bf16[8,80,256]{2,1,0:T(8,128)(2,1)S(1)}, u32[]{:S(2)}, u32[]{:S(2)}) async-start(bf16[8,80,256]{2,1,0:T(8,128)(2,1)} %pack.1), calls=%async_computation | async-start | bytes 655360 | tf_op jit(solution)/shard_map/all_to_all | solution.py:185
  7.1 2.7 %collective-permute-start.1 = (bf16[64,512]{1,0:T(8,128)(2,1)S(1)}, bf16[64,512]{1,0:T(8,128)(2,1)S(1)}, u32[]{:S(2)}, u32[]{:S(2)}) collective-permute-start(bf16[64,512]{1,0:T(8,128)(2,1)S(1)} %copy-done.3), channel_id=1, source_target_pairs={{0,8},{1,9},{2,10},{3,11},{4,12},{5,13},{6,14},{7,15},{8,0},{9,1},... | collective-permute-start | bytes 196616 | tf_op jit(solution)/shard_map/ppermute | solution.py:162
  9.8 5.5 %all-to-all-done.held = bf16[8,80,256]{2,1,0:T(8,128)(2,1)S(1)} async-done(((bf16[8,80,256]{2,1,0:T(8,128)(2,1)}), bf16[8,80,256]{2,1,0:T(8,128)(2,1)S(1)}, u32[]{:S(2)}, u32[]{:S(2)}) %all-to-all-start) | async-done | bytes 327712 | tf_op jit(solution)/shard_map/all_to_all | solution.py:185
  15.3 0.7 pick.1
  16.0 1.8 %collective-permute-start = (bf16[5,80,256]{2,1,0:T(8,128)(2,1)S(1)}, bf16[5,80,256]{2,1,0:T(8,128)(2,1)S(1)}, u32[]{:S(2)}, u32[]{:S(2)}) collective-permute-start(bf16[5,80,256]{2,1,0:T(8,128)(2,1)S(1)} %pick.1), channel_id=1, source_target_pairs={{0,8},{1,9},{2,10},{3,11},{4,12},{5,13},{6,14},{7,15},{8,0},{9,1},... | collective-permute-start | bytes 614408 | tf_op jit(solution)/shard_map/ppermute | solution.py:162
  17.8 0.0 collective-permute-done.1
  17.8 1.6 %collective-permute-start.2 = (bf16[64,512]{1,0:T(8,128)(2,1)S(1)}, bf16[64,512]{1,0:T(8,128)(2,1)S(1)}, u32[]{:S(2)}, u32[]{:S(2)}) collective-permute-start(bf16[64,512]{1,0:T(8,128)(2,1)S(1)} %get-tuple-element.39), channel_id=1, source_target_pairs={{0,16},{16,0},{1,17},{17,1},{2,18},{18,2},{3,19},{19,3},{4,20},{20... | collective-permute-start | bytes 196616 | tf_op jit(solution)/shard_map/ppermute | solution.py:165
  19.3 2.8 %collective-permute-done.2 = bf16[64,512]{1,0:T(8,128)(2,1)S(1)} collective-permute-done((bf16[64,512]{1,0:T(8,128)(2,1)S(1)}, bf16[64,512]{1,0:T(8,128)(2,1)S(1)}, u32[]{:S(2)}, u32[]{:S(2)}) %collective-permute-start.2) | collective-permute-done | bytes 65568 | tf_op jit(solution)/shard_map/ppermute | solution.py:165
  22.1 5.8 %collective-permute-done.refs_0_ = bf16[5,80,256]{2,1,0:T(8,128)(2,1)S(1)} collective-permute-done((bf16[5,80,256]{2,1,0:T(8,128)(2,1)S(1)}, bf16[5,80,256]{2,1,0:T(8,128)(2,1)S(1)}, u32[]{:S(2)}, u32[]{:S(2)}) %collective-permute-start) | collective-permute-done | bytes 204832 | tf_op jit(solution)/shard_map/ppermute | solution.py:162
  27.9 1.3 %collective-permute-start.11 = (bf16[1,64,512]{2,1,0:T(8,128)(2,1)S(1)}, bf16[1,64,512]{2,1,0:T(8,128)(2,1)S(1)}, u32[]{:S(2)}, u32[]{:S(2)}) collective-permute-start(bf16[1,64,512]{2,1,0:T(8,128)(2,1)S(1)} %bitcast.5), channel_id=1, source_target_pairs={{0,2},{1,3},{2,0},{3,1},{4,6},{5,7},{6,4},{7,5},{8,10},{9,11},{10,... | collective-permute-start | bytes 196616 | tf_op jit(solution)/shard_map/ppermute | solution.py:162
  29.2 0.0 collective-permute-start.12
  29.2 0.6 order.1
  29.8 2.1 %collective-permute-start.9 = (bf16[1,2,80,256]{3,2,1,0:T(8,128)(2,1)S(1)}, bf16[1,2,80,256]{3,2,1,0:T(8,128)(2,1)S(1)}, u32[]{:S(2)}, u32[]{:S(2)}) collective-permute-start(bf16[1,2,80,256]{3,2,1,0:T(8,128)(2,1)S(1)} %get-tuple-element.27), channel_id=1, source_target_pairs={{0,4},{1,5},{2,6},{3,7},{4,0},{5,1},{6,2},{7,3},{8,12},{9,13},{10,... | collective-permute-start | bytes 245768 | tf_op jit(solution)/shard_map/ppermute | solution.py:162
  31.9 0.7 %collective-permute-start.6 = (bf16[1,2,80,256]{3,2,1,0:T(8,128)(2,1)S(1)}, bf16[1,2,80,256]{3,2,1,0:T(8,128)(2,1)S(1)}, u32[]{:S(2)}, u32[]{:S(2)}) collective-permute-start(bf16[1,2,80,256]{3,2,1,0:T(8,128)(2,1)S(1)} %get-tuple-element.26), channel_id=1, source_target_pairs={{0,2},{1,3},{2,0},{3,1},{4,6},{5,7},{6,4},{7,5},{8,10},{9,11},{10,... | collective-permute-start | bytes 245768 | tf_op jit(solution)/shard_map/ppermute | solution.py:162
  32.6 1.5 %collective-permute-start.3 = (bf16[1,2,80,256]{3,2,1,0:T(8,128)(2,1)S(1)}, bf16[1,2,80,256]{3,2,1,0:T(8,128)(2,1)S(1)}, u32[]{:S(2)}, u32[]{:S(2)}) collective-permute-start(bf16[1,2,80,256]{3,2,1,0:T(8,128)(2,1)S(1)} %get-tuple-element.25), channel_id=1, source_target_pairs={{0,16},{16,0},{1,17},{17,1},{2,18},{18,2},{3,19},{19,3},{4,20},{20... | collective-permute-start | bytes 245768 | tf_op jit(solution)/shard_map/ppermute | solution.py:165
  34.2 0.1 collective-permute-start.13
  34.3 1.4 %collective-permute-start.14 = (bf16[2,64,512]{2,1,0:T(8,128)(2,1)S(1)}, bf16[2,64,512]{2,1,0:T(8,128)(2,1)S(1)}, u32[]{:S(2)}, u32[]{:S(2)}) collective-permute-start(bf16[2,64,512]{2,1,0:T(8,128)(2,1)S(1)} %pad_maximum_fusion.6), channel_id=1, source_target_pairs={{0,2},{1,3},{2,0},{3,1},{4,6},{5,7},{6,4},{7,5},{8,10},{9,11},{10,... | collective-permute-start | bytes 393224 | tf_op jit(solution)/shard_map/ppermute | solution.py:162
  35.7 0.0 collective-permute-done.9
  35.7 0.1 collective-permute-start.15
  35.8 1.2 %collective-permute-done.6 = bf16[1,2,80,256]{3,2,1,0:T(8,128)(2,1)S(1)} collective-permute-done((bf16[1,2,80,256]{3,2,1,0:T(8,128)(2,1)S(1)}, bf16[1,2,80,256]{3,2,1,0:T(8,128)(2,1)S(1)}, u32[]{:S(2)}, u32[]{:S(2)}) %collective-permute-start.6) | collective-permute-done | bytes 81952 | tf_op jit(solution)/shard_map/ppermute | solution.py:162
  37.0 1.6 %collective-permute-start.10 = (bf16[2,2,80,256]{3,2,1,0:T(8,128)(2,1)S(1)}, bf16[2,2,80,256]{3,2,1,0:T(8,128)(2,1)S(1)}, u32[]{:S(2)}, u32[]{:S(2)}) collective-permute-start(bf16[2,2,80,256]{3,2,1,0:T(8,128)(2,1)S(1)} %pad_maximum_fusion.4), channel_id=1, source_target_pairs={{0,16},{16,0},{1,17},{17,1},{2,18},{18,2},{3,19},{19,3},{4,20},{20... | collective-permute-start | bytes 491528 | tf_op jit(solution)/shard_map/ppermute | solution.py:165
  38.6 0.0 collective-permute-done.3
  38.7 0.1 collective-permute-start.7
  38.8 0.0 copy-start
  38.9 0.3 collective-permute-done.13
  39.2 1.3 %collective-permute-start.4 = (bf16[2,2,80,256]{3,2,1,0:T(8,128)(2,1)S(1)}, bf16[2,2,80,256]{3,2,1,0:T(8,128)(2,1)S(1)}, u32[]{:S(2)}, u32[]{:S(2)}) collective-permute-start(bf16[2,2,80,256]{3,2,1,0:T(8,128)(2,1)S(1)} %pad_maximum_fusion.2), channel_id=1, source_target_pairs={{0,2},{1,3},{2,0},{3,1},{4,6},{5,7},{6,4},{7,5},{8,10},{9,11},{10,... | collective-permute-start | bytes 491528 | tf_op jit(solution)/shard_map/ppermute | solution.py:162
  40.5 0.0 collective-permute-done.14
  40.5 0.1 collective-permute-start.16
  40.6 3.4 %collective-permute-done.7 = bf16[2,2,80,256]{3,2,1,0:T(8,128)(2,1)S(1)} collective-permute-done((bf16[2,2,80,256]{3,2,1,0:T(8,128)(2,1)S(1)}, bf16[2,2,80,256]{3,2,1,0:T(8,128)(2,1)S(1)}, u32[]{:S(2)}, u32[]{:S(2)}) %collective-permute-start.7) | collective-permute-done | bytes 163872 | tf_op jit(solution)/shard_map/ppermute | solution.py:162
  44.1 0.6 collective-permute-start.8
  44.6 0.3 collective-permute-done.4
  45.0 1.5 %collective-permute-start.5 = (bf16[4,2,80,256]{3,2,1,0:T(8,128)(2,1)S(1)}, bf16[4,2,80,256]{3,2,1,0:T(8,128)(2,1)S(1)}, u32[]{:S(2)}, u32[]{:S(2)}) collective-permute-start(bf16[4,2,80,256]{3,2,1,0:T(8,128)(2,1)S(1)} %constant_dynamic-update-slice_fusion.refs_0_), channel_id=1, source_target_pairs={{0,4},{1,5},{2,6},{3,7},{4,0},{5,1},{6,2},{7,3},{8,12},{9,13},{10,... | collective-permute-start | bytes 983048 | tf_op jit(solution)/shard_map/ppermute | solution.py:162
  46.5 0.0 collective-permute-done.15.refs_2_
  46.5 0.5 merge.1
  47.0 0.8 %collective-permute-start.17 = (bf16[4,2,80,256]{3,2,1,0:T(8,128)(2,1)S(1)}, bf16[4,2,80,256]{3,2,1,0:T(8,128)(2,1)S(1)}, u32[]{:S(2)}, u32[]{:S(2)}) collective-permute-start(bf16[4,2,80,256]{3,2,1,0:T(8,128)(2,1)S(1)} %pad_maximum_fusion.refs_4_), channel_id=1, source_target_pairs={{0,2},{1,3},{2,0},{3,1},{4,6},{5,7},{6,4},{7,5},{8,10},{9,11},{10,... | collective-permute-start | bytes 983048 | tf_op jit(solution)/shard_map/ppermute | solution.py:162
  47.8 0.9 %collective-permute-start.18 = (f32[64,128]{1,0:T(8,128)S(1)}, f32[64,128]{1,0:T(8,128)S(1)}, u32[]{:S(2)}, u32[]{:S(2)}) collective-permute-start(f32[64,128]{1,0:T(8,128)S(1)} %get-tuple-element.34), channel_id=1, source_target_pairs={{0,16},{16,0},{1,17},{17,1},{2,18},{18,2},{3,19},{19,3},{4,20},{20... | collective-permute-start | bytes 98312 | tf_op jit(solution)/shard_map/ppermute | solution.py:165
  48.7 3.7 %collective-permute-done.18 = f32[64,128]{1,0:T(8,128)S(1)} collective-permute-done((f32[64,128]{1,0:T(8,128)S(1)}, f32[64,128]{1,0:T(8,128)S(1)}, u32[]{:S(2)}, u32[]{:S(2)}) %collective-permute-start.18) | collective-permute-done | bytes 32800 | tf_op jit(solution)/shard_map/ppermute | solution.py:165
  52.5 11.3 %all_to_all.10.start = f32[16,4,128]{2,1,0:T(4,128)S(1)} all-to-all(f32[16,4,128]{2,1,0:T(4,128)S(1)} %bitcast.13), channel_id=1, replica_groups=mesh['row'=2,'col'=16] {'col'}, dimensions={0} | all-to-all | bytes 65536 | tf_op jit(solution)/shard_map/all_to_all | solution.py:268
  63.8 0.1 collective-permute-start.20
  63.8 0.5 collective-permute-start.21
  64.3 0.1 collective-permute-start.23
  64.4 0.4 collective-permute-start.22
  64.8 0.1 collective-permute-start.24
  64.9 0.5 collective-permute-done.20.refs_3_
  65.5 1.9 %chain0.1.start = f32[8,2048]{1,0:T(8,128)S(1)} custom-call(s32[6]{0:T(128)S(1)} %copy-done.1, f32[16,4,128]{2,1,0:T(4,128)S(1)} %all_to_all.10.start, bf16[4,2,80,256]{3,2,1,0:T(8,128)(2,1)S(1)} %constant_dynamic-update-slice_fusion.refs_0_, bf16[4,2,80,256]{3,2,1,0:T(8,128)(2,1)S(1)} %collective-permute-done.5.refs_1_, ...), custom_call_target="tpu_custom_call" | custom-call | flops 67108864 | bytes 1310720 | tf_op jit(solution)/shard_map/chain0/pallas_call | solution.py:286
  67.4 3.8 %chain1.1 = bf16[4,2048]{1,0:T(4,128)(2,1)} custom-call(s32[6]{0:T(128)S(1)} %copy-done.1, f32[8,2048]{1,0:T(8,128)S(1)} %chain0.1.start, bf16[4,2,80,256]{3,2,1,0:T(8,128)(2,1)S(1)} %constant_dynamic-update-slice_fusion.3.refs_0_, bf16[4,2,80,256]{3,2,1,0:T(8,128)(2,1)S(1)} %collective-permute-done.8.refs_1_, ...), custom_call_target="tpu_custom_call" | custom-call | flops 134217728 | bytes 2621440 | tf_op jit(solution)/shard_map/chain1/pallas_call | solution.py:286
  (35 shorter events, 0.3 us)
Async XLA Ops:
  1.7 5.4 %copy-start.3 = (bf16[64,512]{1,0:T(8,128)(2,1)S(1)}, bf16[64,512]{1,0:T(8,128)(2,1)}, u32[]{:S(2)}) copy-start(bf16[64,512]{1,0:T(8,128)(2,1)} %param.7) | copy-start | bytes 196612
  1.7 13.5 %all-to-all-start = ((bf16[8,80,256]{2,1,0:T(8,128)(2,1)}), bf16[8,80,256]{2,1,0:T(8,128)(2,1)S(1)}, u32[]{:S(2)}, u32[]{:S(2)}) async-start(bf16[8,80,256]{2,1,0:T(8,128)(2,1)} %pack.1), calls=%async_computation | async-start | bytes 655360 | tf_op jit(solution)/shard_map/all_to_all | solution.py:185
  7.1 10.6 %collective-permute-start.1 = (bf16[64,512]{1,0:T(8,128)(2,1)S(1)}, bf16[64,512]{1,0:T(8,128)(2,1)S(1)}, u32[]{:S(2)}, u32[]{:S(2)}) collective-permute-start(bf16[64,512]{1,0:T(8,128)(2,1)S(1)} %copy-done.3), channel_id=1, source_target_pairs={{0,8},{1,9},{2,10},{3,11},{4,12},{5,13},{6,14},{7,15},{8,0},{9,1},... | collective-permute-start | bytes 196616 | tf_op jit(solution)/shard_map/ppermute | solution.py:162
  9.8 5.5 %copy-start.2 = (s32[6]{0:T(128)S(1)}, s32[6]{0:T(128)}, u32[]{:S(2)}) copy-start(s32[6]{0:T(128)} %owners.3) | copy-start | bytes 76
  16.0 11.9 %collective-permute-start = (bf16[5,80,256]{2,1,0:T(8,128)(2,1)S(1)}, bf16[5,80,256]{2,1,0:T(8,128)(2,1)S(1)}, u32[]{:S(2)}, u32[]{:S(2)}) collective-permute-start(bf16[5,80,256]{2,1,0:T(8,128)(2,1)S(1)} %pick.1), channel_id=1, source_target_pairs={{0,8},{1,9},{2,10},{3,11},{4,12},{5,13},{6,14},{7,15},{8,0},{9,1},... | collective-permute-start | bytes 614408 | tf_op jit(solution)/shard_map/ppermute | solution.py:162
  17.8 4.3 %collective-permute-start.2 = (bf16[64,512]{1,0:T(8,128)(2,1)S(1)}, bf16[64,512]{1,0:T(8,128)(2,1)S(1)}, u32[]{:S(2)}, u32[]{:S(2)}) collective-permute-start(bf16[64,512]{1,0:T(8,128)(2,1)S(1)} %get-tuple-element.39), channel_id=1, source_target_pairs={{0,16},{16,0},{1,17},{17,1},{2,18},{18,2},{3,19},{19,3},{4,20},{20... | collective-permute-start | bytes 196616 | tf_op jit(solution)/shard_map/ppermute | solution.py:165
  27.9 6.2 %collective-permute-start.11 = (bf16[1,64,512]{2,1,0:T(8,128)(2,1)S(1)}, bf16[1,64,512]{2,1,0:T(8,128)(2,1)S(1)}, u32[]{:S(2)}, u32[]{:S(2)}) collective-permute-start(bf16[1,64,512]{2,1,0:T(8,128)(2,1)S(1)} %bitcast.5), channel_id=1, source_target_pairs={{0,2},{1,3},{2,0},{3,1},{4,6},{5,7},{6,4},{7,5},{8,10},{9,11},{10,... | collective-permute-start | bytes 196616 | tf_op jit(solution)/shard_map/ppermute | solution.py:162
  29.2 5.1 %collective-permute-start.12 = (bf16[1,64,512]{2,1,0:T(8,128)(2,1)S(1)}, bf16[1,64,512]{2,1,0:T(8,128)(2,1)S(1)}, u32[]{:S(2)}, u32[]{:S(2)}) collective-permute-start(bf16[1,64,512]{2,1,0:T(8,128)(2,1)S(1)} %bitcast.9), channel_id=1, source_target_pairs={{0,4},{1,5},{2,6},{3,7},{4,0},{5,1},{6,2},{7,3},{8,12},{9,13},{10,... | collective-permute-start | bytes 196616 | tf_op jit(solution)/shard_map/ppermute | solution.py:162
  29.8 5.9 %collective-permute-start.9 = (bf16[1,2,80,256]{3,2,1,0:T(8,128)(2,1)S(1)}, bf16[1,2,80,256]{3,2,1,0:T(8,128)(2,1)S(1)}, u32[]{:S(2)}, u32[]{:S(2)}) collective-permute-start(bf16[1,2,80,256]{3,2,1,0:T(8,128)(2,1)S(1)} %get-tuple-element.27), channel_id=1, source_target_pairs={{0,4},{1,5},{2,6},{3,7},{4,0},{5,1},{6,2},{7,3},{8,12},{9,13},{10,... | collective-permute-start | bytes 245768 | tf_op jit(solution)/shard_map/ppermute | solution.py:162
  31.9 5.2 %collective-permute-start.6 = (bf16[1,2,80,256]{3,2,1,0:T(8,128)(2,1)S(1)}, bf16[1,2,80,256]{3,2,1,0:T(8,128)(2,1)S(1)}, u32[]{:S(2)}, u32[]{:S(2)}) collective-permute-start(bf16[1,2,80,256]{3,2,1,0:T(8,128)(2,1)S(1)} %get-tuple-element.26), channel_id=1, source_target_pairs={{0,2},{1,3},{2,0},{3,1},{4,6},{5,7},{6,4},{7,5},{8,10},{9,11},{10,... | collective-permute-start | bytes 245768 | tf_op jit(solution)/shard_map/ppermute | solution.py:162
  32.6 6.0 %collective-permute-start.3 = (bf16[1,2,80,256]{3,2,1,0:T(8,128)(2,1)S(1)}, bf16[1,2,80,256]{3,2,1,0:T(8,128)(2,1)S(1)}, u32[]{:S(2)}, u32[]{:S(2)}) collective-permute-start(bf16[1,2,80,256]{3,2,1,0:T(8,128)(2,1)S(1)} %get-tuple-element.25), channel_id=1, source_target_pairs={{0,16},{16,0},{1,17},{17,1},{2,18},{18,2},{3,19},{19,3},{4,20},{20... | collective-permute-start | bytes 245768 | tf_op jit(solution)/shard_map/ppermute | solution.py:165
  34.2 5.0 %collective-permute-start.13 = (bf16[2,64,512]{2,1,0:T(8,128)(2,1)S(1)}, bf16[2,64,512]{2,1,0:T(8,128)(2,1)S(1)}, u32[]{:S(2)}, u32[]{:S(2)}) collective-permute-start(bf16[2,64,512]{2,1,0:T(8,128)(2,1)S(1)} %pad_maximum_fusion.5), channel_id=1, source_target_pairs={{0,4},{1,5},{2,6},{3,7},{4,0},{5,1},{6,2},{7,3},{8,12},{9,13},{10,... | collective-permute-start | bytes 393224 | tf_op jit(solution)/shard_map/ppermute | solution.py:162
  34.3 6.2 %collective-permute-start.14 = (bf16[2,64,512]{2,1,0:T(8,128)(2,1)S(1)}, bf16[2,64,512]{2,1,0:T(8,128)(2,1)S(1)}, u32[]{:S(2)}, u32[]{:S(2)}) collective-permute-start(bf16[2,64,512]{2,1,0:T(8,128)(2,1)S(1)} %pad_maximum_fusion.6), channel_id=1, source_target_pairs={{0,2},{1,3},{2,0},{3,1},{4,6},{5,7},{6,4},{7,5},{8,10},{9,11},{10,... | collective-permute-start | bytes 393224 | tf_op jit(solution)/shard_map/ppermute | solution.py:162
  35.7 10.8 %collective-permute-start.15 = (bf16[4,64,512]{2,1,0:T(8,128)(2,1)S(1)}, bf16[4,64,512]{2,1,0:T(8,128)(2,1)S(1)}, u32[]{:S(2)}, u32[]{:S(2)}) collective-permute-start(bf16[4,64,512]{2,1,0:T(8,128)(2,1)S(1)} %pad_maximum_fusion.1.refs_0_), channel_id=1, source_target_pairs={{0,1},{1,0},{2,3},{3,2},{4,5},{5,4},{6,7},{7,6},{8,9},{9,8},{10,11... | collective-permute-start | bytes 786440 | tf_op jit(solution)/shard_map/ppermute | solution.py:162
  37.0 9.4 %collective-permute-start.10 = (bf16[2,2,80,256]{3,2,1,0:T(8,128)(2,1)S(1)}, bf16[2,2,80,256]{3,2,1,0:T(8,128)(2,1)S(1)}, u32[]{:S(2)}, u32[]{:S(2)}) collective-permute-start(bf16[2,2,80,256]{3,2,1,0:T(8,128)(2,1)S(1)} %pad_maximum_fusion.4), channel_id=1, source_target_pairs={{0,16},{16,0},{1,17},{17,1},{2,18},{18,2},{3,19},{19,3},{4,20},{20... | collective-permute-start | bytes 491528 | tf_op jit(solution)/shard_map/ppermute | solution.py:165
  38.7 5.4 %collective-permute-start.7 = (bf16[2,2,80,256]{3,2,1,0:T(8,128)(2,1)S(1)}, bf16[2,2,80,256]{3,2,1,0:T(8,128)(2,1)S(1)}, u32[]{:S(2)}, u32[]{:S(2)}) collective-permute-start(bf16[2,2,80,256]{3,2,1,0:T(8,128)(2,1)S(1)} %pad_maximum_fusion.3), channel_id=1, source_target_pairs={{0,4},{1,5},{2,6},{3,7},{4,0},{5,1},{6,2},{7,3},{8,12},{9,13},{10,... | collective-permute-start | bytes 491528 | tf_op jit(solution)/shard_map/ppermute | solution.py:162
  38.8 7.7 %copy-start = (bf16[4096,128]{1,0:T(8,128)(2,1)S(1)}, bf16[4096,128]{1,0:T(8,128)(2,1)}, u32[]{:S(2)}) copy-start(bf16[4096,128]{1,0:T(8,128)(2,1)} %sub.6) | copy-start | bytes 3145732
  39.2 5.8 %collective-permute-start.4 = (bf16[2,2,80,256]{3,2,1,0:T(8,128)(2,1)S(1)}, bf16[2,2,80,256]{3,2,1,0:T(8,128)(2,1)S(1)}, u32[]{:S(2)}, u32[]{:S(2)}) collective-permute-start(bf16[2,2,80,256]{3,2,1,0:T(8,128)(2,1)S(1)} %pad_maximum_fusion.2), channel_id=1, source_target_pairs={{0,2},{1,3},{2,0},{3,1},{4,6},{5,7},{6,4},{7,5},{8,10},{9,11},{10,... | collective-permute-start | bytes 491528 | tf_op jit(solution)/shard_map/ppermute | solution.py:162
  40.5 6.0 %collective-permute-start.16 = (bf16[4,64,512]{2,1,0:T(8,128)(2,1)S(1)}, bf16[4,64,512]{2,1,0:T(8,128)(2,1)S(1)}, u32[]{:S(2)}, u32[]{:S(2)}) collective-permute-start(bf16[4,64,512]{2,1,0:T(8,128)(2,1)S(1)} %constant_dynamic-update-slice_fusion.6.refs_1_), channel_id=1, source_target_pairs={{0,1},{1,0},{2,3},{3,2},{4,5},{5,4},{6,7},{7,6},{8,9},{9,8},{10,11... | collective-permute-start | bytes 786440 | tf_op jit(solution)/shard_map/ppermute | solution.py:162
  44.1 19.7 %collective-permute-start.8 = (bf16[4,2,80,256]{3,2,1,0:T(8,128)(2,1)S(1)}, bf16[4,2,80,256]{3,2,1,0:T(8,128)(2,1)S(1)}, u32[]{:S(2)}, u32[]{:S(2)}) collective-permute-start(bf16[4,2,80,256]{3,2,1,0:T(8,128)(2,1)S(1)} %constant_dynamic-update-slice_fusion.3.refs_0_), channel_id=1, source_target_pairs={{0,16},{16,0},{1,17},{17,1},{2,18},{18,2},{3,19},{19,3},{4,20},{20... | collective-permute-start | bytes 983048 | tf_op jit(solution)/shard_map/ppermute | solution.py:165
  45.0 18.7 %collective-permute-start.5 = (bf16[4,2,80,256]{3,2,1,0:T(8,128)(2,1)S(1)}, bf16[4,2,80,256]{3,2,1,0:T(8,128)(2,1)S(1)}, u32[]{:S(2)}, u32[]{:S(2)}) collective-permute-start(bf16[4,2,80,256]{3,2,1,0:T(8,128)(2,1)S(1)} %constant_dynamic-update-slice_fusion.refs_0_), channel_id=1, source_target_pairs={{0,4},{1,5},{2,6},{3,7},{4,0},{5,1},{6,2},{7,3},{8,12},{9,13},{10,... | collective-permute-start | bytes 983048 | tf_op jit(solution)/shard_map/ppermute | solution.py:162
  47.0 16.8 %collective-permute-start.17 = (bf16[4,2,80,256]{3,2,1,0:T(8,128)(2,1)S(1)}, bf16[4,2,80,256]{3,2,1,0:T(8,128)(2,1)S(1)}, u32[]{:S(2)}, u32[]{:S(2)}) collective-permute-start(bf16[4,2,80,256]{3,2,1,0:T(8,128)(2,1)S(1)} %pad_maximum_fusion.refs_4_), channel_id=1, source_target_pairs={{0,2},{1,3},{2,0},{3,1},{4,6},{5,7},{6,4},{7,5},{8,10},{9,11},{10,... | collective-permute-start | bytes 983048 | tf_op jit(solution)/shard_map/ppermute | solution.py:162
  47.8 17.1 %collective-permute-start.19 = (bf16[4,2,80,256]{3,2,1,0:T(8,128)(2,1)S(1)}, bf16[4,2,80,256]{3,2,1,0:T(8,128)(2,1)S(1)}, u32[]{:S(2)}, u32[]{:S(2)}) collective-permute-start(bf16[4,2,80,256]{3,2,1,0:T(8,128)(2,1)S(1)} %constant_dynamic-update-slice_fusion.refs_0_), channel_id=1, source_target_pairs={{0,1},{1,0},{2,3},{3,2},{4,5},{5,4},{6,7},{7,6},{8,9},{9,8},{10,11... | collective-permute-start | bytes 983048 | tf_op jit(solution)/shard_map/ppermute | solution.py:162
  47.8 4.7 %collective-permute-start.18 = (f32[64,128]{1,0:T(8,128)S(1)}, f32[64,128]{1,0:T(8,128)S(1)}, u32[]{:S(2)}, u32[]{:S(2)}) collective-permute-start(f32[64,128]{1,0:T(8,128)S(1)} %get-tuple-element.34), channel_id=1, source_target_pairs={{0,16},{16,0},{1,17},{17,1},{2,18},{18,2},{3,19},{19,3},{4,20},{20... | collective-permute-start | bytes 98312 | tf_op jit(solution)/shard_map/ppermute | solution.py:165
  52.5 13.0 %copy-start.1 = (s32[6]{0:T(128)S(1)}, s32[6]{0:T(128)}, u32[]{:S(2)}) copy-start(s32[6]{0:T(128)} %offsets.3) | copy-start | bytes 76
  63.8 1.7 %collective-permute-start.20 = (bf16[4,2,80,256]{3,2,1,0:T(8,128)(2,1)S(1)}, bf16[4,2,80,256]{3,2,1,0:T(8,128)(2,1)S(1)}, u32[]{:S(2)}, u32[]{:S(2)}) collective-permute-start(bf16[4,2,80,256]{3,2,1,0:T(8,128)(2,1)S(1)} %collective-permute-done.5.refs_1_), channel_id=1, source_target_pairs={{0,1},{1,0},{2,3},{3,2},{4,5},{5,4},{6,7},{7,6},{8,9},{9,8},{10,11... | collective-permute-start | bytes 983048 | tf_op jit(solution)/shard_map/ppermute | solution.py:162
  63.8 3.5 %collective-permute-start.21 = (bf16[4,2,80,256]{3,2,1,0:T(8,128)(2,1)S(1)}, bf16[4,2,80,256]{3,2,1,0:T(8,128)(2,1)S(1)}, u32[]{:S(2)}, u32[]{:S(2)}) collective-permute-start(bf16[4,2,80,256]{3,2,1,0:T(8,128)(2,1)S(1)} %constant_dynamic-update-slice_fusion.3.refs_0_), channel_id=1, source_target_pairs={{0,1},{1,0},{2,3},{3,2},{4,5},{5,4},{6,7},{7,6},{8,9},{9,8},{10,11... | collective-permute-start | bytes 983048 | tf_op jit(solution)/shard_map/ppermute | solution.py:162
  64.3 3.0 %collective-permute-start.23 = (bf16[4,2,80,256]{3,2,1,0:T(8,128)(2,1)S(1)}, bf16[4,2,80,256]{3,2,1,0:T(8,128)(2,1)S(1)}, u32[]{:S(2)}, u32[]{:S(2)}) collective-permute-start(bf16[4,2,80,256]{3,2,1,0:T(8,128)(2,1)S(1)} %pad_maximum_fusion.refs_4_), channel_id=1, source_target_pairs={{0,1},{1,0},{2,3},{3,2},{4,5},{5,4},{6,7},{7,6},{8,9},{9,8},{10,11... | collective-permute-start | bytes 983048 | tf_op jit(solution)/shard_map/ppermute | solution.py:162
  64.4 3.0 %collective-permute-start.22 = (bf16[4,2,80,256]{3,2,1,0:T(8,128)(2,1)S(1)}, bf16[4,2,80,256]{3,2,1,0:T(8,128)(2,1)S(1)}, u32[]{:S(2)}, u32[]{:S(2)}) collective-permute-start(bf16[4,2,80,256]{3,2,1,0:T(8,128)(2,1)S(1)} %collective-permute-done.8.refs_1_), channel_id=1, source_target_pairs={{0,1},{1,0},{2,3},{3,2},{4,5},{5,4},{6,7},{7,6},{8,9},{9,8},{10,11... | collective-permute-start | bytes 983048 | tf_op jit(solution)/shard_map/ppermute | solution.py:162
  64.8 2.5 %collective-permute-start.24 = (bf16[4,2,80,256]{3,2,1,0:T(8,128)(2,1)S(1)}, bf16[4,2,80,256]{3,2,1,0:T(8,128)(2,1)S(1)}, u32[]{:S(2)}, u32[]{:S(2)}) collective-permute-start(bf16[4,2,80,256]{3,2,1,0:T(8,128)(2,1)S(1)} %collective-permute-done.17.refs_5_), channel_id=1, source_target_pairs={{0,1},{1,0},{2,3},{3,2},{4,5},{5,4},{6,7},{7,6},{8,9},{9,8},{10,11... | collective-permute-start | bytes 983048 | tf_op jit(solution)/shard_map/ppermute | solution.py:162

commit v19 on v17

--- a/solution.py
+++ b/solution.py
@@ -60,24 +60,21 @@
     mine = lax.axis_index("col") // HALF
     for group in range(GROUPS):
         half, rank = places(owners, group)
-        rank = jnp.minimum(rank, out.shape[0] - 1)
+        rank = jnp.minimum(rank, out.shape[1] - 1)
 
         @pl.when(half == mine)
         def _():
-            out[rank] = held[lax.rem(owners[group], HALF)]
-
-
-def order_kernel(owners, held, *refs):
-    others, outs = refs[:-COLOURS], refs[-COLOURS:]
-    mine = lax.axis_index("col") // HALF
+            piece = held[lax.rem(owners[group], HALF)]
+            for to in range(out.shape[0]):
+                out[to, rank] = piece
+
+
+def order_kernel(owners, held, *outs):
     each = GROUPS // COLOURS
     for group in range(GROUPS):
         half, rank = places(owners, group)
-        piece = held[lax.rem(owners[group], HALF)]
-        for mask, ref in enumerate(others, 1):
-            other = ref[jnp.minimum(rank, ref.shape[0] - 1)]
-            piece = jnp.where(jnp.bitwise_xor(half, mine) == mask, other, piece)
-        outs[group // each][0, group % each] = piece
+        rank = jnp.minimum(rank, held.shape[1] - 1)
+        outs[group // each][0, group % each] = held[half, rank]
 
 
 def merge_kernel(rows, cols, tags, sub, *refs):
@@ -184,14 +181,15 @@
 
     picked = pl.pallas_call(
         pick_kernel,
-        out_shape=jax.ShapeDtypeStruct((GROUPS - 1,) + piece, dtype),
+        out_shape=jax.ShapeDtypeStruct((halves, GROUPS - 1) + piece, dtype),
         in_specs=[SMEM, VMEM],
         out_specs=VMEM,
         compiler_params=limit(4),
         cost_estimate=cost([slices]),
         name="pick",
     )(owners, slices)
-    others = [over_col(picked, m * HALF) for m in range(1, halves)]
+    members = [[h * HALF + c for h in range(halves)] for c in range(HALF)]
+    gathered = lax.all_to_all(picked, "col", 0, 0, axis_index_groups=members)
 
     across = [merge_factor] + [over_col(merge_factor, m * share) for m in range(1, rows)]
 
@@ -205,7 +203,6 @@
         return block
 
     blocks = [for_row(0)] + [over_row(for_row(m), m) for m in range(1, rows)]
-    others, blocks = lax.optimization_barrier((others, blocks))
     groups = [range(rows // 2), range(rows // 2, rows)]
     sides = [jnp.stack([blocks[m] for m in group]) for group in groups]
     tags = [[(m, 0) for m in group] for group in groups]
@@ -242,12 +239,12 @@
     colours = pl.pallas_call(
         order_kernel,
         out_shape=[jax.ShapeDtypeStruct((1, per) + piece, dtype)] * COLOURS,
-        in_specs=[SMEM, VMEM] + [VMEM] * len(others),
+        in_specs=[SMEM, VMEM],
         out_specs=[VMEM] * COLOURS,
         compiler_params=limit(4),
         cost_estimate=cost([slices]),
         name="order",
-    )(owners, slices, *others)
+    )(owners, gathered)
     colours = list(colours)
     links = [
         (HALF, lambda v: over_row(v, 1)),
@@ -261,13 +258,13 @@
             colours[k] = jnp.concatenate([colours[k], send(colours[k])])
             masks[k] = masks[k] + [m ^ mask for m in masks[k]]
     state = lax.all_to_all(merged.reshape(rows * cols, each, width), ("row", "col"), 0, 0)
+    colours, state = lax.optimization_barrier((colours, state))
     last_round = []
     for k in range(COLOURS):
         mask, send = links[(k + 2) % 3]
         last_round.append(send(colours[k]))
         masks[k] = [masks[k], [m ^ mask for m in masks[k]]]
         masks[k] += [[m ^ 1 for m in ms] for ms in masks[k]]
-    last_round, state = lax.optimization_barrier((last_round, state))
     held = []
     for k in range(COLOURS):
         held.append([colours[k], last_round[k], over_col(colours[k], 1), over_col(last_round[k], 1)])

time: 68.3 us -> 75.1 us (1.100)
  starting transfers between devices: 30.4 us -> 35.9 us
  Pallas kernels: 9.78 us -> 10.6 us
    all_to_all x0 -> x1, waiting for transfers between devices: none -> 12.3 us  [local(): gathered = lax.all_to_all(picked, 'col', 0, 0, axis_index_groups=members)]
    all_to_all x1, waiting for transfers between devices: 5.48 us -> 0.01 us  [local(): slices = lax.all_to_all(packed, 'col', 0, 0, axis_index_groups=members)]
    all_to_all x1, waiting for transfers between devices: 5.03 us -> 0.01 us  [local(): lax.all_to_all(merged.reshape(rows * cols, each, width), ('row', 'col'),...]
    all_to_all x0 -> x1, starting transfers between devices: none -> 3.6 us  [local(): gathered = lax.all_to_all(picked, 'col', 0, 0, axis_index_groups=members)]
    ppermute x20 -> x19, starting transfers between devices: 17.1 us -> 19.8 us  [over_col(): return lax.ppermute(x, 'col', [(c, c ^ mask) for c in range(cols)])]
    ppermute x4, starting transfers between devices: 4.06 us -> 6.18 us  [over_row(): return lax.ppermute(x, 'row', [(r, r ^ mask) for r in range(rows)])]
    all_to_all x1, starting transfers between devices: 5.4 us -> 3.81 us  [local(): slices = lax.all_to_all(packed, 'col', 0, 0, axis_index_groups=members)]
    all_to_all x1, starting transfers between devices: 3.89 us -> 2.55 us  [local(): lax.all_to_all(merged.reshape(rows * cols, each, width), ('row', 'col'),...]
  transfers between devices with their start and end apart: 26 -> 26, of which waited for: 12 -> 10; matrix products, arithmetic and copies ran while one was open for 0% -> 0% of each run, Pallas kernels for 5% -> 7%
where the time goes in v19:
time: 75.1 us; the launch traced here: 74.7 us
  starting transfers between devices  35.9 us (48%)
  waiting for transfers between devices  27.6 us (37%)
  Pallas kernels  10.6 us (14%)
    ppermute x19, starting transfers between devices, over_col(): return lax.ppermute(x, 'col', [(c, c ^ mask) for c in range(cols)])  19.8 us
    all_to_all x1, waiting for transfers between devices, local(): gathered = lax.all_to_all(picked, 'col', 0, 0, axis_index_groups=members)  12.3 us
    ppermute x19, waiting for transfers between devices, over_col(): return lax.ppermute(x, 'col', [(c, c ^ mask) for c in range(cols)])  9.57 us
    ppermute x4, starting transfers between devices, over_row(): return lax.ppermute(x, 'row', [(r, r ^ mask) for r in range(rows)])  6.18 us
    ppermute x4, waiting for transfers between devices, over_row(): return lax.ppermute(x, 'row', [(r, r ^ mask) for r in range(rows)])  5.73 us
    pallas_call x2, Pallas kernels, local(): pl.pallas_call(functools.partial(chain_kernel, cols, groups, slots, sum((...  5.68 us
    all_to_all x1, starting transfers between devices, local(): slices = lax.all_to_all(packed, 'col', 0, 0, axis_index_groups=members)  3.81 us
    all_to_all x1, starting transfers between devices, local(): gathered = lax.all_to_all(picked, 'col', 0, 0, axis_index_groups=members)  3.6 us
  transfers between devices with their start and end apart: 26, of which 10 were waited for; matrix products, arithmetic and copies ran while one was open for 0% of the time, Pallas kernels for 7%

profile of v19, /device:TPU:0, one launch (start us, length us, event | category | flops | bytes accessed | tf_op | source)
XLA Modules:
  0.0 74.7 jit_solution(8162488984848544142)
XLA Ops:
  0.0 1.7 %pack.1 = bf16[8,80,256]{2,1,0:T(8,128)(2,1)} custom-call(bf16[16,64,256]{2,1,0:T(8,128)(2,1)} %bitcast.6, bf16[16,16,256]{2,1,0:T(8,128)(2,1)} %bitcast.10), custom_call_target="tpu_custom_call" | custom-call | bytes 655360 | tf_op jit(solution)/shard_map/pack/pallas_call | solution.py:168
  1.8 4.1 %collective-permute-start.6 = (bf16[64,512]{1,0:T(8,128)(2,1)S(1)}, bf16[64,512]{1,0:T(8,128)(2,1)S(1)}, u32[]{:S(2)}, u32[]{:S(2)}) collective-permute-start(bf16[64,512]{1,0:T(8,128)(2,1)S(1)} %copy-done.3), channel_id=1, source_target_pairs={{0,8},{1,9},{2,10},{3,11},{4,12},{5,13},{6,14},{7,15},{8,0},{9,1},... | collective-permute-start | bytes 196616 | tf_op jit(solution)/shard_map/ppermute | solution.py:157
  5.9 3.8 %all-to-all-start = ((bf16[8,80,256]{2,1,0:T(8,128)(2,1)}), bf16[8,80,256]{2,1,0:T(8,128)(2,1)S(1)}, u32[]{:S(2)}, u32[]{:S(2)}) async-start(bf16[8,80,256]{2,1,0:T(8,128)(2,1)} %pack.1), calls=%async_computation | async-start | bytes 655360 | tf_op jit(solution)/shard_map/all_to_all | solution.py:180
  9.7 0.0 collective-permute-done.6
  9.7 1.6 %collective-permute-start.8 = (bf16[64,512]{1,0:T(8,128)(2,1)S(1)}, bf16[64,512]{1,0:T(8,128)(2,1)S(1)}, u32[]{:S(2)}, u32[]{:S(2)}) collective-permute-start(bf16[64,512]{1,0:T(8,128)(2,1)S(1)} %get-tuple-element.24), channel_id=1, source_target_pairs={{0,16},{16,0},{1,17},{17,1},{2,18},{18,2},{3,19},{19,3},{4,20},{20... | collective-permute-start | bytes 196616 | tf_op jit(solution)/shard_map/ppermute | solution.py:160
  11.3 2.0 %collective-permute-start.7 = (bf16[1,64,512]{2,1,0:T(8,128)(2,1)S(1)}, bf16[1,64,512]{2,1,0:T(8,128)(2,1)S(1)}, u32[]{:S(2)}, u32[]{:S(2)}) collective-permute-start(bf16[1,64,512]{2,1,0:T(8,128)(2,1)S(1)} %get-tuple-element.23), channel_id=1, source_target_pairs={{0,2},{1,3},{2,0},{3,1},{4,6},{5,7},{6,4},{7,5},{8,10},{9,11},{10,... | collective-permute-start | bytes 196616 | tf_op jit(solution)/shard_map/ppermute | solution.py:157
  13.3 1.0 %collective-permute-done.8 = bf16[64,512]{1,0:T(8,128)(2,1)S(1)} collective-permute-done((bf16[64,512]{1,0:T(8,128)(2,1)S(1)}, bf16[64,512]{1,0:T(8,128)(2,1)S(1)}, u32[]{:S(2)}, u32[]{:S(2)}) %collective-permute-start.8) | collective-permute-done | bytes 65568 | tf_op jit(solution)/shard_map/ppermute | solution.py:160
  14.3 1.8 %collective-permute-start.9 = (bf16[1,64,512]{2,1,0:T(8,128)(2,1)S(1)}, bf16[1,64,512]{2,1,0:T(8,128)(2,1)S(1)}, u32[]{:S(2)}, u32[]{:S(2)}) collective-permute-start(bf16[1,64,512]{2,1,0:T(8,128)(2,1)S(1)} %bitcast.7), channel_id=1, source_target_pairs={{0,4},{1,5},{2,6},{3,7},{4,0},{5,1},{6,2},{7,3},{8,12},{9,13},{10,... | collective-permute-start | bytes 196616 | tf_op jit(solution)/shard_map/ppermute | solution.py:157
  16.0 1.8 %collective-permute-done.7 = bf16[1,64,512]{2,1,0:T(8,128)(2,1)S(1)} collective-permute-done((bf16[1,64,512]{2,1,0:T(8,128)(2,1)S(1)}, bf16[1,64,512]{2,1,0:T(8,128)(2,1)S(1)}, u32[]{:S(2)}, u32[]{:S(2)}) %collective-permute-start.7) | collective-permute-done | bytes 65568 | tf_op jit(solution)/shard_map/ppermute | solution.py:157
  17.8 1.5 %collective-permute-start.10 = (bf16[2,64,512]{2,1,0:T(8,128)(2,1)S(1)}, bf16[2,64,512]{2,1,0:T(8,128)(2,1)S(1)}, u32[]{:S(2)}, u32[]{:S(2)}) collective-permute-start(bf16[2,64,512]{2,1,0:T(8,128)(2,1)S(1)} %pad_maximum_fusion.7), channel_id=1, source_target_pairs={{0,4},{1,5},{2,6},{3,7},{4,0},{5,1},{6,2},{7,3},{8,12},{9,13},{10,... | collective-permute-start | bytes 393224 | tf_op jit(solution)/shard_map/ppermute | solution.py:157
  19.4 0.0 collective-permute-done.9
  19.4 0.0 copy-start.1
  19.4 1.0 %collective-permute-start.11 = (bf16[2,64,512]{2,1,0:T(8,128)(2,1)S(1)}, bf16[2,64,512]{2,1,0:T(8,128)(2,1)S(1)}, u32[]{:S(2)}, u32[]{:S(2)}) collective-permute-start(bf16[2,64,512]{2,1,0:T(8,128)(2,1)S(1)} %pad_maximum_fusion.8), channel_id=1, source_target_pairs={{0,2},{1,3},{2,0},{3,1},{4,6},{5,7},{6,4},{7,5},{8,10},{9,11},{10,... | collective-permute-start | bytes 393224 | tf_op jit(solution)/shard_map/ppermute | solution.py:157
  20.4 0.1 collective-permute-start.12
  20.5 0.0 all-to-all-done.held
  20.5 1.5 %pick.1 = bf16[2,5,80,256]{3,2,1,0:T(8,128)(2,1)} custom-call(s32[6]{0:T(128)S(1)} %copy-done.1, bf16[8,80,256]{2,1,0:T(8,128)(2,1)S(1)} %all-to-all-done.held), custom_call_target="tpu_custom_call" | custom-call | bytes 327680 | tf_op jit(solution)/shard_map/pick/pallas_call | solution.py:182
  22.0 3.6 %all-to-all-start.1 = ((bf16[2,5,80,256]{3,2,1,0:T(8,128)(2,1)}), bf16[2,5,80,256]{3,2,1,0:T(8,128)(2,1)S(1)}, u32[]{:S(2)}, u32[]{:S(2)}) async-start(bf16[2,5,80,256]{3,2,1,0:T(8,128)(2,1)} %pick.1), calls=%async_computation.1 | async-start | bytes 819200 | tf_op jit(solution)/shard_map/all_to_all | solution.py:192
  25.6 0.0 collective-permute-done.10
  25.7 0.0 collective-permute-done.11
  25.7 0.5 collective-permute-start.13
  26.2 12.3 %all-to-all-done.1.held = bf16[2,5,80,256]{3,2,1,0:T(8,128)(2,1)S(1)} async-done(((bf16[2,5,80,256]{3,2,1,0:T(8,128)(2,1)}), bf16[2,5,80,256]{3,2,1,0:T(8,128)(2,1)S(1)}, u32[]{:S(2)}, u32[]{:S(2)}) %all-to-all-start.1) | async-done | bytes 409632 | tf_op jit(solution)/shard_map/all_to_all | solution.py:192
  38.6 0.6 order.1
  39.2 1.6 %collective-permute-start = (bf16[1,2,80,256]{3,2,1,0:T(8,128)(2,1)S(1)}, bf16[1,2,80,256]{3,2,1,0:T(8,128)(2,1)S(1)}, u32[]{:S(2)}, u32[]{:S(2)}) collective-permute-start(bf16[1,2,80,256]{3,2,1,0:T(8,128)(2,1)S(1)} %get-tuple-element.15), channel_id=1, source_target_pairs={{0,16},{16,0},{1,17},{17,1},{2,18},{18,2},{3,19},{19,3},{4,20},{20... | collective-permute-start | bytes 245768 | tf_op jit(solution)/shard_map/ppermute | solution.py:160
  40.7 0.0 collective-permute-done.12.refs_2_
  40.7 0.0 collective-permute-done.13.refs_3_
  40.7 1.1 %merge.1 = f32[128,128]{1,0:T(8,128)} custom-call(bf16[4096,128]{1,0:T(8,128)(2,1)S(1)} %copy-done, bf16[4,64,512]{2,1,0:T(8,128)(2,1)S(1)} %pad_maximum_fusion.3.refs_0_, bf16[4,64,512]{2,1,0:T(8,128)(2,1)S(1)} %constant_dynamic-update-slice_fusion.refs_1_, bf16[4,64,512]{2,1,0:T(8,128)(2,1)S(1)} %collective-permute-done.12.refs_2_, ...), custom_call_target="tpu_custom_call" | custom-call | flops 134217728 | bytes 1048576 | tf_op jit(solution)/shard_map/merge/pallas_call | solution.py:229
  41.8 2.5 %all-to-all-start.2 = ((f32[32,4,128]{2,1,0:T(4,128)}), f32[32,4,128]{2,1,0:T(4,128)S(1)}, u32[]{:S(2)}, u32[]{:S(2)}) async-start(f32[32,4,128]{2,1,0:T(4,128)} %bitcast.4), calls=%async_computation.2 | async-start | bytes 131072 | tf_op jit(solution)/shard_map/all_to_all | solution.py:260
  44.4 1.7 %collective-permute-start.2 = (bf16[1,2,80,256]{3,2,1,0:T(8,128)(2,1)S(1)}, bf16[1,2,80,256]{3,2,1,0:T(8,128)(2,1)S(1)}, u32[]{:S(2)}, u32[]{:S(2)}) collective-permute-start(bf16[1,2,80,256]{3,2,1,0:T(8,128)(2,1)S(1)} %get-tuple-element.16), channel_id=1, source_target_pairs={{0,2},{1,3},{2,0},{3,1},{4,6},{5,7},{6,4},{7,5},{8,10},{9,11},{10,... | collective-permute-start | bytes 245768 | tf_op jit(solution)/shard_map/ppermute | solution.py:157
  46.1 1.5 %collective-permute-start.4 = (bf16[1,2,80,256]{3,2,1,0:T(8,128)(2,1)S(1)}, bf16[1,2,80,256]{3,2,1,0:T(8,128)(2,1)S(1)}, u32[]{:S(2)}, u32[]{:S(2)}) collective-permute-start(bf16[1,2,80,256]{3,2,1,0:T(8,128)(2,1)S(1)} %get-tuple-element.17), channel_id=1, source_target_pairs={{0,4},{1,5},{2,6},{3,7},{4,0},{5,1},{6,2},{7,3},{8,12},{9,13},{10,... | collective-permute-start | bytes 245768 | tf_op jit(solution)/shard_map/ppermute | solution.py:157
  47.7 0.6 collective-permute-start.1
  48.3 0.9 %collective-permute-done.2 = bf16[1,2,80,256]{3,2,1,0:T(8,128)(2,1)S(1)} collective-permute-done((bf16[1,2,80,256]{3,2,1,0:T(8,128)(2,1)S(1)}, bf16[1,2,80,256]{3,2,1,0:T(8,128)(2,1)S(1)}, u32[]{:S(2)}, u32[]{:S(2)}) %collective-permute-start.2) | collective-permute-done | bytes 81952 | tf_op jit(solution)/shard_map/ppermute | solution.py:157
  49.2 2.6 %collective-permute-start.3 = (bf16[2,2,80,256]{3,2,1,0:T(8,128)(2,1)S(1)}, bf16[2,2,80,256]{3,2,1,0:T(8,128)(2,1)S(1)}, u32[]{:S(2)}, u32[]{:S(2)}) collective-permute-start(bf16[2,2,80,256]{3,2,1,0:T(8,128)(2,1)S(1)} %pad_maximum_fusion.5), channel_id=1, source_target_pairs={{0,4},{1,5},{2,6},{3,7},{4,0},{5,1},{6,2},{7,3},{8,12},{9,13},{10,... | collective-permute-start | bytes 491528 | tf_op jit(solution)/shard_map/ppermute | solution.py:157
  51.8 0.0 collective-permute-done.4
  51.9 1.6 %collective-permute-start.5 = (bf16[2,2,80,256]{3,2,1,0:T(8,128)(2,1)S(1)}, bf16[2,2,80,256]{3,2,1,0:T(8,128)(2,1)S(1)}, u32[]{:S(2)}, u32[]{:S(2)}) collective-permute-start(bf16[2,2,80,256]{3,2,1,0:T(8,128)(2,1)S(1)} %pad_maximum_fusion.6), channel_id=1, source_target_pairs={{0,16},{16,0},{1,17},{17,1},{2,18},{18,2},{3,19},{19,3},{4,20},{20... | collective-permute-start | bytes 491528 | tf_op jit(solution)/shard_map/ppermute | solution.py:160
  53.4 0.3 collective-permute-done.1
  53.7 1.4 %collective-permute-done.3 = bf16[2,2,80,256]{3,2,1,0:T(8,128)(2,1)S(1)} collective-permute-done((bf16[2,2,80,256]{3,2,1,0:T(8,128)(2,1)S(1)}, bf16[2,2,80,256]{3,2,1,0:T(8,128)(2,1)S(1)}, u32[]{:S(2)}, u32[]{:S(2)}) %collective-permute-start.3) | collective-permute-done | bytes 163872 | tf_op jit(solution)/shard_map/ppermute | solution.py:157
  55.2 0.0 copy-start.2
  55.2 2.1 %collective-permute-done.5 = bf16[2,2,80,256]{3,2,1,0:T(8,128)(2,1)S(1)} collective-permute-done((bf16[2,2,80,256]{3,2,1,0:T(8,128)(2,1)S(1)}, bf16[2,2,80,256]{3,2,1,0:T(8,128)(2,1)S(1)}, u32[]{:S(2)}, u32[]{:S(2)}) %collective-permute-start.5) | collective-permute-done | bytes 163872 | tf_op jit(solution)/shard_map/ppermute | solution.py:160
  57.3 0.3 collective-permute-start.14
  57.6 1.5 %collective-permute-start.17 = (bf16[4,2,80,256]{3,2,1,0:T(8,128)(2,1)S(1)}, bf16[4,2,80,256]{3,2,1,0:T(8,128)(2,1)S(1)}, u32[]{:S(2)}, u32[]{:S(2)}) collective-permute-start(bf16[4,2,80,256]{3,2,1,0:T(8,128)(2,1)S(1)} %pad_maximum_fusion.1.refs_0_), channel_id=1, source_target_pairs={{0,16},{16,0},{1,17},{17,1},{2,18},{18,2},{3,19},{19,3},{4,20},{20... | collective-permute-start | bytes 983048 | tf_op jit(solution)/shard_map/ppermute | solution.py:160
  59.1 1.5 %collective-permute-start.20 = (bf16[4,2,80,256]{3,2,1,0:T(8,128)(2,1)S(1)}, bf16[4,2,80,256]{3,2,1,0:T(8,128)(2,1)S(1)}, u32[]{:S(2)}, u32[]{:S(2)}) collective-permute-start(bf16[4,2,80,256]{3,2,1,0:T(8,128)(2,1)S(1)} %pad_maximum_fusion.2.refs_4_), channel_id=1, source_target_pairs={{0,2},{1,3},{2,0},{3,1},{4,6},{5,7},{6,4},{7,5},{8,10},{9,11},{10,... | collective-permute-start | bytes 983048 | tf_op jit(solution)/shard_map/ppermute | solution.py:157
  60.6 4.0 %collective-permute-done.14.refs_1_ = bf16[4,2,80,256]{3,2,1,0:T(8,128)(2,1)S(1)} collective-permute-done((bf16[4,2,80,256]{3,2,1,0:T(8,128)(2,1)S(1)}, bf16[4,2,80,256]{3,2,1,0:T(8,128)(2,1)S(1)}, u32[]{:S(2)}, u32[]{:S(2)}) %collective-permute-start.14) | collective-permute-done | bytes 327712 | tf_op jit(solution)/shard_map/ppermute | solution.py:157
  64.5 0.5 collective-permute-start.18
  65.0 0.0 collective-permute-start.21
  65.1 2.7 %collective-permute-done.17.refs_1_ = bf16[4,2,80,256]{3,2,1,0:T(8,128)(2,1)S(1)} collective-permute-done((bf16[4,2,80,256]{3,2,1,0:T(8,128)(2,1)S(1)}, bf16[4,2,80,256]{3,2,1,0:T(8,128)(2,1)S(1)}, u32[]{:S(2)}, u32[]{:S(2)}) %collective-permute-start.17) | collective-permute-done | bytes 327712 | tf_op jit(solution)/shard_map/ppermute | solution.py:160
  67.7 1.2 %collective-permute-done.20.refs_5_ = bf16[4,2,80,256]{3,2,1,0:T(8,128)(2,1)S(1)} collective-permute-done((bf16[4,2,80,256]{3,2,1,0:T(8,128)(2,1)S(1)}, bf16[4,2,80,256]{3,2,1,0:T(8,128)(2,1)S(1)}, u32[]{:S(2)}, u32[]{:S(2)}) %collective-permute-start.20) | collective-permute-done | bytes 327712 | tf_op jit(solution)/shard_map/ppermute | solution.py:157
  68.9 1.9 %chain0.1.start = f32[8,2048]{1,0:T(8,128)S(1)} custom-call(s32[6]{0:T(128)S(1)} %copy-done.2, f32[32,4,128]{2,1,0:T(4,128)S(1)} %all-to-all-done.2.start, bf16[4,2,80,256]{3,2,1,0:T(8,128)(2,1)S(1)} %pad_maximum_fusion.refs_0_, bf16[4,2,80,256]{3,2,1,0:T(8,128)(2,1)S(1)} %collective-permute-done.14.refs_1_, ...), custom_call_target="tpu_custom_call" | custom-call | flops 67108864 | bytes 1310720 | tf_op jit(solution)/shard_map/chain0/pallas_call | solution.py:278
  70.9 3.8 %chain1.1 = bf16[4,2048]{1,0:T(4,128)(2,1)} custom-call(s32[6]{0:T(128)S(1)} %copy-done.2, f32[8,2048]{1,0:T(8,128)S(1)} %chain0.1.start, bf16[4,2,80,256]{3,2,1,0:T(8,128)(2,1)S(1)} %pad_maximum_fusion.1.refs_0_, bf16[4,2,80,256]{3,2,1,0:T(8,128)(2,1)S(1)} %collective-permute-done.17.refs_1_, bf16[4,2,80,256]{3,2,1,0:T(8,128)(2,1)S(1)} %collective-permute-done.18.refs_2_, ...), custom_call_target="tpu_custom_call" | custom-call | flops 134217728 | bytes 2621440 | tf_op jit(solution)/shard_map/chain1/pallas_call | solution.py:278
  (30 shorter events, 0.3 us)
Async XLA Ops:
  0.0 1.7 %copy-start.3 = (bf16[64,512]{1,0:T(8,128)(2,1)S(1)}, bf16[64,512]{1,0:T(8,128)(2,1)}, u32[]{:S(2)}) copy-start(bf16[64,512]{1,0:T(8,128)(2,1)} %param.7) | copy-start | bytes 196612
  1.8 7.9 %collective-permute-start.6 = (bf16[64,512]{1,0:T(8,128)(2,1)S(1)}, bf16[64,512]{1,0:T(8,128)(2,1)S(1)}, u32[]{:S(2)}, u32[]{:S(2)}) collective-permute-start(bf16[64,512]{1,0:T(8,128)(2,1)S(1)} %copy-done.3), channel_id=1, source_target_pairs={{0,8},{1,9},{2,10},{3,11},{4,12},{5,13},{6,14},{7,15},{8,0},{9,1},... | collective-permute-start | bytes 196616 | tf_op jit(solution)/shard_map/ppermute | solution.py:157
  5.9 14.7 %all-to-all-start = ((bf16[8,80,256]{2,1,0:T(8,128)(2,1)}), bf16[8,80,256]{2,1,0:T(8,128)(2,1)S(1)}, u32[]{:S(2)}, u32[]{:S(2)}) async-start(bf16[8,80,256]{2,1,0:T(8,128)(2,1)} %pack.1), calls=%async_computation | async-start | bytes 655360 | tf_op jit(solution)/shard_map/all_to_all | solution.py:180
  9.7 4.6 %collective-permute-start.8 = (bf16[64,512]{1,0:T(8,128)(2,1)S(1)}, bf16[64,512]{1,0:T(8,128)(2,1)S(1)}, u32[]{:S(2)}, u32[]{:S(2)}) collective-permute-start(bf16[64,512]{1,0:T(8,128)(2,1)S(1)} %get-tuple-element.24), channel_id=1, source_target_pairs={{0,16},{16,0},{1,17},{17,1},{2,18},{18,2},{3,19},{19,3},{4,20},{20... | collective-permute-start | bytes 196616 | tf_op jit(solution)/shard_map/ppermute | solution.py:160
  11.3 6.5 %collective-permute-start.7 = (bf16[1,64,512]{2,1,0:T(8,128)(2,1)S(1)}, bf16[1,64,512]{2,1,0:T(8,128)(2,1)S(1)}, u32[]{:S(2)}, u32[]{:S(2)}) collective-permute-start(bf16[1,64,512]{2,1,0:T(8,128)(2,1)S(1)} %get-tuple-element.23), channel_id=1, source_target_pairs={{0,2},{1,3},{2,0},{3,1},{4,6},{5,7},{6,4},{7,5},{8,10},{9,11},{10,... | collective-permute-start | bytes 196616 | tf_op jit(solution)/shard_map/ppermute | solution.py:157
  14.3 5.1 %collective-permute-start.9 = (bf16[1,64,512]{2,1,0:T(8,128)(2,1)S(1)}, bf16[1,64,512]{2,1,0:T(8,128)(2,1)S(1)}, u32[]{:S(2)}, u32[]{:S(2)}) collective-permute-start(bf16[1,64,512]{2,1,0:T(8,128)(2,1)S(1)} %bitcast.7), channel_id=1, source_target_pairs={{0,4},{1,5},{2,6},{3,7},{4,0},{5,1},{6,2},{7,3},{8,12},{9,13},{10,... | collective-permute-start | bytes 196616 | tf_op jit(solution)/shard_map/ppermute | solution.py:157
  17.8 7.8 %collective-permute-start.10 = (bf16[2,64,512]{2,1,0:T(8,128)(2,1)S(1)}, bf16[2,64,512]{2,1,0:T(8,128)(2,1)S(1)}, u32[]{:S(2)}, u32[]{:S(2)}) collective-permute-start(bf16[2,64,512]{2,1,0:T(8,128)(2,1)S(1)} %pad_maximum_fusion.7), channel_id=1, source_target_pairs={{0,4},{1,5},{2,6},{3,7},{4,0},{5,1},{6,2},{7,3},{8,12},{9,13},{10,... | collective-permute-start | bytes 393224 | tf_op jit(solution)/shard_map/ppermute | solution.py:157
  19.4 1.2 %copy-start.1 = (s32[6]{0:T(128)S(1)}, s32[6]{0:T(128)}, u32[]{:S(2)}) copy-start(s32[6]{0:T(128)} %owners.3) | copy-start | bytes 76
  19.4 6.3 %collective-permute-start.11 = (bf16[2,64,512]{2,1,0:T(8,128)(2,1)S(1)}, bf16[2,64,512]{2,1,0:T(8,128)(2,1)S(1)}, u32[]{:S(2)}, u32[]{:S(2)}) collective-permute-start(bf16[2,64,512]{2,1,0:T(8,128)(2,1)S(1)} %pad_maximum_fusion.8), channel_id=1, source_target_pairs={{0,2},{1,3},{2,0},{3,1},{4,6},{5,7},{6,4},{7,5},{8,10},{9,11},{10,... | collective-permute-start | bytes 393224 | tf_op jit(solution)/shard_map/ppermute | solution.py:157
  20.4 20.3 %collective-permute-start.12 = (bf16[4,64,512]{2,1,0:T(8,128)(2,1)S(1)}, bf16[4,64,512]{2,1,0:T(8,128)(2,1)S(1)}, u32[]{:S(2)}, u32[]{:S(2)}) collective-permute-start(bf16[4,64,512]{2,1,0:T(8,128)(2,1)S(1)} %pad_maximum_fusion.3.refs_0_), channel_id=1, source_target_pairs={{0,1},{1,0},{2,3},{3,2},{4,5},{5,4},{6,7},{7,6},{8,9},{9,8},{10,11... | collective-permute-start | bytes 786440 | tf_op jit(solution)/shard_map/ppermute | solution.py:157
  22.0 18.7 %copy-start = (bf16[4096,128]{1,0:T(8,128)(2,1)S(1)}, bf16[4096,128]{1,0:T(8,128)(2,1)}, u32[]{:S(2)}) copy-start(bf16[4096,128]{1,0:T(8,128)(2,1)} %sub.6) | copy-start | bytes 3145732
  22.0 16.6 %all-to-all-start.1 = ((bf16[2,5,80,256]{3,2,1,0:T(8,128)(2,1)}), bf16[2,5,80,256]{3,2,1,0:T(8,128)(2,1)S(1)}, u32[]{:S(2)}, u32[]{:S(2)}) async-start(bf16[2,5,80,256]{3,2,1,0:T(8,128)(2,1)} %pick.1), calls=%async_computation.1 | async-start | bytes 819200 | tf_op jit(solution)/shard_map/all_to_all | solution.py:192
  25.7 15.1 %collective-permute-start.13 = (bf16[4,64,512]{2,1,0:T(8,128)(2,1)S(1)}, bf16[4,64,512]{2,1,0:T(8,128)(2,1)S(1)}, u32[]{:S(2)}, u32[]{:S(2)}) collective-permute-start(bf16[4,64,512]{2,1,0:T(8,128)(2,1)S(1)} %constant_dynamic-update-slice_fusion.refs_1_), channel_id=1, source_target_pairs={{0,1},{1,0},{2,3},{3,2},{4,5},{5,4},{6,7},{7,6},{8,9},{9,8},{10,11... | collective-permute-start | bytes 786440 | tf_op jit(solution)/shard_map/ppermute | solution.py:157
  39.2 8.5 %collective-permute-start = (bf16[1,2,80,256]{3,2,1,0:T(8,128)(2,1)S(1)}, bf16[1,2,80,256]{3,2,1,0:T(8,128)(2,1)S(1)}, u32[]{:S(2)}, u32[]{:S(2)}) collective-permute-start(bf16[1,2,80,256]{3,2,1,0:T(8,128)(2,1)S(1)} %get-tuple-element.15), channel_id=1, source_target_pairs={{0,16},{16,0},{1,17},{17,1},{2,18},{18,2},{3,19},{19,3},{4,20},{20... | collective-permute-start | bytes 245768 | tf_op jit(solution)/shard_map/ppermute | solution.py:160
  41.8 15.5 %all-to-all-start.2 = ((f32[32,4,128]{2,1,0:T(4,128)}), f32[32,4,128]{2,1,0:T(4,128)S(1)}, u32[]{:S(2)}, u32[]{:S(2)}) async-start(f32[32,4,128]{2,1,0:T(4,128)} %bitcast.4), calls=%async_computation.2 | async-start | bytes 131072 | tf_op jit(solution)/shard_map/all_to_all | solution.py:260
  44.4 4.8 %collective-permute-start.2 = (bf16[1,2,80,256]{3,2,1,0:T(8,128)(2,1)S(1)}, bf16[1,2,80,256]{3,2,1,0:T(8,128)(2,1)S(1)}, u32[]{:S(2)}, u32[]{:S(2)}) collective-permute-start(bf16[1,2,80,256]{3,2,1,0:T(8,128)(2,1)S(1)} %get-tuple-element.16), channel_id=1, source_target_pairs={{0,2},{1,3},{2,0},{3,1},{4,6},{5,7},{6,4},{7,5},{8,10},{9,11},{10,... | collective-permute-start | bytes 245768 | tf_op jit(solution)/shard_map/ppermute | solution.py:157
  46.1 5.7 %collective-permute-start.4 = (bf16[1,2,80,256]{3,2,1,0:T(8,128)(2,1)S(1)}, bf16[1,2,80,256]{3,2,1,0:T(8,128)(2,1)S(1)}, u32[]{:S(2)}, u32[]{:S(2)}) collective-permute-start(bf16[1,2,80,256]{3,2,1,0:T(8,128)(2,1)S(1)} %get-tuple-element.17), channel_id=1, source_target_pairs={{0,4},{1,5},{2,6},{3,7},{4,0},{5,1},{6,2},{7,3},{8,12},{9,13},{10,... | collective-permute-start | bytes 245768 | tf_op jit(solution)/shard_map/ppermute | solution.py:157
  47.7 6.0 %collective-permute-start.1 = (bf16[2,2,80,256]{3,2,1,0:T(8,128)(2,1)S(1)}, bf16[2,2,80,256]{3,2,1,0:T(8,128)(2,1)S(1)}, u32[]{:S(2)}, u32[]{:S(2)}) collective-permute-start(bf16[2,2,80,256]{3,2,1,0:T(8,128)(2,1)S(1)} %pad_maximum_fusion.4), channel_id=1, source_target_pairs={{0,2},{1,3},{2,0},{3,1},{4,6},{5,7},{6,4},{7,5},{8,10},{9,11},{10,... | collective-permute-start | bytes 491528 | tf_op jit(solution)/shard_map/ppermute | solution.py:157
  49.2 5.9 %collective-permute-start.3 = (bf16[2,2,80,256]{3,2,1,0:T(8,128)(2,1)S(1)}, bf16[2,2,80,256]{3,2,1,0:T(8,128)(2,1)S(1)}, u32[]{:S(2)}, u32[]{:S(2)}) collective-permute-start(bf16[2,2,80,256]{3,2,1,0:T(8,128)(2,1)S(1)} %pad_maximum_fusion.5), channel_id=1, source_target_pairs={{0,4},{1,5},{2,6},{3,7},{4,0},{5,1},{6,2},{7,3},{8,12},{9,13},{10,... | collective-permute-start | bytes 491528 | tf_op jit(solution)/shard_map/ppermute | solution.py:157
  51.9 5.4 %collective-permute-start.5 = (bf16[2,2,80,256]{3,2,1,0:T(8,128)(2,1)S(1)}, bf16[2,2,80,256]{3,2,1,0:T(8,128)(2,1)S(1)}, u32[]{:S(2)}, u32[]{:S(2)}) collective-permute-start(bf16[2,2,80,256]{3,2,1,0:T(8,128)(2,1)S(1)} %pad_maximum_fusion.6), channel_id=1, source_target_pairs={{0,16},{16,0},{1,17},{17,1},{2,18},{18,2},{3,19},{19,3},{4,20},{20... | collective-permute-start | bytes 491528 | tf_op jit(solution)/shard_map/ppermute | solution.py:160
  55.2 13.8 %copy-start.2 = (s32[6]{0:T(128)S(1)}, s32[6]{0:T(128)}, u32[]{:S(2)}) copy-start(s32[6]{0:T(128)} %offsets.3) | copy-start | bytes 76
  57.3 7.2 %collective-permute-start.14 = (bf16[4,2,80,256]{3,2,1,0:T(8,128)(2,1)S(1)}, bf16[4,2,80,256]{3,2,1,0:T(8,128)(2,1)S(1)}, u32[]{:S(2)}, u32[]{:S(2)}) collective-permute-start(bf16[4,2,80,256]{3,2,1,0:T(8,128)(2,1)S(1)} %pad_maximum_fusion.refs_0_), channel_id=1, source_target_pairs={{0,4},{1,5},{2,6},{3,7},{4,0},{5,1},{6,2},{7,3},{8,12},{9,13},{10,... | collective-permute-start | bytes 983048 | tf_op jit(solution)/shard_map/ppermute | solution.py:157
  57.6 7.4 %collective-permute-start.15 = (bf16[4,2,80,256]{3,2,1,0:T(8,128)(2,1)S(1)}, bf16[4,2,80,256]{3,2,1,0:T(8,128)(2,1)S(1)}, u32[]{:S(2)}, u32[]{:S(2)}) collective-permute-start(bf16[4,2,80,256]{3,2,1,0:T(8,128)(2,1)S(1)} %pad_maximum_fusion.refs_0_), channel_id=1, source_target_pairs={{0,1},{1,0},{2,3},{3,2},{4,5},{5,4},{6,7},{7,6},{8,9},{9,8},{10,11... | collective-permute-start | bytes 983048 | tf_op jit(solution)/shard_map/ppermute | solution.py:157
  57.6 10.1 %collective-permute-start.17 = (bf16[4,2,80,256]{3,2,1,0:T(8,128)(2,1)S(1)}, bf16[4,2,80,256]{3,2,1,0:T(8,128)(2,1)S(1)}, u32[]{:S(2)}, u32[]{:S(2)}) collective-permute-start(bf16[4,2,80,256]{3,2,1,0:T(8,128)(2,1)S(1)} %pad_maximum_fusion.1.refs_0_), channel_id=1, source_target_pairs={{0,16},{16,0},{1,17},{17,1},{2,18},{18,2},{3,19},{19,3},{4,20},{20... | collective-permute-start | bytes 983048 | tf_op jit(solution)/shard_map/ppermute | solution.py:160
  59.1 9.8 %collective-permute-start.20 = (bf16[4,2,80,256]{3,2,1,0:T(8,128)(2,1)S(1)}, bf16[4,2,80,256]{3,2,1,0:T(8,128)(2,1)S(1)}, u32[]{:S(2)}, u32[]{:S(2)}) collective-permute-start(bf16[4,2,80,256]{3,2,1,0:T(8,128)(2,1)S(1)} %pad_maximum_fusion.2.refs_4_), channel_id=1, source_target_pairs={{0,2},{1,3},{2,0},{3,1},{4,6},{5,7},{6,4},{7,5},{8,10},{9,11},{10,... | collective-permute-start | bytes 983048 | tf_op jit(solution)/shard_map/ppermute | solution.py:157
  64.5 4.4 %collective-permute-start.16 = (bf16[4,2,80,256]{3,2,1,0:T(8,128)(2,1)S(1)}, bf16[4,2,80,256]{3,2,1,0:T(8,128)(2,1)S(1)}, u32[]{:S(2)}, u32[]{:S(2)}) collective-permute-start(bf16[4,2,80,256]{3,2,1,0:T(8,128)(2,1)S(1)} %collective-permute-done.14.refs_1_), channel_id=1, source_target_pairs={{0,1},{1,0},{2,3},{3,2},{4,5},{5,4},{6,7},{7,6},{8,9},{9,8},{10,11... | collective-permute-start | bytes 983048 | tf_op jit(solution)/shard_map/ppermute | solution.py:157
  64.5 6.3 %collective-permute-start.18 = (bf16[4,2,80,256]{3,2,1,0:T(8,128)(2,1)S(1)}, bf16[4,2,80,256]{3,2,1,0:T(8,128)(2,1)S(1)}, u32[]{:S(2)}, u32[]{:S(2)}) collective-permute-start(bf16[4,2,80,256]{3,2,1,0:T(8,128)(2,1)S(1)} %pad_maximum_fusion.1.refs_0_), channel_id=1, source_target_pairs={{0,1},{1,0},{2,3},{3,2},{4,5},{5,4},{6,7},{7,6},{8,9},{9,8},{10,11... | collective-permute-start | bytes 983048 | tf_op jit(solution)/shard_map/ppermute | solution.py:157
  65.0 5.8 %collective-permute-start.21 = (bf16[4,2,80,256]{3,2,1,0:T(8,128)(2,1)S(1)}, bf16[4,2,80,256]{3,2,1,0:T(8,128)(2,1)S(1)}, u32[]{:S(2)}, u32[]{:S(2)}) collective-permute-start(bf16[4,2,80,256]{3,2,1,0:T(8,128)(2,1)S(1)} %pad_maximum_fusion.2.refs_4_), channel_id=1, source_target_pairs={{0,1},{1,0},{2,3},{3,2},{4,5},{5,4},{6,7},{7,6},{8,9},{9,8},{10,11... | collective-permute-start | bytes 983048 | tf_op jit(solution)/shard_map/ppermute | solution.py:157
  67.7 3.1 %collective-permute-start.19 = (bf16[4,2,80,256]{3,2,1,0:T(8,128)(2,1)S(1)}, bf16[4,2,80,256]{3,2,1,0:T(8,128)(2,1)S(1)}, u32[]{:S(2)}, u32[]{:S(2)}) collective-permute-start(bf16[4,2,80,256]{3,2,1,0:T(8,128)(2,1)S(1)} %collective-permute-done.17.refs_1_), channel_id=1, source_target_pairs={{0,1},{1,0},{2,3},{3,2},{4,5},{5,4},{6,7},{7,6},{8,9},{9,8},{10,11... | collective-permute-start | bytes 983048 | tf_op jit(solution)/shard_map/ppermute | solution.py:157
  68.9 1.9 %collective-permute-start.22 = (bf16[4,2,80,256]{3,2,1,0:T(8,128)(2,1)S(1)}, bf16[4,2,80,256]{3,2,1,0:T(8,128)(2,1)S(1)}, u32[]{:S(2)}, u32[]{:S(2)}) collective-permute-start(bf16[4,2,80,256]{3,2,1,0:T(8,128)(2,1)S(1)} %collective-permute-done.20.refs_5_), channel_id=1, source_target_pairs={{0,1},{1,0},{2,3},{3,2},{4,5},{5,4},{6,7},{7,6},{8,9},{9,8},{10,11... | collective-permute-start | bytes 983048 | tf_op jit(solution)/shard_map/ppermute | solution.py:157

commit v20 on v17

--- a/solution.py
+++ b/solution.py
@@ -9,7 +9,6 @@
 
 GROUPS = 6
 COLOURS = 3
-CHAINS = ((0,), (1, 2))
 HALF = 8
 SLICES = 2 * HALF
 VMEM = pl.BlockSpec(memory_space=pltpu.VMEM)
@@ -104,52 +103,51 @@
     return products[:half] + products[half:]
 
 
-def chain_kernel(cols, groups, slots, masks, first, last, offsets, start, *refs):
-    held, (out, basis_all, factor_all) = refs[: len(masks)], refs[len(masks) :]
+def assemble_kernel(masks, *refs):
+    held, (basis, factor) = refs[:-2], refs[-2:]
     mine = slice_index()
-    pv, pt = basis_all.shape[1] // SLICES, factor_all.shape[1] // SLICES
-    for slot, own_masks, ref in zip(slots, masks, held):
-        to = slice(slot, slot + ref.shape[1])
+    pv, pt = basis.shape[1] // SLICES, factor.shape[1] // SLICES
+    for own_masks, ref in zip(masks, held):
         for index, mask in enumerate(own_masks):
-            e = jnp.bitwise_xor(mine, mask)
-            basis_all[to, aligned(e, pv), :] = ref[index, :, :pv, :]
-            factor_all[to, aligned(e, pt), :] = ref[index, :, pv:, :]
-    if first:
-        n, each, width = start.shape
-        pieces = start[...].reshape(n // cols, cols, each, width).sum(0)
-        x = jnp.concatenate([pieces[c] for c in range(cols)], 1)
-        x = jnp.concatenate([x] + [jnp.zeros_like(x)] * (8 // each - 1), 0)
-    else:
-        x = start[...]
+            at = jnp.bitwise_xor(mine, mask)
+            basis[:, aligned(at, pv), :] = ref[index, :, :pv, :]
+            factor[:, aligned(at, pt), :] = ref[index, :, pv:, :]
+
+
+def chain_kernel(cols, offsets, start, *refs):
+    bases, factors, out = refs[:COLOURS], refs[COLOURS:-1], refs[-1]
+    n, each, width = start.shape
+    pieces = start[...].reshape(n // cols, cols, each, width).sum(0)
+    x = jnp.concatenate([pieces[c] for c in range(cols)], 1)
+    x = jnp.concatenate([x] + [jnp.zeros_like(x)] * (8 // each - 1), 0)
     wide = x.shape[1]
-    group_rows = basis_all.shape[1]
+    group_rows = bases[0].shape[1]
     before = jnp.int32(0)
-    for slot, group in enumerate(groups):
+    per = GROUPS // COLOURS
+    for group in range(GROUPS):
+        basis, factor = bases[group // per][group % per], factors[group // per][group % per]
         offset = offsets[group]
         x = pltpu.roll(x, lax.rem(before - offset + wide, wide), 1)
         before = offset
         block = x[:, :group_rows]
         weights = both(
-            jnp.dot(two_terms(block), basis_all[slot], preferred_element_type=jnp.float32)
+            jnp.dot(two_terms(block), basis, preferred_element_type=jnp.float32)
         )
         scaled = both(
             lax.dot_general(
-                two_terms(weights), factor_all[slot], (((1,), (1,)), ((), ())),
+                two_terms(weights), factor, (((1,), (1,)), ((), ())),
                 preferred_element_type=jnp.float32,
             )
         )
         change = both(
             lax.dot_general(
-                two_terms(scaled), basis_all[slot], (((1,), (1,)), ((), ())),
+                two_terms(scaled), basis, (((1,), (1,)), ((), ())),
                 preferred_element_type=jnp.float32,
             )
         )
         x = jnp.concatenate([block - change, x[:, group_rows:]], 1)
     x = pltpu.roll(x, before, 1)
-    if last:
-        out[...] = x[: out.shape[0]].astype(out.dtype)
-    else:
-        out[...] = x
+    out[...] = x[: out.shape[0]].astype(out.dtype)
 
 
 def local(rows, cols, sub_vectors, merge_factor, reflectors, wy_factors, owners, offsets):
@@ -267,35 +265,32 @@
         last_round.append(send(colours[k]))
         masks[k] = [masks[k], [m ^ mask for m in masks[k]]]
         masks[k] += [[m ^ 1 for m in ms] for ms in masks[k]]
-    last_round, state = lax.optimization_barrier((last_round, state))
-    held = []
+    bases, factors = [], []
     for k in range(COLOURS):
-        held.append([colours[k], last_round[k], over_col(colours[k], 1), over_col(last_round[k], 1)])
-
-    wide = cols * width
-    for members in CHAINS:
-        first, last = members[0] == 0, members[-1] == COLOURS - 1
-        groups = range(members[0] * per, (members[-1] + 1) * per)
-        arrays = [x for k in members for x in held[k]]
-        slots = [per * i for i, k in enumerate(members) for _ in held[k]]
-        state = pl.pallas_call(
-            functools.partial(
-                chain_kernel, cols, groups, slots, sum((masks[k] for k in members), []), first, last
-            ),
-            out_shape=jax.ShapeDtypeStruct(
-                (each, wide) if last else (8, wide), jnp.bfloat16 if last else jnp.float32
-            ),
-            in_specs=[SMEM, VMEM] + [VMEM] * len(arrays),
-            out_specs=VMEM,
-            scratch_shapes=[
-                pltpu.VMEM((len(groups), group_rows, reflect), dtype),
-                pltpu.VMEM((len(groups), reflect, reflect), dtype),
+        held = [colours[k], last_round[k], over_col(colours[k], 1), over_col(last_round[k], 1)]
+        whole = pl.pallas_call(
+            functools.partial(assemble_kernel, masks[k]),
+            out_shape=[
+                jax.ShapeDtypeStruct((per, group_rows, reflect), dtype),
+                jax.ShapeDtypeStruct((per, reflect, reflect), dtype),
             ],
-            compiler_params=limit(12),
-            cost_estimate=cost(arrays, 2 * len(groups) * 64 * group_rows * reflect),
-            name=f"chain{members[0]}",
-        )(offsets, state, *arrays)
-    return state
+            in_specs=[VMEM] * len(held),
+            out_specs=[VMEM, VMEM],
+            compiler_params=limit(4),
+            cost_estimate=cost(held),
+            name="assemble",
+        )(*held)
+        bases.append(whole[0])
+        factors.append(whole[1])
+    return pl.pallas_call(
+        functools.partial(chain_kernel, cols),
+        out_shape=jax.ShapeDtypeStruct((each, cols * width), jnp.bfloat16),
+        in_specs=[SMEM, VMEM] + [VMEM] * (2 * COLOURS),
+        out_specs=VMEM,
+        compiler_params=limit(4),
+        cost_estimate=cost(bases, 2 * GROUPS * 64 * group_rows * reflect),
+        name="chain",
+    )(offsets, state, *bases, *factors)
 
 
 def solution(mesh):

time: 68.3 us -> 79.6 us (1.17)
  local copies, waits for them, and re-layouts: 0.12 us -> 9.11 us
  Pallas kernels: 9.78 us -> 11.5 us
  waiting for transfers between devices: 27.3 us -> 28.3 us
    unnamed x14 -> x38, local copies, waits for them, and re-layouts: 0.07 us -> 9.06 us
    ppermute x20, waiting for transfers between devices: 9.88 us -> 16.6 us  [over_col(): return lax.ppermute(x, 'col', [(c, c ^ mask) for c in range(cols)])]
    all_to_all x1, waiting for transfers between devices: 5.03 us -> 0.01 us  [local(): lax.all_to_all(merged.reshape(rows * cols, each, width), ('row', 'col'),...]
    pallas_call x2 -> x4, Pallas kernels: 5.68 us -> 7.39 us  [the longest x1 4.92 us: local(): pl.pallas_call(functools.partial(chain_kernel, cols), out_shape=jax.Shape...]
    ppermute x20, starting transfers between devices: 17.1 us -> 16 us  [over_col(): return lax.ppermute(x, 'col', [(c, c ^ mask) for c in range(cols)])]
  transfers between devices with their start and end apart: 26 -> 26, of which waited for: 12 -> 10; matrix products, arithmetic and copies ran while one was open for 0% -> 0% of each run, Pallas kernels for 5% -> 5%
where the time goes in v20:
time: 79.6 us; the launch traced here: 79.1 us
  starting transfers between devices  29.7 us (37%)
  waiting for transfers between devices  28.3 us (36%)
  Pallas kernels  11.5 us (14%)
  local copies, waits for them, and re-layouts  9.11 us (11%)
    ppermute x20, waiting for transfers between devices, over_col(): return lax.ppermute(x, 'col', [(c, c ^ mask) for c in range(cols)])  16.6 us
    ppermute x20, starting transfers between devices, over_col(): return lax.ppermute(x, 'col', [(c, c ^ mask) for c in range(cols)])  16 us
    unnamed x38, local copies, waits for them, and re-layouts  9.06 us
    ppermute x4, waiting for transfers between devices, over_row(): return lax.ppermute(x, 'row', [(r, r ^ mask) for r in range(rows)])  6.27 us
    all_to_all x1, waiting for transfers between devices, local(): slices = lax.all_to_all(packed, 'col', 0, 0, axis_index_groups=members)  5.48 us
    all_to_all x1, starting transfers between devices, local(): slices = lax.all_to_all(packed, 'col', 0, 0, axis_index_groups=members)  5.4 us
    pallas_call x1, Pallas kernels, local(): pl.pallas_call(functools.partial(chain_kernel, cols), out_shape=jax.Shape...  4.92 us
    ppermute x4, starting transfers between devices, over_row(): return lax.ppermute(x, 'row', [(r, r ^ mask) for r in range(rows)])  4.64 us
  transfers between devices with their start and end apart: 26, of which 10 were waited for; matrix products, arithmetic and copies ran while one was open for 0% of the time, Pallas kernels for 5%

profile of v20, /device:TPU:0, one launch (start us, length us, event | category | flops | bytes accessed | tf_op | source)
XLA Modules:
  0.0 79.1 jit_solution(13888306829540853946)
XLA Ops:
  0.0 1.7 %pack.1 = bf16[8,80,256]{2,1,0:T(8,128)(2,1)} custom-call(bf16[16,64,256]{2,1,0:T(8,128)(2,1)} %bitcast.8, bf16[16,16,256]{2,1,0:T(8,128)(2,1)} %bitcast.12), custom_call_target="tpu_custom_call" | custom-call | bytes 655360 | tf_op jit(solution)/shard_map/pack/pallas_call | solution.py:169
  1.7 5.4 %all-to-all-start = ((bf16[8,80,256]{2,1,0:T(8,128)(2,1)}), bf16[8,80,256]{2,1,0:T(8,128)(2,1)S(1)}, u32[]{:S(2)}, u32[]{:S(2)}) async-start(bf16[8,80,256]{2,1,0:T(8,128)(2,1)} %pack.1), calls=%async_computation | async-start | bytes 655360 | tf_op jit(solution)/shard_map/all_to_all | solution.py:181
  7.1 2.7 %collective-permute-start.1 = (bf16[64,512]{1,0:T(8,128)(2,1)S(1)}, bf16[64,512]{1,0:T(8,128)(2,1)S(1)}, u32[]{:S(2)}, u32[]{:S(2)}) collective-permute-start(bf16[64,512]{1,0:T(8,128)(2,1)S(1)} %copy-done.15), channel_id=1, source_target_pairs={{0,8},{1,9},{2,10},{3,11},{4,12},{5,13},{6,14},{7,15},{8,0},{9,1},... | collective-permute-start | bytes 196616 | tf_op jit(solution)/shard_map/ppermute | solution.py:158
  9.8 5.5 %all-to-all-done.held = bf16[8,80,256]{2,1,0:T(8,128)(2,1)S(1)} async-done(((bf16[8,80,256]{2,1,0:T(8,128)(2,1)}), bf16[8,80,256]{2,1,0:T(8,128)(2,1)S(1)}, u32[]{:S(2)}, u32[]{:S(2)}) %all-to-all-start) | async-done | bytes 327712 | tf_op jit(solution)/shard_map/all_to_all | solution.py:181
  15.3 0.7 pick.1
  16.0 1.8 %collective-permute-start = (bf16[5,80,256]{2,1,0:T(8,128)(2,1)S(1)}, bf16[5,80,256]{2,1,0:T(8,128)(2,1)S(1)}, u32[]{:S(2)}, u32[]{:S(2)}) collective-permute-start(bf16[5,80,256]{2,1,0:T(8,128)(2,1)S(1)} %pick.1), channel_id=1, source_target_pairs={{0,8},{1,9},{2,10},{3,11},{4,12},{5,13},{6,14},{7,15},{8,0},{9,1},... | collective-permute-start | bytes 614408 | tf_op jit(solution)/shard_map/ppermute | solution.py:158
  17.8 1.6 %collective-permute-start.2 = (bf16[64,512]{1,0:T(8,128)(2,1)S(1)}, bf16[64,512]{1,0:T(8,128)(2,1)S(1)}, u32[]{:S(2)}, u32[]{:S(2)}) collective-permute-start(bf16[64,512]{1,0:T(8,128)(2,1)S(1)} %get-tuple-element.33), channel_id=1, source_target_pairs={{0,16},{16,0},{1,17},{17,1},{2,18},{18,2},{3,19},{19,3},{4,20},{20... | collective-permute-start | bytes 196616 | tf_op jit(solution)/shard_map/ppermute | solution.py:161
  19.3 2.8 %collective-permute-done.2 = bf16[64,512]{1,0:T(8,128)(2,1)S(1)} collective-permute-done((bf16[64,512]{1,0:T(8,128)(2,1)S(1)}, bf16[64,512]{1,0:T(8,128)(2,1)S(1)}, u32[]{:S(2)}, u32[]{:S(2)}) %collective-permute-start.2) | collective-permute-done | bytes 65568 | tf_op jit(solution)/shard_map/ppermute | solution.py:161
  22.1 5.8 %collective-permute-done.refs_0_ = bf16[5,80,256]{2,1,0:T(8,128)(2,1)S(1)} collective-permute-done((bf16[5,80,256]{2,1,0:T(8,128)(2,1)S(1)}, bf16[5,80,256]{2,1,0:T(8,128)(2,1)S(1)}, u32[]{:S(2)}, u32[]{:S(2)}) %collective-permute-start) | collective-permute-done | bytes 204832 | tf_op jit(solution)/shard_map/ppermute | solution.py:158
  27.9 0.6 order.1
  28.5 1.6 %collective-permute-start.9 = (bf16[1,2,80,256]{3,2,1,0:T(8,128)(2,1)S(1)}, bf16[1,2,80,256]{3,2,1,0:T(8,128)(2,1)S(1)}, u32[]{:S(2)}, u32[]{:S(2)}) collective-permute-start(bf16[1,2,80,256]{3,2,1,0:T(8,128)(2,1)S(1)} %get-tuple-element.24), channel_id=1, source_target_pairs={{0,16},{16,0},{1,17},{17,1},{2,18},{18,2},{3,19},{19,3},{4,20},{20... | collective-permute-start | bytes 245768 | tf_op jit(solution)/shard_map/ppermute | solution.py:161
  30.0 1.3 %collective-permute-start.14 = (bf16[1,2,80,256]{3,2,1,0:T(8,128)(2,1)S(1)}, bf16[1,2,80,256]{3,2,1,0:T(8,128)(2,1)S(1)}, u32[]{:S(2)}, u32[]{:S(2)}) collective-permute-start(bf16[1,2,80,256]{3,2,1,0:T(8,128)(2,1)S(1)} %get-tuple-element.26), channel_id=1, source_target_pairs={{0,2},{1,3},{2,0},{3,1},{4,6},{5,7},{6,4},{7,5},{8,10},{9,11},{10,... | collective-permute-start | bytes 245768 | tf_op jit(solution)/shard_map/ppermute | solution.py:158
  31.4 0.8 %collective-permute-start.3 = (bf16[1,64,512]{2,1,0:T(8,128)(2,1)S(1)}, bf16[1,64,512]{2,1,0:T(8,128)(2,1)S(1)}, u32[]{:S(2)}, u32[]{:S(2)}) collective-permute-start(bf16[1,64,512]{2,1,0:T(8,128)(2,1)S(1)} %bitcast.5), channel_id=1, source_target_pairs={{0,2},{1,3},{2,0},{3,1},{4,6},{5,7},{6,4},{7,5},{8,10},{9,11},{10,... | collective-permute-start | bytes 196616 | tf_op jit(solution)/shard_map/ppermute | solution.py:158
  32.2 1.9 %collective-permute-start.19 = (bf16[1,2,80,256]{3,2,1,0:T(8,128)(2,1)S(1)}, bf16[1,2,80,256]{3,2,1,0:T(8,128)(2,1)S(1)}, u32[]{:S(2)}, u32[]{:S(2)}) collective-permute-start(bf16[1,2,80,256]{3,2,1,0:T(8,128)(2,1)S(1)} %get-tuple-element.28), channel_id=1, source_target_pairs={{0,4},{1,5},{2,6},{3,7},{4,0},{5,1},{6,2},{7,3},{8,12},{9,13},{10,... | collective-permute-start | bytes 245768 | tf_op jit(solution)/shard_map/ppermute | solution.py:158
  34.2 1.5 %collective-permute-done.4 = bf16[1,64,512]{2,1,0:T(8,128)(2,1)S(1)} collective-permute-done((bf16[1,64,512]{2,1,0:T(8,128)(2,1)S(1)}, bf16[1,64,512]{2,1,0:T(8,128)(2,1)S(1)}, u32[]{:S(2)}, u32[]{:S(2)}) %collective-permute-start.4) | collective-permute-done | bytes 65568 | tf_op jit(solution)/shard_map/ppermute | solution.py:158
  35.7 1.2 %collective-permute-start.6 = (bf16[2,64,512]{2,1,0:T(8,128)(2,1)S(1)}, bf16[2,64,512]{2,1,0:T(8,128)(2,1)S(1)}, u32[]{:S(2)}, u32[]{:S(2)}) collective-permute-start(bf16[2,64,512]{2,1,0:T(8,128)(2,1)S(1)} %pad_maximum_fusion.5), channel_id=1, source_target_pairs={{0,2},{1,3},{2,0},{3,1},{4,6},{5,7},{6,4},{7,5},{8,10},{9,11},{10,... | collective-permute-start | bytes 393224 | tf_op jit(solution)/shard_map/ppermute | solution.py:158
  36.9 1.5 %collective-permute-start.5 = (bf16[2,64,512]{2,1,0:T(8,128)(2,1)S(1)}, bf16[2,64,512]{2,1,0:T(8,128)(2,1)S(1)}, u32[]{:S(2)}, u32[]{:S(2)}) collective-permute-start(bf16[2,64,512]{2,1,0:T(8,128)(2,1)S(1)} %pad_maximum_fusion.4), channel_id=1, source_target_pairs={{0,4},{1,5},{2,6},{3,7},{4,0},{5,1},{6,2},{7,3},{8,12},{9,13},{10,... | collective-permute-start | bytes 393224 | tf_op jit(solution)/shard_map/ppermute | solution.py:158
  38.7 0.6 collective-permute-start.10
  39.2 0.6 collective-permute-start.20
  39.9 2.1 %collective-permute-done.5 = bf16[2,64,512]{2,1,0:T(8,128)(2,1)S(1)} collective-permute-done((bf16[2,64,512]{2,1,0:T(8,128)(2,1)S(1)}, bf16[2,64,512]{2,1,0:T(8,128)(2,1)S(1)}, u32[]{:S(2)}, u32[]{:S(2)}) %collective-permute-start.5) | collective-permute-done | bytes 131104 | tf_op jit(solution)/shard_map/ppermute | solution.py:158
  42.0 1.5 %collective-permute-start.15 = (bf16[2,2,80,256]{3,2,1,0:T(8,128)(2,1)S(1)}, bf16[2,2,80,256]{3,2,1,0:T(8,128)(2,1)S(1)}, u32[]{:S(2)}, u32[]{:S(2)}) collective-permute-start(bf16[2,2,80,256]{3,2,1,0:T(8,128)(2,1)S(1)} %pad_maximum_fusion.2), channel_id=1, source_target_pairs={{0,4},{1,5},{2,6},{3,7},{4,0},{5,1},{6,2},{7,3},{8,12},{9,13},{10,... | collective-permute-start | bytes 491528 | tf_op jit(solution)/shard_map/ppermute | solution.py:158
  43.5 2.2 %collective-permute-done.20 = bf16[2,2,80,256]{3,2,1,0:T(8,128)(2,1)S(1)} collective-permute-done((bf16[2,2,80,256]{3,2,1,0:T(8,128)(2,1)S(1)}, bf16[2,2,80,256]{3,2,1,0:T(8,128)(2,1)S(1)}, u32[]{:S(2)}, u32[]{:S(2)}) %collective-permute-start.20) | collective-permute-done | bytes 163872 | tf_op jit(solution)/shard_map/ppermute | solution.py:161
  45.7 1.6 %collective-permute-done.15 = bf16[2,2,80,256]{3,2,1,0:T(8,128)(2,1)S(1)} collective-permute-done((bf16[2,2,80,256]{3,2,1,0:T(8,128)(2,1)S(1)}, bf16[2,2,80,256]{3,2,1,0:T(8,128)(2,1)S(1)}, u32[]{:S(2)}, u32[]{:S(2)}) %collective-permute-start.15) | collective-permute-done | bytes 163872 | tf_op jit(solution)/shard_map/ppermute | solution.py:158
  47.3 0.9 %collective-permute-start.21 = (bf16[4,2,80,256]{3,2,1,0:T(8,128)(2,1)S(1)}, bf16[4,2,80,256]{3,2,1,0:T(8,128)(2,1)S(1)}, u32[]{:S(2)}, u32[]{:S(2)}) collective-permute-start(bf16[4,2,80,256]{3,2,1,0:T(8,128)(2,1)S(1)} %constant_dynamic-update-slice_fusion.8.refs_0_), channel_id=1, source_target_pairs={{0,2},{1,3},{2,0},{3,1},{4,6},{5,7},{6,4},{7,5},{8,10},{9,11},{10,... | collective-permute-start | bytes 983048 | tf_op jit(solution)/shard_map/ppermute | solution.py:158
  48.2 0.9 %collective-permute-start.16 = (bf16[4,2,80,256]{3,2,1,0:T(8,128)(2,1)S(1)}, bf16[4,2,80,256]{3,2,1,0:T(8,128)(2,1)S(1)}, u32[]{:S(2)}, u32[]{:S(2)}) collective-permute-start(bf16[4,2,80,256]{3,2,1,0:T(8,128)(2,1)S(1)} %constant_dynamic-update-slice_fusion.5.refs_0_), channel_id=1, source_target_pairs={{0,16},{16,0},{1,17},{17,1},{2,18},{18,2},{3,19},{19,3},{4,20},{20... | collective-permute-start | bytes 983048 | tf_op jit(solution)/shard_map/ppermute | solution.py:161
  49.2 0.8 %collective-permute-start.11 = (bf16[4,2,80,256]{3,2,1,0:T(8,128)(2,1)S(1)}, bf16[4,2,80,256]{3,2,1,0:T(8,128)(2,1)}, u32[]{:S(2)}, u32[]{:S(2)}) collective-permute-start(bf16[4,2,80,256]{3,2,1,0:T(8,128)(2,1)S(1)} %constant_dynamic-update-slice_fusion.2.refs_0_), channel_id=1, source_target_pairs={{0,4},{1,5},{2,6},{3,7},{4,0},{5,1},{6,2},{7,3},{8,12},{9,13},{10,... | collective-permute-start | bytes 983048 | tf_op jit(solution)/shard_map/ppermute | solution.py:158
  50.1 1.5 %collective-permute-done.8.refs_3_ = bf16[4,64,512]{2,1,0:T(8,128)(2,1)S(1)} collective-permute-done((bf16[4,64,512]{2,1,0:T(8,128)(2,1)S(1)}, bf16[4,64,512]{2,1,0:T(8,128)(2,1)S(1)}, u32[]{:S(2)}, u32[]{:S(2)}) %collective-permute-start.8) | collective-permute-done | bytes 262176 | tf_op jit(solution)/shard_map/ppermute | solution.py:158
  51.6 0.1 collective-permute-start.17
  51.8 4.1 %collective-permute-done.21.refs_1_ = bf16[4,2,80,256]{3,2,1,0:T(8,128)(2,1)S(1)} collective-permute-done((bf16[4,2,80,256]{3,2,1,0:T(8,128)(2,1)S(1)}, bf16[4,2,80,256]{3,2,1,0:T(8,128)(2,1)S(1)}, u32[]{:S(2)}, u32[]{:S(2)}) %collective-permute-start.21) | collective-permute-done | bytes 327712 | tf_op jit(solution)/shard_map/ppermute | solution.py:158
  55.8 1.3 %collective-permute-done.16.refs_1_ = bf16[4,2,80,256]{3,2,1,0:T(8,128)(2,1)S(1)} collective-permute-done((bf16[4,2,80,256]{3,2,1,0:T(8,128)(2,1)S(1)}, bf16[4,2,80,256]{3,2,1,0:T(8,128)(2,1)S(1)}, u32[]{:S(2)}, u32[]{:S(2)}) %collective-permute-start.16) | collective-permute-done | bytes 327712 | tf_op jit(solution)/shard_map/ppermute | solution.py:161
  57.2 0.5 collective-permute-start.12
  57.8 1.1 %merge.1 = f32[128,128]{1,0:T(8,128)} custom-call(bf16[4096,128]{1,0:T(8,128)(2,1)S(1)} %copy-done, bf16[4,64,512]{2,1,0:T(8,128)(2,1)S(1)} %pad_maximum_fusion.refs_0_, bf16[4,64,512]{2,1,0:T(8,128)(2,1)S(1)} %constant_dynamic-update-slice_fusion.refs_1_, bf16[4,64,512]{2,1,0:T(8,128)(2,1)S(1)} %collective-permute-done.7.refs_2_, ...), custom_call_target="tpu_custom_call" | custom-call | flops 134217728 | bytes 1048576 | tf_op jit(solution)/shard_map/merge/pallas_call | solution.py:230
  58.9 3.7 %all-to-all-start.1 = ((f32[32,4,128]{2,1,0:T(4,128)}), f32[32,4,128]{2,1,0:T(4,128)S(1)}, u32[]{:S(2)}, u32[]{:S(2)}) async-start(f32[32,4,128]{2,1,0:T(4,128)} %bitcast.4), calls=%async_computation.1 | async-start | bytes 131072 | tf_op jit(solution)/shard_map/all_to_all | solution.py:261
  62.6 0.7 copy-done.5
  63.3 1.0 %copy-done.6 = bf16[4,2,80,256]{3,2,1,0:T(8,128)(2,1)S(1)} copy-done((bf16[4,2,80,256]{3,2,1,0:T(8,128)(2,1)S(1)}, bf16[4,2,80,256]{3,2,1,0:T(8,128)(2,1)}, u32[]{:S(2)}) %copy-start.6) | copy-done | bytes 327704
  64.3 0.1 assemble.5
  64.4 0.7 copy-done.7
  65.1 0.7 copy-done.3
  65.9 1.0 %copy-done.4 = bf16[4,2,80,256]{3,2,1,0:T(8,128)(2,1)S(1)} copy-done((bf16[4,2,80,256]{3,2,1,0:T(8,128)(2,1)S(1)}, bf16[4,2,80,256]{3,2,1,0:T(8,128)(2,1)}, u32[]{:S(2)}) %copy-start.4) | copy-done | bytes 327704
  66.8 1.1 %assemble.4 = (bf16[2,1024,256]{2,1,0:T(8,128)(2,1)S(1)}, bf16[2,256,256]{2,1,0:T(8,128)(2,1)S(1)}) custom-call(bf16[4,2,80,256]{3,2,1,0:T(8,128)(2,1)S(1)} %constant_dynamic-update-slice_fusion.5.refs_0_, bf16[4,2,80,256]{3,2,1,0:T(8,128)(2,1)S(1)} %copy-done.2, bf16[4,2,80,256]{3,2,1,0:T(8,128)(2,1)S(1)} %copy-done.4, ...), custom_call_target="tpu_custom_call" | custom-call | bytes 1310720 | tf_op jit(solution)/shard_map/assemble/pallas_call | solution.py:271
  67.9 0.7 copy-done.9
  68.6 1.3 %assemble.3 = (bf16[2,1024,256]{2,1,0:T(8,128)(2,1)S(1)}, bf16[2,256,256]{2,1,0:T(8,128)(2,1)S(1)}) custom-call(bf16[4,2,80,256]{3,2,1,0:T(8,128)(2,1)S(1)} %constant_dynamic-update-slice_fusion.2.refs_0_, bf16[4,2,80,256]{3,2,1,0:T(8,128)(2,1)} %collective-permute-done.11.refs_1_, bf16[4,2,80,256]{3,2,1,0:T(8,128)(2,1)} %collective-permute-done.12.refs_2_, ...), custom_call_target="tpu_custom_call" | custom-call | bytes 1310720 | tf_op jit(solution)/shard_map/assemble/pallas_call | solution.py:271
  69.9 0.7 copy-done.11
  70.6 0.7 copy-done.14
  71.3 0.9 %copy-done.8 = bf16[2,256,256]{2,1,0:T(8,128)(2,1)S(1)} copy-done((bf16[2,256,256]{2,1,0:T(8,128)(2,1)S(1)}, bf16[2,256,256]{2,1,0:T(8,128)(2,1)}, u32[]{:S(2)}) %copy-start.8) | copy-done | bytes 262168
  72.3 0.9 %copy-done.10 = bf16[2,256,256]{2,1,0:T(8,128)(2,1)S(1)} copy-done((bf16[2,256,256]{2,1,0:T(8,128)(2,1)S(1)}, bf16[2,256,256]{2,1,0:T(8,128)(2,1)}, u32[]{:S(2)}) %copy-start.10) | copy-done | bytes 262168
  73.2 0.9 %copy-done.12 = bf16[2,256,256]{2,1,0:T(8,128)(2,1)S(1)} copy-done((bf16[2,256,256]{2,1,0:T(8,128)(2,1)S(1)}, bf16[2,256,256]{2,1,0:T(8,128)(2,1)}, u32[]{:S(2)}) %copy-start.12) | copy-done | bytes 262168
  74.2 4.9 %chain.1 = bf16[4,2048]{1,0:T(4,128)(2,1)} custom-call(s32[6]{0:T(128)S(1)} %copy-done.14, f32[32,4,128]{2,1,0:T(4,128)S(1)} %all-to-all-done.1.start, bf16[2,1024,256]{2,1,0:T(8,128)(2,1)S(1)} %get-tuple-element.25.refs_0_, bf16[2,1024,256]{2,1,0:T(8,128)(2,1)S(1)} %get-tuple-element.27.refs_1_, bf16[2,1024,256]{2,1,0:T(8,128)(2,1)S(1)} %get-tuple-element.29.refs_2_, ...), custom_call_target="tpu_custom_call" | custom-call | flops 201326592 | bytes 3145728 | tf_op jit(solution)/shard_map/chain/pallas_call | solution.py:285
  (61 shorter events, 0.7 us)
Async XLA Ops:
  1.7 5.4 %copy-start.15 = (bf16[64,512]{1,0:T(8,128)(2,1)S(1)}, bf16[64,512]{1,0:T(8,128)(2,1)}, u32[]{:S(2)}) copy-start(bf16[64,512]{1,0:T(8,128)(2,1)} %param.7) | copy-start | bytes 196612
  1.7 13.5 %all-to-all-start = ((bf16[8,80,256]{2,1,0:T(8,128)(2,1)}), bf16[8,80,256]{2,1,0:T(8,128)(2,1)S(1)}, u32[]{:S(2)}, u32[]{:S(2)}) async-start(bf16[8,80,256]{2,1,0:T(8,128)(2,1)} %pack.1), calls=%async_computation | async-start | bytes 655360 | tf_op jit(solution)/shard_map/all_to_all | solution.py:181
  7.1 10.6 %collective-permute-start.1 = (bf16[64,512]{1,0:T(8,128)(2,1)S(1)}, bf16[64,512]{1,0:T(8,128)(2,1)S(1)}, u32[]{:S(2)}, u32[]{:S(2)}) collective-permute-start(bf16[64,512]{1,0:T(8,128)(2,1)S(1)} %copy-done.15), channel_id=1, source_target_pairs={{0,8},{1,9},{2,10},{3,11},{4,12},{5,13},{6,14},{7,15},{8,0},{9,1},... | collective-permute-start | bytes 196616 | tf_op jit(solution)/shard_map/ppermute | solution.py:158
  9.8 5.5 %copy-start.13 = (s32[6]{0:T(128)S(1)}, s32[6]{0:T(128)}, u32[]{:S(2)}) copy-start(s32[6]{0:T(128)} %owners.3) | copy-start | bytes 76
  16.0 11.9 %collective-permute-start = (bf16[5,80,256]{2,1,0:T(8,128)(2,1)S(1)}, bf16[5,80,256]{2,1,0:T(8,128)(2,1)S(1)}, u32[]{:S(2)}, u32[]{:S(2)}) collective-permute-start(bf16[5,80,256]{2,1,0:T(8,128)(2,1)S(1)} %pick.1), channel_id=1, source_target_pairs={{0,8},{1,9},{2,10},{3,11},{4,12},{5,13},{6,14},{7,15},{8,0},{9,1},... | collective-permute-start | bytes 614408 | tf_op jit(solution)/shard_map/ppermute | solution.py:158
  17.8 4.3 %collective-permute-start.2 = (bf16[64,512]{1,0:T(8,128)(2,1)S(1)}, bf16[64,512]{1,0:T(8,128)(2,1)S(1)}, u32[]{:S(2)}, u32[]{:S(2)}) collective-permute-start(bf16[64,512]{1,0:T(8,128)(2,1)S(1)} %get-tuple-element.33), channel_id=1, source_target_pairs={{0,16},{16,0},{1,17},{17,1},{2,18},{18,2},{3,19},{19,3},{4,20},{20... | collective-permute-start | bytes 196616 | tf_op jit(solution)/shard_map/ppermute | solution.py:161
  28.5 10.0 %collective-permute-start.9 = (bf16[1,2,80,256]{3,2,1,0:T(8,128)(2,1)S(1)}, bf16[1,2,80,256]{3,2,1,0:T(8,128)(2,1)S(1)}, u32[]{:S(2)}, u32[]{:S(2)}) collective-permute-start(bf16[1,2,80,256]{3,2,1,0:T(8,128)(2,1)S(1)} %get-tuple-element.24), channel_id=1, source_target_pairs={{0,16},{16,0},{1,17},{17,1},{2,18},{18,2},{3,19},{19,3},{4,20},{20... | collective-permute-start | bytes 245768 | tf_op jit(solution)/shard_map/ppermute | solution.py:161
  30.0 9.2 %collective-permute-start.14 = (bf16[1,2,80,256]{3,2,1,0:T(8,128)(2,1)S(1)}, bf16[1,2,80,256]{3,2,1,0:T(8,128)(2,1)S(1)}, u32[]{:S(2)}, u32[]{:S(2)}) collective-permute-start(bf16[1,2,80,256]{3,2,1,0:T(8,128)(2,1)S(1)} %get-tuple-element.26), channel_id=1, source_target_pairs={{0,2},{1,3},{2,0},{3,1},{4,6},{5,7},{6,4},{7,5},{8,10},{9,11},{10,... | collective-permute-start | bytes 245768 | tf_op jit(solution)/shard_map/ppermute | solution.py:158
  31.4 4.4 %collective-permute-start.4 = (bf16[1,64,512]{2,1,0:T(8,128)(2,1)S(1)}, bf16[1,64,512]{2,1,0:T(8,128)(2,1)S(1)}, u32[]{:S(2)}, u32[]{:S(2)}) collective-permute-start(bf16[1,64,512]{2,1,0:T(8,128)(2,1)S(1)} %bitcast.9), channel_id=1, source_target_pairs={{0,4},{1,5},{2,6},{3,7},{4,0},{5,1},{6,2},{7,3},{8,12},{9,13},{10,... | collective-permute-start | bytes 196616 | tf_op jit(solution)/shard_map/ppermute | solution.py:158
  31.4 5.5 %collective-permute-start.3 = (bf16[1,64,512]{2,1,0:T(8,128)(2,1)S(1)}, bf16[1,64,512]{2,1,0:T(8,128)(2,1)S(1)}, u32[]{:S(2)}, u32[]{:S(2)}) collective-permute-start(bf16[1,64,512]{2,1,0:T(8,128)(2,1)S(1)} %bitcast.5), channel_id=1, source_target_pairs={{0,2},{1,3},{2,0},{3,1},{4,6},{5,7},{6,4},{7,5},{8,10},{9,11},{10,... | collective-permute-start | bytes 196616 | tf_op jit(solution)/shard_map/ppermute | solution.py:158
  32.2 6.4 %collective-permute-start.19 = (bf16[1,2,80,256]{3,2,1,0:T(8,128)(2,1)S(1)}, bf16[1,2,80,256]{3,2,1,0:T(8,128)(2,1)S(1)}, u32[]{:S(2)}, u32[]{:S(2)}) collective-permute-start(bf16[1,2,80,256]{3,2,1,0:T(8,128)(2,1)S(1)} %get-tuple-element.28), channel_id=1, source_target_pairs={{0,4},{1,5},{2,6},{3,7},{4,0},{5,1},{6,2},{7,3},{8,12},{9,13},{10,... | collective-permute-start | bytes 245768 | tf_op jit(solution)/shard_map/ppermute | solution.py:158
  35.7 13.4 %collective-permute-start.6 = (bf16[2,64,512]{2,1,0:T(8,128)(2,1)S(1)}, bf16[2,64,512]{2,1,0:T(8,128)(2,1)S(1)}, u32[]{:S(2)}, u32[]{:S(2)}) collective-permute-start(bf16[2,64,512]{2,1,0:T(8,128)(2,1)S(1)} %pad_maximum_fusion.5), channel_id=1, source_target_pairs={{0,2},{1,3},{2,0},{3,1},{4,6},{5,7},{6,4},{7,5},{8,10},{9,11},{10,... | collective-permute-start | bytes 393224 | tf_op jit(solution)/shard_map/ppermute | solution.py:158
  36.9 5.0 %collective-permute-start.5 = (bf16[2,64,512]{2,1,0:T(8,128)(2,1)S(1)}, bf16[2,64,512]{2,1,0:T(8,128)(2,1)S(1)}, u32[]{:S(2)}, u32[]{:S(2)}) collective-permute-start(bf16[2,64,512]{2,1,0:T(8,128)(2,1)S(1)} %pad_maximum_fusion.4), channel_id=1, source_target_pairs={{0,4},{1,5},{2,6},{3,7},{4,0},{5,1},{6,2},{7,3},{8,12},{9,13},{10,... | collective-permute-start | bytes 393224 | tf_op jit(solution)/shard_map/ppermute | solution.py:158
  38.5 11.5 %collective-permute-start.7 = (bf16[4,64,512]{2,1,0:T(8,128)(2,1)S(1)}, bf16[4,64,512]{2,1,0:T(8,128)(2,1)S(1)}, u32[]{:S(2)}, u32[]{:S(2)}) collective-permute-start(bf16[4,64,512]{2,1,0:T(8,128)(2,1)S(1)} %pad_maximum_fusion.refs_0_), channel_id=1, source_target_pairs={{0,1},{1,0},{2,3},{3,2},{4,5},{5,4},{6,7},{7,6},{8,9},{9,8},{10,11... | collective-permute-start | bytes 786440 | tf_op jit(solution)/shard_map/ppermute | solution.py:158
  38.7 9.6 %collective-permute-start.10 = (bf16[2,2,80,256]{3,2,1,0:T(8,128)(2,1)S(1)}, bf16[2,2,80,256]{3,2,1,0:T(8,128)(2,1)S(1)}, u32[]{:S(2)}, u32[]{:S(2)}) collective-permute-start(bf16[2,2,80,256]{3,2,1,0:T(8,128)(2,1)S(1)} %pad_maximum_fusion.1), channel_id=1, source_target_pairs={{0,2},{1,3},{2,0},{3,1},{4,6},{5,7},{6,4},{7,5},{8,10},{9,11},{10,... | collective-permute-start | bytes 491528 | tf_op jit(solution)/shard_map/ppermute | solution.py:158
  39.2 6.4 %collective-permute-start.20 = (bf16[2,2,80,256]{3,2,1,0:T(8,128)(2,1)S(1)}, bf16[2,2,80,256]{3,2,1,0:T(8,128)(2,1)S(1)}, u32[]{:S(2)}, u32[]{:S(2)}) collective-permute-start(bf16[2,2,80,256]{3,2,1,0:T(8,128)(2,1)S(1)} %pad_maximum_fusion.3), channel_id=1, source_target_pairs={{0,16},{16,0},{1,17},{17,1},{2,18},{18,2},{3,19},{19,3},{4,20},{20... | collective-permute-start | bytes 491528 | tf_op jit(solution)/shard_map/ppermute | solution.py:161
  39.9 17.9 %copy-start = (bf16[4096,128]{1,0:T(8,128)(2,1)S(1)}, bf16[4096,128]{1,0:T(8,128)(2,1)}, u32[]{:S(2)}) copy-start(bf16[4096,128]{1,0:T(8,128)(2,1)} %sub.6) | copy-start | bytes 3145732
  42.0 5.3 %collective-permute-start.15 = (bf16[2,2,80,256]{3,2,1,0:T(8,128)(2,1)S(1)}, bf16[2,2,80,256]{3,2,1,0:T(8,128)(2,1)S(1)}, u32[]{:S(2)}, u32[]{:S(2)}) collective-permute-start(bf16[2,2,80,256]{3,2,1,0:T(8,128)(2,1)S(1)} %pad_maximum_fusion.2), channel_id=1, source_target_pairs={{0,4},{1,5},{2,6},{3,7},{4,0},{5,1},{6,2},{7,3},{8,12},{9,13},{10,... | collective-permute-start | bytes 491528 | tf_op jit(solution)/shard_map/ppermute | solution.py:158
  45.6 11.5 %collective-permute-start.22 = (bf16[4,2,80,256]{3,2,1,0:T(8,128)(2,1)S(1)}, bf16[4,2,80,256]{3,2,1,0:T(8,128)(2,1)S(1)}, u32[]{:S(2)}, u32[]{:S(2)}) collective-permute-start(bf16[4,2,80,256]{3,2,1,0:T(8,128)(2,1)S(1)} %constant_dynamic-update-slice_fusion.8.refs_0_), channel_id=1, source_target_pairs={{0,1},{1,0},{2,3},{3,2},{4,5},{5,4},{6,7},{7,6},{8,9},{9,8},{10,11... | collective-permute-start | bytes 983048 | tf_op jit(solution)/shard_map/ppermute | solution.py:158
  47.3 8.5 %collective-permute-start.21 = (bf16[4,2,80,256]{3,2,1,0:T(8,128)(2,1)S(1)}, bf16[4,2,80,256]{3,2,1,0:T(8,128)(2,1)S(1)}, u32[]{:S(2)}, u32[]{:S(2)}) collective-permute-start(bf16[4,2,80,256]{3,2,1,0:T(8,128)(2,1)S(1)} %constant_dynamic-update-slice_fusion.8.refs_0_), channel_id=1, source_target_pairs={{0,2},{1,3},{2,0},{3,1},{4,6},{5,7},{6,4},{7,5},{8,10},{9,11},{10,... | collective-permute-start | bytes 983048 | tf_op jit(solution)/shard_map/ppermute | solution.py:158
  48.2 9.0 %collective-permute-start.16 = (bf16[4,2,80,256]{3,2,1,0:T(8,128)(2,1)S(1)}, bf16[4,2,80,256]{3,2,1,0:T(8,128)(2,1)S(1)}, u32[]{:S(2)}, u32[]{:S(2)}) collective-permute-start(bf16[4,2,80,256]{3,2,1,0:T(8,128)(2,1)S(1)} %constant_dynamic-update-slice_fusion.5.refs_0_), channel_id=1, source_target_pairs={{0,16},{16,0},{1,17},{17,1},{2,18},{18,2},{3,19},{19,3},{4,20},{20... | collective-permute-start | bytes 983048 | tf_op jit(solution)/shard_map/ppermute | solution.py:161
  49.2 8.5 %collective-permute-start.11 = (bf16[4,2,80,256]{3,2,1,0:T(8,128)(2,1)S(1)}, bf16[4,2,80,256]{3,2,1,0:T(8,128)(2,1)}, u32[]{:S(2)}, u32[]{:S(2)}) collective-permute-start(bf16[4,2,80,256]{3,2,1,0:T(8,128)(2,1)S(1)} %constant_dynamic-update-slice_fusion.2.refs_0_), channel_id=1, source_target_pairs={{0,4},{1,5},{2,6},{3,7},{4,0},{5,1},{6,2},{7,3},{8,12},{9,13},{10,... | collective-permute-start | bytes 983048 | tf_op jit(solution)/shard_map/ppermute | solution.py:158
  50.0 1.6 %collective-permute-start.8 = (bf16[4,64,512]{2,1,0:T(8,128)(2,1)S(1)}, bf16[4,64,512]{2,1,0:T(8,128)(2,1)S(1)}, u32[]{:S(2)}, u32[]{:S(2)}) collective-permute-start(bf16[4,64,512]{2,1,0:T(8,128)(2,1)S(1)} %constant_dynamic-update-slice_fusion.refs_1_), channel_id=1, source_target_pairs={{0,1},{1,0},{2,3},{3,2},{4,5},{5,4},{6,7},{7,6},{8,9},{9,8},{10,11... | collective-permute-start | bytes 786440 | tf_op jit(solution)/shard_map/ppermute | solution.py:158
  51.6 13.5 %collective-permute-start.17 = (bf16[4,2,80,256]{3,2,1,0:T(8,128)(2,1)S(1)}, bf16[4,2,80,256]{3,2,1,0:T(8,128)(2,1)S(1)}, u32[]{:S(2)}, u32[]{:S(2)}) collective-permute-start(bf16[4,2,80,256]{3,2,1,0:T(8,128)(2,1)S(1)} %constant_dynamic-update-slice_fusion.5.refs_0_), channel_id=1, source_target_pairs={{0,1},{1,0},{2,3},{3,2},{4,5},{5,4},{6,7},{7,6},{8,9},{9,8},{10,11... | collective-permute-start | bytes 983048 | tf_op jit(solution)/shard_map/ppermute | solution.py:158
  55.8 6.8 %collective-permute-start.23 = (bf16[4,2,80,256]{3,2,1,0:T(8,128)(2,1)S(1)}, bf16[4,2,80,256]{3,2,1,0:T(8,128)(2,1)S(1)}, u32[]{:S(2)}, u32[]{:S(2)}) collective-permute-start(bf16[4,2,80,256]{3,2,1,0:T(8,128)(2,1)S(1)} %collective-permute-done.21.refs_1_), channel_id=1, source_target_pairs={{0,1},{1,0},{2,3},{3,2},{4,5},{5,4},{6,7},{7,6},{8,9},{9,8},{10,11... | collective-permute-start | bytes 983048 | tf_op jit(solution)/shard_map/ppermute | solution.py:158
  57.2 1.7 %copy-start.1 = (bf16[4,2,80,256]{3,2,1,0:T(8,128)(2,1)}, bf16[4,2,80,256]{3,2,1,0:T(8,128)(2,1)S(1)}, u32[]{:S(2)}) copy-start(bf16[4,2,80,256]{3,2,1,0:T(8,128)(2,1)S(1)} %collective-permute-done.16.refs_1_) | copy-start | bytes 983044
  57.2 8.7 %collective-permute-start.18 = (bf16[4,2,80,256]{3,2,1,0:T(8,128)(2,1)S(1)}, bf16[4,2,80,256]{3,2,1,0:T(8,128)(2,1)}, u32[]{:S(2)}, u32[]{:S(2)}) collective-permute-start(bf16[4,2,80,256]{3,2,1,0:T(8,128)(2,1)S(1)} %collective-permute-done.16.refs_1_), channel_id=1, source_target_pairs={{0,1},{1,0},{2,3},{3,2},{4,5},{5,4},{6,7},{7,6},{8,9},{9,8},{10,11... | collective-permute-start | bytes 983048 | tf_op jit(solution)/shard_map/ppermute | solution.py:158
  57.2 11.4 %collective-permute-start.12 = (bf16[4,2,80,256]{3,2,1,0:T(8,128)(2,1)S(1)}, bf16[4,2,80,256]{3,2,1,0:T(8,128)(2,1)}, u32[]{:S(2)}, u32[]{:S(2)}) collective-permute-start(bf16[4,2,80,256]{3,2,1,0:T(8,128)(2,1)S(1)} %constant_dynamic-update-slice_fusion.2.refs_0_), channel_id=1, source_target_pairs={{0,1},{1,0},{2,3},{3,2},{4,5},{5,4},{6,7},{7,6},{8,9},{9,8},{10,11... | collective-permute-start | bytes 983048 | tf_op jit(solution)/shard_map/ppermute | solution.py:158
  57.7 10.9 %collective-permute-start.13 = (bf16[4,2,80,256]{3,2,1,0:T(8,128)(2,1)}, bf16[4,2,80,256]{3,2,1,0:T(8,128)(2,1)}, u32[]{:S(2)}, u32[]{:S(2)}) collective-permute-start(bf16[4,2,80,256]{3,2,1,0:T(8,128)(2,1)} %collective-permute-done.11.refs_1_), channel_id=1, source_target_pairs={{0,1},{1,0},{2,3},{3,2},{4,5},{5,4},{6,7},{7,6},{8,9},{9,8},{10,11... | collective-permute-start | bytes 983048 | tf_op jit(solution)/shard_map/ppermute | solution.py:158
  58.9 11.8 %all-to-all-start.1 = ((f32[32,4,128]{2,1,0:T(4,128)}), f32[32,4,128]{2,1,0:T(4,128)S(1)}, u32[]{:S(2)}, u32[]{:S(2)}) async-start(f32[32,4,128]{2,1,0:T(4,128)} %bitcast.4), calls=%async_computation.1 | async-start | bytes 131072 | tf_op jit(solution)/shard_map/all_to_all | solution.py:261
  62.6 3.3 %copy-start.2 = (bf16[4,2,80,256]{3,2,1,0:T(8,128)(2,1)S(1)}, bf16[4,2,80,256]{3,2,1,0:T(8,128)(2,1)}, u32[]{:S(2)}) copy-start(bf16[4,2,80,256]{3,2,1,0:T(8,128)(2,1)} %copy-done.1) | copy-start | bytes 983044
  62.6 0.7 copy-start.5
  63.3 1.0 %copy-start.6 = (bf16[4,2,80,256]{3,2,1,0:T(8,128)(2,1)S(1)}, bf16[4,2,80,256]{3,2,1,0:T(8,128)(2,1)}, u32[]{:S(2)}) copy-start(bf16[4,2,80,256]{3,2,1,0:T(8,128)(2,1)} %copy-done.5) | copy-start | bytes 983044
  64.4 0.7 copy-start.7
  65.1 0.7 copy-start.3
  65.9 1.0 %copy-start.4 = (bf16[4,2,80,256]{3,2,1,0:T(8,128)(2,1)S(1)}, bf16[4,2,80,256]{3,2,1,0:T(8,128)(2,1)}, u32[]{:S(2)}) copy-start(bf16[4,2,80,256]{3,2,1,0:T(8,128)(2,1)} %copy-done.3) | copy-start | bytes 983044
  67.9 0.7 copy-start.9
  69.9 0.7 copy-start.11
  70.6 0.7 copy-start.14
  71.3 0.9 %copy-start.8 = (bf16[2,256,256]{2,1,0:T(8,128)(2,1)S(1)}, bf16[2,256,256]{2,1,0:T(8,128)(2,1)}, u32[]{:S(2)}) copy-start(bf16[2,256,256]{2,1,0:T(8,128)(2,1)} %copy-done.7) | copy-start | bytes 786436
  72.2 0.9 %copy-start.10 = (bf16[2,256,256]{2,1,0:T(8,128)(2,1)S(1)}, bf16[2,256,256]{2,1,0:T(8,128)(2,1)}, u32[]{:S(2)}) copy-start(bf16[2,256,256]{2,1,0:T(8,128)(2,1)} %copy-done.9) | copy-start | bytes 786436
  73.2 0.9 %copy-start.12 = (bf16[2,256,256]{2,1,0:T(8,128)(2,1)S(1)}, bf16[2,256,256]{2,1,0:T(8,128)(2,1)}, u32[]{:S(2)}) copy-start(bf16[2,256,256]{2,1,0:T(8,128)(2,1)} %copy-done.11) | copy-start | bytes 786436

commit v21 on v17

--- a/solution.py
+++ b/solution.py
@@ -9,7 +9,7 @@
 
 GROUPS = 6
 COLOURS = 3
-CHAINS = ((0,), (1, 2))
+CHAINS = ((0, 1, 2),)
 HALF = 8
 SLICES = 2 * HALF
 VMEM = pl.BlockSpec(memory_space=pltpu.VMEM)
@@ -191,7 +191,6 @@
         cost_estimate=cost([slices]),
         name="pick",
     )(owners, slices)
-    others = [over_col(picked, m * HALF) for m in range(1, halves)]
 
     across = [merge_factor] + [over_col(merge_factor, m * share) for m in range(1, rows)]
 
@@ -205,7 +204,8 @@
         return block
 
     blocks = [for_row(0)] + [over_row(for_row(m), m) for m in range(1, rows)]
-    others, blocks = lax.optimization_barrier((others, blocks))
+    picked, blocks = lax.optimization_barrier((picked, blocks))
+    others = [over_col(picked, m * HALF) for m in range(1, halves)]
     groups = [range(rows // 2), range(rows // 2, rows)]
     sides = [jnp.stack([blocks[m] for m in group]) for group in groups]
     tags = [[(m, 0) for m in group] for group in groups]
@@ -221,6 +221,7 @@
         bit //= 2
     double(0, 2)
     double(1, 4)
+    others, sides = lax.optimization_barrier((others, sides))
     late = jnp.concatenate([over_col(sides[0], 4), over_col(sides[1], 2)])
     late_tags = [(m, c ^ 4) for m, c in tags[0]] + [(m, c ^ 2) for m, c in tags[1]]
     m_held = [jnp.concatenate(sides), late]
@@ -261,13 +262,13 @@
             colours[k] = jnp.concatenate([colours[k], send(colours[k])])
             masks[k] = masks[k] + [m ^ mask for m in masks[k]]
     state = lax.all_to_all(merged.reshape(rows * cols, each, width), ("row", "col"), 0, 0)
+    colours[0], state = lax.optimization_barrier((colours[0], state))
     last_round = []
     for k in range(COLOURS):
         mask, send = links[(k + 2) % 3]
         last_round.append(send(colours[k]))
         masks[k] = [masks[k], [m ^ mask for m in masks[k]]]
         masks[k] += [[m ^ 1 for m in ms] for ms in masks[k]]
-    last_round, state = lax.optimization_barrier((last_round, state))
     held = []
     for k in range(COLOURS):
         held.append([colours[k], last_round[k], over_col(colours[k], 1), over_col(last_round[k], 1)])

time: 68.3 us -> 79.4 us (1.16)
  waiting for transfers between devices: 27.3 us -> 37.5 us
  starting transfers between devices: 30.4 us -> 32 us
    ppermute x20, waiting for transfers between devices: 9.88 us -> 21.5 us  [over_col(): return lax.ppermute(x, 'col', [(c, c ^ mask) for c in range(cols)])]
    all_to_all x1, waiting for transfers between devices: 5.48 us -> 0.45 us  [local(): slices = lax.all_to_all(packed, 'col', 0, 0, axis_index_groups=members)]
    ppermute x4, waiting for transfers between devices: 6.94 us -> 10 us  [over_row(): return lax.ppermute(x, 'row', [(r, r ^ mask) for r in range(rows)])]
    ppermute x4, starting transfers between devices: 4.06 us -> 6.5 us  [over_row(): return lax.ppermute(x, 'row', [(r, r ^ mask) for r in range(rows)])]
    ppermute x20, starting transfers between devices: 17.1 us -> 16.2 us  [over_col(): return lax.ppermute(x, 'col', [(c, c ^ mask) for c in range(cols)])]
    pallas_call x2 -> x1, Pallas kernels: 5.68 us -> 5.08 us  [local(): pl.pallas_call(functools.partial(chain_kernel, cols, groups, slots, sum((...]
  transfers between devices with their start and end apart: 26 -> 26, of which waited for: 12 -> 11; matrix products, arithmetic and copies ran while one was open for 0% -> 0% of each run, Pallas kernels for 5% -> 3%
where the time goes in v21:
time: 79.4 us; the launch traced here: 79.1 us
  waiting for transfers between devices  37.5 us (47%)
  starting transfers between devices  32 us (40%)
  Pallas kernels  9.17 us (12%)
    ppermute x20, waiting for transfers between devices, over_col(): return lax.ppermute(x, 'col', [(c, c ^ mask) for c in range(cols)])  21.5 us
    ppermute x20, starting transfers between devices, over_col(): return lax.ppermute(x, 'col', [(c, c ^ mask) for c in range(cols)])  16.2 us
    ppermute x4, waiting for transfers between devices, over_row(): return lax.ppermute(x, 'row', [(r, r ^ mask) for r in range(rows)])  10 us
    ppermute x4, starting transfers between devices, over_row(): return lax.ppermute(x, 'row', [(r, r ^ mask) for r in range(rows)])  6.5 us
    all_to_all x1, waiting for transfers between devices, local(): lax.all_to_all(merged.reshape(rows * cols, each, width), ('row', 'col'),...  5.5 us
    all_to_all x1, starting transfers between devices, local(): slices = lax.all_to_all(packed, 'col', 0, 0, axis_index_groups=members)  5.4 us
    pallas_call x1, Pallas kernels, local(): pl.pallas_call(functools.partial(chain_kernel, cols, groups, slots, sum((...  5.08 us
    all_to_all x1, starting transfers between devices, local(): lax.all_to_all(merged.reshape(rows * cols, each, width), ('row', 'col'),...  3.92 us
  transfers between devices with their start and end apart: 26, of which 11 were waited for; matrix products, arithmetic and copies ran while one was open for 0% of the time, Pallas kernels for 3%

profile of v21, /device:TPU:0, one launch (start us, length us, event | category | flops | bytes accessed | tf_op | source)
XLA Modules:
  0.0 79.1 jit_solution(17612895861506446085)
XLA Ops:
  0.0 1.7 %pack.1 = bf16[8,80,256]{2,1,0:T(8,128)(2,1)} custom-call(bf16[16,64,256]{2,1,0:T(8,128)(2,1)} %bitcast.5, bf16[16,16,256]{2,1,0:T(8,128)(2,1)} %bitcast.8), custom_call_target="tpu_custom_call" | custom-call | bytes 655360 | tf_op jit(solution)/shard_map/pack/pallas_call | solution.py:171
  1.7 0.0 copy-start.3
  1.7 5.4 %all-to-all-start = ((bf16[8,80,256]{2,1,0:T(8,128)(2,1)}), bf16[8,80,256]{2,1,0:T(8,128)(2,1)S(1)}, u32[]{:S(2)}, u32[]{:S(2)}) async-start(bf16[8,80,256]{2,1,0:T(8,128)(2,1)} %pack.1), calls=%async_computation | async-start | bytes 655360 | tf_op jit(solution)/shard_map/all_to_all | solution.py:183
  7.1 2.7 %collective-permute-start = (bf16[64,512]{1,0:T(8,128)(2,1)S(1)}, bf16[64,512]{1,0:T(8,128)(2,1)S(1)}, u32[]{:S(2)}, u32[]{:S(2)}) collective-permute-start(bf16[64,512]{1,0:T(8,128)(2,1)S(1)} %copy-done.3), channel_id=1, source_target_pairs={{0,8},{1,9},{2,10},{3,11},{4,12},{5,13},{6,14},{7,15},{8,0},{9,1},... | collective-permute-start | bytes 196616 | tf_op jit(solution)/shard_map/ppermute | solution.py:160
  9.8 3.4 %collective-permute-done = bf16[64,512]{1,0:T(8,128)(2,1)S(1)} collective-permute-done((bf16[64,512]{1,0:T(8,128)(2,1)S(1)}, bf16[64,512]{1,0:T(8,128)(2,1)S(1)}, u32[]{:S(2)}, u32[]{:S(2)}) %collective-permute-start) | collective-permute-done | bytes 65568 | tf_op jit(solution)/shard_map/ppermute | solution.py:160
  13.2 0.0 copy-start.1
  13.3 1.6 %collective-permute-start.1 = (bf16[64,512]{1,0:T(8,128)(2,1)S(1)}, bf16[64,512]{1,0:T(8,128)(2,1)S(1)}, u32[]{:S(2)}, u32[]{:S(2)}) collective-permute-start(bf16[64,512]{1,0:T(8,128)(2,1)S(1)} %get-tuple-element.31), channel_id=1, source_target_pairs={{0,16},{16,0},{1,17},{17,1},{2,18},{18,2},{3,19},{19,3},{4,20},{20... | collective-permute-start | bytes 196616 | tf_op jit(solution)/shard_map/ppermute | solution.py:163
  14.8 0.4 all-to-all-done.held
  15.3 0.7 pick.1
  16.0 1.6 %collective-permute-done.1 = bf16[64,512]{1,0:T(8,128)(2,1)S(1)} collective-permute-done((bf16[64,512]{1,0:T(8,128)(2,1)S(1)}, bf16[64,512]{1,0:T(8,128)(2,1)S(1)}, u32[]{:S(2)}, u32[]{:S(2)}) %collective-permute-start.1) | collective-permute-done | bytes 65568 | tf_op jit(solution)/shard_map/ppermute | solution.py:163
  17.6 1.6 %collective-permute-start.3 = (bf16[1,64,512]{2,1,0:T(8,128)(2,1)S(1)}, bf16[1,64,512]{2,1,0:T(8,128)(2,1)S(1)}, u32[]{:S(2)}, u32[]{:S(2)}) collective-permute-start(bf16[1,64,512]{2,1,0:T(8,128)(2,1)S(1)} %bitcast.6), channel_id=1, source_target_pairs={{0,2},{1,3},{2,0},{3,1},{4,6},{5,7},{6,4},{7,5},{8,10},{9,11},{10,... | collective-permute-start | bytes 196616 | tf_op jit(solution)/shard_map/ppermute | solution.py:160
  19.2 4.5 %collective-permute-start.4 = (bf16[1,64,512]{2,1,0:T(8,128)(2,1)S(1)}, bf16[1,64,512]{2,1,0:T(8,128)(2,1)S(1)}, u32[]{:S(2)}, u32[]{:S(2)}) collective-permute-start(bf16[1,64,512]{2,1,0:T(8,128)(2,1)S(1)} %bitcast.9), channel_id=1, source_target_pairs={{0,4},{1,5},{2,6},{3,7},{4,0},{5,1},{6,2},{7,3},{8,12},{9,13},{10,... | collective-permute-start | bytes 196616 | tf_op jit(solution)/shard_map/ppermute | solution.py:160
  23.7 0.0 collective-permute-start.2
  23.7 0.0 collective-permute-done.3
  23.8 2.5 %collective-permute-done.4 = bf16[1,64,512]{2,1,0:T(8,128)(2,1)S(1)} collective-permute-done((bf16[1,64,512]{2,1,0:T(8,128)(2,1)S(1)}, bf16[1,64,512]{2,1,0:T(8,128)(2,1)S(1)}, u32[]{:S(2)}, u32[]{:S(2)}) %collective-permute-start.4) | collective-permute-done | bytes 65568 | tf_op jit(solution)/shard_map/ppermute | solution.py:160
  26.3 7.4 %collective-permute-done.2.refs_0_ = bf16[5,80,256]{2,1,0:T(8,128)(2,1)S(1)} collective-permute-done((bf16[5,80,256]{2,1,0:T(8,128)(2,1)S(1)}, bf16[5,80,256]{2,1,0:T(8,128)(2,1)S(1)}, u32[]{:S(2)}, u32[]{:S(2)}) %collective-permute-start.2) | collective-permute-done | bytes 204832 | tf_op jit(solution)/shard_map/ppermute | solution.py:160
  33.6 0.0 collective-permute-start.7
  33.7 0.6 order.1
  34.3 0.6 collective-permute-start.14
  34.9 2.0 %collective-permute-start.19 = (bf16[1,2,80,256]{3,2,1,0:T(8,128)(2,1)S(1)}, bf16[1,2,80,256]{3,2,1,0:T(8,128)(2,1)S(1)}, u32[]{:S(2)}, u32[]{:S(2)}) collective-permute-start(bf16[1,2,80,256]{3,2,1,0:T(8,128)(2,1)S(1)} %get-tuple-element.30), channel_id=1, source_target_pairs={{0,4},{1,5},{2,6},{3,7},{4,0},{5,1},{6,2},{7,3},{8,12},{9,13},{10,... | collective-permute-start | bytes 245768 | tf_op jit(solution)/shard_map/ppermute | solution.py:160
  36.9 1.6 %collective-permute-start.5 = (bf16[1,2,80,256]{3,2,1,0:T(8,128)(2,1)S(1)}, bf16[1,2,80,256]{3,2,1,0:T(8,128)(2,1)S(1)}, u32[]{:S(2)}, u32[]{:S(2)}) collective-permute-start(bf16[1,2,80,256]{3,2,1,0:T(8,128)(2,1)S(1)} %get-tuple-element.24), channel_id=1, source_target_pairs={{0,16},{16,0},{1,17},{17,1},{2,18},{18,2},{3,19},{19,3},{4,20},{20... | collective-permute-start | bytes 245768 | tf_op jit(solution)/shard_map/ppermute | solution.py:163
  38.5 1.5 %collective-permute-start.8 = (bf16[2,64,512]{2,1,0:T(8,128)(2,1)S(1)}, bf16[2,64,512]{2,1,0:T(8,128)(2,1)S(1)}, u32[]{:S(2)}, u32[]{:S(2)}) collective-permute-start(bf16[2,64,512]{2,1,0:T(8,128)(2,1)S(1)} %pad_maximum_fusion.5), channel_id=1, source_target_pairs={{0,2},{1,3},{2,0},{3,1},{4,6},{5,7},{6,4},{7,5},{8,10},{9,11},{10,... | collective-permute-start | bytes 393224 | tf_op jit(solution)/shard_map/ppermute | solution.py:160
  40.0 0.0 copy-start
  40.0 1.5 %collective-permute-done.5 = bf16[1,2,80,256]{3,2,1,0:T(8,128)(2,1)S(1)} collective-permute-done((bf16[1,2,80,256]{3,2,1,0:T(8,128)(2,1)S(1)}, bf16[1,2,80,256]{3,2,1,0:T(8,128)(2,1)S(1)}, u32[]{:S(2)}, u32[]{:S(2)}) %collective-permute-start.5) | collective-permute-done | bytes 81952 | tf_op jit(solution)/shard_map/ppermute | solution.py:163
  41.5 0.0 collective-permute-start.9
  41.5 1.5 %collective-permute-start.6 = (bf16[2,2,80,256]{3,2,1,0:T(8,128)(2,1)S(1)}, bf16[2,2,80,256]{3,2,1,0:T(8,128)(2,1)S(1)}, u32[]{:S(2)}, u32[]{:S(2)}) collective-permute-start(bf16[2,2,80,256]{3,2,1,0:T(8,128)(2,1)S(1)} %pad_maximum_fusion.1), channel_id=1, source_target_pairs={{0,2},{1,3},{2,0},{3,1},{4,6},{5,7},{6,4},{7,5},{8,10},{9,11},{10,... | collective-permute-start | bytes 491528 | tf_op jit(solution)/shard_map/ppermute | solution.py:160
  43.0 0.1 collective-permute-start.15
  43.2 0.0 collective-permute-done.7
  43.2 1.6 %collective-permute-start.20 = (bf16[2,2,80,256]{3,2,1,0:T(8,128)(2,1)S(1)}, bf16[2,2,80,256]{3,2,1,0:T(8,128)(2,1)S(1)}, u32[]{:S(2)}, u32[]{:S(2)}) collective-permute-start(bf16[2,2,80,256]{3,2,1,0:T(8,128)(2,1)S(1)} %pad_maximum_fusion.3), channel_id=1, source_target_pairs={{0,16},{16,0},{1,17},{17,1},{2,18},{18,2},{3,19},{19,3},{4,20},{20... | collective-permute-start | bytes 491528 | tf_op jit(solution)/shard_map/ppermute | solution.py:163
  44.7 0.0 collective-permute-done.8
  44.8 0.1 collective-permute-start.10
  44.9 4.7 %collective-permute-done.20 = bf16[2,2,80,256]{3,2,1,0:T(8,128)(2,1)S(1)} collective-permute-done((bf16[2,2,80,256]{3,2,1,0:T(8,128)(2,1)S(1)}, bf16[2,2,80,256]{3,2,1,0:T(8,128)(2,1)S(1)}, u32[]{:S(2)}, u32[]{:S(2)}) %collective-permute-start.20) | collective-permute-done | bytes 163872 | tf_op jit(solution)/shard_map/ppermute | solution.py:163
  49.6 0.1 collective-permute-start.22
  49.7 0.0 collective-permute-done.9.refs_2_
  49.7 0.6 collective-permute-start.21
  50.3 0.0 collective-permute-done.10.refs_3_
  50.3 1.1 %merge.1 = f32[128,128]{1,0:T(8,128)} custom-call(bf16[4096,128]{1,0:T(8,128)(2,1)S(1)} %copy-done, bf16[4,64,512]{2,1,0:T(8,128)(2,1)S(1)} %constant_dynamic-update-slice_fusion.refs_0_, bf16[4,64,512]{2,1,0:T(8,128)(2,1)S(1)} %constant_dynamic-update-slice_fusion.2.refs_1_, bf16[4,64,512]{2,1,0:T(8,128)(2,1)S(1)} %collective-permute-done.9.refs_2_, ...), custom_call_target="tpu_custom_call" | custom-call | flops 134217728 | bytes 1048576 | tf_op jit(solution)/shard_map/merge/pallas_call | solution.py:233
  51.4 3.9 %all-to-all-start.1 = ((f32[32,4,128]{2,1,0:T(4,128)}), f32[32,4,128]{2,1,0:T(4,128)S(1)}, u32[]{:S(2)}, u32[]{:S(2)}) async-start(f32[32,4,128]{2,1,0:T(4,128)} %bitcast.4), calls=%async_computation.1 | async-start | bytes 131072 | tf_op jit(solution)/shard_map/all_to_all | solution.py:264
  55.3 0.0 copy-start.2
  55.3 1.8 %collective-permute-start.16 = (bf16[4,2,80,256]{3,2,1,0:T(8,128)(2,1)S(1)}, bf16[4,2,80,256]{3,2,1,0:T(8,128)(2,1)S(1)}, u32[]{:S(2)}, u32[]{:S(2)}) collective-permute-start(bf16[4,2,80,256]{3,2,1,0:T(8,128)(2,1)S(1)} %constant_dynamic-update-slice_fusion.4.refs_4_), channel_id=1, source_target_pairs={{0,16},{16,0},{1,17},{17,1},{2,18},{18,2},{3,19},{19,3},{4,20},{20... | collective-permute-start | bytes 983048 | tf_op jit(solution)/shard_map/ppermute | solution.py:163
  57.2 5.5 %all-to-all-done.1.start = f32[32,4,128]{2,1,0:T(4,128)S(1)} async-done(((f32[32,4,128]{2,1,0:T(4,128)}), f32[32,4,128]{2,1,0:T(4,128)S(1)}, u32[]{:S(2)}, u32[]{:S(2)}) %all-to-all-start.1) | async-done | bytes 65568 | tf_op jit(solution)/shard_map/all_to_all | solution.py:264
  62.7 0.3 collective-permute-start.11
  63.1 0.5 collective-permute-start.12
  63.6 0.1 collective-permute-start.23
  63.6 2.3 %collective-permute-done.16.refs_5_ = bf16[4,2,80,256]{3,2,1,0:T(8,128)(2,1)S(1)} collective-permute-done((bf16[4,2,80,256]{3,2,1,0:T(8,128)(2,1)S(1)}, bf16[4,2,80,256]{3,2,1,0:T(8,128)(2,1)S(1)}, u32[]{:S(2)}, u32[]{:S(2)}) %collective-permute-start.16) | collective-permute-done | bytes 327712 | tf_op jit(solution)/shard_map/ppermute | solution.py:163
  65.9 6.5 %collective-permute-done.11.refs_1_ = bf16[4,2,80,256]{3,2,1,0:T(8,128)(2,1)S(1)} collective-permute-done((bf16[4,2,80,256]{3,2,1,0:T(8,128)(2,1)S(1)}, bf16[4,2,80,256]{3,2,1,0:T(8,128)(2,1)S(1)}, u32[]{:S(2)}, u32[]{:S(2)}) %collective-permute-start.11) | collective-permute-done | bytes 327712 | tf_op jit(solution)/shard_map/ppermute | solution.py:160
  72.5 1.6 %collective-permute-done.13.refs_3_ = bf16[4,2,80,256]{3,2,1,0:T(8,128)(2,1)S(1)} collective-permute-done((bf16[4,2,80,256]{3,2,1,0:T(8,128)(2,1)S(1)}, bf16[4,2,80,256]{3,2,1,0:T(8,128)(2,1)S(1)}, u32[]{:S(2)}, u32[]{:S(2)}) %collective-permute-start.13) | collective-permute-done | bytes 327712 | tf_op jit(solution)/shard_map/ppermute | solution.py:160
  74.1 5.1 %chain0.1 = bf16[4,2048]{1,0:T(4,128)(2,1)} custom-call(s32[6]{0:T(128)S(1)} %copy-done.2, f32[32,4,128]{2,1,0:T(4,128)S(1)} %all-to-all-done.1.start, bf16[4,2,80,256]{3,2,1,0:T(8,128)(2,1)S(1)} %pad_maximum_fusion.refs_0_, bf16[4,2,80,256]{3,2,1,0:T(8,128)(2,1)S(1)} %collective-permute-done.11.refs_1_, ...), custom_call_target="tpu_custom_call" | custom-call | flops 201326592 | bytes 3932160 | tf_op jit(solution)/shard_map/chain0/pallas_call | solution.py:282
  (33 shorter events, 0.3 us)
Async XLA Ops:
  1.7 5.4 %copy-start.3 = (bf16[64,512]{1,0:T(8,128)(2,1)S(1)}, bf16[64,512]{1,0:T(8,128)(2,1)}, u32[]{:S(2)}) copy-start(bf16[64,512]{1,0:T(8,128)(2,1)} %param.7) | copy-start | bytes 196612
  1.7 13.5 %all-to-all-start = ((bf16[8,80,256]{2,1,0:T(8,128)(2,1)}), bf16[8,80,256]{2,1,0:T(8,128)(2,1)S(1)}, u32[]{:S(2)}, u32[]{:S(2)}) async-start(bf16[8,80,256]{2,1,0:T(8,128)(2,1)} %pack.1), calls=%async_computation | async-start | bytes 655360 | tf_op jit(solution)/shard_map/all_to_all | solution.py:183
  7.1 6.1 %collective-permute-start = (bf16[64,512]{1,0:T(8,128)(2,1)S(1)}, bf16[64,512]{1,0:T(8,128)(2,1)S(1)}, u32[]{:S(2)}, u32[]{:S(2)}) collective-permute-start(bf16[64,512]{1,0:T(8,128)(2,1)S(1)} %copy-done.3), channel_id=1, source_target_pairs={{0,8},{1,9},{2,10},{3,11},{4,12},{5,13},{6,14},{7,15},{8,0},{9,1},... | collective-permute-start | bytes 196616 | tf_op jit(solution)/shard_map/ppermute | solution.py:160
  13.2 2.0 %copy-start.1 = (s32[6]{0:T(128)S(1)}, s32[6]{0:T(128)}, u32[]{:S(2)}) copy-start(s32[6]{0:T(128)} %owners.3) | copy-start | bytes 76
  13.3 4.3 %collective-permute-start.1 = (bf16[64,512]{1,0:T(8,128)(2,1)S(1)}, bf16[64,512]{1,0:T(8,128)(2,1)S(1)}, u32[]{:S(2)}, u32[]{:S(2)}) collective-permute-start(bf16[64,512]{1,0:T(8,128)(2,1)S(1)} %get-tuple-element.31), channel_id=1, source_target_pairs={{0,16},{16,0},{1,17},{17,1},{2,18},{18,2},{3,19},{19,3},{4,20},{20... | collective-permute-start | bytes 196616 | tf_op jit(solution)/shard_map/ppermute | solution.py:163
  17.6 6.1 %collective-permute-start.3 = (bf16[1,64,512]{2,1,0:T(8,128)(2,1)S(1)}, bf16[1,64,512]{2,1,0:T(8,128)(2,1)S(1)}, u32[]{:S(2)}, u32[]{:S(2)}) collective-permute-start(bf16[1,64,512]{2,1,0:T(8,128)(2,1)S(1)} %bitcast.6), channel_id=1, source_target_pairs={{0,2},{1,3},{2,0},{3,1},{4,6},{5,7},{6,4},{7,5},{8,10},{9,11},{10,... | collective-permute-start | bytes 196616 | tf_op jit(solution)/shard_map/ppermute | solution.py:160
  19.2 7.1 %collective-permute-start.4 = (bf16[1,64,512]{2,1,0:T(8,128)(2,1)S(1)}, bf16[1,64,512]{2,1,0:T(8,128)(2,1)S(1)}, u32[]{:S(2)}, u32[]{:S(2)}) collective-permute-start(bf16[1,64,512]{2,1,0:T(8,128)(2,1)S(1)} %bitcast.9), channel_id=1, source_target_pairs={{0,4},{1,5},{2,6},{3,7},{4,0},{5,1},{6,2},{7,3},{8,12},{9,13},{10,... | collective-permute-start | bytes 196616 | tf_op jit(solution)/shard_map/ppermute | solution.py:160
  23.7 9.9 %collective-permute-start.2 = (bf16[5,80,256]{2,1,0:T(8,128)(2,1)S(1)}, bf16[5,80,256]{2,1,0:T(8,128)(2,1)S(1)}, u32[]{:S(2)}, u32[]{:S(2)}) collective-permute-start(bf16[5,80,256]{2,1,0:T(8,128)(2,1)S(1)} %pick.1), channel_id=1, source_target_pairs={{0,8},{1,9},{2,10},{3,11},{4,12},{5,13},{6,14},{7,15},{8,0},{9,1},... | collective-permute-start | bytes 614408 | tf_op jit(solution)/shard_map/ppermute | solution.py:160
  33.6 9.5 %collective-permute-start.7 = (bf16[2,64,512]{2,1,0:T(8,128)(2,1)S(1)}, bf16[2,64,512]{2,1,0:T(8,128)(2,1)S(1)}, u32[]{:S(2)}, u32[]{:S(2)}) collective-permute-start(bf16[2,64,512]{2,1,0:T(8,128)(2,1)S(1)} %pad_maximum_fusion.4), channel_id=1, source_target_pairs={{0,4},{1,5},{2,6},{3,7},{4,0},{5,1},{6,2},{7,3},{8,12},{9,13},{10,... | collective-permute-start | bytes 393224 | tf_op jit(solution)/shard_map/ppermute | solution.py:160
  34.3 7.2 %collective-permute-start.14 = (bf16[1,2,80,256]{3,2,1,0:T(8,128)(2,1)S(1)}, bf16[1,2,80,256]{3,2,1,0:T(8,128)(2,1)S(1)}, u32[]{:S(2)}, u32[]{:S(2)}) collective-permute-start(bf16[1,2,80,256]{3,2,1,0:T(8,128)(2,1)S(1)} %get-tuple-element.29), channel_id=1, source_target_pairs={{0,2},{1,3},{2,0},{3,1},{4,6},{5,7},{6,4},{7,5},{8,10},{9,11},{10,... | collective-permute-start | bytes 245768 | tf_op jit(solution)/shard_map/ppermute | solution.py:160
  34.9 8.1 %collective-permute-start.19 = (bf16[1,2,80,256]{3,2,1,0:T(8,128)(2,1)S(1)}, bf16[1,2,80,256]{3,2,1,0:T(8,128)(2,1)S(1)}, u32[]{:S(2)}, u32[]{:S(2)}) collective-permute-start(bf16[1,2,80,256]{3,2,1,0:T(8,128)(2,1)S(1)} %get-tuple-element.30), channel_id=1, source_target_pairs={{0,4},{1,5},{2,6},{3,7},{4,0},{5,1},{6,2},{7,3},{8,12},{9,13},{10,... | collective-permute-start | bytes 245768 | tf_op jit(solution)/shard_map/ppermute | solution.py:160
  36.9 4.5 %collective-permute-start.5 = (bf16[1,2,80,256]{3,2,1,0:T(8,128)(2,1)S(1)}, bf16[1,2,80,256]{3,2,1,0:T(8,128)(2,1)S(1)}, u32[]{:S(2)}, u32[]{:S(2)}) collective-permute-start(bf16[1,2,80,256]{3,2,1,0:T(8,128)(2,1)S(1)} %get-tuple-element.24), channel_id=1, source_target_pairs={{0,16},{16,0},{1,17},{17,1},{2,18},{18,2},{3,19},{19,3},{4,20},{20... | collective-permute-start | bytes 245768 | tf_op jit(solution)/shard_map/ppermute | solution.py:163
  38.5 6.2 %collective-permute-start.8 = (bf16[2,64,512]{2,1,0:T(8,128)(2,1)S(1)}, bf16[2,64,512]{2,1,0:T(8,128)(2,1)S(1)}, u32[]{:S(2)}, u32[]{:S(2)}) collective-permute-start(bf16[2,64,512]{2,1,0:T(8,128)(2,1)S(1)} %pad_maximum_fusion.5), channel_id=1, source_target_pairs={{0,2},{1,3},{2,0},{3,1},{4,6},{5,7},{6,4},{7,5},{8,10},{9,11},{10,... | collective-permute-start | bytes 393224 | tf_op jit(solution)/shard_map/ppermute | solution.py:160
  40.0 10.3 %copy-start = (bf16[4096,128]{1,0:T(8,128)(2,1)S(1)}, bf16[4096,128]{1,0:T(8,128)(2,1)}, u32[]{:S(2)}) copy-start(bf16[4096,128]{1,0:T(8,128)(2,1)} %sub.6) | copy-start | bytes 3145732
  41.5 8.2 %collective-permute-start.9 = (bf16[4,64,512]{2,1,0:T(8,128)(2,1)S(1)}, bf16[4,64,512]{2,1,0:T(8,128)(2,1)S(1)}, u32[]{:S(2)}, u32[]{:S(2)}) collective-permute-start(bf16[4,64,512]{2,1,0:T(8,128)(2,1)S(1)} %constant_dynamic-update-slice_fusion.refs_0_), channel_id=1, source_target_pairs={{0,1},{1,0},{2,3},{3,2},{4,5},{5,4},{6,7},{7,6},{8,9},{9,8},{10,11... | collective-permute-start | bytes 786440 | tf_op jit(solution)/shard_map/ppermute | solution.py:160
  41.5 15.7 %collective-permute-start.6 = (bf16[2,2,80,256]{3,2,1,0:T(8,128)(2,1)S(1)}, bf16[2,2,80,256]{3,2,1,0:T(8,128)(2,1)S(1)}, u32[]{:S(2)}, u32[]{:S(2)}) collective-permute-start(bf16[2,2,80,256]{3,2,1,0:T(8,128)(2,1)S(1)} %pad_maximum_fusion.1), channel_id=1, source_target_pairs={{0,2},{1,3},{2,0},{3,1},{4,6},{5,7},{6,4},{7,5},{8,10},{9,11},{10,... | collective-permute-start | bytes 491528 | tf_op jit(solution)/shard_map/ppermute | solution.py:160
  43.0 12.2 %collective-permute-start.15 = (bf16[2,2,80,256]{3,2,1,0:T(8,128)(2,1)S(1)}, bf16[2,2,80,256]{3,2,1,0:T(8,128)(2,1)S(1)}, u32[]{:S(2)}, u32[]{:S(2)}) collective-permute-start(bf16[2,2,80,256]{3,2,1,0:T(8,128)(2,1)S(1)} %pad_maximum_fusion.2), channel_id=1, source_target_pairs={{0,4},{1,5},{2,6},{3,7},{4,0},{5,1},{6,2},{7,3},{8,12},{9,13},{10,... | collective-permute-start | bytes 491528 | tf_op jit(solution)/shard_map/ppermute | solution.py:160
  43.2 6.4 %collective-permute-start.20 = (bf16[2,2,80,256]{3,2,1,0:T(8,128)(2,1)S(1)}, bf16[2,2,80,256]{3,2,1,0:T(8,128)(2,1)S(1)}, u32[]{:S(2)}, u32[]{:S(2)}) collective-permute-start(bf16[2,2,80,256]{3,2,1,0:T(8,128)(2,1)S(1)} %pad_maximum_fusion.3), channel_id=1, source_target_pairs={{0,16},{16,0},{1,17},{17,1},{2,18},{18,2},{3,19},{19,3},{4,20},{20... | collective-permute-start | bytes 491528 | tf_op jit(solution)/shard_map/ppermute | solution.py:163
  44.8 5.5 %collective-permute-start.10 = (bf16[4,64,512]{2,1,0:T(8,128)(2,1)S(1)}, bf16[4,64,512]{2,1,0:T(8,128)(2,1)S(1)}, u32[]{:S(2)}, u32[]{:S(2)}) collective-permute-start(bf16[4,64,512]{2,1,0:T(8,128)(2,1)S(1)} %constant_dynamic-update-slice_fusion.2.refs_1_), channel_id=1, source_target_pairs={{0,1},{1,0},{2,3},{3,2},{4,5},{5,4},{6,7},{7,6},{8,9},{9,8},{10,11... | collective-permute-start | bytes 786440 | tf_op jit(solution)/shard_map/ppermute | solution.py:160
  49.6 13.5 %collective-permute-start.22 = (bf16[4,2,80,256]{3,2,1,0:T(8,128)(2,1)S(1)}, bf16[4,2,80,256]{3,2,1,0:T(8,128)(2,1)S(1)}, u32[]{:S(2)}, u32[]{:S(2)}) collective-permute-start(bf16[4,2,80,256]{3,2,1,0:T(8,128)(2,1)S(1)} %constant_dynamic-update-slice_fusion.7.refs_8_), channel_id=1, source_target_pairs={{0,1},{1,0},{2,3},{3,2},{4,5},{5,4},{6,7},{7,6},{8,9},{9,8},{10,11... | collective-permute-start | bytes 983048 | tf_op jit(solution)/shard_map/ppermute | solution.py:160
  49.7 13.9 %collective-permute-start.21 = (bf16[4,2,80,256]{3,2,1,0:T(8,128)(2,1)S(1)}, bf16[4,2,80,256]{3,2,1,0:T(8,128)(2,1)S(1)}, u32[]{:S(2)}, u32[]{:S(2)}) collective-permute-start(bf16[4,2,80,256]{3,2,1,0:T(8,128)(2,1)S(1)} %constant_dynamic-update-slice_fusion.7.refs_8_), channel_id=1, source_target_pairs={{0,2},{1,3},{2,0},{3,1},{4,6},{5,7},{6,4},{7,5},{8,10},{9,11},{10,... | collective-permute-start | bytes 983048 | tf_op jit(solution)/shard_map/ppermute | solution.py:160
  51.4 11.3 %all-to-all-start.1 = ((f32[32,4,128]{2,1,0:T(4,128)}), f32[32,4,128]{2,1,0:T(4,128)S(1)}, u32[]{:S(2)}, u32[]{:S(2)}) async-start(f32[32,4,128]{2,1,0:T(4,128)} %bitcast.4), calls=%async_computation.1 | async-start | bytes 131072 | tf_op jit(solution)/shard_map/all_to_all | solution.py:264
  55.3 18.7 %copy-start.2 = (s32[6]{0:T(128)S(1)}, s32[6]{0:T(128)}, u32[]{:S(2)}) copy-start(s32[6]{0:T(128)} %offsets.1) | copy-start | bytes 76
  55.3 10.6 %collective-permute-start.16 = (bf16[4,2,80,256]{3,2,1,0:T(8,128)(2,1)S(1)}, bf16[4,2,80,256]{3,2,1,0:T(8,128)(2,1)S(1)}, u32[]{:S(2)}, u32[]{:S(2)}) collective-permute-start(bf16[4,2,80,256]{3,2,1,0:T(8,128)(2,1)S(1)} %constant_dynamic-update-slice_fusion.4.refs_4_), channel_id=1, source_target_pairs={{0,16},{16,0},{1,17},{17,1},{2,18},{18,2},{3,19},{19,3},{4,20},{20... | collective-permute-start | bytes 983048 | tf_op jit(solution)/shard_map/ppermute | solution.py:163
  62.7 9.7 %collective-permute-start.11 = (bf16[4,2,80,256]{3,2,1,0:T(8,128)(2,1)S(1)}, bf16[4,2,80,256]{3,2,1,0:T(8,128)(2,1)S(1)}, u32[]{:S(2)}, u32[]{:S(2)}) collective-permute-start(bf16[4,2,80,256]{3,2,1,0:T(8,128)(2,1)S(1)} %pad_maximum_fusion.refs_0_), channel_id=1, source_target_pairs={{0,4},{1,5},{2,6},{3,7},{4,0},{5,1},{6,2},{7,3},{8,12},{9,13},{10,... | collective-permute-start | bytes 983048 | tf_op jit(solution)/shard_map/ppermute | solution.py:160
  63.1 9.4 %collective-permute-start.17 = (bf16[4,2,80,256]{3,2,1,0:T(8,128)(2,1)S(1)}, bf16[4,2,80,256]{3,2,1,0:T(8,128)(2,1)S(1)}, u32[]{:S(2)}, u32[]{:S(2)}) collective-permute-start(bf16[4,2,80,256]{3,2,1,0:T(8,128)(2,1)S(1)} %constant_dynamic-update-slice_fusion.4.refs_4_), channel_id=1, source_target_pairs={{0,1},{1,0},{2,3},{3,2},{4,5},{5,4},{6,7},{7,6},{8,9},{9,8},{10,11... | collective-permute-start | bytes 983048 | tf_op jit(solution)/shard_map/ppermute | solution.py:160
  63.1 9.4 %collective-permute-start.12 = (bf16[4,2,80,256]{3,2,1,0:T(8,128)(2,1)S(1)}, bf16[4,2,80,256]{3,2,1,0:T(8,128)(2,1)S(1)}, u32[]{:S(2)}, u32[]{:S(2)}) collective-permute-start(bf16[4,2,80,256]{3,2,1,0:T(8,128)(2,1)S(1)} %pad_maximum_fusion.refs_0_), channel_id=1, source_target_pairs={{0,1},{1,0},{2,3},{3,2},{4,5},{5,4},{6,7},{7,6},{8,9},{9,8},{10,11... | collective-permute-start | bytes 983048 | tf_op jit(solution)/shard_map/ppermute | solution.py:160
  63.6 8.9 %collective-permute-start.23 = (bf16[4,2,80,256]{3,2,1,0:T(8,128)(2,1)S(1)}, bf16[4,2,80,256]{3,2,1,0:T(8,128)(2,1)S(1)}, u32[]{:S(2)}, u32[]{:S(2)}) collective-permute-start(bf16[4,2,80,256]{3,2,1,0:T(8,128)(2,1)S(1)} %collective-permute-done.21.refs_9_), channel_id=1, source_target_pairs={{0,1},{1,0},{2,3},{3,2},{4,5},{5,4},{6,7},{7,6},{8,9},{9,8},{10,11... | collective-permute-start | bytes 983048 | tf_op jit(solution)/shard_map/ppermute | solution.py:160
  65.9 6.5 %collective-permute-start.18 = (bf16[4,2,80,256]{3,2,1,0:T(8,128)(2,1)S(1)}, bf16[4,2,80,256]{3,2,1,0:T(8,128)(2,1)S(1)}, u32[]{:S(2)}, u32[]{:S(2)}) collective-permute-start(bf16[4,2,80,256]{3,2,1,0:T(8,128)(2,1)S(1)} %collective-permute-done.16.refs_5_), channel_id=1, source_target_pairs={{0,1},{1,0},{2,3},{3,2},{4,5},{5,4},{6,7},{7,6},{8,9},{9,8},{10,11... | collective-permute-start | bytes 983048 | tf_op jit(solution)/shard_map/ppermute | solution.py:160
  72.4 1.6 %collective-permute-start.13 = (bf16[4,2,80,256]{3,2,1,0:T(8,128)(2,1)S(1)}, bf16[4,2,80,256]{3,2,1,0:T(8,128)(2,1)S(1)}, u32[]{:S(2)}, u32[]{:S(2)}) collective-permute-start(bf16[4,2,80,256]{3,2,1,0:T(8,128)(2,1)S(1)} %collective-permute-done.11.refs_1_), channel_id=1, source_target_pairs={{0,1},{1,0},{2,3},{3,2},{4,5},{5,4},{6,7},{7,6},{8,9},{9,8},{10,11... | collective-permute-start | bytes 983048 | tf_op jit(solution)/shard_map/ppermute | solution.py:160

commit v22 on v17

--- a/solution.py
+++ b/solution.py
@@ -9,7 +9,8 @@
 
 GROUPS = 6
 COLOURS = 3
-CHAINS = ((0,), (1, 2))
+CHAINS = ((0, 1, 2),)
+HEAD = 16
 HALF = 8
 SLICES = 2 * HALF
 VMEM = pl.BlockSpec(memory_space=pltpu.VMEM)
@@ -74,8 +75,13 @@
     for group in range(GROUPS):
         half, rank = places(owners, group)
         piece = held[lax.rem(owners[group], HALF)]
-        for mask, ref in enumerate(others, 1):
-            other = ref[jnp.minimum(rank, ref.shape[0] - 1)]
+        tall = piece.shape[0]
+        for mask in range(1, len(others) // 2 + 1):
+            head, tail = others[2 * mask - 2 : 2 * mask]
+            at = jnp.clip(rank * tall - HEAD, 0, tail.shape[0] - tall)
+            other = tail[pl.ds(pl.multiple_of(at, HEAD), tall), :]
+            first = jnp.concatenate([head[...], tail[: tall - HEAD, :]], 0)
+            other = jnp.where(rank == 0, first, other)
             piece = jnp.where(jnp.bitwise_xor(half, mine) == mask, other, piece)
         outs[group // each][0, group % each] = piece
 
@@ -191,7 +197,9 @@
         cost_estimate=cost([slices]),
         name="pick",
     )(owners, slices)
-    others = [over_col(picked, m * HALF) for m in range(1, halves)]
+    picked = picked.reshape(-1, reflect)
+    heads = [over_col(picked[:HEAD], m * HALF) for m in range(1, halves)]
+    tails = [over_col(picked[HEAD:], m * HALF) for m in range(1, halves)]
 
     across = [merge_factor] + [over_col(merge_factor, m * share) for m in range(1, rows)]
 
@@ -205,7 +213,8 @@
         return block
 
     blocks = [for_row(0)] + [over_row(for_row(m), m) for m in range(1, rows)]
-    others, blocks = lax.optimization_barrier((others, blocks))
+    heads, blocks = lax.optimization_barrier((heads, blocks))
+    others = [x for pair in zip(heads, tails) for x in pair]
     groups = [range(rows // 2), range(rows // 2, rows)]
     sides = [jnp.stack([blocks[m] for m in group]) for group in groups]
     tags = [[(m, 0) for m in group] for group in groups]

time: 68.3 us -> 70.4 us (1.031)
  starting transfers between devices: 30.4 us -> 39 us
  waiting for transfers between devices: 27.3 us -> 21.4 us
    ppermute x20 -> x21, starting transfers between devices: 17.1 us -> 24 us  [over_col(): return lax.ppermute(x, 'col', [(c, c ^ mask) for c in range(cols)])]
    all_to_all x1, waiting for transfers between devices: 5.48 us -> 0.45 us  [local(): slices = lax.all_to_all(packed, 'col', 0, 0, axis_index_groups=members)]
    all_to_all x1, waiting for transfers between devices: 5.03 us -> 6.83 us  [local(): lax.all_to_all(merged.reshape(rows * cols, each, width), ('row', 'col'),...]
    ppermute x4, waiting for transfers between devices: 6.94 us -> 5.53 us  [over_row(): return lax.ppermute(x, 'row', [(r, r ^ mask) for r in range(rows)])]
    ppermute x20 -> x21, waiting for transfers between devices: 9.88 us -> 8.62 us  [over_col(): return lax.ppermute(x, 'col', [(c, c ^ mask) for c in range(cols)])]
    all_to_all x1, starting transfers between devices: 3.89 us -> 4.78 us  [local(): lax.all_to_all(merged.reshape(rows * cols, each, width), ('row', 'col'),...]
    ppermute x4, starting transfers between devices: 4.06 us -> 4.86 us  [over_row(): return lax.ppermute(x, 'row', [(r, r ^ mask) for r in range(rows)])]
    pallas_call x2 -> x1, Pallas kernels: 5.68 us -> 5.08 us  [local(): pl.pallas_call(functools.partial(chain_kernel, cols, groups, slots, sum((...]
  transfers between devices with their start and end apart: 26 -> 27, of which waited for: 12 -> 11; matrix products, arithmetic and copies ran while one was open for 0% -> 0% of each run, Pallas kernels for 5% -> 3%
where the time goes in v22:
time: 70.4 us; the launch traced here: 70.1 us
  starting transfers between devices  39 us (55%)
  waiting for transfers between devices  21.4 us (30%)
  Pallas kernels  9.2 us (13%)
    ppermute x21, starting transfers between devices, over_col(): return lax.ppermute(x, 'col', [(c, c ^ mask) for c in range(cols)])  24 us
    ppermute x21, waiting for transfers between devices, over_col(): return lax.ppermute(x, 'col', [(c, c ^ mask) for c in range(cols)])  8.62 us
    all_to_all x1, waiting for transfers between devices, local(): lax.all_to_all(merged.reshape(rows * cols, each, width), ('row', 'col'),...  6.83 us
    ppermute x4, waiting for transfers between devices, over_row(): return lax.ppermute(x, 'row', [(r, r ^ mask) for r in range(rows)])  5.53 us
    all_to_all x1, starting transfers between devices, local(): slices = lax.all_to_all(packed, 'col', 0, 0, axis_index_groups=members)  5.4 us
    pallas_call x1, Pallas kernels, local(): pl.pallas_call(functools.partial(chain_kernel, cols, groups, slots, sum((...  5.08 us
    ppermute x4, starting transfers between devices, over_row(): return lax.ppermute(x, 'row', [(r, r ^ mask) for r in range(rows)])  4.86 us
    all_to_all x1, starting transfers between devices, local(): lax.all_to_all(merged.reshape(rows * cols, each, width), ('row', 'col'),...  4.78 us
  transfers between devices with their start and end apart: 27, of which 11 were waited for; matrix products, arithmetic and copies ran while one was open for 0% of the time, Pallas kernels for 3%

profile of v22, /device:TPU:0, one launch (start us, length us, event | category | flops | bytes accessed | tf_op | source)
XLA Modules:
  0.0 70.1 jit_solution(8593870510934661603)
XLA Ops:
  0.0 1.7 %pack.1 = bf16[8,80,256]{2,1,0:T(8,128)(2,1)} custom-call(bf16[16,64,256]{2,1,0:T(8,128)(2,1)} %bitcast.11, bf16[16,16,256]{2,1,0:T(8,128)(2,1)} %bitcast.15), custom_call_target="tpu_custom_call" | custom-call | bytes 655360 | tf_op jit(solution)/shard_map/pack/pallas_call | solution.py:177
  1.7 0.0 copy-start.3
  1.7 5.4 %all-to-all-start = ((bf16[8,80,256]{2,1,0:T(8,128)(2,1)}), bf16[8,80,256]{2,1,0:T(8,128)(2,1)S(1)}, u32[]{:S(2)}, u32[]{:S(2)}) async-start(bf16[8,80,256]{2,1,0:T(8,128)(2,1)} %pack.1), calls=%async_computation | async-start | bytes 655360 | tf_op jit(solution)/shard_map/all_to_all | solution.py:189
  7.1 2.7 %collective-permute-start.1 = (bf16[64,512]{1,0:T(8,128)(2,1)S(1)}, bf16[64,512]{1,0:T(8,128)(2,1)S(1)}, u32[]{:S(2)}, u32[]{:S(2)}) collective-permute-start(bf16[64,512]{1,0:T(8,128)(2,1)S(1)} %copy-done.3), channel_id=1, source_target_pairs={{0,8},{1,9},{2,10},{3,11},{4,12},{5,13},{6,14},{7,15},{8,0},{9,1},... | collective-permute-start | bytes 196616 | tf_op jit(solution)/shard_map/ppermute | solution.py:166
  9.8 3.4 %collective-permute-done.1 = bf16[64,512]{1,0:T(8,128)(2,1)S(1)} collective-permute-done((bf16[64,512]{1,0:T(8,128)(2,1)S(1)}, bf16[64,512]{1,0:T(8,128)(2,1)S(1)}, u32[]{:S(2)}, u32[]{:S(2)}) %collective-permute-start.1) | collective-permute-done | bytes 65568 | tf_op jit(solution)/shard_map/ppermute | solution.py:166
  13.2 0.0 copy-start.1
  13.3 1.6 %collective-permute-start.2 = (bf16[64,512]{1,0:T(8,128)(2,1)S(1)}, bf16[64,512]{1,0:T(8,128)(2,1)S(1)}, u32[]{:S(2)}, u32[]{:S(2)}) collective-permute-start(bf16[64,512]{1,0:T(8,128)(2,1)S(1)} %get-tuple-element.29), channel_id=1, source_target_pairs={{0,16},{16,0},{1,17},{17,1},{2,18},{18,2},{3,19},{19,3},{4,20},{20... | collective-permute-start | bytes 196616 | tf_op jit(solution)/shard_map/ppermute | solution.py:169
  14.8 0.4 all-to-all-done.held
  15.3 0.7 %pick.1 = bf16[5,80,256]{2,1,0:T(8,128)(2,1)S(1)} custom-call(s32[6]{0:T(128)S(1)} %copy-done.1, bf16[8,80,256]{2,1,0:T(8,128)(2,1)S(1)} %all-to-all-done.held), custom_call_target="tpu_custom_call" | custom-call | bytes 327680 | tf_op jit(solution)/shard_map/pick/pallas_call | solution.py:191
  16.0 3.1 %collective-permute-start = (bf16[16,256]{1,0:T(8,128)(2,1)S(1)}, bf16[16,256]{1,0:T(8,128)(2,1)S(1)}, u32[]{:S(2)}, u32[]{:S(2)}) collective-permute-start(bf16[16,256]{1,0:T(8,128)(2,1)S(1)} %slice.8), channel_id=1, source_target_pairs={{0,8},{1,9},{2,10},{3,11},{4,12},{5,13},{6,14},{7,15},{8,0},{9,1},... | collective-permute-start | bytes 24584 | tf_op jit(solution)/shard_map/ppermute | solution.py:166
  19.1 0.0 collective-permute-done.2
  19.1 1.6 %collective-permute-done.refs_0_ = bf16[16,256]{1,0:T(8,128)(2,1)S(1)} collective-permute-done((bf16[16,256]{1,0:T(8,128)(2,1)S(1)}, bf16[16,256]{1,0:T(8,128)(2,1)S(1)}, u32[]{:S(2)}, u32[]{:S(2)}) %collective-permute-start) | collective-permute-done | bytes 8224 | tf_op jit(solution)/shard_map/ppermute | solution.py:166
  20.7 1.6 %collective-permute-start.13 = (bf16[1,64,512]{2,1,0:T(8,128)(2,1)S(1)}, bf16[1,64,512]{2,1,0:T(8,128)(2,1)S(1)}, u32[]{:S(2)}, u32[]{:S(2)}) collective-permute-start(bf16[1,64,512]{2,1,0:T(8,128)(2,1)S(1)} %bitcast.8), channel_id=1, source_target_pairs={{0,2},{1,3},{2,0},{3,1},{4,6},{5,7},{6,4},{7,5},{8,10},{9,11},{10,... | collective-permute-start | bytes 196616 | tf_op jit(solution)/shard_map/ppermute | solution.py:166
  22.3 3.0 %collective-permute-start.3 = (bf16[384,256]{1,0:T(8,128)(2,1)S(1)}, bf16[384,256]{1,0:T(8,128)(2,1)S(1)}, u32[]{:S(2)}, u32[]{:S(2)}) collective-permute-start(bf16[384,256]{1,0:T(8,128)(2,1)S(1)} %slice.9), channel_id=1, source_target_pairs={{0,8},{1,9},{2,10},{3,11},{4,12},{5,13},{6,14},{7,15},{8,0},{9,1},... | collective-permute-start | bytes 589832 | tf_op jit(solution)/shard_map/ppermute | solution.py:166
  25.3 1.2 %collective-permute-start.14 = (bf16[1,64,512]{2,1,0:T(8,128)(2,1)S(1)}, bf16[1,64,512]{2,1,0:T(8,128)(2,1)S(1)}, u32[]{:S(2)}, u32[]{:S(2)}) collective-permute-start(bf16[1,64,512]{2,1,0:T(8,128)(2,1)S(1)} %bitcast.12), channel_id=1, source_target_pairs={{0,4},{1,5},{2,6},{3,7},{4,0},{5,1},{6,2},{7,3},{8,12},{9,13},{10,... | collective-permute-start | bytes 196616 | tf_op jit(solution)/shard_map/ppermute | solution.py:166
  26.6 2.7 %collective-permute-start.15 = (bf16[2,64,512]{2,1,0:T(8,128)(2,1)S(1)}, bf16[2,64,512]{2,1,0:T(8,128)(2,1)S(1)}, u32[]{:S(2)}, u32[]{:S(2)}) collective-permute-start(bf16[2,64,512]{2,1,0:T(8,128)(2,1)S(1)} %pad_maximum_fusion.4), channel_id=1, source_target_pairs={{0,4},{1,5},{2,6},{3,7},{4,0},{5,1},{6,2},{7,3},{8,12},{9,13},{10,... | collective-permute-start | bytes 393224 | tf_op jit(solution)/shard_map/ppermute | solution.py:166
  29.3 1.4 %collective-permute-done.14 = bf16[1,64,512]{2,1,0:T(8,128)(2,1)S(1)} collective-permute-done((bf16[1,64,512]{2,1,0:T(8,128)(2,1)S(1)}, bf16[1,64,512]{2,1,0:T(8,128)(2,1)S(1)}, u32[]{:S(2)}, u32[]{:S(2)}) %collective-permute-start.14) | collective-permute-done | bytes 65568 | tf_op jit(solution)/shard_map/ppermute | solution.py:166
  30.7 1.5 %collective-permute-start.16 = (bf16[2,64,512]{2,1,0:T(8,128)(2,1)S(1)}, bf16[2,64,512]{2,1,0:T(8,128)(2,1)S(1)}, u32[]{:S(2)}, u32[]{:S(2)}) collective-permute-start(bf16[2,64,512]{2,1,0:T(8,128)(2,1)S(1)} %pad_maximum_fusion.5), channel_id=1, source_target_pairs={{0,2},{1,3},{2,0},{3,1},{4,6},{5,7},{6,4},{7,5},{8,10},{9,11},{10,... | collective-permute-start | bytes 393224 | tf_op jit(solution)/shard_map/ppermute | solution.py:166
  32.2 0.1 collective-permute-start.17
  32.3 0.0 collective-permute-done.3.refs_1_
  32.3 0.6 order.1
  32.9 1.4 %collective-permute-start.4 = (bf16[1,2,80,256]{3,2,1,0:T(8,128)(2,1)S(1)}, bf16[1,2,80,256]{3,2,1,0:T(8,128)(2,1)S(1)}, u32[]{:S(2)}, u32[]{:S(2)}) collective-permute-start(bf16[1,2,80,256]{3,2,1,0:T(8,128)(2,1)S(1)} %get-tuple-element.20), channel_id=1, source_target_pairs={{0,16},{16,0},{1,17},{17,1},{2,18},{18,2},{3,19},{19,3},{4,20},{20... | collective-permute-start | bytes 245768 | tf_op jit(solution)/shard_map/ppermute | solution.py:169
  34.3 0.7 collective-permute-start.7
  35.0 0.0 collective-permute-done.15
  35.0 1.8 %collective-permute-start.10 = (bf16[1,2,80,256]{3,2,1,0:T(8,128)(2,1)S(1)}, bf16[1,2,80,256]{3,2,1,0:T(8,128)(2,1)S(1)}, u32[]{:S(2)}, u32[]{:S(2)}) collective-permute-start(bf16[1,2,80,256]{3,2,1,0:T(8,128)(2,1)S(1)} %get-tuple-element.22), channel_id=1, source_target_pairs={{0,4},{1,5},{2,6},{3,7},{4,0},{5,1},{6,2},{7,3},{8,12},{9,13},{10,... | collective-permute-start | bytes 245768 | tf_op jit(solution)/shard_map/ppermute | solution.py:166
  36.8 0.1 collective-permute-start.18
  36.9 0.9 %collective-permute-done.4 = bf16[1,2,80,256]{3,2,1,0:T(8,128)(2,1)S(1)} collective-permute-done((bf16[1,2,80,256]{3,2,1,0:T(8,128)(2,1)S(1)}, bf16[1,2,80,256]{3,2,1,0:T(8,128)(2,1)S(1)}, u32[]{:S(2)}, u32[]{:S(2)}) %collective-permute-start.4) | collective-permute-done | bytes 81952 | tf_op jit(solution)/shard_map/ppermute | solution.py:169
  37.9 0.0 copy-start
  37.9 0.7 collective-permute-start.5
  38.5 0.2 collective-permute-done.7
  38.8 2.3 %collective-permute-start.8 = (bf16[2,2,80,256]{3,2,1,0:T(8,128)(2,1)S(1)}, bf16[2,2,80,256]{3,2,1,0:T(8,128)(2,1)S(1)}, u32[]{:S(2)}, u32[]{:S(2)}) collective-permute-start(bf16[2,2,80,256]{3,2,1,0:T(8,128)(2,1)S(1)} %pad_maximum_fusion.2), channel_id=1, source_target_pairs={{0,4},{1,5},{2,6},{3,7},{4,0},{5,1},{6,2},{7,3},{8,12},{9,13},{10,... | collective-permute-start | bytes 491528 | tf_op jit(solution)/shard_map/ppermute | solution.py:166
  41.0 0.8 %collective-permute-start.11 = (bf16[2,2,80,256]{3,2,1,0:T(8,128)(2,1)S(1)}, bf16[2,2,80,256]{3,2,1,0:T(8,128)(2,1)S(1)}, u32[]{:S(2)}, u32[]{:S(2)}) collective-permute-start(bf16[2,2,80,256]{3,2,1,0:T(8,128)(2,1)S(1)} %pad_maximum_fusion.3), channel_id=1, source_target_pairs={{0,16},{16,0},{1,17},{17,1},{2,18},{18,2},{3,19},{19,3},{4,20},{20... | collective-permute-start | bytes 491528 | tf_op jit(solution)/shard_map/ppermute | solution.py:169
  41.8 4.6 %collective-permute-done.11 = bf16[2,2,80,256]{3,2,1,0:T(8,128)(2,1)S(1)} collective-permute-done((bf16[2,2,80,256]{3,2,1,0:T(8,128)(2,1)S(1)}, bf16[2,2,80,256]{3,2,1,0:T(8,128)(2,1)S(1)}, u32[]{:S(2)}, u32[]{:S(2)}) %collective-permute-start.11) | collective-permute-done | bytes 163872 | tf_op jit(solution)/shard_map/ppermute | solution.py:169
  46.4 0.6 collective-permute-start.12
  47.1 1.2 %collective-permute-start.9 = (bf16[4,2,80,256]{3,2,1,0:T(8,128)(2,1)S(1)}, bf16[4,2,80,256]{3,2,1,0:T(8,128)(2,1)S(1)}, u32[]{:S(2)}, u32[]{:S(2)}) collective-permute-start(bf16[4,2,80,256]{3,2,1,0:T(8,128)(2,1)S(1)} %constant_dynamic-update-slice_fusion.3.refs_4_), channel_id=1, source_target_pairs={{0,16},{16,0},{1,17},{17,1},{2,18},{18,2},{3,19},{19,3},{4,20},{20... | collective-permute-start | bytes 983048 | tf_op jit(solution)/shard_map/ppermute | solution.py:169
  48.3 0.9 %collective-permute-start.6 = (bf16[4,2,80,256]{3,2,1,0:T(8,128)(2,1)S(1)}, bf16[4,2,80,256]{3,2,1,0:T(8,128)(2,1)S(1)}, u32[]{:S(2)}, u32[]{:S(2)}) collective-permute-start(bf16[4,2,80,256]{3,2,1,0:T(8,128)(2,1)S(1)} %constant_dynamic-update-slice_fusion.refs_0_), channel_id=1, source_target_pairs={{0,4},{1,5},{2,6},{3,7},{4,0},{5,1},{6,2},{7,3},{8,12},{9,13},{10,... | collective-permute-start | bytes 983048 | tf_op jit(solution)/shard_map/ppermute | solution.py:166
  49.2 1.1 %merge.1 = f32[128,128]{1,0:T(8,128)} custom-call(bf16[4096,128]{1,0:T(8,128)(2,1)S(1)} %copy-done, bf16[4,64,512]{2,1,0:T(8,128)(2,1)S(1)} %pad_maximum_fusion.refs_0_, bf16[4,64,512]{2,1,0:T(8,128)(2,1)S(1)} %constant_dynamic-update-slice_fusion.9.refs_1_, bf16[4,64,512]{2,1,0:T(8,128)(2,1)S(1)} %collective-permute-done.17.refs_2_, ...), custom_call_target="tpu_custom_call" | custom-call | flops 134217728 | bytes 1048576 | tf_op jit(solution)/shard_map/merge/pallas_call | solution.py:241
  50.2 4.8 %all-to-all-start.1 = ((f32[32,4,128]{2,1,0:T(4,128)}), f32[32,4,128]{2,1,0:T(4,128)S(1)}, u32[]{:S(2)}, u32[]{:S(2)}) async-start(f32[32,4,128]{2,1,0:T(4,128)} %bitcast.5), calls=%async_computation.1 | async-start | bytes 131072 | tf_op jit(solution)/shard_map/all_to_all | solution.py:272
  55.0 0.3 collective-permute-start.21
  55.3 0.3 collective-permute-start.19
  55.6 6.8 %all-to-all-done.1.start = f32[32,4,128]{2,1,0:T(4,128)S(1)} async-done(((f32[32,4,128]{2,1,0:T(4,128)}), f32[32,4,128]{2,1,0:T(4,128)S(1)}, u32[]{:S(2)}, u32[]{:S(2)}) %all-to-all-start.1) | async-done | bytes 65568 | tf_op jit(solution)/shard_map/all_to_all | solution.py:272
  62.4 0.1 collective-permute-start.20
  62.6 0.4 collective-permute-start.22
  63.0 0.1 collective-permute-start.24
  63.1 1.0 %collective-permute-done.20.refs_3_ = bf16[4,2,80,256]{3,2,1,0:T(8,128)(2,1)S(1)} collective-permute-done((bf16[4,2,80,256]{3,2,1,0:T(8,128)(2,1)S(1)}, bf16[4,2,80,256]{3,2,1,0:T(8,128)(2,1)S(1)}, u32[]{:S(2)}, u32[]{:S(2)}) %collective-permute-start.20) | collective-permute-done | bytes 327712 | tf_op jit(solution)/shard_map/ppermute | solution.py:166
  64.1 0.5 collective-permute-done.22.refs_7_
  64.5 0.5 collective-permute-done.24.refs_11_
  65.0 5.1 %chain0.1 = bf16[4,2048]{1,0:T(4,128)(2,1)} custom-call(s32[6]{0:T(128)S(1)} %copy-done.2, f32[32,4,128]{2,1,0:T(4,128)S(1)} %all-to-all-done.1.start, bf16[4,2,80,256]{3,2,1,0:T(8,128)(2,1)S(1)} %constant_dynamic-update-slice_fusion.refs_0_, bf16[4,2,80,256]{3,2,1,0:T(8,128)(2,1)S(1)} %collective-permute-done.6.refs_1_, ...), custom_call_target="tpu_custom_call" | custom-call | flops 201326592 | bytes 3932160 | tf_op jit(solution)/shard_map/chain0/pallas_call | solution.py:290
  (38 shorter events, 0.3 us)
Async XLA Ops:
  1.7 5.4 %copy-start.3 = (bf16[64,512]{1,0:T(8,128)(2,1)S(1)}, bf16[64,512]{1,0:T(8,128)(2,1)}, u32[]{:S(2)}) copy-start(bf16[64,512]{1,0:T(8,128)(2,1)} %param.7) | copy-start | bytes 196612
  1.7 13.5 %all-to-all-start = ((bf16[8,80,256]{2,1,0:T(8,128)(2,1)}), bf16[8,80,256]{2,1,0:T(8,128)(2,1)S(1)}, u32[]{:S(2)}, u32[]{:S(2)}) async-start(bf16[8,80,256]{2,1,0:T(8,128)(2,1)} %pack.1), calls=%async_computation | async-start | bytes 655360 | tf_op jit(solution)/shard_map/all_to_all | solution.py:189
  7.1 6.1 %collective-permute-start.1 = (bf16[64,512]{1,0:T(8,128)(2,1)S(1)}, bf16[64,512]{1,0:T(8,128)(2,1)S(1)}, u32[]{:S(2)}, u32[]{:S(2)}) collective-permute-start(bf16[64,512]{1,0:T(8,128)(2,1)S(1)} %copy-done.3), channel_id=1, source_target_pairs={{0,8},{1,9},{2,10},{3,11},{4,12},{5,13},{6,14},{7,15},{8,0},{9,1},... | collective-permute-start | bytes 196616 | tf_op jit(solution)/shard_map/ppermute | solution.py:166
  13.2 2.0 %copy-start.1 = (s32[6]{0:T(128)S(1)}, s32[6]{0:T(128)}, u32[]{:S(2)}) copy-start(s32[6]{0:T(128)} %owners.3) | copy-start | bytes 76
  13.3 5.8 %collective-permute-start.2 = (bf16[64,512]{1,0:T(8,128)(2,1)S(1)}, bf16[64,512]{1,0:T(8,128)(2,1)S(1)}, u32[]{:S(2)}, u32[]{:S(2)}) collective-permute-start(bf16[64,512]{1,0:T(8,128)(2,1)S(1)} %get-tuple-element.29), channel_id=1, source_target_pairs={{0,16},{16,0},{1,17},{17,1},{2,18},{18,2},{3,19},{19,3},{4,20},{20... | collective-permute-start | bytes 196616 | tf_op jit(solution)/shard_map/ppermute | solution.py:169
  16.0 4.7 %collective-permute-start = (bf16[16,256]{1,0:T(8,128)(2,1)S(1)}, bf16[16,256]{1,0:T(8,128)(2,1)S(1)}, u32[]{:S(2)}, u32[]{:S(2)}) collective-permute-start(bf16[16,256]{1,0:T(8,128)(2,1)S(1)} %slice.8), channel_id=1, source_target_pairs={{0,8},{1,9},{2,10},{3,11},{4,12},{5,13},{6,14},{7,15},{8,0},{9,1},... | collective-permute-start | bytes 24584 | tf_op jit(solution)/shard_map/ppermute | solution.py:166
  20.7 5.9 %collective-permute-start.13 = (bf16[1,64,512]{2,1,0:T(8,128)(2,1)S(1)}, bf16[1,64,512]{2,1,0:T(8,128)(2,1)S(1)}, u32[]{:S(2)}, u32[]{:S(2)}) collective-permute-start(bf16[1,64,512]{2,1,0:T(8,128)(2,1)S(1)} %bitcast.8), channel_id=1, source_target_pairs={{0,2},{1,3},{2,0},{3,1},{4,6},{5,7},{6,4},{7,5},{8,10},{9,11},{10,... | collective-permute-start | bytes 196616 | tf_op jit(solution)/shard_map/ppermute | solution.py:166
  22.3 10.0 %collective-permute-start.3 = (bf16[384,256]{1,0:T(8,128)(2,1)S(1)}, bf16[384,256]{1,0:T(8,128)(2,1)S(1)}, u32[]{:S(2)}, u32[]{:S(2)}) collective-permute-start(bf16[384,256]{1,0:T(8,128)(2,1)S(1)} %slice.9), channel_id=1, source_target_pairs={{0,8},{1,9},{2,10},{3,11},{4,12},{5,13},{6,14},{7,15},{8,0},{9,1},... | collective-permute-start | bytes 589832 | tf_op jit(solution)/shard_map/ppermute | solution.py:166
  25.3 5.3 %collective-permute-start.14 = (bf16[1,64,512]{2,1,0:T(8,128)(2,1)S(1)}, bf16[1,64,512]{2,1,0:T(8,128)(2,1)S(1)}, u32[]{:S(2)}, u32[]{:S(2)}) collective-permute-start(bf16[1,64,512]{2,1,0:T(8,128)(2,1)S(1)} %bitcast.12), channel_id=1, source_target_pairs={{0,4},{1,5},{2,6},{3,7},{4,0},{5,1},{6,2},{7,3},{8,12},{9,13},{10,... | collective-permute-start | bytes 196616 | tf_op jit(solution)/shard_map/ppermute | solution.py:166
  26.6 8.4 %collective-permute-start.15 = (bf16[2,64,512]{2,1,0:T(8,128)(2,1)S(1)}, bf16[2,64,512]{2,1,0:T(8,128)(2,1)S(1)}, u32[]{:S(2)}, u32[]{:S(2)}) collective-permute-start(bf16[2,64,512]{2,1,0:T(8,128)(2,1)S(1)} %pad_maximum_fusion.4), channel_id=1, source_target_pairs={{0,4},{1,5},{2,6},{3,7},{4,0},{5,1},{6,2},{7,3},{8,12},{9,13},{10,... | collective-permute-start | bytes 393224 | tf_op jit(solution)/shard_map/ppermute | solution.py:166
  30.7 6.1 %collective-permute-start.16 = (bf16[2,64,512]{2,1,0:T(8,128)(2,1)S(1)}, bf16[2,64,512]{2,1,0:T(8,128)(2,1)S(1)}, u32[]{:S(2)}, u32[]{:S(2)}) collective-permute-start(bf16[2,64,512]{2,1,0:T(8,128)(2,1)S(1)} %pad_maximum_fusion.5), channel_id=1, source_target_pairs={{0,2},{1,3},{2,0},{3,1},{4,6},{5,7},{6,4},{7,5},{8,10},{9,11},{10,... | collective-permute-start | bytes 393224 | tf_op jit(solution)/shard_map/ppermute | solution.py:166
  32.2 16.9 %collective-permute-start.17 = (bf16[4,64,512]{2,1,0:T(8,128)(2,1)S(1)}, bf16[4,64,512]{2,1,0:T(8,128)(2,1)S(1)}, u32[]{:S(2)}, u32[]{:S(2)}) collective-permute-start(bf16[4,64,512]{2,1,0:T(8,128)(2,1)S(1)} %pad_maximum_fusion.refs_0_), channel_id=1, source_target_pairs={{0,1},{1,0},{2,3},{3,2},{4,5},{5,4},{6,7},{7,6},{8,9},{9,8},{10,11... | collective-permute-start | bytes 786440 | tf_op jit(solution)/shard_map/ppermute | solution.py:166
  32.9 4.9 %collective-permute-start.4 = (bf16[1,2,80,256]{3,2,1,0:T(8,128)(2,1)S(1)}, bf16[1,2,80,256]{3,2,1,0:T(8,128)(2,1)S(1)}, u32[]{:S(2)}, u32[]{:S(2)}) collective-permute-start(bf16[1,2,80,256]{3,2,1,0:T(8,128)(2,1)S(1)} %get-tuple-element.20), channel_id=1, source_target_pairs={{0,16},{16,0},{1,17},{17,1},{2,18},{18,2},{3,19},{19,3},{4,20},{20... | collective-permute-start | bytes 245768 | tf_op jit(solution)/shard_map/ppermute | solution.py:169
  34.3 4.4 %collective-permute-start.7 = (bf16[1,2,80,256]{3,2,1,0:T(8,128)(2,1)S(1)}, bf16[1,2,80,256]{3,2,1,0:T(8,128)(2,1)S(1)}, u32[]{:S(2)}, u32[]{:S(2)}) collective-permute-start(bf16[1,2,80,256]{3,2,1,0:T(8,128)(2,1)S(1)} %get-tuple-element.21), channel_id=1, source_target_pairs={{0,2},{1,3},{2,0},{3,1},{4,6},{5,7},{6,4},{7,5},{8,10},{9,11},{10,... | collective-permute-start | bytes 245768 | tf_op jit(solution)/shard_map/ppermute | solution.py:166
  35.0 6.0 %collective-permute-start.10 = (bf16[1,2,80,256]{3,2,1,0:T(8,128)(2,1)S(1)}, bf16[1,2,80,256]{3,2,1,0:T(8,128)(2,1)S(1)}, u32[]{:S(2)}, u32[]{:S(2)}) collective-permute-start(bf16[1,2,80,256]{3,2,1,0:T(8,128)(2,1)S(1)} %get-tuple-element.22), channel_id=1, source_target_pairs={{0,4},{1,5},{2,6},{3,7},{4,0},{5,1},{6,2},{7,3},{8,12},{9,13},{10,... | collective-permute-start | bytes 245768 | tf_op jit(solution)/shard_map/ppermute | solution.py:166
  36.8 12.3 %collective-permute-start.18 = (bf16[4,64,512]{2,1,0:T(8,128)(2,1)S(1)}, bf16[4,64,512]{2,1,0:T(8,128)(2,1)S(1)}, u32[]{:S(2)}, u32[]{:S(2)}) collective-permute-start(bf16[4,64,512]{2,1,0:T(8,128)(2,1)S(1)} %constant_dynamic-update-slice_fusion.9.refs_1_), channel_id=1, source_target_pairs={{0,1},{1,0},{2,3},{3,2},{4,5},{5,4},{6,7},{7,6},{8,9},{9,8},{10,11... | collective-permute-start | bytes 786440 | tf_op jit(solution)/shard_map/ppermute | solution.py:166
  37.9 11.3 %copy-start = (bf16[4096,128]{1,0:T(8,128)(2,1)S(1)}, bf16[4096,128]{1,0:T(8,128)(2,1)}, u32[]{:S(2)}) copy-start(bf16[4096,128]{1,0:T(8,128)(2,1)} %sub.6) | copy-start | bytes 3145732
  37.9 10.4 %collective-permute-start.5 = (bf16[2,2,80,256]{3,2,1,0:T(8,128)(2,1)S(1)}, bf16[2,2,80,256]{3,2,1,0:T(8,128)(2,1)S(1)}, u32[]{:S(2)}, u32[]{:S(2)}) collective-permute-start(bf16[2,2,80,256]{3,2,1,0:T(8,128)(2,1)S(1)} %pad_maximum_fusion.1), channel_id=1, source_target_pairs={{0,2},{1,3},{2,0},{3,1},{4,6},{5,7},{6,4},{7,5},{8,10},{9,11},{10,... | collective-permute-start | bytes 491528 | tf_op jit(solution)/shard_map/ppermute | solution.py:166
  38.8 8.3 %collective-permute-start.8 = (bf16[2,2,80,256]{3,2,1,0:T(8,128)(2,1)S(1)}, bf16[2,2,80,256]{3,2,1,0:T(8,128)(2,1)S(1)}, u32[]{:S(2)}, u32[]{:S(2)}) collective-permute-start(bf16[2,2,80,256]{3,2,1,0:T(8,128)(2,1)S(1)} %pad_maximum_fusion.2), channel_id=1, source_target_pairs={{0,4},{1,5},{2,6},{3,7},{4,0},{5,1},{6,2},{7,3},{8,12},{9,13},{10,... | collective-permute-start | bytes 491528 | tf_op jit(solution)/shard_map/ppermute | solution.py:166
  41.0 5.4 %collective-permute-start.11 = (bf16[2,2,80,256]{3,2,1,0:T(8,128)(2,1)S(1)}, bf16[2,2,80,256]{3,2,1,0:T(8,128)(2,1)S(1)}, u32[]{:S(2)}, u32[]{:S(2)}) collective-permute-start(bf16[2,2,80,256]{3,2,1,0:T(8,128)(2,1)S(1)} %pad_maximum_fusion.3), channel_id=1, source_target_pairs={{0,16},{16,0},{1,17},{17,1},{2,18},{18,2},{3,19},{19,3},{4,20},{20... | collective-permute-start | bytes 491528 | tf_op jit(solution)/shard_map/ppermute | solution.py:169
  46.4 8.9 %collective-permute-start.12 = (bf16[4,2,80,256]{3,2,1,0:T(8,128)(2,1)S(1)}, bf16[4,2,80,256]{3,2,1,0:T(8,128)(2,1)S(1)}, u32[]{:S(2)}, u32[]{:S(2)}) collective-permute-start(bf16[4,2,80,256]{3,2,1,0:T(8,128)(2,1)S(1)} %constant_dynamic-update-slice_fusion.6.refs_8_), channel_id=1, source_target_pairs={{0,2},{1,3},{2,0},{3,1},{4,6},{5,7},{6,4},{7,5},{8,10},{9,11},{10,... | collective-permute-start | bytes 983048 | tf_op jit(solution)/shard_map/ppermute | solution.py:166
  47.1 15.4 %collective-permute-start.9 = (bf16[4,2,80,256]{3,2,1,0:T(8,128)(2,1)S(1)}, bf16[4,2,80,256]{3,2,1,0:T(8,128)(2,1)S(1)}, u32[]{:S(2)}, u32[]{:S(2)}) collective-permute-start(bf16[4,2,80,256]{3,2,1,0:T(8,128)(2,1)S(1)} %constant_dynamic-update-slice_fusion.3.refs_4_), channel_id=1, source_target_pairs={{0,16},{16,0},{1,17},{17,1},{2,18},{18,2},{3,19},{19,3},{4,20},{20... | collective-permute-start | bytes 983048 | tf_op jit(solution)/shard_map/ppermute | solution.py:169
  48.3 14.2 %collective-permute-start.6 = (bf16[4,2,80,256]{3,2,1,0:T(8,128)(2,1)S(1)}, bf16[4,2,80,256]{3,2,1,0:T(8,128)(2,1)S(1)}, u32[]{:S(2)}, u32[]{:S(2)}) collective-permute-start(bf16[4,2,80,256]{3,2,1,0:T(8,128)(2,1)S(1)} %constant_dynamic-update-slice_fusion.refs_0_), channel_id=1, source_target_pairs={{0,4},{1,5},{2,6},{3,7},{4,0},{5,1},{6,2},{7,3},{8,12},{9,13},{10,... | collective-permute-start | bytes 983048 | tf_op jit(solution)/shard_map/ppermute | solution.py:166
  49.1 13.8 %collective-permute-start.23 = (bf16[4,2,80,256]{3,2,1,0:T(8,128)(2,1)S(1)}, bf16[4,2,80,256]{3,2,1,0:T(8,128)(2,1)S(1)}, u32[]{:S(2)}, u32[]{:S(2)}) collective-permute-start(bf16[4,2,80,256]{3,2,1,0:T(8,128)(2,1)S(1)} %constant_dynamic-update-slice_fusion.6.refs_8_), channel_id=1, source_target_pairs={{0,1},{1,0},{2,3},{3,2},{4,5},{5,4},{6,7},{7,6},{8,9},{9,8},{10,11... | collective-permute-start | bytes 983048 | tf_op jit(solution)/shard_map/ppermute | solution.py:166
  50.2 14.8 %copy-start.2 = (s32[6]{0:T(128)S(1)}, s32[6]{0:T(128)}, u32[]{:S(2)}) copy-start(s32[6]{0:T(128)} %offsets.1) | copy-start | bytes 76
  50.2 12.2 %all-to-all-start.1 = ((f32[32,4,128]{2,1,0:T(4,128)}), f32[32,4,128]{2,1,0:T(4,128)S(1)}, u32[]{:S(2)}, u32[]{:S(2)}) async-start(f32[32,4,128]{2,1,0:T(4,128)} %bitcast.5), calls=%async_computation.1 | async-start | bytes 131072 | tf_op jit(solution)/shard_map/all_to_all | solution.py:272
  55.0 8.1 %collective-permute-start.21 = (bf16[4,2,80,256]{3,2,1,0:T(8,128)(2,1)S(1)}, bf16[4,2,80,256]{3,2,1,0:T(8,128)(2,1)S(1)}, u32[]{:S(2)}, u32[]{:S(2)}) collective-permute-start(bf16[4,2,80,256]{3,2,1,0:T(8,128)(2,1)S(1)} %constant_dynamic-update-slice_fusion.3.refs_4_), channel_id=1, source_target_pairs={{0,1},{1,0},{2,3},{3,2},{4,5},{5,4},{6,7},{7,6},{8,9},{9,8},{10,11... | collective-permute-start | bytes 983048 | tf_op jit(solution)/shard_map/ppermute | solution.py:166
  55.3 7.7 %collective-permute-start.19 = (bf16[4,2,80,256]{3,2,1,0:T(8,128)(2,1)S(1)}, bf16[4,2,80,256]{3,2,1,0:T(8,128)(2,1)S(1)}, u32[]{:S(2)}, u32[]{:S(2)}) collective-permute-start(bf16[4,2,80,256]{3,2,1,0:T(8,128)(2,1)S(1)} %constant_dynamic-update-slice_fusion.refs_0_), channel_id=1, source_target_pairs={{0,1},{1,0},{2,3},{3,2},{4,5},{5,4},{6,7},{7,6},{8,9},{9,8},{10,11... | collective-permute-start | bytes 983048 | tf_op jit(solution)/shard_map/ppermute | solution.py:166
  62.4 1.6 %collective-permute-start.20 = (bf16[4,2,80,256]{3,2,1,0:T(8,128)(2,1)S(1)}, bf16[4,2,80,256]{3,2,1,0:T(8,128)(2,1)S(1)}, u32[]{:S(2)}, u32[]{:S(2)}) collective-permute-start(bf16[4,2,80,256]{3,2,1,0:T(8,128)(2,1)S(1)} %collective-permute-done.6.refs_1_), channel_id=1, source_target_pairs={{0,1},{1,0},{2,3},{3,2},{4,5},{5,4},{6,7},{7,6},{8,9},{9,8},{10,11... | collective-permute-start | bytes 983048 | tf_op jit(solution)/shard_map/ppermute | solution.py:166
  62.6 2.0 %collective-permute-start.22 = (bf16[4,2,80,256]{3,2,1,0:T(8,128)(2,1)S(1)}, bf16[4,2,80,256]{3,2,1,0:T(8,128)(2,1)S(1)}, u32[]{:S(2)}, u32[]{:S(2)}) collective-permute-start(bf16[4,2,80,256]{3,2,1,0:T(8,128)(2,1)S(1)} %collective-permute-done.9.refs_5_), channel_id=1, source_target_pairs={{0,1},{1,0},{2,3},{3,2},{4,5},{5,4},{6,7},{7,6},{8,9},{9,8},{10,11... | collective-permute-start | bytes 983048 | tf_op jit(solution)/shard_map/ppermute | solution.py:166
  63.0 2.1 %collective-permute-start.24 = (bf16[4,2,80,256]{3,2,1,0:T(8,128)(2,1)S(1)}, bf16[4,2,80,256]{3,2,1,0:T(8,128)(2,1)S(1)}, u32[]{:S(2)}, u32[]{:S(2)}) collective-permute-start(bf16[4,2,80,256]{3,2,1,0:T(8,128)(2,1)S(1)} %collective-permute-done.12.refs_9_), channel_id=1, source_target_pairs={{0,1},{1,0},{2,3},{3,2},{4,5},{5,4},{6,7},{7,6},{8,9},{9,8},{10,11... | collective-permute-start | bytes 983048 | tf_op jit(solution)/shard_map/ppermute | solution.py:166

commit v23 on v21

--- a/solution.py
+++ b/solution.py
@@ -74,8 +74,10 @@
     for group in range(GROUPS):
         half, rank = places(owners, group)
         piece = held[lax.rem(owners[group], HALF)]
-        for mask, ref in enumerate(others, 1):
-            other = ref[jnp.minimum(rank, ref.shape[0] - 1)]
+        for mask in range(1, len(others) // 2 + 1):
+            head, tail = others[2 * mask - 2 : 2 * mask]
+            other = tail[jnp.clip(rank - 1, 0, tail.shape[0] - 1)]
+            other = jnp.where(rank == 0, head[0], other)
             piece = jnp.where(jnp.bitwise_xor(half, mine) == mask, other, piece)
         outs[group // each][0, group % each] = piece
 
@@ -168,6 +170,8 @@
     pv, pt = group_rows // SLICES, reflect // SLICES
     piece = (pv + pt, reflect)
 
+    across = [merge_factor] + [over_col(merge_factor, m * share) for m in range(1, rows)]
+
     packed = pl.pallas_call(
         pack_kernel,
         out_shape=jax.ShapeDtypeStruct((HALF,) + piece, dtype),
@@ -178,9 +182,35 @@
         cost_estimate=cost([basis, factor]),
         name="pack",
     )(basis.reshape(SLICES, pv, reflect), factor.reshape(SLICES, pt, reflect))
-    packed, merge_factor = lax.optimization_barrier((packed, merge_factor))
     members = [[h * HALF + c for c in range(HALF)] for h in range(halves)]
     slices = lax.all_to_all(packed, "col", 0, 0, axis_index_groups=members)
+
+    row, top = lax.axis_index("row"), lax.axis_index("col") // share
+
+    def for_row(mask):
+        index = top ^ row ^ mask
+        block = across[0]
+        for k in range(1, rows):
+            block = jnp.where(index == k, across[k], block)
+        return block
+
+    blocks = [for_row(0)] + [over_row(for_row(m), m) for m in range(1, rows)]
+    groups = [range(rows // 2), range(rows // 2, rows)]
+    sides = [jnp.stack([blocks[m] for m in group]) for group in groups]
+    tags = [[(m, 0) for m in group] for group in groups]
+
+    def double(side, bit):
+        sides[side] = jnp.concatenate([sides[side], over_col(sides[side], bit)])
+        tags[side] = tags[side] + [(m, c ^ bit) for m, c in tags[side]]
+
+    bit = share // 2
+    while bit > 4:
+        double(0, bit)
+        double(1, bit)
+        bit //= 2
+    double(0, 2)
+    double(1, 4)
+    slices, sides = lax.optimization_barrier((slices, sides))
 
     picked = pl.pallas_call(
         pick_kernel,
@@ -191,37 +221,10 @@
         cost_estimate=cost([slices]),
         name="pick",
     )(owners, slices)
-
-    across = [merge_factor] + [over_col(merge_factor, m * share) for m in range(1, rows)]
-
-    row, top = lax.axis_index("row"), lax.axis_index("col") // share
-
-    def for_row(mask):
-        index = top ^ row ^ mask
-        block = across[0]
-        for k in range(1, rows):
-            block = jnp.where(index == k, across[k], block)
-        return block
-
-    blocks = [for_row(0)] + [over_row(for_row(m), m) for m in range(1, rows)]
-    picked, blocks = lax.optimization_barrier((picked, blocks))
-    others = [over_col(picked, m * HALF) for m in range(1, halves)]
-    groups = [range(rows // 2), range(rows // 2, rows)]
-    sides = [jnp.stack([blocks[m] for m in group]) for group in groups]
-    tags = [[(m, 0) for m in group] for group in groups]
-
-    def double(side, bit):
-        sides[side] = jnp.concatenate([sides[side], over_col(sides[side], bit)])
-        tags[side] = tags[side] + [(m, c ^ bit) for m, c in tags[side]]
-
-    bit = share // 2
-    while bit > 4:
-        double(0, bit)
-        double(1, bit)
-        bit //= 2
-    double(0, 2)
-    double(1, 4)
-    others, sides = lax.optimization_barrier((others, sides))
+    heads = [over_col(picked[:1], m * HALF) for m in range(1, halves)]
+    tails = [over_col(picked[1:], m * HALF) for m in range(1, halves)]
+    heads, sides = lax.optimization_barrier((heads, sides))
+    others = [x for pair in zip(heads, tails) for x in pair]
     late = jnp.concatenate([over_col(sides[0], 4), over_col(sides[1], 2)])
     late_tags = [(m, c ^ 4) for m, c in tags[0]] + [(m, c ^ 2) for m, c in tags[1]]
     m_held = [jnp.concatenate(sides), late]
@@ -262,7 +265,7 @@
             colours[k] = jnp.concatenate([colours[k], send(colours[k])])
             masks[k] = masks[k] + [m ^ mask for m in masks[k]]
     state = lax.all_to_all(merged.reshape(rows * cols, each, width), ("row", "col"), 0, 0)
-    colours[0], state = lax.optimization_barrier((colours[0], state))
+    colours, state = lax.optimization_barrier((colours, state))
     last_round = []
     for k in range(COLOURS):
         mask, send = links[(k + 2) % 3]

time: 79.4 us -> 72.6 us (0.914)
  starting transfers between devices: 32 us -> 28.3 us
  waiting for transfers between devices: 37.5 us -> 34.4 us
    ppermute x4, waiting for transfers between devices: 10 us -> 2.85 us  [over_row(): return lax.ppermute(x, 'row', [(r, r ^ mask) for r in range(rows)])]
    ppermute x20 -> x21, waiting for transfers between devices: 21.5 us -> 24.2 us  [over_col(): return lax.ppermute(x, 'col', [(c, c ^ mask) for c in range(cols)])]
    all_to_all x1, waiting for transfers between devices: 5.5 us -> 7.29 us  [local(): lax.all_to_all(merged.reshape(rows * cols, each, width), ('row', 'col'),...]
    ppermute x4, starting transfers between devices: 6.5 us -> 4.74 us  [over_row(): return lax.ppermute(x, 'row', [(r, r ^ mask) for r in range(rows)])]
    all_to_all x1, starting transfers between devices: 5.4 us -> 3.95 us  [local(): slices = lax.all_to_all(packed, 'col', 0, 0, axis_index_groups=members)]
    ppermute x20 -> x21, starting transfers between devices: 16.2 us -> 15.3 us  [over_col(): return lax.ppermute(x, 'col', [(c, c ^ mask) for c in range(cols)])]
  transfers between devices with their start and end apart: 26 -> 27, of which waited for: 11 -> 15; matrix products, arithmetic and copies ran while one was open for 0% -> 0% of each run, Pallas kernels for 3% -> 5%
where the time goes in v23:
time: 72.6 us; the launch traced here: 72.4 us
  waiting for transfers between devices  34.4 us (47%)
  starting transfers between devices  28.3 us (39%)
  Pallas kernels  9.2 us (13%)
    ppermute x21, waiting for transfers between devices, over_col(): return lax.ppermute(x, 'col', [(c, c ^ mask) for c in range(cols)])  24.2 us
    ppermute x21, starting transfers between devices, over_col(): return lax.ppermute(x, 'col', [(c, c ^ mask) for c in range(cols)])  15.3 us
    all_to_all x1, waiting for transfers between devices, local(): lax.all_to_all(merged.reshape(rows * cols, each, width), ('row', 'col'),...  7.29 us
    pallas_call x1, Pallas kernels, local(): pl.pallas_call(functools.partial(chain_kernel, cols, groups, slots, sum((...  5.08 us
    ppermute x4, starting transfers between devices, over_row(): return lax.ppermute(x, 'row', [(r, r ^ mask) for r in range(rows)])  4.74 us
    all_to_all x1, starting transfers between devices, local(): lax.all_to_all(merged.reshape(rows * cols, each, width), ('row', 'col'),...  4.23 us
    all_to_all x1, starting transfers between devices, local(): slices = lax.all_to_all(packed, 'col', 0, 0, axis_index_groups=members)  3.95 us
    ppermute x4, waiting for transfers between devices, over_row(): return lax.ppermute(x, 'row', [(r, r ^ mask) for r in range(rows)])  2.85 us
  transfers between devices with their start and end apart: 27, of which 15 were waited for; matrix products, arithmetic and copies ran while one was open for 0% of the time, Pallas kernels for 5%

profile of v23, /device:TPU:0, one launch (start us, length us, event | category | flops | bytes accessed | tf_op | source)
XLA Modules:
  0.0 72.4 jit_solution(6843232190676792090)
XLA Ops:
  0.0 4.0 %collective-permute-start = (bf16[64,512]{1,0:T(8,128)(2,1)}, bf16[64,512]{1,0:T(8,128)(2,1)S(1)}, u32[]{:S(2)}, u32[]{:S(2)}) collective-permute-start(bf16[64,512]{1,0:T(8,128)(2,1)} %param.7), channel_id=1, source_target_pairs={{0,8},{1,9},{2,10},{3,11},{4,12},{5,13},{6,14},{7,15},{8,0},{9,1},... | collective-permute-start | bytes 196616 | tf_op jit(solution)/shard_map/ppermute | solution.py:162
  4.0 1.7 %pack.1 = bf16[8,80,256]{2,1,0:T(8,128)(2,1)} custom-call(bf16[16,64,256]{2,1,0:T(8,128)(2,1)} %bitcast.6, bf16[16,16,256]{2,1,0:T(8,128)(2,1)} %bitcast.7), custom_call_target="tpu_custom_call" | custom-call | bytes 655360 | tf_op jit(solution)/shard_map/pack/pallas_call | solution.py:175
  5.7 0.0 copy-start.3
  5.8 4.0 %all-to-all-start = ((bf16[8,80,256]{2,1,0:T(8,128)(2,1)}), bf16[8,80,256]{2,1,0:T(8,128)(2,1)S(1)}, u32[]{:S(2)}, u32[]{:S(2)}) async-start(bf16[8,80,256]{2,1,0:T(8,128)(2,1)} %pack.1), calls=%async_computation | async-start | bytes 655360 | tf_op jit(solution)/shard_map/all_to_all | solution.py:186
  9.7 0.0 collective-permute-done
  9.7 1.6 %collective-permute-start.2 = (bf16[64,512]{1,0:T(8,128)(2,1)S(1)}, bf16[64,512]{1,0:T(8,128)(2,1)S(1)}, u32[]{:S(2)}, u32[]{:S(2)}) collective-permute-start(bf16[64,512]{1,0:T(8,128)(2,1)S(1)} %get-tuple-element.31), channel_id=1, source_target_pairs={{0,16},{16,0},{1,17},{17,1},{2,18},{18,2},{3,19},{19,3},{4,20},{20... | collective-permute-start | bytes 196616 | tf_op jit(solution)/shard_map/ppermute | solution.py:165
  11.3 2.0 %collective-permute-start.1 = (bf16[1,64,512]{2,1,0:T(8,128)(2,1)S(1)}, bf16[1,64,512]{2,1,0:T(8,128)(2,1)S(1)}, u32[]{:S(2)}, u32[]{:S(2)}) collective-permute-start(bf16[1,64,512]{2,1,0:T(8,128)(2,1)S(1)} %get-tuple-element.32), channel_id=1, source_target_pairs={{0,2},{1,3},{2,0},{3,1},{4,6},{5,7},{6,4},{7,5},{8,10},{9,11},{10,... | collective-permute-start | bytes 196616 | tf_op jit(solution)/shard_map/ppermute | solution.py:162
  13.3 1.0 %collective-permute-done.2 = bf16[64,512]{1,0:T(8,128)(2,1)S(1)} collective-permute-done((bf16[64,512]{1,0:T(8,128)(2,1)S(1)}, bf16[64,512]{1,0:T(8,128)(2,1)S(1)}, u32[]{:S(2)}, u32[]{:S(2)}) %collective-permute-start.2) | collective-permute-done | bytes 65568 | tf_op jit(solution)/shard_map/ppermute | solution.py:165
  14.3 1.8 %collective-permute-start.3 = (bf16[1,64,512]{2,1,0:T(8,128)(2,1)S(1)}, bf16[1,64,512]{2,1,0:T(8,128)(2,1)S(1)}, u32[]{:S(2)}, u32[]{:S(2)}) collective-permute-start(bf16[1,64,512]{2,1,0:T(8,128)(2,1)S(1)} %bitcast.8), channel_id=1, source_target_pairs={{0,4},{1,5},{2,6},{3,7},{4,0},{5,1},{6,2},{7,3},{8,12},{9,13},{10,... | collective-permute-start | bytes 196616 | tf_op jit(solution)/shard_map/ppermute | solution.py:162
  16.1 1.8 %collective-permute-done.1 = bf16[1,64,512]{2,1,0:T(8,128)(2,1)S(1)} collective-permute-done((bf16[1,64,512]{2,1,0:T(8,128)(2,1)S(1)}, bf16[1,64,512]{2,1,0:T(8,128)(2,1)S(1)}, u32[]{:S(2)}, u32[]{:S(2)}) %collective-permute-start.1) | collective-permute-done | bytes 65568 | tf_op jit(solution)/shard_map/ppermute | solution.py:162
  17.9 0.0 copy-start.1
  17.9 0.7 collective-permute-done.3
  18.6 0.7 pick.1
  19.3 0.4 collective-permute-start.4
  19.8 2.7 %collective-permute-start.5 = (bf16[4,80,256]{2,1,0:T(8,128)(2,1)S(1)}, bf16[4,80,256]{2,1,0:T(8,128)(2,1)S(1)}, u32[]{:S(2)}, u32[]{:S(2)}) collective-permute-start(bf16[4,80,256]{2,1,0:T(8,128)(2,1)S(1)} %slice.9), channel_id=1, source_target_pairs={{0,8},{1,9},{2,10},{3,11},{4,12},{5,13},{6,14},{7,15},{8,0},{9,1},... | collective-permute-start | bytes 491528 | tf_op jit(solution)/shard_map/ppermute | solution.py:162
  22.4 5.6 %collective-permute-done.4.refs_0_ = bf16[1,80,256]{2,1,0:T(8,128)(2,1)S(1)} collective-permute-done((bf16[1,80,256]{2,1,0:T(8,128)(2,1)S(1)}, bf16[1,80,256]{2,1,0:T(8,128)(2,1)S(1)}, u32[]{:S(2)}, u32[]{:S(2)}) %collective-permute-start.4) | collective-permute-done | bytes 40992 | tf_op jit(solution)/shard_map/ppermute | solution.py:162
  28.0 0.1 collective-permute-start.13
  28.2 0.1 collective-permute-start.14
  28.2 3.0 %collective-permute-done.5.refs_1_ = bf16[4,80,256]{2,1,0:T(8,128)(2,1)S(1)} collective-permute-done((bf16[4,80,256]{2,1,0:T(8,128)(2,1)S(1)}, bf16[4,80,256]{2,1,0:T(8,128)(2,1)S(1)}, u32[]{:S(2)}, u32[]{:S(2)}) %collective-permute-start.5) | collective-permute-done | bytes 163872 | tf_op jit(solution)/shard_map/ppermute | solution.py:162
  31.2 0.6 order.1
  31.9 1.6 %collective-permute-start.6 = (bf16[1,2,80,256]{3,2,1,0:T(8,128)(2,1)S(1)}, bf16[1,2,80,256]{3,2,1,0:T(8,128)(2,1)S(1)}, u32[]{:S(2)}, u32[]{:S(2)}) collective-permute-start(bf16[1,2,80,256]{3,2,1,0:T(8,128)(2,1)S(1)} %get-tuple-element.22), channel_id=1, source_target_pairs={{0,16},{16,0},{1,17},{17,1},{2,18},{18,2},{3,19},{19,3},{4,20},{20... | collective-permute-start | bytes 245768 | tf_op jit(solution)/shard_map/ppermute | solution.py:165
  33.4 0.7 collective-permute-start.8
  34.1 0.3 collective-permute-start.10
  34.5 0.1 collective-permute-start.15
  34.6 1.8 %collective-permute-done.6 = bf16[1,2,80,256]{3,2,1,0:T(8,128)(2,1)S(1)} collective-permute-done((bf16[1,2,80,256]{3,2,1,0:T(8,128)(2,1)S(1)}, bf16[1,2,80,256]{3,2,1,0:T(8,128)(2,1)S(1)}, u32[]{:S(2)}, u32[]{:S(2)}) %collective-permute-start.6) | collective-permute-done | bytes 81952 | tf_op jit(solution)/shard_map/ppermute | solution.py:165
  36.4 0.9 %collective-permute-start.7 = (bf16[2,2,80,256]{3,2,1,0:T(8,128)(2,1)S(1)}, bf16[2,2,80,256]{3,2,1,0:T(8,128)(2,1)S(1)}, u32[]{:S(2)}, u32[]{:S(2)}) collective-permute-start(bf16[2,2,80,256]{3,2,1,0:T(8,128)(2,1)S(1)} %pad_maximum_fusion.3), channel_id=1, source_target_pairs={{0,2},{1,3},{2,0},{3,1},{4,6},{5,7},{6,4},{7,5},{8,10},{9,11},{10,... | collective-permute-start | bytes 491528 | tf_op jit(solution)/shard_map/ppermute | solution.py:162
  37.3 0.7 %collective-permute-done.8 = bf16[1,2,80,256]{3,2,1,0:T(8,128)(2,1)S(1)} collective-permute-done((bf16[1,2,80,256]{3,2,1,0:T(8,128)(2,1)S(1)}, bf16[1,2,80,256]{3,2,1,0:T(8,128)(2,1)S(1)}, u32[]{:S(2)}, u32[]{:S(2)}) %collective-permute-start.8) | collective-permute-done | bytes 81952 | tf_op jit(solution)/shard_map/ppermute | solution.py:162
  38.0 0.1 collective-permute-start.9
  38.1 0.4 collective-permute-done.10
  38.6 1.0 %collective-permute-start.11 = (bf16[2,2,80,256]{3,2,1,0:T(8,128)(2,1)S(1)}, bf16[2,2,80,256]{3,2,1,0:T(8,128)(2,1)S(1)}, u32[]{:S(2)}, u32[]{:S(2)}) collective-permute-start(bf16[2,2,80,256]{3,2,1,0:T(8,128)(2,1)S(1)} %pad_maximum_fusion.5), channel_id=1, source_target_pairs={{0,16},{16,0},{1,17},{17,1},{2,18},{18,2},{3,19},{19,3},{4,20},{20... | collective-permute-start | bytes 491528 | tf_op jit(solution)/shard_map/ppermute | solution.py:165
  39.6 2.2 %collective-permute-done.7 = bf16[2,2,80,256]{3,2,1,0:T(8,128)(2,1)S(1)} collective-permute-done((bf16[2,2,80,256]{3,2,1,0:T(8,128)(2,1)S(1)}, bf16[2,2,80,256]{3,2,1,0:T(8,128)(2,1)S(1)}, u32[]{:S(2)}, u32[]{:S(2)}) %collective-permute-start.7) | collective-permute-done | bytes 163872 | tf_op jit(solution)/shard_map/ppermute | solution.py:162
  41.9 1.1 %merge.1 = f32[128,128]{1,0:T(8,128)} custom-call(bf16[4096,128]{1,0:T(8,128)(2,1)S(1)} %copy-done, bf16[4,64,512]{2,1,0:T(8,128)(2,1)S(1)} %constant_dynamic-update-slice_fusion.refs_0_, bf16[4,64,512]{2,1,0:T(8,128)(2,1)S(1)} %constant_dynamic-update-slice_fusion.2.refs_1_, bf16[4,64,512]{2,1,0:T(8,128)(2,1)S(1)} %collective-permute-done.14.refs_2_, ...), custom_call_target="tpu_custom_call" | custom-call | flops 134217728 | bytes 1048576 | tf_op jit(solution)/shard_map/merge/pallas_call | solution.py:236
  42.9 4.2 %all-to-all-start.1 = ((f32[32,4,128]{2,1,0:T(4,128)}), f32[32,4,128]{2,1,0:T(4,128)S(1)}, u32[]{:S(2)}, u32[]{:S(2)}) async-start(f32[32,4,128]{2,1,0:T(4,128)} %bitcast.4), calls=%async_computation.1 | async-start | bytes 131072 | tf_op jit(solution)/shard_map/all_to_all | solution.py:267
  47.2 0.0 copy-start.2
  47.3 7.3 %all-to-all-done.1.start = f32[32,4,128]{2,1,0:T(4,128)S(1)} async-done(((f32[32,4,128]{2,1,0:T(4,128)}), f32[32,4,128]{2,1,0:T(4,128)S(1)}, u32[]{:S(2)}, u32[]{:S(2)}) %all-to-all-start.1) | async-done | bytes 65568 | tf_op jit(solution)/shard_map/all_to_all | solution.py:267
  54.6 0.1 collective-permute-start.17
  54.7 0.4 collective-permute-start.16
  55.1 0.7 collective-permute-start.19
  55.7 0.7 collective-permute-start.22
  56.4 0.5 collective-permute-start.23
  56.9 7.8 %collective-permute-done.16.refs_1_ = bf16[4,2,80,256]{3,2,1,0:T(8,128)(2,1)S(1)} collective-permute-done((bf16[4,2,80,256]{3,2,1,0:T(8,128)(2,1)S(1)}, bf16[4,2,80,256]{3,2,1,0:T(8,128)(2,1)S(1)}, u32[]{:S(2)}, u32[]{:S(2)}) %collective-permute-start.16) | collective-permute-done | bytes 327712 | tf_op jit(solution)/shard_map/ppermute | solution.py:162
  64.7 0.1 collective-permute-done.19.refs_5_
  64.8 0.4 collective-permute-start.21
  65.2 0.1 collective-permute-start.24
  65.3 1.0 %collective-permute-done.18.refs_3_ = bf16[4,2,80,256]{3,2,1,0:T(8,128)(2,1)S(1)} collective-permute-done((bf16[4,2,80,256]{3,2,1,0:T(8,128)(2,1)S(1)}, bf16[4,2,80,256]{3,2,1,0:T(8,128)(2,1)S(1)}, u32[]{:S(2)}, u32[]{:S(2)}) %collective-permute-start.18) | collective-permute-done | bytes 327712 | tf_op jit(solution)/shard_map/ppermute | solution.py:162
  66.3 0.5 collective-permute-done.21.refs_7_
  66.8 0.5 collective-permute-done.24.refs_11_
  67.3 5.1 %chain0.1 = bf16[4,2048]{1,0:T(4,128)(2,1)} custom-call(s32[6]{0:T(128)S(1)} %copy-done.2, f32[32,4,128]{2,1,0:T(4,128)S(1)} %all-to-all-done.1.start, bf16[4,2,80,256]{3,2,1,0:T(8,128)(2,1)S(1)} %pad_maximum_fusion.refs_0_, bf16[4,2,80,256]{3,2,1,0:T(8,128)(2,1)S(1)} %collective-permute-done.16.refs_1_, ...), custom_call_target="tpu_custom_call" | custom-call | flops 201326592 | bytes 3932160 | tf_op jit(solution)/shard_map/chain0/pallas_call | solution.py:285
  (34 shorter events, 0.3 us)
Async XLA Ops:
  0.0 9.7 %collective-permute-start = (bf16[64,512]{1,0:T(8,128)(2,1)}, bf16[64,512]{1,0:T(8,128)(2,1)S(1)}, u32[]{:S(2)}, u32[]{:S(2)}) collective-permute-start(bf16[64,512]{1,0:T(8,128)(2,1)} %param.7), channel_id=1, source_target_pairs={{0,8},{1,9},{2,10},{3,11},{4,12},{5,13},{6,14},{7,15},{8,0},{9,1},... | collective-permute-start | bytes 196616 | tf_op jit(solution)/shard_map/ppermute | solution.py:162
  5.7 4.0 %copy-start.3 = (bf16[64,512]{1,0:T(8,128)(2,1)S(1)}, bf16[64,512]{1,0:T(8,128)(2,1)}, u32[]{:S(2)}) copy-start(bf16[64,512]{1,0:T(8,128)(2,1)} %param.7) | copy-start | bytes 196612
  5.8 12.8 %all-to-all-start = ((bf16[8,80,256]{2,1,0:T(8,128)(2,1)}), bf16[8,80,256]{2,1,0:T(8,128)(2,1)S(1)}, u32[]{:S(2)}, u32[]{:S(2)}) async-start(bf16[8,80,256]{2,1,0:T(8,128)(2,1)} %pack.1), calls=%async_computation | async-start | bytes 655360 | tf_op jit(solution)/shard_map/all_to_all | solution.py:186
  9.7 4.6 %collective-permute-start.2 = (bf16[64,512]{1,0:T(8,128)(2,1)S(1)}, bf16[64,512]{1,0:T(8,128)(2,1)S(1)}, u32[]{:S(2)}, u32[]{:S(2)}) collective-permute-start(bf16[64,512]{1,0:T(8,128)(2,1)S(1)} %get-tuple-element.31), channel_id=1, source_target_pairs={{0,16},{16,0},{1,17},{17,1},{2,18},{18,2},{3,19},{19,3},{4,20},{20... | collective-permute-start | bytes 196616 | tf_op jit(solution)/shard_map/ppermute | solution.py:165
  11.3 6.5 %collective-permute-start.1 = (bf16[1,64,512]{2,1,0:T(8,128)(2,1)S(1)}, bf16[1,64,512]{2,1,0:T(8,128)(2,1)S(1)}, u32[]{:S(2)}, u32[]{:S(2)}) collective-permute-start(bf16[1,64,512]{2,1,0:T(8,128)(2,1)S(1)} %get-tuple-element.32), channel_id=1, source_target_pairs={{0,2},{1,3},{2,0},{3,1},{4,6},{5,7},{6,4},{7,5},{8,10},{9,11},{10,... | collective-permute-start | bytes 196616 | tf_op jit(solution)/shard_map/ppermute | solution.py:162
  14.3 4.3 %collective-permute-start.3 = (bf16[1,64,512]{2,1,0:T(8,128)(2,1)S(1)}, bf16[1,64,512]{2,1,0:T(8,128)(2,1)S(1)}, u32[]{:S(2)}, u32[]{:S(2)}) collective-permute-start(bf16[1,64,512]{2,1,0:T(8,128)(2,1)S(1)} %bitcast.8), channel_id=1, source_target_pairs={{0,4},{1,5},{2,6},{3,7},{4,0},{5,1},{6,2},{7,3},{8,12},{9,13},{10,... | collective-permute-start | bytes 196616 | tf_op jit(solution)/shard_map/ppermute | solution.py:162
  17.9 0.7 %copy-start.1 = (s32[6]{0:T(128)S(1)}, s32[6]{0:T(128)}, u32[]{:S(2)}) copy-start(s32[6]{0:T(128)} %owners.3) | copy-start | bytes 76
  19.3 8.7 %collective-permute-start.4 = (bf16[1,80,256]{2,1,0:T(8,128)(2,1)S(1)}, bf16[1,80,256]{2,1,0:T(8,128)(2,1)S(1)}, u32[]{:S(2)}, u32[]{:S(2)}) collective-permute-start(bf16[1,80,256]{2,1,0:T(8,128)(2,1)S(1)} %slice.8), channel_id=1, source_target_pairs={{0,8},{1,9},{2,10},{3,11},{4,12},{5,13},{6,14},{7,15},{8,0},{9,1},... | collective-permute-start | bytes 122888 | tf_op jit(solution)/shard_map/ppermute | solution.py:162
  19.8 11.5 %collective-permute-start.5 = (bf16[4,80,256]{2,1,0:T(8,128)(2,1)S(1)}, bf16[4,80,256]{2,1,0:T(8,128)(2,1)S(1)}, u32[]{:S(2)}, u32[]{:S(2)}) collective-permute-start(bf16[4,80,256]{2,1,0:T(8,128)(2,1)S(1)} %slice.9), channel_id=1, source_target_pairs={{0,8},{1,9},{2,10},{3,11},{4,12},{5,13},{6,14},{7,15},{8,0},{9,1},... | collective-permute-start | bytes 491528 | tf_op jit(solution)/shard_map/ppermute | solution.py:162
  28.0 6.1 %collective-permute-start.12 = (bf16[2,64,512]{2,1,0:T(8,128)(2,1)S(1)}, bf16[2,64,512]{2,1,0:T(8,128)(2,1)S(1)}, u32[]{:S(2)}, u32[]{:S(2)}) collective-permute-start(bf16[2,64,512]{2,1,0:T(8,128)(2,1)S(1)} %pad_maximum_fusion.6), channel_id=1, source_target_pairs={{0,4},{1,5},{2,6},{3,7},{4,0},{5,1},{6,2},{7,3},{8,12},{9,13},{10,... | collective-permute-start | bytes 393224 | tf_op jit(solution)/shard_map/ppermute | solution.py:162
  28.0 6.4 %collective-permute-start.13 = (bf16[2,64,512]{2,1,0:T(8,128)(2,1)S(1)}, bf16[2,64,512]{2,1,0:T(8,128)(2,1)S(1)}, u32[]{:S(2)}, u32[]{:S(2)}) collective-permute-start(bf16[2,64,512]{2,1,0:T(8,128)(2,1)S(1)} %pad_maximum_fusion.7), channel_id=1, source_target_pairs={{0,2},{1,3},{2,0},{3,1},{4,6},{5,7},{6,4},{7,5},{8,10},{9,11},{10,... | collective-permute-start | bytes 393224 | tf_op jit(solution)/shard_map/ppermute | solution.py:162
  28.2 13.7 %collective-permute-start.14 = (bf16[4,64,512]{2,1,0:T(8,128)(2,1)S(1)}, bf16[4,64,512]{2,1,0:T(8,128)(2,1)S(1)}, u32[]{:S(2)}, u32[]{:S(2)}) collective-permute-start(bf16[4,64,512]{2,1,0:T(8,128)(2,1)S(1)} %constant_dynamic-update-slice_fusion.refs_0_), channel_id=1, source_target_pairs={{0,1},{1,0},{2,3},{3,2},{4,5},{5,4},{6,7},{7,6},{8,9},{9,8},{10,11... | collective-permute-start | bytes 786440 | tf_op jit(solution)/shard_map/ppermute | solution.py:162
  31.9 4.5 %collective-permute-start.6 = (bf16[1,2,80,256]{3,2,1,0:T(8,128)(2,1)S(1)}, bf16[1,2,80,256]{3,2,1,0:T(8,128)(2,1)S(1)}, u32[]{:S(2)}, u32[]{:S(2)}) collective-permute-start(bf16[1,2,80,256]{3,2,1,0:T(8,128)(2,1)S(1)} %get-tuple-element.22), channel_id=1, source_target_pairs={{0,16},{16,0},{1,17},{17,1},{2,18},{18,2},{3,19},{19,3},{4,20},{20... | collective-permute-start | bytes 245768 | tf_op jit(solution)/shard_map/ppermute | solution.py:165
  33.4 4.6 %collective-permute-start.8 = (bf16[1,2,80,256]{3,2,1,0:T(8,128)(2,1)S(1)}, bf16[1,2,80,256]{3,2,1,0:T(8,128)(2,1)S(1)}, u32[]{:S(2)}, u32[]{:S(2)}) collective-permute-start(bf16[1,2,80,256]{3,2,1,0:T(8,128)(2,1)S(1)} %get-tuple-element.23), channel_id=1, source_target_pairs={{0,2},{1,3},{2,0},{3,1},{4,6},{5,7},{6,4},{7,5},{8,10},{9,11},{10,... | collective-permute-start | bytes 245768 | tf_op jit(solution)/shard_map/ppermute | solution.py:162
  34.1 7.7 %copy-start = (bf16[4096,128]{1,0:T(8,128)(2,1)S(1)}, bf16[4096,128]{1,0:T(8,128)(2,1)}, u32[]{:S(2)}) copy-start(bf16[4096,128]{1,0:T(8,128)(2,1)} %sub.6) | copy-start | bytes 3145732
  34.1 4.4 %collective-permute-start.10 = (bf16[1,2,80,256]{3,2,1,0:T(8,128)(2,1)S(1)}, bf16[1,2,80,256]{3,2,1,0:T(8,128)(2,1)S(1)}, u32[]{:S(2)}, u32[]{:S(2)}) collective-permute-start(bf16[1,2,80,256]{3,2,1,0:T(8,128)(2,1)S(1)} %get-tuple-element.24), channel_id=1, source_target_pairs={{0,4},{1,5},{2,6},{3,7},{4,0},{5,1},{6,2},{7,3},{8,12},{9,13},{10,... | collective-permute-start | bytes 245768 | tf_op jit(solution)/shard_map/ppermute | solution.py:162
  34.5 7.3 %collective-permute-start.15 = (bf16[4,64,512]{2,1,0:T(8,128)(2,1)S(1)}, bf16[4,64,512]{2,1,0:T(8,128)(2,1)S(1)}, u32[]{:S(2)}, u32[]{:S(2)}) collective-permute-start(bf16[4,64,512]{2,1,0:T(8,128)(2,1)S(1)} %constant_dynamic-update-slice_fusion.2.refs_1_), channel_id=1, source_target_pairs={{0,1},{1,0},{2,3},{3,2},{4,5},{5,4},{6,7},{7,6},{8,9},{9,8},{10,11... | collective-permute-start | bytes 786440 | tf_op jit(solution)/shard_map/ppermute | solution.py:162
  36.4 5.4 %collective-permute-start.7 = (bf16[2,2,80,256]{3,2,1,0:T(8,128)(2,1)S(1)}, bf16[2,2,80,256]{3,2,1,0:T(8,128)(2,1)S(1)}, u32[]{:S(2)}, u32[]{:S(2)}) collective-permute-start(bf16[2,2,80,256]{3,2,1,0:T(8,128)(2,1)S(1)} %pad_maximum_fusion.3), channel_id=1, source_target_pairs={{0,2},{1,3},{2,0},{3,1},{4,6},{5,7},{6,4},{7,5},{8,10},{9,11},{10,... | collective-permute-start | bytes 491528 | tf_op jit(solution)/shard_map/ppermute | solution.py:162
  38.0 9.1 %collective-permute-start.9 = (bf16[2,2,80,256]{3,2,1,0:T(8,128)(2,1)S(1)}, bf16[2,2,80,256]{3,2,1,0:T(8,128)(2,1)S(1)}, u32[]{:S(2)}, u32[]{:S(2)}) collective-permute-start(bf16[2,2,80,256]{3,2,1,0:T(8,128)(2,1)S(1)} %pad_maximum_fusion.4), channel_id=1, source_target_pairs={{0,4},{1,5},{2,6},{3,7},{4,0},{5,1},{6,2},{7,3},{8,12},{9,13},{10,... | collective-permute-start | bytes 491528 | tf_op jit(solution)/shard_map/ppermute | solution.py:162
  38.6 8.7 %collective-permute-start.11 = (bf16[2,2,80,256]{3,2,1,0:T(8,128)(2,1)S(1)}, bf16[2,2,80,256]{3,2,1,0:T(8,128)(2,1)S(1)}, u32[]{:S(2)}, u32[]{:S(2)}) collective-permute-start(bf16[2,2,80,256]{3,2,1,0:T(8,128)(2,1)S(1)} %pad_maximum_fusion.5), channel_id=1, source_target_pairs={{0,16},{16,0},{1,17},{17,1},{2,18},{18,2},{3,19},{19,3},{4,20},{20... | collective-permute-start | bytes 491528 | tf_op jit(solution)/shard_map/ppermute | solution.py:165
  42.9 11.7 %all-to-all-start.1 = ((f32[32,4,128]{2,1,0:T(4,128)}), f32[32,4,128]{2,1,0:T(4,128)S(1)}, u32[]{:S(2)}, u32[]{:S(2)}) async-start(f32[32,4,128]{2,1,0:T(4,128)} %bitcast.4), calls=%async_computation.1 | async-start | bytes 131072 | tf_op jit(solution)/shard_map/all_to_all | solution.py:267
  47.2 20.1 %copy-start.2 = (s32[6]{0:T(128)S(1)}, s32[6]{0:T(128)}, u32[]{:S(2)}) copy-start(s32[6]{0:T(128)} %offsets.1) | copy-start | bytes 76
  54.6 1.9 %collective-permute-start.17 = (bf16[4,2,80,256]{3,2,1,0:T(8,128)(2,1)S(1)}, bf16[4,2,80,256]{3,2,1,0:T(8,128)(2,1)S(1)}, u32[]{:S(2)}, u32[]{:S(2)}) collective-permute-start(bf16[4,2,80,256]{3,2,1,0:T(8,128)(2,1)S(1)} %pad_maximum_fusion.refs_0_), channel_id=1, source_target_pairs={{0,1},{1,0},{2,3},{3,2},{4,5},{5,4},{6,7},{7,6},{8,9},{9,8},{10,11... | collective-permute-start | bytes 983048 | tf_op jit(solution)/shard_map/ppermute | solution.py:162
  54.7 10.0 %collective-permute-start.16 = (bf16[4,2,80,256]{3,2,1,0:T(8,128)(2,1)S(1)}, bf16[4,2,80,256]{3,2,1,0:T(8,128)(2,1)S(1)}, u32[]{:S(2)}, u32[]{:S(2)}) collective-permute-start(bf16[4,2,80,256]{3,2,1,0:T(8,128)(2,1)S(1)} %pad_maximum_fusion.refs_0_), channel_id=1, source_target_pairs={{0,4},{1,5},{2,6},{3,7},{4,0},{5,1},{6,2},{7,3},{8,12},{9,13},{10,... | collective-permute-start | bytes 983048 | tf_op jit(solution)/shard_map/ppermute | solution.py:162
  55.1 9.7 %collective-permute-start.19 = (bf16[4,2,80,256]{3,2,1,0:T(8,128)(2,1)S(1)}, bf16[4,2,80,256]{3,2,1,0:T(8,128)(2,1)S(1)}, u32[]{:S(2)}, u32[]{:S(2)}) collective-permute-start(bf16[4,2,80,256]{3,2,1,0:T(8,128)(2,1)S(1)} %pad_maximum_fusion.1.refs_4_), channel_id=1, source_target_pairs={{0,16},{16,0},{1,17},{17,1},{2,18},{18,2},{3,19},{19,3},{4,20},{20... | collective-permute-start | bytes 983048 | tf_op jit(solution)/shard_map/ppermute | solution.py:165
  55.7 9.5 %collective-permute-start.22 = (bf16[4,2,80,256]{3,2,1,0:T(8,128)(2,1)S(1)}, bf16[4,2,80,256]{3,2,1,0:T(8,128)(2,1)S(1)}, u32[]{:S(2)}, u32[]{:S(2)}) collective-permute-start(bf16[4,2,80,256]{3,2,1,0:T(8,128)(2,1)S(1)} %pad_maximum_fusion.2.refs_8_), channel_id=1, source_target_pairs={{0,2},{1,3},{2,0},{3,1},{4,6},{5,7},{6,4},{7,5},{8,10},{9,11},{10,... | collective-permute-start | bytes 983048 | tf_op jit(solution)/shard_map/ppermute | solution.py:162
  56.4 8.9 %collective-permute-start.20 = (bf16[4,2,80,256]{3,2,1,0:T(8,128)(2,1)S(1)}, bf16[4,2,80,256]{3,2,1,0:T(8,128)(2,1)S(1)}, u32[]{:S(2)}, u32[]{:S(2)}) collective-permute-start(bf16[4,2,80,256]{3,2,1,0:T(8,128)(2,1)S(1)} %pad_maximum_fusion.1.refs_4_), channel_id=1, source_target_pairs={{0,1},{1,0},{2,3},{3,2},{4,5},{5,4},{6,7},{7,6},{8,9},{9,8},{10,11... | collective-permute-start | bytes 983048 | tf_op jit(solution)/shard_map/ppermute | solution.py:162
  56.4 8.9 %collective-permute-start.23 = (bf16[4,2,80,256]{3,2,1,0:T(8,128)(2,1)S(1)}, bf16[4,2,80,256]{3,2,1,0:T(8,128)(2,1)S(1)}, u32[]{:S(2)}, u32[]{:S(2)}) collective-permute-start(bf16[4,2,80,256]{3,2,1,0:T(8,128)(2,1)S(1)} %pad_maximum_fusion.2.refs_8_), channel_id=1, source_target_pairs={{0,1},{1,0},{2,3},{3,2},{4,5},{5,4},{6,7},{7,6},{8,9},{9,8},{10,11... | collective-permute-start | bytes 983048 | tf_op jit(solution)/shard_map/ppermute | solution.py:162
  64.7 1.6 %collective-permute-start.18 = (bf16[4,2,80,256]{3,2,1,0:T(8,128)(2,1)S(1)}, bf16[4,2,80,256]{3,2,1,0:T(8,128)(2,1)S(1)}, u32[]{:S(2)}, u32[]{:S(2)}) collective-permute-start(bf16[4,2,80,256]{3,2,1,0:T(8,128)(2,1)S(1)} %collective-permute-done.16.refs_1_), channel_id=1, source_target_pairs={{0,1},{1,0},{2,3},{3,2},{4,5},{5,4},{6,7},{7,6},{8,9},{9,8},{10,11... | collective-permute-start | bytes 983048 | tf_op jit(solution)/shard_map/ppermute | solution.py:162
  64.8 2.0 %collective-permute-start.21 = (bf16[4,2,80,256]{3,2,1,0:T(8,128)(2,1)S(1)}, bf16[4,2,80,256]{3,2,1,0:T(8,128)(2,1)S(1)}, u32[]{:S(2)}, u32[]{:S(2)}) collective-permute-start(bf16[4,2,80,256]{3,2,1,0:T(8,128)(2,1)S(1)} %collective-permute-done.19.refs_5_), channel_id=1, source_target_pairs={{0,1},{1,0},{2,3},{3,2},{4,5},{5,4},{6,7},{7,6},{8,9},{9,8},{10,11... | collective-permute-start | bytes 983048 | tf_op jit(solution)/shard_map/ppermute | solution.py:162
  65.2 2.0 %collective-permute-start.24 = (bf16[4,2,80,256]{3,2,1,0:T(8,128)(2,1)S(1)}, bf16[4,2,80,256]{3,2,1,0:T(8,128)(2,1)S(1)}, u32[]{:S(2)}, u32[]{:S(2)}) collective-permute-start(bf16[4,2,80,256]{3,2,1,0:T(8,128)(2,1)S(1)} %collective-permute-done.22.refs_9_), channel_id=1, source_target_pairs={{0,1},{1,0},{2,3},{3,2},{4,5},{5,4},{6,7},{7,6},{8,9},{9,8},{10,11... | collective-permute-start | bytes 983048 | tf_op jit(solution)/shard_map/ppermute | solution.py:162

commit v24 on v23

--- a/solution.py
+++ b/solution.py
@@ -265,13 +265,13 @@
             colours[k] = jnp.concatenate([colours[k], send(colours[k])])
             masks[k] = masks[k] + [m ^ mask for m in masks[k]]
     state = lax.all_to_all(merged.reshape(rows * cols, each, width), ("row", "col"), 0, 0)
-    colours, state = lax.optimization_barrier((colours, state))
     last_round = []
     for k in range(COLOURS):
         mask, send = links[(k + 2) % 3]
         last_round.append(send(colours[k]))
         masks[k] = [masks[k], [m ^ mask for m in masks[k]]]
         masks[k] += [[m ^ 1 for m in ms] for ms in masks[k]]
+    last_round, state = lax.optimization_barrier((last_round, state))
     held = []
     for k in range(COLOURS):
         held.append([colours[k], last_round[k], over_col(colours[k], 1), over_col(last_round[k], 1)])

time: 72.6 us -> 68 us (0.937)
  waiting for transfers between devices: 34.4 us -> 28.3 us
  starting transfers between devices: 28.3 us -> 29.7 us
    ppermute x21, waiting for transfers between devices: 24.2 us -> 14.3 us  [over_col(): return lax.ppermute(x, 'col', [(c, c ^ mask) for c in range(cols)])]
    ppermute x4, waiting for transfers between devices: 2.85 us -> 7.16 us  [over_row(): return lax.ppermute(x, 'row', [(r, r ^ mask) for r in range(rows)])]
    ppermute x21, starting transfers between devices: 15.3 us -> 17.8 us  [over_col(): return lax.ppermute(x, 'col', [(c, c ^ mask) for c in range(cols)])]
  transfers between devices with their start and end apart: 27 -> 27, of which waited for: 15 -> 13; matrix products, arithmetic and copies ran while one was open for 0% -> 0% of each run, Pallas kernels for 5% -> 5%
where the time goes in v24:
time: 68 us; the launch traced here: 67.7 us
  starting transfers between devices  29.7 us (44%)
  waiting for transfers between devices  28.3 us (42%)
  Pallas kernels  9.18 us (14%)
    ppermute x21, starting transfers between devices, over_col(): return lax.ppermute(x, 'col', [(c, c ^ mask) for c in range(cols)])  17.8 us
    ppermute x21, waiting for transfers between devices, over_col(): return lax.ppermute(x, 'col', [(c, c ^ mask) for c in range(cols)])  14.3 us
    ppermute x4, waiting for transfers between devices, over_row(): return lax.ppermute(x, 'row', [(r, r ^ mask) for r in range(rows)])  7.16 us
    all_to_all x1, waiting for transfers between devices, local(): lax.all_to_all(merged.reshape(rows * cols, each, width), ('row', 'col'),...  6.83 us
    pallas_call x1, Pallas kernels, local(): pl.pallas_call(functools.partial(chain_kernel, cols, groups, slots, sum((...  5.08 us
    ppermute x4, starting transfers between devices, over_row(): return lax.ppermute(x, 'row', [(r, r ^ mask) for r in range(rows)])  4.24 us
    all_to_all x1, starting transfers between devices, local(): slices = lax.all_to_all(packed, 'col', 0, 0, axis_index_groups=members)  3.95 us
    all_to_all x1, starting transfers between devices, local(): lax.all_to_all(merged.reshape(rows * cols, each, width), ('row', 'col'),...  3.75 us
  transfers between devices with their start and end apart: 27, of which 13 were waited for; matrix products, arithmetic and copies ran while one was open for 0% of the time, Pallas kernels for 5%

profile of v24, /device:TPU:0, one launch (start us, length us, event | category | flops | bytes accessed | tf_op | source)
XLA Modules:
  0.0 67.7 jit_solution(9504650684960233844)
XLA Ops:
  0.0 4.0 %collective-permute-start = (bf16[64,512]{1,0:T(8,128)(2,1)}, bf16[64,512]{1,0:T(8,128)(2,1)S(1)}, u32[]{:S(2)}, u32[]{:S(2)}) collective-permute-start(bf16[64,512]{1,0:T(8,128)(2,1)} %param.7), channel_id=1, source_target_pairs={{0,8},{1,9},{2,10},{3,11},{4,12},{5,13},{6,14},{7,15},{8,0},{9,1},... | collective-permute-start | bytes 196616 | tf_op jit(solution)/shard_map/ppermute | solution.py:162
  4.0 1.7 %pack.1 = bf16[8,80,256]{2,1,0:T(8,128)(2,1)} custom-call(bf16[16,64,256]{2,1,0:T(8,128)(2,1)} %bitcast.6, bf16[16,16,256]{2,1,0:T(8,128)(2,1)} %bitcast.7), custom_call_target="tpu_custom_call" | custom-call | bytes 655360 | tf_op jit(solution)/shard_map/pack/pallas_call | solution.py:175
  5.7 0.0 copy-start.3
  5.8 4.0 %all-to-all-start = ((bf16[8,80,256]{2,1,0:T(8,128)(2,1)}), bf16[8,80,256]{2,1,0:T(8,128)(2,1)S(1)}, u32[]{:S(2)}, u32[]{:S(2)}) async-start(bf16[8,80,256]{2,1,0:T(8,128)(2,1)} %pack.1), calls=%async_computation | async-start | bytes 655360 | tf_op jit(solution)/shard_map/all_to_all | solution.py:186
  9.7 0.0 collective-permute-done
  9.7 1.6 %collective-permute-start.2 = (bf16[64,512]{1,0:T(8,128)(2,1)S(1)}, bf16[64,512]{1,0:T(8,128)(2,1)S(1)}, u32[]{:S(2)}, u32[]{:S(2)}) collective-permute-start(bf16[64,512]{1,0:T(8,128)(2,1)S(1)} %get-tuple-element.31), channel_id=1, source_target_pairs={{0,16},{16,0},{1,17},{17,1},{2,18},{18,2},{3,19},{19,3},{4,20},{20... | collective-permute-start | bytes 196616 | tf_op jit(solution)/shard_map/ppermute | solution.py:165
  11.3 2.0 %collective-permute-start.1 = (bf16[1,64,512]{2,1,0:T(8,128)(2,1)S(1)}, bf16[1,64,512]{2,1,0:T(8,128)(2,1)S(1)}, u32[]{:S(2)}, u32[]{:S(2)}) collective-permute-start(bf16[1,64,512]{2,1,0:T(8,128)(2,1)S(1)} %get-tuple-element.32), channel_id=1, source_target_pairs={{0,2},{1,3},{2,0},{3,1},{4,6},{5,7},{6,4},{7,5},{8,10},{9,11},{10,... | collective-permute-start | bytes 196616 | tf_op jit(solution)/shard_map/ppermute | solution.py:162
  13.3 1.0 %collective-permute-done.2 = bf16[64,512]{1,0:T(8,128)(2,1)S(1)} collective-permute-done((bf16[64,512]{1,0:T(8,128)(2,1)S(1)}, bf16[64,512]{1,0:T(8,128)(2,1)S(1)}, u32[]{:S(2)}, u32[]{:S(2)}) %collective-permute-start.2) | collective-permute-done | bytes 65568 | tf_op jit(solution)/shard_map/ppermute | solution.py:165
  14.3 1.8 %collective-permute-start.3 = (bf16[1,64,512]{2,1,0:T(8,128)(2,1)S(1)}, bf16[1,64,512]{2,1,0:T(8,128)(2,1)S(1)}, u32[]{:S(2)}, u32[]{:S(2)}) collective-permute-start(bf16[1,64,512]{2,1,0:T(8,128)(2,1)S(1)} %bitcast.8), channel_id=1, source_target_pairs={{0,4},{1,5},{2,6},{3,7},{4,0},{5,1},{6,2},{7,3},{8,12},{9,13},{10,... | collective-permute-start | bytes 196616 | tf_op jit(solution)/shard_map/ppermute | solution.py:162
  16.1 1.8 %collective-permute-done.1 = bf16[1,64,512]{2,1,0:T(8,128)(2,1)S(1)} collective-permute-done((bf16[1,64,512]{2,1,0:T(8,128)(2,1)S(1)}, bf16[1,64,512]{2,1,0:T(8,128)(2,1)S(1)}, u32[]{:S(2)}, u32[]{:S(2)}) %collective-permute-start.1) | collective-permute-done | bytes 65568 | tf_op jit(solution)/shard_map/ppermute | solution.py:162
  17.9 0.0 copy-start.1
  17.9 0.7 %collective-permute-done.3 = bf16[1,64,512]{2,1,0:T(8,128)(2,1)S(1)} collective-permute-done((bf16[1,64,512]{2,1,0:T(8,128)(2,1)S(1)}, bf16[1,64,512]{2,1,0:T(8,128)(2,1)S(1)}, u32[]{:S(2)}, u32[]{:S(2)}) %collective-permute-start.3) | collective-permute-done | bytes 65568 | tf_op jit(solution)/shard_map/ppermute | solution.py:162
  18.6 0.7 %pick.1 = bf16[5,80,256]{2,1,0:T(8,128)(2,1)S(1)} custom-call(s32[6]{0:T(128)S(1)} %copy-done.1, bf16[8,80,256]{2,1,0:T(8,128)(2,1)S(1)} %all-to-all-done.held), custom_call_target="tpu_custom_call" | custom-call | bytes 327680 | tf_op jit(solution)/shard_map/pick/pallas_call | solution.py:215
  19.3 0.4 collective-permute-start.4
  19.8 2.6 %collective-permute-start.5 = (bf16[4,80,256]{2,1,0:T(8,128)(2,1)S(1)}, bf16[4,80,256]{2,1,0:T(8,128)(2,1)S(1)}, u32[]{:S(2)}, u32[]{:S(2)}) collective-permute-start(bf16[4,80,256]{2,1,0:T(8,128)(2,1)S(1)} %slice.9), channel_id=1, source_target_pairs={{0,8},{1,9},{2,10},{3,11},{4,12},{5,13},{6,14},{7,15},{8,0},{9,1},... | collective-permute-start | bytes 491528 | tf_op jit(solution)/shard_map/ppermute | solution.py:162
  22.4 5.6 %collective-permute-done.4.refs_0_ = bf16[1,80,256]{2,1,0:T(8,128)(2,1)S(1)} collective-permute-done((bf16[1,80,256]{2,1,0:T(8,128)(2,1)S(1)}, bf16[1,80,256]{2,1,0:T(8,128)(2,1)S(1)}, u32[]{:S(2)}, u32[]{:S(2)}) %collective-permute-start.4) | collective-permute-done | bytes 40992 | tf_op jit(solution)/shard_map/ppermute | solution.py:162
  28.0 0.1 collective-permute-start.16
  28.1 0.1 collective-permute-start.17
  28.2 3.0 %collective-permute-done.5.refs_1_ = bf16[4,80,256]{2,1,0:T(8,128)(2,1)S(1)} collective-permute-done((bf16[4,80,256]{2,1,0:T(8,128)(2,1)S(1)}, bf16[4,80,256]{2,1,0:T(8,128)(2,1)S(1)}, u32[]{:S(2)}, u32[]{:S(2)}) %collective-permute-start.5) | collective-permute-done | bytes 163872 | tf_op jit(solution)/shard_map/ppermute | solution.py:162
  31.2 0.6 order.1
  31.9 1.6 %collective-permute-start.6 = (bf16[1,2,80,256]{3,2,1,0:T(8,128)(2,1)S(1)}, bf16[1,2,80,256]{3,2,1,0:T(8,128)(2,1)S(1)}, u32[]{:S(2)}, u32[]{:S(2)}) collective-permute-start(bf16[1,2,80,256]{3,2,1,0:T(8,128)(2,1)S(1)} %get-tuple-element.22), channel_id=1, source_target_pairs={{0,16},{16,0},{1,17},{17,1},{2,18},{18,2},{3,19},{19,3},{4,20},{20... | collective-permute-start | bytes 245768 | tf_op jit(solution)/shard_map/ppermute | solution.py:165
  33.4 0.7 %collective-permute-start.9 = (bf16[1,2,80,256]{3,2,1,0:T(8,128)(2,1)S(1)}, bf16[1,2,80,256]{3,2,1,0:T(8,128)(2,1)S(1)}, u32[]{:S(2)}, u32[]{:S(2)}) collective-permute-start(bf16[1,2,80,256]{3,2,1,0:T(8,128)(2,1)S(1)} %get-tuple-element.23), channel_id=1, source_target_pairs={{0,2},{1,3},{2,0},{3,1},{4,6},{5,7},{6,4},{7,5},{8,10},{9,11},{10,... | collective-permute-start | bytes 245768 | tf_op jit(solution)/shard_map/ppermute | solution.py:162
  34.1 0.0 collective-permute-done.15
  34.1 0.4 collective-permute-start.12
  34.6 0.1 collective-permute-start.18
  34.7 1.7 %collective-permute-done.6 = bf16[1,2,80,256]{3,2,1,0:T(8,128)(2,1)S(1)} collective-permute-done((bf16[1,2,80,256]{3,2,1,0:T(8,128)(2,1)S(1)}, bf16[1,2,80,256]{3,2,1,0:T(8,128)(2,1)S(1)}, u32[]{:S(2)}, u32[]{:S(2)}) %collective-permute-start.6) | collective-permute-done | bytes 81952 | tf_op jit(solution)/shard_map/ppermute | solution.py:165
  36.4 0.0 copy-start
  36.4 0.9 %collective-permute-start.7 = (bf16[2,2,80,256]{3,2,1,0:T(8,128)(2,1)S(1)}, bf16[2,2,80,256]{3,2,1,0:T(8,128)(2,1)S(1)}, u32[]{:S(2)}, u32[]{:S(2)}) collective-permute-start(bf16[2,2,80,256]{3,2,1,0:T(8,128)(2,1)S(1)} %pad_maximum_fusion), channel_id=1, source_target_pairs={{0,2},{1,3},{2,0},{3,1},{4,6},{5,7},{6,4},{7,5},{8,10},{9,11},{10,... | collective-permute-start | bytes 491528 | tf_op jit(solution)/shard_map/ppermute | solution.py:162
  37.3 0.6 collective-permute-done.9
  37.9 0.1 collective-permute-start.10
  38.0 0.7 collective-permute-done.12
  38.7 0.9 %collective-permute-start.13 = (bf16[2,2,80,256]{3,2,1,0:T(8,128)(2,1)S(1)}, bf16[2,2,80,256]{3,2,1,0:T(8,128)(2,1)S(1)}, u32[]{:S(2)}, u32[]{:S(2)}) collective-permute-start(bf16[2,2,80,256]{3,2,1,0:T(8,128)(2,1)S(1)} %pad_maximum_fusion.2), channel_id=1, source_target_pairs={{0,16},{16,0},{1,17},{17,1},{2,18},{18,2},{3,19},{19,3},{4,20},{20... | collective-permute-start | bytes 491528 | tf_op jit(solution)/shard_map/ppermute | solution.py:165
  39.6 4.5 %collective-permute-done.13 = bf16[2,2,80,256]{3,2,1,0:T(8,128)(2,1)S(1)} collective-permute-done((bf16[2,2,80,256]{3,2,1,0:T(8,128)(2,1)S(1)}, bf16[2,2,80,256]{3,2,1,0:T(8,128)(2,1)S(1)}, u32[]{:S(2)}, u32[]{:S(2)}) %collective-permute-start.13) | collective-permute-done | bytes 163872 | tf_op jit(solution)/shard_map/ppermute | solution.py:165
  44.1 1.8 %collective-permute-start.14 = (bf16[4,2,80,256]{3,2,1,0:T(8,128)(2,1)S(1)}, bf16[4,2,80,256]{3,2,1,0:T(8,128)(2,1)S(1)}, u32[]{:S(2)}, u32[]{:S(2)}) collective-permute-start(bf16[4,2,80,256]{3,2,1,0:T(8,128)(2,1)S(1)} %constant_dynamic-update-slice_fusion.6.refs_8_), channel_id=1, source_target_pairs={{0,2},{1,3},{2,0},{3,1},{4,6},{5,7},{6,4},{7,5},{8,10},{9,11},{10,... | collective-permute-start | bytes 983048 | tf_op jit(solution)/shard_map/ppermute | solution.py:162
  45.8 0.2 collective-permute-start.11
  46.1 1.6 %collective-permute-start.8 = (bf16[4,2,80,256]{3,2,1,0:T(8,128)(2,1)S(1)}, bf16[4,2,80,256]{3,2,1,0:T(8,128)(2,1)S(1)}, u32[]{:S(2)}, u32[]{:S(2)}) collective-permute-start(bf16[4,2,80,256]{3,2,1,0:T(8,128)(2,1)S(1)} %constant_dynamic-update-slice_fusion.refs_0_), channel_id=1, source_target_pairs={{0,4},{1,5},{2,6},{3,7},{4,0},{5,1},{6,2},{7,3},{8,12},{9,13},{10,... | collective-permute-start | bytes 983048 | tf_op jit(solution)/shard_map/ppermute | solution.py:162
  47.8 1.1 %merge.1 = f32[128,128]{1,0:T(8,128)} custom-call(bf16[4096,128]{1,0:T(8,128)(2,1)S(1)} %copy-done, bf16[4,64,512]{2,1,0:T(8,128)(2,1)S(1)} %constant_dynamic-update-slice_fusion.9.refs_0_, bf16[4,64,512]{2,1,0:T(8,128)(2,1)S(1)} %constant_dynamic-update-slice_fusion.11.refs_1_, bf16[4,64,512]{2,1,0:T(8,128)(2,1)S(1)} %collective-permute-done.17.refs_2_, ...), custom_call_target="tpu_custom_call" | custom-call | flops 134217728 | bytes 1048576 | tf_op jit(solution)/shard_map/merge/pallas_call | solution.py:236
  48.8 3.7 %all-to-all-start.1 = ((f32[32,4,128]{2,1,0:T(4,128)}), f32[32,4,128]{2,1,0:T(4,128)S(1)}, u32[]{:S(2)}, u32[]{:S(2)}) async-start(f32[32,4,128]{2,1,0:T(4,128)} %bitcast.4), calls=%async_computation.1 | async-start | bytes 131072 | tf_op jit(solution)/shard_map/all_to_all | solution.py:267
  52.6 0.3 collective-permute-start.21
  52.9 0.3 collective-permute-start.19
  53.2 6.8 %all-to-all-done.1.start = f32[32,4,128]{2,1,0:T(4,128)S(1)} async-done(((f32[32,4,128]{2,1,0:T(4,128)}), f32[32,4,128]{2,1,0:T(4,128)S(1)}, u32[]{:S(2)}, u32[]{:S(2)}) %all-to-all-start.1) | async-done | bytes 65568 | tf_op jit(solution)/shard_map/all_to_all | solution.py:267
  60.0 0.1 collective-permute-start.20
  60.1 0.4 collective-permute-start.22
  60.5 0.1 collective-permute-start.24
  60.7 1.0 %collective-permute-done.20.refs_3_ = bf16[4,2,80,256]{3,2,1,0:T(8,128)(2,1)S(1)} collective-permute-done((bf16[4,2,80,256]{3,2,1,0:T(8,128)(2,1)S(1)}, bf16[4,2,80,256]{3,2,1,0:T(8,128)(2,1)S(1)}, u32[]{:S(2)}, u32[]{:S(2)}) %collective-permute-start.20) | collective-permute-done | bytes 327712 | tf_op jit(solution)/shard_map/ppermute | solution.py:162
  61.7 0.5 collective-permute-done.22.refs_7_
  62.1 0.5 collective-permute-done.24.refs_11_
  62.6 5.1 %chain0.1 = bf16[4,2048]{1,0:T(4,128)(2,1)} custom-call(s32[6]{0:T(128)S(1)} %copy-done.2, f32[32,4,128]{2,1,0:T(4,128)S(1)} %all-to-all-done.1.start, bf16[4,2,80,256]{3,2,1,0:T(8,128)(2,1)S(1)} %constant_dynamic-update-slice_fusion.refs_0_, bf16[4,2,80,256]{3,2,1,0:T(8,128)(2,1)S(1)} %collective-permute-done.8.refs_1_, ...), custom_call_target="tpu_custom_call" | custom-call | flops 201326592 | bytes 3932160 | tf_op jit(solution)/shard_map/chain0/pallas_call | solution.py:285
  (39 shorter events, 0.3 us)
Async XLA Ops:
  0.0 9.7 %collective-permute-start = (bf16[64,512]{1,0:T(8,128)(2,1)}, bf16[64,512]{1,0:T(8,128)(2,1)S(1)}, u32[]{:S(2)}, u32[]{:S(2)}) collective-permute-start(bf16[64,512]{1,0:T(8,128)(2,1)} %param.7), channel_id=1, source_target_pairs={{0,8},{1,9},{2,10},{3,11},{4,12},{5,13},{6,14},{7,15},{8,0},{9,1},... | collective-permute-start | bytes 196616 | tf_op jit(solution)/shard_map/ppermute | solution.py:162
  5.7 4.0 %copy-start.3 = (bf16[64,512]{1,0:T(8,128)(2,1)S(1)}, bf16[64,512]{1,0:T(8,128)(2,1)}, u32[]{:S(2)}) copy-start(bf16[64,512]{1,0:T(8,128)(2,1)} %param.7) | copy-start | bytes 196612
  5.8 12.8 %all-to-all-start = ((bf16[8,80,256]{2,1,0:T(8,128)(2,1)}), bf16[8,80,256]{2,1,0:T(8,128)(2,1)S(1)}, u32[]{:S(2)}, u32[]{:S(2)}) async-start(bf16[8,80,256]{2,1,0:T(8,128)(2,1)} %pack.1), calls=%async_computation | async-start | bytes 655360 | tf_op jit(solution)/shard_map/all_to_all | solution.py:186
  9.7 4.6 %collective-permute-start.2 = (bf16[64,512]{1,0:T(8,128)(2,1)S(1)}, bf16[64,512]{1,0:T(8,128)(2,1)S(1)}, u32[]{:S(2)}, u32[]{:S(2)}) collective-permute-start(bf16[64,512]{1,0:T(8,128)(2,1)S(1)} %get-tuple-element.31), channel_id=1, source_target_pairs={{0,16},{16,0},{1,17},{17,1},{2,18},{18,2},{3,19},{19,3},{4,20},{20... | collective-permute-start | bytes 196616 | tf_op jit(solution)/shard_map/ppermute | solution.py:165
  11.3 6.5 %collective-permute-start.1 = (bf16[1,64,512]{2,1,0:T(8,128)(2,1)S(1)}, bf16[1,64,512]{2,1,0:T(8,128)(2,1)S(1)}, u32[]{:S(2)}, u32[]{:S(2)}) collective-permute-start(bf16[1,64,512]{2,1,0:T(8,128)(2,1)S(1)} %get-tuple-element.32), channel_id=1, source_target_pairs={{0,2},{1,3},{2,0},{3,1},{4,6},{5,7},{6,4},{7,5},{8,10},{9,11},{10,... | collective-permute-start | bytes 196616 | tf_op jit(solution)/shard_map/ppermute | solution.py:162
  14.3 4.3 %collective-permute-start.3 = (bf16[1,64,512]{2,1,0:T(8,128)(2,1)S(1)}, bf16[1,64,512]{2,1,0:T(8,128)(2,1)S(1)}, u32[]{:S(2)}, u32[]{:S(2)}) collective-permute-start(bf16[1,64,512]{2,1,0:T(8,128)(2,1)S(1)} %bitcast.8), channel_id=1, source_target_pairs={{0,4},{1,5},{2,6},{3,7},{4,0},{5,1},{6,2},{7,3},{8,12},{9,13},{10,... | collective-permute-start | bytes 196616 | tf_op jit(solution)/shard_map/ppermute | solution.py:162
  17.9 0.7 %copy-start.1 = (s32[6]{0:T(128)S(1)}, s32[6]{0:T(128)}, u32[]{:S(2)}) copy-start(s32[6]{0:T(128)} %owners.3) | copy-start | bytes 76
  19.3 8.7 %collective-permute-start.4 = (bf16[1,80,256]{2,1,0:T(8,128)(2,1)S(1)}, bf16[1,80,256]{2,1,0:T(8,128)(2,1)S(1)}, u32[]{:S(2)}, u32[]{:S(2)}) collective-permute-start(bf16[1,80,256]{2,1,0:T(8,128)(2,1)S(1)} %slice.8), channel_id=1, source_target_pairs={{0,8},{1,9},{2,10},{3,11},{4,12},{5,13},{6,14},{7,15},{8,0},{9,1},... | collective-permute-start | bytes 122888 | tf_op jit(solution)/shard_map/ppermute | solution.py:162
  19.8 11.4 %collective-permute-start.5 = (bf16[4,80,256]{2,1,0:T(8,128)(2,1)S(1)}, bf16[4,80,256]{2,1,0:T(8,128)(2,1)S(1)}, u32[]{:S(2)}, u32[]{:S(2)}) collective-permute-start(bf16[4,80,256]{2,1,0:T(8,128)(2,1)S(1)} %slice.9), channel_id=1, source_target_pairs={{0,8},{1,9},{2,10},{3,11},{4,12},{5,13},{6,14},{7,15},{8,0},{9,1},... | collective-permute-start | bytes 491528 | tf_op jit(solution)/shard_map/ppermute | solution.py:162
  28.0 6.1 %collective-permute-start.15 = (bf16[2,64,512]{2,1,0:T(8,128)(2,1)S(1)}, bf16[2,64,512]{2,1,0:T(8,128)(2,1)S(1)}, u32[]{:S(2)}, u32[]{:S(2)}) collective-permute-start(bf16[2,64,512]{2,1,0:T(8,128)(2,1)S(1)} %pad_maximum_fusion.3), channel_id=1, source_target_pairs={{0,4},{1,5},{2,6},{3,7},{4,0},{5,1},{6,2},{7,3},{8,12},{9,13},{10,... | collective-permute-start | bytes 393224 | tf_op jit(solution)/shard_map/ppermute | solution.py:162
  28.0 6.5 %collective-permute-start.16 = (bf16[2,64,512]{2,1,0:T(8,128)(2,1)S(1)}, bf16[2,64,512]{2,1,0:T(8,128)(2,1)S(1)}, u32[]{:S(2)}, u32[]{:S(2)}) collective-permute-start(bf16[2,64,512]{2,1,0:T(8,128)(2,1)S(1)} %pad_maximum_fusion.4), channel_id=1, source_target_pairs={{0,2},{1,3},{2,0},{3,1},{4,6},{5,7},{6,4},{7,5},{8,10},{9,11},{10,... | collective-permute-start | bytes 393224 | tf_op jit(solution)/shard_map/ppermute | solution.py:162
  28.1 19.6 %collective-permute-start.17 = (bf16[4,64,512]{2,1,0:T(8,128)(2,1)S(1)}, bf16[4,64,512]{2,1,0:T(8,128)(2,1)S(1)}, u32[]{:S(2)}, u32[]{:S(2)}) collective-permute-start(bf16[4,64,512]{2,1,0:T(8,128)(2,1)S(1)} %constant_dynamic-update-slice_fusion.9.refs_0_), channel_id=1, source_target_pairs={{0,1},{1,0},{2,3},{3,2},{4,5},{5,4},{6,7},{7,6},{8,9},{9,8},{10,11... | collective-permute-start | bytes 786440 | tf_op jit(solution)/shard_map/ppermute | solution.py:162
  31.9 4.5 %collective-permute-start.6 = (bf16[1,2,80,256]{3,2,1,0:T(8,128)(2,1)S(1)}, bf16[1,2,80,256]{3,2,1,0:T(8,128)(2,1)S(1)}, u32[]{:S(2)}, u32[]{:S(2)}) collective-permute-start(bf16[1,2,80,256]{3,2,1,0:T(8,128)(2,1)S(1)} %get-tuple-element.22), channel_id=1, source_target_pairs={{0,16},{16,0},{1,17},{17,1},{2,18},{18,2},{3,19},{19,3},{4,20},{20... | collective-permute-start | bytes 245768 | tf_op jit(solution)/shard_map/ppermute | solution.py:165
  33.4 4.4 %collective-permute-start.9 = (bf16[1,2,80,256]{3,2,1,0:T(8,128)(2,1)S(1)}, bf16[1,2,80,256]{3,2,1,0:T(8,128)(2,1)S(1)}, u32[]{:S(2)}, u32[]{:S(2)}) collective-permute-start(bf16[1,2,80,256]{3,2,1,0:T(8,128)(2,1)S(1)} %get-tuple-element.23), channel_id=1, source_target_pairs={{0,2},{1,3},{2,0},{3,1},{4,6},{5,7},{6,4},{7,5},{8,10},{9,11},{10,... | collective-permute-start | bytes 245768 | tf_op jit(solution)/shard_map/ppermute | solution.py:162
  34.1 4.5 %collective-permute-start.12 = (bf16[1,2,80,256]{3,2,1,0:T(8,128)(2,1)S(1)}, bf16[1,2,80,256]{3,2,1,0:T(8,128)(2,1)S(1)}, u32[]{:S(2)}, u32[]{:S(2)}) collective-permute-start(bf16[1,2,80,256]{3,2,1,0:T(8,128)(2,1)S(1)} %get-tuple-element.24), channel_id=1, source_target_pairs={{0,4},{1,5},{2,6},{3,7},{4,0},{5,1},{6,2},{7,3},{8,12},{9,13},{10,... | collective-permute-start | bytes 245768 | tf_op jit(solution)/shard_map/ppermute | solution.py:162
  34.6 13.2 %collective-permute-start.18 = (bf16[4,64,512]{2,1,0:T(8,128)(2,1)S(1)}, bf16[4,64,512]{2,1,0:T(8,128)(2,1)S(1)}, u32[]{:S(2)}, u32[]{:S(2)}) collective-permute-start(bf16[4,64,512]{2,1,0:T(8,128)(2,1)S(1)} %constant_dynamic-update-slice_fusion.11.refs_1_), channel_id=1, source_target_pairs={{0,1},{1,0},{2,3},{3,2},{4,5},{5,4},{6,7},{7,6},{8,9},{9,8},{10,11... | collective-permute-start | bytes 786440 | tf_op jit(solution)/shard_map/ppermute | solution.py:162
  36.4 11.4 %copy-start = (bf16[4096,128]{1,0:T(8,128)(2,1)S(1)}, bf16[4096,128]{1,0:T(8,128)(2,1)}, u32[]{:S(2)}) copy-start(bf16[4096,128]{1,0:T(8,128)(2,1)} %sub.6) | copy-start | bytes 3145732
  36.4 9.7 %collective-permute-start.7 = (bf16[2,2,80,256]{3,2,1,0:T(8,128)(2,1)S(1)}, bf16[2,2,80,256]{3,2,1,0:T(8,128)(2,1)S(1)}, u32[]{:S(2)}, u32[]{:S(2)}) collective-permute-start(bf16[2,2,80,256]{3,2,1,0:T(8,128)(2,1)S(1)} %pad_maximum_fusion), channel_id=1, source_target_pairs={{0,2},{1,3},{2,0},{3,1},{4,6},{5,7},{6,4},{7,5},{8,10},{9,11},{10,... | collective-permute-start | bytes 491528 | tf_op jit(solution)/shard_map/ppermute | solution.py:162
  37.9 8.0 %collective-permute-start.10 = (bf16[2,2,80,256]{3,2,1,0:T(8,128)(2,1)S(1)}, bf16[2,2,80,256]{3,2,1,0:T(8,128)(2,1)S(1)}, u32[]{:S(2)}, u32[]{:S(2)}) collective-permute-start(bf16[2,2,80,256]{3,2,1,0:T(8,128)(2,1)S(1)} %pad_maximum_fusion.1), channel_id=1, source_target_pairs={{0,4},{1,5},{2,6},{3,7},{4,0},{5,1},{6,2},{7,3},{8,12},{9,13},{10,... | collective-permute-start | bytes 491528 | tf_op jit(solution)/shard_map/ppermute | solution.py:162
  38.7 5.4 %collective-permute-start.13 = (bf16[2,2,80,256]{3,2,1,0:T(8,128)(2,1)S(1)}, bf16[2,2,80,256]{3,2,1,0:T(8,128)(2,1)S(1)}, u32[]{:S(2)}, u32[]{:S(2)}) collective-permute-start(bf16[2,2,80,256]{3,2,1,0:T(8,128)(2,1)S(1)} %pad_maximum_fusion.2), channel_id=1, source_target_pairs={{0,16},{16,0},{1,17},{17,1},{2,18},{18,2},{3,19},{19,3},{4,20},{20... | collective-permute-start | bytes 491528 | tf_op jit(solution)/shard_map/ppermute | solution.py:165
  44.1 8.9 %collective-permute-start.14 = (bf16[4,2,80,256]{3,2,1,0:T(8,128)(2,1)S(1)}, bf16[4,2,80,256]{3,2,1,0:T(8,128)(2,1)S(1)}, u32[]{:S(2)}, u32[]{:S(2)}) collective-permute-start(bf16[4,2,80,256]{3,2,1,0:T(8,128)(2,1)S(1)} %constant_dynamic-update-slice_fusion.6.refs_8_), channel_id=1, source_target_pairs={{0,2},{1,3},{2,0},{3,1},{4,6},{5,7},{6,4},{7,5},{8,10},{9,11},{10,... | collective-permute-start | bytes 983048 | tf_op jit(solution)/shard_map/ppermute | solution.py:162
  45.8 14.2 %collective-permute-start.11 = (bf16[4,2,80,256]{3,2,1,0:T(8,128)(2,1)S(1)}, bf16[4,2,80,256]{3,2,1,0:T(8,128)(2,1)S(1)}, u32[]{:S(2)}, u32[]{:S(2)}) collective-permute-start(bf16[4,2,80,256]{3,2,1,0:T(8,128)(2,1)S(1)} %constant_dynamic-update-slice_fusion.3.refs_4_), channel_id=1, source_target_pairs={{0,16},{16,0},{1,17},{17,1},{2,18},{18,2},{3,19},{19,3},{4,20},{20... | collective-permute-start | bytes 983048 | tf_op jit(solution)/shard_map/ppermute | solution.py:165
  46.1 13.9 %collective-permute-start.8 = (bf16[4,2,80,256]{3,2,1,0:T(8,128)(2,1)S(1)}, bf16[4,2,80,256]{3,2,1,0:T(8,128)(2,1)S(1)}, u32[]{:S(2)}, u32[]{:S(2)}) collective-permute-start(bf16[4,2,80,256]{3,2,1,0:T(8,128)(2,1)S(1)} %constant_dynamic-update-slice_fusion.refs_0_), channel_id=1, source_target_pairs={{0,4},{1,5},{2,6},{3,7},{4,0},{5,1},{6,2},{7,3},{8,12},{9,13},{10,... | collective-permute-start | bytes 983048 | tf_op jit(solution)/shard_map/ppermute | solution.py:162
  47.8 12.8 %collective-permute-start.23 = (bf16[4,2,80,256]{3,2,1,0:T(8,128)(2,1)S(1)}, bf16[4,2,80,256]{3,2,1,0:T(8,128)(2,1)S(1)}, u32[]{:S(2)}, u32[]{:S(2)}) collective-permute-start(bf16[4,2,80,256]{3,2,1,0:T(8,128)(2,1)S(1)} %constant_dynamic-update-slice_fusion.6.refs_8_), channel_id=1, source_target_pairs={{0,1},{1,0},{2,3},{3,2},{4,5},{5,4},{6,7},{7,6},{8,9},{9,8},{10,11... | collective-permute-start | bytes 983048 | tf_op jit(solution)/shard_map/ppermute | solution.py:162
  48.8 13.7 %copy-start.2 = (s32[6]{0:T(128)S(1)}, s32[6]{0:T(128)}, u32[]{:S(2)}) copy-start(s32[6]{0:T(128)} %offsets.1) | copy-start | bytes 76
  48.8 11.2 %all-to-all-start.1 = ((f32[32,4,128]{2,1,0:T(4,128)}), f32[32,4,128]{2,1,0:T(4,128)S(1)}, u32[]{:S(2)}, u32[]{:S(2)}) async-start(f32[32,4,128]{2,1,0:T(4,128)} %bitcast.4), calls=%async_computation.1 | async-start | bytes 131072 | tf_op jit(solution)/shard_map/all_to_all | solution.py:267
  52.6 8.1 %collective-permute-start.21 = (bf16[4,2,80,256]{3,2,1,0:T(8,128)(2,1)S(1)}, bf16[4,2,80,256]{3,2,1,0:T(8,128)(2,1)S(1)}, u32[]{:S(2)}, u32[]{:S(2)}) collective-permute-start(bf16[4,2,80,256]{3,2,1,0:T(8,128)(2,1)S(1)} %constant_dynamic-update-slice_fusion.3.refs_4_), channel_id=1, source_target_pairs={{0,1},{1,0},{2,3},{3,2},{4,5},{5,4},{6,7},{7,6},{8,9},{9,8},{10,11... | collective-permute-start | bytes 983048 | tf_op jit(solution)/shard_map/ppermute | solution.py:162
  52.9 7.7 %collective-permute-start.19 = (bf16[4,2,80,256]{3,2,1,0:T(8,128)(2,1)S(1)}, bf16[4,2,80,256]{3,2,1,0:T(8,128)(2,1)S(1)}, u32[]{:S(2)}, u32[]{:S(2)}) collective-permute-start(bf16[4,2,80,256]{3,2,1,0:T(8,128)(2,1)S(1)} %constant_dynamic-update-slice_fusion.refs_0_), channel_id=1, source_target_pairs={{0,1},{1,0},{2,3},{3,2},{4,5},{5,4},{6,7},{7,6},{8,9},{9,8},{10,11... | collective-permute-start | bytes 983048 | tf_op jit(solution)/shard_map/ppermute | solution.py:162
  60.0 1.6 %collective-permute-start.20 = (bf16[4,2,80,256]{3,2,1,0:T(8,128)(2,1)S(1)}, bf16[4,2,80,256]{3,2,1,0:T(8,128)(2,1)S(1)}, u32[]{:S(2)}, u32[]{:S(2)}) collective-permute-start(bf16[4,2,80,256]{3,2,1,0:T(8,128)(2,1)S(1)} %collective-permute-done.8.refs_1_), channel_id=1, source_target_pairs={{0,1},{1,0},{2,3},{3,2},{4,5},{5,4},{6,7},{7,6},{8,9},{9,8},{10,11... | collective-permute-start | bytes 983048 | tf_op jit(solution)/shard_map/ppermute | solution.py:162
  60.1 2.0 %collective-permute-start.22 = (bf16[4,2,80,256]{3,2,1,0:T(8,128)(2,1)S(1)}, bf16[4,2,80,256]{3,2,1,0:T(8,128)(2,1)S(1)}, u32[]{:S(2)}, u32[]{:S(2)}) collective-permute-start(bf16[4,2,80,256]{3,2,1,0:T(8,128)(2,1)S(1)} %collective-permute-done.11.refs_5_), channel_id=1, source_target_pairs={{0,1},{1,0},{2,3},{3,2},{4,5},{5,4},{6,7},{7,6},{8,9},{9,8},{10,11... | collective-permute-start | bytes 983048 | tf_op jit(solution)/shard_map/ppermute | solution.py:162
  60.5 2.1 %collective-permute-start.24 = (bf16[4,2,80,256]{3,2,1,0:T(8,128)(2,1)S(1)}, bf16[4,2,80,256]{3,2,1,0:T(8,128)(2,1)S(1)}, u32[]{:S(2)}, u32[]{:S(2)}) collective-permute-start(bf16[4,2,80,256]{3,2,1,0:T(8,128)(2,1)S(1)} %collective-permute-done.14.refs_9_), channel_id=1, source_target_pairs={{0,1},{1,0},{2,3},{3,2},{4,5},{5,4},{6,7},{7,6},{8,9},{9,8},{10,11... | collective-permute-start | bytes 983048 | tf_op jit(solution)/shard_map/ppermute | solution.py:162

commit v25 on v24

--- a/solution.py
+++ b/solution.py
@@ -264,6 +264,8 @@
             mask, send = links[(k + step) % 3]
             colours[k] = jnp.concatenate([colours[k], send(colours[k])])
             masks[k] = masks[k] + [m ^ mask for m in masks[k]]
+        if step == 0:
+            colours = list(lax.optimization_barrier(colours))
     state = lax.all_to_all(merged.reshape(rows * cols, each, width), ("row", "col"), 0, 0)
     last_round = []
     for k in range(COLOURS):

time: 68 us -> 69.7 us (1.025)
  waiting for transfers between devices: 28.3 us -> 29.5 us
    ppermute x21, waiting for transfers between devices: 14.3 us -> 15.1 us  [over_col(): return lax.ppermute(x, 'col', [(c, c ^ mask) for c in range(cols)])]
where the time goes in v25:
time: 69.7 us; the launch traced here: 69.4 us
  starting transfers between devices  30.2 us (43%)
  waiting for transfers between devices  29.5 us (42%)
  Pallas kernels  9.19 us (13%)
    ppermute x21, starting transfers between devices, over_col(): return lax.ppermute(x, 'col', [(c, c ^ mask) for c in range(cols)])  17.7 us
    ppermute x21, waiting for transfers between devices, over_col(): return lax.ppermute(x, 'col', [(c, c ^ mask) for c in range(cols)])  15.1 us
    ppermute x4, waiting for transfers between devices, over_row(): return lax.ppermute(x, 'row', [(r, r ^ mask) for r in range(rows)])  7.54 us
    all_to_all x1, waiting for transfers between devices, local(): lax.all_to_all(merged.reshape(rows * cols, each, width), ('row', 'col'),...  6.83 us
    pallas_call x1, Pallas kernels, local(): pl.pallas_call(functools.partial(chain_kernel, cols, groups, slots, sum((...  5.08 us
    ppermute x4, starting transfers between devices, over_row(): return lax.ppermute(x, 'row', [(r, r ^ mask) for r in range(rows)])  4.31 us
    all_to_all x1, starting transfers between devices, local(): lax.all_to_all(merged.reshape(rows * cols, each, width), ('row', 'col'),...  4.21 us
    all_to_all x1, starting transfers between devices, local(): slices = lax.all_to_all(packed, 'col', 0, 0, axis_index_groups=members)  3.95 us
  transfers between devices with their start and end apart: 27, of which 13 were waited for; matrix products, arithmetic and copies ran while one was open for 0% of the time, Pallas kernels for 5%

profile of v25, /device:TPU:0, one launch (start us, length us, event | category | flops | bytes accessed | tf_op | source)
XLA Modules:
  0.0 69.4 jit_solution(7615659388379184861)
XLA Ops:
  0.0 4.0 %collective-permute-start = (bf16[64,512]{1,0:T(8,128)(2,1)}, bf16[64,512]{1,0:T(8,128)(2,1)S(1)}, u32[]{:S(2)}, u32[]{:S(2)}) collective-permute-start(bf16[64,512]{1,0:T(8,128)(2,1)} %param.7), channel_id=1, source_target_pairs={{0,8},{1,9},{2,10},{3,11},{4,12},{5,13},{6,14},{7,15},{8,0},{9,1},... | collective-permute-start | bytes 196616 | tf_op jit(solution)/shard_map/ppermute | solution.py:162
  4.0 1.7 %pack.1 = bf16[8,80,256]{2,1,0:T(8,128)(2,1)} custom-call(bf16[16,64,256]{2,1,0:T(8,128)(2,1)} %bitcast.6, bf16[16,16,256]{2,1,0:T(8,128)(2,1)} %bitcast.7), custom_call_target="tpu_custom_call" | custom-call | bytes 655360 | tf_op jit(solution)/shard_map/pack/pallas_call | solution.py:175
  5.7 0.0 copy-start.3
  5.8 4.0 %all-to-all-start = ((bf16[8,80,256]{2,1,0:T(8,128)(2,1)}), bf16[8,80,256]{2,1,0:T(8,128)(2,1)S(1)}, u32[]{:S(2)}, u32[]{:S(2)}) async-start(bf16[8,80,256]{2,1,0:T(8,128)(2,1)} %pack.1), calls=%async_computation | async-start | bytes 655360 | tf_op jit(solution)/shard_map/all_to_all | solution.py:186
  9.7 1.6 %collective-permute-start.2 = (bf16[64,512]{1,0:T(8,128)(2,1)S(1)}, bf16[64,512]{1,0:T(8,128)(2,1)S(1)}, u32[]{:S(2)}, u32[]{:S(2)}) collective-permute-start(bf16[64,512]{1,0:T(8,128)(2,1)S(1)} %get-tuple-element.37), channel_id=1, source_target_pairs={{0,16},{16,0},{1,17},{17,1},{2,18},{18,2},{3,19},{19,3},{4,20},{20... | collective-permute-start | bytes 196616 | tf_op jit(solution)/shard_map/ppermute | solution.py:165
  11.3 2.0 %collective-permute-start.1 = (bf16[1,64,512]{2,1,0:T(8,128)(2,1)S(1)}, bf16[1,64,512]{2,1,0:T(8,128)(2,1)S(1)}, u32[]{:S(2)}, u32[]{:S(2)}) collective-permute-start(bf16[1,64,512]{2,1,0:T(8,128)(2,1)S(1)} %get-tuple-element.38), channel_id=1, source_target_pairs={{0,2},{1,3},{2,0},{3,1},{4,6},{5,7},{6,4},{7,5},{8,10},{9,11},{10,... | collective-permute-start | bytes 196616 | tf_op jit(solution)/shard_map/ppermute | solution.py:162
  13.3 1.0 %collective-permute-done.2 = bf16[64,512]{1,0:T(8,128)(2,1)S(1)} collective-permute-done((bf16[64,512]{1,0:T(8,128)(2,1)S(1)}, bf16[64,512]{1,0:T(8,128)(2,1)S(1)}, u32[]{:S(2)}, u32[]{:S(2)}) %collective-permute-start.2) | collective-permute-done | bytes 65568 | tf_op jit(solution)/shard_map/ppermute | solution.py:165
  14.3 1.8 %collective-permute-start.3 = (bf16[1,64,512]{2,1,0:T(8,128)(2,1)S(1)}, bf16[1,64,512]{2,1,0:T(8,128)(2,1)S(1)}, u32[]{:S(2)}, u32[]{:S(2)}) collective-permute-start(bf16[1,64,512]{2,1,0:T(8,128)(2,1)S(1)} %bitcast.8), channel_id=1, source_target_pairs={{0,4},{1,5},{2,6},{3,7},{4,0},{5,1},{6,2},{7,3},{8,12},{9,13},{10,... | collective-permute-start | bytes 196616 | tf_op jit(solution)/shard_map/ppermute | solution.py:162
  16.1 1.8 %collective-permute-done.1 = bf16[1,64,512]{2,1,0:T(8,128)(2,1)S(1)} collective-permute-done((bf16[1,64,512]{2,1,0:T(8,128)(2,1)S(1)}, bf16[1,64,512]{2,1,0:T(8,128)(2,1)S(1)}, u32[]{:S(2)}, u32[]{:S(2)}) %collective-permute-start.1) | collective-permute-done | bytes 65568 | tf_op jit(solution)/shard_map/ppermute | solution.py:162
  17.9 0.0 copy-start.1
  17.9 0.7 %collective-permute-done.3 = bf16[1,64,512]{2,1,0:T(8,128)(2,1)S(1)} collective-permute-done((bf16[1,64,512]{2,1,0:T(8,128)(2,1)S(1)}, bf16[1,64,512]{2,1,0:T(8,128)(2,1)S(1)}, u32[]{:S(2)}, u32[]{:S(2)}) %collective-permute-start.3) | collective-permute-done | bytes 65568 | tf_op jit(solution)/shard_map/ppermute | solution.py:162
  18.6 0.0 all-to-all-done.held
  18.6 0.7 %pick.1 = bf16[5,80,256]{2,1,0:T(8,128)(2,1)S(1)} custom-call(s32[6]{0:T(128)S(1)} %copy-done.1, bf16[8,80,256]{2,1,0:T(8,128)(2,1)S(1)} %all-to-all-done.held), custom_call_target="tpu_custom_call" | custom-call | bytes 327680 | tf_op jit(solution)/shard_map/pick/pallas_call | solution.py:215
  19.3 0.4 collective-permute-start.4
  19.8 2.6 %collective-permute-start.5 = (bf16[4,80,256]{2,1,0:T(8,128)(2,1)S(1)}, bf16[4,80,256]{2,1,0:T(8,128)(2,1)S(1)}, u32[]{:S(2)}, u32[]{:S(2)}) collective-permute-start(bf16[4,80,256]{2,1,0:T(8,128)(2,1)S(1)} %slice.9), channel_id=1, source_target_pairs={{0,8},{1,9},{2,10},{3,11},{4,12},{5,13},{6,14},{7,15},{8,0},{9,1},... | collective-permute-start | bytes 491528 | tf_op jit(solution)/shard_map/ppermute | solution.py:162
  22.4 5.6 %collective-permute-done.4.refs_0_ = bf16[1,80,256]{2,1,0:T(8,128)(2,1)S(1)} collective-permute-done((bf16[1,80,256]{2,1,0:T(8,128)(2,1)S(1)}, bf16[1,80,256]{2,1,0:T(8,128)(2,1)S(1)}, u32[]{:S(2)}, u32[]{:S(2)}) %collective-permute-start.4) | collective-permute-done | bytes 40992 | tf_op jit(solution)/shard_map/ppermute | solution.py:162
  28.0 0.0 collective-permute-start.15
  28.0 0.1 collective-permute-start.16
  28.2 0.1 collective-permute-start.17
  28.2 3.0 %collective-permute-done.5.refs_1_ = bf16[4,80,256]{2,1,0:T(8,128)(2,1)S(1)} collective-permute-done((bf16[4,80,256]{2,1,0:T(8,128)(2,1)S(1)}, bf16[4,80,256]{2,1,0:T(8,128)(2,1)S(1)}, u32[]{:S(2)}, u32[]{:S(2)}) %collective-permute-start.5) | collective-permute-done | bytes 163872 | tf_op jit(solution)/shard_map/ppermute | solution.py:162
  31.2 0.6 order.1
  31.9 1.6 %collective-permute-start.6 = (bf16[1,2,80,256]{3,2,1,0:T(8,128)(2,1)S(1)}, bf16[1,2,80,256]{3,2,1,0:T(8,128)(2,1)S(1)}, u32[]{:S(2)}, u32[]{:S(2)}) collective-permute-start(bf16[1,2,80,256]{3,2,1,0:T(8,128)(2,1)S(1)} %get-tuple-element.25), channel_id=1, source_target_pairs={{0,16},{16,0},{1,17},{17,1},{2,18},{18,2},{3,19},{19,3},{4,20},{20... | collective-permute-start | bytes 245768 | tf_op jit(solution)/shard_map/ppermute | solution.py:165
  33.4 0.7 collective-permute-start.7
  34.1 0.3 collective-permute-start.8
  34.5 0.1 collective-permute-start.18
  34.6 1.8 %collective-permute-done.6 = bf16[1,2,80,256]{3,2,1,0:T(8,128)(2,1)S(1)} collective-permute-done((bf16[1,2,80,256]{3,2,1,0:T(8,128)(2,1)S(1)}, bf16[1,2,80,256]{3,2,1,0:T(8,128)(2,1)S(1)}, u32[]{:S(2)}, u32[]{:S(2)}) %collective-permute-start.6) | collective-permute-done | bytes 81952 | tf_op jit(solution)/shard_map/ppermute | solution.py:165
  36.4 1.5 %collective-permute-done.7 = bf16[1,2,80,256]{3,2,1,0:T(8,128)(2,1)S(1)} collective-permute-done((bf16[1,2,80,256]{3,2,1,0:T(8,128)(2,1)S(1)}, bf16[1,2,80,256]{3,2,1,0:T(8,128)(2,1)S(1)}, u32[]{:S(2)}, u32[]{:S(2)}) %collective-permute-start.7) | collective-permute-done | bytes 81952 | tf_op jit(solution)/shard_map/ppermute | solution.py:162
  37.9 0.7 collective-permute-done.8
  38.6 0.0 copy-start
  38.6 1.4 %collective-permute-start.9 = (bf16[2,2,80,256]{3,2,1,0:T(8,128)(2,1)S(1)}, bf16[2,2,80,256]{3,2,1,0:T(8,128)(2,1)S(1)}, u32[]{:S(2)}, u32[]{:S(2)}) collective-permute-start(bf16[2,2,80,256]{3,2,1,0:T(8,128)(2,1)S(1)} %pad_maximum_fusion), channel_id=1, source_target_pairs={{0,2},{1,3},{2,0},{3,1},{4,6},{5,7},{6,4},{7,5},{8,10},{9,11},{10,... | collective-permute-start | bytes 491528 | tf_op jit(solution)/shard_map/ppermute | solution.py:162
  40.0 0.1 collective-permute-start.11
  40.1 0.6 collective-permute-start.13
  40.7 4.7 %collective-permute-done.13 = bf16[2,2,80,256]{3,2,1,0:T(8,128)(2,1)S(1)} collective-permute-done((bf16[2,2,80,256]{3,2,1,0:T(8,128)(2,1)S(1)}, bf16[2,2,80,256]{3,2,1,0:T(8,128)(2,1)S(1)}, u32[]{:S(2)}, u32[]{:S(2)}) %collective-permute-start.13) | collective-permute-done | bytes 163872 | tf_op jit(solution)/shard_map/ppermute | solution.py:165
  45.5 1.0 %collective-permute-start.14 = (bf16[4,2,80,256]{3,2,1,0:T(8,128)(2,1)S(1)}, bf16[4,2,80,256]{3,2,1,0:T(8,128)(2,1)S(1)}, u32[]{:S(2)}, u32[]{:S(2)}) collective-permute-start(bf16[4,2,80,256]{3,2,1,0:T(8,128)(2,1)S(1)} %constant_dynamic-update-slice_fusion.4.refs_8_), channel_id=1, source_target_pairs={{0,2},{1,3},{2,0},{3,1},{4,6},{5,7},{6,4},{7,5},{8,10},{9,11},{10,... | collective-permute-start | bytes 983048 | tf_op jit(solution)/shard_map/ppermute | solution.py:162
  46.5 0.6 collective-permute-start.12
  47.1 1.9 %collective-permute-start.10 = (bf16[4,2,80,256]{3,2,1,0:T(8,128)(2,1)S(1)}, bf16[4,2,80,256]{3,2,1,0:T(8,128)(2,1)S(1)}, u32[]{:S(2)}, u32[]{:S(2)}) collective-permute-start(bf16[4,2,80,256]{3,2,1,0:T(8,128)(2,1)S(1)} %constant_dynamic-update-slice_fusion.refs_0_), channel_id=1, source_target_pairs={{0,4},{1,5},{2,6},{3,7},{4,0},{5,1},{6,2},{7,3},{8,12},{9,13},{10,... | collective-permute-start | bytes 983048 | tf_op jit(solution)/shard_map/ppermute | solution.py:162
  49.0 1.1 %merge.1 = f32[128,128]{1,0:T(8,128)} custom-call(bf16[4096,128]{1,0:T(8,128)(2,1)S(1)} %copy-done, bf16[4,64,512]{2,1,0:T(8,128)(2,1)S(1)} %constant_dynamic-update-slice_fusion.6.refs_0_, bf16[4,64,512]{2,1,0:T(8,128)(2,1)S(1)} %constant_dynamic-update-slice_fusion.8.refs_1_, bf16[4,64,512]{2,1,0:T(8,128)(2,1)S(1)} %collective-permute-done.17.refs_2_, ...), custom_call_target="tpu_custom_call" | custom-call | flops 134217728 | bytes 1048576 | tf_op jit(solution)/shard_map/merge/pallas_call | solution.py:236
  50.1 4.2 %all-to-all-start.1 = ((f32[32,4,128]{2,1,0:T(4,128)}), f32[32,4,128]{2,1,0:T(4,128)S(1)}, u32[]{:S(2)}, u32[]{:S(2)}) async-start(f32[32,4,128]{2,1,0:T(4,128)} %bitcast.4), calls=%async_computation.1 | async-start | bytes 131072 | tf_op jit(solution)/shard_map/all_to_all | solution.py:269
  54.3 0.3 collective-permute-start.21
  54.6 0.3 collective-permute-start.19
  54.9 6.8 %all-to-all-done.1.start = f32[32,4,128]{2,1,0:T(4,128)S(1)} async-done(((f32[32,4,128]{2,1,0:T(4,128)}), f32[32,4,128]{2,1,0:T(4,128)S(1)}, u32[]{:S(2)}, u32[]{:S(2)}) %all-to-all-start.1) | async-done | bytes 65568 | tf_op jit(solution)/shard_map/all_to_all | solution.py:269
  61.7 0.1 collective-permute-start.20
  61.9 0.4 collective-permute-start.22
  62.3 0.1 collective-permute-start.24
  62.4 1.0 %collective-permute-done.20.refs_3_ = bf16[4,2,80,256]{3,2,1,0:T(8,128)(2,1)S(1)} collective-permute-done((bf16[4,2,80,256]{3,2,1,0:T(8,128)(2,1)S(1)}, bf16[4,2,80,256]{3,2,1,0:T(8,128)(2,1)S(1)}, u32[]{:S(2)}, u32[]{:S(2)}) %collective-permute-start.20) | collective-permute-done | bytes 327712 | tf_op jit(solution)/shard_map/ppermute | solution.py:162
  63.4 0.5 collective-permute-done.22.refs_7_
  63.8 0.5 collective-permute-done.24.refs_11_
  64.3 5.1 %chain0.1 = bf16[4,2048]{1,0:T(4,128)(2,1)} custom-call(s32[6]{0:T(128)S(1)} %copy-done.2, f32[32,4,128]{2,1,0:T(4,128)S(1)} %all-to-all-done.1.start, bf16[4,2,80,256]{3,2,1,0:T(8,128)(2,1)S(1)} %constant_dynamic-update-slice_fusion.refs_0_, bf16[4,2,80,256]{3,2,1,0:T(8,128)(2,1)S(1)} %collective-permute-done.10.refs_1_, ...), custom_call_target="tpu_custom_call" | custom-call | flops 201326592 | bytes 3932160 | tf_op jit(solution)/shard_map/chain0/pallas_call | solution.py:287
  (37 shorter events, 0.3 us)
Async XLA Ops:
  0.0 9.7 %collective-permute-start = (bf16[64,512]{1,0:T(8,128)(2,1)}, bf16[64,512]{1,0:T(8,128)(2,1)S(1)}, u32[]{:S(2)}, u32[]{:S(2)}) collective-permute-start(bf16[64,512]{1,0:T(8,128)(2,1)} %param.7), channel_id=1, source_target_pairs={{0,8},{1,9},{2,10},{3,11},{4,12},{5,13},{6,14},{7,15},{8,0},{9,1},... | collective-permute-start | bytes 196616 | tf_op jit(solution)/shard_map/ppermute | solution.py:162
  5.7 4.0 %copy-start.3 = (bf16[64,512]{1,0:T(8,128)(2,1)S(1)}, bf16[64,512]{1,0:T(8,128)(2,1)}, u32[]{:S(2)}) copy-start(bf16[64,512]{1,0:T(8,128)(2,1)} %param.7) | copy-start | bytes 196612
  5.8 12.8 %all-to-all-start = ((bf16[8,80,256]{2,1,0:T(8,128)(2,1)}), bf16[8,80,256]{2,1,0:T(8,128)(2,1)S(1)}, u32[]{:S(2)}, u32[]{:S(2)}) async-start(bf16[8,80,256]{2,1,0:T(8,128)(2,1)} %pack.1), calls=%async_computation | async-start | bytes 655360 | tf_op jit(solution)/shard_map/all_to_all | solution.py:186
  9.7 4.6 %collective-permute-start.2 = (bf16[64,512]{1,0:T(8,128)(2,1)S(1)}, bf16[64,512]{1,0:T(8,128)(2,1)S(1)}, u32[]{:S(2)}, u32[]{:S(2)}) collective-permute-start(bf16[64,512]{1,0:T(8,128)(2,1)S(1)} %get-tuple-element.37), channel_id=1, source_target_pairs={{0,16},{16,0},{1,17},{17,1},{2,18},{18,2},{3,19},{19,3},{4,20},{20... | collective-permute-start | bytes 196616 | tf_op jit(solution)/shard_map/ppermute | solution.py:165
  11.3 6.5 %collective-permute-start.1 = (bf16[1,64,512]{2,1,0:T(8,128)(2,1)S(1)}, bf16[1,64,512]{2,1,0:T(8,128)(2,1)S(1)}, u32[]{:S(2)}, u32[]{:S(2)}) collective-permute-start(bf16[1,64,512]{2,1,0:T(8,128)(2,1)S(1)} %get-tuple-element.38), channel_id=1, source_target_pairs={{0,2},{1,3},{2,0},{3,1},{4,6},{5,7},{6,4},{7,5},{8,10},{9,11},{10,... | collective-permute-start | bytes 196616 | tf_op jit(solution)/shard_map/ppermute | solution.py:162
  14.3 4.3 %collective-permute-start.3 = (bf16[1,64,512]{2,1,0:T(8,128)(2,1)S(1)}, bf16[1,64,512]{2,1,0:T(8,128)(2,1)S(1)}, u32[]{:S(2)}, u32[]{:S(2)}) collective-permute-start(bf16[1,64,512]{2,1,0:T(8,128)(2,1)S(1)} %bitcast.8), channel_id=1, source_target_pairs={{0,4},{1,5},{2,6},{3,7},{4,0},{5,1},{6,2},{7,3},{8,12},{9,13},{10,... | collective-permute-start | bytes 196616 | tf_op jit(solution)/shard_map/ppermute | solution.py:162
  17.9 0.7 %copy-start.1 = (s32[6]{0:T(128)S(1)}, s32[6]{0:T(128)}, u32[]{:S(2)}) copy-start(s32[6]{0:T(128)} %owners.3) | copy-start | bytes 76
  19.3 8.7 %collective-permute-start.4 = (bf16[1,80,256]{2,1,0:T(8,128)(2,1)S(1)}, bf16[1,80,256]{2,1,0:T(8,128)(2,1)S(1)}, u32[]{:S(2)}, u32[]{:S(2)}) collective-permute-start(bf16[1,80,256]{2,1,0:T(8,128)(2,1)S(1)} %slice.8), channel_id=1, source_target_pairs={{0,8},{1,9},{2,10},{3,11},{4,12},{5,13},{6,14},{7,15},{8,0},{9,1},... | collective-permute-start | bytes 122888 | tf_op jit(solution)/shard_map/ppermute | solution.py:162
  19.8 11.5 %collective-permute-start.5 = (bf16[4,80,256]{2,1,0:T(8,128)(2,1)S(1)}, bf16[4,80,256]{2,1,0:T(8,128)(2,1)S(1)}, u32[]{:S(2)}, u32[]{:S(2)}) collective-permute-start(bf16[4,80,256]{2,1,0:T(8,128)(2,1)S(1)} %slice.9), channel_id=1, source_target_pairs={{0,8},{1,9},{2,10},{3,11},{4,12},{5,13},{6,14},{7,15},{8,0},{9,1},... | collective-permute-start | bytes 491528 | tf_op jit(solution)/shard_map/ppermute | solution.py:162
  28.0 6.1 %collective-permute-start.15 = (bf16[2,64,512]{2,1,0:T(8,128)(2,1)S(1)}, bf16[2,64,512]{2,1,0:T(8,128)(2,1)S(1)}, u32[]{:S(2)}, u32[]{:S(2)}) collective-permute-start(bf16[2,64,512]{2,1,0:T(8,128)(2,1)S(1)} %pad_maximum_fusion.3), channel_id=1, source_target_pairs={{0,4},{1,5},{2,6},{3,7},{4,0},{5,1},{6,2},{7,3},{8,12},{9,13},{10,... | collective-permute-start | bytes 393224 | tf_op jit(solution)/shard_map/ppermute | solution.py:162
  28.0 6.4 %collective-permute-start.16 = (bf16[2,64,512]{2,1,0:T(8,128)(2,1)S(1)}, bf16[2,64,512]{2,1,0:T(8,128)(2,1)S(1)}, u32[]{:S(2)}, u32[]{:S(2)}) collective-permute-start(bf16[2,64,512]{2,1,0:T(8,128)(2,1)S(1)} %pad_maximum_fusion.4), channel_id=1, source_target_pairs={{0,2},{1,3},{2,0},{3,1},{4,6},{5,7},{6,4},{7,5},{8,10},{9,11},{10,... | collective-permute-start | bytes 393224 | tf_op jit(solution)/shard_map/ppermute | solution.py:162
  28.2 20.9 %collective-permute-start.17 = (bf16[4,64,512]{2,1,0:T(8,128)(2,1)S(1)}, bf16[4,64,512]{2,1,0:T(8,128)(2,1)S(1)}, u32[]{:S(2)}, u32[]{:S(2)}) collective-permute-start(bf16[4,64,512]{2,1,0:T(8,128)(2,1)S(1)} %constant_dynamic-update-slice_fusion.6.refs_0_), channel_id=1, source_target_pairs={{0,1},{1,0},{2,3},{3,2},{4,5},{5,4},{6,7},{7,6},{8,9},{9,8},{10,11... | collective-permute-start | bytes 786440 | tf_op jit(solution)/shard_map/ppermute | solution.py:162
  31.9 4.5 %collective-permute-start.6 = (bf16[1,2,80,256]{3,2,1,0:T(8,128)(2,1)S(1)}, bf16[1,2,80,256]{3,2,1,0:T(8,128)(2,1)S(1)}, u32[]{:S(2)}, u32[]{:S(2)}) collective-permute-start(bf16[1,2,80,256]{3,2,1,0:T(8,128)(2,1)S(1)} %get-tuple-element.25), channel_id=1, source_target_pairs={{0,16},{16,0},{1,17},{17,1},{2,18},{18,2},{3,19},{19,3},{4,20},{20... | collective-permute-start | bytes 245768 | tf_op jit(solution)/shard_map/ppermute | solution.py:165
  33.4 4.4 %collective-permute-start.7 = (bf16[1,2,80,256]{3,2,1,0:T(8,128)(2,1)S(1)}, bf16[1,2,80,256]{3,2,1,0:T(8,128)(2,1)S(1)}, u32[]{:S(2)}, u32[]{:S(2)}) collective-permute-start(bf16[1,2,80,256]{3,2,1,0:T(8,128)(2,1)S(1)} %get-tuple-element.26), channel_id=1, source_target_pairs={{0,2},{1,3},{2,0},{3,1},{4,6},{5,7},{6,4},{7,5},{8,10},{9,11},{10,... | collective-permute-start | bytes 245768 | tf_op jit(solution)/shard_map/ppermute | solution.py:162
  34.1 4.4 %collective-permute-start.8 = (bf16[1,2,80,256]{3,2,1,0:T(8,128)(2,1)S(1)}, bf16[1,2,80,256]{3,2,1,0:T(8,128)(2,1)S(1)}, u32[]{:S(2)}, u32[]{:S(2)}) collective-permute-start(bf16[1,2,80,256]{3,2,1,0:T(8,128)(2,1)S(1)} %get-tuple-element.27), channel_id=1, source_target_pairs={{0,4},{1,5},{2,6},{3,7},{4,0},{5,1},{6,2},{7,3},{8,12},{9,13},{10,... | collective-permute-start | bytes 245768 | tf_op jit(solution)/shard_map/ppermute | solution.py:162
  34.5 14.5 %collective-permute-start.18 = (bf16[4,64,512]{2,1,0:T(8,128)(2,1)S(1)}, bf16[4,64,512]{2,1,0:T(8,128)(2,1)S(1)}, u32[]{:S(2)}, u32[]{:S(2)}) collective-permute-start(bf16[4,64,512]{2,1,0:T(8,128)(2,1)S(1)} %constant_dynamic-update-slice_fusion.8.refs_1_), channel_id=1, source_target_pairs={{0,1},{1,0},{2,3},{3,2},{4,5},{5,4},{6,7},{7,6},{8,9},{9,8},{10,11... | collective-permute-start | bytes 786440 | tf_op jit(solution)/shard_map/ppermute | solution.py:162
  38.6 10.5 %copy-start = (bf16[4096,128]{1,0:T(8,128)(2,1)S(1)}, bf16[4096,128]{1,0:T(8,128)(2,1)}, u32[]{:S(2)}) copy-start(bf16[4096,128]{1,0:T(8,128)(2,1)} %sub.6) | copy-start | bytes 3145732
  38.6 8.5 %collective-permute-start.9 = (bf16[2,2,80,256]{3,2,1,0:T(8,128)(2,1)S(1)}, bf16[2,2,80,256]{3,2,1,0:T(8,128)(2,1)S(1)}, u32[]{:S(2)}, u32[]{:S(2)}) collective-permute-start(bf16[2,2,80,256]{3,2,1,0:T(8,128)(2,1)S(1)} %pad_maximum_fusion), channel_id=1, source_target_pairs={{0,2},{1,3},{2,0},{3,1},{4,6},{5,7},{6,4},{7,5},{8,10},{9,11},{10,... | collective-permute-start | bytes 491528 | tf_op jit(solution)/shard_map/ppermute | solution.py:162
  40.0 6.5 %collective-permute-start.11 = (bf16[2,2,80,256]{3,2,1,0:T(8,128)(2,1)S(1)}, bf16[2,2,80,256]{3,2,1,0:T(8,128)(2,1)S(1)}, u32[]{:S(2)}, u32[]{:S(2)}) collective-permute-start(bf16[2,2,80,256]{3,2,1,0:T(8,128)(2,1)S(1)} %pad_maximum_fusion.1), channel_id=1, source_target_pairs={{0,4},{1,5},{2,6},{3,7},{4,0},{5,1},{6,2},{7,3},{8,12},{9,13},{10,... | collective-permute-start | bytes 491528 | tf_op jit(solution)/shard_map/ppermute | solution.py:162
  40.1 5.4 %collective-permute-start.13 = (bf16[2,2,80,256]{3,2,1,0:T(8,128)(2,1)S(1)}, bf16[2,2,80,256]{3,2,1,0:T(8,128)(2,1)S(1)}, u32[]{:S(2)}, u32[]{:S(2)}) collective-permute-start(bf16[2,2,80,256]{3,2,1,0:T(8,128)(2,1)S(1)} %pad_maximum_fusion.2), channel_id=1, source_target_pairs={{0,16},{16,0},{1,17},{17,1},{2,18},{18,2},{3,19},{19,3},{4,20},{20... | collective-permute-start | bytes 491528 | tf_op jit(solution)/shard_map/ppermute | solution.py:165
  45.5 9.2 %collective-permute-start.14 = (bf16[4,2,80,256]{3,2,1,0:T(8,128)(2,1)S(1)}, bf16[4,2,80,256]{3,2,1,0:T(8,128)(2,1)S(1)}, u32[]{:S(2)}, u32[]{:S(2)}) collective-permute-start(bf16[4,2,80,256]{3,2,1,0:T(8,128)(2,1)S(1)} %constant_dynamic-update-slice_fusion.4.refs_8_), channel_id=1, source_target_pairs={{0,2},{1,3},{2,0},{3,1},{4,6},{5,7},{6,4},{7,5},{8,10},{9,11},{10,... | collective-permute-start | bytes 983048 | tf_op jit(solution)/shard_map/ppermute | solution.py:162
  46.5 15.2 %collective-permute-start.12 = (bf16[4,2,80,256]{3,2,1,0:T(8,128)(2,1)S(1)}, bf16[4,2,80,256]{3,2,1,0:T(8,128)(2,1)S(1)}, u32[]{:S(2)}, u32[]{:S(2)}) collective-permute-start(bf16[4,2,80,256]{3,2,1,0:T(8,128)(2,1)S(1)} %constant_dynamic-update-slice_fusion.2.refs_4_), channel_id=1, source_target_pairs={{0,16},{16,0},{1,17},{17,1},{2,18},{18,2},{3,19},{19,3},{4,20},{20... | collective-permute-start | bytes 983048 | tf_op jit(solution)/shard_map/ppermute | solution.py:165
  47.1 14.6 %collective-permute-start.10 = (bf16[4,2,80,256]{3,2,1,0:T(8,128)(2,1)S(1)}, bf16[4,2,80,256]{3,2,1,0:T(8,128)(2,1)S(1)}, u32[]{:S(2)}, u32[]{:S(2)}) collective-permute-start(bf16[4,2,80,256]{3,2,1,0:T(8,128)(2,1)S(1)} %constant_dynamic-update-slice_fusion.refs_0_), channel_id=1, source_target_pairs={{0,4},{1,5},{2,6},{3,7},{4,0},{5,1},{6,2},{7,3},{8,12},{9,13},{10,... | collective-permute-start | bytes 983048 | tf_op jit(solution)/shard_map/ppermute | solution.py:162
  49.0 13.2 %collective-permute-start.23 = (bf16[4,2,80,256]{3,2,1,0:T(8,128)(2,1)S(1)}, bf16[4,2,80,256]{3,2,1,0:T(8,128)(2,1)S(1)}, u32[]{:S(2)}, u32[]{:S(2)}) collective-permute-start(bf16[4,2,80,256]{3,2,1,0:T(8,128)(2,1)S(1)} %constant_dynamic-update-slice_fusion.4.refs_8_), channel_id=1, source_target_pairs={{0,1},{1,0},{2,3},{3,2},{4,5},{5,4},{6,7},{7,6},{8,9},{9,8},{10,11... | collective-permute-start | bytes 983048 | tf_op jit(solution)/shard_map/ppermute | solution.py:162
  50.1 14.2 %copy-start.2 = (s32[6]{0:T(128)S(1)}, s32[6]{0:T(128)}, u32[]{:S(2)}) copy-start(s32[6]{0:T(128)} %offsets.1) | copy-start | bytes 76
  50.1 11.6 %all-to-all-start.1 = ((f32[32,4,128]{2,1,0:T(4,128)}), f32[32,4,128]{2,1,0:T(4,128)S(1)}, u32[]{:S(2)}, u32[]{:S(2)}) async-start(f32[32,4,128]{2,1,0:T(4,128)} %bitcast.4), calls=%async_computation.1 | async-start | bytes 131072 | tf_op jit(solution)/shard_map/all_to_all | solution.py:269
  54.3 8.1 %collective-permute-start.21 = (bf16[4,2,80,256]{3,2,1,0:T(8,128)(2,1)S(1)}, bf16[4,2,80,256]{3,2,1,0:T(8,128)(2,1)S(1)}, u32[]{:S(2)}, u32[]{:S(2)}) collective-permute-start(bf16[4,2,80,256]{3,2,1,0:T(8,128)(2,1)S(1)} %constant_dynamic-update-slice_fusion.2.refs_4_), channel_id=1, source_target_pairs={{0,1},{1,0},{2,3},{3,2},{4,5},{5,4},{6,7},{7,6},{8,9},{9,8},{10,11... | collective-permute-start | bytes 983048 | tf_op jit(solution)/shard_map/ppermute | solution.py:162
  54.6 7.7 %collective-permute-start.19 = (bf16[4,2,80,256]{3,2,1,0:T(8,128)(2,1)S(1)}, bf16[4,2,80,256]{3,2,1,0:T(8,128)(2,1)S(1)}, u32[]{:S(2)}, u32[]{:S(2)}) collective-permute-start(bf16[4,2,80,256]{3,2,1,0:T(8,128)(2,1)S(1)} %constant_dynamic-update-slice_fusion.refs_0_), channel_id=1, source_target_pairs={{0,1},{1,0},{2,3},{3,2},{4,5},{5,4},{6,7},{7,6},{8,9},{9,8},{10,11... | collective-permute-start | bytes 983048 | tf_op jit(solution)/shard_map/ppermute | solution.py:162
  61.7 1.6 %collective-permute-start.20 = (bf16[4,2,80,256]{3,2,1,0:T(8,128)(2,1)S(1)}, bf16[4,2,80,256]{3,2,1,0:T(8,128)(2,1)S(1)}, u32[]{:S(2)}, u32[]{:S(2)}) collective-permute-start(bf16[4,2,80,256]{3,2,1,0:T(8,128)(2,1)S(1)} %collective-permute-done.10.refs_1_), channel_id=1, source_target_pairs={{0,1},{1,0},{2,3},{3,2},{4,5},{5,4},{6,7},{7,6},{8,9},{9,8},{10,11... | collective-permute-start | bytes 983048 | tf_op jit(solution)/shard_map/ppermute | solution.py:162
  61.9 2.0 %collective-permute-start.22 = (bf16[4,2,80,256]{3,2,1,0:T(8,128)(2,1)S(1)}, bf16[4,2,80,256]{3,2,1,0:T(8,128)(2,1)S(1)}, u32[]{:S(2)}, u32[]{:S(2)}) collective-permute-start(bf16[4,2,80,256]{3,2,1,0:T(8,128)(2,1)S(1)} %collective-permute-done.12.refs_5_), channel_id=1, source_target_pairs={{0,1},{1,0},{2,3},{3,2},{4,5},{5,4},{6,7},{7,6},{8,9},{9,8},{10,11... | collective-permute-start | bytes 983048 | tf_op jit(solution)/shard_map/ppermute | solution.py:162
  62.3 2.1 %collective-permute-start.24 = (bf16[4,2,80,256]{3,2,1,0:T(8,128)(2,1)S(1)}, bf16[4,2,80,256]{3,2,1,0:T(8,128)(2,1)S(1)}, u32[]{:S(2)}, u32[]{:S(2)}) collective-permute-start(bf16[4,2,80,256]{3,2,1,0:T(8,128)(2,1)S(1)} %collective-permute-done.14.refs_9_), channel_id=1, source_target_pairs={{0,1},{1,0},{2,3},{3,2},{4,5},{5,4},{6,7},{7,6},{8,9},{9,8},{10,11... | collective-permute-start | bytes 983048 | tf_op jit(solution)/shard_map/ppermute | solution.py:162

commit v26 on v25

--- a/solution.py
+++ b/solution.py
@@ -265,7 +265,7 @@
             colours[k] = jnp.concatenate([colours[k], send(colours[k])])
             masks[k] = masks[k] + [m ^ mask for m in masks[k]]
         if step == 0:
-            colours = list(lax.optimization_barrier(colours))
+            colours, merged = lax.optimization_barrier((colours, merged))
     state = lax.all_to_all(merged.reshape(rows * cols, each, width), ("row", "col"), 0, 0)
     last_round = []
     for k in range(COLOURS):

time: 69.7 us -> 69.6 us (level)
  transfers between devices with their start and end apart: 27 -> 27, of which waited for: 13 -> 13; matrix products, arithmetic and copies ran while one was open for 0% -> 0% of each run, Pallas kernels for 5% -> 3%
where the time goes in v26:
time: 69.6 us; the launch traced here: 69.4 us
  starting transfers between devices  30.2 us (43%)
  waiting for transfers between devices  29.5 us (42%)
  Pallas kernels  9.2 us (13%)
    ppermute x21, starting transfers between devices, over_col(): return lax.ppermute(x, 'col', [(c, c ^ mask) for c in range(cols)])  17.7 us
    ppermute x21, waiting for transfers between devices, over_col(): return lax.ppermute(x, 'col', [(c, c ^ mask) for c in range(cols)])  15.1 us
    ppermute x4, waiting for transfers between devices, over_row(): return lax.ppermute(x, 'row', [(r, r ^ mask) for r in range(rows)])  7.53 us
    all_to_all x1, waiting for transfers between devices, local(): lax.all_to_all(merged.reshape(rows * cols, each, width), ('row', 'col'),...  6.83 us
    pallas_call x1, Pallas kernels, local(): pl.pallas_call(functools.partial(chain_kernel, cols, groups, slots, sum((...  5.08 us
    ppermute x4, starting transfers between devices, over_row(): return lax.ppermute(x, 'row', [(r, r ^ mask) for r in range(rows)])  4.31 us
    all_to_all x1, starting transfers between devices, local(): lax.all_to_all(merged.reshape(rows * cols, each, width), ('row', 'col'),...  4.23 us
    all_to_all x1, starting transfers between devices, local(): slices = lax.all_to_all(packed, 'col', 0, 0, axis_index_groups=members)  3.95 us
  transfers between devices with their start and end apart: 27, of which 13 were waited for; matrix products, arithmetic and copies ran while one was open for 0% of the time, Pallas kernels for 3%

profile of v26, /device:TPU:0, one launch (start us, length us, event | category | flops | bytes accessed | tf_op | source)
XLA Modules:
  0.0 69.4 jit_solution(12141630352712206743)
XLA Ops:
  0.0 4.0 %collective-permute-start = (bf16[64,512]{1,0:T(8,128)(2,1)}, bf16[64,512]{1,0:T(8,128)(2,1)S(1)}, u32[]{:S(2)}, u32[]{:S(2)}) collective-permute-start(bf16[64,512]{1,0:T(8,128)(2,1)} %param.7), channel_id=1, source_target_pairs={{0,8},{1,9},{2,10},{3,11},{4,12},{5,13},{6,14},{7,15},{8,0},{9,1},... | collective-permute-start | bytes 196616 | tf_op jit(solution)/shard_map/ppermute | solution.py:162
  4.0 1.7 %pack.1 = bf16[8,80,256]{2,1,0:T(8,128)(2,1)} custom-call(bf16[16,64,256]{2,1,0:T(8,128)(2,1)} %bitcast.6, bf16[16,16,256]{2,1,0:T(8,128)(2,1)} %bitcast.7), custom_call_target="tpu_custom_call" | custom-call | bytes 655360 | tf_op jit(solution)/shard_map/pack/pallas_call | solution.py:175
  5.7 0.0 copy-start.3
  5.8 4.0 %all-to-all-start = ((bf16[8,80,256]{2,1,0:T(8,128)(2,1)}), bf16[8,80,256]{2,1,0:T(8,128)(2,1)S(1)}, u32[]{:S(2)}, u32[]{:S(2)}) async-start(bf16[8,80,256]{2,1,0:T(8,128)(2,1)} %pack.1), calls=%async_computation | async-start | bytes 655360 | tf_op jit(solution)/shard_map/all_to_all | solution.py:186
  9.7 1.6 %collective-permute-start.2 = (bf16[64,512]{1,0:T(8,128)(2,1)S(1)}, bf16[64,512]{1,0:T(8,128)(2,1)S(1)}, u32[]{:S(2)}, u32[]{:S(2)}) collective-permute-start(bf16[64,512]{1,0:T(8,128)(2,1)S(1)} %get-tuple-element.39), channel_id=1, source_target_pairs={{0,16},{16,0},{1,17},{17,1},{2,18},{18,2},{3,19},{19,3},{4,20},{20... | collective-permute-start | bytes 196616 | tf_op jit(solution)/shard_map/ppermute | solution.py:165
  11.3 2.0 %collective-permute-start.1 = (bf16[1,64,512]{2,1,0:T(8,128)(2,1)S(1)}, bf16[1,64,512]{2,1,0:T(8,128)(2,1)S(1)}, u32[]{:S(2)}, u32[]{:S(2)}) collective-permute-start(bf16[1,64,512]{2,1,0:T(8,128)(2,1)S(1)} %get-tuple-element.40), channel_id=1, source_target_pairs={{0,2},{1,3},{2,0},{3,1},{4,6},{5,7},{6,4},{7,5},{8,10},{9,11},{10,... | collective-permute-start | bytes 196616 | tf_op jit(solution)/shard_map/ppermute | solution.py:162
  13.3 1.0 %collective-permute-done.2 = bf16[64,512]{1,0:T(8,128)(2,1)S(1)} collective-permute-done((bf16[64,512]{1,0:T(8,128)(2,1)S(1)}, bf16[64,512]{1,0:T(8,128)(2,1)S(1)}, u32[]{:S(2)}, u32[]{:S(2)}) %collective-permute-start.2) | collective-permute-done | bytes 65568 | tf_op jit(solution)/shard_map/ppermute | solution.py:165
  14.3 1.8 %collective-permute-start.3 = (bf16[1,64,512]{2,1,0:T(8,128)(2,1)S(1)}, bf16[1,64,512]{2,1,0:T(8,128)(2,1)S(1)}, u32[]{:S(2)}, u32[]{:S(2)}) collective-permute-start(bf16[1,64,512]{2,1,0:T(8,128)(2,1)S(1)} %bitcast.8), channel_id=1, source_target_pairs={{0,4},{1,5},{2,6},{3,7},{4,0},{5,1},{6,2},{7,3},{8,12},{9,13},{10,... | collective-permute-start | bytes 196616 | tf_op jit(solution)/shard_map/ppermute | solution.py:162
  16.1 1.8 %collective-permute-done.1 = bf16[1,64,512]{2,1,0:T(8,128)(2,1)S(1)} collective-permute-done((bf16[1,64,512]{2,1,0:T(8,128)(2,1)S(1)}, bf16[1,64,512]{2,1,0:T(8,128)(2,1)S(1)}, u32[]{:S(2)}, u32[]{:S(2)}) %collective-permute-start.1) | collective-permute-done | bytes 65568 | tf_op jit(solution)/shard_map/ppermute | solution.py:162
  17.9 0.0 copy-start.1
  17.9 0.7 %collective-permute-done.3 = bf16[1,64,512]{2,1,0:T(8,128)(2,1)S(1)} collective-permute-done((bf16[1,64,512]{2,1,0:T(8,128)(2,1)S(1)}, bf16[1,64,512]{2,1,0:T(8,128)(2,1)S(1)}, u32[]{:S(2)}, u32[]{:S(2)}) %collective-permute-start.3) | collective-permute-done | bytes 65568 | tf_op jit(solution)/shard_map/ppermute | solution.py:162
  18.6 0.0 all-to-all-done.held
  18.6 0.7 %pick.1 = bf16[5,80,256]{2,1,0:T(8,128)(2,1)S(1)} custom-call(s32[6]{0:T(128)S(1)} %copy-done.1, bf16[8,80,256]{2,1,0:T(8,128)(2,1)S(1)} %all-to-all-done.held), custom_call_target="tpu_custom_call" | custom-call | bytes 327680 | tf_op jit(solution)/shard_map/pick/pallas_call | solution.py:215
  19.3 0.4 collective-permute-start.4
  19.8 2.7 %collective-permute-start.5 = (bf16[4,80,256]{2,1,0:T(8,128)(2,1)S(1)}, bf16[4,80,256]{2,1,0:T(8,128)(2,1)S(1)}, u32[]{:S(2)}, u32[]{:S(2)}) collective-permute-start(bf16[4,80,256]{2,1,0:T(8,128)(2,1)S(1)} %slice.9), channel_id=1, source_target_pairs={{0,8},{1,9},{2,10},{3,11},{4,12},{5,13},{6,14},{7,15},{8,0},{9,1},... | collective-permute-start | bytes 491528 | tf_op jit(solution)/shard_map/ppermute | solution.py:162
  22.4 5.6 %collective-permute-done.4.refs_0_ = bf16[1,80,256]{2,1,0:T(8,128)(2,1)S(1)} collective-permute-done((bf16[1,80,256]{2,1,0:T(8,128)(2,1)S(1)}, bf16[1,80,256]{2,1,0:T(8,128)(2,1)S(1)}, u32[]{:S(2)}, u32[]{:S(2)}) %collective-permute-start.4) | collective-permute-done | bytes 40992 | tf_op jit(solution)/shard_map/ppermute | solution.py:162
  28.0 0.0 collective-permute-start.9
  28.0 0.1 collective-permute-start.10
  28.2 0.0 copy-start
  28.2 0.1 collective-permute-start.11
  28.2 3.0 %collective-permute-done.5.refs_1_ = bf16[4,80,256]{2,1,0:T(8,128)(2,1)S(1)} collective-permute-done((bf16[4,80,256]{2,1,0:T(8,128)(2,1)S(1)}, bf16[4,80,256]{2,1,0:T(8,128)(2,1)S(1)}, u32[]{:S(2)}, u32[]{:S(2)}) %collective-permute-start.5) | collective-permute-done | bytes 163872 | tf_op jit(solution)/shard_map/ppermute | solution.py:162
  31.2 0.6 order.1
  31.9 1.6 %collective-permute-start.6 = (bf16[1,2,80,256]{3,2,1,0:T(8,128)(2,1)S(1)}, bf16[1,2,80,256]{3,2,1,0:T(8,128)(2,1)S(1)}, u32[]{:S(2)}, u32[]{:S(2)}) collective-permute-start(bf16[1,2,80,256]{3,2,1,0:T(8,128)(2,1)S(1)} %get-tuple-element.26), channel_id=1, source_target_pairs={{0,16},{16,0},{1,17},{17,1},{2,18},{18,2},{3,19},{19,3},{4,20},{20... | collective-permute-start | bytes 245768 | tf_op jit(solution)/shard_map/ppermute | solution.py:165
  33.4 0.7 collective-permute-start.7
  34.1 0.4 collective-permute-start.8
  34.5 0.1 collective-permute-start.12
  34.6 1.8 %collective-permute-done.6 = bf16[1,2,80,256]{3,2,1,0:T(8,128)(2,1)S(1)} collective-permute-done((bf16[1,2,80,256]{3,2,1,0:T(8,128)(2,1)S(1)}, bf16[1,2,80,256]{3,2,1,0:T(8,128)(2,1)S(1)}, u32[]{:S(2)}, u32[]{:S(2)}) %collective-permute-start.6) | collective-permute-done | bytes 81952 | tf_op jit(solution)/shard_map/ppermute | solution.py:165
  36.4 1.5 %collective-permute-done.7 = bf16[1,2,80,256]{3,2,1,0:T(8,128)(2,1)S(1)} collective-permute-done((bf16[1,2,80,256]{3,2,1,0:T(8,128)(2,1)S(1)}, bf16[1,2,80,256]{3,2,1,0:T(8,128)(2,1)S(1)}, u32[]{:S(2)}, u32[]{:S(2)}) %collective-permute-start.7) | collective-permute-done | bytes 81952 | tf_op jit(solution)/shard_map/ppermute | solution.py:162
  37.9 0.7 collective-permute-done.8
  38.6 1.1 %merge.1 = f32[128,128]{1,0:T(8,128)} custom-call(bf16[4096,128]{1,0:T(8,128)(2,1)S(1)} %copy-done, bf16[4,64,512]{2,1,0:T(8,128)(2,1)S(1)} %constant_dynamic-update-slice_fusion.refs_0_, bf16[4,64,512]{2,1,0:T(8,128)(2,1)S(1)} %constant_dynamic-update-slice_fusion.2.refs_1_, bf16[4,64,512]{2,1,0:T(8,128)(2,1)S(1)} %collective-permute-done.11.refs_2_, ...), custom_call_target="tpu_custom_call" | custom-call | flops 134217728 | bytes 1048576 | tf_op jit(solution)/shard_map/merge/pallas_call | solution.py:236
  39.7 1.3 %collective-permute-start.13 = (bf16[2,2,80,256]{3,2,1,0:T(8,128)(2,1)S(1)}, bf16[2,2,80,256]{3,2,1,0:T(8,128)(2,1)S(1)}, u32[]{:S(2)}, u32[]{:S(2)}) collective-permute-start(bf16[2,2,80,256]{3,2,1,0:T(8,128)(2,1)S(1)} %pad_maximum_fusion), channel_id=1, source_target_pairs={{0,2},{1,3},{2,0},{3,1},{4,6},{5,7},{6,4},{7,5},{8,10},{9,11},{10,... | collective-permute-start | bytes 491528 | tf_op jit(solution)/shard_map/ppermute | solution.py:162
  41.0 0.1 collective-permute-start.15
  41.1 0.6 collective-permute-start.17
  41.8 4.7 %collective-permute-done.17 = bf16[2,2,80,256]{3,2,1,0:T(8,128)(2,1)S(1)} collective-permute-done((bf16[2,2,80,256]{3,2,1,0:T(8,128)(2,1)S(1)}, bf16[2,2,80,256]{3,2,1,0:T(8,128)(2,1)S(1)}, u32[]{:S(2)}, u32[]{:S(2)}) %collective-permute-start.17) | collective-permute-done | bytes 163872 | tf_op jit(solution)/shard_map/ppermute | solution.py:165
  46.5 1.0 %collective-permute-start.18 = (bf16[4,2,80,256]{3,2,1,0:T(8,128)(2,1)S(1)}, bf16[4,2,80,256]{3,2,1,0:T(8,128)(2,1)S(1)}, u32[]{:S(2)}, u32[]{:S(2)}) collective-permute-start(bf16[4,2,80,256]{3,2,1,0:T(8,128)(2,1)S(1)} %constant_dynamic-update-slice_fusion.8.refs_8_), channel_id=1, source_target_pairs={{0,2},{1,3},{2,0},{3,1},{4,6},{5,7},{6,4},{7,5},{8,10},{9,11},{10,... | collective-permute-start | bytes 983048 | tf_op jit(solution)/shard_map/ppermute | solution.py:162
  47.6 0.6 collective-permute-start.16
  48.2 1.9 %collective-permute-start.14 = (bf16[4,2,80,256]{3,2,1,0:T(8,128)(2,1)S(1)}, bf16[4,2,80,256]{3,2,1,0:T(8,128)(2,1)S(1)}, u32[]{:S(2)}, u32[]{:S(2)}) collective-permute-start(bf16[4,2,80,256]{3,2,1,0:T(8,128)(2,1)S(1)} %constant_dynamic-update-slice_fusion.4.refs_0_), channel_id=1, source_target_pairs={{0,4},{1,5},{2,6},{3,7},{4,0},{5,1},{6,2},{7,3},{8,12},{9,13},{10,... | collective-permute-start | bytes 983048 | tf_op jit(solution)/shard_map/ppermute | solution.py:162
  50.0 4.2 %all-to-all-start.1 = ((f32[32,4,128]{2,1,0:T(4,128)}), f32[32,4,128]{2,1,0:T(4,128)S(1)}, u32[]{:S(2)}, u32[]{:S(2)}) async-start(f32[32,4,128]{2,1,0:T(4,128)} %bitcast.4), calls=%async_computation.1 | async-start | bytes 131072 | tf_op jit(solution)/shard_map/all_to_all | solution.py:269
  54.3 0.3 collective-permute-start.21
  54.6 0.3 collective-permute-start.19
  54.9 6.8 %all-to-all-done.1.start = f32[32,4,128]{2,1,0:T(4,128)S(1)} async-done(((f32[32,4,128]{2,1,0:T(4,128)}), f32[32,4,128]{2,1,0:T(4,128)S(1)}, u32[]{:S(2)}, u32[]{:S(2)}) %all-to-all-start.1) | async-done | bytes 65568 | tf_op jit(solution)/shard_map/all_to_all | solution.py:269
  61.7 0.1 collective-permute-start.20
  61.8 0.4 collective-permute-start.22
  62.2 0.1 collective-permute-start.24
  62.3 1.0 %collective-permute-done.20.refs_3_ = bf16[4,2,80,256]{3,2,1,0:T(8,128)(2,1)S(1)} collective-permute-done((bf16[4,2,80,256]{3,2,1,0:T(8,128)(2,1)S(1)}, bf16[4,2,80,256]{3,2,1,0:T(8,128)(2,1)S(1)}, u32[]{:S(2)}, u32[]{:S(2)}) %collective-permute-start.20) | collective-permute-done | bytes 327712 | tf_op jit(solution)/shard_map/ppermute | solution.py:162
  63.3 0.5 collective-permute-done.22.refs_7_
  63.8 0.5 collective-permute-done.24.refs_11_
  64.3 5.1 %chain0.1 = bf16[4,2048]{1,0:T(4,128)(2,1)} custom-call(s32[6]{0:T(128)S(1)} %copy-done.2, f32[32,4,128]{2,1,0:T(4,128)S(1)} %all-to-all-done.1.start, bf16[4,2,80,256]{3,2,1,0:T(8,128)(2,1)S(1)} %constant_dynamic-update-slice_fusion.4.refs_0_, bf16[4,2,80,256]{3,2,1,0:T(8,128)(2,1)S(1)} %collective-permute-done.14.refs_1_, ...), custom_call_target="tpu_custom_call" | custom-call | flops 201326592 | bytes 3932160 | tf_op jit(solution)/shard_map/chain0/pallas_call | solution.py:287
  (37 shorter events, 0.3 us)
Async XLA Ops:
  0.0 9.7 %collective-permute-start = (bf16[64,512]{1,0:T(8,128)(2,1)}, bf16[64,512]{1,0:T(8,128)(2,1)S(1)}, u32[]{:S(2)}, u32[]{:S(2)}) collective-permute-start(bf16[64,512]{1,0:T(8,128)(2,1)} %param.7), channel_id=1, source_target_pairs={{0,8},{1,9},{2,10},{3,11},{4,12},{5,13},{6,14},{7,15},{8,0},{9,1},... | collective-permute-start | bytes 196616 | tf_op jit(solution)/shard_map/ppermute | solution.py:162
  5.7 4.0 %copy-start.3 = (bf16[64,512]{1,0:T(8,128)(2,1)S(1)}, bf16[64,512]{1,0:T(8,128)(2,1)}, u32[]{:S(2)}) copy-start(bf16[64,512]{1,0:T(8,128)(2,1)} %param.7) | copy-start | bytes 196612
  5.8 12.8 %all-to-all-start = ((bf16[8,80,256]{2,1,0:T(8,128)(2,1)}), bf16[8,80,256]{2,1,0:T(8,128)(2,1)S(1)}, u32[]{:S(2)}, u32[]{:S(2)}) async-start(bf16[8,80,256]{2,1,0:T(8,128)(2,1)} %pack.1), calls=%async_computation | async-start | bytes 655360 | tf_op jit(solution)/shard_map/all_to_all | solution.py:186
  9.7 4.6 %collective-permute-start.2 = (bf16[64,512]{1,0:T(8,128)(2,1)S(1)}, bf16[64,512]{1,0:T(8,128)(2,1)S(1)}, u32[]{:S(2)}, u32[]{:S(2)}) collective-permute-start(bf16[64,512]{1,0:T(8,128)(2,1)S(1)} %get-tuple-element.39), channel_id=1, source_target_pairs={{0,16},{16,0},{1,17},{17,1},{2,18},{18,2},{3,19},{19,3},{4,20},{20... | collective-permute-start | bytes 196616 | tf_op jit(solution)/shard_map/ppermute | solution.py:165
  11.3 6.5 %collective-permute-start.1 = (bf16[1,64,512]{2,1,0:T(8,128)(2,1)S(1)}, bf16[1,64,512]{2,1,0:T(8,128)(2,1)S(1)}, u32[]{:S(2)}, u32[]{:S(2)}) collective-permute-start(bf16[1,64,512]{2,1,0:T(8,128)(2,1)S(1)} %get-tuple-element.40), channel_id=1, source_target_pairs={{0,2},{1,3},{2,0},{3,1},{4,6},{5,7},{6,4},{7,5},{8,10},{9,11},{10,... | collective-permute-start | bytes 196616 | tf_op jit(solution)/shard_map/ppermute | solution.py:162
  14.3 4.3 %collective-permute-start.3 = (bf16[1,64,512]{2,1,0:T(8,128)(2,1)S(1)}, bf16[1,64,512]{2,1,0:T(8,128)(2,1)S(1)}, u32[]{:S(2)}, u32[]{:S(2)}) collective-permute-start(bf16[1,64,512]{2,1,0:T(8,128)(2,1)S(1)} %bitcast.8), channel_id=1, source_target_pairs={{0,4},{1,5},{2,6},{3,7},{4,0},{5,1},{6,2},{7,3},{8,12},{9,13},{10,... | collective-permute-start | bytes 196616 | tf_op jit(solution)/shard_map/ppermute | solution.py:162
  17.9 0.7 %copy-start.1 = (s32[6]{0:T(128)S(1)}, s32[6]{0:T(128)}, u32[]{:S(2)}) copy-start(s32[6]{0:T(128)} %owners.3) | copy-start | bytes 76
  19.3 8.7 %collective-permute-start.4 = (bf16[1,80,256]{2,1,0:T(8,128)(2,1)S(1)}, bf16[1,80,256]{2,1,0:T(8,128)(2,1)S(1)}, u32[]{:S(2)}, u32[]{:S(2)}) collective-permute-start(bf16[1,80,256]{2,1,0:T(8,128)(2,1)S(1)} %slice.8), channel_id=1, source_target_pairs={{0,8},{1,9},{2,10},{3,11},{4,12},{5,13},{6,14},{7,15},{8,0},{9,1},... | collective-permute-start | bytes 122888 | tf_op jit(solution)/shard_map/ppermute | solution.py:162
  19.8 11.5 %collective-permute-start.5 = (bf16[4,80,256]{2,1,0:T(8,128)(2,1)S(1)}, bf16[4,80,256]{2,1,0:T(8,128)(2,1)S(1)}, u32[]{:S(2)}, u32[]{:S(2)}) collective-permute-start(bf16[4,80,256]{2,1,0:T(8,128)(2,1)S(1)} %slice.9), channel_id=1, source_target_pairs={{0,8},{1,9},{2,10},{3,11},{4,12},{5,13},{6,14},{7,15},{8,0},{9,1},... | collective-permute-start | bytes 491528 | tf_op jit(solution)/shard_map/ppermute | solution.py:162
  28.0 6.1 %collective-permute-start.9 = (bf16[2,64,512]{2,1,0:T(8,128)(2,1)S(1)}, bf16[2,64,512]{2,1,0:T(8,128)(2,1)S(1)}, u32[]{:S(2)}, u32[]{:S(2)}) collective-permute-start(bf16[2,64,512]{2,1,0:T(8,128)(2,1)S(1)} %pad_maximum_fusion.3), channel_id=1, source_target_pairs={{0,4},{1,5},{2,6},{3,7},{4,0},{5,1},{6,2},{7,3},{8,12},{9,13},{10,... | collective-permute-start | bytes 393224 | tf_op jit(solution)/shard_map/ppermute | solution.py:162
  28.0 6.4 %collective-permute-start.10 = (bf16[2,64,512]{2,1,0:T(8,128)(2,1)S(1)}, bf16[2,64,512]{2,1,0:T(8,128)(2,1)S(1)}, u32[]{:S(2)}, u32[]{:S(2)}) collective-permute-start(bf16[2,64,512]{2,1,0:T(8,128)(2,1)S(1)} %pad_maximum_fusion.4), channel_id=1, source_target_pairs={{0,2},{1,3},{2,0},{3,1},{4,6},{5,7},{6,4},{7,5},{8,10},{9,11},{10,... | collective-permute-start | bytes 393224 | tf_op jit(solution)/shard_map/ppermute | solution.py:162
  28.2 10.4 %copy-start = (bf16[4096,128]{1,0:T(8,128)(2,1)S(1)}, bf16[4096,128]{1,0:T(8,128)(2,1)}, u32[]{:S(2)}) copy-start(bf16[4096,128]{1,0:T(8,128)(2,1)} %sub.6) | copy-start | bytes 3145732
  28.2 10.4 %collective-permute-start.11 = (bf16[4,64,512]{2,1,0:T(8,128)(2,1)S(1)}, bf16[4,64,512]{2,1,0:T(8,128)(2,1)S(1)}, u32[]{:S(2)}, u32[]{:S(2)}) collective-permute-start(bf16[4,64,512]{2,1,0:T(8,128)(2,1)S(1)} %constant_dynamic-update-slice_fusion.refs_0_), channel_id=1, source_target_pairs={{0,1},{1,0},{2,3},{3,2},{4,5},{5,4},{6,7},{7,6},{8,9},{9,8},{10,11... | collective-permute-start | bytes 786440 | tf_op jit(solution)/shard_map/ppermute | solution.py:162
  31.9 4.5 %collective-permute-start.6 = (bf16[1,2,80,256]{3,2,1,0:T(8,128)(2,1)S(1)}, bf16[1,2,80,256]{3,2,1,0:T(8,128)(2,1)S(1)}, u32[]{:S(2)}, u32[]{:S(2)}) collective-permute-start(bf16[1,2,80,256]{3,2,1,0:T(8,128)(2,1)S(1)} %get-tuple-element.26), channel_id=1, source_target_pairs={{0,16},{16,0},{1,17},{17,1},{2,18},{18,2},{3,19},{19,3},{4,20},{20... | collective-permute-start | bytes 245768 | tf_op jit(solution)/shard_map/ppermute | solution.py:165
  33.4 4.4 %collective-permute-start.7 = (bf16[1,2,80,256]{3,2,1,0:T(8,128)(2,1)S(1)}, bf16[1,2,80,256]{3,2,1,0:T(8,128)(2,1)S(1)}, u32[]{:S(2)}, u32[]{:S(2)}) collective-permute-start(bf16[1,2,80,256]{3,2,1,0:T(8,128)(2,1)S(1)} %get-tuple-element.27), channel_id=1, source_target_pairs={{0,2},{1,3},{2,0},{3,1},{4,6},{5,7},{6,4},{7,5},{8,10},{9,11},{10,... | collective-permute-start | bytes 245768 | tf_op jit(solution)/shard_map/ppermute | solution.py:162
  34.1 4.4 %collective-permute-start.8 = (bf16[1,2,80,256]{3,2,1,0:T(8,128)(2,1)S(1)}, bf16[1,2,80,256]{3,2,1,0:T(8,128)(2,1)S(1)}, u32[]{:S(2)}, u32[]{:S(2)}) collective-permute-start(bf16[1,2,80,256]{3,2,1,0:T(8,128)(2,1)S(1)} %get-tuple-element.28), channel_id=1, source_target_pairs={{0,4},{1,5},{2,6},{3,7},{4,0},{5,1},{6,2},{7,3},{8,12},{9,13},{10,... | collective-permute-start | bytes 245768 | tf_op jit(solution)/shard_map/ppermute | solution.py:162
  34.5 4.1 %collective-permute-start.12 = (bf16[4,64,512]{2,1,0:T(8,128)(2,1)S(1)}, bf16[4,64,512]{2,1,0:T(8,128)(2,1)S(1)}, u32[]{:S(2)}, u32[]{:S(2)}) collective-permute-start(bf16[4,64,512]{2,1,0:T(8,128)(2,1)S(1)} %constant_dynamic-update-slice_fusion.2.refs_1_), channel_id=1, source_target_pairs={{0,1},{1,0},{2,3},{3,2},{4,5},{5,4},{6,7},{7,6},{8,9},{9,8},{10,11... | collective-permute-start | bytes 786440 | tf_op jit(solution)/shard_map/ppermute | solution.py:162
  39.7 8.5 %collective-permute-start.13 = (bf16[2,2,80,256]{3,2,1,0:T(8,128)(2,1)S(1)}, bf16[2,2,80,256]{3,2,1,0:T(8,128)(2,1)S(1)}, u32[]{:S(2)}, u32[]{:S(2)}) collective-permute-start(bf16[2,2,80,256]{3,2,1,0:T(8,128)(2,1)S(1)} %pad_maximum_fusion), channel_id=1, source_target_pairs={{0,2},{1,3},{2,0},{3,1},{4,6},{5,7},{6,4},{7,5},{8,10},{9,11},{10,... | collective-permute-start | bytes 491528 | tf_op jit(solution)/shard_map/ppermute | solution.py:162
  41.0 6.5 %collective-permute-start.15 = (bf16[2,2,80,256]{3,2,1,0:T(8,128)(2,1)S(1)}, bf16[2,2,80,256]{3,2,1,0:T(8,128)(2,1)S(1)}, u32[]{:S(2)}, u32[]{:S(2)}) collective-permute-start(bf16[2,2,80,256]{3,2,1,0:T(8,128)(2,1)S(1)} %pad_maximum_fusion.1), channel_id=1, source_target_pairs={{0,4},{1,5},{2,6},{3,7},{4,0},{5,1},{6,2},{7,3},{8,12},{9,13},{10,... | collective-permute-start | bytes 491528 | tf_op jit(solution)/shard_map/ppermute | solution.py:162
  41.1 5.4 %collective-permute-start.17 = (bf16[2,2,80,256]{3,2,1,0:T(8,128)(2,1)S(1)}, bf16[2,2,80,256]{3,2,1,0:T(8,128)(2,1)S(1)}, u32[]{:S(2)}, u32[]{:S(2)}) collective-permute-start(bf16[2,2,80,256]{3,2,1,0:T(8,128)(2,1)S(1)} %pad_maximum_fusion.2), channel_id=1, source_target_pairs={{0,16},{16,0},{1,17},{17,1},{2,18},{18,2},{3,19},{19,3},{4,20},{20... | collective-permute-start | bytes 491528 | tf_op jit(solution)/shard_map/ppermute | solution.py:165
  46.5 8.1 %collective-permute-start.18 = (bf16[4,2,80,256]{3,2,1,0:T(8,128)(2,1)S(1)}, bf16[4,2,80,256]{3,2,1,0:T(8,128)(2,1)S(1)}, u32[]{:S(2)}, u32[]{:S(2)}) collective-permute-start(bf16[4,2,80,256]{3,2,1,0:T(8,128)(2,1)S(1)} %constant_dynamic-update-slice_fusion.8.refs_8_), channel_id=1, source_target_pairs={{0,2},{1,3},{2,0},{3,1},{4,6},{5,7},{6,4},{7,5},{8,10},{9,11},{10,... | collective-permute-start | bytes 983048 | tf_op jit(solution)/shard_map/ppermute | solution.py:162
  47.6 14.1 %collective-permute-start.16 = (bf16[4,2,80,256]{3,2,1,0:T(8,128)(2,1)S(1)}, bf16[4,2,80,256]{3,2,1,0:T(8,128)(2,1)S(1)}, u32[]{:S(2)}, u32[]{:S(2)}) collective-permute-start(bf16[4,2,80,256]{3,2,1,0:T(8,128)(2,1)S(1)} %constant_dynamic-update-slice_fusion.6.refs_4_), channel_id=1, source_target_pairs={{0,16},{16,0},{1,17},{17,1},{2,18},{18,2},{3,19},{19,3},{4,20},{20... | collective-permute-start | bytes 983048 | tf_op jit(solution)/shard_map/ppermute | solution.py:165
  48.2 13.5 %collective-permute-start.14 = (bf16[4,2,80,256]{3,2,1,0:T(8,128)(2,1)S(1)}, bf16[4,2,80,256]{3,2,1,0:T(8,128)(2,1)S(1)}, u32[]{:S(2)}, u32[]{:S(2)}) collective-permute-start(bf16[4,2,80,256]{3,2,1,0:T(8,128)(2,1)S(1)} %constant_dynamic-update-slice_fusion.4.refs_0_), channel_id=1, source_target_pairs={{0,4},{1,5},{2,6},{3,7},{4,0},{5,1},{6,2},{7,3},{8,12},{9,13},{10,... | collective-permute-start | bytes 983048 | tf_op jit(solution)/shard_map/ppermute | solution.py:162
  50.0 12.2 %collective-permute-start.23 = (bf16[4,2,80,256]{3,2,1,0:T(8,128)(2,1)S(1)}, bf16[4,2,80,256]{3,2,1,0:T(8,128)(2,1)S(1)}, u32[]{:S(2)}, u32[]{:S(2)}) collective-permute-start(bf16[4,2,80,256]{3,2,1,0:T(8,128)(2,1)S(1)} %constant_dynamic-update-slice_fusion.8.refs_8_), channel_id=1, source_target_pairs={{0,1},{1,0},{2,3},{3,2},{4,5},{5,4},{6,7},{7,6},{8,9},{9,8},{10,11... | collective-permute-start | bytes 983048 | tf_op jit(solution)/shard_map/ppermute | solution.py:162
  50.0 14.2 %copy-start.2 = (s32[6]{0:T(128)S(1)}, s32[6]{0:T(128)}, u32[]{:S(2)}) copy-start(s32[6]{0:T(128)} %offsets.1) | copy-start | bytes 76
  50.0 11.6 %all-to-all-start.1 = ((f32[32,4,128]{2,1,0:T(4,128)}), f32[32,4,128]{2,1,0:T(4,128)S(1)}, u32[]{:S(2)}, u32[]{:S(2)}) async-start(f32[32,4,128]{2,1,0:T(4,128)} %bitcast.4), calls=%async_computation.1 | async-start | bytes 131072 | tf_op jit(solution)/shard_map/all_to_all | solution.py:269
  54.3 8.1 %collective-permute-start.21 = (bf16[4,2,80,256]{3,2,1,0:T(8,128)(2,1)S(1)}, bf16[4,2,80,256]{3,2,1,0:T(8,128)(2,1)S(1)}, u32[]{:S(2)}, u32[]{:S(2)}) collective-permute-start(bf16[4,2,80,256]{3,2,1,0:T(8,128)(2,1)S(1)} %constant_dynamic-update-slice_fusion.6.refs_4_), channel_id=1, source_target_pairs={{0,1},{1,0},{2,3},{3,2},{4,5},{5,4},{6,7},{7,6},{8,9},{9,8},{10,11... | collective-permute-start | bytes 983048 | tf_op jit(solution)/shard_map/ppermute | solution.py:162
  54.6 7.7 %collective-permute-start.19 = (bf16[4,2,80,256]{3,2,1,0:T(8,128)(2,1)S(1)}, bf16[4,2,80,256]{3,2,1,0:T(8,128)(2,1)S(1)}, u32[]{:S(2)}, u32[]{:S(2)}) collective-permute-start(bf16[4,2,80,256]{3,2,1,0:T(8,128)(2,1)S(1)} %constant_dynamic-update-slice_fusion.4.refs_0_), channel_id=1, source_target_pairs={{0,1},{1,0},{2,3},{3,2},{4,5},{5,4},{6,7},{7,6},{8,9},{9,8},{10,11... | collective-permute-start | bytes 983048 | tf_op jit(solution)/shard_map/ppermute | solution.py:162
  61.7 1.6 %collective-permute-start.20 = (bf16[4,2,80,256]{3,2,1,0:T(8,128)(2,1)S(1)}, bf16[4,2,80,256]{3,2,1,0:T(8,128)(2,1)S(1)}, u32[]{:S(2)}, u32[]{:S(2)}) collective-permute-start(bf16[4,2,80,256]{3,2,1,0:T(8,128)(2,1)S(1)} %collective-permute-done.14.refs_1_), channel_id=1, source_target_pairs={{0,1},{1,0},{2,3},{3,2},{4,5},{5,4},{6,7},{7,6},{8,9},{9,8},{10,11... | collective-permute-start | bytes 983048 | tf_op jit(solution)/shard_map/ppermute | solution.py:162
  61.8 2.0 %collective-permute-start.22 = (bf16[4,2,80,256]{3,2,1,0:T(8,128)(2,1)S(1)}, bf16[4,2,80,256]{3,2,1,0:T(8,128)(2,1)S(1)}, u32[]{:S(2)}, u32[]{:S(2)}) collective-permute-start(bf16[4,2,80,256]{3,2,1,0:T(8,128)(2,1)S(1)} %collective-permute-done.16.refs_5_), channel_id=1, source_target_pairs={{0,1},{1,0},{2,3},{3,2},{4,5},{5,4},{6,7},{7,6},{8,9},{9,8},{10,11... | collective-permute-start | bytes 983048 | tf_op jit(solution)/shard_map/ppermute | solution.py:162
  62.2 2.1 %collective-permute-start.24 = (bf16[4,2,80,256]{3,2,1,0:T(8,128)(2,1)S(1)}, bf16[4,2,80,256]{3,2,1,0:T(8,128)(2,1)S(1)}, u32[]{:S(2)}, u32[]{:S(2)}) collective-permute-start(bf16[4,2,80,256]{3,2,1,0:T(8,128)(2,1)S(1)} %collective-permute-done.18.refs_9_), channel_id=1, source_target_pairs={{0,1},{1,0},{2,3},{3,2},{4,5},{5,4},{6,7},{7,6},{8,9},{9,8},{10,11... | collective-permute-start | bytes 983048 | tf_op jit(solution)/shard_map/ppermute | solution.py:162

commit v27 on v24

--- a/solution.py
+++ b/solution.py
@@ -9,7 +9,7 @@
 
 GROUPS = 6
 COLOURS = 3
-CHAINS = ((0, 1, 2),)
+CHAINS = ((0,), (1, 2))
 HALF = 8
 SLICES = 2 * HALF
 VMEM = pl.BlockSpec(memory_space=pltpu.VMEM)

time: 68 us -> 66 us (0.971)
  blocking collectives: 0 us -> 11.9 us
  waiting for transfers between devices: 28.3 us -> 18.7 us
  starting transfers between devices: 29.7 us -> 25.4 us
    all_to_all x0 -> x1, blocking collectives: none -> 11.9 us  [local(): lax.all_to_all(merged.reshape(rows * cols, each, width), ('row', 'col'),...]
    all_to_all x1 -> x0, waiting for transfers between devices: 6.83 us -> none  [local(): lax.all_to_all(merged.reshape(rows * cols, each, width), ('row', 'col'),...]
    ppermute x4, waiting for transfers between devices: 7.16 us -> 3.19 us  [over_row(): return lax.ppermute(x, 'row', [(r, r ^ mask) for r in range(rows)])]
    all_to_all x1 -> x0, starting transfers between devices: 3.75 us -> none  [local(): lax.all_to_all(merged.reshape(rows * cols, each, width), ('row', 'col'),...]
    ppermute x21, starting transfers between devices: 17.8 us -> 16 us  [over_col(): return lax.ppermute(x, 'col', [(c, c ^ mask) for c in range(cols)])]
    ppermute x21, waiting for transfers between devices: 14.3 us -> 15.5 us  [over_col(): return lax.ppermute(x, 'col', [(c, c ^ mask) for c in range(cols)])]
    ppermute x4, starting transfers between devices: 4.24 us -> 5.41 us  [over_row(): return lax.ppermute(x, 'row', [(r, r ^ mask) for r in range(rows)])]
    pallas_call x1 -> x2, Pallas kernels: 5.08 us -> 5.68 us  [local(): pl.pallas_call(functools.partial(chain_kernel, cols, groups, slots, sum((...]
  transfers between devices with their start and end apart: 27 -> 26, of which waited for: 13 -> 10; matrix products, arithmetic and copies ran while one was open for 0% -> 0% of each run, Pallas kernels for 5% -> 7%
where the time goes in v27:
time: 66 us; the launch traced here: 65.7 us
  starting transfers between devices  25.4 us (38%)
  waiting for transfers between devices  18.7 us (28%)
  blocking collectives  11.9 us (18%)
  Pallas kernels  9.18 us (14%)
    ppermute x21, starting transfers between devices, over_col(): return lax.ppermute(x, 'col', [(c, c ^ mask) for c in range(cols)])  16 us
    ppermute x21, waiting for transfers between devices, over_col(): return lax.ppermute(x, 'col', [(c, c ^ mask) for c in range(cols)])  15.5 us
    all_to_all x1, blocking collectives, local(): lax.all_to_all(merged.reshape(rows * cols, each, width), ('row', 'col'),...  11.9 us
    pallas_call x2, Pallas kernels, local(): pl.pallas_call(functools.partial(chain_kernel, cols, groups, slots, sum((...  5.68 us
    ppermute x4, starting transfers between devices, over_row(): return lax.ppermute(x, 'row', [(r, r ^ mask) for r in range(rows)])  5.41 us
    all_to_all x1, starting transfers between devices, local(): slices = lax.all_to_all(packed, 'col', 0, 0, axis_index_groups=members)  3.95 us
    ppermute x4, waiting for transfers between devices, over_row(): return lax.ppermute(x, 'row', [(r, r ^ mask) for r in range(rows)])  3.19 us
    pallas_call x1, Pallas kernels, local(): pl.pallas_call(pack_kernel, out_shape=jax.ShapeDtypeStruct((HALF,) + piec...  1.69 us
  transfers between devices with their start and end apart: 26, of which 10 were waited for; matrix products, arithmetic and copies ran while one was open for 0% of the time, Pallas kernels for 7%

profile of v27, /device:TPU:0, one launch (start us, length us, event | category | flops | bytes accessed | tf_op | source)
XLA Modules:
  0.0 65.7 jit_solution(10533959717843267271)
XLA Ops:
  0.0 4.0 %collective-permute-start = (bf16[64,512]{1,0:T(8,128)(2,1)}, bf16[64,512]{1,0:T(8,128)(2,1)S(1)}, u32[]{:S(2)}, u32[]{:S(2)}) collective-permute-start(bf16[64,512]{1,0:T(8,128)(2,1)} %param.7), channel_id=1, source_target_pairs={{0,8},{1,9},{2,10},{3,11},{4,12},{5,13},{6,14},{7,15},{8,0},{9,1},... | collective-permute-start | bytes 196616 | tf_op jit(solution)/shard_map/ppermute | solution.py:162
  4.0 1.7 %pack.1 = bf16[8,80,256]{2,1,0:T(8,128)(2,1)} custom-call(bf16[16,64,256]{2,1,0:T(8,128)(2,1)} %bitcast.7, bf16[16,16,256]{2,1,0:T(8,128)(2,1)} %bitcast.8), custom_call_target="tpu_custom_call" | custom-call | bytes 655360 | tf_op jit(solution)/shard_map/pack/pallas_call | solution.py:175
  5.7 0.0 copy-start.3
  5.7 4.0 %all-to-all-start = ((bf16[8,80,256]{2,1,0:T(8,128)(2,1)}), bf16[8,80,256]{2,1,0:T(8,128)(2,1)S(1)}, u32[]{:S(2)}, u32[]{:S(2)}) async-start(bf16[8,80,256]{2,1,0:T(8,128)(2,1)} %pack.1), calls=%async_computation | async-start | bytes 655360 | tf_op jit(solution)/shard_map/all_to_all | solution.py:186
  9.7 1.6 %collective-permute-start.2 = (bf16[64,512]{1,0:T(8,128)(2,1)S(1)}, bf16[64,512]{1,0:T(8,128)(2,1)S(1)}, u32[]{:S(2)}, u32[]{:S(2)}) collective-permute-start(bf16[64,512]{1,0:T(8,128)(2,1)S(1)} %get-tuple-element.31), channel_id=1, source_target_pairs={{0,16},{16,0},{1,17},{17,1},{2,18},{18,2},{3,19},{19,3},{4,20},{20... | collective-permute-start | bytes 196616 | tf_op jit(solution)/shard_map/ppermute | solution.py:165
  11.3 2.0 %collective-permute-start.1 = (bf16[1,64,512]{2,1,0:T(8,128)(2,1)S(1)}, bf16[1,64,512]{2,1,0:T(8,128)(2,1)S(1)}, u32[]{:S(2)}, u32[]{:S(2)}) collective-permute-start(bf16[1,64,512]{2,1,0:T(8,128)(2,1)S(1)} %get-tuple-element.32), channel_id=1, source_target_pairs={{0,2},{1,3},{2,0},{3,1},{4,6},{5,7},{6,4},{7,5},{8,10},{9,11},{10,... | collective-permute-start | bytes 196616 | tf_op jit(solution)/shard_map/ppermute | solution.py:162
  13.3 1.0 %collective-permute-done.2 = bf16[64,512]{1,0:T(8,128)(2,1)S(1)} collective-permute-done((bf16[64,512]{1,0:T(8,128)(2,1)S(1)}, bf16[64,512]{1,0:T(8,128)(2,1)S(1)}, u32[]{:S(2)}, u32[]{:S(2)}) %collective-permute-start.2) | collective-permute-done | bytes 65568 | tf_op jit(solution)/shard_map/ppermute | solution.py:165
  14.3 1.8 %collective-permute-start.3 = (bf16[1,64,512]{2,1,0:T(8,128)(2,1)S(1)}, bf16[1,64,512]{2,1,0:T(8,128)(2,1)S(1)}, u32[]{:S(2)}, u32[]{:S(2)}) collective-permute-start(bf16[1,64,512]{2,1,0:T(8,128)(2,1)S(1)} %bitcast.9), channel_id=1, source_target_pairs={{0,4},{1,5},{2,6},{3,7},{4,0},{5,1},{6,2},{7,3},{8,12},{9,13},{10,... | collective-permute-start | bytes 196616 | tf_op jit(solution)/shard_map/ppermute | solution.py:162
  16.1 1.8 %collective-permute-done.1 = bf16[1,64,512]{2,1,0:T(8,128)(2,1)S(1)} collective-permute-done((bf16[1,64,512]{2,1,0:T(8,128)(2,1)S(1)}, bf16[1,64,512]{2,1,0:T(8,128)(2,1)S(1)}, u32[]{:S(2)}, u32[]{:S(2)}) %collective-permute-start.1) | collective-permute-done | bytes 65568 | tf_op jit(solution)/shard_map/ppermute | solution.py:162
  17.9 0.0 copy-start.1
  17.9 0.7 %collective-permute-done.3 = bf16[1,64,512]{2,1,0:T(8,128)(2,1)S(1)} collective-permute-done((bf16[1,64,512]{2,1,0:T(8,128)(2,1)S(1)}, bf16[1,64,512]{2,1,0:T(8,128)(2,1)S(1)}, u32[]{:S(2)}, u32[]{:S(2)}) %collective-permute-start.3) | collective-permute-done | bytes 65568 | tf_op jit(solution)/shard_map/ppermute | solution.py:162
  18.6 0.0 all-to-all-done.held
  18.6 0.7 %pick.1 = bf16[5,80,256]{2,1,0:T(8,128)(2,1)S(1)} custom-call(s32[6]{0:T(128)S(1)} %copy-done.1, bf16[8,80,256]{2,1,0:T(8,128)(2,1)S(1)} %all-to-all-done.held), custom_call_target="tpu_custom_call" | custom-call | bytes 327680 | tf_op jit(solution)/shard_map/pick/pallas_call | solution.py:215
  19.3 0.4 collective-permute-start.4
  19.8 2.6 %collective-permute-start.5 = (bf16[4,80,256]{2,1,0:T(8,128)(2,1)S(1)}, bf16[4,80,256]{2,1,0:T(8,128)(2,1)S(1)}, u32[]{:S(2)}, u32[]{:S(2)}) collective-permute-start(bf16[4,80,256]{2,1,0:T(8,128)(2,1)S(1)} %slice.9), channel_id=1, source_target_pairs={{0,8},{1,9},{2,10},{3,11},{4,12},{5,13},{6,14},{7,15},{8,0},{9,1},... | collective-permute-start | bytes 491528 | tf_op jit(solution)/shard_map/ppermute | solution.py:162
  22.4 5.6 %collective-permute-done.4.refs_0_ = bf16[1,80,256]{2,1,0:T(8,128)(2,1)S(1)} collective-permute-done((bf16[1,80,256]{2,1,0:T(8,128)(2,1)S(1)}, bf16[1,80,256]{2,1,0:T(8,128)(2,1)S(1)}, u32[]{:S(2)}, u32[]{:S(2)}) %collective-permute-start.4) | collective-permute-done | bytes 40992 | tf_op jit(solution)/shard_map/ppermute | solution.py:162
  28.0 0.1 collective-permute-start.16
  28.1 0.1 collective-permute-start.17
  28.2 3.0 %collective-permute-done.5.refs_1_ = bf16[4,80,256]{2,1,0:T(8,128)(2,1)S(1)} collective-permute-done((bf16[4,80,256]{2,1,0:T(8,128)(2,1)S(1)}, bf16[4,80,256]{2,1,0:T(8,128)(2,1)S(1)}, u32[]{:S(2)}, u32[]{:S(2)}) %collective-permute-start.5) | collective-permute-done | bytes 163872 | tf_op jit(solution)/shard_map/ppermute | solution.py:162
  31.2 0.6 order.1
  31.9 0.1 collective-permute-start.12
  32.0 1.0 %collective-permute-start.9 = (bf16[1,2,80,256]{3,2,1,0:T(8,128)(2,1)S(1)}, bf16[1,2,80,256]{3,2,1,0:T(8,128)(2,1)S(1)}, u32[]{:S(2)}, u32[]{:S(2)}) collective-permute-start(bf16[1,2,80,256]{3,2,1,0:T(8,128)(2,1)S(1)} %get-tuple-element.23), channel_id=1, source_target_pairs={{0,2},{1,3},{2,0},{3,1},{4,6},{5,7},{6,4},{7,5},{8,10},{9,11},{10,... | collective-permute-start | bytes 245768 | tf_op jit(solution)/shard_map/ppermute | solution.py:162
  33.0 0.0 collective-permute-done.15
  33.0 1.6 %collective-permute-start.6 = (bf16[1,2,80,256]{3,2,1,0:T(8,128)(2,1)S(1)}, bf16[1,2,80,256]{3,2,1,0:T(8,128)(2,1)S(1)}, u32[]{:S(2)}, u32[]{:S(2)}) collective-permute-start(bf16[1,2,80,256]{3,2,1,0:T(8,128)(2,1)S(1)} %get-tuple-element.22), channel_id=1, source_target_pairs={{0,16},{16,0},{1,17},{17,1},{2,18},{18,2},{3,19},{19,3},{4,20},{20... | collective-permute-start | bytes 245768 | tf_op jit(solution)/shard_map/ppermute | solution.py:165
  34.6 0.1 collective-permute-start.18
  34.7 1.7 %collective-permute-done.12 = bf16[1,2,80,256]{3,2,1,0:T(8,128)(2,1)S(1)} collective-permute-done((bf16[1,2,80,256]{3,2,1,0:T(8,128)(2,1)S(1)}, bf16[1,2,80,256]{3,2,1,0:T(8,128)(2,1)S(1)}, u32[]{:S(2)}, u32[]{:S(2)}) %collective-permute-start.12) | collective-permute-done | bytes 81952 | tf_op jit(solution)/shard_map/ppermute | solution.py:162
  36.4 0.0 copy-start
  36.4 1.6 %collective-permute-start.13 = (bf16[2,2,80,256]{3,2,1,0:T(8,128)(2,1)S(1)}, bf16[2,2,80,256]{3,2,1,0:T(8,128)(2,1)S(1)}, u32[]{:S(2)}, u32[]{:S(2)}) collective-permute-start(bf16[2,2,80,256]{3,2,1,0:T(8,128)(2,1)S(1)} %pad_maximum_fusion.2), channel_id=1, source_target_pairs={{0,16},{16,0},{1,17},{17,1},{2,18},{18,2},{3,19},{19,3},{4,20},{20... | collective-permute-start | bytes 491528 | tf_op jit(solution)/shard_map/ppermute | solution.py:165
  38.0 0.5 collective-permute-start.10
  38.5 1.0 %collective-permute-start.7 = (bf16[2,2,80,256]{3,2,1,0:T(8,128)(2,1)S(1)}, bf16[2,2,80,256]{3,2,1,0:T(8,128)(2,1)S(1)}, u32[]{:S(2)}, u32[]{:S(2)}) collective-permute-start(bf16[2,2,80,256]{3,2,1,0:T(8,128)(2,1)S(1)} %pad_maximum_fusion), channel_id=1, source_target_pairs={{0,2},{1,3},{2,0},{3,1},{4,6},{5,7},{6,4},{7,5},{8,10},{9,11},{10,... | collective-permute-start | bytes 491528 | tf_op jit(solution)/shard_map/ppermute | solution.py:162
  39.6 2.2 %collective-permute-done.13 = bf16[2,2,80,256]{3,2,1,0:T(8,128)(2,1)S(1)} collective-permute-done((bf16[2,2,80,256]{3,2,1,0:T(8,128)(2,1)S(1)}, bf16[2,2,80,256]{3,2,1,0:T(8,128)(2,1)S(1)}, u32[]{:S(2)}, u32[]{:S(2)}) %collective-permute-start.13) | collective-permute-done | bytes 163872 | tf_op jit(solution)/shard_map/ppermute | solution.py:165
  41.8 0.9 %collective-permute-start.14 = (bf16[4,2,80,256]{3,2,1,0:T(8,128)(2,1)S(1)}, bf16[4,2,80,256]{3,2,1,0:T(8,128)(2,1)S(1)}, u32[]{:S(2)}, u32[]{:S(2)}) collective-permute-start(bf16[4,2,80,256]{3,2,1,0:T(8,128)(2,1)S(1)} %constant_dynamic-update-slice_fusion.6.refs_4_), channel_id=1, source_target_pairs={{0,2},{1,3},{2,0},{3,1},{4,6},{5,7},{6,4},{7,5},{8,10},{9,11},{10,... | collective-permute-start | bytes 983048 | tf_op jit(solution)/shard_map/ppermute | solution.py:162
  42.7 0.7 %collective-permute-done.10 = bf16[2,2,80,256]{3,2,1,0:T(8,128)(2,1)S(1)} collective-permute-done((bf16[2,2,80,256]{3,2,1,0:T(8,128)(2,1)S(1)}, bf16[2,2,80,256]{3,2,1,0:T(8,128)(2,1)S(1)}, u32[]{:S(2)}, u32[]{:S(2)}) %collective-permute-start.10) | collective-permute-done | bytes 163872 | tf_op jit(solution)/shard_map/ppermute | solution.py:162
  43.4 0.7 %collective-permute-start.11 = (bf16[4,2,80,256]{3,2,1,0:T(8,128)(2,1)S(1)}, bf16[4,2,80,256]{3,2,1,0:T(8,128)(2,1)S(1)}, u32[]{:S(2)}, u32[]{:S(2)}) collective-permute-start(bf16[4,2,80,256]{3,2,1,0:T(8,128)(2,1)S(1)} %constant_dynamic-update-slice_fusion.3.refs_0_), channel_id=1, source_target_pairs={{0,16},{16,0},{1,17},{17,1},{2,18},{18,2},{3,19},{19,3},{4,20},{20... | collective-permute-start | bytes 983048 | tf_op jit(solution)/shard_map/ppermute | solution.py:165
  44.1 1.5 %collective-permute-done.7 = bf16[2,2,80,256]{3,2,1,0:T(8,128)(2,1)S(1)} collective-permute-done((bf16[2,2,80,256]{3,2,1,0:T(8,128)(2,1)S(1)}, bf16[2,2,80,256]{3,2,1,0:T(8,128)(2,1)S(1)}, u32[]{:S(2)}, u32[]{:S(2)}) %collective-permute-start.7) | collective-permute-done | bytes 163872 | tf_op jit(solution)/shard_map/ppermute | solution.py:162
  45.7 0.1 collective-permute-start.8
  45.8 0.1 collective-permute-start.19
  45.9 0.5 merge.1
  46.3 0.0 copy-start.2
  46.4 11.9 %all_to_all.10.start = f32[32,4,128]{2,1,0:T(4,128)S(1)} all-to-all(f32[32,4,128]{2,1,0:T(4,128)S(1)} %bitcast.6), channel_id=1, replica_groups=mesh['row'=2,'col'=16] {'row','col'}, dimensions={0} | all-to-all | bytes 131072 | tf_op jit(solution)/shard_map/all_to_all | solution.py:267
  58.3 0.2 collective-permute-start.20
  58.5 0.4 collective-permute-start.23
  58.9 0.1 collective-permute-start.21
  59.0 0.4 collective-permute-start.22
  59.4 0.1 collective-permute-start.24
  59.5 0.5 collective-permute-done.20.refs_3_
  60.0 1.9 %chain0.1.start = f32[8,2048]{1,0:T(8,128)S(1)} custom-call(s32[6]{0:T(128)S(1)} %copy-done.2, f32[32,4,128]{2,1,0:T(4,128)S(1)} %all_to_all.10.start, bf16[4,2,80,256]{3,2,1,0:T(8,128)(2,1)S(1)} %constant_dynamic-update-slice_fusion.refs_0_, bf16[4,2,80,256]{3,2,1,0:T(8,128)(2,1)S(1)} %collective-permute-done.8.refs_1_, ...), custom_call_target="tpu_custom_call" | custom-call | flops 67108864 | bytes 1310720 | tf_op jit(solution)/shard_map/chain0/pallas_call | solution.py:285
  61.9 3.8 %chain1.1 = bf16[4,2048]{1,0:T(4,128)(2,1)} custom-call(s32[6]{0:T(128)S(1)} %copy-done.2, f32[8,2048]{1,0:T(8,128)S(1)} %chain0.1.start, bf16[4,2,80,256]{3,2,1,0:T(8,128)(2,1)S(1)} %constant_dynamic-update-slice_fusion.3.refs_0_, bf16[4,2,80,256]{3,2,1,0:T(8,128)(2,1)S(1)} %collective-permute-done.11.refs_1_, ...), custom_call_target="tpu_custom_call" | custom-call | flops 134217728 | bytes 2621440 | tf_op jit(solution)/shard_map/chain1/pallas_call | solution.py:285
  (39 shorter events, 0.3 us)
Async XLA Ops:
  0.0 9.7 %collective-permute-start = (bf16[64,512]{1,0:T(8,128)(2,1)}, bf16[64,512]{1,0:T(8,128)(2,1)S(1)}, u32[]{:S(2)}, u32[]{:S(2)}) collective-permute-start(bf16[64,512]{1,0:T(8,128)(2,1)} %param.7), channel_id=1, source_target_pairs={{0,8},{1,9},{2,10},{3,11},{4,12},{5,13},{6,14},{7,15},{8,0},{9,1},... | collective-permute-start | bytes 196616 | tf_op jit(solution)/shard_map/ppermute | solution.py:162
  5.7 4.0 %copy-start.3 = (bf16[64,512]{1,0:T(8,128)(2,1)S(1)}, bf16[64,512]{1,0:T(8,128)(2,1)}, u32[]{:S(2)}) copy-start(bf16[64,512]{1,0:T(8,128)(2,1)} %param.7) | copy-start | bytes 196612
  5.7 12.8 %all-to-all-start = ((bf16[8,80,256]{2,1,0:T(8,128)(2,1)}), bf16[8,80,256]{2,1,0:T(8,128)(2,1)S(1)}, u32[]{:S(2)}, u32[]{:S(2)}) async-start(bf16[8,80,256]{2,1,0:T(8,128)(2,1)} %pack.1), calls=%async_computation | async-start | bytes 655360 | tf_op jit(solution)/shard_map/all_to_all | solution.py:186
  9.7 4.6 %collective-permute-start.2 = (bf16[64,512]{1,0:T(8,128)(2,1)S(1)}, bf16[64,512]{1,0:T(8,128)(2,1)S(1)}, u32[]{:S(2)}, u32[]{:S(2)}) collective-permute-start(bf16[64,512]{1,0:T(8,128)(2,1)S(1)} %get-tuple-element.31), channel_id=1, source_target_pairs={{0,16},{16,0},{1,17},{17,1},{2,18},{18,2},{3,19},{19,3},{4,20},{20... | collective-permute-start | bytes 196616 | tf_op jit(solution)/shard_map/ppermute | solution.py:165
  11.3 6.5 %collective-permute-start.1 = (bf16[1,64,512]{2,1,0:T(8,128)(2,1)S(1)}, bf16[1,64,512]{2,1,0:T(8,128)(2,1)S(1)}, u32[]{:S(2)}, u32[]{:S(2)}) collective-permute-start(bf16[1,64,512]{2,1,0:T(8,128)(2,1)S(1)} %get-tuple-element.32), channel_id=1, source_target_pairs={{0,2},{1,3},{2,0},{3,1},{4,6},{5,7},{6,4},{7,5},{8,10},{9,11},{10,... | collective-permute-start | bytes 196616 | tf_op jit(solution)/shard_map/ppermute | solution.py:162
  14.3 4.3 %collective-permute-start.3 = (bf16[1,64,512]{2,1,0:T(8,128)(2,1)S(1)}, bf16[1,64,512]{2,1,0:T(8,128)(2,1)S(1)}, u32[]{:S(2)}, u32[]{:S(2)}) collective-permute-start(bf16[1,64,512]{2,1,0:T(8,128)(2,1)S(1)} %bitcast.9), channel_id=1, source_target_pairs={{0,4},{1,5},{2,6},{3,7},{4,0},{5,1},{6,2},{7,3},{8,12},{9,13},{10,... | collective-permute-start | bytes 196616 | tf_op jit(solution)/shard_map/ppermute | solution.py:162
  17.9 0.7 %copy-start.1 = (s32[6]{0:T(128)S(1)}, s32[6]{0:T(128)}, u32[]{:S(2)}) copy-start(s32[6]{0:T(128)} %owners.3) | copy-start | bytes 76
  19.3 8.7 %collective-permute-start.4 = (bf16[1,80,256]{2,1,0:T(8,128)(2,1)S(1)}, bf16[1,80,256]{2,1,0:T(8,128)(2,1)S(1)}, u32[]{:S(2)}, u32[]{:S(2)}) collective-permute-start(bf16[1,80,256]{2,1,0:T(8,128)(2,1)S(1)} %slice.8), channel_id=1, source_target_pairs={{0,8},{1,9},{2,10},{3,11},{4,12},{5,13},{6,14},{7,15},{8,0},{9,1},... | collective-permute-start | bytes 122888 | tf_op jit(solution)/shard_map/ppermute | solution.py:162
  19.8 11.5 %collective-permute-start.5 = (bf16[4,80,256]{2,1,0:T(8,128)(2,1)S(1)}, bf16[4,80,256]{2,1,0:T(8,128)(2,1)S(1)}, u32[]{:S(2)}, u32[]{:S(2)}) collective-permute-start(bf16[4,80,256]{2,1,0:T(8,128)(2,1)S(1)} %slice.9), channel_id=1, source_target_pairs={{0,8},{1,9},{2,10},{3,11},{4,12},{5,13},{6,14},{7,15},{8,0},{9,1},... | collective-permute-start | bytes 491528 | tf_op jit(solution)/shard_map/ppermute | solution.py:162
  28.0 5.0 %collective-permute-start.15 = (bf16[2,64,512]{2,1,0:T(8,128)(2,1)S(1)}, bf16[2,64,512]{2,1,0:T(8,128)(2,1)S(1)}, u32[]{:S(2)}, u32[]{:S(2)}) collective-permute-start(bf16[2,64,512]{2,1,0:T(8,128)(2,1)S(1)} %pad_maximum_fusion.3), channel_id=1, source_target_pairs={{0,4},{1,5},{2,6},{3,7},{4,0},{5,1},{6,2},{7,3},{8,12},{9,13},{10,... | collective-permute-start | bytes 393224 | tf_op jit(solution)/shard_map/ppermute | solution.py:162
  28.0 6.5 %collective-permute-start.16 = (bf16[2,64,512]{2,1,0:T(8,128)(2,1)S(1)}, bf16[2,64,512]{2,1,0:T(8,128)(2,1)S(1)}, u32[]{:S(2)}, u32[]{:S(2)}) collective-permute-start(bf16[2,64,512]{2,1,0:T(8,128)(2,1)S(1)} %pad_maximum_fusion.4), channel_id=1, source_target_pairs={{0,2},{1,3},{2,0},{3,1},{4,6},{5,7},{6,4},{7,5},{8,10},{9,11},{10,... | collective-permute-start | bytes 393224 | tf_op jit(solution)/shard_map/ppermute | solution.py:162
  28.1 17.6 %collective-permute-start.17 = (bf16[4,64,512]{2,1,0:T(8,128)(2,1)S(1)}, bf16[4,64,512]{2,1,0:T(8,128)(2,1)S(1)}, u32[]{:S(2)}, u32[]{:S(2)}) collective-permute-start(bf16[4,64,512]{2,1,0:T(8,128)(2,1)S(1)} %constant_dynamic-update-slice_fusion.9.refs_0_), channel_id=1, source_target_pairs={{0,1},{1,0},{2,3},{3,2},{4,5},{5,4},{6,7},{7,6},{8,9},{9,8},{10,11... | collective-permute-start | bytes 786440 | tf_op jit(solution)/shard_map/ppermute | solution.py:162
  31.9 4.5 %collective-permute-start.12 = (bf16[1,2,80,256]{3,2,1,0:T(8,128)(2,1)S(1)}, bf16[1,2,80,256]{3,2,1,0:T(8,128)(2,1)S(1)}, u32[]{:S(2)}, u32[]{:S(2)}) collective-permute-start(bf16[1,2,80,256]{3,2,1,0:T(8,128)(2,1)S(1)} %get-tuple-element.24), channel_id=1, source_target_pairs={{0,4},{1,5},{2,6},{3,7},{4,0},{5,1},{6,2},{7,3},{8,12},{9,13},{10,... | collective-permute-start | bytes 245768 | tf_op jit(solution)/shard_map/ppermute | solution.py:162
  32.0 6.0 %collective-permute-start.9 = (bf16[1,2,80,256]{3,2,1,0:T(8,128)(2,1)S(1)}, bf16[1,2,80,256]{3,2,1,0:T(8,128)(2,1)S(1)}, u32[]{:S(2)}, u32[]{:S(2)}) collective-permute-start(bf16[1,2,80,256]{3,2,1,0:T(8,128)(2,1)S(1)} %get-tuple-element.23), channel_id=1, source_target_pairs={{0,2},{1,3},{2,0},{3,1},{4,6},{5,7},{6,4},{7,5},{8,10},{9,11},{10,... | collective-permute-start | bytes 245768 | tf_op jit(solution)/shard_map/ppermute | solution.py:162
  33.0 5.5 %collective-permute-start.6 = (bf16[1,2,80,256]{3,2,1,0:T(8,128)(2,1)S(1)}, bf16[1,2,80,256]{3,2,1,0:T(8,128)(2,1)S(1)}, u32[]{:S(2)}, u32[]{:S(2)}) collective-permute-start(bf16[1,2,80,256]{3,2,1,0:T(8,128)(2,1)S(1)} %get-tuple-element.22), channel_id=1, source_target_pairs={{0,16},{16,0},{1,17},{17,1},{2,18},{18,2},{3,19},{19,3},{4,20},{20... | collective-permute-start | bytes 245768 | tf_op jit(solution)/shard_map/ppermute | solution.py:165
  34.6 11.3 %collective-permute-start.18 = (bf16[4,64,512]{2,1,0:T(8,128)(2,1)S(1)}, bf16[4,64,512]{2,1,0:T(8,128)(2,1)S(1)}, u32[]{:S(2)}, u32[]{:S(2)}) collective-permute-start(bf16[4,64,512]{2,1,0:T(8,128)(2,1)S(1)} %constant_dynamic-update-slice_fusion.11.refs_1_), channel_id=1, source_target_pairs={{0,1},{1,0},{2,3},{3,2},{4,5},{5,4},{6,7},{7,6},{8,9},{9,8},{10,11... | collective-permute-start | bytes 786440 | tf_op jit(solution)/shard_map/ppermute | solution.py:162
  36.4 9.5 %copy-start = (bf16[4096,128]{1,0:T(8,128)(2,1)S(1)}, bf16[4096,128]{1,0:T(8,128)(2,1)}, u32[]{:S(2)}) copy-start(bf16[4096,128]{1,0:T(8,128)(2,1)} %sub.6) | copy-start | bytes 3145732
  36.4 5.4 %collective-permute-start.13 = (bf16[2,2,80,256]{3,2,1,0:T(8,128)(2,1)S(1)}, bf16[2,2,80,256]{3,2,1,0:T(8,128)(2,1)S(1)}, u32[]{:S(2)}, u32[]{:S(2)}) collective-permute-start(bf16[2,2,80,256]{3,2,1,0:T(8,128)(2,1)S(1)} %pad_maximum_fusion.2), channel_id=1, source_target_pairs={{0,16},{16,0},{1,17},{17,1},{2,18},{18,2},{3,19},{19,3},{4,20},{20... | collective-permute-start | bytes 491528 | tf_op jit(solution)/shard_map/ppermute | solution.py:165
  38.0 5.4 %collective-permute-start.10 = (bf16[2,2,80,256]{3,2,1,0:T(8,128)(2,1)S(1)}, bf16[2,2,80,256]{3,2,1,0:T(8,128)(2,1)S(1)}, u32[]{:S(2)}, u32[]{:S(2)}) collective-permute-start(bf16[2,2,80,256]{3,2,1,0:T(8,128)(2,1)S(1)} %pad_maximum_fusion.1), channel_id=1, source_target_pairs={{0,4},{1,5},{2,6},{3,7},{4,0},{5,1},{6,2},{7,3},{8,12},{9,13},{10,... | collective-permute-start | bytes 491528 | tf_op jit(solution)/shard_map/ppermute | solution.py:162
  38.5 7.1 %collective-permute-start.7 = (bf16[2,2,80,256]{3,2,1,0:T(8,128)(2,1)S(1)}, bf16[2,2,80,256]{3,2,1,0:T(8,128)(2,1)S(1)}, u32[]{:S(2)}, u32[]{:S(2)}) collective-permute-start(bf16[2,2,80,256]{3,2,1,0:T(8,128)(2,1)S(1)} %pad_maximum_fusion), channel_id=1, source_target_pairs={{0,2},{1,3},{2,0},{3,1},{4,6},{5,7},{6,4},{7,5},{8,10},{9,11},{10,... | collective-permute-start | bytes 491528 | tf_op jit(solution)/shard_map/ppermute | solution.py:162
  41.8 16.5 %collective-permute-start.14 = (bf16[4,2,80,256]{3,2,1,0:T(8,128)(2,1)S(1)}, bf16[4,2,80,256]{3,2,1,0:T(8,128)(2,1)S(1)}, u32[]{:S(2)}, u32[]{:S(2)}) collective-permute-start(bf16[4,2,80,256]{3,2,1,0:T(8,128)(2,1)S(1)} %constant_dynamic-update-slice_fusion.6.refs_4_), channel_id=1, source_target_pairs={{0,2},{1,3},{2,0},{3,1},{4,6},{5,7},{6,4},{7,5},{8,10},{9,11},{10,... | collective-permute-start | bytes 983048 | tf_op jit(solution)/shard_map/ppermute | solution.py:162
  43.4 14.9 %collective-permute-start.11 = (bf16[4,2,80,256]{3,2,1,0:T(8,128)(2,1)S(1)}, bf16[4,2,80,256]{3,2,1,0:T(8,128)(2,1)S(1)}, u32[]{:S(2)}, u32[]{:S(2)}) collective-permute-start(bf16[4,2,80,256]{3,2,1,0:T(8,128)(2,1)S(1)} %constant_dynamic-update-slice_fusion.3.refs_0_), channel_id=1, source_target_pairs={{0,16},{16,0},{1,17},{17,1},{2,18},{18,2},{3,19},{19,3},{4,20},{20... | collective-permute-start | bytes 983048 | tf_op jit(solution)/shard_map/ppermute | solution.py:165
  45.7 12.6 %collective-permute-start.8 = (bf16[4,2,80,256]{3,2,1,0:T(8,128)(2,1)S(1)}, bf16[4,2,80,256]{3,2,1,0:T(8,128)(2,1)S(1)}, u32[]{:S(2)}, u32[]{:S(2)}) collective-permute-start(bf16[4,2,80,256]{3,2,1,0:T(8,128)(2,1)S(1)} %constant_dynamic-update-slice_fusion.refs_0_), channel_id=1, source_target_pairs={{0,4},{1,5},{2,6},{3,7},{4,0},{5,1},{6,2},{7,3},{8,12},{9,13},{10,... | collective-permute-start | bytes 983048 | tf_op jit(solution)/shard_map/ppermute | solution.py:162
  45.8 13.6 %collective-permute-start.19 = (bf16[4,2,80,256]{3,2,1,0:T(8,128)(2,1)S(1)}, bf16[4,2,80,256]{3,2,1,0:T(8,128)(2,1)S(1)}, u32[]{:S(2)}, u32[]{:S(2)}) collective-permute-start(bf16[4,2,80,256]{3,2,1,0:T(8,128)(2,1)S(1)} %constant_dynamic-update-slice_fusion.refs_0_), channel_id=1, source_target_pairs={{0,1},{1,0},{2,3},{3,2},{4,5},{5,4},{6,7},{7,6},{8,9},{9,8},{10,11... | collective-permute-start | bytes 983048 | tf_op jit(solution)/shard_map/ppermute | solution.py:162
  46.3 13.6 %copy-start.2 = (s32[6]{0:T(128)S(1)}, s32[6]{0:T(128)}, u32[]{:S(2)}) copy-start(s32[6]{0:T(128)} %offsets.3) | copy-start | bytes 76
  58.3 1.7 %collective-permute-start.20 = (bf16[4,2,80,256]{3,2,1,0:T(8,128)(2,1)S(1)}, bf16[4,2,80,256]{3,2,1,0:T(8,128)(2,1)S(1)}, u32[]{:S(2)}, u32[]{:S(2)}) collective-permute-start(bf16[4,2,80,256]{3,2,1,0:T(8,128)(2,1)S(1)} %collective-permute-done.8.refs_1_), channel_id=1, source_target_pairs={{0,1},{1,0},{2,3},{3,2},{4,5},{5,4},{6,7},{7,6},{8,9},{9,8},{10,11... | collective-permute-start | bytes 983048 | tf_op jit(solution)/shard_map/ppermute | solution.py:162
  58.5 3.4 %collective-permute-start.23 = (bf16[4,2,80,256]{3,2,1,0:T(8,128)(2,1)S(1)}, bf16[4,2,80,256]{3,2,1,0:T(8,128)(2,1)S(1)}, u32[]{:S(2)}, u32[]{:S(2)}) collective-permute-start(bf16[4,2,80,256]{3,2,1,0:T(8,128)(2,1)S(1)} %constant_dynamic-update-slice_fusion.6.refs_4_), channel_id=1, source_target_pairs={{0,1},{1,0},{2,3},{3,2},{4,5},{5,4},{6,7},{7,6},{8,9},{9,8},{10,11... | collective-permute-start | bytes 983048 | tf_op jit(solution)/shard_map/ppermute | solution.py:162
  58.9 3.0 %collective-permute-start.21 = (bf16[4,2,80,256]{3,2,1,0:T(8,128)(2,1)S(1)}, bf16[4,2,80,256]{3,2,1,0:T(8,128)(2,1)S(1)}, u32[]{:S(2)}, u32[]{:S(2)}) collective-permute-start(bf16[4,2,80,256]{3,2,1,0:T(8,128)(2,1)S(1)} %constant_dynamic-update-slice_fusion.3.refs_0_), channel_id=1, source_target_pairs={{0,1},{1,0},{2,3},{3,2},{4,5},{5,4},{6,7},{7,6},{8,9},{9,8},{10,11... | collective-permute-start | bytes 983048 | tf_op jit(solution)/shard_map/ppermute | solution.py:162
  59.0 2.9 %collective-permute-start.22 = (bf16[4,2,80,256]{3,2,1,0:T(8,128)(2,1)S(1)}, bf16[4,2,80,256]{3,2,1,0:T(8,128)(2,1)S(1)}, u32[]{:S(2)}, u32[]{:S(2)}) collective-permute-start(bf16[4,2,80,256]{3,2,1,0:T(8,128)(2,1)S(1)} %collective-permute-done.11.refs_1_), channel_id=1, source_target_pairs={{0,1},{1,0},{2,3},{3,2},{4,5},{5,4},{6,7},{7,6},{8,9},{9,8},{10,11... | collective-permute-start | bytes 983048 | tf_op jit(solution)/shard_map/ppermute | solution.py:162
  59.4 2.5 %collective-permute-start.24 = (bf16[4,2,80,256]{3,2,1,0:T(8,128)(2,1)S(1)}, bf16[4,2,80,256]{3,2,1,0:T(8,128)(2,1)S(1)}, u32[]{:S(2)}, u32[]{:S(2)}) collective-permute-start(bf16[4,2,80,256]{3,2,1,0:T(8,128)(2,1)S(1)} %collective-permute-done.14.refs_5_), channel_id=1, source_target_pairs={{0,1},{1,0},{2,3},{3,2},{4,5},{5,4},{6,7},{7,6},{8,9},{9,8},{10,11... | collective-permute-start | bytes 983048 | tf_op jit(solution)/shard_map/ppermute | solution.py:162

commit v28 on v27

--- a/solution.py
+++ b/solution.py
@@ -271,7 +271,7 @@
         last_round.append(send(colours[k]))
         masks[k] = [masks[k], [m ^ mask for m in masks[k]]]
         masks[k] += [[m ^ 1 for m in ms] for ms in masks[k]]
-    last_round, state = lax.optimization_barrier((last_round, state))
+    last_round[0], state = lax.optimization_barrier((last_round[0], state))
     held = []
     for k in range(COLOURS):
         held.append([colours[k], last_round[k], over_col(colours[k], 1), over_col(last_round[k], 1)])

time: 66 us -> 66 us (level)
    ppermute x21, starting transfers between devices: 16 us -> 17.2 us  [over_col(): return lax.ppermute(x, 'col', [(c, c ^ mask) for c in range(cols)])]
    ppermute x4, starting transfers between devices: 5.41 us -> 4.73 us  [over_row(): return lax.ppermute(x, 'row', [(r, r ^ mask) for r in range(rows)])]
  transfers between devices with their start and end apart: 26 -> 26, of which waited for: 10 -> 12; matrix products, arithmetic and copies ran while one was open for 0% -> 0% of each run, Pallas kernels for 7% -> 7%
where the time goes in v28:
time: 66 us; the launch traced here: 65.7 us
  starting transfers between devices  25.8 us (39%)
  waiting for transfers between devices  18.6 us (28%)
  blocking collectives  11.6 us (18%)
  Pallas kernels  9.18 us (14%)
    ppermute x21, starting transfers between devices, over_col(): return lax.ppermute(x, 'col', [(c, c ^ mask) for c in range(cols)])  17.2 us
    ppermute x21, waiting for transfers between devices, over_col(): return lax.ppermute(x, 'col', [(c, c ^ mask) for c in range(cols)])  15.2 us
    all_to_all x1, blocking collectives, local(): lax.all_to_all(merged.reshape(rows * cols, each, width), ('row', 'col'),...  11.6 us
    pallas_call x2, Pallas kernels, local(): pl.pallas_call(functools.partial(chain_kernel, cols, groups, slots, sum((...  5.68 us
    ppermute x4, starting transfers between devices, over_row(): return lax.ppermute(x, 'row', [(r, r ^ mask) for r in range(rows)])  4.73 us
    all_to_all x1, starting transfers between devices, local(): slices = lax.all_to_all(packed, 'col', 0, 0, axis_index_groups=members)  3.95 us
    ppermute x4, waiting for transfers between devices, over_row(): return lax.ppermute(x, 'row', [(r, r ^ mask) for r in range(rows)])  3.32 us
    pallas_call x1, Pallas kernels, local(): pl.pallas_call(pack_kernel, out_shape=jax.ShapeDtypeStruct((HALF,) + piec...  1.69 us
  transfers between devices with their start and end apart: 26, of which 12 were waited for; matrix products, arithmetic and copies ran while one was open for 0% of the time, Pallas kernels for 7%

profile of v28, /device:TPU:0, one launch (start us, length us, event | category | flops | bytes accessed | tf_op | source)
XLA Modules:
  0.0 65.7 jit_solution(9810111072259216322)
XLA Ops:
  0.0 4.0 %collective-permute-start = (bf16[64,512]{1,0:T(8,128)(2,1)}, bf16[64,512]{1,0:T(8,128)(2,1)S(1)}, u32[]{:S(2)}, u32[]{:S(2)}) collective-permute-start(bf16[64,512]{1,0:T(8,128)(2,1)} %param.7), channel_id=1, source_target_pairs={{0,8},{1,9},{2,10},{3,11},{4,12},{5,13},{6,14},{7,15},{8,0},{9,1},... | collective-permute-start | bytes 196616 | tf_op jit(solution)/shard_map/ppermute | solution.py:162
  4.0 1.7 %pack.1 = bf16[8,80,256]{2,1,0:T(8,128)(2,1)} custom-call(bf16[16,64,256]{2,1,0:T(8,128)(2,1)} %bitcast.7, bf16[16,16,256]{2,1,0:T(8,128)(2,1)} %bitcast.8), custom_call_target="tpu_custom_call" | custom-call | bytes 655360 | tf_op jit(solution)/shard_map/pack/pallas_call | solution.py:175
  5.7 0.0 copy-start.3
  5.7 4.0 %all-to-all-start = ((bf16[8,80,256]{2,1,0:T(8,128)(2,1)}), bf16[8,80,256]{2,1,0:T(8,128)(2,1)S(1)}, u32[]{:S(2)}, u32[]{:S(2)}) async-start(bf16[8,80,256]{2,1,0:T(8,128)(2,1)} %pack.1), calls=%async_computation | async-start | bytes 655360 | tf_op jit(solution)/shard_map/all_to_all | solution.py:186
  9.7 1.6 %collective-permute-start.2 = (bf16[64,512]{1,0:T(8,128)(2,1)S(1)}, bf16[64,512]{1,0:T(8,128)(2,1)S(1)}, u32[]{:S(2)}, u32[]{:S(2)}) collective-permute-start(bf16[64,512]{1,0:T(8,128)(2,1)S(1)} %get-tuple-element.27), channel_id=1, source_target_pairs={{0,16},{16,0},{1,17},{17,1},{2,18},{18,2},{3,19},{19,3},{4,20},{20... | collective-permute-start | bytes 196616 | tf_op jit(solution)/shard_map/ppermute | solution.py:165
  11.3 2.0 %collective-permute-start.1 = (bf16[1,64,512]{2,1,0:T(8,128)(2,1)S(1)}, bf16[1,64,512]{2,1,0:T(8,128)(2,1)S(1)}, u32[]{:S(2)}, u32[]{:S(2)}) collective-permute-start(bf16[1,64,512]{2,1,0:T(8,128)(2,1)S(1)} %get-tuple-element.28), channel_id=1, source_target_pairs={{0,2},{1,3},{2,0},{3,1},{4,6},{5,7},{6,4},{7,5},{8,10},{9,11},{10,... | collective-permute-start | bytes 196616 | tf_op jit(solution)/shard_map/ppermute | solution.py:162
  13.3 1.0 %collective-permute-done.2 = bf16[64,512]{1,0:T(8,128)(2,1)S(1)} collective-permute-done((bf16[64,512]{1,0:T(8,128)(2,1)S(1)}, bf16[64,512]{1,0:T(8,128)(2,1)S(1)}, u32[]{:S(2)}, u32[]{:S(2)}) %collective-permute-start.2) | collective-permute-done | bytes 65568 | tf_op jit(solution)/shard_map/ppermute | solution.py:165
  14.3 1.8 %collective-permute-start.3 = (bf16[1,64,512]{2,1,0:T(8,128)(2,1)S(1)}, bf16[1,64,512]{2,1,0:T(8,128)(2,1)S(1)}, u32[]{:S(2)}, u32[]{:S(2)}) collective-permute-start(bf16[1,64,512]{2,1,0:T(8,128)(2,1)S(1)} %bitcast.9), channel_id=1, source_target_pairs={{0,4},{1,5},{2,6},{3,7},{4,0},{5,1},{6,2},{7,3},{8,12},{9,13},{10,... | collective-permute-start | bytes 196616 | tf_op jit(solution)/shard_map/ppermute | solution.py:162
  16.1 1.8 %collective-permute-done.1 = bf16[1,64,512]{2,1,0:T(8,128)(2,1)S(1)} collective-permute-done((bf16[1,64,512]{2,1,0:T(8,128)(2,1)S(1)}, bf16[1,64,512]{2,1,0:T(8,128)(2,1)S(1)}, u32[]{:S(2)}, u32[]{:S(2)}) %collective-permute-start.1) | collective-permute-done | bytes 65568 | tf_op jit(solution)/shard_map/ppermute | solution.py:162
  17.9 0.0 copy-start.1
  17.9 0.7 %collective-permute-done.3 = bf16[1,64,512]{2,1,0:T(8,128)(2,1)S(1)} collective-permute-done((bf16[1,64,512]{2,1,0:T(8,128)(2,1)S(1)}, bf16[1,64,512]{2,1,0:T(8,128)(2,1)S(1)}, u32[]{:S(2)}, u32[]{:S(2)}) %collective-permute-start.3) | collective-permute-done | bytes 65568 | tf_op jit(solution)/shard_map/ppermute | solution.py:162
  18.6 0.7 %pick.1 = bf16[5,80,256]{2,1,0:T(8,128)(2,1)S(1)} custom-call(s32[6]{0:T(128)S(1)} %copy-done.1, bf16[8,80,256]{2,1,0:T(8,128)(2,1)S(1)} %all-to-all-done.held), custom_call_target="tpu_custom_call" | custom-call | bytes 327680 | tf_op jit(solution)/shard_map/pick/pallas_call | solution.py:215
  19.3 0.4 collective-permute-start.4
  19.8 2.6 %collective-permute-start.5 = (bf16[4,80,256]{2,1,0:T(8,128)(2,1)S(1)}, bf16[4,80,256]{2,1,0:T(8,128)(2,1)S(1)}, u32[]{:S(2)}, u32[]{:S(2)}) collective-permute-start(bf16[4,80,256]{2,1,0:T(8,128)(2,1)S(1)} %slice.9), channel_id=1, source_target_pairs={{0,8},{1,9},{2,10},{3,11},{4,12},{5,13},{6,14},{7,15},{8,0},{9,1},... | collective-permute-start | bytes 491528 | tf_op jit(solution)/shard_map/ppermute | solution.py:162
  22.4 5.6 %collective-permute-done.4.refs_0_ = bf16[1,80,256]{2,1,0:T(8,128)(2,1)S(1)} collective-permute-done((bf16[1,80,256]{2,1,0:T(8,128)(2,1)S(1)}, bf16[1,80,256]{2,1,0:T(8,128)(2,1)S(1)}, u32[]{:S(2)}, u32[]{:S(2)}) %collective-permute-start.4) | collective-permute-done | bytes 40992 | tf_op jit(solution)/shard_map/ppermute | solution.py:162
  28.0 0.1 collective-permute-start.9
  28.1 0.1 collective-permute-start.10
  28.2 0.1 collective-permute-start.11
  28.3 2.9 %collective-permute-done.5.refs_1_ = bf16[4,80,256]{2,1,0:T(8,128)(2,1)S(1)} collective-permute-done((bf16[4,80,256]{2,1,0:T(8,128)(2,1)S(1)}, bf16[4,80,256]{2,1,0:T(8,128)(2,1)S(1)}, u32[]{:S(2)}, u32[]{:S(2)}) %collective-permute-start.5) | collective-permute-done | bytes 163872 | tf_op jit(solution)/shard_map/ppermute | solution.py:162
  31.2 0.6 order.1
  31.9 1.6 %collective-permute-start.6 = (bf16[1,2,80,256]{3,2,1,0:T(8,128)(2,1)S(1)}, bf16[1,2,80,256]{3,2,1,0:T(8,128)(2,1)S(1)}, u32[]{:S(2)}, u32[]{:S(2)}) collective-permute-start(bf16[1,2,80,256]{3,2,1,0:T(8,128)(2,1)S(1)} %get-tuple-element.20), channel_id=1, source_target_pairs={{0,16},{16,0},{1,17},{17,1},{2,18},{18,2},{3,19},{19,3},{4,20},{20... | collective-permute-start | bytes 245768 | tf_op jit(solution)/shard_map/ppermute | solution.py:165
  33.4 0.7 %collective-permute-start.15 = (bf16[1,2,80,256]{3,2,1,0:T(8,128)(2,1)S(1)}, bf16[1,2,80,256]{3,2,1,0:T(8,128)(2,1)S(1)}, u32[]{:S(2)}, u32[]{:S(2)}) collective-permute-start(bf16[1,2,80,256]{3,2,1,0:T(8,128)(2,1)S(1)} %get-tuple-element.25), channel_id=1, source_target_pairs={{0,2},{1,3},{2,0},{3,1},{4,6},{5,7},{6,4},{7,5},{8,10},{9,11},{10,... | collective-permute-start | bytes 245768 | tf_op jit(solution)/shard_map/ppermute | solution.py:162
  34.2 0.4 collective-permute-start.20
  34.6 0.1 collective-permute-start.12
  34.7 1.6 %collective-permute-done.6 = bf16[1,2,80,256]{3,2,1,0:T(8,128)(2,1)S(1)} collective-permute-done((bf16[1,2,80,256]{3,2,1,0:T(8,128)(2,1)S(1)}, bf16[1,2,80,256]{3,2,1,0:T(8,128)(2,1)S(1)}, u32[]{:S(2)}, u32[]{:S(2)}) %collective-permute-start.6) | collective-permute-done | bytes 81952 | tf_op jit(solution)/shard_map/ppermute | solution.py:165
  36.4 0.0 copy-start
  36.4 0.9 %collective-permute-start.7 = (bf16[2,2,80,256]{3,2,1,0:T(8,128)(2,1)S(1)}, bf16[2,2,80,256]{3,2,1,0:T(8,128)(2,1)S(1)}, u32[]{:S(2)}, u32[]{:S(2)}) collective-permute-start(bf16[2,2,80,256]{3,2,1,0:T(8,128)(2,1)S(1)} %pad_maximum_fusion), channel_id=1, source_target_pairs={{0,2},{1,3},{2,0},{3,1},{4,6},{5,7},{6,4},{7,5},{8,10},{9,11},{10,... | collective-permute-start | bytes 491528 | tf_op jit(solution)/shard_map/ppermute | solution.py:162
  37.3 0.7 %collective-permute-done.15 = bf16[1,2,80,256]{3,2,1,0:T(8,128)(2,1)S(1)} collective-permute-done((bf16[1,2,80,256]{3,2,1,0:T(8,128)(2,1)S(1)}, bf16[1,2,80,256]{3,2,1,0:T(8,128)(2,1)S(1)}, u32[]{:S(2)}, u32[]{:S(2)}) %collective-permute-start.15) | collective-permute-done | bytes 81952 | tf_op jit(solution)/shard_map/ppermute | solution.py:162
  38.0 0.1 collective-permute-start.16
  38.1 0.6 collective-permute-done.20
  38.7 0.8 %collective-permute-start.21 = (bf16[2,2,80,256]{3,2,1,0:T(8,128)(2,1)S(1)}, bf16[2,2,80,256]{3,2,1,0:T(8,128)(2,1)S(1)}, u32[]{:S(2)}, u32[]{:S(2)}) collective-permute-start(bf16[2,2,80,256]{3,2,1,0:T(8,128)(2,1)S(1)} %pad_maximum_fusion.2), channel_id=1, source_target_pairs={{0,16},{16,0},{1,17},{17,1},{2,18},{18,2},{3,19},{19,3},{4,20},{20... | collective-permute-start | bytes 491528 | tf_op jit(solution)/shard_map/ppermute | solution.py:165
  39.6 2.2 %collective-permute-done.7 = bf16[2,2,80,256]{3,2,1,0:T(8,128)(2,1)S(1)} collective-permute-done((bf16[2,2,80,256]{3,2,1,0:T(8,128)(2,1)S(1)}, bf16[2,2,80,256]{3,2,1,0:T(8,128)(2,1)S(1)}, u32[]{:S(2)}, u32[]{:S(2)}) %collective-permute-start.7) | collective-permute-done | bytes 163872 | tf_op jit(solution)/shard_map/ppermute | solution.py:162
  41.8 1.4 %collective-permute-start.8 = (bf16[4,2,80,256]{3,2,1,0:T(8,128)(2,1)S(1)}, bf16[4,2,80,256]{3,2,1,0:T(8,128)(2,1)S(1)}, u32[]{:S(2)}, u32[]{:S(2)}) collective-permute-start(bf16[4,2,80,256]{3,2,1,0:T(8,128)(2,1)S(1)} %constant_dynamic-update-slice_fusion.refs_0_), channel_id=1, source_target_pairs={{0,4},{1,5},{2,6},{3,7},{4,0},{5,1},{6,2},{7,3},{8,12},{9,13},{10,... | collective-permute-start | bytes 983048 | tf_op jit(solution)/shard_map/ppermute | solution.py:162
  43.2 0.2 collective-permute-done.16
  43.4 0.7 %collective-permute-done.21 = bf16[2,2,80,256]{3,2,1,0:T(8,128)(2,1)S(1)} collective-permute-done((bf16[2,2,80,256]{3,2,1,0:T(8,128)(2,1)S(1)}, bf16[2,2,80,256]{3,2,1,0:T(8,128)(2,1)S(1)}, u32[]{:S(2)}, u32[]{:S(2)}) %collective-permute-start.21) | collective-permute-done | bytes 163872 | tf_op jit(solution)/shard_map/ppermute | solution.py:165
  44.1 0.8 %collective-permute-start.17 = (bf16[4,2,80,256]{3,2,1,0:T(8,128)(2,1)S(1)}, bf16[4,2,80,256]{3,2,1,0:T(8,128)(2,1)S(1)}, u32[]{:S(2)}, u32[]{:S(2)}) collective-permute-start(bf16[4,2,80,256]{3,2,1,0:T(8,128)(2,1)S(1)} %constant_dynamic-update-slice_fusion.7.refs_0_), channel_id=1, source_target_pairs={{0,16},{16,0},{1,17},{17,1},{2,18},{18,2},{3,19},{19,3},{4,20},{20... | collective-permute-start | bytes 983048 | tf_op jit(solution)/shard_map/ppermute | solution.py:165
  44.9 1.4 %collective-permute-start.22 = (bf16[4,2,80,256]{3,2,1,0:T(8,128)(2,1)S(1)}, bf16[4,2,80,256]{3,2,1,0:T(8,128)(2,1)S(1)}, u32[]{:S(2)}, u32[]{:S(2)}) collective-permute-start(bf16[4,2,80,256]{3,2,1,0:T(8,128)(2,1)S(1)} %constant_dynamic-update-slice_fusion.10.refs_4_), channel_id=1, source_target_pairs={{0,2},{1,3},{2,0},{3,1},{4,6},{5,7},{6,4},{7,5},{8,10},{9,11},{10,... | collective-permute-start | bytes 983048 | tf_op jit(solution)/shard_map/ppermute | solution.py:162
  46.3 0.5 merge.1
  46.8 0.0 copy-start.2
  46.8 11.6 %all_to_all.10.start = f32[32,4,128]{2,1,0:T(4,128)S(1)} all-to-all(f32[32,4,128]{2,1,0:T(4,128)S(1)} %bitcast.6), channel_id=1, replica_groups=mesh['row'=2,'col'=16] {'row','col'}, dimensions={0} | all-to-all | bytes 131072 | tf_op jit(solution)/shard_map/all_to_all | solution.py:267
  58.4 0.1 collective-permute-start.14
  58.5 0.4 collective-permute-start.18
  58.9 0.1 collective-permute-start.23
  59.0 0.4 collective-permute-start.19
  59.4 0.1 collective-permute-start.24
  59.5 0.5 collective-permute-done.14.refs_3_
  60.0 1.9 %chain0.1.start = f32[8,2048]{1,0:T(8,128)S(1)} custom-call(s32[6]{0:T(128)S(1)} %copy-done.2, f32[32,4,128]{2,1,0:T(4,128)S(1)} %all_to_all.10.start, bf16[4,2,80,256]{3,2,1,0:T(8,128)(2,1)S(1)} %constant_dynamic-update-slice_fusion.refs_0_, bf16[4,2,80,256]{3,2,1,0:T(8,128)(2,1)S(1)} %collective-permute-done.8.refs_1_, ...), custom_call_target="tpu_custom_call" | custom-call | flops 67108864 | bytes 1310720 | tf_op jit(solution)/shard_map/chain0/pallas_call | solution.py:285
  61.9 3.8 %chain1.1 = bf16[4,2048]{1,0:T(4,128)(2,1)} custom-call(s32[6]{0:T(128)S(1)} %copy-done.2, f32[8,2048]{1,0:T(8,128)S(1)} %chain0.1.start, bf16[4,2,80,256]{3,2,1,0:T(8,128)(2,1)S(1)} %constant_dynamic-update-slice_fusion.7.refs_0_, bf16[4,2,80,256]{3,2,1,0:T(8,128)(2,1)S(1)} %collective-permute-done.17.refs_1_, ...), custom_call_target="tpu_custom_call" | custom-call | flops 134217728 | bytes 2621440 | tf_op jit(solution)/shard_map/chain1/pallas_call | solution.py:285
  (39 shorter events, 0.3 us)
Async XLA Ops:
  0.0 9.7 %collective-permute-start = (bf16[64,512]{1,0:T(8,128)(2,1)}, bf16[64,512]{1,0:T(8,128)(2,1)S(1)}, u32[]{:S(2)}, u32[]{:S(2)}) collective-permute-start(bf16[64,512]{1,0:T(8,128)(2,1)} %param.7), channel_id=1, source_target_pairs={{0,8},{1,9},{2,10},{3,11},{4,12},{5,13},{6,14},{7,15},{8,0},{9,1},... | collective-permute-start | bytes 196616 | tf_op jit(solution)/shard_map/ppermute | solution.py:162
  5.7 4.0 %copy-start.3 = (bf16[64,512]{1,0:T(8,128)(2,1)S(1)}, bf16[64,512]{1,0:T(8,128)(2,1)}, u32[]{:S(2)}) copy-start(bf16[64,512]{1,0:T(8,128)(2,1)} %param.7) | copy-start | bytes 196612
  5.7 12.8 %all-to-all-start = ((bf16[8,80,256]{2,1,0:T(8,128)(2,1)}), bf16[8,80,256]{2,1,0:T(8,128)(2,1)S(1)}, u32[]{:S(2)}, u32[]{:S(2)}) async-start(bf16[8,80,256]{2,1,0:T(8,128)(2,1)} %pack.1), calls=%async_computation | async-start | bytes 655360 | tf_op jit(solution)/shard_map/all_to_all | solution.py:186
  9.7 4.6 %collective-permute-start.2 = (bf16[64,512]{1,0:T(8,128)(2,1)S(1)}, bf16[64,512]{1,0:T(8,128)(2,1)S(1)}, u32[]{:S(2)}, u32[]{:S(2)}) collective-permute-start(bf16[64,512]{1,0:T(8,128)(2,1)S(1)} %get-tuple-element.27), channel_id=1, source_target_pairs={{0,16},{16,0},{1,17},{17,1},{2,18},{18,2},{3,19},{19,3},{4,20},{20... | collective-permute-start | bytes 196616 | tf_op jit(solution)/shard_map/ppermute | solution.py:165
  11.3 6.5 %collective-permute-start.1 = (bf16[1,64,512]{2,1,0:T(8,128)(2,1)S(1)}, bf16[1,64,512]{2,1,0:T(8,128)(2,1)S(1)}, u32[]{:S(2)}, u32[]{:S(2)}) collective-permute-start(bf16[1,64,512]{2,1,0:T(8,128)(2,1)S(1)} %get-tuple-element.28), channel_id=1, source_target_pairs={{0,2},{1,3},{2,0},{3,1},{4,6},{5,7},{6,4},{7,5},{8,10},{9,11},{10,... | collective-permute-start | bytes 196616 | tf_op jit(solution)/shard_map/ppermute | solution.py:162
  14.3 4.3 %collective-permute-start.3 = (bf16[1,64,512]{2,1,0:T(8,128)(2,1)S(1)}, bf16[1,64,512]{2,1,0:T(8,128)(2,1)S(1)}, u32[]{:S(2)}, u32[]{:S(2)}) collective-permute-start(bf16[1,64,512]{2,1,0:T(8,128)(2,1)S(1)} %bitcast.9), channel_id=1, source_target_pairs={{0,4},{1,5},{2,6},{3,7},{4,0},{5,1},{6,2},{7,3},{8,12},{9,13},{10,... | collective-permute-start | bytes 196616 | tf_op jit(solution)/shard_map/ppermute | solution.py:162
  17.9 0.7 %copy-start.1 = (s32[6]{0:T(128)S(1)}, s32[6]{0:T(128)}, u32[]{:S(2)}) copy-start(s32[6]{0:T(128)} %owners.3) | copy-start | bytes 76
  19.3 8.7 %collective-permute-start.4 = (bf16[1,80,256]{2,1,0:T(8,128)(2,1)S(1)}, bf16[1,80,256]{2,1,0:T(8,128)(2,1)S(1)}, u32[]{:S(2)}, u32[]{:S(2)}) collective-permute-start(bf16[1,80,256]{2,1,0:T(8,128)(2,1)S(1)} %slice.8), channel_id=1, source_target_pairs={{0,8},{1,9},{2,10},{3,11},{4,12},{5,13},{6,14},{7,15},{8,0},{9,1},... | collective-permute-start | bytes 122888 | tf_op jit(solution)/shard_map/ppermute | solution.py:162
  19.8 11.5 %collective-permute-start.5 = (bf16[4,80,256]{2,1,0:T(8,128)(2,1)S(1)}, bf16[4,80,256]{2,1,0:T(8,128)(2,1)S(1)}, u32[]{:S(2)}, u32[]{:S(2)}) collective-permute-start(bf16[4,80,256]{2,1,0:T(8,128)(2,1)S(1)} %slice.9), channel_id=1, source_target_pairs={{0,8},{1,9},{2,10},{3,11},{4,12},{5,13},{6,14},{7,15},{8,0},{9,1},... | collective-permute-start | bytes 491528 | tf_op jit(solution)/shard_map/ppermute | solution.py:162
  28.0 6.2 %collective-permute-start.9 = (bf16[2,64,512]{2,1,0:T(8,128)(2,1)S(1)}, bf16[2,64,512]{2,1,0:T(8,128)(2,1)S(1)}, u32[]{:S(2)}, u32[]{:S(2)}) collective-permute-start(bf16[2,64,512]{2,1,0:T(8,128)(2,1)S(1)} %pad_maximum_fusion.3), channel_id=1, source_target_pairs={{0,4},{1,5},{2,6},{3,7},{4,0},{5,1},{6,2},{7,3},{8,12},{9,13},{10,... | collective-permute-start | bytes 393224 | tf_op jit(solution)/shard_map/ppermute | solution.py:162
  28.1 6.5 %collective-permute-start.10 = (bf16[2,64,512]{2,1,0:T(8,128)(2,1)S(1)}, bf16[2,64,512]{2,1,0:T(8,128)(2,1)S(1)}, u32[]{:S(2)}, u32[]{:S(2)}) collective-permute-start(bf16[2,64,512]{2,1,0:T(8,128)(2,1)S(1)} %pad_maximum_fusion.4), channel_id=1, source_target_pairs={{0,2},{1,3},{2,0},{3,1},{4,6},{5,7},{6,4},{7,5},{8,10},{9,11},{10,... | collective-permute-start | bytes 393224 | tf_op jit(solution)/shard_map/ppermute | solution.py:162
  28.2 16.7 %collective-permute-start.11 = (bf16[4,64,512]{2,1,0:T(8,128)(2,1)S(1)}, bf16[4,64,512]{2,1,0:T(8,128)(2,1)S(1)}, u32[]{:S(2)}, u32[]{:S(2)}) collective-permute-start(bf16[4,64,512]{2,1,0:T(8,128)(2,1)S(1)} %constant_dynamic-update-slice_fusion.3.refs_0_), channel_id=1, source_target_pairs={{0,1},{1,0},{2,3},{3,2},{4,5},{5,4},{6,7},{7,6},{8,9},{9,8},{10,11... | collective-permute-start | bytes 786440 | tf_op jit(solution)/shard_map/ppermute | solution.py:162
  31.9 4.5 %collective-permute-start.6 = (bf16[1,2,80,256]{3,2,1,0:T(8,128)(2,1)S(1)}, bf16[1,2,80,256]{3,2,1,0:T(8,128)(2,1)S(1)}, u32[]{:S(2)}, u32[]{:S(2)}) collective-permute-start(bf16[1,2,80,256]{3,2,1,0:T(8,128)(2,1)S(1)} %get-tuple-element.20), channel_id=1, source_target_pairs={{0,16},{16,0},{1,17},{17,1},{2,18},{18,2},{3,19},{19,3},{4,20},{20... | collective-permute-start | bytes 245768 | tf_op jit(solution)/shard_map/ppermute | solution.py:165
  33.4 4.6 %collective-permute-start.15 = (bf16[1,2,80,256]{3,2,1,0:T(8,128)(2,1)S(1)}, bf16[1,2,80,256]{3,2,1,0:T(8,128)(2,1)S(1)}, u32[]{:S(2)}, u32[]{:S(2)}) collective-permute-start(bf16[1,2,80,256]{3,2,1,0:T(8,128)(2,1)S(1)} %get-tuple-element.25), channel_id=1, source_target_pairs={{0,2},{1,3},{2,0},{3,1},{4,6},{5,7},{6,4},{7,5},{8,10},{9,11},{10,... | collective-permute-start | bytes 245768 | tf_op jit(solution)/shard_map/ppermute | solution.py:162
  34.2 4.5 %collective-permute-start.20 = (bf16[1,2,80,256]{3,2,1,0:T(8,128)(2,1)S(1)}, bf16[1,2,80,256]{3,2,1,0:T(8,128)(2,1)S(1)}, u32[]{:S(2)}, u32[]{:S(2)}) collective-permute-start(bf16[1,2,80,256]{3,2,1,0:T(8,128)(2,1)S(1)} %get-tuple-element.26), channel_id=1, source_target_pairs={{0,4},{1,5},{2,6},{3,7},{4,0},{5,1},{6,2},{7,3},{8,12},{9,13},{10,... | collective-permute-start | bytes 245768 | tf_op jit(solution)/shard_map/ppermute | solution.py:162
  34.6 11.6 %collective-permute-start.12 = (bf16[4,64,512]{2,1,0:T(8,128)(2,1)S(1)}, bf16[4,64,512]{2,1,0:T(8,128)(2,1)S(1)}, u32[]{:S(2)}, u32[]{:S(2)}) collective-permute-start(bf16[4,64,512]{2,1,0:T(8,128)(2,1)S(1)} %constant_dynamic-update-slice_fusion.5.refs_1_), channel_id=1, source_target_pairs={{0,1},{1,0},{2,3},{3,2},{4,5},{5,4},{6,7},{7,6},{8,9},{9,8},{10,11... | collective-permute-start | bytes 786440 | tf_op jit(solution)/shard_map/ppermute | solution.py:162
  36.4 9.9 %copy-start = (bf16[4096,128]{1,0:T(8,128)(2,1)S(1)}, bf16[4096,128]{1,0:T(8,128)(2,1)}, u32[]{:S(2)}) copy-start(bf16[4096,128]{1,0:T(8,128)(2,1)} %sub.6) | copy-start | bytes 3145732
  36.4 5.4 %collective-permute-start.7 = (bf16[2,2,80,256]{3,2,1,0:T(8,128)(2,1)S(1)}, bf16[2,2,80,256]{3,2,1,0:T(8,128)(2,1)S(1)}, u32[]{:S(2)}, u32[]{:S(2)}) collective-permute-start(bf16[2,2,80,256]{3,2,1,0:T(8,128)(2,1)S(1)} %pad_maximum_fusion), channel_id=1, source_target_pairs={{0,2},{1,3},{2,0},{3,1},{4,6},{5,7},{6,4},{7,5},{8,10},{9,11},{10,... | collective-permute-start | bytes 491528 | tf_op jit(solution)/shard_map/ppermute | solution.py:162
  38.0 5.4 %collective-permute-start.16 = (bf16[2,2,80,256]{3,2,1,0:T(8,128)(2,1)S(1)}, bf16[2,2,80,256]{3,2,1,0:T(8,128)(2,1)S(1)}, u32[]{:S(2)}, u32[]{:S(2)}) collective-permute-start(bf16[2,2,80,256]{3,2,1,0:T(8,128)(2,1)S(1)} %pad_maximum_fusion.1), channel_id=1, source_target_pairs={{0,4},{1,5},{2,6},{3,7},{4,0},{5,1},{6,2},{7,3},{8,12},{9,13},{10,... | collective-permute-start | bytes 491528 | tf_op jit(solution)/shard_map/ppermute | solution.py:162
  38.7 5.4 %collective-permute-start.21 = (bf16[2,2,80,256]{3,2,1,0:T(8,128)(2,1)S(1)}, bf16[2,2,80,256]{3,2,1,0:T(8,128)(2,1)S(1)}, u32[]{:S(2)}, u32[]{:S(2)}) collective-permute-start(bf16[2,2,80,256]{3,2,1,0:T(8,128)(2,1)S(1)} %pad_maximum_fusion.2), channel_id=1, source_target_pairs={{0,16},{16,0},{1,17},{17,1},{2,18},{18,2},{3,19},{19,3},{4,20},{20... | collective-permute-start | bytes 491528 | tf_op jit(solution)/shard_map/ppermute | solution.py:165
  41.8 16.6 %collective-permute-start.8 = (bf16[4,2,80,256]{3,2,1,0:T(8,128)(2,1)S(1)}, bf16[4,2,80,256]{3,2,1,0:T(8,128)(2,1)S(1)}, u32[]{:S(2)}, u32[]{:S(2)}) collective-permute-start(bf16[4,2,80,256]{3,2,1,0:T(8,128)(2,1)S(1)} %constant_dynamic-update-slice_fusion.refs_0_), channel_id=1, source_target_pairs={{0,4},{1,5},{2,6},{3,7},{4,0},{5,1},{6,2},{7,3},{8,12},{9,13},{10,... | collective-permute-start | bytes 983048 | tf_op jit(solution)/shard_map/ppermute | solution.py:162
  43.4 15.5 %collective-permute-start.13 = (bf16[4,2,80,256]{3,2,1,0:T(8,128)(2,1)S(1)}, bf16[4,2,80,256]{3,2,1,0:T(8,128)(2,1)S(1)}, u32[]{:S(2)}, u32[]{:S(2)}) collective-permute-start(bf16[4,2,80,256]{3,2,1,0:T(8,128)(2,1)S(1)} %constant_dynamic-update-slice_fusion.refs_0_), channel_id=1, source_target_pairs={{0,1},{1,0},{2,3},{3,2},{4,5},{5,4},{6,7},{7,6},{8,9},{9,8},{10,11... | collective-permute-start | bytes 983048 | tf_op jit(solution)/shard_map/ppermute | solution.py:162
  44.1 14.9 %collective-permute-start.17 = (bf16[4,2,80,256]{3,2,1,0:T(8,128)(2,1)S(1)}, bf16[4,2,80,256]{3,2,1,0:T(8,128)(2,1)S(1)}, u32[]{:S(2)}, u32[]{:S(2)}) collective-permute-start(bf16[4,2,80,256]{3,2,1,0:T(8,128)(2,1)S(1)} %constant_dynamic-update-slice_fusion.7.refs_0_), channel_id=1, source_target_pairs={{0,16},{16,0},{1,17},{17,1},{2,18},{18,2},{3,19},{19,3},{4,20},{20... | collective-permute-start | bytes 983048 | tf_op jit(solution)/shard_map/ppermute | solution.py:165
  44.9 14.5 %collective-permute-start.22 = (bf16[4,2,80,256]{3,2,1,0:T(8,128)(2,1)S(1)}, bf16[4,2,80,256]{3,2,1,0:T(8,128)(2,1)S(1)}, u32[]{:S(2)}, u32[]{:S(2)}) collective-permute-start(bf16[4,2,80,256]{3,2,1,0:T(8,128)(2,1)S(1)} %constant_dynamic-update-slice_fusion.10.refs_4_), channel_id=1, source_target_pairs={{0,2},{1,3},{2,0},{3,1},{4,6},{5,7},{6,4},{7,5},{8,10},{9,11},{10,... | collective-permute-start | bytes 983048 | tf_op jit(solution)/shard_map/ppermute | solution.py:162
  46.8 13.3 %copy-start.2 = (s32[6]{0:T(128)S(1)}, s32[6]{0:T(128)}, u32[]{:S(2)}) copy-start(s32[6]{0:T(128)} %offsets.3) | copy-start | bytes 76
  58.4 1.6 %collective-permute-start.14 = (bf16[4,2,80,256]{3,2,1,0:T(8,128)(2,1)S(1)}, bf16[4,2,80,256]{3,2,1,0:T(8,128)(2,1)S(1)}, u32[]{:S(2)}, u32[]{:S(2)}) collective-permute-start(bf16[4,2,80,256]{3,2,1,0:T(8,128)(2,1)S(1)} %collective-permute-done.8.refs_1_), channel_id=1, source_target_pairs={{0,1},{1,0},{2,3},{3,2},{4,5},{5,4},{6,7},{7,6},{8,9},{9,8},{10,11... | collective-permute-start | bytes 983048 | tf_op jit(solution)/shard_map/ppermute | solution.py:162
  58.5 3.4 %collective-permute-start.18 = (bf16[4,2,80,256]{3,2,1,0:T(8,128)(2,1)S(1)}, bf16[4,2,80,256]{3,2,1,0:T(8,128)(2,1)S(1)}, u32[]{:S(2)}, u32[]{:S(2)}) collective-permute-start(bf16[4,2,80,256]{3,2,1,0:T(8,128)(2,1)S(1)} %constant_dynamic-update-slice_fusion.7.refs_0_), channel_id=1, source_target_pairs={{0,1},{1,0},{2,3},{3,2},{4,5},{5,4},{6,7},{7,6},{8,9},{9,8},{10,11... | collective-permute-start | bytes 983048 | tf_op jit(solution)/shard_map/ppermute | solution.py:162
  58.9 3.0 %collective-permute-start.23 = (bf16[4,2,80,256]{3,2,1,0:T(8,128)(2,1)S(1)}, bf16[4,2,80,256]{3,2,1,0:T(8,128)(2,1)S(1)}, u32[]{:S(2)}, u32[]{:S(2)}) collective-permute-start(bf16[4,2,80,256]{3,2,1,0:T(8,128)(2,1)S(1)} %constant_dynamic-update-slice_fusion.10.refs_4_), channel_id=1, source_target_pairs={{0,1},{1,0},{2,3},{3,2},{4,5},{5,4},{6,7},{7,6},{8,9},{9,8},{10,11... | collective-permute-start | bytes 983048 | tf_op jit(solution)/shard_map/ppermute | solution.py:162
  59.0 2.9 %collective-permute-start.19 = (bf16[4,2,80,256]{3,2,1,0:T(8,128)(2,1)S(1)}, bf16[4,2,80,256]{3,2,1,0:T(8,128)(2,1)S(1)}, u32[]{:S(2)}, u32[]{:S(2)}) collective-permute-start(bf16[4,2,80,256]{3,2,1,0:T(8,128)(2,1)S(1)} %collective-permute-done.17.refs_1_), channel_id=1, source_target_pairs={{0,1},{1,0},{2,3},{3,2},{4,5},{5,4},{6,7},{7,6},{8,9},{9,8},{10,11... | collective-permute-start | bytes 983048 | tf_op jit(solution)/shard_map/ppermute | solution.py:162
  59.4 2.5 %collective-permute-start.24 = (bf16[4,2,80,256]{3,2,1,0:T(8,128)(2,1)S(1)}, bf16[4,2,80,256]{3,2,1,0:T(8,128)(2,1)S(1)}, u32[]{:S(2)}, u32[]{:S(2)}) collective-permute-start(bf16[4,2,80,256]{3,2,1,0:T(8,128)(2,1)S(1)} %collective-permute-done.22.refs_5_), channel_id=1, source_target_pairs={{0,1},{1,0},{2,3},{3,2},{4,5},{5,4},{6,7},{7,6},{8,9},{9,8},{10,11... | collective-permute-start | bytes 983048 | tf_op jit(solution)/shard_map/ppermute | solution.py:162

commit v29 on v27

--- a/solution.py
+++ b/solution.py
@@ -74,10 +74,8 @@
     for group in range(GROUPS):
         half, rank = places(owners, group)
         piece = held[lax.rem(owners[group], HALF)]
-        for mask in range(1, len(others) // 2 + 1):
-            head, tail = others[2 * mask - 2 : 2 * mask]
-            other = tail[jnp.clip(rank - 1, 0, tail.shape[0] - 1)]
-            other = jnp.where(rank == 0, head[0], other)
+        for mask, ref in enumerate(others, 1):
+            other = ref[jnp.minimum(rank, ref.shape[0] - 1)]
             piece = jnp.where(jnp.bitwise_xor(half, mine) == mask, other, piece)
         outs[group // each][0, group % each] = piece
 
@@ -221,10 +219,8 @@
         cost_estimate=cost([slices]),
         name="pick",
     )(owners, slices)
-    heads = [over_col(picked[:1], m * HALF) for m in range(1, halves)]
-    tails = [over_col(picked[1:], m * HALF) for m in range(1, halves)]
-    heads, sides = lax.optimization_barrier((heads, sides))
-    others = [x for pair in zip(heads, tails) for x in pair]
+    others = [over_col(picked, m * HALF) for m in range(1, halves)]
+    others, sides = lax.optimization_barrier((others, sides))
     late = jnp.concatenate([over_col(sides[0], 4), over_col(sides[1], 2)])
     late_tags = [(m, c ^ 4) for m, c in tags[0]] + [(m, c ^ 2) for m, c in tags[1]]
     m_held = [jnp.concatenate(sides), late]

time: 66 us -> 69.1 us (1.047)
  starting transfers between devices: 25.4 us -> 28.3 us
  waiting for transfers between devices: 18.7 us -> 20.8 us
  blocking collectives: 11.9 us -> 10.1 us
    ppermute x21 -> x20, starting transfers between devices: 16 us -> 19.2 us  [over_col(): return lax.ppermute(x, 'col', [(c, c ^ mask) for c in range(cols)])]
    all_to_all x1, blocking collectives: 11.9 us -> 10.1 us  [local(): lax.all_to_all(merged.reshape(rows * cols, each, width), ('row', 'col'),...]
    ppermute x21 -> x20, waiting for transfers between devices: 15.5 us -> 16.9 us  [over_col(): return lax.ppermute(x, 'col', [(c, c ^ mask) for c in range(cols)])]
    ppermute x4, waiting for transfers between devices: 3.19 us -> 3.92 us  [over_row(): return lax.ppermute(x, 'row', [(r, r ^ mask) for r in range(rows)])]
  transfers between devices with their start and end apart: 26 -> 25, of which waited for: 10 -> 7; matrix products, arithmetic and copies ran while one was open for 0% -> 0% of each run, Pallas kernels for 7% -> 7%
where the time goes in v29:
time: 69.1 us; the launch traced here: 68.8 us
  starting transfers between devices  28.3 us (41%)
  waiting for transfers between devices  20.8 us (30%)
  blocking collectives  10.1 us (15%)
  Pallas kernels  9.17 us (13%)
    ppermute x20, starting transfers between devices, over_col(): return lax.ppermute(x, 'col', [(c, c ^ mask) for c in range(cols)])  19.2 us
    ppermute x20, waiting for transfers between devices, over_col(): return lax.ppermute(x, 'col', [(c, c ^ mask) for c in range(cols)])  16.9 us
    all_to_all x1, blocking collectives, local(): lax.all_to_all(merged.reshape(rows * cols, each, width), ('row', 'col'),...  10.1 us
    pallas_call x2, Pallas kernels, local(): pl.pallas_call(functools.partial(chain_kernel, cols, groups, slots, sum((...  5.68 us
    ppermute x4, starting transfers between devices, over_row(): return lax.ppermute(x, 'row', [(r, r ^ mask) for r in range(rows)])  5.08 us
    all_to_all x1, starting transfers between devices, local(): slices = lax.all_to_all(packed, 'col', 0, 0, axis_index_groups=members)  3.95 us
    ppermute x4, waiting for transfers between devices, over_row(): return lax.ppermute(x, 'row', [(r, r ^ mask) for r in range(rows)])  3.92 us
    pallas_call x1, Pallas kernels, local(): pl.pallas_call(pack_kernel, out_shape=jax.ShapeDtypeStruct((HALF,) + piec...  1.69 us
  transfers between devices with their start and end apart: 25, of which 7 were waited for; matrix products, arithmetic and copies ran while one was open for 0% of the time, Pallas kernels for 7%

profile of v29, /device:TPU:0, one launch (start us, length us, event | category | flops | bytes accessed | tf_op | source)
XLA Modules:
  0.0 68.8 jit_solution(4379737693231573038)
XLA Ops:
  0.0 4.0 %collective-permute-start = (bf16[64,512]{1,0:T(8,128)(2,1)}, bf16[64,512]{1,0:T(8,128)(2,1)S(1)}, u32[]{:S(2)}, u32[]{:S(2)}) collective-permute-start(bf16[64,512]{1,0:T(8,128)(2,1)} %param.7), channel_id=1, source_target_pairs={{0,8},{1,9},{2,10},{3,11},{4,12},{5,13},{6,14},{7,15},{8,0},{9,1},... | collective-permute-start | bytes 196616 | tf_op jit(solution)/shard_map/ppermute | solution.py:160
  4.0 1.7 %pack.1 = bf16[8,80,256]{2,1,0:T(8,128)(2,1)} custom-call(bf16[16,64,256]{2,1,0:T(8,128)(2,1)} %bitcast.7, bf16[16,16,256]{2,1,0:T(8,128)(2,1)} %bitcast.8), custom_call_target="tpu_custom_call" | custom-call | bytes 655360 | tf_op jit(solution)/shard_map/pack/pallas_call | solution.py:173
  5.7 0.0 copy-start.3
  5.7 4.0 %all-to-all-start = ((bf16[8,80,256]{2,1,0:T(8,128)(2,1)}), bf16[8,80,256]{2,1,0:T(8,128)(2,1)S(1)}, u32[]{:S(2)}, u32[]{:S(2)}) async-start(bf16[8,80,256]{2,1,0:T(8,128)(2,1)} %pack.1), calls=%async_computation | async-start | bytes 655360 | tf_op jit(solution)/shard_map/all_to_all | solution.py:184
  9.7 1.6 %collective-permute-start.2 = (bf16[64,512]{1,0:T(8,128)(2,1)S(1)}, bf16[64,512]{1,0:T(8,128)(2,1)S(1)}, u32[]{:S(2)}, u32[]{:S(2)}) collective-permute-start(bf16[64,512]{1,0:T(8,128)(2,1)S(1)} %get-tuple-element.31), channel_id=1, source_target_pairs={{0,16},{16,0},{1,17},{17,1},{2,18},{18,2},{3,19},{19,3},{4,20},{20... | collective-permute-start | bytes 196616 | tf_op jit(solution)/shard_map/ppermute | solution.py:163
  11.3 2.0 %collective-permute-start.1 = (bf16[1,64,512]{2,1,0:T(8,128)(2,1)S(1)}, bf16[1,64,512]{2,1,0:T(8,128)(2,1)S(1)}, u32[]{:S(2)}, u32[]{:S(2)}) collective-permute-start(bf16[1,64,512]{2,1,0:T(8,128)(2,1)S(1)} %get-tuple-element.32), channel_id=1, source_target_pairs={{0,2},{1,3},{2,0},{3,1},{4,6},{5,7},{6,4},{7,5},{8,10},{9,11},{10,... | collective-permute-start | bytes 196616 | tf_op jit(solution)/shard_map/ppermute | solution.py:160
  13.3 1.0 %collective-permute-done.2 = bf16[64,512]{1,0:T(8,128)(2,1)S(1)} collective-permute-done((bf16[64,512]{1,0:T(8,128)(2,1)S(1)}, bf16[64,512]{1,0:T(8,128)(2,1)S(1)}, u32[]{:S(2)}, u32[]{:S(2)}) %collective-permute-start.2) | collective-permute-done | bytes 65568 | tf_op jit(solution)/shard_map/ppermute | solution.py:163
  14.3 1.8 %collective-permute-start.3 = (bf16[1,64,512]{2,1,0:T(8,128)(2,1)S(1)}, bf16[1,64,512]{2,1,0:T(8,128)(2,1)S(1)}, u32[]{:S(2)}, u32[]{:S(2)}) collective-permute-start(bf16[1,64,512]{2,1,0:T(8,128)(2,1)S(1)} %bitcast.9), channel_id=1, source_target_pairs={{0,4},{1,5},{2,6},{3,7},{4,0},{5,1},{6,2},{7,3},{8,12},{9,13},{10,... | collective-permute-start | bytes 196616 | tf_op jit(solution)/shard_map/ppermute | solution.py:160
  16.1 1.8 %collective-permute-done.1 = bf16[1,64,512]{2,1,0:T(8,128)(2,1)S(1)} collective-permute-done((bf16[1,64,512]{2,1,0:T(8,128)(2,1)S(1)}, bf16[1,64,512]{2,1,0:T(8,128)(2,1)S(1)}, u32[]{:S(2)}, u32[]{:S(2)}) %collective-permute-start.1) | collective-permute-done | bytes 65568 | tf_op jit(solution)/shard_map/ppermute | solution.py:160
  17.9 0.0 copy-start.1
  17.9 0.7 %collective-permute-done.3 = bf16[1,64,512]{2,1,0:T(8,128)(2,1)S(1)} collective-permute-done((bf16[1,64,512]{2,1,0:T(8,128)(2,1)S(1)}, bf16[1,64,512]{2,1,0:T(8,128)(2,1)S(1)}, u32[]{:S(2)}, u32[]{:S(2)}) %collective-permute-start.3) | collective-permute-done | bytes 65568 | tf_op jit(solution)/shard_map/ppermute | solution.py:160
  18.6 0.0 all-to-all-done.held
  18.6 0.7 %pick.1 = bf16[5,80,256]{2,1,0:T(8,128)(2,1)S(1)} custom-call(s32[6]{0:T(128)S(1)} %copy-done.1, bf16[8,80,256]{2,1,0:T(8,128)(2,1)S(1)} %all-to-all-done.held), custom_call_target="tpu_custom_call" | custom-call | bytes 327680 | tf_op jit(solution)/shard_map/pick/pallas_call | solution.py:213
  19.3 0.4 collective-permute-start.4
  19.7 11.5 %collective-permute-done.4.refs_0_ = bf16[5,80,256]{2,1,0:T(8,128)(2,1)S(1)} collective-permute-done((bf16[5,80,256]{2,1,0:T(8,128)(2,1)S(1)}, bf16[5,80,256]{2,1,0:T(8,128)(2,1)S(1)}, u32[]{:S(2)}, u32[]{:S(2)}) %collective-permute-start.4) | collective-permute-done | bytes 204832 | tf_op jit(solution)/shard_map/ppermute | solution.py:160
  31.2 0.0 collective-permute-start.14
  31.2 0.6 order.1
  31.8 0.8 %collective-permute-start.8 = (bf16[1,2,80,256]{3,2,1,0:T(8,128)(2,1)S(1)}, bf16[1,2,80,256]{3,2,1,0:T(8,128)(2,1)S(1)}, u32[]{:S(2)}, u32[]{:S(2)}) collective-permute-start(bf16[1,2,80,256]{3,2,1,0:T(8,128)(2,1)S(1)} %get-tuple-element.23), channel_id=1, source_target_pairs={{0,2},{1,3},{2,0},{3,1},{4,6},{5,7},{6,4},{7,5},{8,10},{9,11},{10,... | collective-permute-start | bytes 245768 | tf_op jit(solution)/shard_map/ppermute | solution.py:160
  32.7 1.4 %collective-permute-start.5 = (bf16[1,2,80,256]{3,2,1,0:T(8,128)(2,1)S(1)}, bf16[1,2,80,256]{3,2,1,0:T(8,128)(2,1)S(1)}, u32[]{:S(2)}, u32[]{:S(2)}) collective-permute-start(bf16[1,2,80,256]{3,2,1,0:T(8,128)(2,1)S(1)} %get-tuple-element.22), channel_id=1, source_target_pairs={{0,16},{16,0},{1,17},{17,1},{2,18},{18,2},{3,19},{19,3},{4,20},{20... | collective-permute-start | bytes 245768 | tf_op jit(solution)/shard_map/ppermute | solution.py:163
  34.1 1.4 %collective-permute-start.15 = (bf16[2,64,512]{2,1,0:T(8,128)(2,1)S(1)}, bf16[2,64,512]{2,1,0:T(8,128)(2,1)S(1)}, u32[]{:S(2)}, u32[]{:S(2)}) collective-permute-start(bf16[2,64,512]{2,1,0:T(8,128)(2,1)S(1)} %pad_maximum_fusion.4), channel_id=1, source_target_pairs={{0,2},{1,3},{2,0},{3,1},{4,6},{5,7},{6,4},{7,5},{8,10},{9,11},{10,... | collective-permute-start | bytes 393224 | tf_op jit(solution)/shard_map/ppermute | solution.py:160
  35.5 2.1 %collective-permute-start.11 = (bf16[1,2,80,256]{3,2,1,0:T(8,128)(2,1)S(1)}, bf16[1,2,80,256]{3,2,1,0:T(8,128)(2,1)S(1)}, u32[]{:S(2)}, u32[]{:S(2)}) collective-permute-start(bf16[1,2,80,256]{3,2,1,0:T(8,128)(2,1)S(1)} %get-tuple-element.24), channel_id=1, source_target_pairs={{0,4},{1,5},{2,6},{3,7},{4,0},{5,1},{6,2},{7,3},{8,12},{9,13},{10,... | collective-permute-start | bytes 245768 | tf_op jit(solution)/shard_map/ppermute | solution.py:160
  37.6 2.4 %collective-permute-done.11 = bf16[1,2,80,256]{3,2,1,0:T(8,128)(2,1)S(1)} collective-permute-done((bf16[1,2,80,256]{3,2,1,0:T(8,128)(2,1)S(1)}, bf16[1,2,80,256]{3,2,1,0:T(8,128)(2,1)S(1)}, u32[]{:S(2)}, u32[]{:S(2)}) %collective-permute-start.11) | collective-permute-done | bytes 81952 | tf_op jit(solution)/shard_map/ppermute | solution.py:160
  40.0 0.0 collective-permute-start.16
  40.1 0.0 collective-permute-done.8
  40.1 0.6 collective-permute-start.12
  40.7 0.0 copy-start
  40.7 0.0 collective-permute-done.5
  40.7 2.1 %collective-permute-start.9 = (bf16[2,2,80,256]{3,2,1,0:T(8,128)(2,1)S(1)}, bf16[2,2,80,256]{3,2,1,0:T(8,128)(2,1)S(1)}, u32[]{:S(2)}, u32[]{:S(2)}) collective-permute-start(bf16[2,2,80,256]{3,2,1,0:T(8,128)(2,1)S(1)} %pad_maximum_fusion.1), channel_id=1, source_target_pairs={{0,4},{1,5},{2,6},{3,7},{4,0},{5,1},{6,2},{7,3},{8,12},{9,13},{10,... | collective-permute-start | bytes 491528 | tf_op jit(solution)/shard_map/ppermute | solution.py:160
  42.9 0.0 collective-permute-done.14
  42.9 0.8 %collective-permute-start.6 = (bf16[2,2,80,256]{3,2,1,0:T(8,128)(2,1)S(1)}, bf16[2,2,80,256]{3,2,1,0:T(8,128)(2,1)S(1)}, u32[]{:S(2)}, u32[]{:S(2)}) collective-permute-start(bf16[2,2,80,256]{3,2,1,0:T(8,128)(2,1)S(1)} %pad_maximum_fusion), channel_id=1, source_target_pairs={{0,2},{1,3},{2,0},{3,1},{4,6},{5,7},{6,4},{7,5},{8,10},{9,11},{10,... | collective-permute-start | bytes 491528 | tf_op jit(solution)/shard_map/ppermute | solution.py:160
  43.7 0.0 collective-permute-done.15
  43.7 0.1 collective-permute-start.17
  43.8 2.9 %collective-permute-done.12 = bf16[2,2,80,256]{3,2,1,0:T(8,128)(2,1)S(1)} collective-permute-done((bf16[2,2,80,256]{3,2,1,0:T(8,128)(2,1)S(1)}, bf16[2,2,80,256]{3,2,1,0:T(8,128)(2,1)S(1)}, u32[]{:S(2)}, u32[]{:S(2)}) %collective-permute-start.12) | collective-permute-done | bytes 163872 | tf_op jit(solution)/shard_map/ppermute | solution.py:163
  46.8 0.7 %collective-permute-start.13 = (bf16[4,2,80,256]{3,2,1,0:T(8,128)(2,1)S(1)}, bf16[4,2,80,256]{3,2,1,0:T(8,128)(2,1)S(1)}, u32[]{:S(2)}, u32[]{:S(2)}) collective-permute-start(bf16[4,2,80,256]{3,2,1,0:T(8,128)(2,1)S(1)} %constant_dynamic-update-slice_fusion.6.refs_4_), channel_id=1, source_target_pairs={{0,2},{1,3},{2,0},{3,1},{4,6},{5,7},{6,4},{7,5},{8,10},{9,11},{10,... | collective-permute-start | bytes 983048 | tf_op jit(solution)/shard_map/ppermute | solution.py:160
  47.5 1.5 %collective-permute-start.10 = (bf16[4,2,80,256]{3,2,1,0:T(8,128)(2,1)S(1)}, bf16[4,2,80,256]{3,2,1,0:T(8,128)(2,1)S(1)}, u32[]{:S(2)}, u32[]{:S(2)}) collective-permute-start(bf16[4,2,80,256]{3,2,1,0:T(8,128)(2,1)S(1)} %constant_dynamic-update-slice_fusion.3.refs_0_), channel_id=1, source_target_pairs={{0,16},{16,0},{1,17},{17,1},{2,18},{18,2},{3,19},{19,3},{4,20},{20... | collective-permute-start | bytes 983048 | tf_op jit(solution)/shard_map/ppermute | solution.py:163
  49.0 0.0 collective-permute-done.6
  49.0 1.8 %collective-permute-start.7 = (bf16[4,2,80,256]{3,2,1,0:T(8,128)(2,1)S(1)}, bf16[4,2,80,256]{3,2,1,0:T(8,128)(2,1)S(1)}, u32[]{:S(2)}, u32[]{:S(2)}) collective-permute-start(bf16[4,2,80,256]{3,2,1,0:T(8,128)(2,1)S(1)} %constant_dynamic-update-slice_fusion.refs_0_), channel_id=1, source_target_pairs={{0,4},{1,5},{2,6},{3,7},{4,0},{5,1},{6,2},{7,3},{8,12},{9,13},{10,... | collective-permute-start | bytes 983048 | tf_op jit(solution)/shard_map/ppermute | solution.py:160
  50.8 0.5 merge.1
  51.3 0.0 copy-start.2
  51.3 10.1 %all_to_all.10.start = f32[32,4,128]{2,1,0:T(4,128)S(1)} all-to-all(f32[32,4,128]{2,1,0:T(4,128)S(1)} %bitcast.6), channel_id=1, replica_groups=mesh['row'=2,'col'=16] {'row','col'}, dimensions={0} | all-to-all | bytes 131072 | tf_op jit(solution)/shard_map/all_to_all | solution.py:263
  61.4 0.2 collective-permute-start.19
  61.6 0.4 collective-permute-start.22
  62.0 0.1 collective-permute-start.20
  62.1 0.4 collective-permute-start.21
  62.5 0.1 collective-permute-start.23
  62.6 0.5 collective-permute-done.19.refs_3_
  63.1 1.9 %chain0.1.start = f32[8,2048]{1,0:T(8,128)S(1)} custom-call(s32[6]{0:T(128)S(1)} %copy-done.2, f32[32,4,128]{2,1,0:T(4,128)S(1)} %all_to_all.10.start, bf16[4,2,80,256]{3,2,1,0:T(8,128)(2,1)S(1)} %constant_dynamic-update-slice_fusion.refs_0_, bf16[4,2,80,256]{3,2,1,0:T(8,128)(2,1)S(1)} %collective-permute-done.7.refs_1_, ...), custom_call_target="tpu_custom_call" | custom-call | flops 67108864 | bytes 1310720 | tf_op jit(solution)/shard_map/chain0/pallas_call | solution.py:281
  65.0 3.8 %chain1.1 = bf16[4,2048]{1,0:T(4,128)(2,1)} custom-call(s32[6]{0:T(128)S(1)} %copy-done.2, f32[8,2048]{1,0:T(8,128)S(1)} %chain0.1.start, bf16[4,2,80,256]{3,2,1,0:T(8,128)(2,1)S(1)} %constant_dynamic-update-slice_fusion.3.refs_0_, bf16[4,2,80,256]{3,2,1,0:T(8,128)(2,1)S(1)} %collective-permute-done.10.refs_1_, ...), custom_call_target="tpu_custom_call" | custom-call | flops 134217728 | bytes 2621440 | tf_op jit(solution)/shard_map/chain1/pallas_call | solution.py:281
  (35 shorter events, 0.3 us)
Async XLA Ops:
  0.0 9.7 %collective-permute-start = (bf16[64,512]{1,0:T(8,128)(2,1)}, bf16[64,512]{1,0:T(8,128)(2,1)S(1)}, u32[]{:S(2)}, u32[]{:S(2)}) collective-permute-start(bf16[64,512]{1,0:T(8,128)(2,1)} %param.7), channel_id=1, source_target_pairs={{0,8},{1,9},{2,10},{3,11},{4,12},{5,13},{6,14},{7,15},{8,0},{9,1},... | collective-permute-start | bytes 196616 | tf_op jit(solution)/shard_map/ppermute | solution.py:160
  5.7 4.0 %copy-start.3 = (bf16[64,512]{1,0:T(8,128)(2,1)S(1)}, bf16[64,512]{1,0:T(8,128)(2,1)}, u32[]{:S(2)}) copy-start(bf16[64,512]{1,0:T(8,128)(2,1)} %param.7) | copy-start | bytes 196612
  5.7 12.8 %all-to-all-start = ((bf16[8,80,256]{2,1,0:T(8,128)(2,1)}), bf16[8,80,256]{2,1,0:T(8,128)(2,1)S(1)}, u32[]{:S(2)}, u32[]{:S(2)}) async-start(bf16[8,80,256]{2,1,0:T(8,128)(2,1)} %pack.1), calls=%async_computation | async-start | bytes 655360 | tf_op jit(solution)/shard_map/all_to_all | solution.py:184
  9.7 4.6 %collective-permute-start.2 = (bf16[64,512]{1,0:T(8,128)(2,1)S(1)}, bf16[64,512]{1,0:T(8,128)(2,1)S(1)}, u32[]{:S(2)}, u32[]{:S(2)}) collective-permute-start(bf16[64,512]{1,0:T(8,128)(2,1)S(1)} %get-tuple-element.31), channel_id=1, source_target_pairs={{0,16},{16,0},{1,17},{17,1},{2,18},{18,2},{3,19},{19,3},{4,20},{20... | collective-permute-start | bytes 196616 | tf_op jit(solution)/shard_map/ppermute | solution.py:163
  11.3 6.5 %collective-permute-start.1 = (bf16[1,64,512]{2,1,0:T(8,128)(2,1)S(1)}, bf16[1,64,512]{2,1,0:T(8,128)(2,1)S(1)}, u32[]{:S(2)}, u32[]{:S(2)}) collective-permute-start(bf16[1,64,512]{2,1,0:T(8,128)(2,1)S(1)} %get-tuple-element.32), channel_id=1, source_target_pairs={{0,2},{1,3},{2,0},{3,1},{4,6},{5,7},{6,4},{7,5},{8,10},{9,11},{10,... | collective-permute-start | bytes 196616 | tf_op jit(solution)/shard_map/ppermute | solution.py:160
  14.3 4.3 %collective-permute-start.3 = (bf16[1,64,512]{2,1,0:T(8,128)(2,1)S(1)}, bf16[1,64,512]{2,1,0:T(8,128)(2,1)S(1)}, u32[]{:S(2)}, u32[]{:S(2)}) collective-permute-start(bf16[1,64,512]{2,1,0:T(8,128)(2,1)S(1)} %bitcast.9), channel_id=1, source_target_pairs={{0,4},{1,5},{2,6},{3,7},{4,0},{5,1},{6,2},{7,3},{8,12},{9,13},{10,... | collective-permute-start | bytes 196616 | tf_op jit(solution)/shard_map/ppermute | solution.py:160
  17.9 0.7 %copy-start.1 = (s32[6]{0:T(128)S(1)}, s32[6]{0:T(128)}, u32[]{:S(2)}) copy-start(s32[6]{0:T(128)} %owners.3) | copy-start | bytes 76
  19.3 11.9 %collective-permute-start.4 = (bf16[5,80,256]{2,1,0:T(8,128)(2,1)S(1)}, bf16[5,80,256]{2,1,0:T(8,128)(2,1)S(1)}, u32[]{:S(2)}, u32[]{:S(2)}) collective-permute-start(bf16[5,80,256]{2,1,0:T(8,128)(2,1)S(1)} %pick.1), channel_id=1, source_target_pairs={{0,8},{1,9},{2,10},{3,11},{4,12},{5,13},{6,14},{7,15},{8,0},{9,1},... | collective-permute-start | bytes 614408 | tf_op jit(solution)/shard_map/ppermute | solution.py:160
  31.2 11.7 %collective-permute-start.14 = (bf16[2,64,512]{2,1,0:T(8,128)(2,1)S(1)}, bf16[2,64,512]{2,1,0:T(8,128)(2,1)S(1)}, u32[]{:S(2)}, u32[]{:S(2)}) collective-permute-start(bf16[2,64,512]{2,1,0:T(8,128)(2,1)S(1)} %pad_maximum_fusion.3), channel_id=1, source_target_pairs={{0,4},{1,5},{2,6},{3,7},{4,0},{5,1},{6,2},{7,3},{8,12},{9,13},{10,... | collective-permute-start | bytes 393224 | tf_op jit(solution)/shard_map/ppermute | solution.py:160
  31.8 8.2 %collective-permute-start.8 = (bf16[1,2,80,256]{3,2,1,0:T(8,128)(2,1)S(1)}, bf16[1,2,80,256]{3,2,1,0:T(8,128)(2,1)S(1)}, u32[]{:S(2)}, u32[]{:S(2)}) collective-permute-start(bf16[1,2,80,256]{3,2,1,0:T(8,128)(2,1)S(1)} %get-tuple-element.23), channel_id=1, source_target_pairs={{0,2},{1,3},{2,0},{3,1},{4,6},{5,7},{6,4},{7,5},{8,10},{9,11},{10,... | collective-permute-start | bytes 245768 | tf_op jit(solution)/shard_map/ppermute | solution.py:160
  32.7 8.0 %collective-permute-start.5 = (bf16[1,2,80,256]{3,2,1,0:T(8,128)(2,1)S(1)}, bf16[1,2,80,256]{3,2,1,0:T(8,128)(2,1)S(1)}, u32[]{:S(2)}, u32[]{:S(2)}) collective-permute-start(bf16[1,2,80,256]{3,2,1,0:T(8,128)(2,1)S(1)} %get-tuple-element.22), channel_id=1, source_target_pairs={{0,16},{16,0},{1,17},{17,1},{2,18},{18,2},{3,19},{19,3},{4,20},{20... | collective-permute-start | bytes 245768 | tf_op jit(solution)/shard_map/ppermute | solution.py:163
  34.1 9.6 %collective-permute-start.15 = (bf16[2,64,512]{2,1,0:T(8,128)(2,1)S(1)}, bf16[2,64,512]{2,1,0:T(8,128)(2,1)S(1)}, u32[]{:S(2)}, u32[]{:S(2)}) collective-permute-start(bf16[2,64,512]{2,1,0:T(8,128)(2,1)S(1)} %pad_maximum_fusion.4), channel_id=1, source_target_pairs={{0,2},{1,3},{2,0},{3,1},{4,6},{5,7},{6,4},{7,5},{8,10},{9,11},{10,... | collective-permute-start | bytes 393224 | tf_op jit(solution)/shard_map/ppermute | solution.py:160
  35.5 4.5 %collective-permute-start.11 = (bf16[1,2,80,256]{3,2,1,0:T(8,128)(2,1)S(1)}, bf16[1,2,80,256]{3,2,1,0:T(8,128)(2,1)S(1)}, u32[]{:S(2)}, u32[]{:S(2)}) collective-permute-start(bf16[1,2,80,256]{3,2,1,0:T(8,128)(2,1)S(1)} %get-tuple-element.24), channel_id=1, source_target_pairs={{0,4},{1,5},{2,6},{3,7},{4,0},{5,1},{6,2},{7,3},{8,12},{9,13},{10,... | collective-permute-start | bytes 245768 | tf_op jit(solution)/shard_map/ppermute | solution.py:160
  40.0 10.8 %collective-permute-start.16 = (bf16[4,64,512]{2,1,0:T(8,128)(2,1)S(1)}, bf16[4,64,512]{2,1,0:T(8,128)(2,1)S(1)}, u32[]{:S(2)}, u32[]{:S(2)}) collective-permute-start(bf16[4,64,512]{2,1,0:T(8,128)(2,1)S(1)} %constant_dynamic-update-slice_fusion.9.refs_0_), channel_id=1, source_target_pairs={{0,1},{1,0},{2,3},{3,2},{4,5},{5,4},{6,7},{7,6},{8,9},{9,8},{10,11... | collective-permute-start | bytes 786440 | tf_op jit(solution)/shard_map/ppermute | solution.py:160
  40.1 6.7 %collective-permute-start.12 = (bf16[2,2,80,256]{3,2,1,0:T(8,128)(2,1)S(1)}, bf16[2,2,80,256]{3,2,1,0:T(8,128)(2,1)S(1)}, u32[]{:S(2)}, u32[]{:S(2)}) collective-permute-start(bf16[2,2,80,256]{3,2,1,0:T(8,128)(2,1)S(1)} %pad_maximum_fusion.2), channel_id=1, source_target_pairs={{0,16},{16,0},{1,17},{17,1},{2,18},{18,2},{3,19},{19,3},{4,20},{20... | collective-permute-start | bytes 491528 | tf_op jit(solution)/shard_map/ppermute | solution.py:163
  40.7 10.1 %copy-start = (bf16[4096,128]{1,0:T(8,128)(2,1)S(1)}, bf16[4096,128]{1,0:T(8,128)(2,1)}, u32[]{:S(2)}) copy-start(bf16[4096,128]{1,0:T(8,128)(2,1)} %sub.6) | copy-start | bytes 3145732
  40.7 6.8 %collective-permute-start.9 = (bf16[2,2,80,256]{3,2,1,0:T(8,128)(2,1)S(1)}, bf16[2,2,80,256]{3,2,1,0:T(8,128)(2,1)S(1)}, u32[]{:S(2)}, u32[]{:S(2)}) collective-permute-start(bf16[2,2,80,256]{3,2,1,0:T(8,128)(2,1)S(1)} %pad_maximum_fusion.1), channel_id=1, source_target_pairs={{0,4},{1,5},{2,6},{3,7},{4,0},{5,1},{6,2},{7,3},{8,12},{9,13},{10,... | collective-permute-start | bytes 491528 | tf_op jit(solution)/shard_map/ppermute | solution.py:160
  42.9 6.1 %collective-permute-start.6 = (bf16[2,2,80,256]{3,2,1,0:T(8,128)(2,1)S(1)}, bf16[2,2,80,256]{3,2,1,0:T(8,128)(2,1)S(1)}, u32[]{:S(2)}, u32[]{:S(2)}) collective-permute-start(bf16[2,2,80,256]{3,2,1,0:T(8,128)(2,1)S(1)} %pad_maximum_fusion), channel_id=1, source_target_pairs={{0,2},{1,3},{2,0},{3,1},{4,6},{5,7},{6,4},{7,5},{8,10},{9,11},{10,... | collective-permute-start | bytes 491528 | tf_op jit(solution)/shard_map/ppermute | solution.py:160
  43.7 7.1 %collective-permute-start.17 = (bf16[4,64,512]{2,1,0:T(8,128)(2,1)S(1)}, bf16[4,64,512]{2,1,0:T(8,128)(2,1)S(1)}, u32[]{:S(2)}, u32[]{:S(2)}) collective-permute-start(bf16[4,64,512]{2,1,0:T(8,128)(2,1)S(1)} %constant_dynamic-update-slice_fusion.11.refs_1_), channel_id=1, source_target_pairs={{0,1},{1,0},{2,3},{3,2},{4,5},{5,4},{6,7},{7,6},{8,9},{9,8},{10,11... | collective-permute-start | bytes 786440 | tf_op jit(solution)/shard_map/ppermute | solution.py:160
  46.8 14.6 %collective-permute-start.13 = (bf16[4,2,80,256]{3,2,1,0:T(8,128)(2,1)S(1)}, bf16[4,2,80,256]{3,2,1,0:T(8,128)(2,1)S(1)}, u32[]{:S(2)}, u32[]{:S(2)}) collective-permute-start(bf16[4,2,80,256]{3,2,1,0:T(8,128)(2,1)S(1)} %constant_dynamic-update-slice_fusion.6.refs_4_), channel_id=1, source_target_pairs={{0,2},{1,3},{2,0},{3,1},{4,6},{5,7},{6,4},{7,5},{8,10},{9,11},{10,... | collective-permute-start | bytes 983048 | tf_op jit(solution)/shard_map/ppermute | solution.py:160
  47.5 13.9 %collective-permute-start.10 = (bf16[4,2,80,256]{3,2,1,0:T(8,128)(2,1)S(1)}, bf16[4,2,80,256]{3,2,1,0:T(8,128)(2,1)S(1)}, u32[]{:S(2)}, u32[]{:S(2)}) collective-permute-start(bf16[4,2,80,256]{3,2,1,0:T(8,128)(2,1)S(1)} %constant_dynamic-update-slice_fusion.3.refs_0_), channel_id=1, source_target_pairs={{0,16},{16,0},{1,17},{17,1},{2,18},{18,2},{3,19},{19,3},{4,20},{20... | collective-permute-start | bytes 983048 | tf_op jit(solution)/shard_map/ppermute | solution.py:163
  49.0 12.4 %collective-permute-start.7 = (bf16[4,2,80,256]{3,2,1,0:T(8,128)(2,1)S(1)}, bf16[4,2,80,256]{3,2,1,0:T(8,128)(2,1)S(1)}, u32[]{:S(2)}, u32[]{:S(2)}) collective-permute-start(bf16[4,2,80,256]{3,2,1,0:T(8,128)(2,1)S(1)} %constant_dynamic-update-slice_fusion.refs_0_), channel_id=1, source_target_pairs={{0,4},{1,5},{2,6},{3,7},{4,0},{5,1},{6,2},{7,3},{8,12},{9,13},{10,... | collective-permute-start | bytes 983048 | tf_op jit(solution)/shard_map/ppermute | solution.py:160
  50.8 11.7 %collective-permute-start.18 = (bf16[4,2,80,256]{3,2,1,0:T(8,128)(2,1)S(1)}, bf16[4,2,80,256]{3,2,1,0:T(8,128)(2,1)S(1)}, u32[]{:S(2)}, u32[]{:S(2)}) collective-permute-start(bf16[4,2,80,256]{3,2,1,0:T(8,128)(2,1)S(1)} %constant_dynamic-update-slice_fusion.refs_0_), channel_id=1, source_target_pairs={{0,1},{1,0},{2,3},{3,2},{4,5},{5,4},{6,7},{7,6},{8,9},{9,8},{10,11... | collective-permute-start | bytes 983048 | tf_op jit(solution)/shard_map/ppermute | solution.py:160
  51.3 11.8 %copy-start.2 = (s32[6]{0:T(128)S(1)}, s32[6]{0:T(128)}, u32[]{:S(2)}) copy-start(s32[6]{0:T(128)} %offsets.3) | copy-start | bytes 76
  61.4 1.7 %collective-permute-start.19 = (bf16[4,2,80,256]{3,2,1,0:T(8,128)(2,1)S(1)}, bf16[4,2,80,256]{3,2,1,0:T(8,128)(2,1)S(1)}, u32[]{:S(2)}, u32[]{:S(2)}) collective-permute-start(bf16[4,2,80,256]{3,2,1,0:T(8,128)(2,1)S(1)} %collective-permute-done.7.refs_1_), channel_id=1, source_target_pairs={{0,1},{1,0},{2,3},{3,2},{4,5},{5,4},{6,7},{7,6},{8,9},{9,8},{10,11... | collective-permute-start | bytes 983048 | tf_op jit(solution)/shard_map/ppermute | solution.py:160
  61.6 3.4 %collective-permute-start.22 = (bf16[4,2,80,256]{3,2,1,0:T(8,128)(2,1)S(1)}, bf16[4,2,80,256]{3,2,1,0:T(8,128)(2,1)S(1)}, u32[]{:S(2)}, u32[]{:S(2)}) collective-permute-start(bf16[4,2,80,256]{3,2,1,0:T(8,128)(2,1)S(1)} %constant_dynamic-update-slice_fusion.6.refs_4_), channel_id=1, source_target_pairs={{0,1},{1,0},{2,3},{3,2},{4,5},{5,4},{6,7},{7,6},{8,9},{9,8},{10,11... | collective-permute-start | bytes 983048 | tf_op jit(solution)/shard_map/ppermute | solution.py:160
  62.0 3.0 %collective-permute-start.20 = (bf16[4,2,80,256]{3,2,1,0:T(8,128)(2,1)S(1)}, bf16[4,2,80,256]{3,2,1,0:T(8,128)(2,1)S(1)}, u32[]{:S(2)}, u32[]{:S(2)}) collective-permute-start(bf16[4,2,80,256]{3,2,1,0:T(8,128)(2,1)S(1)} %constant_dynamic-update-slice_fusion.3.refs_0_), channel_id=1, source_target_pairs={{0,1},{1,0},{2,3},{3,2},{4,5},{5,4},{6,7},{7,6},{8,9},{9,8},{10,11... | collective-permute-start | bytes 983048 | tf_op jit(solution)/shard_map/ppermute | solution.py:160
  62.1 2.9 %collective-permute-start.21 = (bf16[4,2,80,256]{3,2,1,0:T(8,128)(2,1)S(1)}, bf16[4,2,80,256]{3,2,1,0:T(8,128)(2,1)S(1)}, u32[]{:S(2)}, u32[]{:S(2)}) collective-permute-start(bf16[4,2,80,256]{3,2,1,0:T(8,128)(2,1)S(1)} %collective-permute-done.10.refs_1_), channel_id=1, source_target_pairs={{0,1},{1,0},{2,3},{3,2},{4,5},{5,4},{6,7},{7,6},{8,9},{9,8},{10,11... | collective-permute-start | bytes 983048 | tf_op jit(solution)/shard_map/ppermute | solution.py:160
  62.5 2.5 %collective-permute-start.23 = (bf16[4,2,80,256]{3,2,1,0:T(8,128)(2,1)S(1)}, bf16[4,2,80,256]{3,2,1,0:T(8,128)(2,1)S(1)}, u32[]{:S(2)}, u32[]{:S(2)}) collective-permute-start(bf16[4,2,80,256]{3,2,1,0:T(8,128)(2,1)S(1)} %collective-permute-done.13.refs_5_), channel_id=1, source_target_pairs={{0,1},{1,0},{2,3},{3,2},{4,5},{5,4},{6,7},{7,6},{8,9},{9,8},{10,11... | collective-permute-start | bytes 983048 | tf_op jit(solution)/shard_map/ppermute | solution.py:160

commit v30 on v27

--- a/solution.py
+++ b/solution.py
@@ -38,10 +38,17 @@
 def pack_kernel(basis, factor, out, sems):
     at = aligned(lax.rem(lax.axis_index("row"), 2), HALF)
     pv = basis.shape[1]
+    start = lax.rem(lax.axis_index("row"), 2) * HALF
+    step = HALF // 4
     copies = [
-        pltpu.make_async_copy(basis.at[at], out.at[:, :pv, :], sems.at[0]),
-        pltpu.make_async_copy(factor.at[at], out.at[:, pv:, :], sems.at[1]),
+        pltpu.make_async_copy(
+            basis.at[pl.ds(start + k * step, step)],
+            out.at[k * step : (k + 1) * step, :pv, :],
+            sems.at[k],
+        )
+        for k in range(4)
     ]
+    copies.append(pltpu.make_async_copy(factor.at[at], out.at[:, pv:, :], sems.at[4]))
     for copy in copies:
         copy.start()
     for copy in copies:
@@ -177,7 +184,7 @@
         out_shape=jax.ShapeDtypeStruct((HALF,) + piece, dtype),
         in_specs=[HBM, HBM],
         out_specs=VMEM,
-        scratch_shapes=[pltpu.SemaphoreType.DMA((2,))],
+        scratch_shapes=[pltpu.SemaphoreType.DMA((5,))],
         compiler_params=limit(56),
         cost_estimate=cost([basis, factor]),
         name="pack",

time: 66 us -> 66.1 us (level)
  no operation moved by 1% of the time
where the time goes in v30:
time: 66.1 us; the launch traced here: 65.8 us
  starting transfers between devices  25.4 us (38%)
  waiting for transfers between devices  18.7 us (28%)
  blocking collectives  11.9 us (18%)
  Pallas kernels  9.22 us (14%)
    ppermute x21, starting transfers between devices, over_col(): return lax.ppermute(x, 'col', [(c, c ^ mask) for c in range(cols)])  16 us
    ppermute x21, waiting for transfers between devices, over_col(): return lax.ppermute(x, 'col', [(c, c ^ mask) for c in range(cols)])  15.5 us
    all_to_all x1, blocking collectives, local(): lax.all_to_all(merged.reshape(rows * cols, each, width), ('row', 'col'),...  11.9 us
    pallas_call x2, Pallas kernels, local(): pl.pallas_call(functools.partial(chain_kernel, cols, groups, slots, sum((...  5.68 us
    ppermute x4, starting transfers between devices, over_row(): return lax.ppermute(x, 'row', [(r, r ^ mask) for r in range(rows)])  5.41 us
    all_to_all x1, starting transfers between devices, local(): slices = lax.all_to_all(packed, 'col', 0, 0, axis_index_groups=members)  3.95 us
    ppermute x4, waiting for transfers between devices, over_row(): return lax.ppermute(x, 'row', [(r, r ^ mask) for r in range(rows)])  3.19 us
    pallas_call x1, Pallas kernels, local(): pl.pallas_call(pack_kernel, out_shape=jax.ShapeDtypeStruct((HALF,) + piec...  1.73 us
  transfers between devices with their start and end apart: 26, of which 10 were waited for; matrix products, arithmetic and copies ran while one was open for 0% of the time, Pallas kernels for 7%

profile of v30, /device:TPU:0, one launch (start us, length us, event | category | flops | bytes accessed | tf_op | source)
XLA Modules:
  0.0 65.8 jit_solution(3588176115776528976)
XLA Ops:
  0.0 4.0 %collective-permute-start = (bf16[64,512]{1,0:T(8,128)(2,1)}, bf16[64,512]{1,0:T(8,128)(2,1)S(1)}, u32[]{:S(2)}, u32[]{:S(2)}) collective-permute-start(bf16[64,512]{1,0:T(8,128)(2,1)} %param.7), channel_id=1, source_target_pairs={{0,8},{1,9},{2,10},{3,11},{4,12},{5,13},{6,14},{7,15},{8,0},{9,1},... | collective-permute-start | bytes 196616 | tf_op jit(solution)/shard_map/ppermute | solution.py:169
  4.0 1.7 %pack.1 = bf16[8,80,256]{2,1,0:T(8,128)(2,1)} custom-call(bf16[16,64,256]{2,1,0:T(8,128)(2,1)} %bitcast.7, bf16[16,16,256]{2,1,0:T(8,128)(2,1)} %bitcast.8), custom_call_target="tpu_custom_call" | custom-call | bytes 655360 | tf_op jit(solution)/shard_map/pack/pallas_call | solution.py:182
  5.8 0.0 copy-start.3
  5.8 4.0 %all-to-all-start = ((bf16[8,80,256]{2,1,0:T(8,128)(2,1)}), bf16[8,80,256]{2,1,0:T(8,128)(2,1)S(1)}, u32[]{:S(2)}, u32[]{:S(2)}) async-start(bf16[8,80,256]{2,1,0:T(8,128)(2,1)} %pack.1), calls=%async_computation | async-start | bytes 655360 | tf_op jit(solution)/shard_map/all_to_all | solution.py:193
  9.8 1.6 %collective-permute-start.2 = (bf16[64,512]{1,0:T(8,128)(2,1)S(1)}, bf16[64,512]{1,0:T(8,128)(2,1)S(1)}, u32[]{:S(2)}, u32[]{:S(2)}) collective-permute-start(bf16[64,512]{1,0:T(8,128)(2,1)S(1)} %get-tuple-element.31), channel_id=1, source_target_pairs={{0,16},{16,0},{1,17},{17,1},{2,18},{18,2},{3,19},{19,3},{4,20},{20... | collective-permute-start | bytes 196616 | tf_op jit(solution)/shard_map/ppermute | solution.py:172
  11.3 2.0 %collective-permute-start.1 = (bf16[1,64,512]{2,1,0:T(8,128)(2,1)S(1)}, bf16[1,64,512]{2,1,0:T(8,128)(2,1)S(1)}, u32[]{:S(2)}, u32[]{:S(2)}) collective-permute-start(bf16[1,64,512]{2,1,0:T(8,128)(2,1)S(1)} %get-tuple-element.32), channel_id=1, source_target_pairs={{0,2},{1,3},{2,0},{3,1},{4,6},{5,7},{6,4},{7,5},{8,10},{9,11},{10,... | collective-permute-start | bytes 196616 | tf_op jit(solution)/shard_map/ppermute | solution.py:169
  13.4 1.0 %collective-permute-done.2 = bf16[64,512]{1,0:T(8,128)(2,1)S(1)} collective-permute-done((bf16[64,512]{1,0:T(8,128)(2,1)S(1)}, bf16[64,512]{1,0:T(8,128)(2,1)S(1)}, u32[]{:S(2)}, u32[]{:S(2)}) %collective-permute-start.2) | collective-permute-done | bytes 65568 | tf_op jit(solution)/shard_map/ppermute | solution.py:172
  14.3 1.8 %collective-permute-start.3 = (bf16[1,64,512]{2,1,0:T(8,128)(2,1)S(1)}, bf16[1,64,512]{2,1,0:T(8,128)(2,1)S(1)}, u32[]{:S(2)}, u32[]{:S(2)}) collective-permute-start(bf16[1,64,512]{2,1,0:T(8,128)(2,1)S(1)} %bitcast.9), channel_id=1, source_target_pairs={{0,4},{1,5},{2,6},{3,7},{4,0},{5,1},{6,2},{7,3},{8,12},{9,13},{10,... | collective-permute-start | bytes 196616 | tf_op jit(solution)/shard_map/ppermute | solution.py:169
  16.1 1.8 %collective-permute-done.1 = bf16[1,64,512]{2,1,0:T(8,128)(2,1)S(1)} collective-permute-done((bf16[1,64,512]{2,1,0:T(8,128)(2,1)S(1)}, bf16[1,64,512]{2,1,0:T(8,128)(2,1)S(1)}, u32[]{:S(2)}, u32[]{:S(2)}) %collective-permute-start.1) | collective-permute-done | bytes 65568 | tf_op jit(solution)/shard_map/ppermute | solution.py:169
  17.9 0.0 copy-start.1
  17.9 0.7 %collective-permute-done.3 = bf16[1,64,512]{2,1,0:T(8,128)(2,1)S(1)} collective-permute-done((bf16[1,64,512]{2,1,0:T(8,128)(2,1)S(1)}, bf16[1,64,512]{2,1,0:T(8,128)(2,1)S(1)}, u32[]{:S(2)}, u32[]{:S(2)}) %collective-permute-start.3) | collective-permute-done | bytes 65568 | tf_op jit(solution)/shard_map/ppermute | solution.py:169
  18.6 0.0 all-to-all-done.held
  18.6 0.7 %pick.1 = bf16[5,80,256]{2,1,0:T(8,128)(2,1)S(1)} custom-call(s32[6]{0:T(128)S(1)} %copy-done.1, bf16[8,80,256]{2,1,0:T(8,128)(2,1)S(1)} %all-to-all-done.held), custom_call_target="tpu_custom_call" | custom-call | bytes 327680 | tf_op jit(solution)/shard_map/pick/pallas_call | solution.py:222
  19.4 0.4 collective-permute-start.4
  19.8 2.6 %collective-permute-start.5 = (bf16[4,80,256]{2,1,0:T(8,128)(2,1)S(1)}, bf16[4,80,256]{2,1,0:T(8,128)(2,1)S(1)}, u32[]{:S(2)}, u32[]{:S(2)}) collective-permute-start(bf16[4,80,256]{2,1,0:T(8,128)(2,1)S(1)} %slice.9), channel_id=1, source_target_pairs={{0,8},{1,9},{2,10},{3,11},{4,12},{5,13},{6,14},{7,15},{8,0},{9,1},... | collective-permute-start | bytes 491528 | tf_op jit(solution)/shard_map/ppermute | solution.py:169
  22.4 5.6 %collective-permute-done.4.refs_0_ = bf16[1,80,256]{2,1,0:T(8,128)(2,1)S(1)} collective-permute-done((bf16[1,80,256]{2,1,0:T(8,128)(2,1)S(1)}, bf16[1,80,256]{2,1,0:T(8,128)(2,1)S(1)}, u32[]{:S(2)}, u32[]{:S(2)}) %collective-permute-start.4) | collective-permute-done | bytes 40992 | tf_op jit(solution)/shard_map/ppermute | solution.py:169
  28.0 0.0 collective-permute-start.15
  28.1 0.1 collective-permute-start.16
  28.2 0.1 collective-permute-start.17
  28.3 3.0 %collective-permute-done.5.refs_1_ = bf16[4,80,256]{2,1,0:T(8,128)(2,1)S(1)} collective-permute-done((bf16[4,80,256]{2,1,0:T(8,128)(2,1)S(1)}, bf16[4,80,256]{2,1,0:T(8,128)(2,1)S(1)}, u32[]{:S(2)}, u32[]{:S(2)}) %collective-permute-start.5) | collective-permute-done | bytes 163872 | tf_op jit(solution)/shard_map/ppermute | solution.py:169
  31.3 0.6 order.1
  31.9 0.1 collective-permute-start.12
  32.0 1.0 %collective-permute-start.9 = (bf16[1,2,80,256]{3,2,1,0:T(8,128)(2,1)S(1)}, bf16[1,2,80,256]{3,2,1,0:T(8,128)(2,1)S(1)}, u32[]{:S(2)}, u32[]{:S(2)}) collective-permute-start(bf16[1,2,80,256]{3,2,1,0:T(8,128)(2,1)S(1)} %get-tuple-element.23), channel_id=1, source_target_pairs={{0,2},{1,3},{2,0},{3,1},{4,6},{5,7},{6,4},{7,5},{8,10},{9,11},{10,... | collective-permute-start | bytes 245768 | tf_op jit(solution)/shard_map/ppermute | solution.py:169
  33.0 1.6 %collective-permute-start.6 = (bf16[1,2,80,256]{3,2,1,0:T(8,128)(2,1)S(1)}, bf16[1,2,80,256]{3,2,1,0:T(8,128)(2,1)S(1)}, u32[]{:S(2)}, u32[]{:S(2)}) collective-permute-start(bf16[1,2,80,256]{3,2,1,0:T(8,128)(2,1)S(1)} %get-tuple-element.22), channel_id=1, source_target_pairs={{0,16},{16,0},{1,17},{17,1},{2,18},{18,2},{3,19},{19,3},{4,20},{20... | collective-permute-start | bytes 245768 | tf_op jit(solution)/shard_map/ppermute | solution.py:172
  34.6 0.1 collective-permute-start.18
  34.7 1.7 %collective-permute-done.12 = bf16[1,2,80,256]{3,2,1,0:T(8,128)(2,1)S(1)} collective-permute-done((bf16[1,2,80,256]{3,2,1,0:T(8,128)(2,1)S(1)}, bf16[1,2,80,256]{3,2,1,0:T(8,128)(2,1)S(1)}, u32[]{:S(2)}, u32[]{:S(2)}) %collective-permute-start.12) | collective-permute-done | bytes 81952 | tf_op jit(solution)/shard_map/ppermute | solution.py:169
  36.4 0.0 copy-start
  36.5 1.6 %collective-permute-start.13 = (bf16[2,2,80,256]{3,2,1,0:T(8,128)(2,1)S(1)}, bf16[2,2,80,256]{3,2,1,0:T(8,128)(2,1)S(1)}, u32[]{:S(2)}, u32[]{:S(2)}) collective-permute-start(bf16[2,2,80,256]{3,2,1,0:T(8,128)(2,1)S(1)} %pad_maximum_fusion.2), channel_id=1, source_target_pairs={{0,16},{16,0},{1,17},{17,1},{2,18},{18,2},{3,19},{19,3},{4,20},{20... | collective-permute-start | bytes 491528 | tf_op jit(solution)/shard_map/ppermute | solution.py:172
  38.0 0.5 collective-permute-start.10
  38.6 1.0 %collective-permute-start.7 = (bf16[2,2,80,256]{3,2,1,0:T(8,128)(2,1)S(1)}, bf16[2,2,80,256]{3,2,1,0:T(8,128)(2,1)S(1)}, u32[]{:S(2)}, u32[]{:S(2)}) collective-permute-start(bf16[2,2,80,256]{3,2,1,0:T(8,128)(2,1)S(1)} %pad_maximum_fusion), channel_id=1, source_target_pairs={{0,2},{1,3},{2,0},{3,1},{4,6},{5,7},{6,4},{7,5},{8,10},{9,11},{10,... | collective-permute-start | bytes 491528 | tf_op jit(solution)/shard_map/ppermute | solution.py:169
  39.6 2.2 %collective-permute-done.13 = bf16[2,2,80,256]{3,2,1,0:T(8,128)(2,1)S(1)} collective-permute-done((bf16[2,2,80,256]{3,2,1,0:T(8,128)(2,1)S(1)}, bf16[2,2,80,256]{3,2,1,0:T(8,128)(2,1)S(1)}, u32[]{:S(2)}, u32[]{:S(2)}) %collective-permute-start.13) | collective-permute-done | bytes 163872 | tf_op jit(solution)/shard_map/ppermute | solution.py:172
  41.9 0.9 %collective-permute-start.14 = (bf16[4,2,80,256]{3,2,1,0:T(8,128)(2,1)S(1)}, bf16[4,2,80,256]{3,2,1,0:T(8,128)(2,1)S(1)}, u32[]{:S(2)}, u32[]{:S(2)}) collective-permute-start(bf16[4,2,80,256]{3,2,1,0:T(8,128)(2,1)S(1)} %constant_dynamic-update-slice_fusion.6.refs_4_), channel_id=1, source_target_pairs={{0,2},{1,3},{2,0},{3,1},{4,6},{5,7},{6,4},{7,5},{8,10},{9,11},{10,... | collective-permute-start | bytes 983048 | tf_op jit(solution)/shard_map/ppermute | solution.py:169
  42.7 0.7 %collective-permute-done.10 = bf16[2,2,80,256]{3,2,1,0:T(8,128)(2,1)S(1)} collective-permute-done((bf16[2,2,80,256]{3,2,1,0:T(8,128)(2,1)S(1)}, bf16[2,2,80,256]{3,2,1,0:T(8,128)(2,1)S(1)}, u32[]{:S(2)}, u32[]{:S(2)}) %collective-permute-start.10) | collective-permute-done | bytes 163872 | tf_op jit(solution)/shard_map/ppermute | solution.py:169
  43.4 0.7 %collective-permute-start.11 = (bf16[4,2,80,256]{3,2,1,0:T(8,128)(2,1)S(1)}, bf16[4,2,80,256]{3,2,1,0:T(8,128)(2,1)S(1)}, u32[]{:S(2)}, u32[]{:S(2)}) collective-permute-start(bf16[4,2,80,256]{3,2,1,0:T(8,128)(2,1)S(1)} %constant_dynamic-update-slice_fusion.3.refs_0_), channel_id=1, source_target_pairs={{0,16},{16,0},{1,17},{17,1},{2,18},{18,2},{3,19},{19,3},{4,20},{20... | collective-permute-start | bytes 983048 | tf_op jit(solution)/shard_map/ppermute | solution.py:172
  44.2 1.5 %collective-permute-done.7 = bf16[2,2,80,256]{3,2,1,0:T(8,128)(2,1)S(1)} collective-permute-done((bf16[2,2,80,256]{3,2,1,0:T(8,128)(2,1)S(1)}, bf16[2,2,80,256]{3,2,1,0:T(8,128)(2,1)S(1)}, u32[]{:S(2)}, u32[]{:S(2)}) %collective-permute-start.7) | collective-permute-done | bytes 163872 | tf_op jit(solution)/shard_map/ppermute | solution.py:169
  45.7 0.1 collective-permute-start.8
  45.8 0.1 collective-permute-start.19
  45.9 0.5 merge.1
  46.4 0.0 copy-start.2
  46.4 11.9 %all_to_all.10.start = f32[32,4,128]{2,1,0:T(4,128)S(1)} all-to-all(f32[32,4,128]{2,1,0:T(4,128)S(1)} %bitcast.6), channel_id=1, replica_groups=mesh['row'=2,'col'=16] {'row','col'}, dimensions={0} | all-to-all | bytes 131072 | tf_op jit(solution)/shard_map/all_to_all | solution.py:274
  58.3 0.2 collective-permute-start.20
  58.5 0.4 collective-permute-start.23
  58.9 0.1 collective-permute-start.21
  59.0 0.4 collective-permute-start.22
  59.4 0.1 collective-permute-start.24
  59.5 0.5 collective-permute-done.20.refs_3_
  60.0 1.9 %chain0.1.start = f32[8,2048]{1,0:T(8,128)S(1)} custom-call(s32[6]{0:T(128)S(1)} %copy-done.2, f32[32,4,128]{2,1,0:T(4,128)S(1)} %all_to_all.10.start, bf16[4,2,80,256]{3,2,1,0:T(8,128)(2,1)S(1)} %constant_dynamic-update-slice_fusion.refs_0_, bf16[4,2,80,256]{3,2,1,0:T(8,128)(2,1)S(1)} %collective-permute-done.8.refs_1_, ...), custom_call_target="tpu_custom_call" | custom-call | flops 67108864 | bytes 1310720 | tf_op jit(solution)/shard_map/chain0/pallas_call | solution.py:292
  62.0 3.8 %chain1.1 = bf16[4,2048]{1,0:T(4,128)(2,1)} custom-call(s32[6]{0:T(128)S(1)} %copy-done.2, f32[8,2048]{1,0:T(8,128)S(1)} %chain0.1.start, bf16[4,2,80,256]{3,2,1,0:T(8,128)(2,1)S(1)} %constant_dynamic-update-slice_fusion.3.refs_0_, bf16[4,2,80,256]{3,2,1,0:T(8,128)(2,1)S(1)} %collective-permute-done.11.refs_1_, ...), custom_call_target="tpu_custom_call" | custom-call | flops 134217728 | bytes 2621440 | tf_op jit(solution)/shard_map/chain1/pallas_call | solution.py:292
  (39 shorter events, 0.3 us)
Async XLA Ops:
  0.0 9.7 %collective-permute-start = (bf16[64,512]{1,0:T(8,128)(2,1)}, bf16[64,512]{1,0:T(8,128)(2,1)S(1)}, u32[]{:S(2)}, u32[]{:S(2)}) collective-permute-start(bf16[64,512]{1,0:T(8,128)(2,1)} %param.7), channel_id=1, source_target_pairs={{0,8},{1,9},{2,10},{3,11},{4,12},{5,13},{6,14},{7,15},{8,0},{9,1},... | collective-permute-start | bytes 196616 | tf_op jit(solution)/shard_map/ppermute | solution.py:169
  5.8 4.0 %copy-start.3 = (bf16[64,512]{1,0:T(8,128)(2,1)S(1)}, bf16[64,512]{1,0:T(8,128)(2,1)}, u32[]{:S(2)}) copy-start(bf16[64,512]{1,0:T(8,128)(2,1)} %param.7) | copy-start | bytes 196612
  5.8 12.8 %all-to-all-start = ((bf16[8,80,256]{2,1,0:T(8,128)(2,1)}), bf16[8,80,256]{2,1,0:T(8,128)(2,1)S(1)}, u32[]{:S(2)}, u32[]{:S(2)}) async-start(bf16[8,80,256]{2,1,0:T(8,128)(2,1)} %pack.1), calls=%async_computation | async-start | bytes 655360 | tf_op jit(solution)/shard_map/all_to_all | solution.py:193
  9.8 4.6 %collective-permute-start.2 = (bf16[64,512]{1,0:T(8,128)(2,1)S(1)}, bf16[64,512]{1,0:T(8,128)(2,1)S(1)}, u32[]{:S(2)}, u32[]{:S(2)}) collective-permute-start(bf16[64,512]{1,0:T(8,128)(2,1)S(1)} %get-tuple-element.31), channel_id=1, source_target_pairs={{0,16},{16,0},{1,17},{17,1},{2,18},{18,2},{3,19},{19,3},{4,20},{20... | collective-permute-start | bytes 196616 | tf_op jit(solution)/shard_map/ppermute | solution.py:172
  11.3 6.5 %collective-permute-start.1 = (bf16[1,64,512]{2,1,0:T(8,128)(2,1)S(1)}, bf16[1,64,512]{2,1,0:T(8,128)(2,1)S(1)}, u32[]{:S(2)}, u32[]{:S(2)}) collective-permute-start(bf16[1,64,512]{2,1,0:T(8,128)(2,1)S(1)} %get-tuple-element.32), channel_id=1, source_target_pairs={{0,2},{1,3},{2,0},{3,1},{4,6},{5,7},{6,4},{7,5},{8,10},{9,11},{10,... | collective-permute-start | bytes 196616 | tf_op jit(solution)/shard_map/ppermute | solution.py:169
  14.3 4.3 %collective-permute-start.3 = (bf16[1,64,512]{2,1,0:T(8,128)(2,1)S(1)}, bf16[1,64,512]{2,1,0:T(8,128)(2,1)S(1)}, u32[]{:S(2)}, u32[]{:S(2)}) collective-permute-start(bf16[1,64,512]{2,1,0:T(8,128)(2,1)S(1)} %bitcast.9), channel_id=1, source_target_pairs={{0,4},{1,5},{2,6},{3,7},{4,0},{5,1},{6,2},{7,3},{8,12},{9,13},{10,... | collective-permute-start | bytes 196616 | tf_op jit(solution)/shard_map/ppermute | solution.py:169
  17.9 0.7 %copy-start.1 = (s32[6]{0:T(128)S(1)}, s32[6]{0:T(128)}, u32[]{:S(2)}) copy-start(s32[6]{0:T(128)} %owners.3) | copy-start | bytes 76
  19.4 8.7 %collective-permute-start.4 = (bf16[1,80,256]{2,1,0:T(8,128)(2,1)S(1)}, bf16[1,80,256]{2,1,0:T(8,128)(2,1)S(1)}, u32[]{:S(2)}, u32[]{:S(2)}) collective-permute-start(bf16[1,80,256]{2,1,0:T(8,128)(2,1)S(1)} %slice.8), channel_id=1, source_target_pairs={{0,8},{1,9},{2,10},{3,11},{4,12},{5,13},{6,14},{7,15},{8,0},{9,1},... | collective-permute-start | bytes 122888 | tf_op jit(solution)/shard_map/ppermute | solution.py:169
  19.8 11.5 %collective-permute-start.5 = (bf16[4,80,256]{2,1,0:T(8,128)(2,1)S(1)}, bf16[4,80,256]{2,1,0:T(8,128)(2,1)S(1)}, u32[]{:S(2)}, u32[]{:S(2)}) collective-permute-start(bf16[4,80,256]{2,1,0:T(8,128)(2,1)S(1)} %slice.9), channel_id=1, source_target_pairs={{0,8},{1,9},{2,10},{3,11},{4,12},{5,13},{6,14},{7,15},{8,0},{9,1},... | collective-permute-start | bytes 491528 | tf_op jit(solution)/shard_map/ppermute | solution.py:169
  28.0 5.0 %collective-permute-start.15 = (bf16[2,64,512]{2,1,0:T(8,128)(2,1)S(1)}, bf16[2,64,512]{2,1,0:T(8,128)(2,1)S(1)}, u32[]{:S(2)}, u32[]{:S(2)}) collective-permute-start(bf16[2,64,512]{2,1,0:T(8,128)(2,1)S(1)} %pad_maximum_fusion.3), channel_id=1, source_target_pairs={{0,4},{1,5},{2,6},{3,7},{4,0},{5,1},{6,2},{7,3},{8,12},{9,13},{10,... | collective-permute-start | bytes 393224 | tf_op jit(solution)/shard_map/ppermute | solution.py:169
  28.1 6.5 %collective-permute-start.16 = (bf16[2,64,512]{2,1,0:T(8,128)(2,1)S(1)}, bf16[2,64,512]{2,1,0:T(8,128)(2,1)S(1)}, u32[]{:S(2)}, u32[]{:S(2)}) collective-permute-start(bf16[2,64,512]{2,1,0:T(8,128)(2,1)S(1)} %pad_maximum_fusion.4), channel_id=1, source_target_pairs={{0,2},{1,3},{2,0},{3,1},{4,6},{5,7},{6,4},{7,5},{8,10},{9,11},{10,... | collective-permute-start | bytes 393224 | tf_op jit(solution)/shard_map/ppermute | solution.py:169
  28.2 17.6 %collective-permute-start.17 = (bf16[4,64,512]{2,1,0:T(8,128)(2,1)S(1)}, bf16[4,64,512]{2,1,0:T(8,128)(2,1)S(1)}, u32[]{:S(2)}, u32[]{:S(2)}) collective-permute-start(bf16[4,64,512]{2,1,0:T(8,128)(2,1)S(1)} %constant_dynamic-update-slice_fusion.9.refs_0_), channel_id=1, source_target_pairs={{0,1},{1,0},{2,3},{3,2},{4,5},{5,4},{6,7},{7,6},{8,9},{9,8},{10,11... | collective-permute-start | bytes 786440 | tf_op jit(solution)/shard_map/ppermute | solution.py:169
  31.9 4.5 %collective-permute-start.12 = (bf16[1,2,80,256]{3,2,1,0:T(8,128)(2,1)S(1)}, bf16[1,2,80,256]{3,2,1,0:T(8,128)(2,1)S(1)}, u32[]{:S(2)}, u32[]{:S(2)}) collective-permute-start(bf16[1,2,80,256]{3,2,1,0:T(8,128)(2,1)S(1)} %get-tuple-element.24), channel_id=1, source_target_pairs={{0,4},{1,5},{2,6},{3,7},{4,0},{5,1},{6,2},{7,3},{8,12},{9,13},{10,... | collective-permute-start | bytes 245768 | tf_op jit(solution)/shard_map/ppermute | solution.py:169
  32.0 6.0 %collective-permute-start.9 = (bf16[1,2,80,256]{3,2,1,0:T(8,128)(2,1)S(1)}, bf16[1,2,80,256]{3,2,1,0:T(8,128)(2,1)S(1)}, u32[]{:S(2)}, u32[]{:S(2)}) collective-permute-start(bf16[1,2,80,256]{3,2,1,0:T(8,128)(2,1)S(1)} %get-tuple-element.23), channel_id=1, source_target_pairs={{0,2},{1,3},{2,0},{3,1},{4,6},{5,7},{6,4},{7,5},{8,10},{9,11},{10,... | collective-permute-start | bytes 245768 | tf_op jit(solution)/shard_map/ppermute | solution.py:169
  33.0 5.5 %collective-permute-start.6 = (bf16[1,2,80,256]{3,2,1,0:T(8,128)(2,1)S(1)}, bf16[1,2,80,256]{3,2,1,0:T(8,128)(2,1)S(1)}, u32[]{:S(2)}, u32[]{:S(2)}) collective-permute-start(bf16[1,2,80,256]{3,2,1,0:T(8,128)(2,1)S(1)} %get-tuple-element.22), channel_id=1, source_target_pairs={{0,16},{16,0},{1,17},{17,1},{2,18},{18,2},{3,19},{19,3},{4,20},{20... | collective-permute-start | bytes 245768 | tf_op jit(solution)/shard_map/ppermute | solution.py:172
  34.6 11.3 %collective-permute-start.18 = (bf16[4,64,512]{2,1,0:T(8,128)(2,1)S(1)}, bf16[4,64,512]{2,1,0:T(8,128)(2,1)S(1)}, u32[]{:S(2)}, u32[]{:S(2)}) collective-permute-start(bf16[4,64,512]{2,1,0:T(8,128)(2,1)S(1)} %constant_dynamic-update-slice_fusion.11.refs_1_), channel_id=1, source_target_pairs={{0,1},{1,0},{2,3},{3,2},{4,5},{5,4},{6,7},{7,6},{8,9},{9,8},{10,11... | collective-permute-start | bytes 786440 | tf_op jit(solution)/shard_map/ppermute | solution.py:169
  36.4 9.5 %copy-start = (bf16[4096,128]{1,0:T(8,128)(2,1)S(1)}, bf16[4096,128]{1,0:T(8,128)(2,1)}, u32[]{:S(2)}) copy-start(bf16[4096,128]{1,0:T(8,128)(2,1)} %sub.6) | copy-start | bytes 3145732
  36.5 5.4 %collective-permute-start.13 = (bf16[2,2,80,256]{3,2,1,0:T(8,128)(2,1)S(1)}, bf16[2,2,80,256]{3,2,1,0:T(8,128)(2,1)S(1)}, u32[]{:S(2)}, u32[]{:S(2)}) collective-permute-start(bf16[2,2,80,256]{3,2,1,0:T(8,128)(2,1)S(1)} %pad_maximum_fusion.2), channel_id=1, source_target_pairs={{0,16},{16,0},{1,17},{17,1},{2,18},{18,2},{3,19},{19,3},{4,20},{20... | collective-permute-start | bytes 491528 | tf_op jit(solution)/shard_map/ppermute | solution.py:172
  38.0 5.4 %collective-permute-start.10 = (bf16[2,2,80,256]{3,2,1,0:T(8,128)(2,1)S(1)}, bf16[2,2,80,256]{3,2,1,0:T(8,128)(2,1)S(1)}, u32[]{:S(2)}, u32[]{:S(2)}) collective-permute-start(bf16[2,2,80,256]{3,2,1,0:T(8,128)(2,1)S(1)} %pad_maximum_fusion.1), channel_id=1, source_target_pairs={{0,4},{1,5},{2,6},{3,7},{4,0},{5,1},{6,2},{7,3},{8,12},{9,13},{10,... | collective-permute-start | bytes 491528 | tf_op jit(solution)/shard_map/ppermute | solution.py:169
  38.6 7.1 %collective-permute-start.7 = (bf16[2,2,80,256]{3,2,1,0:T(8,128)(2,1)S(1)}, bf16[2,2,80,256]{3,2,1,0:T(8,128)(2,1)S(1)}, u32[]{:S(2)}, u32[]{:S(2)}) collective-permute-start(bf16[2,2,80,256]{3,2,1,0:T(8,128)(2,1)S(1)} %pad_maximum_fusion), channel_id=1, source_target_pairs={{0,2},{1,3},{2,0},{3,1},{4,6},{5,7},{6,4},{7,5},{8,10},{9,11},{10,... | collective-permute-start | bytes 491528 | tf_op jit(solution)/shard_map/ppermute | solution.py:169
  41.9 16.5 %collective-permute-start.14 = (bf16[4,2,80,256]{3,2,1,0:T(8,128)(2,1)S(1)}, bf16[4,2,80,256]{3,2,1,0:T(8,128)(2,1)S(1)}, u32[]{:S(2)}, u32[]{:S(2)}) collective-permute-start(bf16[4,2,80,256]{3,2,1,0:T(8,128)(2,1)S(1)} %constant_dynamic-update-slice_fusion.6.refs_4_), channel_id=1, source_target_pairs={{0,2},{1,3},{2,0},{3,1},{4,6},{5,7},{6,4},{7,5},{8,10},{9,11},{10,... | collective-permute-start | bytes 983048 | tf_op jit(solution)/shard_map/ppermute | solution.py:169
  43.4 14.9 %collective-permute-start.11 = (bf16[4,2,80,256]{3,2,1,0:T(8,128)(2,1)S(1)}, bf16[4,2,80,256]{3,2,1,0:T(8,128)(2,1)S(1)}, u32[]{:S(2)}, u32[]{:S(2)}) collective-permute-start(bf16[4,2,80,256]{3,2,1,0:T(8,128)(2,1)S(1)} %constant_dynamic-update-slice_fusion.3.refs_0_), channel_id=1, source_target_pairs={{0,16},{16,0},{1,17},{17,1},{2,18},{18,2},{3,19},{19,3},{4,20},{20... | collective-permute-start | bytes 983048 | tf_op jit(solution)/shard_map/ppermute | solution.py:172
  45.7 12.6 %collective-permute-start.8 = (bf16[4,2,80,256]{3,2,1,0:T(8,128)(2,1)S(1)}, bf16[4,2,80,256]{3,2,1,0:T(8,128)(2,1)S(1)}, u32[]{:S(2)}, u32[]{:S(2)}) collective-permute-start(bf16[4,2,80,256]{3,2,1,0:T(8,128)(2,1)S(1)} %constant_dynamic-update-slice_fusion.refs_0_), channel_id=1, source_target_pairs={{0,4},{1,5},{2,6},{3,7},{4,0},{5,1},{6,2},{7,3},{8,12},{9,13},{10,... | collective-permute-start | bytes 983048 | tf_op jit(solution)/shard_map/ppermute | solution.py:169
  45.8 13.6 %collective-permute-start.19 = (bf16[4,2,80,256]{3,2,1,0:T(8,128)(2,1)S(1)}, bf16[4,2,80,256]{3,2,1,0:T(8,128)(2,1)S(1)}, u32[]{:S(2)}, u32[]{:S(2)}) collective-permute-start(bf16[4,2,80,256]{3,2,1,0:T(8,128)(2,1)S(1)} %constant_dynamic-update-slice_fusion.refs_0_), channel_id=1, source_target_pairs={{0,1},{1,0},{2,3},{3,2},{4,5},{5,4},{6,7},{7,6},{8,9},{9,8},{10,11... | collective-permute-start | bytes 983048 | tf_op jit(solution)/shard_map/ppermute | solution.py:169
  46.4 13.6 %copy-start.2 = (s32[6]{0:T(128)S(1)}, s32[6]{0:T(128)}, u32[]{:S(2)}) copy-start(s32[6]{0:T(128)} %offsets.3) | copy-start | bytes 76
  58.3 1.7 %collective-permute-start.20 = (bf16[4,2,80,256]{3,2,1,0:T(8,128)(2,1)S(1)}, bf16[4,2,80,256]{3,2,1,0:T(8,128)(2,1)S(1)}, u32[]{:S(2)}, u32[]{:S(2)}) collective-permute-start(bf16[4,2,80,256]{3,2,1,0:T(8,128)(2,1)S(1)} %collective-permute-done.8.refs_1_), channel_id=1, source_target_pairs={{0,1},{1,0},{2,3},{3,2},{4,5},{5,4},{6,7},{7,6},{8,9},{9,8},{10,11... | collective-permute-start | bytes 983048 | tf_op jit(solution)/shard_map/ppermute | solution.py:169
  58.5 3.4 %collective-permute-start.23 = (bf16[4,2,80,256]{3,2,1,0:T(8,128)(2,1)S(1)}, bf16[4,2,80,256]{3,2,1,0:T(8,128)(2,1)S(1)}, u32[]{:S(2)}, u32[]{:S(2)}) collective-permute-start(bf16[4,2,80,256]{3,2,1,0:T(8,128)(2,1)S(1)} %constant_dynamic-update-slice_fusion.6.refs_4_), channel_id=1, source_target_pairs={{0,1},{1,0},{2,3},{3,2},{4,5},{5,4},{6,7},{7,6},{8,9},{9,8},{10,11... | collective-permute-start | bytes 983048 | tf_op jit(solution)/shard_map/ppermute | solution.py:169
  58.9 3.0 %collective-permute-start.21 = (bf16[4,2,80,256]{3,2,1,0:T(8,128)(2,1)S(1)}, bf16[4,2,80,256]{3,2,1,0:T(8,128)(2,1)S(1)}, u32[]{:S(2)}, u32[]{:S(2)}) collective-permute-start(bf16[4,2,80,256]{3,2,1,0:T(8,128)(2,1)S(1)} %constant_dynamic-update-slice_fusion.3.refs_0_), channel_id=1, source_target_pairs={{0,1},{1,0},{2,3},{3,2},{4,5},{5,4},{6,7},{7,6},{8,9},{9,8},{10,11... | collective-permute-start | bytes 983048 | tf_op jit(solution)/shard_map/ppermute | solution.py:169
  59.0 2.9 %collective-permute-start.22 = (bf16[4,2,80,256]{3,2,1,0:T(8,128)(2,1)S(1)}, bf16[4,2,80,256]{3,2,1,0:T(8,128)(2,1)S(1)}, u32[]{:S(2)}, u32[]{:S(2)}) collective-permute-start(bf16[4,2,80,256]{3,2,1,0:T(8,128)(2,1)S(1)} %collective-permute-done.11.refs_1_), channel_id=1, source_target_pairs={{0,1},{1,0},{2,3},{3,2},{4,5},{5,4},{6,7},{7,6},{8,9},{9,8},{10,11... | collective-permute-start | bytes 983048 | tf_op jit(solution)/shard_map/ppermute | solution.py:169
  59.4 2.5 %collective-permute-start.24 = (bf16[4,2,80,256]{3,2,1,0:T(8,128)(2,1)S(1)}, bf16[4,2,80,256]{3,2,1,0:T(8,128)(2,1)S(1)}, u32[]{:S(2)}, u32[]{:S(2)}) collective-permute-start(bf16[4,2,80,256]{3,2,1,0:T(8,128)(2,1)S(1)} %collective-permute-done.14.refs_5_), channel_id=1, source_target_pairs={{0,1},{1,0},{2,3},{3,2},{4,5},{5,4},{6,7},{7,6},{8,9},{9,8},{10,11... | collective-permute-start | bytes 983048 | tf_op jit(solution)/shard_map/ppermute | solution.py:169
